TPU v7x, 128 devices: a whole 4x4x4 slice. The times are simulated.
128 devices in a mesh: blk: 4 (over y_lo, core), grp: 32 (over x, z, y_hi).
Axes of the slice: x: 4, y: 4 (y_hi: 2, y_lo: 2; y = y_hi * 2 + y_lo), z: 4, core: 2. Of those that a mesh axis runs over, the one named last changes fastest.
Arguments:
- picture_vectors_raw: bfloat16 [16384, 1152], P(('blk', 'grp')), may hold values from -0.1875 to 0.1875
- caption_vectors_raw: bfloat16 [16384, 1152], P(('blk', 'grp')), may hold values from -0.1875 to 0.1875
- logit_multiplier: float32 [1], replicated, may hold values from 60 to 120
- offset_term: float32 [1], replicated, may hold values from -3 to -1
- incoming_adjoint: float32 [1], replicated, may hold values from 100 to 300
Outputs:
- image_grad: float32 [16384, 1152], P(('blk', 'grp'))
- text_grad: float32 [16384, 1152], P(('blk', 'grp'))
All inputs are finite; a program needn't handle non-finite values.
Results may differ from a plain program's by a relative error of at most 0.0079.
The roundings to bfloat16 on the way count: a program that leaves them out, or rounds other values in their place, can miss the bound.
Values may be sent and summed in bfloat16 or wider, within the bound.
No kernel may reach another device: no remote copies, remote signals or barrier semaphores. Data moves between devices by JAX's collectives and lax.ppermute only.
A program may use at most 128 MiB of HBM per device.

v0:
```python
import math

import jax
import jax.numpy as jnp
from jax import lax
from jax.sharding import PartitionSpec as P


def passed_along(value, axis, steps):
    count = lax.axis_size(axis)
    pairs = [(source, (source + steps) % count) for source in range(count)]
    return lax.ppermute(value, axis, pairs)


def unit_rows(embedding):
    values = embedding.astype(jnp.float32)
    row_scale = lax.rsqrt(jnp.mean(values * values, axis=1, keepdims=True) + 1e-06) / math.sqrt(
        values.shape[1]
    )
    return (values * row_scale, row_scale)


def unit_grad(unit_vals, row_scale, upstream_grad):
    return row_scale * (
        upstream_grad - unit_vals * jnp.sum(unit_vals * upstream_grad, axis=1, keepdims=True)
    )


def assemble_interaction(
    first_operand_lines,
    second_operand_lines,
    source_position,
    target_position,
    logit_multiplier,
    offset_term,
):
    similarity_energies = lax.dot_general(
        first_operand_lines,
        second_operand_lines,
        (((1,), (1,)), ((), ())),
        preferred_element_type=jnp.float32,
    )
    similarity_matrix = logit_multiplier[0] * similarity_energies + offset_term[0]
    diag_mask = (source_position[:, None] == target_position[None, :]).astype(jnp.float32)
    return (jax.nn.sigmoid(similarity_matrix) - diag_mask).astype(jnp.bfloat16)


def column_term(all_tiles, all_rows):
    return lax.dot_general(
        all_tiles, all_rows, (((0,), (0,)), ((), ())), preferred_element_type=jnp.float32
    )


def on_device(
    picture_vectors_raw, caption_vectors_raw, logit_multiplier, offset_term, incoming_adjoint
):
    local_vectors = picture_vectors_raw.shape[0]
    embed_width = picture_vectors_raw.shape[1]
    cluster_length = lax.axis_size("grp")
    number_tiles = lax.axis_size("blk")
    block_index = lax.axis_index("blk")
    group_index = lax.axis_index("grp")
    image_unit, image_scale = unit_rows(picture_vectors_raw)
    text_unit, text_scale = unit_rows(caption_vectors_raw)
    image_half = image_unit.astype(jnp.bfloat16)
    text_half = text_unit.astype(jnp.bfloat16)
    derivative_multiplier = (
        incoming_adjoint[0] * logit_multiplier[0] / (local_vectors * cluster_length * number_tiles)
    )
    moving = (image_half, image_unit, image_scale)
    staying = (text_half, text_unit, text_scale)
    lines_each_cluster = lax.all_gather(staying[0], "grp", axis=0, tiled=True)
    group_width = lines_each_cluster.shape[0]
    target_position = block_index * group_width + lax.iota(jnp.int32, group_width)
    local_index = lax.iota(jnp.int32, local_vectors)
    current_quantity = moving[0]
    carried = jnp.zeros((local_vectors, embed_width), jnp.float32)
    tile_list = []
    rows_seen = []
    for rounds in range(number_tiles):
        if rounds > 0:
            current_quantity = passed_along(current_quantity, "blk", 1)
            carried = passed_along(carried, "blk", 1)
        source = (block_index - rounds) % number_tiles
        source_position = (source * cluster_length + group_index) * local_vectors + local_index
        coupling_tile = assemble_interaction(
            current_quantity,
            lines_each_cluster,
            source_position,
            target_position,
            logit_multiplier,
            offset_term,
        )
        carried = carried + jnp.dot(
            coupling_tile, lines_each_cluster, preferred_element_type=jnp.float32
        )
        tile_list.append(coupling_tile)
        rows_seen.append(current_quantity)
    moving_total = passed_along(carried, "blk", 1)
    all_tiles = jnp.concatenate(tile_list, axis=0)
    all_rows = jnp.concatenate(rows_seen, axis=0)
    staying_total = lax.psum_scatter(
        column_term(all_tiles, all_rows), "grp", scatter_dimension=0, tiled=True
    )
    moving_grad = unit_grad(moving[1], moving[2], derivative_multiplier * moving_total)
    staying_grad = unit_grad(staying[1], staying[2], derivative_multiplier * staying_total)
    return (moving_grad, staying_grad)


def solution(mesh):
    placed = (P(("blk", "grp"), None), P(("blk", "grp"), None), P(), P(), P())
    return jax.shard_map(
        on_device,
        mesh=mesh,
        in_specs=placed,
        out_specs=(P(("blk", "grp"), None), P(("blk", "grp"), None)),
        check_vma=False,
    )
```

profile of v0, /device:TPU:1, one launch (start us, length us, event | category | flops | bytes accessed | tf_op | source)
XLA Modules:
  0.0 446.0 jit_solution(2037879552342168333)
XLA Ops:
  7.2 0.0 all-gather.2.cloned.1.call-start
  7.2 1.1 fusion.56
  8.3 1.8 fusion.45
  10.1 0.0 all-gather.2.cloned.1.call-update
  10.1 0.0 reduce-scatter.2.cloned.1.call-start
  10.2 1.1 fusion.52
  11.3 1.1 fusion.48
  12.4 2.8 collective-permute-start.1
  16.5 2.3 collective-permute-done.1
  18.8 2.5 collective-permute-start.3
  21.3 3.7 collective-permute-done.3
  25.0 2.5 collective-permute-start.5
  27.5 97.6 %all-gather.2.cloned.1.call-done = bf16[4096,1152]{1,0:T(8,128)(2,1)} async-done(((bf16[128,1152]{1,0:T(8,128)(2,1)}), bf16[4096,1152]{1,0:T(8,128)(2,1)}) %all-gather.2.cloned.1.call-update) | async-done | bytes 9437200 | tf_op jit(solution)/shard_map/all_gather | solution.py:72
  125.0 7.0 %fusion.21 = bf16[128,4096]{1,0:T(8,128)(2,1)S(1)} fusion(bf16[128,1152]{1,0:T(8,128)(2,1)S(1)} %collective-permute-done.3, bf16[4096,1152]{1,0:T(8,128)(2,1)} %all-gather.2.cloned.1.call-done, s32[4096]{0:T(1024)S(1)} %iota_add_fusion, f32[]{:T(128)} %bitcast.26, f32[]{:T(128)} %bitcast.22, s32[128]{0:T(128)S(1)} %iota_add_fusion.2), kind=kOutput, calls=%fused_computation.25 | convolution fusion | flops 1212678144 | bytes 10797576 | tf_op jit(solution)/shard_map/dot_general | solution.py:37
  132.1 3.2 fusion.24
  135.3 3.2 fusion.27
  138.6 0.0 collective-permute-done.5
  138.6 0.0 copy-start.7
  138.6 4.6 %fusion.18 = bf16[128,4096]{1,0:T(8,128)(2,1)S(1)} fusion(bf16[128,1152]{1,0:T(8,128)(2,1)} %collective-permute-done.5, bf16[4096,1152]{1,0:T(8,128)(2,1)S(1)} %copy-done, s32[4096]{0:T(1024)S(1)} %iota_add_fusion, f32[]{:T(128)} %bitcast.25, f32[]{:T(128)} %bitcast.21, s32[128]{0:T(128)S(1)} %iota_add_fusion.1), kind=kOutput, calls=%fused_computation.22 | convolution fusion | flops 1212678144 | bytes 10797576 | tf_op jit(solution)/shard_map/dot_general | solution.py:37
  143.2 0.0 copy-done.3
  143.2 0.0 copy-done.5
  143.2 0.0 copy-done.7
  143.2 10.5 %fusion.28 = f32[4096,1152]{1,0:T(8,128)} fusion(bf16[128,4096]{1,0:T(8,128)(2,1)S(1)} %fusion.18, bf16[128,4096]{1,0:T(8,128)(2,1)S(1)} %fusion.21, bf16[128,4096]{1,0:T(8,128)(2,1)S(1)} %fusion.24, bf16[128,4096]{1,0:T(8,128)(2,1)S(1)} %fusion.27, bf16[128,1152]{1,0:T(8,128)(2,1)} %collective-permute-done.5, bf16[128,1152]{1,0:T(8,128)(2,1)S(1)} %copy-done.7, ...), kind=kOutput, calls=%fused_computation.32 | convolution fusion | flops 4853334016 | bytes 24248320 | tf_op jit(solution)/shard_map/dot_general | solution.py:49
  153.7 0.0 reduce-scatter.2.cloned.1.call-update
  153.7 0.0 slice-start
  153.8 0.0 slice-start.1
  153.8 5.7 %fusion.58 = f32[128,1152]{1,0:T(8,128)S(1)} fusion(bf16[128,4096]{1,0:T(8,128)(2,1)} %copy-done.3, bf16[4096,1152]{1,0:T(8,128)(2,1)} %all-gather.2.cloned.1.call-done), kind=kOutput, calls=%fused_computation.74 | convolution fusion | flops 1207959552 | bytes 11075584 | tf_op jit(solution)/shard_map/dot_general | solution.py:94
  159.5 0.0 slice-start.2
  159.5 1.5 collective-permute-start
  161.0 11.0 %collective-permute-done = f32[128,1152]{1,0:T(8,128)S(1)} collective-permute-done((f32[128,1152]{1,0:T(8,128)S(1)}, f32[128,1152]{1,0:T(8,128)S(1)}, u32[]{:S(2)}, u32[]{:S(2)}) %collective-permute-start) | collective-permute-done | bytes 589856 | tf_op jit(solution)/shard_map/ppermute | solution.py:12
  172.0 5.4 %convolution_add_fusion = f32[128,1152]{1,0:T(8,128)S(1)} fusion(f32[128,1152]{1,0:T(8,128)S(1)} %collective-permute-done, bf16[128,4096]{1,0:T(8,128)(2,1)S(1)} %fusion.24, bf16[4096,1152]{1,0:T(8,128)(2,1)} %all-gather.2.cloned.1.call-done), kind=kOutput, calls=%fused_computation.40 | convolution fusion | flops 1208107008 | bytes 11665408 | tf_op jit(solution)/shard_map/dot_general | solution.py:94
  177.4 2.5 collective-permute-start.2
  180.0 1.6 fusion.59
  181.5 8.4 %collective-permute-done.2 = f32[128,1152]{1,0:T(8,128)S(1)} collective-permute-done((f32[128,1152]{1,0:T(8,128)S(1)}, f32[128,1152]{1,0:T(8,128)S(1)}, u32[]{:S(2)}, u32[]{:S(2)}) %collective-permute-start.2) | collective-permute-done | bytes 589856 | tf_op jit(solution)/shard_map/ppermute | solution.py:12
  189.9 0.1 add.159
  190.0 0.0 copy-start.1
  190.0 2.5 collective-permute-start.4
  192.5 1.6 fusion.60
  194.1 0.0 copy-start.2
  194.1 8.4 %collective-permute-done.4 = f32[128,1152]{1,0:T(8,128)S(1)} collective-permute-done((f32[128,1152]{1,0:T(8,128)S(1)}, f32[128,1152]{1,0:T(8,128)S(1)}, u32[]{:S(2)}, u32[]{:S(2)}) %collective-permute-start.4) | collective-permute-done | bytes 589856 | tf_op jit(solution)/shard_map/ppermute | solution.py:12
  202.5 0.1 add.166
  202.6 2.5 collective-permute-start.6
  205.8 10.4 %collective-permute-done.6 = f32[128,1152]{1,0:T(8,128)S(1)} collective-permute-done((f32[128,1152]{1,0:T(8,128)S(1)}, f32[128,1152]{1,0:T(8,128)S(1)}, u32[]{:S(2)}, u32[]{:S(2)}) %collective-permute-start.6) | collective-permute-done | bytes 589856 | tf_op jit(solution)/shard_map/ppermute | solution.py:12
  216.2 0.2 fusion.49
  216.4 1.0 fusion.51
  217.5 218.4 %reduce-scatter.2.cloned.1.call-done = f32[128,1152]{1,0:T(8,128)} async-done(((f32[4096,1152]{1,0:T(8,128)}), f32[128,1152]{1,0:T(8,128)}) %reduce-scatter.2.cloned.1.call-update) | async-done | bytes 589840 | tf_op jit(solution)/shard_map/reduce_scatter | solution.py:102
  435.8 1.3 fusion.53
  437.1 2.1 fusion.55
  (21 shorter events, 0.1 us)
Async XLA Ops:
  7.2 117.9 %all-gather.2.cloned.1.call-start = ((), (), s32[]{:S(2)}) async-start(), calls=%async_computation.1 | async-start | bytes 9732096 | tf_op jit(solution)/shard_map/all_gather | solution.py:72
  10.1 425.7 %reduce-scatter.2.cloned.1.call-start = ((), (), s32[]{:S(2)}) async-start(), calls=%async_computation.2 | async-start | bytes 19464192 | tf_op jit(solution)/shard_map/reduce_scatter | solution.py:102
  12.4 6.4 %collective-permute-start.1 = (bf16[128,1152]{1,0:T(8,128)(2,1)S(1)}, bf16[128,1152]{1,0:T(8,128)(2,1)S(1)}, u32[]{:S(2)}, u32[]{:S(2)}) collective-permute-start(bf16[128,1152]{1,0:T(8,128)(2,1)S(1)} %fusion.48), channel_id=1, source_target_pairs={{0,32},{32,64},{64,96},{96,0},{1,33},{33,65},{65,97},{97,1},{2,34}... | collective-permute-start | bytes 884744 | tf_op jit(solution)/shard_map/ppermute | solution.py:12
  18.8 113.2 %copy-start.4 = (bf16[128,1152]{1,0:T(8,128)(2,1)}, bf16[128,1152]{1,0:T(8,128)(2,1)S(1)}, u32[]{:S(2)}) copy-start(bf16[128,1152]{1,0:T(8,128)(2,1)S(1)} %collective-permute-done.1) | copy-start | bytes 884740
  18.8 6.1 %collective-permute-start.3 = (bf16[128,1152]{1,0:T(8,128)(2,1)S(1)}, bf16[128,1152]{1,0:T(8,128)(2,1)S(1)}, u32[]{:S(2)}, u32[]{:S(2)}) collective-permute-start(bf16[128,1152]{1,0:T(8,128)(2,1)S(1)} %collective-permute-done.1), channel_id=1, source_target_pairs={{0,32},{32,64},{64,96},{96,0},{1,33},{33,65},{65,97},{97,1},{2,34}... | collective-permute-start | bytes 884744 | tf_op jit(solution)/shard_map/ppermute | solution.py:12
  25.0 107.1 %copy-start.6 = (bf16[128,1152]{1,0:T(8,128)(2,1)}, bf16[128,1152]{1,0:T(8,128)(2,1)S(1)}, u32[]{:S(2)}) copy-start(bf16[128,1152]{1,0:T(8,128)(2,1)S(1)} %collective-permute-done.3) | copy-start | bytes 884740
  25.0 113.6 %collective-permute-start.5 = (bf16[128,1152]{1,0:T(8,128)(2,1)S(1)}, bf16[128,1152]{1,0:T(8,128)(2,1)}, u32[]{:S(2)}, u32[]{:S(2)}) collective-permute-start(bf16[128,1152]{1,0:T(8,128)(2,1)S(1)} %collective-permute-done.3), channel_id=1, source_target_pairs={{0,32},{32,64},{64,96},{96,0},{1,33},{33,65},{65,97},{97,1},{2,34}... | collective-permute-start | bytes 884744 | tf_op jit(solution)/shard_map/ppermute | solution.py:12
  125.0 7.0 %copy-start = (bf16[4096,1152]{1,0:T(8,128)(2,1)S(1)}, bf16[4096,1152]{1,0:T(8,128)(2,1)}, u32[]{:S(2)}) copy-start(bf16[4096,1152]{1,0:T(8,128)(2,1)} %all-gather.2.cloned.1.call-done) | copy-start | bytes 28311556
  138.6 4.6 %copy-start.3 = (bf16[128,4096]{1,0:T(8,128)(2,1)}, bf16[128,4096]{1,0:T(8,128)(2,1)S(1)}, u32[]{:S(2)}) copy-start(bf16[128,4096]{1,0:T(8,128)(2,1)S(1)} %fusion.27) | copy-start | bytes 3145732
  138.6 4.6 %copy-start.5 = (bf16[128,1152]{1,0:T(8,128)(2,1)S(1)}, bf16[128,1152]{1,0:T(8,128)(2,1)}, u32[]{:S(2)}) copy-start(bf16[128,1152]{1,0:T(8,128)(2,1)} %copy-done.4) | copy-start | bytes 884740
  138.6 4.6 %copy-start.7 = (bf16[128,1152]{1,0:T(8,128)(2,1)S(1)}, bf16[128,1152]{1,0:T(8,128)(2,1)}, u32[]{:S(2)}) copy-start(bf16[128,1152]{1,0:T(8,128)(2,1)} %copy-done.6) | copy-start | bytes 884740
  153.7 26.2 %slice-start = ((s8[9437184]{0:T(1024)(128)(4,1)}), s8[4194304]{0:T(1024)(128)(4,1)S(1)}, s32[]{:S(2)}) async-start(s8[9437184]{0:T(1024)(128)(4,1)} %bitcast.29), calls=%async_computation.3 | async-start | bytes 8388608
  153.8 26.2 %slice-start.1 = ((s8[9437184]{0:T(1024)(128)(4,1)}), s8[4194304]{0:T(1024)(128)(4,1)S(1)}, s32[]{:S(2)}) async-start(s8[9437184]{0:T(1024)(128)(4,1)} %bitcast.29), calls=%async_computation.4 | async-start | bytes 8388608
  159.5 20.5 %slice-start.2 = ((s8[9437184]{0:T(1024)(128)(4,1)}), s8[1048576]{0:T(1024)(128)(4,1)S(1)}, s32[]{:S(2)}) async-start(s8[9437184]{0:T(1024)(128)(4,1)} %bitcast.29), calls=%async_computation.5 | async-start | bytes 2097152
  159.5 12.6 %collective-permute-start = (f32[128,1152]{1,0:T(8,128)S(1)}, f32[128,1152]{1,0:T(8,128)S(1)}, u32[]{:S(2)}, u32[]{:S(2)}) collective-permute-start(f32[128,1152]{1,0:T(8,128)S(1)} %fusion.58), channel_id=1, source_target_pairs={{0,32},{32,64},{64,96},{96,0},{1,33},{33,65},{65,97},{97,1},{2,34}... | collective-permute-start | bytes 1769480 | tf_op jit(solution)/shard_map/ppermute | solution.py:12
  177.4 12.5 %collective-permute-start.2 = (f32[128,1152]{1,0:T(8,128)S(1)}, f32[128,1152]{1,0:T(8,128)S(1)}, u32[]{:S(2)}, u32[]{:S(2)}) collective-permute-start(f32[128,1152]{1,0:T(8,128)S(1)} %convolution_add_fusion), channel_id=1, source_target_pairs={{0,32},{32,64},{64,96},{96,0},{1,33},{33,65},{65,97},{97,1},{2,34}... | collective-permute-start | bytes 1769480 | tf_op jit(solution)/shard_map/ppermute | solution.py:12
  190.0 26.2 %copy-start.1 = (bf16[128,1152]{1,0:T(8,128)(2,1)S(1)}, bf16[128,1152]{1,0:T(8,128)(2,1)}, u32[]{:S(2)}) copy-start(bf16[128,1152]{1,0:T(8,128)(2,1)} %param.5) | copy-start | bytes 884740
  190.0 12.5 %collective-permute-start.4 = (f32[128,1152]{1,0:T(8,128)S(1)}, f32[128,1152]{1,0:T(8,128)S(1)}, u32[]{:S(2)}, u32[]{:S(2)}) collective-permute-start(f32[128,1152]{1,0:T(8,128)S(1)} %add.159), channel_id=1, source_target_pairs={{0,32},{32,64},{64,96},{96,0},{1,33},{33,65},{65,97},{97,1},{2,34}... | collective-permute-start | bytes 1769480 | tf_op jit(solution)/shard_map/ppermute | solution.py:12
  194.1 241.7 %copy-start.2 = (bf16[128,1152]{1,0:T(8,128)(2,1)S(1)}, bf16[128,1152]{1,0:T(8,128)(2,1)}, u32[]{:S(2)}) copy-start(bf16[128,1152]{1,0:T(8,128)(2,1)} %param.6) | copy-start | bytes 884740
  202.6 13.6 %collective-permute-start.6 = (f32[128,1152]{1,0:T(8,128)S(1)}, f32[128,1152]{1,0:T(8,128)S(1)}, u32[]{:S(2)}, u32[]{:S(2)}) collective-permute-start(f32[128,1152]{1,0:T(8,128)S(1)} %add.166), channel_id=1, source_target_pairs={{0,32},{32,64},{64,96},{96,0},{1,33},{33,65},{65,97},{97,1},{2,34}... | collective-permute-start | bytes 1769480 | tf_op jit(solution)/shard_map/ppermute | solution.py:12
Sparse Core Ops, SparseCore 0:
  11.5 113.4 all-gather.1
  153.9 281.8 reduce-scatter.1
where the time goes:
time: 447 us; the launch traced here: 446 us
  waiting for transfers between devices  360 us (81%)
  matrix products  42.7 us (10%)
  starting transfers between devices  17 us (4%)
  between operations  16.2 us (4%)
  other arithmetic  9.91 us (2%)
    reduce_scatter x1, waiting for transfers between devices, on_device(): lax.psum_scatter(column_term(all_tiles, all_rows), 'grp', scatter_dimensi...  218 us
    all_gather x1, waiting for transfers between devices, on_device(): lines_each_cluster = lax.all_gather(staying[0], 'grp', axis=0, tiled=True)  97.6 us
    ppermute x7, waiting for transfers between devices, passed_along(): return lax.ppermute(value, axis, pairs)  44.2 us
    dot_general x4, matrix products, assemble_interaction(): lax.dot_general(first_operand_lines, second_operand_lines, (((1,), (1,)),...  18 us
    ppermute x7, starting transfers between devices, passed_along(): return lax.ppermute(value, axis, pairs)  16.9 us
    dot_general x4, matrix products, on_device(): jnp.dot(coupling_tile, lines_each_cluster, preferred_element_type=jnp.flo...  14.2 us
    dot_general x1, matrix products, column_term(): lax.dot_general(all_tiles, all_rows, (((0,), (0,)), ((), ())), preferred_...  10.5 us
  transfers between devices with their start and end apart: 9, of which 8 were waited for; matrix products, arithmetic and copies ran while one was open for 7% of the time, Pallas kernels for 0%

commit v1 on v0

v1 whole, which is shorter than its diff:
```python
import functools
import math

import jax
import jax.numpy as jnp
from jax import lax
from jax.experimental import pallas as pl
from jax.experimental.pallas import tpu as pltpu
from jax.sharding import Mesh
from jax.sharding import PartitionSpec as P

FINE_AXES = ("y_lo", "core", "x", "z", "y_hi")
FINE_SIZES = (2, 2, 4, 4, 2)
RING = 4
SIDE = 8
VMEM_BYTES = 48 * 1024 * 1024


def along(value, axis, steps):
    return lax.ppermute(value, axis, [(k, (k + steps) % RING) for k in range(RING)])


def other_core(value):
    return lax.ppermute(value, "core", [(0, 1), (1, 0)])


def y_partner(value, wrapped):
    place = lambda y: (y % 2) * 2 + y // 2
    pairs = []
    for y in range(RING):
        if wrapped:
            mate = (y + 1) % RING if y % 2 else (y - 1) % RING
        else:
            mate = y ^ 1
        pairs.append((place(y), place(mate)))
    return lax.ppermute(value, ("y_lo", "y_hi"), pairs)


def gathered(own, axis, wrapped):
    partner = y_partner(own, wrapped)
    left_own = along(own, axis, 1)
    right_own = along(own, axis, -1)
    left_partner = along(partner, axis, 1)
    right_partner = along(partner, axis, -1)
    far_own = along(left_own, axis, 1)
    far_partner = along(right_partner, axis, -1)
    return [own, partner, left_own, left_partner, right_own, right_partner, far_own, far_partner]


def plus(*terms):
    total = terms[0].astype(jnp.float32)
    for term in terms[1:]:
        total = total + term.astype(jnp.float32)
    return total


def scattered(parts, axis, wrapped):
    own, partner, left_own, left_partner, right_own, right_partner, far_own, far_partner = parts
    half = jnp.bfloat16
    from_far_partner = along(far_partner, axis, 1)
    from_far_own = along(far_own, axis, -1)
    partner_a = along(left_partner, axis, -1)
    partner_b = along(plus(right_partner, from_far_partner).astype(half), axis, 1)
    own_a = along(right_own, axis, 1)
    own_b = along(plus(left_own, from_far_own).astype(half), axis, -1)
    from_partner = y_partner(plus(partner, partner_a, partner_b).astype(half), wrapped)
    return plus(own, own_a, own_b, from_partner)


def unit_rows(embedding):
    values = embedding.astype(jnp.float32)
    row_scale = lax.rsqrt(jnp.mean(values * values, axis=1, keepdims=True) + 1e-06) / math.sqrt(
        values.shape[1]
    )
    return (values * row_scale, row_scale)


def unit_grad(unit_vals, row_scale, upstream_grad):
    return row_scale * (
        upstream_grad - unit_vals * jnp.sum(unit_vals * upstream_grad, axis=1, keepdims=True)
    )


def coupling_kernel(diagonal, rows, *refs):
    affine = refs[0]
    image_refs = refs[1 : 1 + SIDE]
    text_refs = refs[1 + SIDE : 1 + 2 * SIDE]
    coupling_ref = refs[1 + 2 * SIDE]
    part_refs = refs[2 + 2 * SIDE : 2 + 3 * SIDE]
    images, texts, image_sems, text_sems = refs[2 + 3 * SIDE :]
    copies = []
    for k in range(SIDE):
        copies.append(
            pltpu.make_async_copy(text_refs[k], texts.at[pl.ds(k * rows, rows)], text_sems.at[k])
        )
        copies.append(
            pltpu.make_async_copy(image_refs[k], images.at[pl.ds(k * rows, rows)], image_sems.at[k])
        )
    for copy in copies:
        copy.start()
    for copy in copies:
        copy.wait()
    slope = affine[0]
    shift = affine[1]
    block = 2 * rows
    for k in range(SIDE // 2):
        here = images[pl.ds(k * block, block), :]
        energies = lax.dot_general(
            here, texts[...], (((1,), (1,)), ((), ())), preferred_element_type=jnp.float32
        )
        coupling = 0.5 * jnp.tanh(slope * energies + shift) + 0.5
        if diagonal and k == 0:
            row = lax.broadcasted_iota(jnp.int32, coupling.shape, 0)
            column = lax.broadcasted_iota(jnp.int32, coupling.shape, 1)
            coupling = coupling - jnp.where((row == column) & (row < rows), 1.0, 0.0)
        coupling = coupling.astype(jnp.bfloat16)
        coupling_ref[pl.ds(k * block, block), :] = coupling
        part = jnp.dot(coupling, texts[...], preferred_element_type=jnp.float32)
        part = part.astype(jnp.bfloat16)
        part_refs[2 * k][...] = part[:rows]
        part_refs[2 * k + 1][...] = part[rows:]


def coupled(affine, image_shards, text_shards, diagonal):
    rows, width = image_shards[0].shape
    whole = pl.BlockSpec(memory_space=pltpu.VMEM)
    anywhere = pl.BlockSpec(memory_space=pl.ANY)
    shard = jax.ShapeDtypeStruct((rows, width), jnp.bfloat16)
    out = pl.pallas_call(
        functools.partial(coupling_kernel, diagonal, rows),
        out_shape=[jax.ShapeDtypeStruct((SIDE * rows, SIDE * rows), jnp.bfloat16)] + [shard] * SIDE,
        in_specs=[pl.BlockSpec(memory_space=pltpu.SMEM)] + [anywhere] * (2 * SIDE),
        out_specs=[whole] * (1 + SIDE),
        scratch_shapes=[
            pltpu.VMEM((SIDE * rows, width), jnp.bfloat16),
            pltpu.VMEM((SIDE * rows, width), jnp.bfloat16),
            pltpu.SemaphoreType.DMA((SIDE,)),
            pltpu.SemaphoreType.DMA((SIDE,)),
        ],
        cost_estimate=pl.CostEstimate(
            flops=4 * (SIDE * rows) ** 2 * width,
            bytes_accessed=6 * SIDE * rows * width + 2 * (SIDE * rows) ** 2,
            transcendentals=(SIDE * rows) ** 2,
        ),
        compiler_params=pltpu.CompilerParams(vmem_limit_bytes=VMEM_BYTES),
    )(affine, *image_shards, *text_shards)
    return out[0], out[1:]


def text_kernel(rows, *refs):
    couplings = refs[:2]
    image_refs = refs[2 : 2 + 2 * SIDE]
    part_refs = refs[2 + 2 * SIDE : 2 + 3 * SIDE]
    images, image_sems = refs[2 + 3 * SIDE :]
    copies = [
        pltpu.make_async_copy(image_refs[k], images.at[pl.ds(k * rows, rows)], image_sems.at[k])
        for k in range(2 * SIDE)
    ]
    for copy in copies:
        copy.start()
    for copy in copies:
        copy.wait()
    block = 2 * rows
    for k in range(SIDE // 2 - 1, -1, -1):
        part = None
        for which in range(2):
            term = lax.dot_general(
                couplings[which][:, pl.ds(k * block, block)],
                images[pl.ds(which * SIDE * rows, SIDE * rows), :],
                (((0,), (0,)), ((), ())),
                preferred_element_type=jnp.float32,
            )
            part = term if part is None else part + term
        part = part.astype(jnp.bfloat16)
        part_refs[2 * k][...] = part[:rows]
        part_refs[2 * k + 1][...] = part[rows:]


def text_parts(couplings, image_shards):
    rows, width = image_shards[0].shape
    whole = pl.BlockSpec(memory_space=pltpu.VMEM)
    anywhere = pl.BlockSpec(memory_space=pl.ANY)
    shard = jax.ShapeDtypeStruct((rows, width), jnp.bfloat16)
    return pl.pallas_call(
        functools.partial(text_kernel, rows),
        out_shape=[shard] * SIDE,
        in_specs=[whole] * 2 + [anywhere] * (2 * SIDE),
        out_specs=[whole] * SIDE,
        scratch_shapes=[
            pltpu.VMEM((2 * SIDE * rows, width), jnp.bfloat16),
            pltpu.SemaphoreType.DMA((2 * SIDE,)),
        ],
        cost_estimate=pl.CostEstimate(
            flops=4 * (SIDE * rows) ** 2 * width,
            bytes_accessed=6 * SIDE * rows * width + 4 * (SIDE * rows) ** 2,
            transcendentals=0,
        ),
        compiler_params=pltpu.CompilerParams(vmem_limit_bytes=VMEM_BYTES),
    )(*couplings, *image_shards)


def on_device(
    picture_vectors_raw, caption_vectors_raw, logit_multiplier, offset_term, incoming_adjoint
):
    image_unit, image_scale = unit_rows(picture_vectors_raw)
    text_unit, text_scale = unit_rows(caption_vectors_raw)
    pairs = picture_vectors_raw.shape[0] * math.prod(FINE_SIZES)
    derivative_multiplier = incoming_adjoint[0] * logit_multiplier[0] / pairs
    affine = jnp.concatenate([0.5 * logit_multiplier, 0.5 * offset_term])
    images = gathered(image_unit.astype(jnp.bfloat16), "x", False)
    texts = gathered(text_unit.astype(jnp.bfloat16), "z", True)
    images_there = [other_core(shard) for shard in images]
    coupling_there, parts_there = coupled(affine, images_there, texts, False)
    coupling_here, parts_here = coupled(affine, images, texts, True)
    parts_back = [other_core(part) for part in parts_there]
    image_sums = [plus(a, b).astype(jnp.bfloat16) for a, b in zip(parts_here, parts_back)]
    text_sums = text_parts([coupling_there, coupling_here], images_there + images)
    image_total = scattered(image_sums, "x", False)
    text_total = scattered(text_sums, "z", True)
    image_grad = unit_grad(image_unit, image_scale, derivative_multiplier * image_total)
    text_grad = unit_grad(text_unit, text_scale, derivative_multiplier * text_total)
    return (image_grad, text_grad)


def solution(mesh):
    fine = Mesh(mesh.devices.reshape(FINE_SIZES), FINE_AXES)
    rows = P(FINE_AXES, None)
    return jax.shard_map(
        on_device,
        mesh=fine,
        in_specs=(rows, rows, P(), P(), P()),
        out_specs=(rows, rows),
        check_vma=False,
    )
```

time: 447 us -> 141 us (0.32)
  the two profiles are of different devices: /device:TPU:1 before, /device:TPU:2 now
where the time goes in v1:
time: 141 us; the launch traced here: 140 us
  waiting for transfers between devices  59.7 us (42%)
  starting transfers between devices  41.7 us (30%)
  Pallas kernels  27.7 us (20%)
  other arithmetic  8.29 us (6%)
  between operations  2.86 us (2%)
    ppermute x24, waiting for transfers between devices, along(): lax.ppermute(value, axis, [(k, (k + steps) % RING) for k in range(RING)])  52.8 us
    ppermute x24, starting transfers between devices, along(): lax.ppermute(value, axis, [(k, (k + steps) % RING) for k in range(RING)])  30.5 us
    pallas_call x2, Pallas kernels, coupled(): pl.pallas_call(functools.partial(coupling_kernel, diagonal, rows), out_sh...  17.7 us
    pallas_call x1, Pallas kernels, text_parts(): pl.pallas_call(functools.partial(text_kernel, rows), out_shape=[shard] *...  9.97 us
    ppermute x4, starting transfers between devices, y_partner(): return lax.ppermute(value, ('y_lo', 'y_hi'), pairs)  7.6 us
    ppermute x4, waiting for transfers between devices, y_partner(): return lax.ppermute(value, ('y_lo', 'y_hi'), pairs)  5.44 us
    ppermute x16, starting transfers between devices, other_core(): return lax.ppermute(value, 'core', [(0, 1), (1, 0)])  3.6 us
  transfers between devices with their start and end apart: 44, of which 20 were waited for; matrix products, arithmetic and copies ran while one was open for 3% of the time, Pallas kernels for 13%

profile of v1, /device:TPU:2, one launch (start us, length us, event | category | flops | bytes accessed | tf_op | source)
XLA Modules:
  0.0 140.2 jit_solution(12562959678291510169)
XLA Ops:
  0.6 1.1 fusion.13
  1.7 1.1 fusion.2.refs_9_
  2.8 4.1 %collective-permute-start.10 = (bf16[128,1152]{1,0:T(8,128)(2,1)S(1)}, bf16[128,1152]{1,0:T(8,128)(2,1)S(1)}, u32[]{:S(2)}, u32[]{:S(2)}) collective-permute-start(bf16[128,1152]{1,0:T(8,128)(2,1)S(1)} %fusion.2.refs_9_), channel_id=1, source_target_pairs={{0,6},{2,0},{4,2},{6,4},{1,7},{3,1},{5,3},{7,5},{8,14},{10,8},{12,... | collective-permute-start | bytes 884744 | tf_op jit(solution)/shard_map/ppermute | solution.py:20
  6.9 3.0 %collective-permute-start.7 = (bf16[128,1152]{1,0:T(8,128)(2,1)S(1)}, bf16[128,1152]{1,0:T(8,128)(2,1)S(1)}, u32[]{:S(2)}, u32[]{:S(2)}) collective-permute-start(bf16[128,1152]{1,0:T(8,128)(2,1)S(1)} %fusion.2.refs_9_), channel_id=1, source_target_pairs={{0,65},{64,1},{1,64},{65,0},{2,67},{66,3},{3,66},{67,2},{4,69},{68... | collective-permute-start | bytes 884744 | tf_op jit(solution)/shard_map/ppermute | solution.py:36
  10.0 1.1 fusion.9
  11.1 1.1 fusion.5.refs_1_.refs_10_
  12.2 0.6 collective-permute-start.3
  13.2 1.5 %collective-permute-start.1 = (bf16[128,1152]{1,0:T(8,128)(2,1)S(1)}, bf16[128,1152]{1,0:T(8,128)(2,1)S(1)}, u32[]{:S(2)}, u32[]{:S(2)}) collective-permute-start(bf16[128,1152]{1,0:T(8,128)(2,1)S(1)} %fusion.5.refs_1_.refs_10_), channel_id=1, source_target_pairs={{0,8},{8,16},{16,24},{24,0},{1,9},{9,17},{17,25},{25,1},{2,10},{10... | collective-permute-start | bytes 884744 | tf_op jit(solution)/shard_map/ppermute | solution.py:20
  14.7 1.9 %collective-permute-done.8.refs_11_ = bf16[128,1152]{1,0:T(8,128)(2,1)S(1)} collective-permute-done((bf16[128,1152]{1,0:T(8,128)(2,1)S(1)}, bf16[128,1152]{1,0:T(8,128)(2,1)S(1)}, u32[]{:S(2)}, u32[]{:S(2)}) %collective-permute-start.8) | collective-permute-done | bytes 294944 | tf_op jit(solution)/shard_map/ppermute | solution.py:20
  16.6 1.6 %collective-permute-start = (bf16[128,1152]{1,0:T(8,128)(2,1)S(1)}, bf16[128,1152]{1,0:T(8,128)(2,1)S(1)}, u32[]{:S(2)}, u32[]{:S(2)}) collective-permute-start(bf16[128,1152]{1,0:T(8,128)(2,1)S(1)} %fusion.5.refs_1_.refs_10_), channel_id=1, source_target_pairs={{0,64},{64,0},{1,65},{65,1},{2,66},{66,2},{3,67},{67,3},{4,68},{68... | collective-permute-start | bytes 884744 | tf_op jit(solution)/shard_map/ppermute | solution.py:36
  18.2 3.2 %collective-permute-start.11 = (bf16[128,1152]{1,0:T(8,128)(2,1)S(1)}, bf16[128,1152]{1,0:T(8,128)(2,1)S(1)}, u32[]{:S(2)}, u32[]{:S(2)}) collective-permute-start(bf16[128,1152]{1,0:T(8,128)(2,1)S(1)} %collective-permute-done.7.refs_10_), channel_id=1, source_target_pairs={{0,6},{2,0},{4,2},{6,4},{1,7},{3,1},{5,3},{7,5},{8,14},{10,8},{12,... | collective-permute-start | bytes 884744 | tf_op jit(solution)/shard_map/ppermute | solution.py:20
  21.7 1.3 collective-permute-done.1.refs_3_.refs_12_
  23.0 1.2 collective-permute-done.refs_2_.refs_11_
  24.2 1.7 %collective-permute-start.4 = (bf16[128,1152]{1,0:T(8,128)(2,1)S(1)}, bf16[128,1152]{1,0:T(8,128)(2,1)S(1)}, u32[]{:S(2)}, u32[]{:S(2)}) collective-permute-start(bf16[128,1152]{1,0:T(8,128)(2,1)S(1)} %collective-permute-done.refs_2_.refs_11_), channel_id=1, source_target_pairs={{0,24},{8,0},{16,8},{24,16},{1,25},{9,1},{17,9},{25,17},{2,26},{10... | collective-permute-start | bytes 884744 | tf_op jit(solution)/shard_map/ppermute | solution.py:20
  25.9 2.0 %collective-permute-done.12.refs_15_ = bf16[128,1152]{1,0:T(8,128)(2,1)S(1)} collective-permute-done((bf16[128,1152]{1,0:T(8,128)(2,1)S(1)}, bf16[128,1152]{1,0:T(8,128)(2,1)S(1)}, u32[]{:S(2)}, u32[]{:S(2)}) %collective-permute-start.12) | collective-permute-done | bytes 294944 | tf_op jit(solution)/shard_map/ppermute | solution.py:20
  27.9 1.6 %collective-permute-start.5 = (bf16[128,1152]{1,0:T(8,128)(2,1)S(1)}, bf16[128,1152]{1,0:T(8,128)(2,1)S(1)}, u32[]{:S(2)}, u32[]{:S(2)}) collective-permute-start(bf16[128,1152]{1,0:T(8,128)(2,1)S(1)} %collective-permute-done.1.refs_3_.refs_12_), channel_id=1, source_target_pairs={{0,8},{8,16},{16,24},{24,0},{1,9},{9,17},{17,25},{25,1},{2,10},{10... | collective-permute-start | bytes 884744 | tf_op jit(solution)/shard_map/ppermute | solution.py:20
  29.5 3.5 %collective-permute-done.9.refs_12_ = bf16[128,1152]{1,0:T(8,128)(2,1)S(1)} collective-permute-done((bf16[128,1152]{1,0:T(8,128)(2,1)S(1)}, bf16[128,1152]{1,0:T(8,128)(2,1)S(1)}, u32[]{:S(2)}, u32[]{:S(2)}) %collective-permute-start.9) | collective-permute-done | bytes 294944 | tf_op jit(solution)/shard_map/ppermute | solution.py:20
  33.0 1.5 %collective-permute-start.2 = (bf16[128,1152]{1,0:T(8,128)(2,1)S(1)}, bf16[128,1152]{1,0:T(8,128)(2,1)S(1)}, u32[]{:S(2)}, u32[]{:S(2)}) collective-permute-start(bf16[128,1152]{1,0:T(8,128)(2,1)S(1)} %collective-permute-done.refs_2_.refs_11_), channel_id=1, source_target_pairs={{0,8},{8,16},{16,24},{24,0},{1,9},{9,17},{17,25},{25,1},{2,10},{10... | collective-permute-start | bytes 884744 | tf_op jit(solution)/shard_map/ppermute | solution.py:20
  34.5 0.5 collective-permute-start.13
  35.0 0.7 collective-permute-start.6
  38.2 5.4 %collective-permute-done.2.refs_4_.refs_13_ = bf16[128,1152]{1,0:T(8,128)(2,1)S(1)} collective-permute-done((bf16[128,1152]{1,0:T(8,128)(2,1)S(1)}, bf16[128,1152]{1,0:T(8,128)(2,1)S(1)}, u32[]{:S(2)}, u32[]{:S(2)}) %collective-permute-start.2) | collective-permute-done | bytes 294944 | tf_op jit(solution)/shard_map/ppermute | solution.py:20
  43.7 0.5 collective-permute-start.17
  44.5 8.8 %shard_map.68 = (bf16[1024,1024]{1,0:T(8,128)(2,1)}, bf16[128,1152]{1,0:T(8,128)(2,1)S(1)}, bf16[128,1152]{1,0:T(8,128)(2,1)S(1)}, bf16[128,1152]{1,0:T(8,128)(2...) custom-call(f32[2]{0:T(128)S(1)} %pad_maximum_fusion.refs_0_, ...), custom_call_target="tpu_custom_call" | custom-call | flops 4831838208 | bytes 9175040 | tf_op jit(solution)/shard_map/pallas_call | solution.py:129
  53.4 8.9 %shard_map.69 = (bf16[1024,1024]{1,0:T(8,128)(2,1)}, bf16[128,1152]{1,0:T(8,128)(2,1)S(1)}, bf16[128,1152]{1,0:T(8,128)(2,1)S(1)}, bf16[128,1152]{1,0:T(8,128)(2...) custom-call(f32[2]{0:T(128)S(1)} %pad_maximum_fusion.refs_0_, ...), custom_call_target="tpu_custom_call" | custom-call | flops 4831838208 | bytes 9175040 | tf_op jit(solution)/shard_map/pallas_call | solution.py:129
  62.3 0.5 collective-permute-start.22
  63.8 10.0 %shard_map.70 = (bf16[128,1152]{1,0:T(8,128)(2,1)S(1)}, bf16[128,1152]{1,0:T(8,128)(2,1)S(1)}, bf16[128,1152]{1,0:T(8,128)(2,1)S(1)}, bf16[128,1152]{1,0:T(8,128...) custom-call(bf16[1024,1024]{1,0:T(8,128)(2,1)} %get-tuple-element.44, ...), custom_call_target="tpu_custom_call" | custom-call | flops 4831838208 | bytes 11272192 | tf_op jit(solution)/shard_map/pallas_call | solution.py:184
  74.1 1.4 %collective-permute-done.30 = bf16[128,1152]{1,0:T(8,128)(2,1)S(1)} collective-permute-done((bf16[128,1152]{1,0:T(8,128)(2,1)S(1)}, bf16[128,1152]{1,0:T(8,128)(2,1)S(1)}, u32[]{:S(2)}, u32[]{:S(2)}) %collective-permute-start.30) | collective-permute-done | bytes 294944 | tf_op jit(solution)/shard_map/ppermute | solution.py:24
  76.2 1.3 collective-permute-start.38
  77.6 7.7 %collective-permute-done.38 = bf16[128,1152]{1,0:T(8,128)(2,1)S(1)} collective-permute-done((bf16[128,1152]{1,0:T(8,128)(2,1)S(1)}, bf16[128,1152]{1,0:T(8,128)(2,1)S(1)}, u32[]{:S(2)}, u32[]{:S(2)}) %collective-permute-start.38) | collective-permute-done | bytes 294944 | tf_op jit(solution)/shard_map/ppermute | solution.py:20
  85.4 9.4 %collective-permute-done.41 = bf16[128,1152]{1,0:T(8,128)(2,1)S(1)} collective-permute-done((bf16[128,1152]{1,0:T(8,128)(2,1)S(1)}, bf16[128,1152]{1,0:T(8,128)(2,1)S(1)}, u32[]{:S(2)}, u32[]{:S(2)}) %collective-permute-start.41) | collective-permute-done | bytes 294944 | tf_op jit(solution)/shard_map/ppermute | solution.py:20
  94.8 2.5 %collective-permute-start.27 = (bf16[128,1152]{1,0:T(8,128)(2,1)S(1)}, bf16[128,1152]{1,0:T(8,128)(2,1)S(1)}, u32[]{:S(2)}, u32[]{:S(2)}) collective-permute-start(bf16[128,1152]{1,0:T(8,128)(2,1)S(1)} %add_convert_fusion.10), channel_id=1, source_target_pairs={{0,24},{8,0},{16,8},{24,16},{1,25},{9,1},{17,9},{25,17},{2,26},{10... | collective-permute-start | bytes 884744 | tf_op jit(solution)/shard_map/ppermute | solution.py:20
  97.4 4.9 %collective-permute-done.27 = bf16[128,1152]{1,0:T(8,128)(2,1)S(1)} collective-permute-done((bf16[128,1152]{1,0:T(8,128)(2,1)S(1)}, bf16[128,1152]{1,0:T(8,128)(2,1)S(1)}, u32[]{:S(2)}, u32[]{:S(2)}) %collective-permute-start.27) | collective-permute-done | bytes 294944 | tf_op jit(solution)/shard_map/ppermute | solution.py:20
  102.4 1.2 collective-permute-start.34
  103.7 1.3 collective-permute-start.40
  105.0 4.8 %collective-permute-done.34 = bf16[128,1152]{1,0:T(8,128)(2,1)S(1)} collective-permute-done((bf16[128,1152]{1,0:T(8,128)(2,1)S(1)}, bf16[128,1152]{1,0:T(8,128)(2,1)S(1)}, u32[]{:S(2)}, u32[]{:S(2)}) %collective-permute-start.34) | collective-permute-done | bytes 294944 | tf_op jit(solution)/shard_map/ppermute | solution.py:20
  109.9 0.6 collective-permute-done.40
  110.5 2.5 %collective-permute-start.31 = (bf16[128,1152]{1,0:T(8,128)(2,1)S(1)}, bf16[128,1152]{1,0:T(8,128)(2,1)S(1)}, u32[]{:S(2)}, u32[]{:S(2)}) collective-permute-start(bf16[128,1152]{1,0:T(8,128)(2,1)S(1)} %add_convert_fusion.7), channel_id=1, source_target_pairs={{0,24},{8,0},{16,8},{24,16},{1,25},{9,1},{17,9},{25,17},{2,26},{10... | collective-permute-start | bytes 884744 | tf_op jit(solution)/shard_map/ppermute | solution.py:20
  113.0 4.7 %collective-permute-done.42 = bf16[128,1152]{1,0:T(8,128)(2,1)S(1)} collective-permute-done((bf16[128,1152]{1,0:T(8,128)(2,1)S(1)}, bf16[128,1152]{1,0:T(8,128)(2,1)S(1)}, u32[]{:S(2)}, u32[]{:S(2)}) %collective-permute-start.42) | collective-permute-done | bytes 294944 | tf_op jit(solution)/shard_map/ppermute | solution.py:20
  117.7 0.5 collective-permute-start.35
  118.4 2.3 %collective-permute-start.24 = (bf16[128,1152]{1,0:T(8,128)(2,1)S(1)}, bf16[128,1152]{1,0:T(8,128)(2,1)S(1)}, u32[]{:S(2)}, u32[]{:S(2)}) collective-permute-start(bf16[128,1152]{1,0:T(8,128)(2,1)S(1)} %add_convert_fusion.12), channel_id=1, source_target_pairs={{0,8},{8,16},{16,24},{24,0},{1,9},{9,17},{17,25},{25,1},{2,10},{10... | collective-permute-start | bytes 884744 | tf_op jit(solution)/shard_map/ppermute | solution.py:20
  121.1 5.4 %collective-permute-done.35 = bf16[128,1152]{1,0:T(8,128)(2,1)S(1)} collective-permute-done((bf16[128,1152]{1,0:T(8,128)(2,1)S(1)}, bf16[128,1152]{1,0:T(8,128)(2,1)S(1)}, u32[]{:S(2)}, u32[]{:S(2)}) %collective-permute-start.35) | collective-permute-done | bytes 294944 | tf_op jit(solution)/shard_map/ppermute | solution.py:20
  126.5 2.3 %collective-permute-start.43 = (bf16[128,1152]{1,0:T(8,128)(2,1)S(1)}, bf16[128,1152]{1,0:T(8,128)(2,1)S(1)}, u32[]{:S(2)}, u32[]{:S(2)}) collective-permute-start(bf16[128,1152]{1,0:T(8,128)(2,1)S(1)} %add_convert_fusion), channel_id=1, source_target_pairs={{0,65},{64,1},{1,64},{65,0},{2,67},{66,3},{3,66},{67,2},{4,69},{68... | collective-permute-start | bytes 884744 | tf_op jit(solution)/shard_map/ppermute | solution.py:36
  129.0 3.0 %collective-permute-start.28 = (bf16[128,1152]{1,0:T(8,128)(2,1)S(1)}, bf16[128,1152]{1,0:T(8,128)(2,1)S(1)}, u32[]{:S(2)}, u32[]{:S(2)}) collective-permute-start(bf16[128,1152]{1,0:T(8,128)(2,1)S(1)} %add_convert_fusion.9), channel_id=1, source_target_pairs={{0,24},{8,0},{16,8},{24,16},{1,25},{9,1},{17,9},{25,17},{2,26},{10... | collective-permute-start | bytes 884744 | tf_op jit(solution)/shard_map/ppermute | solution.py:20
  132.0 0.7 collective-permute-start.36
  132.7 1.7 %collective-permute-done.43 = bf16[128,1152]{1,0:T(8,128)(2,1)S(1)} collective-permute-done((bf16[128,1152]{1,0:T(8,128)(2,1)S(1)}, bf16[128,1152]{1,0:T(8,128)(2,1)S(1)}, u32[]{:S(2)}, u32[]{:S(2)}) %collective-permute-start.43) | collective-permute-done | bytes 294944 | tf_op jit(solution)/shard_map/ppermute | solution.py:36
  134.8 1.1 fusion.12
  136.3 2.5 %collective-permute-done.36 = bf16[128,1152]{1,0:T(8,128)(2,1)S(1)} collective-permute-done((bf16[128,1152]{1,0:T(8,128)(2,1)S(1)}, bf16[128,1152]{1,0:T(8,128)(2,1)S(1)}, u32[]{:S(2)}, u32[]{:S(2)}) %collective-permute-start.36) | collective-permute-done | bytes 294944 | tf_op jit(solution)/shard_map/ppermute | solution.py:36
  139.1 1.1 fusion.8
  (80 shorter events, 5.9 us)
Async XLA Ops:
  2.8 10.4 %collective-permute-start.10 = (bf16[128,1152]{1,0:T(8,128)(2,1)S(1)}, bf16[128,1152]{1,0:T(8,128)(2,1)S(1)}, u32[]{:S(2)}, u32[]{:S(2)}) collective-permute-start(bf16[128,1152]{1,0:T(8,128)(2,1)S(1)} %fusion.2.refs_9_), channel_id=1, source_target_pairs={{0,6},{2,0},{4,2},{6,4},{1,7},{3,1},{5,3},{7,5},{8,14},{10,8},{12,... | collective-permute-start | bytes 884744 | tf_op jit(solution)/shard_map/ppermute | solution.py:20
  6.9 9.7 %collective-permute-start.8 = (bf16[128,1152]{1,0:T(8,128)(2,1)S(1)}, bf16[128,1152]{1,0:T(8,128)(2,1)S(1)}, u32[]{:S(2)}, u32[]{:S(2)}) collective-permute-start(bf16[128,1152]{1,0:T(8,128)(2,1)S(1)} %fusion.2.refs_9_), channel_id=1, source_target_pairs={{0,2},{2,4},{4,6},{6,0},{1,3},{3,5},{5,7},{7,1},{8,10},{10,12},{12... | collective-permute-start | bytes 884744 | tf_op jit(solution)/shard_map/ppermute | solution.py:20
  6.9 11.3 %collective-permute-start.7 = (bf16[128,1152]{1,0:T(8,128)(2,1)S(1)}, bf16[128,1152]{1,0:T(8,128)(2,1)S(1)}, u32[]{:S(2)}, u32[]{:S(2)}) collective-permute-start(bf16[128,1152]{1,0:T(8,128)(2,1)S(1)} %fusion.2.refs_9_), channel_id=1, source_target_pairs={{0,65},{64,1},{1,64},{65,0},{2,67},{66,3},{3,66},{67,2},{4,69},{68... | collective-permute-start | bytes 884744 | tf_op jit(solution)/shard_map/ppermute | solution.py:36
  12.2 6.0 %collective-permute-start.14 = (bf16[128,1152]{1,0:T(8,128)(2,1)S(1)}, bf16[128,1152]{1,0:T(8,128)(2,1)S(1)}, u32[]{:S(2)}, u32[]{:S(2)}) collective-permute-start(bf16[128,1152]{1,0:T(8,128)(2,1)S(1)} %fusion.5.refs_1_.refs_10_), channel_id=1, source_target_pairs={{0,32},{32,0},{1,33},{33,1},{2,34},{34,2},{3,35},{35,3},{4,36},{36... | collective-permute-start | bytes 884744 | tf_op jit(solution)/shard_map/ppermute | solution.py:24
  12.2 9.4 %collective-permute-start.3 = (bf16[128,1152]{1,0:T(8,128)(2,1)S(1)}, bf16[128,1152]{1,0:T(8,128)(2,1)S(1)}, u32[]{:S(2)}, u32[]{:S(2)}) collective-permute-start(bf16[128,1152]{1,0:T(8,128)(2,1)S(1)} %fusion.5.refs_1_.refs_10_), channel_id=1, source_target_pairs={{0,24},{8,0},{16,8},{24,16},{1,25},{9,1},{17,9},{25,17},{2,26},{10... | collective-permute-start | bytes 884744 | tf_op jit(solution)/shard_map/ppermute | solution.py:20
  13.2 9.7 %collective-permute-start.1 = (bf16[128,1152]{1,0:T(8,128)(2,1)S(1)}, bf16[128,1152]{1,0:T(8,128)(2,1)S(1)}, u32[]{:S(2)}, u32[]{:S(2)}) collective-permute-start(bf16[128,1152]{1,0:T(8,128)(2,1)S(1)} %fusion.5.refs_1_.refs_10_), channel_id=1, source_target_pairs={{0,8},{8,16},{16,24},{24,0},{1,9},{9,17},{17,25},{25,1},{2,10},{10... | collective-permute-start | bytes 884744 | tf_op jit(solution)/shard_map/ppermute | solution.py:20
  16.6 7.6 %collective-permute-start = (bf16[128,1152]{1,0:T(8,128)(2,1)S(1)}, bf16[128,1152]{1,0:T(8,128)(2,1)S(1)}, u32[]{:S(2)}, u32[]{:S(2)}) collective-permute-start(bf16[128,1152]{1,0:T(8,128)(2,1)S(1)} %fusion.5.refs_1_.refs_10_), channel_id=1, source_target_pairs={{0,64},{64,0},{1,65},{65,1},{2,66},{66,2},{3,67},{67,3},{4,68},{68... | collective-permute-start | bytes 884744 | tf_op jit(solution)/shard_map/ppermute | solution.py:36
  18.2 9.7 %collective-permute-start.12 = (bf16[128,1152]{1,0:T(8,128)(2,1)S(1)}, bf16[128,1152]{1,0:T(8,128)(2,1)S(1)}, u32[]{:S(2)}, u32[]{:S(2)}) collective-permute-start(bf16[128,1152]{1,0:T(8,128)(2,1)S(1)} %collective-permute-done.8.refs_11_), channel_id=1, source_target_pairs={{0,2},{2,4},{4,6},{6,0},{1,3},{3,5},{5,7},{7,1},{8,10},{10,12},{12... | collective-permute-start | bytes 884744 | tf_op jit(solution)/shard_map/ppermute | solution.py:20
  18.2 9.7 %collective-permute-start.11 = (bf16[128,1152]{1,0:T(8,128)(2,1)S(1)}, bf16[128,1152]{1,0:T(8,128)(2,1)S(1)}, u32[]{:S(2)}, u32[]{:S(2)}) collective-permute-start(bf16[128,1152]{1,0:T(8,128)(2,1)S(1)} %collective-permute-done.7.refs_10_), channel_id=1, source_target_pairs={{0,6},{2,0},{4,2},{6,4},{1,7},{3,1},{5,3},{7,5},{8,14},{10,8},{12,... | collective-permute-start | bytes 884744 | tf_op jit(solution)/shard_map/ppermute | solution.py:20
  21.7 11.3 %collective-permute-start.9 = (bf16[128,1152]{1,0:T(8,128)(2,1)S(1)}, bf16[128,1152]{1,0:T(8,128)(2,1)S(1)}, u32[]{:S(2)}, u32[]{:S(2)}) collective-permute-start(bf16[128,1152]{1,0:T(8,128)(2,1)S(1)} %collective-permute-done.7.refs_10_), channel_id=1, source_target_pairs={{0,2},{2,4},{4,6},{6,0},{1,3},{3,5},{5,7},{7,1},{8,10},{10,12},{12... | collective-permute-start | bytes 884744 | tf_op jit(solution)/shard_map/ppermute | solution.py:20
  22.9 11.6 %collective-permute-start.18 = (bf16[128,1152]{1,0:T(8,128)(2,1)S(1)}, bf16[128,1152]{1,0:T(8,128)(2,1)S(1)}, u32[]{:S(2)}, u32[]{:S(2)}) collective-permute-start(bf16[128,1152]{1,0:T(8,128)(2,1)S(1)} %collective-permute-done.3.refs_5_.refs_14_), channel_id=1, source_target_pairs={{0,32},{32,0},{1,33},{33,1},{2,34},{34,2},{3,35},{35,3},{4,36},{36... | collective-permute-start | bytes 884744 | tf_op jit(solution)/shard_map/ppermute | solution.py:24
  24.2 10.8 %collective-permute-start.4 = (bf16[128,1152]{1,0:T(8,128)(2,1)S(1)}, bf16[128,1152]{1,0:T(8,128)(2,1)S(1)}, u32[]{:S(2)}, u32[]{:S(2)}) collective-permute-start(bf16[128,1152]{1,0:T(8,128)(2,1)S(1)} %collective-permute-done.refs_2_.refs_11_), channel_id=1, source_target_pairs={{0,24},{8,0},{16,8},{24,16},{1,25},{9,1},{17,9},{25,17},{2,26},{10... | collective-permute-start | bytes 884744 | tf_op jit(solution)/shard_map/ppermute | solution.py:20
  27.9 16.6 %copy-start.5 = (bf16[128,1152]{1,0:T(8,128)(2,1)}, bf16[128,1152]{1,0:T(8,128)(2,1)S(1)}, u32[]{:S(2)}) copy-start(bf16[128,1152]{1,0:T(8,128)(2,1)S(1)} %collective-permute-done.12.refs_15_) | copy-start | bytes 884740
  27.9 9.8 %collective-permute-start.16 = (bf16[128,1152]{1,0:T(8,128)(2,1)S(1)}, bf16[128,1152]{1,0:T(8,128)(2,1)S(1)}, u32[]{:S(2)}, u32[]{:S(2)}) collective-permute-start(bf16[128,1152]{1,0:T(8,128)(2,1)S(1)} %collective-permute-done.1.refs_3_.refs_12_), channel_id=1, source_target_pairs={{0,32},{32,0},{1,33},{33,1},{2,34},{34,2},{3,35},{35,3},{4,36},{36... | collective-permute-start | bytes 884744 | tf_op jit(solution)/shard_map/ppermute | solution.py:24
  27.9 16.6 %copy-start.6 = (bf16[128,1152]{1,0:T(8,128)(2,1)}, bf16[128,1152]{1,0:T(8,128)(2,1)S(1)}, u32[]{:S(2)}) copy-start(bf16[128,1152]{1,0:T(8,128)(2,1)S(1)} %collective-permute-done.11.refs_14_) | copy-start | bytes 884740
  27.9 9.9 %collective-permute-start.5 = (bf16[128,1152]{1,0:T(8,128)(2,1)S(1)}, bf16[128,1152]{1,0:T(8,128)(2,1)S(1)}, u32[]{:S(2)}, u32[]{:S(2)}) collective-permute-start(bf16[128,1152]{1,0:T(8,128)(2,1)S(1)} %collective-permute-done.1.refs_3_.refs_12_), channel_id=1, source_target_pairs={{0,8},{8,16},{16,24},{24,0},{1,9},{9,17},{17,25},{25,1},{2,10},{10... | collective-permute-start | bytes 884744 | tf_op jit(solution)/shard_map/ppermute | solution.py:20
  33.0 10.7 %collective-permute-start.2 = (bf16[128,1152]{1,0:T(8,128)(2,1)S(1)}, bf16[128,1152]{1,0:T(8,128)(2,1)S(1)}, u32[]{:S(2)}, u32[]{:S(2)}) collective-permute-start(bf16[128,1152]{1,0:T(8,128)(2,1)S(1)} %collective-permute-done.refs_2_.refs_11_), channel_id=1, source_target_pairs={{0,8},{8,16},{16,24},{24,0},{1,9},{9,17},{17,25},{25,1},{2,10},{10... | collective-permute-start | bytes 884744 | tf_op jit(solution)/shard_map/ppermute | solution.py:20
  34.5 9.2 %collective-permute-start.13 = (bf16[128,1152]{1,0:T(8,128)(2,1)S(1)}, bf16[128,1152]{1,0:T(8,128)(2,1)S(1)}, u32[]{:S(2)}, u32[]{:S(2)}) collective-permute-start(bf16[128,1152]{1,0:T(8,128)(2,1)S(1)} %collective-permute-done.11.refs_14_), channel_id=1, source_target_pairs={{0,6},{2,0},{4,2},{6,4},{1,7},{3,1},{5,3},{7,5},{8,14},{10,8},{12,... | collective-permute-start | bytes 884744 | tf_op jit(solution)/shard_map/ppermute | solution.py:20
  35.0 18.4 %copy-start = (bf16[128,1152]{1,0:T(8,128)(2,1)}, bf16[128,1152]{1,0:T(8,128)(2,1)S(1)}, u32[]{:S(2)}) copy-start(bf16[128,1152]{1,0:T(8,128)(2,1)S(1)} %collective-permute-done.4.refs_6_.refs_15_) | copy-start | bytes 884740
  35.0 9.2 %collective-permute-start.6 = (bf16[128,1152]{1,0:T(8,128)(2,1)S(1)}, bf16[128,1152]{1,0:T(8,128)(2,1)S(1)}, u32[]{:S(2)}, u32[]{:S(2)}) collective-permute-start(bf16[128,1152]{1,0:T(8,128)(2,1)S(1)} %collective-permute-done.4.refs_6_.refs_15_), channel_id=1, source_target_pairs={{0,24},{8,0},{16,8},{24,16},{1,25},{9,1},{17,9},{25,17},{2,26},{10... | collective-permute-start | bytes 884744 | tf_op jit(solution)/shard_map/ppermute | solution.py:20
  37.7 15.7 %collective-permute-start.15 = (bf16[128,1152]{1,0:T(8,128)(2,1)S(1)}, bf16[128,1152]{1,0:T(8,128)(2,1)S(1)}, u32[]{:S(2)}, u32[]{:S(2)}) collective-permute-start(bf16[128,1152]{1,0:T(8,128)(2,1)S(1)} %collective-permute-done.refs_2_.refs_11_), channel_id=1, source_target_pairs={{0,32},{32,0},{1,33},{33,1},{2,34},{34,2},{3,35},{35,3},{4,36},{36... | collective-permute-start | bytes 884744 | tf_op jit(solution)/shard_map/ppermute | solution.py:24
  37.8 15.6 %collective-permute-start.19 = (bf16[128,1152]{1,0:T(8,128)(2,1)S(1)}, bf16[128,1152]{1,0:T(8,128)(2,1)S(1)}, u32[]{:S(2)}, u32[]{:S(2)}) collective-permute-start(bf16[128,1152]{1,0:T(8,128)(2,1)S(1)} %collective-permute-done.4.refs_6_.refs_15_), channel_id=1, source_target_pairs={{0,32},{32,0},{1,33},{33,1},{2,34},{34,2},{3,35},{35,3},{4,36},{36... | collective-permute-start | bytes 884744 | tf_op jit(solution)/shard_map/ppermute | solution.py:24
  43.7 9.7 %collective-permute-start.20 = (bf16[128,1152]{1,0:T(8,128)(2,1)S(1)}, bf16[128,1152]{1,0:T(8,128)(2,1)S(1)}, u32[]{:S(2)}, u32[]{:S(2)}) collective-permute-start(bf16[128,1152]{1,0:T(8,128)(2,1)S(1)} %collective-permute-done.5.refs_7_.refs_16_), channel_id=1, source_target_pairs={{0,32},{32,0},{1,33},{33,1},{2,34},{34,2},{3,35},{35,3},{4,36},{36... | collective-permute-start | bytes 884744 | tf_op jit(solution)/shard_map/ppermute | solution.py:24
  43.7 9.7 %collective-permute-start.17 = (bf16[128,1152]{1,0:T(8,128)(2,1)S(1)}, bf16[128,1152]{1,0:T(8,128)(2,1)S(1)}, u32[]{:S(2)}, u32[]{:S(2)}) collective-permute-start(bf16[128,1152]{1,0:T(8,128)(2,1)S(1)} %collective-permute-done.2.refs_4_.refs_13_), channel_id=1, source_target_pairs={{0,32},{32,0},{1,33},{33,1},{2,34},{34,2},{3,35},{35,3},{4,36},{36... | collective-permute-start | bytes 884744 | tf_op jit(solution)/shard_map/ppermute | solution.py:24
  44.2 9.2 %collective-permute-start.21 = (bf16[128,1152]{1,0:T(8,128)(2,1)S(1)}, bf16[128,1152]{1,0:T(8,128)(2,1)S(1)}, u32[]{:S(2)}, u32[]{:S(2)}) collective-permute-start(bf16[128,1152]{1,0:T(8,128)(2,1)S(1)} %collective-permute-done.6.refs_8_.refs_17_), channel_id=1, source_target_pairs={{0,32},{32,0},{1,33},{33,1},{2,34},{34,2},{3,35},{35,3},{4,36},{36... | collective-permute-start | bytes 884744 | tf_op jit(solution)/shard_map/ppermute | solution.py:24
  62.3 73.6 %collective-permute-start.22 = (bf16[128,1152]{1,0:T(8,128)(2,1)S(1)}, bf16[128,1152]{1,0:T(8,128)(2,1)S(1)}, u32[]{:S(2)}, u32[]{:S(2)}) collective-permute-start(bf16[128,1152]{1,0:T(8,128)(2,1)S(1)} %get-tuple-element.29), channel_id=1, source_target_pairs={{0,32},{32,0},{1,33},{33,1},{2,34},{34,2},{3,35},{35,3},{4,36},{36... | collective-permute-start | bytes 884744 | tf_op jit(solution)/shard_map/ppermute | solution.py:24
  62.8 13.4 %collective-permute-start.23 = (bf16[128,1152]{1,0:T(8,128)(2,1)S(1)}, bf16[128,1152]{1,0:T(8,128)(2,1)S(1)}, u32[]{:S(2)}, u32[]{:S(2)}) collective-permute-start(bf16[128,1152]{1,0:T(8,128)(2,1)S(1)} %get-tuple-element.31), channel_id=1, source_target_pairs={{0,32},{32,0},{1,33},{33,1},{2,34},{34,2},{3,35},{35,3},{4,36},{36... | collective-permute-start | bytes 884744 | tf_op jit(solution)/shard_map/ppermute | solution.py:24
  62.9 34.4 %collective-permute-start.25 = (bf16[128,1152]{1,0:T(8,128)(2,1)S(1)}, bf16[128,1152]{1,0:T(8,128)(2,1)S(1)}, u32[]{:S(2)}, u32[]{:S(2)}) collective-permute-start(bf16[128,1152]{1,0:T(8,128)(2,1)S(1)} %get-tuple-element.33), channel_id=1, source_target_pairs={{0,32},{32,0},{1,33},{33,1},{2,34},{34,2},{3,35},{35,3},{4,36},{36... | collective-permute-start | bytes 884744 | tf_op jit(solution)/shard_map/ppermute | solution.py:24
  63.3 12.4 %collective-permute-start.26 = (bf16[128,1152]{1,0:T(8,128)(2,1)S(1)}, bf16[128,1152]{1,0:T(8,128)(2,1)S(1)}, u32[]{:S(2)}, u32[]{:S(2)}) collective-permute-start(bf16[128,1152]{1,0:T(8,128)(2,1)S(1)} %get-tuple-element.35), channel_id=1, source_target_pairs={{0,32},{32,0},{1,33},{33,1},{2,34},{34,2},{3,35},{35,3},{4,36},{36... | collective-permute-start | bytes 884744 | tf_op jit(solution)/shard_map/ppermute | solution.py:24
  63.4 10.4 %collective-permute-start.33 = (bf16[128,1152]{1,0:T(8,128)(2,1)S(1)}, bf16[128,1152]{1,0:T(8,128)(2,1)S(1)}, u32[]{:S(2)}, u32[]{:S(2)}) collective-permute-start(bf16[128,1152]{1,0:T(8,128)(2,1)S(1)} %get-tuple-element.43), channel_id=1, source_target_pairs={{0,32},{32,0},{1,33},{33,1},{2,34},{34,2},{3,35},{35,3},{4,36},{36... | collective-permute-start | bytes 884744 | tf_op jit(solution)/shard_map/ppermute | solution.py:24
  73.8 1.7 %collective-permute-start.30 = (bf16[128,1152]{1,0:T(8,128)(2,1)S(1)}, bf16[128,1152]{1,0:T(8,128)(2,1)S(1)}, u32[]{:S(2)}, u32[]{:S(2)}) collective-permute-start(bf16[128,1152]{1,0:T(8,128)(2,1)S(1)} %get-tuple-element.39), channel_id=1, source_target_pairs={{0,32},{32,0},{1,33},{33,1},{2,34},{34,2},{3,35},{35,3},{4,36},{36... | collective-permute-start | bytes 884744 | tf_op jit(solution)/shard_map/ppermute | solution.py:24
  75.5 42.9 %collective-permute-start.29 = (bf16[128,1152]{1,0:T(8,128)(2,1)S(1)}, bf16[128,1152]{1,0:T(8,128)(2,1)S(1)}, u32[]{:S(2)}, u32[]{:S(2)}) collective-permute-start(bf16[128,1152]{1,0:T(8,128)(2,1)S(1)} %get-tuple-element.37), channel_id=1, source_target_pairs={{0,32},{32,0},{1,33},{33,1},{2,34},{34,2},{3,35},{35,3},{4,36},{36... | collective-permute-start | bytes 884744 | tf_op jit(solution)/shard_map/ppermute | solution.py:24
  75.7 28.0 %collective-permute-start.32 = (bf16[128,1152]{1,0:T(8,128)(2,1)S(1)}, bf16[128,1152]{1,0:T(8,128)(2,1)S(1)}, u32[]{:S(2)}, u32[]{:S(2)}) collective-permute-start(bf16[128,1152]{1,0:T(8,128)(2,1)S(1)} %get-tuple-element.41), channel_id=1, source_target_pairs={{0,32},{32,0},{1,33},{33,1},{2,34},{34,2},{3,35},{35,3},{4,36},{36... | collective-permute-start | bytes 884744 | tf_op jit(solution)/shard_map/ppermute | solution.py:24
  76.2 9.1 %collective-permute-start.38 = (bf16[128,1152]{1,0:T(8,128)(2,1)S(1)}, bf16[128,1152]{1,0:T(8,128)(2,1)S(1)}, u32[]{:S(2)}, u32[]{:S(2)}) collective-permute-start(bf16[128,1152]{1,0:T(8,128)(2,1)S(1)} %get-tuple-element.49), channel_id=1, source_target_pairs={{0,6},{2,0},{4,2},{6,4},{1,7},{3,1},{5,3},{7,5},{8,14},{10,8},{12,... | collective-permute-start | bytes 884744 | tf_op jit(solution)/shard_map/ppermute | solution.py:20
  85.3 9.4 %collective-permute-start.41 = (bf16[128,1152]{1,0:T(8,128)(2,1)S(1)}, bf16[128,1152]{1,0:T(8,128)(2,1)S(1)}, u32[]{:S(2)}, u32[]{:S(2)}) collective-permute-start(bf16[128,1152]{1,0:T(8,128)(2,1)S(1)} %get-tuple-element.53), channel_id=1, source_target_pairs={{0,2},{2,4},{4,6},{6,0},{1,3},{3,5},{5,7},{7,1},{8,10},{10,12},{12... | collective-permute-start | bytes 884744 | tf_op jit(solution)/shard_map/ppermute | solution.py:20
  94.8 7.6 %collective-permute-start.27 = (bf16[128,1152]{1,0:T(8,128)(2,1)S(1)}, bf16[128,1152]{1,0:T(8,128)(2,1)S(1)}, u32[]{:S(2)}, u32[]{:S(2)}) collective-permute-start(bf16[128,1152]{1,0:T(8,128)(2,1)S(1)} %add_convert_fusion.10), channel_id=1, source_target_pairs={{0,24},{8,0},{16,8},{24,16},{1,25},{9,1},{17,9},{25,17},{2,26},{10... | collective-permute-start | bytes 884744 | tf_op jit(solution)/shard_map/ppermute | solution.py:20
  97.3 31.7 %collective-permute-start.37 = (bf16[128,1152]{1,0:T(8,128)(2,1)S(1)}, bf16[128,1152]{1,0:T(8,128)(2,1)S(1)}, u32[]{:S(2)}, u32[]{:S(2)}) collective-permute-start(bf16[128,1152]{1,0:T(8,128)(2,1)S(1)} %get-tuple-element.47), channel_id=1, source_target_pairs={{0,2},{2,4},{4,6},{6,0},{1,3},{3,5},{5,7},{7,1},{8,10},{10,12},{12... | collective-permute-start | bytes 884744 | tf_op jit(solution)/shard_map/ppermute | solution.py:20
  102.4 7.4 %collective-permute-start.34 = (bf16[128,1152]{1,0:T(8,128)(2,1)S(1)}, bf16[128,1152]{1,0:T(8,128)(2,1)S(1)}, u32[]{:S(2)}, u32[]{:S(2)}) collective-permute-start(bf16[128,1152]{1,0:T(8,128)(2,1)S(1)} %add_convert_fusion.5), channel_id=1, source_target_pairs={{0,8},{8,16},{16,24},{24,0},{1,9},{9,17},{17,25},{25,1},{2,10},{10... | collective-permute-start | bytes 884744 | tf_op jit(solution)/shard_map/ppermute | solution.py:20
  103.7 30.7 %copy-start.4 = (bf16[128,1152]{1,0:T(8,128)(2,1)S(1)}, bf16[128,1152]{1,0:T(8,128)(2,1)}, u32[]{:S(2)}) copy-start(bf16[128,1152]{1,0:T(8,128)(2,1)} %param.6) | copy-start | bytes 884740
  103.7 6.8 %collective-permute-start.40 = (bf16[128,1152]{1,0:T(8,128)(2,1)S(1)}, bf16[128,1152]{1,0:T(8,128)(2,1)S(1)}, u32[]{:S(2)}, u32[]{:S(2)}) collective-permute-start(bf16[128,1152]{1,0:T(8,128)(2,1)S(1)} %get-tuple-element.51), channel_id=1, source_target_pairs={{0,6},{2,0},{4,2},{6,4},{1,7},{3,1},{5,3},{7,5},{8,14},{10,8},{12,... | collective-permute-start | bytes 884744 | tf_op jit(solution)/shard_map/ppermute | solution.py:20
  109.8 7.9 %collective-permute-start.42 = (bf16[128,1152]{1,0:T(8,128)(2,1)S(1)}, bf16[128,1152]{1,0:T(8,128)(2,1)S(1)}, u32[]{:S(2)}, u32[]{:S(2)}) collective-permute-start(bf16[128,1152]{1,0:T(8,128)(2,1)S(1)} %add_convert_fusion.1), channel_id=1, source_target_pairs={{0,2},{2,4},{4,6},{6,0},{1,3},{3,5},{5,7},{7,1},{8,10},{10,12},{12... | collective-permute-start | bytes 884744 | tf_op jit(solution)/shard_map/ppermute | solution.py:20
  110.5 10.2 %collective-permute-start.31 = (bf16[128,1152]{1,0:T(8,128)(2,1)S(1)}, bf16[128,1152]{1,0:T(8,128)(2,1)S(1)}, u32[]{:S(2)}, u32[]{:S(2)}) collective-permute-start(bf16[128,1152]{1,0:T(8,128)(2,1)S(1)} %add_convert_fusion.7), channel_id=1, source_target_pairs={{0,24},{8,0},{16,8},{24,16},{1,25},{9,1},{17,9},{25,17},{2,26},{10... | collective-permute-start | bytes 884744 | tf_op jit(solution)/shard_map/ppermute | solution.py:20
  117.7 8.8 %collective-permute-start.35 = (bf16[128,1152]{1,0:T(8,128)(2,1)S(1)}, bf16[128,1152]{1,0:T(8,128)(2,1)S(1)}, u32[]{:S(2)}, u32[]{:S(2)}) collective-permute-start(bf16[128,1152]{1,0:T(8,128)(2,1)S(1)} %add_convert_fusion.4), channel_id=1, source_target_pairs={{0,8},{8,16},{16,24},{24,0},{1,9},{9,17},{17,25},{25,1},{2,10},{10... | collective-permute-start | bytes 884744 | tf_op jit(solution)/shard_map/ppermute | solution.py:20
  118.4 17.5 %collective-permute-start.24 = (bf16[128,1152]{1,0:T(8,128)(2,1)S(1)}, bf16[128,1152]{1,0:T(8,128)(2,1)S(1)}, u32[]{:S(2)}, u32[]{:S(2)}) collective-permute-start(bf16[128,1152]{1,0:T(8,128)(2,1)S(1)} %add_convert_fusion.12), channel_id=1, source_target_pairs={{0,8},{8,16},{16,24},{24,0},{1,9},{9,17},{17,25},{25,1},{2,10},{10... | collective-permute-start | bytes 884744 | tf_op jit(solution)/shard_map/ppermute | solution.py:20
  120.7 11.3 %collective-permute-start.39 = (bf16[128,1152]{1,0:T(8,128)(2,1)S(1)}, bf16[128,1152]{1,0:T(8,128)(2,1)S(1)}, u32[]{:S(2)}, u32[]{:S(2)}) collective-permute-start(bf16[128,1152]{1,0:T(8,128)(2,1)S(1)} %add_convert_fusion.2), channel_id=1, source_target_pairs={{0,6},{2,0},{4,2},{6,4},{1,7},{3,1},{5,3},{7,5},{8,14},{10,8},{12,... | collective-permute-start | bytes 884744 | tf_op jit(solution)/shard_map/ppermute | solution.py:20
  126.5 7.9 %collective-permute-start.43 = (bf16[128,1152]{1,0:T(8,128)(2,1)S(1)}, bf16[128,1152]{1,0:T(8,128)(2,1)S(1)}, u32[]{:S(2)}, u32[]{:S(2)}) collective-permute-start(bf16[128,1152]{1,0:T(8,128)(2,1)S(1)} %add_convert_fusion), channel_id=1, source_target_pairs={{0,65},{64,1},{1,64},{65,0},{2,67},{66,3},{3,66},{67,2},{4,69},{68... | collective-permute-start | bytes 884744 | tf_op jit(solution)/shard_map/ppermute | solution.py:36
  129.0 7.3 %collective-permute-start.28 = (bf16[128,1152]{1,0:T(8,128)(2,1)S(1)}, bf16[128,1152]{1,0:T(8,128)(2,1)S(1)}, u32[]{:S(2)}, u32[]{:S(2)}) collective-permute-start(bf16[128,1152]{1,0:T(8,128)(2,1)S(1)} %add_convert_fusion.9), channel_id=1, source_target_pairs={{0,24},{8,0},{16,8},{24,16},{1,25},{9,1},{17,9},{25,17},{2,26},{10... | collective-permute-start | bytes 884744 | tf_op jit(solution)/shard_map/ppermute | solution.py:20
  132.0 6.7 %collective-permute-start.36 = (bf16[128,1152]{1,0:T(8,128)(2,1)S(1)}, bf16[128,1152]{1,0:T(8,128)(2,1)S(1)}, u32[]{:S(2)}, u32[]{:S(2)}) collective-permute-start(bf16[128,1152]{1,0:T(8,128)(2,1)S(1)} %add_convert_fusion.3), channel_id=1, source_target_pairs={{0,64},{64,0},{1,65},{65,1},{2,66},{66,2},{3,67},{67,3},{4,68},{68... | collective-permute-start | bytes 884744 | tf_op jit(solution)/shard_map/ppermute | solution.py:36
  (4 other events, 35.3 us)

commit v2 on v0

v2 whole, which is shorter than its diff:
```python
import functools
import math

import jax
import jax.numpy as jnp
from jax import lax
from jax.experimental import pallas as pl
from jax.experimental.pallas import tpu as pltpu
from jax.sharding import Mesh
from jax.sharding import PartitionSpec as P

FINE_AXES = ("y_lo", "core", "x", "z", "y_hi")
FINE_SIZES = (2, 2, 4, 4, 2)
RING = 4
VMEM_BYTES = 40 * 1024 * 1024
HALF = jnp.bfloat16
FULL = jnp.float32

VMEM = pl.BlockSpec(memory_space=pltpu.VMEM)
SMEM = pl.BlockSpec(memory_space=pltpu.SMEM)
ANY = pl.BlockSpec(memory_space=pl.ANY)
PARAMS = pltpu.CompilerParams(vmem_limit_bytes=VMEM_BYTES)


def both_ways(value, axis, sign):
    pairs = []
    for core in range(2):
        step = sign if core == 0 else -sign
        for k in range(RING):
            pairs.append((core * RING + k, core * RING + (k + step) % RING))
    return lax.ppermute(value, ("core", axis), pairs)


def other_core(value):
    return lax.ppermute(value, "core", [(0, 1), (1, 0)])


def y_partner(value, wrapped):
    pairs = []
    for y in range(RING):
        if wrapped:
            mate = (y + 1) % RING if y % 2 else (y - 1) % RING
        else:
            mate = y ^ 1
        pairs.append(((y % 2) * 2 + y // 2, (mate % 2) * 2 + mate // 2))
    return lax.ppermute(value, ("y_lo", "y_hi"), pairs)


def local(body, outs, scalars, arrays, passed=()):
    n_scalars, n_arrays, n_outs, n_passed = len(scalars), len(arrays), len(outs), len(passed)

    def kernel(*refs):
        given = refs[: n_scalars + n_arrays]
        results = refs[n_scalars + n_arrays + n_passed :][:n_outs]
        for ref, value in zip(results, body(given[:n_scalars], given[n_scalars:]), strict=True):
            ref[...] = value.astype(ref.dtype)

    first = n_scalars + n_arrays
    return pl.pallas_call(
        kernel,
        out_shape=[jax.ShapeDtypeStruct(s, d) for s, d in outs]
        + [jax.ShapeDtypeStruct(a.shape, a.dtype) for a in passed],
        in_specs=[SMEM] * n_scalars + [VMEM] * n_arrays + [ANY] * n_passed,
        out_specs=[VMEM] * n_outs + [ANY] * n_passed,
        input_output_aliases={first + k: n_outs + k for k in range(n_passed)},
        compiler_params=PARAMS,
    )(*scalars, *arrays, *passed)


def assembled(body, outs, scalars, whole, stacks, flops):
    flat = [piece for stack in stacks for piece in stack]
    n_scalars, n_whole, n_flat, n_outs = len(scalars), len(whole), len(flat), len(outs)

    def kernel(*refs):
        scalar_refs, refs = refs[:n_scalars], refs[n_scalars:]
        whole_refs, refs = refs[:n_whole], refs[n_whole:]
        piece_refs, refs = refs[:n_flat], refs[n_flat:]
        out_refs, refs = refs[:n_outs], refs[n_outs:]
        buffers, sems = refs[: len(stacks)], refs[len(stacks)]
        copies = []
        for buffer, stack in zip(buffers, stacks, strict=True):
            row = 0
            for piece in stack:
                rows = piece.shape[0]
                k = len(copies)
                copies.append(
                    pltpu.make_async_copy(
                        piece_refs[k], buffer.at[pl.ds(row, rows)], sems.at[k]
                    )
                )
                row += rows
        for copy in copies:
            copy.start()
        for copy in copies:
            copy.wait()
        body(scalar_refs, whole_refs, buffers, out_refs)

    return pl.pallas_call(
        kernel,
        out_shape=[jax.ShapeDtypeStruct(s, d) for s, d in outs],
        in_specs=[SMEM] * n_scalars + [VMEM] * n_whole + [ANY] * n_flat,
        out_specs=[VMEM] * n_outs,
        scratch_shapes=[
            pltpu.VMEM((sum(p.shape[0] for p in stack), stack[0].shape[1]), stack[0].dtype)
            for stack in stacks
        ]
        + [pltpu.SemaphoreType.DMA((n_flat,))],
        cost_estimate=pl.CostEstimate(
            flops=flops,
            bytes_accessed=sum(a.size * a.dtype.itemsize for a in flat),
            transcendentals=0,
        ),
        compiler_params=PARAMS,
    )(*scalars, *whole, *flat)


def dot(a, b, contract):
    return lax.dot_general(a, b, ((contract[:1], contract[1:]), ((), ())), preferred_element_type=FULL)


def unit_rows(raw):
    values = raw.astype(FULL)
    scale = lax.rsqrt(jnp.mean(values * values, axis=1, keepdims=True) + 1e-06) / math.sqrt(
        values.shape[1]
    )
    return values * scale, scale


def coupling_block(affine, texts, images):
    energies = dot(texts, images, (1, 1))
    return 0.5 * jnp.tanh(affine[0] * energies + affine[1]) + 0.5


def on_device(
    picture_vectors_raw, caption_vectors_raw, logit_multiplier, offset_term, incoming_adjoint
):
    rows, width = picture_vectors_raw.shape
    pairs = rows * math.prod(FINE_SIZES)
    is_first = (lax.axis_index("core") == 0).astype(FULL).reshape(1)
    affine = jnp.concatenate([0.5 * logit_multiplier, 0.5 * offset_term])
    derivative_multiplier = incoming_adjoint * logit_multiplier / pairs
    one, two = ((rows, width), HALF), ((2 * rows, width), HALF)
    one_full = ((rows, width), FULL)
    block = 2 * rows
    block_flops = 2 * block * block * width


    image_raw_there = other_core(picture_vectors_raw)
    text_raw_there = other_core(caption_vectors_raw)

    def normalize(_, refs):
        image, image_there, text, text_there = [unit_rows(ref[...])[0].astype(HALF) for ref in refs]
        return [
            jnp.concatenate([image, image_there], 0),
            jnp.concatenate([text, text_there], 0),
            image,
            text,
        ]

    io, to, image_own, text_own = local(
        normalize,
        [two, two, one, one],
        [],
        [picture_vectors_raw, image_raw_there, caption_vectors_raw, text_raw_there],
    )
    ia = both_ways(io, "x", 1)
    ta = both_ways(to, "z", 1)
    ip_mine = y_partner(image_own, False)
    tp_mine = y_partner(text_own, True)

    i_on, t_on, ia, ta, ip_mine, tp_mine = local(
        lambda _, refs: [refs[0][:rows], refs[1][:rows]],
        [one, one],
        [],
        [ia, ta],
        [ia, ta, ip_mine, tp_mine],
    )
    im = both_ways(i_on, "x", 1)
    tm = both_ways(t_on, "z", 1)
    ip_there = other_core(ip_mine)
    tp_there = other_core(tp_mine)
    ib = other_core(ia)

    def partners(scalars, refs):
        image_mine, image_there, text_mine, text_there, text_own_chip = [ref[...] for ref in refs]
        image_pair = jnp.concatenate([image_mine, image_there], 0)
        text_pair = jnp.concatenate([text_mine, text_there], 0)
        return [image_pair, text_pair, jnp.where(scalars[0][0] > 0, text_own_chip, text_pair)]

    ip, tp, te, im, tm, ib = local(
        partners,
        [two, two, two],
        [is_first],
        [ip_mine, ip_there, tp_mine, tp_there, to],
        [im, tm, ib],
    )
    ia2 = both_ways(ip, "x", 1)
    ta2 = both_ways(tp, "z", 1)
    im2 = y_partner(im, False)
    tm2 = y_partner(tm, True)
    it = other_core(im)

    images_early = [io, ip, ia, ib, im, it]
    texts_early = [te, ta, tm]
    n_ie, n_te, n_il, n_tl = 10 * rows, 5 * rows, 6 * rows, 3 * rows
    n_t = n_te + n_tl

    def early(scalars, _, stacks, outs):
        images, texts = stacks
        for k in range(n_ie // block):
            cols = pl.ds(k * block, block)
            tile = coupling_block(scalars[0], texts[...], images[cols, :])
            if k == 0:
                row = lax.broadcasted_iota(jnp.int32, tile.shape, 0)
                column = lax.broadcasted_iota(jnp.int32, tile.shape, 1)
                tile = tile - jnp.where(row == column, scalars[1][0], 0.0)
            outs[0][:, cols] = tile.astype(HALF)

    (c_ee,) = assembled(
        early,
        [((n_te, n_ie), HALF)],
        [affine, is_first],
        [],
        [images_early, texts_early],
        12 * block_flops,
    )

    ia2, ta2, im2, tm2, it, c_ee = local(lambda *_: [], [], [], [], [ia2, ta2, im2, tm2, it, c_ee])
    images_early = [io, ip, ia, ib, im, it]
    texts_late = [ta2, tm2]
    ib2 = other_core(ia2)
    it2 = other_core(im2)

    def late_texts(scalars, _, stacks, outs):
        images, texts = stacks
        for k in range(n_ie // block):
            cols = pl.ds(k * block, block)
            outs[0][:, cols] = coupling_block(scalars[0], texts[...], images[cols, :]).astype(HALF)

    (c_le,) = assembled(
        late_texts,
        [((n_tl, n_ie), HALF)],
        [affine],
        [],
        [images_early, texts_late],
        8 * block_flops,
    )

    images_late = [ia2, ib2, im2, it2]

    def late_images(scalars, _, stacks, outs):
        images, texts = stacks
        for k in range(n_il // block):
            cols = pl.ds(k * block, block)
            tile = coupling_block(scalars[0], texts[...], images[cols, :]).astype(HALF)
            outs[0][:, cols] = tile
            part = dot(tile, texts[...], (0, 0)).astype(HALF)
            if k < 2:
                outs[1 + k][:block, :] = part
            else:
                outs[1][block:, :] = part[:rows]
                outs[2][block:, :] = part[rows:]

    c_l, gi_late, gi_late_there = assembled(
        late_images,
        [((n_t, n_il), HALF), ((3 * rows, width), HALF), ((3 * rows, width), HALF)],
        [affine],
        [],
        [images_late, texts_early + texts_late],
        24 * block_flops,
    )
    gi_late_back = other_core(gi_late_there)

    def late_text_parts(_, whole, stacks, outs):
        c_le, c_l = whole
        (images,) = stacks
        part = dot(c_le[...], images[:n_ie, :], (1, 0))
        part = part + dot(c_l[n_te:, :], images[n_ie:, :], (1, 0))
        part = part.astype(HALF)
        outs[0][...] = part[:block]
        outs[1][...] = part[block:]

    ga2_t, gm2_t = assembled(
        late_text_parts,
        [two, one],
        [],
        [c_le, c_l],
        [images_early + images_late],
        12 * block_flops,
    )

    def add_late(_, refs):
        total = refs[0][...].astype(FULL) + refs[1][...].astype(FULL)
        return [total[:block], total[block:]]

    ga2_i, gm2_i, ga2_t, gm2_t = local(
        add_late, [two, one], [], [gi_late, gi_late_back], [ga2_t, gm2_t]
    )
    p_in_i = both_ways(ga2_i, "x", -1)
    p_in_t = both_ways(ga2_t, "z", -1)
    m_in_i = y_partner(gm2_i, False)
    m_in_t = y_partner(gm2_t, True)

    def image_part(couplings, texts, first, count):
        cols = pl.ds(first, count)
        part = dot(couplings[0][:, cols], texts[:n_te, :], (0, 0))
        return (part + dot(couplings[1][:, cols], texts[n_te:, :], (0, 0))).astype(HALF)

    def text_part(couplings, images, first, count):
        at = pl.ds(first, count)
        part = dot(couplings[0][at, :], images[:n_ie, :], (1, 0))
        return (part + dot(couplings[2][at, :], images[n_ie:, :], (1, 0))).astype(HALF)

    def parts_first(_, couplings, stacks, outs):
        images, texts = stacks
        outs[0][...] = image_part(couplings, texts, block, block)
        part = image_part(couplings, texts, 4 * block, block)
        outs[1][...] = part[:rows]
        outs[2][...] = part[rows:]
        outs[3][...] = text_part(couplings, images, 0, block)
        outs[4][...] = text_part(couplings, images, 2 * block, rows)

    gp_i, gm_i, gt_i, ge_t, gm_t = assembled(
        parts_first,
        [two, one, one, two, one],
        [],
        [c_ee, c_le, c_l],
        [images_early + images_late, texts_early + texts_late],
        20 * block_flops,
    )
    gt_back = other_core(gt_i)

    def round_one(scalars, refs):
        p_in_i, p_in_t, m_in_i, m_in_t, gp_i, gm_i, gt_back, ge_t, gm_t = [
            ref[...].astype(FULL) for ref in refs
        ]
        p_i = p_in_i + gp_i
        p_t = p_in_t + ge_t * (1.0 - scalars[0][0])
        return [
            p_i[:rows],
            p_i[rows:],
            p_t[:rows],
            p_t[rows:],
            gm_i + gt_back + m_in_i,
            gm_t + m_in_t,
        ]

    p_i, p_i_there, p_t, p_t_there, m_i, m_t = local(
        round_one,
        [one_full, one, one_full, one, one, one],
        [is_first],
        [p_in_i, p_in_t, m_in_i, m_in_t, gp_i, gm_i, gt_back, ge_t, gm_t],
    )
    a_in_i = both_ways(m_i, "x", -1)
    a_in_t = both_ways(m_t, "z", -1)
    p_back_i = other_core(p_i_there)
    p_back_t = other_core(p_t_there)

    def parts_second(_, couplings, stacks, outs):
        images, texts = stacks
        outs[0][...] = image_part(couplings, texts, 3 * block, block)
        outs[1][...] = image_part(couplings, texts, 2 * block, block)
        outs[2][...] = image_part(couplings, texts, 0, block)
        outs[3][...] = text_part(couplings, images, block, block)

    gb_i, ga_i, go_i, ga_t = assembled(
        parts_second,
        [two, two, two, two],
        [],
        [c_ee, c_le, c_l],
        [images_early + images_late, texts_early + texts_late],
        24 * block_flops,
    )
    gb_back = other_core(gb_i)

    def round_two(_, refs):
        p_i, p_back_i, p_t, p_back_t, a_in_i, a_in_t, ga_i, gb_back, ga_t = [
            ref[...].astype(FULL) for ref in refs
        ]
        a_i = ga_i + gb_back
        return [
            p_i + p_back_i,
            p_t + p_back_t,
            jnp.concatenate([a_i[:rows] + a_in_i, a_i[rows:]], 0),
            jnp.concatenate([ga_t[:rows] + a_in_t, ga_t[rows:]], 0),
        ]

    p_i, p_t, a_i, a_t = local(
        round_two,
        [one, one, two, two],
        [],
        [p_i, p_back_i, p_t, p_back_t, a_in_i, a_in_t, ga_i, gb_back, ga_t],
    )
    o_in_i = both_ways(a_i, "x", -1)
    o_in_t = both_ways(a_t, "z", -1)
    y_in_i = y_partner(p_i, False)
    y_in_t = y_partner(p_t, True)

    def round_three(scalars, refs):
        o_in_i, o_in_t, y_in_i, y_in_t, go_i, ge_t = [ref[...].astype(FULL) for ref in refs]
        o_i = o_in_i + go_i
        o_t = o_in_t + ge_t * scalars[0][0]
        return [o_i[:rows] + y_in_i, o_i[rows:], o_t[:rows] + y_in_t, o_t[rows:]]

    o_i, o_i_there, o_t, o_t_there = local(
        round_three,
        [one_full, one, one_full, one],
        [is_first],
        [o_in_i, o_in_t, y_in_i, y_in_t, go_i, ge_t],
    )
    o_back_i = other_core(o_i_there)
    o_back_t = other_core(o_t_there)

    def finish(scalars, refs):
        multiplier = scalars[0][0]
        results = []
        for raw, mine, back in (refs[:3], refs[3:]):
            unit, scale = unit_rows(raw[...])
            grad = multiplier * (mine[...] + back[...].astype(FULL))
            results.append(scale * (grad - unit * jnp.sum(unit * grad, axis=1, keepdims=True)))
        return results

    return tuple(
        local(
            finish,
            [one_full, one_full],
            [derivative_multiplier],
            [picture_vectors_raw, o_i, o_back_i, caption_vectors_raw, o_t, o_back_t],
        )
    )


def solution(mesh):
    fine = Mesh(mesh.devices.reshape(FINE_SIZES), FINE_AXES)
    rows = P(FINE_AXES, None)
    return jax.shard_map(
        on_device,
        mesh=fine,
        in_specs=(rows, rows, P(), P(), P()),
        out_specs=(rows, rows),
        check_vma=False,
    )
```

time: 447 us -> 111 us (0.25)
  waiting for transfers between devices: 360 us -> 32.7 us
  matrix products: 42.7 us -> 0 us
  Pallas kernels: 0 us -> 35.1 us
  starting transfers between devices: 17 us -> 37 us
  between operations: 16.2 us -> 2.76 us
  other arithmetic: 9.91 us -> 0.08 us
    reduce_scatter x1 -> x0, waiting for transfers between devices: 218 us -> none  [on_device(): lax.psum_scatter(column_term(all_tiles, all_rows), 'grp', scatter_dimensi...]
    all_gather x1 -> x0, waiting for transfers between devices: 97.6 us -> none  [on_device(): lines_each_cluster = lax.all_gather(staying[0], 'grp', axis=0, tiled=True)]
    dot_general x9 -> x0, matrix products: 42.7 us -> none  [the longest x4 18 us: assemble_interaction(): lax.dot_general(first_operand_lines, second_operand_lines, (((1,), (1,)),...]
    pallas_call x0 -> x15, Pallas kernels: none -> 35.1 us  [the longest x6 29.6 us: assembled(): pl.pallas_call(kernel, out_shape=[jax.ShapeDtypeStruct(s, d) for s, d in...]
    ppermute x7 -> x35, starting transfers between devices: 16.9 us -> 37 us  [the longest x15 14.6 us: other_core(): return lax.ppermute(value, 'core', [(0, 1), (1, 0)])]
    ppermute x7 -> x35, waiting for transfers between devices: 44.2 us -> 32.7 us  [the longest x12 16.2 us: both_ways(): return lax.ppermute(value, ('core', axis), pairs)]
  transfers between devices with their start and end apart: 9 -> 35, of which waited for: 8 -> 20; matrix products, arithmetic and copies ran while one was open for 7% -> 0% of each run, Pallas kernels for 0% -> 20%
where the time goes in v2:
time: 111 us
  starting transfers between devices  37 us (33%)
  Pallas kernels  35.1 us (32%)
  waiting for transfers between devices  32.7 us (29%)
  local copies, waits for them, and re-layouts  3.1 us (3%)
  between operations  2.76 us (2%)
    pallas_call x6, Pallas kernels, assembled(): pl.pallas_call(kernel, out_shape=[jax.ShapeDtypeStruct(s, d) for s, d in...  29.6 us
    ppermute x12, waiting for transfers between devices, both_ways(): return lax.ppermute(value, ('core', axis), pairs)  16.2 us
    ppermute x15, starting transfers between devices, other_core(): return lax.ppermute(value, 'core', [(0, 1), (1, 0)])  14.6 us
    ppermute x12, starting transfers between devices, both_ways(): return lax.ppermute(value, ('core', axis), pairs)  13.4 us
    ppermute x8, waiting for transfers between devices, y_partner(): return lax.ppermute(value, ('y_lo', 'y_hi'), pairs)  10.5 us
    ppermute x8, starting transfers between devices, y_partner(): return lax.ppermute(value, ('y_lo', 'y_hi'), pairs)  9.01 us
    ppermute x15, waiting for transfers between devices, other_core(): return lax.ppermute(value, 'core', [(0, 1), (1, 0)])  6.04 us
    pallas_call x9, Pallas kernels, local(): pl.pallas_call(kernel, out_shape=[jax.ShapeDtypeStruct(s, d) for s, d in...  5.44 us
  transfers between devices with their start and end apart: 35, of which 20 were waited for; matrix products, arithmetic and copies ran while one was open for 0% of the time, Pallas kernels for 20%

profile of v2, /device:TPU:1, one launch (start us, length us, event | category | flops | bytes accessed | tf_op | source)
XLA Modules:
  0.0 110.7 jit_solution(3406229221557064123)
XLA Ops:
  0.6 1.5 %collective-permute-start = (bf16[128,1152]{1,0:T(8,128)(2,1)}, bf16[128,1152]{1,0:T(8,128)(2,1)S(1)}, u32[]{:S(2)}, u32[]{:S(2)}) collective-permute-start(bf16[128,1152]{1,0:T(8,128)(2,1)} %refs_1_.1), channel_id=1, source_target_pairs={{0,32},{32,0},{1,33},{33,1},{2,34},{34,2},{3,35},{35,3},{4,36},{36... | collective-permute-start | bytes 884744 | tf_op jit(solution)/shard_map/ppermute | solution.py:35
  2.2 1.3 %collective-permute-done.refs_1_ = bf16[128,1152]{1,0:T(8,128)(2,1)S(1)} collective-permute-done((bf16[128,1152]{1,0:T(8,128)(2,1)}, bf16[128,1152]{1,0:T(8,128)(2,1)S(1)}, u32[]{:S(2)}, u32[]{:S(2)}) %collective-permute-start) | collective-permute-done | bytes 294944 | tf_op jit(solution)/shard_map/ppermute | solution.py:35
  4.0 1.0 copy-done
  4.9 1.0 copy-done.2
  6.3 2.6 %collective-permute-start.2 = (bf16[256,1152]{1,0:T(8,128)(2,1)S(1)}, bf16[256,1152]{1,0:T(8,128)(2,1)S(1)}, u32[]{:S(2)}, u32[]{:S(2)}) collective-permute-start(bf16[256,1152]{1,0:T(8,128)(2,1)S(1)} %get-tuple-element.56.refs_2_.refs_1_.refs_3_), channel_id=1, source_target_pairs={{0,8},{8,16},{16,24},{24,0},{32,56},{40,32},{48,40},{56,48},{1,9},... | collective-permute-start | bytes 1769480 | tf_op jit(solution)/shard_map/ppermute | solution.py:31
  8.9 3.8 %collective-permute-start.3 = (bf16[256,1152]{1,0:T(8,128)(2,1)S(1)}, bf16[256,1152]{1,0:T(8,128)(2,1)S(1)}, u32[]{:S(2)}, u32[]{:S(2)}) collective-permute-start(bf16[256,1152]{1,0:T(8,128)(2,1)S(1)} %get-tuple-element.57.refs_5_), channel_id=1, source_target_pairs={{0,2},{2,4},{4,6},{6,0},{32,38},{34,32},{36,34},{38,36},{1,3},{3,5... | collective-permute-start | bytes 1769480 | tf_op jit(solution)/shard_map/ppermute | solution.py:31
  12.7 1.3 %collective-permute-start.4 = (bf16[128,1152]{1,0:T(8,128)(2,1)S(1)}, bf16[128,1152]{1,0:T(8,128)(2,1)S(1)}, u32[]{:S(2)}, u32[]{:S(2)}) collective-permute-start(bf16[128,1152]{1,0:T(8,128)(2,1)S(1)} %get-tuple-element.58), channel_id=1, source_target_pairs={{0,64},{64,0},{1,65},{65,1},{2,66},{66,2},{3,67},{67,3},{4,68},{68... | collective-permute-start | bytes 884744 | tf_op jit(solution)/shard_map/ppermute | solution.py:46
  14.0 1.9 %collective-permute-start.5 = (bf16[128,1152]{1,0:T(8,128)(2,1)S(1)}, bf16[128,1152]{1,0:T(8,128)(2,1)S(1)}, u32[]{:S(2)}, u32[]{:S(2)}) collective-permute-start(bf16[128,1152]{1,0:T(8,128)(2,1)S(1)} %get-tuple-element.59), channel_id=1, source_target_pairs={{0,65},{64,1},{1,64},{65,0},{2,67},{66,3},{3,66},{67,2},{4,69},{68... | collective-permute-start | bytes 884744 | tf_op jit(solution)/shard_map/ppermute | solution.py:46
  15.9 3.6 %collective-permute-done.3.refs_1_ = bf16[256,1152]{1,0:T(8,128)(2,1)S(1)} collective-permute-done((bf16[256,1152]{1,0:T(8,128)(2,1)S(1)}, bf16[256,1152]{1,0:T(8,128)(2,1)S(1)}, u32[]{:S(2)}, u32[]{:S(2)}) %collective-permute-start.3) | collective-permute-done | bytes 589856 | tf_op jit(solution)/shard_map/ppermute | solution.py:31
  19.7 2.5 %collective-permute-done.5.refs_5_ = bf16[128,1152]{1,0:T(8,128)(2,1)S(1)} collective-permute-done((bf16[128,1152]{1,0:T(8,128)(2,1)S(1)}, bf16[128,1152]{1,0:T(8,128)(2,1)S(1)}, u32[]{:S(2)}, u32[]{:S(2)}) %collective-permute-start.5) | collective-permute-done | bytes 294944 | tf_op jit(solution)/shard_map/ppermute | solution.py:46
  22.2 0.8 shard_map.69
  23.1 0.5 collective-permute-start.6
  23.6 1.5 %collective-permute-start.8 = (bf16[128,1152]{1,0:T(8,128)(2,1)}, bf16[128,1152]{1,0:T(8,128)(2,1)S(1)}, u32[]{:S(2)}, u32[]{:S(2)}) collective-permute-start(bf16[128,1152]{1,0:T(8,128)(2,1)} %get-tuple-element.62), channel_id=1, source_target_pairs={{0,8},{8,16},{16,24},{24,0},{32,56},{40,32},{48,40},{56,48},{1,9},... | collective-permute-start | bytes 884744 | tf_op jit(solution)/shard_map/ppermute | solution.py:31
  25.0 1.6 %collective-permute-start.9 = (bf16[128,1152]{1,0:T(8,128)(2,1)}, bf16[128,1152]{1,0:T(8,128)(2,1)S(1)}, u32[]{:S(2)}, u32[]{:S(2)}) collective-permute-start(bf16[128,1152]{1,0:T(8,128)(2,1)} %get-tuple-element.63), channel_id=1, source_target_pairs={{0,2},{2,4},{4,6},{6,0},{32,38},{34,32},{36,34},{38,36},{1,3},{3,5... | collective-permute-start | bytes 884744 | tf_op jit(solution)/shard_map/ppermute | solution.py:31
  26.7 3.0 %collective-permute-done.8.refs_6_ = bf16[128,1152]{1,0:T(8,128)(2,1)S(1)} collective-permute-done((bf16[128,1152]{1,0:T(8,128)(2,1)}, bf16[128,1152]{1,0:T(8,128)(2,1)S(1)}, u32[]{:S(2)}, u32[]{:S(2)}) %collective-permute-start.8) | collective-permute-done | bytes 294944 | tf_op jit(solution)/shard_map/ppermute | solution.py:31
  29.7 1.5 %collective-permute-done.9.refs_7_ = bf16[128,1152]{1,0:T(8,128)(2,1)S(1)} collective-permute-done((bf16[128,1152]{1,0:T(8,128)(2,1)}, bf16[128,1152]{1,0:T(8,128)(2,1)S(1)}, u32[]{:S(2)}, u32[]{:S(2)}) %collective-permute-start.9) | collective-permute-done | bytes 294944 | tf_op jit(solution)/shard_map/ppermute | solution.py:31
  31.1 1.1 copy-done.5
  32.2 1.2 %shard_map.70 = (bf16[256,1152]{1,0:T(8,128)(2,1)S(1)}, bf16[256,1152]{1,0:T(8,128)(2,1)S(1)}, bf16[256,1152]{1,0:T(8,128)(2,1)S(1)}, bf16[128,1152]{1,0:T(8,128...) custom-call(f32[1]{0:T(128)} %bitcast.refs_0_.refs_1_, ...), custom_call_target="tpu_custom_call", output_to_operand_aliasing={{3}: (6, {}), {4}: (7, {}), {5}: (8, {})} | custom-call | tf_op jit(solution)/shard_map/pallas_call | solution.py:59
  33.4 1.8 %collective-permute-start.11 = (bf16[256,1152]{1,0:T(8,128)(2,1)S(1)}, bf16[256,1152]{1,0:T(8,128)(2,1)S(1)}, u32[]{:S(2)}, u32[]{:S(2)}) collective-permute-start(bf16[256,1152]{1,0:T(8,128)(2,1)S(1)} %get-tuple-element.65.refs_3_.refs_2_.refs_4_), channel_id=1, source_target_pairs={{0,8},{8,16},{16,24},{24,0},{32,56},{40,32},{48,40},{56,48},{1,9},... | collective-permute-start | bytes 1769480 | tf_op jit(solution)/shard_map/ppermute | solution.py:31
  35.2 1.2 %collective-permute-start.12 = (bf16[256,1152]{1,0:T(8,128)(2,1)S(1)}, bf16[256,1152]{1,0:T(8,128)(2,1)S(1)}, u32[]{:S(2)}, u32[]{:S(2)}) collective-permute-start(bf16[256,1152]{1,0:T(8,128)(2,1)S(1)} %get-tuple-element.66), channel_id=1, source_target_pairs={{0,2},{2,4},{4,6},{6,0},{32,38},{34,32},{36,34},{38,36},{1,3},{3,5... | collective-permute-start | bytes 1769480 | tf_op jit(solution)/shard_map/ppermute | solution.py:31
  36.4 0.9 collective-permute-start.15
  37.3 1.9 %collective-permute-start.14 = (bf16[128,1152]{1,0:T(8,128)(2,1)S(1)}, bf16[128,1152]{1,0:T(8,128)(2,1)S(1)}, u32[]{:S(2)}, u32[]{:S(2)}) collective-permute-start(bf16[128,1152]{1,0:T(8,128)(2,1)S(1)} %get-tuple-element.68.refs_10_.refs_7_.refs_15_), channel_id=1, source_target_pairs={{0,65},{64,1},{1,64},{65,0},{2,67},{66,3},{3,66},{67,2},{4,69},{68... | collective-permute-start | bytes 884744 | tf_op jit(solution)/shard_map/ppermute | solution.py:46
  40.6 3.9 %shard_map.71.refs_5_ = bf16[640,1280]{1,0:T(8,128)(2,1)S(1)} custom-call(f32[2]{0:T(128)S(1)} %pad_maximum_fusion.refs_0_, f32[1]{0:T(128)} %bitcast.refs_0_.refs_1_, bf16[256,1152]{1,0:T(8,128)(2,1)S(1)} %get-tuple-element.56.refs_2_.refs_1_.refs_3_, bf16[256,1152]{1,0:T(8,128)(2,1)S(1)} %get-tuple-element.65.refs_3_.refs_2_.refs_4_, ...), custom_call_target="tpu_custom_call" | custom-call | flops 1811939328 | bytes 4423680 | tf_op jit(solution)/shard_map/pallas_call | solution.py:98
  44.5 1.4 %collective-permute-done.13.refs_2_ = bf16[128,1152]{1,0:T(8,128)(2,1)S(1)} collective-permute-done((bf16[128,1152]{1,0:T(8,128)(2,1)S(1)}, bf16[128,1152]{1,0:T(8,128)(2,1)S(1)}, u32[]{:S(2)}, u32[]{:S(2)}) %collective-permute-start.13) | collective-permute-done | bytes 294944 | tf_op jit(solution)/shard_map/ppermute | solution.py:46
  45.9 0.9 collective-permute-done.14.refs_3_
  46.8 1.6 %collective-permute-start.16 = (bf16[256,1152]{1,0:T(8,128)(2,1)S(1)}, bf16[256,1152]{1,0:T(8,128)(2,1)S(1)}, u32[]{:S(2)}, u32[]{:S(2)}) collective-permute-start(bf16[256,1152]{1,0:T(8,128)(2,1)S(1)} %get-tuple-element.72.refs_1_.refs_8_.refs_9_), channel_id=1, source_target_pairs={{0,32},{32,0},{1,33},{33,1},{2,34},{34,2},{3,35},{35,3},{4,36},{36... | collective-permute-start | bytes 1769480 | tf_op jit(solution)/shard_map/ppermute | solution.py:35
  48.4 2.0 %collective-permute-done.17.refs_4_.refs_11_.refs_12_ = bf16[128,1152]{1,0:T(8,128)(2,1)S(1)} collective-permute-done((bf16[128,1152]{1,0:T(8,128)(2,1)S(1)}, bf16[128,1152]{1,0:T(8,128)(2,1)S(1)}, u32[]{:S(2)}, u32[]{:S(2)}) %collective-permute-start.17) | collective-permute-done | bytes 294944 | tf_op jit(solution)/shard_map/ppermute | solution.py:35
  50.4 8.4 %shard_map.73 = (bf16[1024,768]{1,0:T(8,128)(2,1)S(1)}, bf16[384,1152]{1,0:T(8,128)(2,1)S(1)}, bf16[384,1152]{1,0:T(8,128)(2,1)S(1)}) custom-call(f32[2]{0:T(128)S(1)} %pad_maximum_fusion.refs_0_, bf16[256,1152]{1,0:T(8,128)(2,1)S(1)} %get-tuple-element.72.refs_1_.refs_8_.refs_9_, bf16[256,1152]{1,0:T(8,128)(2,1)S(1)} %collective-permute-done.16.refs_2_.refs_9_.refs_10_, ...), custom_call_target="tpu_custom_call" | custom-call | flops 3623878656 | bytes 4128768 | tf_op jit(solution)/shard_map/pallas_call | solution.py:98
  58.8 0.5 collective-permute-start.18
  59.2 2.9 %shard_map.74.refs_0_.refs_1_ = bf16[384,1280]{1,0:T(8,128)(2,1)S(1)} custom-call(f32[2]{0:T(128)S(1)} %pad_maximum_fusion.refs_0_, bf16[256,1152]{1,0:T(8,128)(2,1)S(1)} %get-tuple-element.56.refs_2_.refs_1_.refs_3_, bf16[256,1152]{1,0:T(8,128)(2,1)S(1)} %get-tuple-element.65.refs_3_.refs_2_.refs_4_, ...), custom_call_target="tpu_custom_call" | custom-call | flops 1207959552 | bytes 3833856 | tf_op jit(solution)/shard_map/pallas_call | solution.py:98
  62.1 5.5 %shard_map.77 = (bf16[256,1152]{1,0:T(8,128)(2,1)S(1)}, bf16[128,1152]{1,0:T(8,128)(2,1)S(1)}, bf16[128,1152]{1,0:T(8,128)(2,1)S(1)}, bf16[256,1152]{1,0:T(8,128)(2,1)S(1)}, bf16[128,1152]{1,0:T(8,128)(2,1)S(1)}) custom-call(bf16[640,1280]{1,0:T(8,128)(2,1)S(1)} %get-tuple-element.86.refs_0_, bf16[384,1280]{1,0:T(8,128)(2,1)S(1)} %shard_map.74.refs_0_.refs_1_, ...), custom_call_target="tpu_custom_call" | custom-call | flops 3019898880 | bytes 7077888 | tf_op jit(solution)/shard_map/pallas_call | solution.py:98
  67.9 3.3 %shard_map.75 = (bf16[256,1152]{1,0:T(8,128)(2,1)S(1)}, bf16[128,1152]{1,0:T(8,128)(2,1)S(1)}) custom-call(bf16[384,1280]{1,0:T(8,128)(2,1)S(1)} %shard_map.74.refs_0_.refs_1_, bf16[1024,768]{1,0:T(8,128)(2,1)S(1)} %get-tuple-element.79.refs_1_.refs_2_, bf16[256,1152]{1,0:T(8,128)(2,1)S(1)} %get-tuple-element.56.refs_2_.refs_1_.refs_3_, ...), custom_call_target="tpu_custom_call" | custom-call | flops 1811939328 | bytes 4718592 | tf_op jit(solution)/shard_map/pallas_call | solution.py:98
  71.4 0.5 collective-permute-start.19
  72.1 1.9 %collective-permute-start.22 = (bf16[128,1152]{1,0:T(8,128)(2,1)S(1)}, bf16[128,1152]{1,0:T(8,128)(2,1)S(1)}, u32[]{:S(2)}, u32[]{:S(2)}) collective-permute-start(bf16[128,1152]{1,0:T(8,128)(2,1)S(1)} %get-tuple-element.85), channel_id=1, source_target_pairs={{0,65},{64,1},{1,64},{65,0},{2,67},{66,3},{3,66},{67,2},{4,69},{68... | collective-permute-start | bytes 884744 | tf_op jit(solution)/shard_map/ppermute | solution.py:46
  74.0 5.6 %shard_map.79 = (bf16[256,1152]{1,0:T(8,128)(2,1)S(1)}, bf16[256,1152]{1,0:T(8,128)(2,1)S(1)}, bf16[256,1152]{1,0:T(8,128)(2,1)S(1)}, bf16[256,1152]{1,0:T(8,128)(2,1)S(1)}) custom-call(bf16[640,1280]{1,0:T(8,128)(2,1)S(1)} %get-tuple-element.86.refs_0_, bf16[384,1280]{1,0:T(8,128)(2,1)S(1)} %shard_map.74.refs_0_.refs_1_, ...), custom_call_target="tpu_custom_call" | custom-call | flops 3623878656 | bytes 7077888 | tf_op jit(solution)/shard_map/pallas_call | solution.py:98
  79.7 5.5 %collective-permute-start.28 = (bf16[256,1152]{1,0:T(8,128)(2,1)S(1)}, bf16[256,1152]{1,0:T(8,128)(2,1)S(1)}, u32[]{:S(2)}, u32[]{:S(2)}) collective-permute-start(bf16[256,1152]{1,0:T(8,128)(2,1)S(1)} %get-tuple-element.99), channel_id=1, source_target_pairs={{0,32},{32,0},{1,33},{33,1},{2,34},{34,2},{3,35},{35,3},{4,36},{36... | collective-permute-start | bytes 1769480 | tf_op jit(solution)/shard_map/ppermute | solution.py:35
  85.1 0.5 shard_map.78
  85.7 0.5 collective-permute-start.25
  86.8 0.5 collective-permute-done.24.refs_1_
  87.7 5.3 %collective-permute-done.26.refs_4_ = bf16[128,1152]{1,0:T(8,128)(2,1)S(1)} collective-permute-done((bf16[128,1152]{1,0:T(8,128)(2,1)S(1)}, bf16[128,1152]{1,0:T(8,128)(2,1)S(1)}, u32[]{:S(2)}, u32[]{:S(2)}) %collective-permute-start.26) | collective-permute-done | bytes 294944 | tf_op jit(solution)/shard_map/ppermute | solution.py:31
  93.7 0.6 collective-permute-start.31
  94.3 1.2 %collective-permute-start.32 = (bf16[128,1152]{1,0:T(8,128)(2,1)S(1)}, bf16[128,1152]{1,0:T(8,128)(2,1)S(1)}, u32[]{:S(2)}, u32[]{:S(2)}) collective-permute-start(bf16[128,1152]{1,0:T(8,128)(2,1)S(1)} %get-tuple-element.104), channel_id=1, source_target_pairs={{0,65},{64,1},{1,64},{65,0},{2,67},{66,3},{3,66},{67,2},{4,69},{68... | collective-permute-start | bytes 884744 | tf_op jit(solution)/shard_map/ppermute | solution.py:46
  95.6 4.0 %collective-permute-done.31.refs_3_ = bf16[128,1152]{1,0:T(8,128)(2,1)S(1)} collective-permute-done((bf16[128,1152]{1,0:T(8,128)(2,1)S(1)}, bf16[128,1152]{1,0:T(8,128)(2,1)S(1)}, u32[]{:S(2)}, u32[]{:S(2)}) %collective-permute-start.31) | collective-permute-done | bytes 294944 | tf_op jit(solution)/shard_map/ppermute | solution.py:46
  99.6 1.5 %collective-permute-done.32.refs_4_ = bf16[128,1152]{1,0:T(8,128)(2,1)S(1)} collective-permute-done((bf16[128,1152]{1,0:T(8,128)(2,1)S(1)}, bf16[128,1152]{1,0:T(8,128)(2,1)S(1)}, u32[]{:S(2)}, u32[]{:S(2)}) %collective-permute-start.32) | collective-permute-done | bytes 294944 | tf_op jit(solution)/shard_map/ppermute | solution.py:46
  101.1 2.6 %collective-permute-done.29.refs_1_ = bf16[256,1152]{1,0:T(8,128)(2,1)S(1)} collective-permute-done((bf16[256,1152]{1,0:T(8,128)(2,1)S(1)}, bf16[256,1152]{1,0:T(8,128)(2,1)S(1)}, u32[]{:S(2)}, u32[]{:S(2)}) %collective-permute-start.29) | collective-permute-done | bytes 589856 | tf_op jit(solution)/shard_map/ppermute | solution.py:31
  104.3 3.2 %collective-permute-start.33 = (bf16[128,1152]{1,0:T(8,128)(2,1)S(1)}, bf16[128,1152]{1,0:T(8,128)(2,1)S(1)}, u32[]{:S(2)}, u32[]{:S(2)}) collective-permute-start(bf16[128,1152]{1,0:T(8,128)(2,1)S(1)} %get-tuple-element.107), channel_id=1, source_target_pairs={{0,32},{32,0},{1,33},{33,1},{2,34},{34,2},{3,35},{35,3},{4,36},{36... | collective-permute-start | bytes 884744 | tf_op jit(solution)/shard_map/ppermute | solution.py:35
  108.3 0.5 collective-permute-done.33.refs_3_
  109.2 1.5 %shard_map.82 = (f32[128,1152]{1,0:T(8,128)}, f32[128,1152]{1,0:T(8,128)}) custom-call(f32[1]{0:T(128)S(6)} %div.3.refs_0_, bf16[128,1152]{1,0:T(8,128)(2,1)S(1)} %copy-done.1, f32[128,1152]{1,0:T(8,128)S(1)} %get-tuple-element.106.refs_2_, bf16[128,1152]{1,0:T(8,128)(2,1)S(1)} %collective-permute-done.33.refs_3_, bf16[128,1152]{1,0:T(8,128)(2,1)S(1)} %copy-done.3, ...), custom_call_target="tpu_custom_call" | custom-call | tf_op jit(solution)/shard_map/pallas_call | solution.py:59
  (52 shorter events, 4.8 us)
Async XLA Ops:
  0.6 2.9 %collective-permute-start = (bf16[128,1152]{1,0:T(8,128)(2,1)}, bf16[128,1152]{1,0:T(8,128)(2,1)S(1)}, u32[]{:S(2)}, u32[]{:S(2)}) collective-permute-start(bf16[128,1152]{1,0:T(8,128)(2,1)} %refs_1_.1), channel_id=1, source_target_pairs={{0,32},{32,0},{1,33},{33,1},{2,34},{34,2},{3,35},{35,3},{4,36},{36... | collective-permute-start | bytes 884744 | tf_op jit(solution)/shard_map/ppermute | solution.py:35
  2.1 1.8 %collective-permute-start.1 = (bf16[128,1152]{1,0:T(8,128)(2,1)}, bf16[128,1152]{1,0:T(8,128)(2,1)S(1)}, u32[]{:S(2)}, u32[]{:S(2)}) collective-permute-start(bf16[128,1152]{1,0:T(8,128)(2,1)} %refs_4_.1), channel_id=1, source_target_pairs={{0,32},{32,0},{1,33},{33,1},{2,34},{34,2},{3,35},{35,3},{4,36},{36... | collective-permute-start | bytes 884744 | tf_op jit(solution)/shard_map/ppermute | solution.py:35
  4.0 1.0 copy-start
  4.9 1.0 copy-start.2
  6.3 16.8 %copy-start.4 = (bf16[256,1152]{1,0:T(8,128)(2,1)}, bf16[256,1152]{1,0:T(8,128)(2,1)S(1)}, u32[]{:S(2)}) copy-start(bf16[256,1152]{1,0:T(8,128)(2,1)S(1)} %get-tuple-element.57.refs_5_) | copy-start | bytes 1769476
  6.3 9.6 %collective-permute-start.2 = (bf16[256,1152]{1,0:T(8,128)(2,1)S(1)}, bf16[256,1152]{1,0:T(8,128)(2,1)S(1)}, u32[]{:S(2)}, u32[]{:S(2)}) collective-permute-start(bf16[256,1152]{1,0:T(8,128)(2,1)S(1)} %get-tuple-element.56.refs_2_.refs_1_.refs_3_), channel_id=1, source_target_pairs={{0,8},{8,16},{16,24},{24,0},{32,56},{40,32},{48,40},{56,48},{1,9},... | collective-permute-start | bytes 1769480 | tf_op jit(solution)/shard_map/ppermute | solution.py:31
  8.9 10.6 %collective-permute-start.3 = (bf16[256,1152]{1,0:T(8,128)(2,1)S(1)}, bf16[256,1152]{1,0:T(8,128)(2,1)S(1)}, u32[]{:S(2)}, u32[]{:S(2)}) collective-permute-start(bf16[256,1152]{1,0:T(8,128)(2,1)S(1)} %get-tuple-element.57.refs_5_), channel_id=1, source_target_pairs={{0,2},{2,4},{4,6},{6,0},{32,38},{34,32},{36,34},{38,36},{1,3},{3,5... | collective-permute-start | bytes 1769480 | tf_op jit(solution)/shard_map/ppermute | solution.py:31
  12.7 7.0 %collective-permute-start.4 = (bf16[128,1152]{1,0:T(8,128)(2,1)S(1)}, bf16[128,1152]{1,0:T(8,128)(2,1)S(1)}, u32[]{:S(2)}, u32[]{:S(2)}) collective-permute-start(bf16[128,1152]{1,0:T(8,128)(2,1)S(1)} %get-tuple-element.58), channel_id=1, source_target_pairs={{0,64},{64,0},{1,65},{65,1},{2,66},{66,2},{3,67},{67,3},{4,68},{68... | collective-permute-start | bytes 884744 | tf_op jit(solution)/shard_map/ppermute | solution.py:46
  14.0 8.2 %collective-permute-start.5 = (bf16[128,1152]{1,0:T(8,128)(2,1)S(1)}, bf16[128,1152]{1,0:T(8,128)(2,1)S(1)}, u32[]{:S(2)}, u32[]{:S(2)}) collective-permute-start(bf16[128,1152]{1,0:T(8,128)(2,1)S(1)} %get-tuple-element.59), channel_id=1, source_target_pairs={{0,65},{64,1},{1,64},{65,0},{2,67},{66,3},{3,66},{67,2},{4,69},{68... | collective-permute-start | bytes 884744 | tf_op jit(solution)/shard_map/ppermute | solution.py:46
  23.1 8.1 %collective-permute-start.10 = (bf16[256,1152]{1,0:T(8,128)(2,1)S(1)}, bf16[256,1152]{1,0:T(8,128)(2,1)S(1)}, u32[]{:S(2)}, u32[]{:S(2)}) collective-permute-start(bf16[256,1152]{1,0:T(8,128)(2,1)S(1)} %get-tuple-element.64.refs_4_.refs_3_.refs_5_), channel_id=1, source_target_pairs={{0,32},{32,0},{1,33},{33,1},{2,34},{34,2},{3,35},{35,3},{4,36},{36... | collective-permute-start | bytes 1769480 | tf_op jit(solution)/shard_map/ppermute | solution.py:35
  23.1 3.6 %collective-permute-start.6 = (bf16[128,1152]{1,0:T(8,128)(2,1)S(1)}, bf16[128,1152]{1,0:T(8,128)(2,1)}, u32[]{:S(2)}, u32[]{:S(2)}) collective-permute-start(bf16[128,1152]{1,0:T(8,128)(2,1)S(1)} %get-tuple-element.60.refs_1_), channel_id=1, source_target_pairs={{0,32},{32,0},{1,33},{33,1},{2,34},{34,2},{3,35},{35,3},{4,36},{36... | collective-permute-start | bytes 884744 | tf_op jit(solution)/shard_map/ppermute | solution.py:35
  23.6 3.1 %collective-permute-start.7 = (bf16[128,1152]{1,0:T(8,128)(2,1)S(1)}, bf16[128,1152]{1,0:T(8,128)(2,1)}, u32[]{:S(2)}, u32[]{:S(2)}) collective-permute-start(bf16[128,1152]{1,0:T(8,128)(2,1)S(1)} %get-tuple-element.61.refs_3_), channel_id=1, source_target_pairs={{0,32},{32,0},{1,33},{33,1},{2,34},{34,2},{3,35},{35,3},{4,36},{36... | collective-permute-start | bytes 884744 | tf_op jit(solution)/shard_map/ppermute | solution.py:35
  23.6 6.1 %collective-permute-start.8 = (bf16[128,1152]{1,0:T(8,128)(2,1)}, bf16[128,1152]{1,0:T(8,128)(2,1)S(1)}, u32[]{:S(2)}, u32[]{:S(2)}) collective-permute-start(bf16[128,1152]{1,0:T(8,128)(2,1)} %get-tuple-element.62), channel_id=1, source_target_pairs={{0,8},{8,16},{16,24},{24,0},{32,56},{40,32},{48,40},{56,48},{1,9},... | collective-permute-start | bytes 884744 | tf_op jit(solution)/shard_map/ppermute | solution.py:31
  25.0 6.1 %collective-permute-start.9 = (bf16[128,1152]{1,0:T(8,128)(2,1)}, bf16[128,1152]{1,0:T(8,128)(2,1)S(1)}, u32[]{:S(2)}, u32[]{:S(2)}) collective-permute-start(bf16[128,1152]{1,0:T(8,128)(2,1)} %get-tuple-element.63), channel_id=1, source_target_pairs={{0,2},{2,4},{4,6},{6,0},{32,38},{34,32},{36,34},{38,36},{1,3},{3,5... | collective-permute-start | bytes 884744 | tf_op jit(solution)/shard_map/ppermute | solution.py:31
  31.1 1.1 copy-start.5
  33.4 13.3 %collective-permute-start.11 = (bf16[256,1152]{1,0:T(8,128)(2,1)S(1)}, bf16[256,1152]{1,0:T(8,128)(2,1)S(1)}, u32[]{:S(2)}, u32[]{:S(2)}) collective-permute-start(bf16[256,1152]{1,0:T(8,128)(2,1)S(1)} %get-tuple-element.65.refs_3_.refs_2_.refs_4_), channel_id=1, source_target_pairs={{0,8},{8,16},{16,24},{24,0},{32,56},{40,32},{48,40},{56,48},{1,9},... | collective-permute-start | bytes 1769480 | tf_op jit(solution)/shard_map/ppermute | solution.py:31
  35.2 11.5 %collective-permute-start.12 = (bf16[256,1152]{1,0:T(8,128)(2,1)S(1)}, bf16[256,1152]{1,0:T(8,128)(2,1)S(1)}, u32[]{:S(2)}, u32[]{:S(2)}) collective-permute-start(bf16[256,1152]{1,0:T(8,128)(2,1)S(1)} %get-tuple-element.66), channel_id=1, source_target_pairs={{0,2},{2,4},{4,6},{6,0},{32,38},{34,32},{36,34},{38,36},{1,3},{3,5... | collective-permute-start | bytes 1769480 | tf_op jit(solution)/shard_map/ppermute | solution.py:31
  36.4 4.1 %collective-permute-start.15 = (bf16[128,1152]{1,0:T(8,128)(2,1)S(1)}, bf16[128,1152]{1,0:T(8,128)(2,1)S(1)}, u32[]{:S(2)}, u32[]{:S(2)}) collective-permute-start(bf16[128,1152]{1,0:T(8,128)(2,1)S(1)} %get-tuple-element.67.refs_6_.refs_5_.refs_7_), channel_id=1, source_target_pairs={{0,32},{32,0},{1,33},{33,1},{2,34},{34,2},{3,35},{35,3},{4,36},{36... | collective-permute-start | bytes 884744 | tf_op jit(solution)/shard_map/ppermute | solution.py:35
  37.3 8.6 %collective-permute-start.13 = (bf16[128,1152]{1,0:T(8,128)(2,1)S(1)}, bf16[128,1152]{1,0:T(8,128)(2,1)S(1)}, u32[]{:S(2)}, u32[]{:S(2)}) collective-permute-start(bf16[128,1152]{1,0:T(8,128)(2,1)S(1)} %get-tuple-element.67.refs_6_.refs_5_.refs_7_), channel_id=1, source_target_pairs={{0,64},{64,0},{1,65},{65,1},{2,66},{66,2},{3,67},{67,3},{4,68},{68... | collective-permute-start | bytes 884744 | tf_op jit(solution)/shard_map/ppermute | solution.py:46
  37.3 9.5 %collective-permute-start.14 = (bf16[128,1152]{1,0:T(8,128)(2,1)S(1)}, bf16[128,1152]{1,0:T(8,128)(2,1)S(1)}, u32[]{:S(2)}, u32[]{:S(2)}) collective-permute-start(bf16[128,1152]{1,0:T(8,128)(2,1)S(1)} %get-tuple-element.68.refs_10_.refs_7_.refs_15_), channel_id=1, source_target_pairs={{0,65},{64,1},{1,64},{65,0},{2,67},{66,3},{3,66},{67,2},{4,69},{68... | collective-permute-start | bytes 884744 | tf_op jit(solution)/shard_map/ppermute | solution.py:46
  46.8 3.6 %collective-permute-start.16 = (bf16[256,1152]{1,0:T(8,128)(2,1)S(1)}, bf16[256,1152]{1,0:T(8,128)(2,1)S(1)}, u32[]{:S(2)}, u32[]{:S(2)}) collective-permute-start(bf16[256,1152]{1,0:T(8,128)(2,1)S(1)} %get-tuple-element.72.refs_1_.refs_8_.refs_9_), channel_id=1, source_target_pairs={{0,32},{32,0},{1,33},{33,1},{2,34},{34,2},{3,35},{35,3},{4,36},{36... | collective-permute-start | bytes 1769480 | tf_op jit(solution)/shard_map/ppermute | solution.py:35
  48.4 2.1 %collective-permute-start.17 = (bf16[128,1152]{1,0:T(8,128)(2,1)S(1)}, bf16[128,1152]{1,0:T(8,128)(2,1)S(1)}, u32[]{:S(2)}, u32[]{:S(2)}) collective-permute-start(bf16[128,1152]{1,0:T(8,128)(2,1)S(1)} %get-tuple-element.73.refs_3_.refs_10_.refs_11_), channel_id=1, source_target_pairs={{0,32},{32,0},{1,33},{33,1},{2,34},{34,2},{3,35},{35,3},{4,36},{36... | collective-permute-start | bytes 884744 | tf_op jit(solution)/shard_map/ppermute | solution.py:35
  58.8 12.4 %collective-permute-start.18 = (bf16[384,1152]{1,0:T(8,128)(2,1)S(1)}, bf16[384,1152]{1,0:T(8,128)(2,1)S(1)}, u32[]{:S(2)}, u32[]{:S(2)}) collective-permute-start(bf16[384,1152]{1,0:T(8,128)(2,1)S(1)} %get-tuple-element.77), channel_id=1, source_target_pairs={{0,32},{32,0},{1,33},{33,1},{2,34},{34,2},{3,35},{35,3},{4,36},{36... | collective-permute-start | bytes 2654216 | tf_op jit(solution)/shard_map/ppermute | solution.py:35
  67.7 12.0 %collective-permute-start.23 = (bf16[128,1152]{1,0:T(8,128)(2,1)S(1)}, bf16[128,1152]{1,0:T(8,128)(2,1)S(1)}, u32[]{:S(2)}, u32[]{:S(2)}) collective-permute-start(bf16[128,1152]{1,0:T(8,128)(2,1)S(1)} %get-tuple-element.89), channel_id=1, source_target_pairs={{0,32},{32,0},{1,33},{33,1},{2,34},{34,2},{3,35},{35,3},{4,36},{36... | collective-permute-start | bytes 884744 | tf_op jit(solution)/shard_map/ppermute | solution.py:35
  71.4 13.7 %collective-permute-start.19 = (bf16[256,1152]{1,0:T(8,128)(2,1)S(1)}, bf16[256,1152]{1,0:T(8,128)(2,1)S(1)}, u32[]{:S(2)}, u32[]{:S(2)}) collective-permute-start(bf16[256,1152]{1,0:T(8,128)(2,1)S(1)} %get-tuple-element.82), channel_id=1, source_target_pairs={{0,24},{8,0},{16,8},{24,16},{32,40},{40,48},{48,56},{56,32},{1,25}... | collective-permute-start | bytes 1769480 | tf_op jit(solution)/shard_map/ppermute | solution.py:31
  71.9 13.2 %collective-permute-start.20 = (bf16[256,1152]{1,0:T(8,128)(2,1)S(1)}, bf16[256,1152]{1,0:T(8,128)(2,1)S(1)}, u32[]{:S(2)}, u32[]{:S(2)}) collective-permute-start(bf16[256,1152]{1,0:T(8,128)(2,1)S(1)} %get-tuple-element.83), channel_id=1, source_target_pairs={{0,6},{2,0},{4,2},{6,4},{32,34},{34,36},{36,38},{38,32},{1,7},{3,1... | collective-permute-start | bytes 1769480 | tf_op jit(solution)/shard_map/ppermute | solution.py:31
  71.9 13.2 %collective-permute-start.21 = (bf16[128,1152]{1,0:T(8,128)(2,1)S(1)}, bf16[128,1152]{1,0:T(8,128)(2,1)S(1)}, u32[]{:S(2)}, u32[]{:S(2)}) collective-permute-start(bf16[128,1152]{1,0:T(8,128)(2,1)S(1)} %get-tuple-element.84), channel_id=1, source_target_pairs={{0,64},{64,0},{1,65},{65,1},{2,66},{66,2},{3,67},{67,3},{4,68},{68... | collective-permute-start | bytes 884744 | tf_op jit(solution)/shard_map/ppermute | solution.py:46
  72.1 13.0 %collective-permute-start.22 = (bf16[128,1152]{1,0:T(8,128)(2,1)S(1)}, bf16[128,1152]{1,0:T(8,128)(2,1)S(1)}, u32[]{:S(2)}, u32[]{:S(2)}) collective-permute-start(bf16[128,1152]{1,0:T(8,128)(2,1)S(1)} %get-tuple-element.85), channel_id=1, source_target_pairs={{0,65},{64,1},{1,64},{65,0},{2,67},{66,3},{3,66},{67,2},{4,69},{68... | collective-permute-start | bytes 884744 | tf_op jit(solution)/shard_map/ppermute | solution.py:46
  79.7 7.1 %collective-permute-start.28 = (bf16[256,1152]{1,0:T(8,128)(2,1)S(1)}, bf16[256,1152]{1,0:T(8,128)(2,1)S(1)}, u32[]{:S(2)}, u32[]{:S(2)}) collective-permute-start(bf16[256,1152]{1,0:T(8,128)(2,1)S(1)} %get-tuple-element.99), channel_id=1, source_target_pairs={{0,32},{32,0},{1,33},{33,1},{2,34},{34,2},{3,35},{35,3},{4,36},{36... | collective-permute-start | bytes 1769480 | tf_op jit(solution)/shard_map/ppermute | solution.py:35
  85.6 1.7 %collective-permute-start.24 = (bf16[128,1152]{1,0:T(8,128)(2,1)S(1)}, bf16[128,1152]{1,0:T(8,128)(2,1)S(1)}, u32[]{:S(2)}, u32[]{:S(2)}) collective-permute-start(bf16[128,1152]{1,0:T(8,128)(2,1)S(1)} %get-tuple-element.93), channel_id=1, source_target_pairs={{0,32},{32,0},{1,33},{33,1},{2,34},{34,2},{3,35},{35,3},{4,36},{36... | collective-permute-start | bytes 884744 | tf_op jit(solution)/shard_map/ppermute | solution.py:35
  85.7 2.0 %collective-permute-start.25 = (bf16[128,1152]{1,0:T(8,128)(2,1)S(1)}, bf16[128,1152]{1,0:T(8,128)(2,1)S(1)}, u32[]{:S(2)}, u32[]{:S(2)}) collective-permute-start(bf16[128,1152]{1,0:T(8,128)(2,1)S(1)} %get-tuple-element.95), channel_id=1, source_target_pairs={{0,32},{32,0},{1,33},{33,1},{2,34},{34,2},{3,35},{35,3},{4,36},{36... | collective-permute-start | bytes 884744 | tf_op jit(solution)/shard_map/ppermute | solution.py:35
  86.2 6.8 %collective-permute-start.26 = (bf16[128,1152]{1,0:T(8,128)(2,1)S(1)}, bf16[128,1152]{1,0:T(8,128)(2,1)S(1)}, u32[]{:S(2)}, u32[]{:S(2)}) collective-permute-start(bf16[128,1152]{1,0:T(8,128)(2,1)S(1)} %get-tuple-element.96), channel_id=1, source_target_pairs={{0,24},{8,0},{16,8},{24,16},{32,40},{40,48},{48,56},{56,32},{1,25}... | collective-permute-start | bytes 884744 | tf_op jit(solution)/shard_map/ppermute | solution.py:31
  86.2 6.8 %collective-permute-start.27 = (bf16[128,1152]{1,0:T(8,128)(2,1)S(1)}, bf16[128,1152]{1,0:T(8,128)(2,1)S(1)}, u32[]{:S(2)}, u32[]{:S(2)}) collective-permute-start(bf16[128,1152]{1,0:T(8,128)(2,1)S(1)} %get-tuple-element.97), channel_id=1, source_target_pairs={{0,6},{2,0},{4,2},{6,4},{32,34},{34,36},{36,38},{38,32},{1,7},{3,1... | collective-permute-start | bytes 884744 | tf_op jit(solution)/shard_map/ppermute | solution.py:31
  93.4 15.8 %copy-start.1 = (bf16[128,1152]{1,0:T(8,128)(2,1)S(1)}, bf16[128,1152]{1,0:T(8,128)(2,1)}, u32[]{:S(2)}) copy-start(bf16[128,1152]{1,0:T(8,128)(2,1)} %refs_1_.1) | copy-start | bytes 884740
  93.4 15.8 %copy-start.3 = (bf16[128,1152]{1,0:T(8,128)(2,1)S(1)}, bf16[128,1152]{1,0:T(8,128)(2,1)}, u32[]{:S(2)}) copy-start(bf16[128,1152]{1,0:T(8,128)(2,1)} %refs_4_.1) | copy-start | bytes 884740
  93.4 10.3 %collective-permute-start.29 = (bf16[256,1152]{1,0:T(8,128)(2,1)S(1)}, bf16[256,1152]{1,0:T(8,128)(2,1)S(1)}, u32[]{:S(2)}, u32[]{:S(2)}) collective-permute-start(bf16[256,1152]{1,0:T(8,128)(2,1)S(1)} %get-tuple-element.101), channel_id=1, source_target_pairs={{0,24},{8,0},{16,8},{24,16},{32,40},{40,48},{48,56},{56,32},{1,25}... | collective-permute-start | bytes 1769480 | tf_op jit(solution)/shard_map/ppermute | solution.py:31
  93.7 10.2 %collective-permute-start.30 = (bf16[256,1152]{1,0:T(8,128)(2,1)S(1)}, bf16[256,1152]{1,0:T(8,128)(2,1)S(1)}, u32[]{:S(2)}, u32[]{:S(2)}) collective-permute-start(bf16[256,1152]{1,0:T(8,128)(2,1)S(1)} %get-tuple-element.102), channel_id=1, source_target_pairs={{0,6},{2,0},{4,2},{6,4},{32,34},{34,36},{36,38},{38,32},{1,7},{3,1... | collective-permute-start | bytes 1769480 | tf_op jit(solution)/shard_map/ppermute | solution.py:31
  93.7 5.9 %collective-permute-start.31 = (bf16[128,1152]{1,0:T(8,128)(2,1)S(1)}, bf16[128,1152]{1,0:T(8,128)(2,1)S(1)}, u32[]{:S(2)}, u32[]{:S(2)}) collective-permute-start(bf16[128,1152]{1,0:T(8,128)(2,1)S(1)} %get-tuple-element.103), channel_id=1, source_target_pairs={{0,64},{64,0},{1,65},{65,1},{2,66},{66,2},{3,67},{67,3},{4,68},{68... | collective-permute-start | bytes 884744 | tf_op jit(solution)/shard_map/ppermute | solution.py:46
  94.3 6.8 %collective-permute-start.32 = (bf16[128,1152]{1,0:T(8,128)(2,1)S(1)}, bf16[128,1152]{1,0:T(8,128)(2,1)S(1)}, u32[]{:S(2)}, u32[]{:S(2)}) collective-permute-start(bf16[128,1152]{1,0:T(8,128)(2,1)S(1)} %get-tuple-element.104), channel_id=1, source_target_pairs={{0,65},{64,1},{1,64},{65,0},{2,67},{66,3},{3,66},{67,2},{4,69},{68... | collective-permute-start | bytes 884744 | tf_op jit(solution)/shard_map/ppermute | solution.py:46
  104.3 4.5 %collective-permute-start.33 = (bf16[128,1152]{1,0:T(8,128)(2,1)S(1)}, bf16[128,1152]{1,0:T(8,128)(2,1)S(1)}, u32[]{:S(2)}, u32[]{:S(2)}) collective-permute-start(bf16[128,1152]{1,0:T(8,128)(2,1)S(1)} %get-tuple-element.107), channel_id=1, source_target_pairs={{0,32},{32,0},{1,33},{33,1},{2,34},{34,2},{3,35},{35,3},{4,36},{36... | collective-permute-start | bytes 884744 | tf_op jit(solution)/shard_map/ppermute | solution.py:35
  107.6 1.6 %collective-permute-start.34 = (bf16[128,1152]{1,0:T(8,128)(2,1)S(1)}, bf16[128,1152]{1,0:T(8,128)(2,1)S(1)}, u32[]{:S(2)}, u32[]{:S(2)}) collective-permute-start(bf16[128,1152]{1,0:T(8,128)(2,1)S(1)} %get-tuple-element.109), channel_id=1, source_target_pairs={{0,32},{32,0},{1,33},{33,1},{2,34},{34,2},{3,35},{35,3},{4,36},{36... | collective-permute-start | bytes 884744 | tf_op jit(solution)/shard_map/ppermute | solution.py:35

commit v3 on v0

v3 whole, which is shorter than its diff:
```python
import functools
import math

import jax
import jax.numpy as jnp
import numpy as np
from jax import lax
from jax.experimental import pallas as pl
from jax.experimental.pallas import tpu as pltpu
from jax.sharding import Mesh
from jax.sharding import PartitionSpec as P

FINE_AXES = ("y_lo", "core", "x", "z", "y_hi")
FINE_SIZES = (2, 2, 4, 4, 2)
RING = 4
VMEM_BYTES = 32 * 1024 * 1024
HALF = jnp.bfloat16
FULL = jnp.float32

VMEM = pl.BlockSpec(memory_space=pltpu.VMEM)
SMEM = pl.BlockSpec(memory_space=pltpu.SMEM)
ANY = pl.BlockSpec(memory_space=pl.ANY)
PARAMS = pltpu.CompilerParams(vmem_limit_bytes=VMEM_BYTES)

WAYS = ((2, 1), (1, 1), (3, 1), (2, 0), (1, 0), (3, 0), (0, 1))


def place(core, x, y, z):
    return int(np.ravel_multi_index((y % 2, core, x, z, y // 2), FINE_SIZES))


def mate(core, y):
    if core == 0:
        return y ^ 1
    return (y + 1) % RING if y % 2 else (y - 1) % RING


def ring_gather(shard):
    groups = []
    for y in range(RING):
        for k in range(RING):
            groups.append([place(0, x, y, k) for x in range(RING)])
            groups.append([place(1, k, y, z) for z in range(RING)])
    return lax.all_gather(shard, FINE_AXES, axis=0, tiled=True, axis_index_groups=groups)


def sent(value, steps, across):
    pairs = []
    for x, y, z in np.ndindex(RING, RING, RING):
        for core in range(2):
            to_y = mate(core, y) if across else y
            to_x = (x + steps) % RING if core == 0 else x
            to_z = (z + steps) % RING if core == 1 else z
            pairs.append((place(core, x, y, z), place(core, to_x, to_y, to_z)))
    return lax.ppermute(value, FINE_AXES, pairs)


def other_core(value):
    return lax.ppermute(value, "core", [(0, 1), (1, 0)])


def dot(a, b, contract):
    return lax.dot_general(a, b, ((contract[:1], contract[1:]), ((), ())), preferred_element_type=FULL)


def unit_rows(raw):
    values = raw.astype(FULL)
    scale = lax.rsqrt(jnp.mean(values * values, axis=1, keepdims=True) + 1e-06) / math.sqrt(
        values.shape[1]
    )
    return values * scale, scale


def normalize_kernel(info, images, texts, there, raw, first, second, both):
    rows = images.shape[0]
    is_first = info[0] == 0
    here = jnp.where(is_first, images[...].astype(FULL), texts[...].astype(FULL)).astype(HALF)
    raw[pl.ds(info[0] * rows, rows), :] = here
    raw[pl.ds((1 - info[0]) * rows, rows), :] = there[...]
    unit = unit_rows(raw[...])[0].astype(HALF)
    first[...] = unit[:rows]
    second[...] = unit[rows:]
    both[...] = unit


def part_kernel(steps, own, n_after, info, affine, mine_a, mine_b, *refs):
    theirs, refs = refs[:4], refs[4 + n_after :]
    part, coupling = refs
    count = mine_a.shape[0]
    rows = count // RING
    at = pl.ds(pl.multiple_of(lax.rem(info[1] + steps, RING) * rows, rows), rows)
    mine = jnp.concatenate([mine_a[at, :], mine_b[at, :]], 0)
    for k, piece in enumerate(theirs):
        energies = dot(mine, piece[...], (1, 1))
        tile = 0.5 * jnp.tanh(affine[0] * energies + affine[1]) + 0.5
        if own and k < 2:
            row = lax.broadcasted_iota(jnp.int32, tile.shape, 0)
            column = lax.broadcasted_iota(jnp.int32, tile.shape, 1)
            same = (row - k * rows == column - info[2] * rows) & (row // rows == k)
            tile = tile - jnp.where(same, 1.0, 0.0)
        coupling[:, pl.ds(k * count, count)] = tile.astype(HALF)
    total = None
    for k, piece in enumerate(theirs):
        term = dot(coupling[:, pl.ds(k * count, count)], piece[...], (1, 0))
        total = term if total is None else total + term
    part[...] = total.astype(HALF)


def part_of(steps, own, info, affine, mine, theirs, after):
    count, width = theirs[0].shape
    unit = 2 * count // RING
    return pl.pallas_call(
        functools.partial(part_kernel, steps, own, len(after)),
        out_shape=jax.ShapeDtypeStruct((unit, width), HALF),
        in_specs=[SMEM, SMEM] + [VMEM] * 6 + [ANY] * len(after),
        out_specs=VMEM,
        scratch_shapes=[pltpu.VMEM((unit, 4 * count), HALF)],
        cost_estimate=pl.CostEstimate(
            flops=16 * unit * count * width,
            bytes_accessed=2 * unit * width,
            transcendentals=4 * unit * count,
        ),
        compiler_params=PARAMS,
    )(info, affine, *mine, *theirs, *after)


def finish_kernel(info, multiplier, raw, *refs):
    parts, (here, there, grads) = refs[:-3], refs[-3:]
    rows = here.shape[0]
    total = parts[0][...].astype(FULL)
    for part in parts[1:]:
        total = total + part[...].astype(FULL)
    unit, scale = unit_rows(raw[...])
    grad = multiplier[0] * total
    grads[...] = scale * (grad - unit * jnp.sum(unit * grad, axis=1, keepdims=True))
    here[...] = grads[pl.ds(info[0] * rows, rows), :]
    there[...] = grads[pl.ds((1 - info[0]) * rows, rows), :]


def on_device(
    picture_vectors_raw, caption_vectors_raw, logit_multiplier, offset_term, incoming_adjoint
):
    rows, width = picture_vectors_raw.shape
    pairs = rows * math.prod(FINE_SIZES)
    core, x, z = (lax.axis_index(name) for name in ("core", "x", "z"))
    is_first = core == 0
    info = jnp.stack([core, jnp.where(is_first, x, z), jnp.where(is_first, z, x)]).astype(jnp.int32)
    affine = jnp.concatenate([0.5 * logit_multiplier, 0.5 * offset_term])
    multiplier = incoming_adjoint * logit_multiplier / pairs
    shard = jax.ShapeDtypeStruct((rows, width), HALF)
    unit = jax.ShapeDtypeStruct((2 * rows, width), HALF)
    shard_full = jax.ShapeDtypeStruct((rows, width), FULL)

    raw_there = other_core(jnp.where(is_first, caption_vectors_raw, picture_vectors_raw))
    raw, own_a, own_b, own = pl.pallas_call(
        normalize_kernel,
        out_shape=[unit, shard, shard, unit],
        in_specs=[SMEM] + [VMEM] * 3,
        out_specs=[VMEM] * 4,
        compiler_params=PARAMS,
    )(info, picture_vectors_raw, caption_vectors_raw, raw_there)

    partner = sent(own, 0, True)
    near = [ring_gather(own_a), ring_gather(own_b)]
    near_there = [other_core(piece) for piece in near]
    far = [ring_gather(partner[:rows]), ring_gather(partner[rows:])]
    far_there = [other_core(piece) for piece in far]
    theirs = near_there + far_there

    arrived = []
    for k, (steps, across) in enumerate(WAYS):
        after = arrived[k - 4 : k - 3] if k >= 4 else []
        mine = far if across else near
        part = part_of(steps, False, info, affine, mine, theirs, after)
        arrived.append(sent(part, steps, across))
    own_part = part_of(0, True, info, affine, near, theirs, arrived[3:4])

    here, there = pl.pallas_call(
        finish_kernel,
        out_shape=[shard_full, shard_full],
        in_specs=[SMEM, SMEM] + [VMEM] * (2 + len(arrived)),
        out_specs=[VMEM] * 2,
        scratch_shapes=[pltpu.VMEM((2 * rows, width), FULL)],
        compiler_params=PARAMS,
    )(info, multiplier, raw, own_part, *arrived)
    back = other_core(there)
    return (jnp.where(is_first, here, back), jnp.where(is_first, back, here))


def solution(mesh):
    fine = Mesh(mesh.devices.reshape(FINE_SIZES), FINE_AXES)
    rows = P(FINE_AXES, None)
    return jax.shard_map(
        on_device,
        mesh=fine,
        in_specs=(rows, rows, P(), P(), P()),
        out_specs=(rows, rows),
        check_vma=False,
    )
```

time: 447 us -> 187 us (0.42)
  waiting for transfers between devices: 360 us -> 98 us
  matrix products: 42.7 us -> 0 us
  Pallas kernels: 0 us -> 37.4 us
  starting transfers between devices: 17 us -> 27.2 us
  other arithmetic: 9.91 us -> 2.25 us
  local copies, waits for them, and re-layouts: 0.05 us -> 5.37 us
    reduce_scatter x1 -> x0, waiting for transfers between devices: 218 us -> none  [on_device(): lax.psum_scatter(column_term(all_tiles, all_rows), 'grp', scatter_dimensi...]
    dot_general x9 -> x0, matrix products: 42.7 us -> none  [the longest x4 18 us: assemble_interaction(): lax.dot_general(first_operand_lines, second_operand_lines, (((1,), (1,)),...]
    pallas_call x0 -> x10, Pallas kernels: none -> 37.4 us  [the longest x8 34.1 us: part_of(): pl.pallas_call(functools.partial(part_kernel, steps, own, len(after)), ou...]
    ppermute x7 -> x14, waiting for transfers between devices: 44.2 us -> 16.7 us  [the longest x8 12.3 us: sent(): return lax.ppermute(value, FINE_AXES, pairs)]
    all_gather x1 -> x4, waiting for transfers between devices: 97.6 us -> 80 us  [ring_gather(): lax.all_gather(shard, FINE_AXES, axis=0, tiled=True, axis_index_groups=gr...]
    ppermute x7 -> x14, starting transfers between devices: 16.9 us -> 27.1 us  [the longest x8 16.5 us: sent(): return lax.ppermute(value, FINE_AXES, pairs)]
  transfers between devices with their start and end apart: 9 -> 18, of which waited for: 8 -> 9; matrix products, arithmetic and copies ran while one was open for 7% -> 1% of each run, Pallas kernels for 0% -> 16%
where the time goes in v3:
time: 187 us; the launch traced here: 186 us
  waiting for transfers between devices  98 us (52%)
  Pallas kernels  37.4 us (20%)
  starting transfers between devices  27.2 us (15%)
  between operations  15.9 us (9%)
  local copies, waits for them, and re-layouts  5.37 us (3%)
  other arithmetic  2.25 us (1%)
    all_gather x4, waiting for transfers between devices, ring_gather(): lax.all_gather(shard, FINE_AXES, axis=0, tiled=True, axis_index_groups=gr...  80 us
    pallas_call x8, Pallas kernels, part_of(): pl.pallas_call(functools.partial(part_kernel, steps, own, len(after)), ou...  34.1 us
    ppermute x8, starting transfers between devices, sent(): return lax.ppermute(value, FINE_AXES, pairs)  16.5 us
    ppermute x8, waiting for transfers between devices, sent(): return lax.ppermute(value, FINE_AXES, pairs)  12.3 us
    ppermute x6, starting transfers between devices, other_core(): return lax.ppermute(value, 'core', [(0, 1), (1, 0)])  10.6 us
    unnamed x16, local copies, waits for them, and re-layouts  4.48 us
    ppermute x6, waiting for transfers between devices, other_core(): return lax.ppermute(value, 'core', [(0, 1), (1, 0)])  4.43 us
  transfers between devices with their start and end apart: 18, of which 9 were waited for; matrix products, arithmetic and copies ran while one was open for 1% of the time, Pallas kernels for 16%

profile of v3, /device:TPU:1, one launch (start us, length us, event | category | flops | bytes accessed | tf_op | source)
XLA Modules:
  0.0 186.1 jit_solution(6933375303266239333)
XLA Ops:
  7.2 0.0 all-gather.5.cloned.1.call-start
  7.2 1.0 broadcast_select_fusion.2
  8.2 1.5 collective-permute-start
  9.7 0.1 pad_add_fusion.info
  9.8 1.1 collective-permute-done.there
  10.9 1.0 copy-done
  11.9 1.0 copy-done.1
  12.9 1.7 shard_map.68
  14.6 0.0 all-gather.7.cloned.1.call-start
  14.6 0.7 all-gather.7.cloned.1.call-update
  15.3 0.0 all-gather.9.cloned.1.call-start
  15.4 2.9 %collective-permute-start.3 = (bf16[256,1152]{1,0:T(8,128)(2,1)S(1)}, bf16[256,1152]{1,0:T(8,128)(2,1)S(1)}, u32[]{:S(2)}, u32[]{:S(2)}) collective-permute-start(bf16[256,1152]{1,0:T(8,128)(2,1)S(1)} %get-tuple-element.11), channel_id=1, source_target_pairs={{0,64},{32,97},{2,66},{34,99},{4,68},{36,101},{6,70},{38,103},{64,... | collective-permute-start | bytes 1769480 | tf_op jit(solution)/shard_map/ppermute | solution.py:55
  18.3 7.3 %collective-permute-done.3 = bf16[256,1152]{1,0:T(8,128)(2,1)S(1)} collective-permute-done((bf16[256,1152]{1,0:T(8,128)(2,1)S(1)}, bf16[256,1152]{1,0:T(8,128)(2,1)S(1)}, u32[]{:S(2)}, u32[]{:S(2)}) %collective-permute-start.3) | collective-permute-done | bytes 589856 | tf_op jit(solution)/shard_map/ppermute | solution.py:55
  25.5 0.9 fusion
  26.4 0.0 all-gather.11.cloned.1.call-start
  26.5 0.5 all-gather.11.cloned.1.call-update
  27.0 11.4 %all-gather.5.cloned.1.call-done.mine_a = bf16[512,1152]{1,0:T(8,128)(2,1)} async-done(((bf16[128,1152]{1,0:T(8,128)(2,1)}), bf16[512,1152]{1,0:T(8,128)(2,1)}) %all-gather.5.cloned.1.call-update) | async-done | bytes 1179664 | tf_op jit(solution)/shard_map/all_gather | solution.py:44
  38.5 2.3 %collective-permute-start.1 = (bf16[512,1152]{1,0:T(8,128)(2,1)}, bf16[512,1152]{1,0:T(8,128)(2,1)S(1)}, u32[]{:S(2)}, u32[]{:S(2)}) collective-permute-start(bf16[512,1152]{1,0:T(8,128)(2,1)} %all-gather.5.cloned.1.call-done.mine_a), channel_id=1, source_target_pairs={{0,32},{32,0},{1,33},{33,1},{2,34},{34,2},{3,35},{35,3},{4,36},{36... | collective-permute-start | bytes 3538952 | tf_op jit(solution)/shard_map/ppermute | solution.py:59
  40.7 23.3 %all-gather.7.cloned.1.call-done.mine_b = bf16[512,1152]{1,0:T(8,128)(2,1)} async-done(((bf16[128,1152]{1,0:T(8,128)(2,1)}), bf16[512,1152]{1,0:T(8,128)(2,1)}) %all-gather.7.cloned.1.call-update) | async-done | bytes 1179664 | tf_op jit(solution)/shard_map/all_gather | solution.py:44
  64.0 2.3 %collective-permute-start.2 = (bf16[512,1152]{1,0:T(8,128)(2,1)}, bf16[512,1152]{1,0:T(8,128)(2,1)S(1)}, u32[]{:S(2)}, u32[]{:S(2)}) collective-permute-start(bf16[512,1152]{1,0:T(8,128)(2,1)} %all-gather.7.cloned.1.call-done.mine_b), channel_id=1, source_target_pairs={{0,32},{32,0},{1,33},{33,1},{2,34},{34,2},{3,35},{35,3},{4,36},{36... | collective-permute-start | bytes 3538952 | tf_op jit(solution)/shard_map/ppermute | solution.py:59
  66.2 22.7 %all-gather.9.cloned.1.call-done.mine_a = bf16[512,1152]{1,0:T(8,128)(2,1)} async-done(((bf16[128,1152]{1,0:T(8,128)(2,1)}), bf16[512,1152]{1,0:T(8,128)(2,1)}) %all-gather.9.cloned.1.call-update) | async-done | bytes 1179664 | tf_op jit(solution)/shard_map/all_gather | solution.py:44
  89.0 2.3 %collective-permute-start.4 = (bf16[512,1152]{1,0:T(8,128)(2,1)}, bf16[512,1152]{1,0:T(8,128)(2,1)}, u32[]{:S(2)}, u32[]{:S(2)}) collective-permute-start(bf16[512,1152]{1,0:T(8,128)(2,1)} %all-gather.9.cloned.1.call-done.mine_a), channel_id=1, source_target_pairs={{0,32},{32,0},{1,33},{33,1},{2,34},{34,2},{3,35},{35,3},{4,36},{36... | collective-permute-start | bytes 3538952 | tf_op jit(solution)/shard_map/ppermute | solution.py:59
  91.2 22.6 %all-gather.11.cloned.1.call-done.mine_b = bf16[512,1152]{1,0:T(8,128)(2,1)} async-done(((bf16[128,1152]{1,0:T(8,128)(2,1)}), bf16[512,1152]{1,0:T(8,128)(2,1)}) %all-gather.11.cloned.1.call-update) | async-done | bytes 1179664 | tf_op jit(solution)/shard_map/all_gather | solution.py:44
  113.8 2.3 %collective-permute-start.5 = (bf16[512,1152]{1,0:T(8,128)(2,1)}, bf16[512,1152]{1,0:T(8,128)(2,1)S(1)}, u32[]{:S(2)}, u32[]{:S(2)}) collective-permute-start(bf16[512,1152]{1,0:T(8,128)(2,1)} %all-gather.11.cloned.1.call-done.mine_b), channel_id=1, source_target_pairs={{0,32},{32,0},{1,33},{33,1},{2,34},{34,2},{3,35},{35,3},{4,36},{36... | collective-permute-start | bytes 3538952 | tf_op jit(solution)/shard_map/ppermute | solution.py:59
  117.3 0.1 pad_maximum_fusion.affine
  117.4 1.3 collective-permute-done.5.refs_3_
  118.7 1.3 copy-done.4
  120.0 1.3 copy-done.6
  121.3 4.4 %shard_map.73 = bf16[256,1152]{1,0:T(8,128)(2,1)S(1)} custom-call(s32[3]{0:T(128)S(1)} %pad_add_fusion.info, f32[2]{0:T(128)S(1)} %pad_maximum_fusion.affine, bf16[512,1152]{1,0:T(8,128)(2,1)S(1)} %copy-done.4, bf16[512,1152]{1,0:T(8,128)(2,1)S(1)} %copy-done.6, bf16[512,1152]{1,0:T(8,128)(2,1)S(1)} %collective-permute-done.1.refs_0_, ...), custom_call_target="tpu_custom_call" | custom-call | flops 2415919104 | bytes 589824 | tf_op jit(solution)/shard_map/pallas_call | solution.py:112
  125.6 4.9 %collective-permute-start.9 = (bf16[256,1152]{1,0:T(8,128)(2,1)S(1)}, bf16[256,1152]{1,0:T(8,128)(2,1)S(1)}, u32[]{:S(2)}, u32[]{:S(2)}) collective-permute-start(bf16[256,1152]{1,0:T(8,128)(2,1)S(1)} %shard_map.73), channel_id=1, source_target_pairs={{0,88},{32,103},{2,90},{34,97},{4,92},{36,99},{6,94},{38,101},{64,... | collective-permute-start | bytes 1769480 | tf_op jit(solution)/shard_map/ppermute | solution.py:55
  130.6 4.2 %shard_map.72 = bf16[256,1152]{1,0:T(8,128)(2,1)S(1)} custom-call(s32[3]{0:T(128)S(1)} %pad_add_fusion.info, f32[2]{0:T(128)S(1)} %pad_maximum_fusion.affine, bf16[512,1152]{1,0:T(8,128)(2,1)S(1)} %copy-done.5, bf16[512,1152]{1,0:T(8,128)(2,1)S(1)} %copy-done.7, bf16[512,1152]{1,0:T(8,128)(2,1)S(1)} %collective-permute-done.1.refs_0_, ...), custom_call_target="tpu_custom_call" | custom-call | flops 2415919104 | bytes 589824 | tf_op jit(solution)/shard_map/pallas_call | solution.py:112
  134.8 0.1 collective-permute-start.8
  134.9 4.4 %shard_map.71 = bf16[256,1152]{1,0:T(8,128)(2,1)S(1)} custom-call(s32[3]{0:T(128)S(1)} %pad_add_fusion.info, f32[2]{0:T(128)S(1)} %pad_maximum_fusion.affine, bf16[512,1152]{1,0:T(8,128)(2,1)S(1)} %copy-done.5, bf16[512,1152]{1,0:T(8,128)(2,1)S(1)} %copy-done.7, bf16[512,1152]{1,0:T(8,128)(2,1)S(1)} %collective-permute-done.1.refs_0_, ...), custom_call_target="tpu_custom_call" | custom-call | flops 2415919104 | bytes 589824 | tf_op jit(solution)/shard_map/pallas_call | solution.py:112
  139.3 3.9 %collective-permute-start.7 = (bf16[256,1152]{1,0:T(8,128)(2,1)S(1)}, bf16[256,1152]{1,0:T(8,128)(2,1)S(1)}, u32[]{:S(2)}, u32[]{:S(2)}) collective-permute-start(bf16[256,1152]{1,0:T(8,128)(2,1)S(1)} %shard_map.71), channel_id=1, source_target_pairs={{0,80},{32,101},{2,82},{34,103},{4,84},{36,97},{6,86},{38,99},{64,... | collective-permute-start | bytes 1769480 | tf_op jit(solution)/shard_map/ppermute | solution.py:55
  143.1 4.2 %shard_map.69 = bf16[256,1152]{1,0:T(8,128)(2,1)S(1)} custom-call(s32[3]{0:T(128)S(1)} %pad_add_fusion.info, f32[2]{0:T(128)S(1)} %pad_maximum_fusion.affine, bf16[512,1152]{1,0:T(8,128)(2,1)S(1)} %copy-done.2, bf16[512,1152]{1,0:T(8,128)(2,1)S(1)} %copy-done.3, bf16[512,1152]{1,0:T(8,128)(2,1)S(1)} %collective-permute-done.1.refs_0_, ...), custom_call_target="tpu_custom_call" | custom-call | flops 2415919104 | bytes 589824 | tf_op jit(solution)/shard_map/pallas_call | solution.py:112
  147.4 0.2 collective-permute-start.6
  147.6 4.2 %shard_map.76 = bf16[256,1152]{1,0:T(8,128)(2,1)S(1)} custom-call(s32[3]{0:T(128)S(1)} %pad_add_fusion.info, f32[2]{0:T(128)S(1)} %pad_maximum_fusion.affine, bf16[512,1152]{1,0:T(8,128)(2,1)S(1)} %copy-done.5, bf16[512,1152]{1,0:T(8,128)(2,1)S(1)} %copy-done.7, bf16[512,1152]{1,0:T(8,128)(2,1)S(1)} %collective-permute-done.1.refs_0_, ...), custom_call_target="tpu_custom_call" | custom-call | flops 2415919104 | bytes 589824 | tf_op jit(solution)/shard_map/pallas_call | solution.py:112
  151.8 1.7 collective-permute-start.12
  153.5 4.2 %shard_map.75 = bf16[256,1152]{1,0:T(8,128)(2,1)S(1)} custom-call(s32[3]{0:T(128)S(1)} %pad_add_fusion.info, f32[2]{0:T(128)S(1)} %pad_maximum_fusion.affine, bf16[512,1152]{1,0:T(8,128)(2,1)S(1)} %copy-done.2, bf16[512,1152]{1,0:T(8,128)(2,1)S(1)} %copy-done.3, bf16[512,1152]{1,0:T(8,128)(2,1)S(1)} %collective-permute-done.1.refs_0_, ...), custom_call_target="tpu_custom_call" | custom-call | flops 2415919104 | bytes 589824 | tf_op jit(solution)/shard_map/pallas_call | solution.py:112
  157.7 2.5 %collective-permute-start.11 = (bf16[256,1152]{1,0:T(8,128)(2,1)S(1)}, bf16[256,1152]{1,0:T(8,128)(2,1)S(1)}, u32[]{:S(2)}, u32[]{:S(2)}) collective-permute-start(bf16[256,1152]{1,0:T(8,128)(2,1)S(1)} %shard_map.75), channel_id=1, source_target_pairs={{0,24},{32,38},{2,26},{34,32},{4,28},{36,34},{6,30},{38,36},{64,88... | collective-permute-start | bytes 1769480 | tf_op jit(solution)/shard_map/ppermute | solution.py:55
  160.2 4.2 %shard_map.74 = bf16[256,1152]{1,0:T(8,128)(2,1)S(1)} custom-call(s32[3]{0:T(128)S(1)} %pad_add_fusion.info, f32[2]{0:T(128)S(1)} %pad_maximum_fusion.affine, bf16[512,1152]{1,0:T(8,128)(2,1)S(1)} %copy-done.2, bf16[512,1152]{1,0:T(8,128)(2,1)S(1)} %copy-done.3, bf16[512,1152]{1,0:T(8,128)(2,1)S(1)} %collective-permute-done.1.refs_0_, ...), custom_call_target="tpu_custom_call" | custom-call | flops 2415919104 | bytes 589824 | tf_op jit(solution)/shard_map/pallas_call | solution.py:112
  164.5 0.3 collective-permute-start.10
  165.4 4.2 %shard_map.70.refs_0_ = bf16[256,1152]{1,0:T(8,128)(2,1)S(1)} custom-call(s32[3]{0:T(128)S(1)} %pad_add_fusion.info, f32[2]{0:T(128)S(1)} %pad_maximum_fusion.affine, bf16[512,1152]{1,0:T(8,128)(2,1)S(1)} %copy-done.2, bf16[512,1152]{1,0:T(8,128)(2,1)S(1)} %copy-done.3, bf16[512,1152]{1,0:T(8,128)(2,1)S(1)} %collective-permute-done.1.refs_0_, ...), custom_call_target="tpu_custom_call" | custom-call | flops 2415919104 | bytes 589824 | tf_op jit(solution)/shard_map/pallas_call | solution.py:112
  169.7 5.0 %collective-permute-done.10.refs_5_ = bf16[256,1152]{1,0:T(8,128)(2,1)S(1)} collective-permute-done((bf16[256,1152]{1,0:T(8,128)(2,1)S(1)}, bf16[256,1152]{1,0:T(8,128)(2,1)S(1)}, u32[]{:S(2)}, u32[]{:S(2)}) %collective-permute-start.10) | collective-permute-done | bytes 589856 | tf_op jit(solution)/shard_map/ppermute | solution.py:55
  174.7 1.7 shard_map.77
  176.4 0.1 collective-permute-start.13
  176.5 2.0 %collective-permute-done.13 = f32[128,1152]{1,0:T(8,128)S(1)} collective-permute-done((f32[128,1152]{1,0:T(8,128)S(1)}, f32[128,1152]{1,0:T(8,128)S(1)}, u32[]{:S(2)}, u32[]{:S(2)}) %collective-permute-start.13) | collective-permute-done | bytes 589856 | tf_op jit(solution)/shard_map/ppermute | solution.py:59
  178.5 1.1 broadcast_select_fusion
  (23 shorter events, 0.1 us)
Async XLA Ops:
  7.2 31.3 %all-gather.5.cloned.1.call-start = ((), (), s32[]{:S(2)}) async-start(), calls=%async_computation | async-start | bytes 1474560 | tf_op jit(solution)/shard_map/all_gather | solution.py:44
  8.2 2.7 %collective-permute-start = (bf16[128,1152]{1,0:T(8,128)(2,1)S(1)}, bf16[128,1152]{1,0:T(8,128)(2,1)S(1)}, u32[]{:S(2)}, u32[]{:S(2)}) collective-permute-start(bf16[128,1152]{1,0:T(8,128)(2,1)S(1)} %broadcast_select_fusion.2), channel_id=1, source_target_pairs={{0,32},{32,0},{1,33},{33,1},{2,34},{34,2},{3,35},{35,3},{4,36},{36... | collective-permute-start | bytes 884744 | tf_op jit(solution)/shard_map/ppermute | solution.py:59
  10.9 1.0 copy-start
  11.9 1.0 copy-start.1
  14.6 49.4 %all-gather.7.cloned.1.call-start = ((), (), s32[]{:S(2)}) async-start(), calls=%async_computation.1 | async-start | bytes 1474560 | tf_op jit(solution)/shard_map/all_gather | solution.py:44
  15.3 73.6 %all-gather.9.cloned.1.call-start = ((), (), s32[]{:S(2)}) async-start(), calls=%async_computation.2 | async-start | bytes 1474560 | tf_op jit(solution)/shard_map/all_gather | solution.py:44
  15.4 10.2 %collective-permute-start.3 = (bf16[256,1152]{1,0:T(8,128)(2,1)S(1)}, bf16[256,1152]{1,0:T(8,128)(2,1)S(1)}, u32[]{:S(2)}, u32[]{:S(2)}) collective-permute-start(bf16[256,1152]{1,0:T(8,128)(2,1)S(1)} %get-tuple-element.11), channel_id=1, source_target_pairs={{0,64},{32,97},{2,66},{34,99},{4,68},{36,101},{6,70},{38,103},{64,... | collective-permute-start | bytes 1769480 | tf_op jit(solution)/shard_map/ppermute | solution.py:55
  26.4 87.3 %all-gather.11.cloned.1.call-start = ((), (), s32[]{:S(2)}) async-start(), calls=%async_computation.3 | async-start | bytes 1474560 | tf_op jit(solution)/shard_map/all_gather | solution.py:44
  38.5 79.0 %collective-permute-start.1 = (bf16[512,1152]{1,0:T(8,128)(2,1)}, bf16[512,1152]{1,0:T(8,128)(2,1)S(1)}, u32[]{:S(2)}, u32[]{:S(2)}) collective-permute-start(bf16[512,1152]{1,0:T(8,128)(2,1)} %all-gather.5.cloned.1.call-done.mine_a), channel_id=1, source_target_pairs={{0,32},{32,0},{1,33},{33,1},{2,34},{34,2},{3,35},{35,3},{4,36},{36... | collective-permute-start | bytes 3538952 | tf_op jit(solution)/shard_map/ppermute | solution.py:59
  64.0 53.4 %collective-permute-start.2 = (bf16[512,1152]{1,0:T(8,128)(2,1)}, bf16[512,1152]{1,0:T(8,128)(2,1)S(1)}, u32[]{:S(2)}, u32[]{:S(2)}) collective-permute-start(bf16[512,1152]{1,0:T(8,128)(2,1)} %all-gather.7.cloned.1.call-done.mine_b), channel_id=1, source_target_pairs={{0,32},{32,0},{1,33},{33,1},{2,34},{34,2},{3,35},{35,3},{4,36},{36... | collective-permute-start | bytes 3538952 | tf_op jit(solution)/shard_map/ppermute | solution.py:59
  89.0 28.5 %collective-permute-start.4 = (bf16[512,1152]{1,0:T(8,128)(2,1)}, bf16[512,1152]{1,0:T(8,128)(2,1)}, u32[]{:S(2)}, u32[]{:S(2)}) collective-permute-start(bf16[512,1152]{1,0:T(8,128)(2,1)} %all-gather.9.cloned.1.call-done.mine_a), channel_id=1, source_target_pairs={{0,32},{32,0},{1,33},{33,1},{2,34},{34,2},{3,35},{35,3},{4,36},{36... | collective-permute-start | bytes 3538952 | tf_op jit(solution)/shard_map/ppermute | solution.py:59
  113.8 4.9 %collective-permute-start.5 = (bf16[512,1152]{1,0:T(8,128)(2,1)}, bf16[512,1152]{1,0:T(8,128)(2,1)S(1)}, u32[]{:S(2)}, u32[]{:S(2)}) collective-permute-start(bf16[512,1152]{1,0:T(8,128)(2,1)} %all-gather.11.cloned.1.call-done.mine_b), channel_id=1, source_target_pairs={{0,32},{32,0},{1,33},{33,1},{2,34},{34,2},{3,35},{35,3},{4,36},{36... | collective-permute-start | bytes 3538952 | tf_op jit(solution)/shard_map/ppermute | solution.py:59
  118.7 1.3 copy-start.4
  120.0 1.3 copy-start.6
  121.3 9.3 %copy-start.5 = (bf16[512,1152]{1,0:T(8,128)(2,1)S(1)}, bf16[512,1152]{1,0:T(8,128)(2,1)}, u32[]{:S(2)}) copy-start(bf16[512,1152]{1,0:T(8,128)(2,1)} %all-gather.9.cloned.1.call-done.mine_a) | copy-start | bytes 3538948
  121.3 9.3 %copy-start.7 = (bf16[512,1152]{1,0:T(8,128)(2,1)S(1)}, bf16[512,1152]{1,0:T(8,128)(2,1)}, u32[]{:S(2)}) copy-start(bf16[512,1152]{1,0:T(8,128)(2,1)} %all-gather.11.cloned.1.call-done.mine_b) | copy-start | bytes 3538948
  125.6 21.9 %collective-permute-start.9 = (bf16[256,1152]{1,0:T(8,128)(2,1)S(1)}, bf16[256,1152]{1,0:T(8,128)(2,1)S(1)}, u32[]{:S(2)}, u32[]{:S(2)}) collective-permute-start(bf16[256,1152]{1,0:T(8,128)(2,1)S(1)} %shard_map.73), channel_id=1, source_target_pairs={{0,88},{32,103},{2,90},{34,97},{4,92},{36,99},{6,94},{38,101},{64,... | collective-permute-start | bytes 1769480 | tf_op jit(solution)/shard_map/ppermute | solution.py:55
  134.8 8.4 %copy-start.2 = (bf16[512,1152]{1,0:T(8,128)(2,1)S(1)}, bf16[512,1152]{1,0:T(8,128)(2,1)}, u32[]{:S(2)}) copy-start(bf16[512,1152]{1,0:T(8,128)(2,1)} %all-gather.5.cloned.1.call-done.mine_a) | copy-start | bytes 3538948
  134.8 8.3 %copy-start.3 = (bf16[512,1152]{1,0:T(8,128)(2,1)S(1)}, bf16[512,1152]{1,0:T(8,128)(2,1)}, u32[]{:S(2)}) copy-start(bf16[512,1152]{1,0:T(8,128)(2,1)} %all-gather.7.cloned.1.call-done.mine_b) | copy-start | bytes 3538948
  134.8 18.7 %collective-permute-start.8 = (bf16[256,1152]{1,0:T(8,128)(2,1)S(1)}, bf16[256,1152]{1,0:T(8,128)(2,1)S(1)}, u32[]{:S(2)}, u32[]{:S(2)}) collective-permute-start(bf16[256,1152]{1,0:T(8,128)(2,1)S(1)} %shard_map.72), channel_id=1, source_target_pairs={{0,72},{32,99},{2,74},{34,101},{4,76},{36,103},{6,78},{38,97},{64,... | collective-permute-start | bytes 1769480 | tf_op jit(solution)/shard_map/ppermute | solution.py:55
  139.3 21.0 %collective-permute-start.7 = (bf16[256,1152]{1,0:T(8,128)(2,1)S(1)}, bf16[256,1152]{1,0:T(8,128)(2,1)S(1)}, u32[]{:S(2)}, u32[]{:S(2)}) collective-permute-start(bf16[256,1152]{1,0:T(8,128)(2,1)S(1)} %shard_map.71), channel_id=1, source_target_pairs={{0,80},{32,101},{2,82},{34,103},{4,84},{36,97},{6,86},{38,99},{64,... | collective-permute-start | bytes 1769480 | tf_op jit(solution)/shard_map/ppermute | solution.py:55
  147.4 18.1 %collective-permute-start.6 = (bf16[256,1152]{1,0:T(8,128)(2,1)S(1)}, bf16[256,1152]{1,0:T(8,128)(2,1)S(1)}, u32[]{:S(2)}, u32[]{:S(2)}) collective-permute-start(bf16[256,1152]{1,0:T(8,128)(2,1)S(1)} %shard_map.69), channel_id=1, source_target_pairs={{0,16},{32,36},{2,18},{34,38},{4,20},{36,32},{6,22},{38,34},{64,80... | collective-permute-start | bytes 1769480 | tf_op jit(solution)/shard_map/ppermute | solution.py:55
  151.8 17.9 %collective-permute-start.12 = (bf16[256,1152]{1,0:T(8,128)(2,1)S(1)}, bf16[256,1152]{1,0:T(8,128)(2,1)S(1)}, u32[]{:S(2)}, u32[]{:S(2)}) collective-permute-start(bf16[256,1152]{1,0:T(8,128)(2,1)S(1)} %shard_map.76), channel_id=1, source_target_pairs={{0,64},{32,97},{2,66},{34,99},{4,68},{36,101},{6,70},{38,103},{64,... | collective-permute-start | bytes 1769480 | tf_op jit(solution)/shard_map/ppermute | solution.py:55
  157.7 12.0 %collective-permute-start.11 = (bf16[256,1152]{1,0:T(8,128)(2,1)S(1)}, bf16[256,1152]{1,0:T(8,128)(2,1)S(1)}, u32[]{:S(2)}, u32[]{:S(2)}) collective-permute-start(bf16[256,1152]{1,0:T(8,128)(2,1)S(1)} %shard_map.75), channel_id=1, source_target_pairs={{0,24},{32,38},{2,26},{34,32},{4,28},{36,34},{6,30},{38,36},{64,88... | collective-permute-start | bytes 1769480 | tf_op jit(solution)/shard_map/ppermute | solution.py:55
  164.5 10.2 %collective-permute-start.10 = (bf16[256,1152]{1,0:T(8,128)(2,1)S(1)}, bf16[256,1152]{1,0:T(8,128)(2,1)S(1)}, u32[]{:S(2)}, u32[]{:S(2)}) collective-permute-start(bf16[256,1152]{1,0:T(8,128)(2,1)S(1)} %shard_map.74), channel_id=1, source_target_pairs={{0,8},{32,34},{2,10},{34,36},{4,12},{36,38},{6,14},{38,32},{64,72}... | collective-permute-start | bytes 1769480 | tf_op jit(solution)/shard_map/ppermute | solution.py:55
  176.4 2.1 %collective-permute-start.13 = (f32[128,1152]{1,0:T(8,128)S(1)}, f32[128,1152]{1,0:T(8,128)S(1)}, u32[]{:S(2)}, u32[]{:S(2)}) collective-permute-start(f32[128,1152]{1,0:T(8,128)S(1)} %get-tuple-element.13), channel_id=1, source_target_pairs={{0,32},{32,0},{1,33},{33,1},{2,34},{34,2},{3,35},{35,3},{4,36},{36... | collective-permute-start | bytes 1769480 | tf_op jit(solution)/shard_map/ppermute | solution.py:59
Sparse Core Ops, SparseCore 0:
  14.7 23.7 all-gather.4
  40.7 23.2 all-gather.6
  65.7 23.2 all-gather.8
  90.5 23.2 all-gather.10

commit v4 on v3

v4 whole, which is shorter than its diff:
```python
import functools
import math

import jax
import jax.numpy as jnp
import numpy as np
from jax import lax
from jax.experimental import pallas as pl
from jax.experimental.pallas import tpu as pltpu
from jax.sharding import Mesh
from jax.sharding import PartitionSpec as P

FINE_AXES = ("y_lo", "core", "x", "z", "y_hi")
FINE_SIZES = (2, 2, 4, 4, 2)
RING = 4
VMEM_BYTES = 16 * 1024 * 1024
HALF = jnp.bfloat16
FULL = jnp.float32

VMEM = pl.BlockSpec(memory_space=pltpu.VMEM)
SMEM = pl.BlockSpec(memory_space=pltpu.SMEM)
ANY = pl.BlockSpec(memory_space=pl.ANY)
PARAMS = pltpu.CompilerParams(vmem_limit_bytes=VMEM_BYTES)

WAYS = ((2, 1), (1, 1), (3, 1), (2, 0), (1, 0), (3, 0), (0, 1))
EARLY = ((0, 1), (1, 0), (3, 0))


def place(core, x, y, z):
    return int(np.ravel_multi_index((y % 2, core, x, z, y // 2), FINE_SIZES))


def mate(core, y):
    if core == 0:
        return y ^ 1
    return (y + 1) % RING if y % 2 else (y - 1) % RING


def sent(value, steps, across):
    pairs = []
    for x, y, z in np.ndindex(RING, RING, RING):
        for core in range(2):
            to_y = mate(core, y) if across else y
            to_x = (x + steps) % RING if core == 0 else x
            to_z = (z + steps) % RING if core == 1 else z
            pairs.append((place(core, x, y, z), place(core, to_x, to_y, to_z)))
    return lax.ppermute(value, FINE_AXES, pairs)


def other_core(value):
    return lax.ppermute(value, "core", [(0, 1), (1, 0)])


def dot(a, b, contract):
    return lax.dot_general(a, b, ((contract[:1], contract[1:]), ((), ())), preferred_element_type=FULL)


def unit_rows(raw):
    values = raw.astype(FULL)
    scale = lax.rsqrt(jnp.mean(values * values, axis=1, keepdims=True) + 1e-06) / math.sqrt(
        values.shape[1]
    )
    return values * scale, scale


def normalize_kernel(is_first, image, text, image_there, text_there, raw, mine, theirs):
    rows = image.shape[0]
    first = is_first[0] > 0
    images = (image[...].astype(FULL), image_there[...].astype(FULL))
    texts = (text[...].astype(FULL), text_there[...].astype(FULL))
    for k in range(2):
        at = pl.ds(k * rows, rows)
        of_image = jnp.where(first, images[k], images[1 - k])
        of_text = jnp.where(first, texts[k], texts[1 - k])
        here = jnp.where(first, of_image, of_text)
        raw[at, :] = here.astype(HALF)
        mine[at, :] = unit_rows(here)[0].astype(HALF)
        theirs[at, :] = unit_rows(jnp.where(first, of_text, of_image))[0].astype(HALF)


def accumulate(affine, mine, theirs, coupling, start, diagonal):
    unit = mine.shape[0]
    for k, other in enumerate(theirs):
        energies = dot(mine, other[...], (1, 1))
        tile = 0.5 * jnp.tanh(affine[0] * energies + affine[1]) + 0.5
        if diagonal and k == 0:
            row = lax.broadcasted_iota(jnp.int32, tile.shape, 0)
            column = lax.broadcasted_iota(jnp.int32, tile.shape, 1)
            tile = tile - jnp.where(row == column, 1.0, 0.0)
        coupling[:, pl.ds(k * unit, unit)] = tile.astype(HALF)
    total = start
    for k, other in enumerate(theirs):
        term = dot(coupling[:, pl.ds(k * unit, unit)], other[...], (1, 0))
        total = term if total is None else total + term
    return total


def early_kernel(count, affine, *refs):
    mine, theirs, sums, coupling = refs[:count], refs[count : 2 * count], refs[2 * count : -1], refs[-1]
    for k in range(count):
        sums[k][...] = accumulate(affine, mine[k][...], theirs, coupling, None, k == 0)


def early_sums(affine, mine, theirs):
    count = len(mine)
    unit, width = mine[0].shape
    return pl.pallas_call(
        functools.partial(early_kernel, count),
        out_shape=[jax.ShapeDtypeStruct((unit, width), FULL)] * count,
        in_specs=[SMEM] + [VMEM] * (2 * count),
        out_specs=[VMEM] * count,
        scratch_shapes=[pltpu.VMEM((unit, count * unit), HALF)],
        cost_estimate=pl.CostEstimate(
            flops=4 * (count * unit) ** 2 * width,
            bytes_accessed=8 * count * unit * width,
            transcendentals=(count * unit) ** 2,
        ),
        compiler_params=PARAMS,
    )(affine, *mine, *theirs)


def part_kernel(count, summed, n_after, affine, mine, *refs):
    theirs, refs = refs[:count], refs[count:]
    start = refs[0][...] if summed else None
    part, coupling = refs[-2:]
    part[...] = accumulate(affine, mine[...], theirs, coupling, start, False).astype(HALF)


def part_of(affine, mine, theirs, start, after):
    unit, width = mine.shape
    count = len(theirs)
    starts = [] if start is None else [start]
    return pl.pallas_call(
        functools.partial(part_kernel, count, len(starts), len(after)),
        out_shape=jax.ShapeDtypeStruct((unit, width), HALF),
        in_specs=[SMEM] + [VMEM] * (1 + count + len(starts)) + [ANY] * len(after),
        out_specs=VMEM,
        scratch_shapes=[pltpu.VMEM((unit, count * unit), HALF)],
        cost_estimate=pl.CostEstimate(
            flops=4 * count * unit**2 * width,
            bytes_accessed=2 * unit * width,
            transcendentals=count * unit**2,
        ),
        compiler_params=PARAMS,
    )(affine, mine, *theirs, *starts, *after)


def finish_kernel(core, multiplier, raw, *refs):
    parts, (here, there, grads) = refs[:-3], refs[-3:]
    rows = here.shape[0]
    total = parts[0][...].astype(FULL)
    for part in parts[1:]:
        total = total + part[...].astype(FULL)
    unit, scale = unit_rows(raw[...])
    grad = multiplier[0] * total
    grads[...] = scale * (grad - unit * jnp.sum(unit * grad, axis=1, keepdims=True))
    here[...] = grads[pl.ds(core[0] * rows, rows), :]
    there[...] = grads[pl.ds((1 - core[0]) * rows, rows), :]


def on_device(
    picture_vectors_raw, caption_vectors_raw, logit_multiplier, offset_term, incoming_adjoint
):
    rows, width = picture_vectors_raw.shape
    pairs = rows * math.prod(FINE_SIZES)
    core = lax.axis_index("core").astype(jnp.int32)
    is_first = core == 0
    affine = jnp.concatenate([0.5 * logit_multiplier, 0.5 * offset_term])
    multiplier = incoming_adjoint * logit_multiplier / pairs
    unit = jax.ShapeDtypeStruct((2 * rows, width), HALF)
    shard_full = jax.ShapeDtypeStruct((rows, width), FULL)

    raw, own, own_theirs = pl.pallas_call(
        normalize_kernel,
        out_shape=[unit] * 3,
        in_specs=[SMEM] + [VMEM] * 4,
        out_specs=[VMEM] * 3,
        compiler_params=PARAMS,
    )(
        is_first.astype(FULL).reshape(1),
        picture_vectors_raw,
        caption_vectors_raw,
        other_core(picture_vectors_raw),
        other_core(caption_vectors_raw),
    )

    mine, theirs = {(0, 0): own}, {(0, 0): own_theirs}
    for steps, across in reversed(WAYS):
        mine[steps, across] = sent(own, -steps, across)
        theirs[steps, across] = other_core(mine[steps, across])
    first = [(0, 0), *EARLY]
    second = [way for way in mine if way not in first]
    sums = early_sums(affine, [mine[w] for w in first], [theirs[w] for w in first])
    sums = dict(zip(first, sums, strict=True))

    arrived = []
    for k, way in enumerate((*WAYS, (0, 0))):
        after = arrived[k - 4 : k - 3] if k >= 4 else []
        if way in sums:
            part = part_of(affine, mine[way], [theirs[w] for w in second], sums[way], after)
        else:
            part = part_of(affine, mine[way], [theirs[w] for w in (*first, *second)], None, after)
        if way != (0, 0):
            arrived.append(sent(part, *way))

    here, there = pl.pallas_call(
        finish_kernel,
        out_shape=[shard_full, shard_full],
        in_specs=[SMEM, SMEM] + [VMEM] * (2 + len(arrived)),
        out_specs=[VMEM] * 2,
        scratch_shapes=[pltpu.VMEM((2 * rows, width), FULL)],
        compiler_params=PARAMS,
    )(core.reshape(1), multiplier, raw, part, *arrived)
    back = other_core(there)
    return (jnp.where(is_first, here, back), jnp.where(is_first, back, here))


def solution(mesh):
    fine = Mesh(mesh.devices.reshape(FINE_SIZES), FINE_AXES)
    rows = P(FINE_AXES, None)
    return jax.shard_map(
        on_device,
        mesh=fine,
        in_specs=(rows, rows, P(), P(), P()),
        out_specs=(rows, rows),
        check_vma=False,
    )
```

time: 187 us -> 105 us (0.56)
  waiting for transfers between devices: 98 us -> 13.7 us
  starting transfers between devices: 27.2 us -> 54.5 us
  between operations: 15.9 us -> 2.73 us
  Pallas kernels: 37.4 us -> 30.3 us
  local copies, waits for them, and re-layouts: 5.37 us -> 1.92 us
    all_gather x4 -> x0, waiting for transfers between devices: 80 us -> none  [ring_gather(): lax.all_gather(shard, FINE_AXES, axis=0, tiled=True, axis_index_groups=gr...]
    ppermute x8 -> x14, starting transfers between devices: 16.5 us -> 31.1 us  [sent(): return lax.ppermute(value, FINE_AXES, pairs)]
    ppermute x6 -> x10, starting transfers between devices: 10.6 us -> 23.4 us  [other_core(): return lax.ppermute(value, 'core', [(0, 1), (1, 0)])]
    pallas_call x9 -> x10, Pallas kernels: 35.7 us -> 29.2 us  [the longest x8 22.4 us: part_of(): pl.pallas_call(functools.partial(part_kernel, count, len(starts), len(aft...]
    ppermute x8 -> x14, waiting for transfers between devices: 12.3 us -> 8.53 us  [sent(): return lax.ppermute(value, FINE_AXES, pairs)]
    unnamed x16 -> x4, local copies, waits for them, and re-layouts: 4.48 us -> 1.92 us
    ppermute x6 -> x10, waiting for transfers between devices: 4.43 us -> 5.16 us  [other_core(): return lax.ppermute(value, 'core', [(0, 1), (1, 0)])]
  transfers between devices with their start and end apart: 18 -> 24, of which waited for: 9 -> 9; matrix products, arithmetic and copies ran while one was open for 1% -> 0% of each run, Pallas kernels for 16% -> 24%
where the time goes in v4:
time: 105 us; the launch traced here: 104 us
  starting transfers between devices  54.5 us (52%)
  Pallas kernels  30.3 us (29%)
  waiting for transfers between devices  13.7 us (13%)
  between operations  2.73 us (3%)
  local copies, waits for them, and re-layouts  1.92 us (2%)
  other arithmetic  1.16 us (1%)
    ppermute x14, starting transfers between devices, sent(): return lax.ppermute(value, FINE_AXES, pairs)  31.1 us
    ppermute x10, starting transfers between devices, other_core(): return lax.ppermute(value, 'core', [(0, 1), (1, 0)])  23.4 us
    pallas_call x8, Pallas kernels, part_of(): pl.pallas_call(functools.partial(part_kernel, count, len(starts), len(aft...  22.4 us
    ppermute x14, waiting for transfers between devices, sent(): return lax.ppermute(value, FINE_AXES, pairs)  8.53 us
    pallas_call x1, Pallas kernels, early_sums(): pl.pallas_call(functools.partial(early_kernel, count), out_shape=[jax.Sha...  6.23 us
    ppermute x10, waiting for transfers between devices, other_core(): return lax.ppermute(value, 'core', [(0, 1), (1, 0)])  5.16 us
  transfers between devices with their start and end apart: 24, of which 9 were waited for; matrix products, arithmetic and copies ran while one was open for 0% of the time, Pallas kernels for 24%

profile of v4, /device:TPU:1, one launch (start us, length us, event | category | flops | bytes accessed | tf_op | source)
XLA Modules:
  0.0 104.4 jit_solution(8288899496426224209)
XLA Ops:
  0.6 1.5 %collective-permute-start = (bf16[128,1152]{1,0:T(8,128)(2,1)}, bf16[128,1152]{1,0:T(8,128)(2,1)S(1)}, u32[]{:S(2)}, u32[]{:S(2)}) collective-permute-start(bf16[128,1152]{1,0:T(8,128)(2,1)} %image.1), channel_id=1, source_target_pairs={{0,32},{32,0},{1,33},{33,1},{2,34},{34,2},{3,35},{35,3},{4,36},{36... | collective-permute-start | bytes 884744 | tf_op jit(solution)/shard_map/ppermute | solution.py:51
  2.1 0.1 collective-permute-start.1
  2.2 1.3 %collective-permute-done.image_there = bf16[128,1152]{1,0:T(8,128)(2,1)S(1)} collective-permute-done((bf16[128,1152]{1,0:T(8,128)(2,1)}, bf16[128,1152]{1,0:T(8,128)(2,1)S(1)}, u32[]{:S(2)}, u32[]{:S(2)}) %collective-permute-start) | collective-permute-done | bytes 294944 | tf_op jit(solution)/shard_map/ppermute | solution.py:51
  3.6 0.4 collective-permute-done.1.text_there
  4.0 1.0 copy-done
  4.9 1.0 copy-done.1
  5.9 0.6 shard_map.68
  6.5 1.8 %collective-permute-start.12 = (bf16[256,1152]{1,0:T(8,128)(2,1)S(1)}, bf16[256,1152]{1,0:T(8,128)(2,1)S(1)}, u32[]{:S(2)}, u32[]{:S(2)}) collective-permute-start(bf16[256,1152]{1,0:T(8,128)(2,1)S(1)} %get-tuple-element.12.refs_0_.mine), channel_id=1, source_target_pairs={{0,8},{32,34},{2,10},{34,36},{4,12},{36,38},{6,14},{38,32},{64,72}... | collective-permute-start | bytes 1769480 | tf_op jit(solution)/shard_map/ppermute | solution.py:47
  8.3 2.2 %collective-permute-start.11 = (bf16[256,1152]{1,0:T(8,128)(2,1)S(1)}, bf16[256,1152]{1,0:T(8,128)(2,1)S(1)}, u32[]{:S(2)}, u32[]{:S(2)}) collective-permute-start(bf16[256,1152]{1,0:T(8,128)(2,1)S(1)} %get-tuple-element.12.refs_0_.mine), channel_id=1, source_target_pairs={{0,24},{32,38},{2,26},{34,32},{4,28},{36,34},{6,30},{38,36},{64,88... | collective-permute-start | bytes 1769480 | tf_op jit(solution)/shard_map/ppermute | solution.py:47
  10.5 2.7 %collective-permute-start.10 = (bf16[256,1152]{1,0:T(8,128)(2,1)S(1)}, bf16[256,1152]{1,0:T(8,128)(2,1)S(1)}, u32[]{:S(2)}, u32[]{:S(2)}) collective-permute-start(bf16[256,1152]{1,0:T(8,128)(2,1)S(1)} %get-tuple-element.12.refs_0_.mine), channel_id=1, source_target_pairs={{0,64},{32,97},{2,66},{34,99},{4,68},{36,101},{6,70},{38,103},{64,... | collective-permute-start | bytes 1769480 | tf_op jit(solution)/shard_map/ppermute | solution.py:47
  13.2 0.9 collective-permute-start.8
  14.2 3.0 %collective-permute-start.6 = (bf16[256,1152]{1,0:T(8,128)(2,1)S(1)}, bf16[256,1152]{1,0:T(8,128)(2,1)S(1)}, u32[]{:S(2)}, u32[]{:S(2)}) collective-permute-start(bf16[256,1152]{1,0:T(8,128)(2,1)S(1)} %get-tuple-element.12.refs_0_.mine), channel_id=1, source_target_pairs={{0,88},{32,103},{2,90},{34,97},{4,92},{36,99},{6,94},{38,101},{64,... | collective-permute-start | bytes 1769480 | tf_op jit(solution)/shard_map/ppermute | solution.py:47
  17.2 0.5 collective-permute-done.12.refs_3_.mine
  17.7 2.1 %collective-permute-start.4 = (bf16[256,1152]{1,0:T(8,128)(2,1)S(1)}, bf16[256,1152]{1,0:T(8,128)(2,1)S(1)}, u32[]{:S(2)}, u32[]{:S(2)}) collective-permute-start(bf16[256,1152]{1,0:T(8,128)(2,1)S(1)} %get-tuple-element.12.refs_0_.mine), channel_id=1, source_target_pairs={{0,72},{32,99},{2,74},{34,101},{4,76},{36,103},{6,78},{38,97},{64,... | collective-permute-start | bytes 1769480 | tf_op jit(solution)/shard_map/ppermute | solution.py:47
  19.8 3.3 %collective-permute-start.2 = (bf16[256,1152]{1,0:T(8,128)(2,1)S(1)}, bf16[256,1152]{1,0:T(8,128)(2,1)S(1)}, u32[]{:S(2)}, u32[]{:S(2)}) collective-permute-start(bf16[256,1152]{1,0:T(8,128)(2,1)S(1)} %get-tuple-element.12.refs_0_.mine), channel_id=1, source_target_pairs={{0,16},{32,36},{2,18},{34,38},{4,20},{36,32},{6,22},{38,34},{64,80... | collective-permute-start | bytes 1769480 | tf_op jit(solution)/shard_map/ppermute | solution.py:47
  23.1 15.1 %collective-permute-start.15 = (bf16[256,1152]{1,0:T(8,128)(2,1)S(1)}, bf16[256,1152]{1,0:T(8,128)(2,1)S(1)}, u32[]{:S(2)}, u32[]{:S(2)}) collective-permute-start(bf16[256,1152]{1,0:T(8,128)(2,1)S(1)} %collective-permute-done.12.refs_3_.mine), channel_id=1, source_target_pairs={{0,32},{32,0},{1,33},{33,1},{2,34},{34,2},{3,35},{35,3},{4,36},{36... | collective-permute-start | bytes 1769480 | tf_op jit(solution)/shard_map/ppermute | solution.py:51
  38.2 0.0 collective-permute-start.14
  38.2 0.0 collective-permute-done.6.mine
  38.2 0.9 collective-permute-start.13
  39.1 1.6 %collective-permute-done.4.mine = bf16[256,1152]{1,0:T(8,128)(2,1)S(1)} collective-permute-done((bf16[256,1152]{1,0:T(8,128)(2,1)S(1)}, bf16[256,1152]{1,0:T(8,128)(2,1)S(1)}, u32[]{:S(2)}, u32[]{:S(2)}) %collective-permute-start.4) | collective-permute-done | bytes 589856 | tf_op jit(solution)/shard_map/ppermute | solution.py:47
  40.7 5.2 %collective-permute-start.7 = (bf16[256,1152]{1,0:T(8,128)(2,1)S(1)}, bf16[256,1152]{1,0:T(8,128)(2,1)S(1)}, u32[]{:S(2)}, u32[]{:S(2)}) collective-permute-start(bf16[256,1152]{1,0:T(8,128)(2,1)S(1)} %collective-permute-done.6.mine), channel_id=1, source_target_pairs={{0,32},{32,0},{1,33},{33,1},{2,34},{34,2},{3,35},{35,3},{4,36},{36... | collective-permute-start | bytes 1769480 | tf_op jit(solution)/shard_map/ppermute | solution.py:51
  45.9 0.0 collective-permute-start.5
  45.9 0.5 collective-permute-start.3
  47.7 0.1 pad_maximum_fusion.affine
  47.8 0.6 collective-permute-done.5.refs_5_.refs_1_
  48.4 0.8 collective-permute-done.3.refs_4_.refs_0_
  49.2 3.5 %shard_map.70 = bf16[256,1152]{1,0:T(8,128)(2,1)S(1)} custom-call(f32[2]{0:T(128)S(1)} %pad_maximum_fusion.affine, bf16[256,1152]{1,0:T(8,128)(2,1)S(1)} %collective-permute-done.2.mine, bf16[256,1152]{1,0:T(8,128)(2,1)S(1)} %get-tuple-element.13.refs_4_.refs_0_, bf16[256,1152]{1,0:T(8,128)(2,1)S(1)} %collective-permute-done.13.refs_5_.refs_1_, ...), custom_call_target="tpu_custom_call" | custom-call | flops 2415919104 | bytes 589824 | tf_op jit(solution)/shard_map/pallas_call | solution.py:133
  52.7 3.7 %collective-permute-start.16 = (bf16[256,1152]{1,0:T(8,128)(2,1)S(1)}, bf16[256,1152]{1,0:T(8,128)(2,1)S(1)}, u32[]{:S(2)}, u32[]{:S(2)}) collective-permute-start(bf16[256,1152]{1,0:T(8,128)(2,1)S(1)} %shard_map.70), channel_id=1, source_target_pairs={{0,16},{32,36},{2,18},{34,38},{4,20},{36,32},{6,22},{38,34},{64,80... | collective-permute-start | bytes 1769480 | tf_op jit(solution)/shard_map/ppermute | solution.py:47
  56.4 3.5 %shard_map.72 = bf16[256,1152]{1,0:T(8,128)(2,1)S(1)} custom-call(f32[2]{0:T(128)S(1)} %pad_maximum_fusion.affine, bf16[256,1152]{1,0:T(8,128)(2,1)S(1)} %collective-permute-done.8.mine, bf16[256,1152]{1,0:T(8,128)(2,1)S(1)} %get-tuple-element.13.refs_4_.refs_0_, bf16[256,1152]{1,0:T(8,128)(2,1)S(1)} %collective-permute-done.13.refs_5_.refs_1_, ...), custom_call_target="tpu_custom_call" | custom-call | flops 2415919104 | bytes 589824 | tf_op jit(solution)/shard_map/pallas_call | solution.py:133
  59.8 2.7 %collective-permute-start.17 = (bf16[256,1152]{1,0:T(8,128)(2,1)S(1)}, bf16[256,1152]{1,0:T(8,128)(2,1)S(1)}, u32[]{:S(2)}, u32[]{:S(2)}) collective-permute-start(bf16[256,1152]{1,0:T(8,128)(2,1)S(1)} %shard_map.72), channel_id=1, source_target_pairs={{0,80},{32,101},{2,82},{34,103},{4,84},{36,97},{6,86},{38,99},{64,... | collective-permute-start | bytes 1769480 | tf_op jit(solution)/shard_map/ppermute | solution.py:47
  62.5 3.5 %shard_map.73 = bf16[256,1152]{1,0:T(8,128)(2,1)S(1)} custom-call(f32[2]{0:T(128)S(1)} %pad_maximum_fusion.affine, bf16[256,1152]{1,0:T(8,128)(2,1)S(1)} %collective-permute-done.6.mine, bf16[256,1152]{1,0:T(8,128)(2,1)S(1)} %get-tuple-element.13.refs_4_.refs_0_, bf16[256,1152]{1,0:T(8,128)(2,1)S(1)} %collective-permute-done.13.refs_5_.refs_1_, ...), custom_call_target="tpu_custom_call" | custom-call | flops 2415919104 | bytes 589824 | tf_op jit(solution)/shard_map/pallas_call | solution.py:133
  66.0 0.8 collective-permute-start.18
  66.8 3.5 %shard_map.74 = bf16[256,1152]{1,0:T(8,128)(2,1)S(1)} custom-call(f32[2]{0:T(128)S(1)} %pad_maximum_fusion.affine, bf16[256,1152]{1,0:T(8,128)(2,1)S(1)} %collective-permute-done.4.mine, bf16[256,1152]{1,0:T(8,128)(2,1)S(1)} %get-tuple-element.13.refs_4_.refs_0_, bf16[256,1152]{1,0:T(8,128)(2,1)S(1)} %collective-permute-done.13.refs_5_.refs_1_, ...), custom_call_target="tpu_custom_call" | custom-call | flops 2415919104 | bytes 589824 | tf_op jit(solution)/shard_map/pallas_call | solution.py:133
  70.3 4.1 %collective-permute-start.19 = (bf16[256,1152]{1,0:T(8,128)(2,1)S(1)}, bf16[256,1152]{1,0:T(8,128)(2,1)S(1)}, u32[]{:S(2)}, u32[]{:S(2)}) collective-permute-start(bf16[256,1152]{1,0:T(8,128)(2,1)S(1)} %shard_map.74), channel_id=1, source_target_pairs={{0,88},{32,103},{2,90},{34,97},{4,92},{36,99},{6,94},{38,101},{64,... | collective-permute-start | bytes 1769480 | tf_op jit(solution)/shard_map/ppermute | solution.py:47
  74.4 6.2 %shard_map.69 = (f32[256,1152]{1,0:T(8,128)S(1)}, f32[256,1152]{1,0:T(8,128)S(1)}, f32[256,1152]{1,0:T(8,128)S(1)}, f32[256,1152]{1,0:T(8,128)S(1)}) custom-call(f32[2]{0:T(128)S(1)} %pad_maximum_fusion.affine, bf16[256,1152]{1,0:T(8,128)(2,1)S(1)} %get-tuple-element.12.refs_0_.mine, bf16[256,1152]{1,0:T(8,128)(2,1)S(1)} %collective-permute-done.10.refs_1_.mine, ...), custom_call_target="tpu_custom_call" | custom-call | flops 4831838208 | bytes 9437184 | tf_op jit(solution)/shard_map/pallas_call | solution.py:107
  80.7 2.1 %shard_map.75 = bf16[256,1152]{1,0:T(8,128)(2,1)S(1)} custom-call(f32[2]{0:T(128)S(1)} %pad_maximum_fusion.affine, bf16[256,1152]{1,0:T(8,128)(2,1)S(1)} %collective-permute-done.11.refs_2_.mine, bf16[256,1152]{1,0:T(8,128)(2,1)S(1)} %collective-permute-done.3.refs_4_.refs_0_, bf16[256,1152]{1,0:T(8,128)(2,1)S(1)} %collective-permute-done.5.refs_5_.refs_1_, ...), custom_call_target="tpu_custom_call" | custom-call | flops 1207959552 | bytes 589824 | tf_op jit(solution)/shard_map/pallas_call | solution.py:133
  82.8 0.3 collective-permute-start.20
  83.1 2.1 %shard_map.76 = bf16[256,1152]{1,0:T(8,128)(2,1)S(1)} custom-call(f32[2]{0:T(128)S(1)} %pad_maximum_fusion.affine, bf16[256,1152]{1,0:T(8,128)(2,1)S(1)} %collective-permute-done.12.refs_3_.mine, bf16[256,1152]{1,0:T(8,128)(2,1)S(1)} %collective-permute-done.3.refs_4_.refs_0_, bf16[256,1152]{1,0:T(8,128)(2,1)S(1)} %collective-permute-done.5.refs_5_.refs_1_, ...), custom_call_target="tpu_custom_call" | custom-call | flops 1207959552 | bytes 589824 | tf_op jit(solution)/shard_map/pallas_call | solution.py:133
  85.2 2.7 %collective-permute-start.21 = (bf16[256,1152]{1,0:T(8,128)(2,1)S(1)}, bf16[256,1152]{1,0:T(8,128)(2,1)S(1)}, u32[]{:S(2)}, u32[]{:S(2)}) collective-permute-start(bf16[256,1152]{1,0:T(8,128)(2,1)S(1)} %shard_map.76), channel_id=1, source_target_pairs={{0,24},{32,38},{2,26},{34,32},{4,28},{36,34},{6,30},{38,36},{64,88... | collective-permute-start | bytes 1769480 | tf_op jit(solution)/shard_map/ppermute | solution.py:47
  87.9 2.1 %shard_map.77 = bf16[256,1152]{1,0:T(8,128)(2,1)S(1)} custom-call(f32[2]{0:T(128)S(1)} %pad_maximum_fusion.affine, bf16[256,1152]{1,0:T(8,128)(2,1)S(1)} %collective-permute-done.10.refs_1_.mine, bf16[256,1152]{1,0:T(8,128)(2,1)S(1)} %collective-permute-done.3.refs_4_.refs_0_, bf16[256,1152]{1,0:T(8,128)(2,1)S(1)} %collective-permute-done.5.refs_5_.refs_1_, ...), custom_call_target="tpu_custom_call" | custom-call | flops 1207959552 | bytes 589824 | tf_op jit(solution)/shard_map/pallas_call | solution.py:133
  90.0 0.8 collective-permute-start.22
  91.5 2.1 %shard_map.71.refs_0_ = bf16[256,1152]{1,0:T(8,128)(2,1)S(1)} custom-call(f32[2]{0:T(128)S(1)} %pad_maximum_fusion.affine, bf16[256,1152]{1,0:T(8,128)(2,1)S(1)} %get-tuple-element.12.refs_0_.mine, bf16[256,1152]{1,0:T(8,128)(2,1)S(1)} %collective-permute-done.3.refs_4_.refs_0_, bf16[256,1152]{1,0:T(8,128)(2,1)S(1)} %collective-permute-done.5.refs_5_.refs_1_, ...), custom_call_target="tpu_custom_call" | custom-call | flops 1207959552 | bytes 589824 | tf_op jit(solution)/shard_map/pallas_call | solution.py:133
  93.7 1.1 %collective-permute-done.21.refs_6_ = bf16[256,1152]{1,0:T(8,128)(2,1)S(1)} collective-permute-done((bf16[256,1152]{1,0:T(8,128)(2,1)S(1)}, bf16[256,1152]{1,0:T(8,128)(2,1)S(1)}, u32[]{:S(2)}, u32[]{:S(2)}) %collective-permute-start.21) | collective-permute-done | bytes 589856 | tf_op jit(solution)/shard_map/ppermute | solution.py:47
  94.8 5.3 %collective-permute-done.22.refs_7_ = bf16[256,1152]{1,0:T(8,128)(2,1)S(1)} collective-permute-done((bf16[256,1152]{1,0:T(8,128)(2,1)S(1)}, bf16[256,1152]{1,0:T(8,128)(2,1)S(1)}, u32[]{:S(2)}, u32[]{:S(2)}) %collective-permute-start.22) | collective-permute-done | bytes 589856 | tf_op jit(solution)/shard_map/ppermute | solution.py:47
  100.1 1.1 %shard_map.78 = (f32[128,1152]{1,0:T(8,128)S(1)}, f32[128,1152]{1,0:T(8,128)S(1)}) custom-call(s32[1]{0:T(128)} %bitcast.core, f32[1]{0:T(128)S(6)} %div.3.multiplier, bf16[256,1152]{1,0:T(8,128)(2,1)S(1)} %get-tuple-element.11.raw, bf16[256,1152]{1,0:T(8,128)(2,1)S(1)} %shard_map.71.refs_0_, bf16[256,1152]{1,0:T(8,128)(2,1)S(1)} %collective-permute-done.17.refs_5_.refs_1_, ...), custom_call_target="tpu_custom_call" | custom-call | tf_op jit(solution)/shard_map/pallas_call | solution.py:206
  101.2 0.1 collective-permute-start.23
  101.3 2.0 %collective-permute-done.23 = f32[128,1152]{1,0:T(8,128)S(1)} collective-permute-done((f32[128,1152]{1,0:T(8,128)S(1)}, f32[128,1152]{1,0:T(8,128)S(1)}, u32[]{:S(2)}, u32[]{:S(2)}) %collective-permute-start.23) | collective-permute-done | bytes 589856 | tf_op jit(solution)/shard_map/ppermute | solution.py:51
  103.3 1.1 %broadcast_select_fusion = (f32[128,1152]{1,0:T(8,128)}, f32[128,1152]{1,0:T(8,128)}) fusion(f32[128,1152]{1,0:T(8,128)S(1)} %collective-permute-done.23, f32[128,1152]{1,0:T(8,128)S(1)} %get-tuple-element.18, pred[]{:T(512)S(6)} %eq.3), kind=kLoop, calls=%fused_computation | loop fusion | flops 294912 | bytes 2359297 | tf_op jit(solution)/shard_map/jit(_where)/select_n | solution.py:215
  (17 shorter events, 0.0 us)
Async XLA Ops:
  0.6 2.9 %collective-permute-start = (bf16[128,1152]{1,0:T(8,128)(2,1)}, bf16[128,1152]{1,0:T(8,128)(2,1)S(1)}, u32[]{:S(2)}, u32[]{:S(2)}) collective-permute-start(bf16[128,1152]{1,0:T(8,128)(2,1)} %image.1), channel_id=1, source_target_pairs={{0,32},{32,0},{1,33},{33,1},{2,34},{34,2},{3,35},{35,3},{4,36},{36... | collective-permute-start | bytes 884744 | tf_op jit(solution)/shard_map/ppermute | solution.py:51
  2.1 1.8 %collective-permute-start.1 = (bf16[128,1152]{1,0:T(8,128)(2,1)}, bf16[128,1152]{1,0:T(8,128)(2,1)S(1)}, u32[]{:S(2)}, u32[]{:S(2)}) collective-permute-start(bf16[128,1152]{1,0:T(8,128)(2,1)} %text.1), channel_id=1, source_target_pairs={{0,32},{32,0},{1,33},{33,1},{2,34},{34,2},{3,35},{35,3},{4,36},{36... | collective-permute-start | bytes 884744 | tf_op jit(solution)/shard_map/ppermute | solution.py:51
  4.0 1.0 copy-start
  4.9 1.0 copy-start.1
  6.5 11.2 %collective-permute-start.12 = (bf16[256,1152]{1,0:T(8,128)(2,1)S(1)}, bf16[256,1152]{1,0:T(8,128)(2,1)S(1)}, u32[]{:S(2)}, u32[]{:S(2)}) collective-permute-start(bf16[256,1152]{1,0:T(8,128)(2,1)S(1)} %get-tuple-element.12.refs_0_.mine), channel_id=1, source_target_pairs={{0,8},{32,34},{2,10},{34,36},{4,12},{36,38},{6,14},{38,32},{64,72}... | collective-permute-start | bytes 1769480 | tf_op jit(solution)/shard_map/ppermute | solution.py:47
  8.3 11.5 %collective-permute-start.11 = (bf16[256,1152]{1,0:T(8,128)(2,1)S(1)}, bf16[256,1152]{1,0:T(8,128)(2,1)S(1)}, u32[]{:S(2)}, u32[]{:S(2)}) collective-permute-start(bf16[256,1152]{1,0:T(8,128)(2,1)S(1)} %get-tuple-element.12.refs_0_.mine), channel_id=1, source_target_pairs={{0,24},{32,38},{2,26},{34,32},{4,28},{36,34},{6,30},{38,36},{64,88... | collective-permute-start | bytes 1769480 | tf_op jit(solution)/shard_map/ppermute | solution.py:47
  10.5 12.6 %collective-permute-start.10 = (bf16[256,1152]{1,0:T(8,128)(2,1)S(1)}, bf16[256,1152]{1,0:T(8,128)(2,1)S(1)}, u32[]{:S(2)}, u32[]{:S(2)}) collective-permute-start(bf16[256,1152]{1,0:T(8,128)(2,1)S(1)} %get-tuple-element.12.refs_0_.mine), channel_id=1, source_target_pairs={{0,64},{32,97},{2,66},{34,99},{4,68},{36,101},{6,70},{38,103},{64,... | collective-permute-start | bytes 1769480 | tf_op jit(solution)/shard_map/ppermute | solution.py:47
  13.2 25.0 %collective-permute-start.8 = (bf16[256,1152]{1,0:T(8,128)(2,1)S(1)}, bf16[256,1152]{1,0:T(8,128)(2,1)S(1)}, u32[]{:S(2)}, u32[]{:S(2)}) collective-permute-start(bf16[256,1152]{1,0:T(8,128)(2,1)S(1)} %get-tuple-element.12.refs_0_.mine), channel_id=1, source_target_pairs={{0,80},{32,101},{2,82},{34,103},{4,84},{36,97},{6,86},{38,99},{64,... | collective-permute-start | bytes 1769480 | tf_op jit(solution)/shard_map/ppermute | solution.py:47
  14.2 24.0 %collective-permute-start.6 = (bf16[256,1152]{1,0:T(8,128)(2,1)S(1)}, bf16[256,1152]{1,0:T(8,128)(2,1)S(1)}, u32[]{:S(2)}, u32[]{:S(2)}) collective-permute-start(bf16[256,1152]{1,0:T(8,128)(2,1)S(1)} %get-tuple-element.12.refs_0_.mine), channel_id=1, source_target_pairs={{0,88},{32,103},{2,90},{34,97},{4,92},{36,99},{6,94},{38,101},{64,... | collective-permute-start | bytes 1769480 | tf_op jit(solution)/shard_map/ppermute | solution.py:47
  17.7 23.0 %collective-permute-start.4 = (bf16[256,1152]{1,0:T(8,128)(2,1)S(1)}, bf16[256,1152]{1,0:T(8,128)(2,1)S(1)}, u32[]{:S(2)}, u32[]{:S(2)}) collective-permute-start(bf16[256,1152]{1,0:T(8,128)(2,1)S(1)} %get-tuple-element.12.refs_0_.mine), channel_id=1, source_target_pairs={{0,72},{32,99},{2,74},{34,101},{4,76},{36,103},{6,78},{38,97},{64,... | collective-permute-start | bytes 1769480 | tf_op jit(solution)/shard_map/ppermute | solution.py:47
  19.8 20.9 %collective-permute-start.2 = (bf16[256,1152]{1,0:T(8,128)(2,1)S(1)}, bf16[256,1152]{1,0:T(8,128)(2,1)S(1)}, u32[]{:S(2)}, u32[]{:S(2)}) collective-permute-start(bf16[256,1152]{1,0:T(8,128)(2,1)S(1)} %get-tuple-element.12.refs_0_.mine), channel_id=1, source_target_pairs={{0,16},{32,36},{2,18},{34,38},{4,20},{36,32},{6,22},{38,34},{64,80... | collective-permute-start | bytes 1769480 | tf_op jit(solution)/shard_map/ppermute | solution.py:47
  23.1 22.8 %collective-permute-start.15 = (bf16[256,1152]{1,0:T(8,128)(2,1)S(1)}, bf16[256,1152]{1,0:T(8,128)(2,1)S(1)}, u32[]{:S(2)}, u32[]{:S(2)}) collective-permute-start(bf16[256,1152]{1,0:T(8,128)(2,1)S(1)} %collective-permute-done.12.refs_3_.mine), channel_id=1, source_target_pairs={{0,32},{32,0},{1,33},{33,1},{2,34},{34,2},{3,35},{35,3},{4,36},{36... | collective-permute-start | bytes 1769480 | tf_op jit(solution)/shard_map/ppermute | solution.py:51
  38.2 7.7 %collective-permute-start.14 = (bf16[256,1152]{1,0:T(8,128)(2,1)S(1)}, bf16[256,1152]{1,0:T(8,128)(2,1)S(1)}, u32[]{:S(2)}, u32[]{:S(2)}) collective-permute-start(bf16[256,1152]{1,0:T(8,128)(2,1)S(1)} %collective-permute-done.11.refs_2_.mine), channel_id=1, source_target_pairs={{0,32},{32,0},{1,33},{33,1},{2,34},{34,2},{3,35},{35,3},{4,36},{36... | collective-permute-start | bytes 1769480 | tf_op jit(solution)/shard_map/ppermute | solution.py:51
  38.2 9.6 %collective-permute-start.13 = (bf16[256,1152]{1,0:T(8,128)(2,1)S(1)}, bf16[256,1152]{1,0:T(8,128)(2,1)S(1)}, u32[]{:S(2)}, u32[]{:S(2)}) collective-permute-start(bf16[256,1152]{1,0:T(8,128)(2,1)S(1)} %collective-permute-done.10.refs_1_.mine), channel_id=1, source_target_pairs={{0,32},{32,0},{1,33},{33,1},{2,34},{34,2},{3,35},{35,3},{4,36},{36... | collective-permute-start | bytes 1769480 | tf_op jit(solution)/shard_map/ppermute | solution.py:51
  40.7 7.1 %collective-permute-start.9 = (bf16[256,1152]{1,0:T(8,128)(2,1)S(1)}, bf16[256,1152]{1,0:T(8,128)(2,1)S(1)}, u32[]{:S(2)}, u32[]{:S(2)}) collective-permute-start(bf16[256,1152]{1,0:T(8,128)(2,1)S(1)} %collective-permute-done.8.mine), channel_id=1, source_target_pairs={{0,32},{32,0},{1,33},{33,1},{2,34},{34,2},{3,35},{35,3},{4,36},{36... | collective-permute-start | bytes 1769480 | tf_op jit(solution)/shard_map/ppermute | solution.py:51
  40.7 7.1 %collective-permute-start.7 = (bf16[256,1152]{1,0:T(8,128)(2,1)S(1)}, bf16[256,1152]{1,0:T(8,128)(2,1)S(1)}, u32[]{:S(2)}, u32[]{:S(2)}) collective-permute-start(bf16[256,1152]{1,0:T(8,128)(2,1)S(1)} %collective-permute-done.6.mine), channel_id=1, source_target_pairs={{0,32},{32,0},{1,33},{33,1},{2,34},{34,2},{3,35},{35,3},{4,36},{36... | collective-permute-start | bytes 1769480 | tf_op jit(solution)/shard_map/ppermute | solution.py:51
  45.9 2.5 %collective-permute-start.5 = (bf16[256,1152]{1,0:T(8,128)(2,1)S(1)}, bf16[256,1152]{1,0:T(8,128)(2,1)S(1)}, u32[]{:S(2)}, u32[]{:S(2)}) collective-permute-start(bf16[256,1152]{1,0:T(8,128)(2,1)S(1)} %collective-permute-done.4.mine), channel_id=1, source_target_pairs={{0,32},{32,0},{1,33},{33,1},{2,34},{34,2},{3,35},{35,3},{4,36},{36... | collective-permute-start | bytes 1769480 | tf_op jit(solution)/shard_map/ppermute | solution.py:51
  45.9 3.3 %collective-permute-start.3 = (bf16[256,1152]{1,0:T(8,128)(2,1)S(1)}, bf16[256,1152]{1,0:T(8,128)(2,1)S(1)}, u32[]{:S(2)}, u32[]{:S(2)}) collective-permute-start(bf16[256,1152]{1,0:T(8,128)(2,1)S(1)} %collective-permute-done.2.mine), channel_id=1, source_target_pairs={{0,32},{32,0},{1,33},{33,1},{2,34},{34,2},{3,35},{35,3},{4,36},{36... | collective-permute-start | bytes 1769480 | tf_op jit(solution)/shard_map/ppermute | solution.py:51
  52.7 38.8 %collective-permute-start.16 = (bf16[256,1152]{1,0:T(8,128)(2,1)S(1)}, bf16[256,1152]{1,0:T(8,128)(2,1)S(1)}, u32[]{:S(2)}, u32[]{:S(2)}) collective-permute-start(bf16[256,1152]{1,0:T(8,128)(2,1)S(1)} %shard_map.70), channel_id=1, source_target_pairs={{0,16},{32,36},{2,18},{34,38},{4,20},{36,32},{6,22},{38,34},{64,80... | collective-permute-start | bytes 1769480 | tf_op jit(solution)/shard_map/ppermute | solution.py:47
  59.8 20.8 %collective-permute-start.17 = (bf16[256,1152]{1,0:T(8,128)(2,1)S(1)}, bf16[256,1152]{1,0:T(8,128)(2,1)S(1)}, u32[]{:S(2)}, u32[]{:S(2)}) collective-permute-start(bf16[256,1152]{1,0:T(8,128)(2,1)S(1)} %shard_map.72), channel_id=1, source_target_pairs={{0,80},{32,101},{2,82},{34,103},{4,84},{36,97},{6,86},{38,99},{64,... | collective-permute-start | bytes 1769480 | tf_op jit(solution)/shard_map/ppermute | solution.py:47
  66.0 17.1 %collective-permute-start.18 = (bf16[256,1152]{1,0:T(8,128)(2,1)S(1)}, bf16[256,1152]{1,0:T(8,128)(2,1)S(1)}, u32[]{:S(2)}, u32[]{:S(2)}) collective-permute-start(bf16[256,1152]{1,0:T(8,128)(2,1)S(1)} %shard_map.73), channel_id=1, source_target_pairs={{0,72},{32,99},{2,74},{34,101},{4,76},{36,103},{6,78},{38,97},{64,... | collective-permute-start | bytes 1769480 | tf_op jit(solution)/shard_map/ppermute | solution.py:47
  70.3 17.6 %collective-permute-start.19 = (bf16[256,1152]{1,0:T(8,128)(2,1)S(1)}, bf16[256,1152]{1,0:T(8,128)(2,1)S(1)}, u32[]{:S(2)}, u32[]{:S(2)}) collective-permute-start(bf16[256,1152]{1,0:T(8,128)(2,1)S(1)} %shard_map.74), channel_id=1, source_target_pairs={{0,88},{32,103},{2,90},{34,97},{4,92},{36,99},{6,94},{38,101},{64,... | collective-permute-start | bytes 1769480 | tf_op jit(solution)/shard_map/ppermute | solution.py:47
  82.8 10.9 %collective-permute-start.20 = (bf16[256,1152]{1,0:T(8,128)(2,1)S(1)}, bf16[256,1152]{1,0:T(8,128)(2,1)S(1)}, u32[]{:S(2)}, u32[]{:S(2)}) collective-permute-start(bf16[256,1152]{1,0:T(8,128)(2,1)S(1)} %shard_map.75), channel_id=1, source_target_pairs={{0,8},{32,34},{2,10},{34,36},{4,12},{36,38},{6,14},{38,32},{64,72}... | collective-permute-start | bytes 1769480 | tf_op jit(solution)/shard_map/ppermute | solution.py:47
  85.2 9.6 %collective-permute-start.21 = (bf16[256,1152]{1,0:T(8,128)(2,1)S(1)}, bf16[256,1152]{1,0:T(8,128)(2,1)S(1)}, u32[]{:S(2)}, u32[]{:S(2)}) collective-permute-start(bf16[256,1152]{1,0:T(8,128)(2,1)S(1)} %shard_map.76), channel_id=1, source_target_pairs={{0,24},{32,38},{2,26},{34,32},{4,28},{36,34},{6,30},{38,36},{64,88... | collective-permute-start | bytes 1769480 | tf_op jit(solution)/shard_map/ppermute | solution.py:47
  90.0 10.0 %collective-permute-start.22 = (bf16[256,1152]{1,0:T(8,128)(2,1)S(1)}, bf16[256,1152]{1,0:T(8,128)(2,1)S(1)}, u32[]{:S(2)}, u32[]{:S(2)}) collective-permute-start(bf16[256,1152]{1,0:T(8,128)(2,1)S(1)} %shard_map.77), channel_id=1, source_target_pairs={{0,64},{32,97},{2,66},{34,99},{4,68},{36,101},{6,70},{38,103},{64,... | collective-permute-start | bytes 1769480 | tf_op jit(solution)/shard_map/ppermute | solution.py:47
  101.2 2.1 %collective-permute-start.23 = (f32[128,1152]{1,0:T(8,128)S(1)}, f32[128,1152]{1,0:T(8,128)S(1)}, u32[]{:S(2)}, u32[]{:S(2)}) collective-permute-start(f32[128,1152]{1,0:T(8,128)S(1)} %get-tuple-element.19), channel_id=1, source_target_pairs={{0,32},{32,0},{1,33},{33,1},{2,34},{34,2},{3,35},{35,3},{4,36},{36... | collective-permute-start | bytes 1769480 | tf_op jit(solution)/shard_map/ppermute | solution.py:51

commit v5 on v4

--- a/solution.py
+++ b/solution.py
@@ -22,8 +22,8 @@
 ANY = pl.BlockSpec(memory_space=pl.ANY)
 PARAMS = pltpu.CompilerParams(vmem_limit_bytes=VMEM_BYTES)
 
-WAYS = ((2, 1), (1, 1), (3, 1), (2, 0), (1, 0), (3, 0), (0, 1))
-EARLY = ((0, 1), (1, 0), (3, 0))
+OWN, RIGHT, LEFT, FAR = (0, 0), (1, 0), (3, 0), (2, 0)
+PARTNER, RIGHT_ACROSS, LEFT_ACROSS, FAR_ACROSS = (0, 1), (1, 1), (3, 1), (2, 1)
 
 
 def place(core, x, y, z):
@@ -63,11 +63,22 @@
     return values * scale, scale
 
 
-def normalize_kernel(is_first, image, text, image_there, text_there, raw, mine, theirs):
-    rows = image.shape[0]
+def normalize_kernel(is_first, *refs):
+    sources, (raw, mine, theirs, held, sems) = refs[:4], refs[4:]
+    rows = sources[0].shape[0]
+    cut = rows // 4
+    copies = []
+    for k, source in enumerate(sources):
+        for n in range(4):
+            at = pl.ds(n * cut, cut)
+            copies.append(pltpu.make_async_copy(source.at[at], held.at[k, at], sems.at[4 * k + n]))
+    for copy in copies:
+        copy.start()
+    for copy in copies:
+        copy.wait()
     first = is_first[0] > 0
-    images = (image[...].astype(FULL), image_there[...].astype(FULL))
-    texts = (text[...].astype(FULL), text_there[...].astype(FULL))
+    image, text, image_there, text_there = [held[k].astype(FULL) for k in range(4)]
+    images, texts = (image, image_there), (text, text_there)
     for k in range(2):
         at = pl.ds(k * rows, rows)
         of_image = jnp.where(first, images[k], images[1 - k])
@@ -95,45 +106,55 @@
     return total
 
 
-def early_kernel(count, affine, *refs):
-    mine, theirs, sums, coupling = refs[:count], refs[count : 2 * count], refs[2 * count : -1], refs[-1]
+def sums_kernel(count, n_theirs, summed, n_unread, diagonal, affine, *refs):
+    mine, refs = refs[:count], refs[count:]
+    theirs, refs = refs[:n_theirs], refs[n_theirs:]
+    starts, refs = refs[: count * summed], refs[count * summed + n_unread :]
+    sums, coupling = refs[:count], refs[-1]
     for k in range(count):
-        sums[k][...] = accumulate(affine, mine[k][...], theirs, coupling, None, k == 0)
-
-
-def early_sums(affine, mine, theirs):
-    count = len(mine)
+        start = starts[k][...] if summed else None
+        sums[k][...] = accumulate(affine, mine[k][...], theirs, coupling, start, diagonal and k == 0)
+
+
+def sums_of(affine, mine, theirs, starts=(), passed=(), after=(), diagonal=False):
+    count, n_theirs = len(mine), len(theirs)
+    before = 1 + count + n_theirs + len(starts)
     unit, width = mine[0].shape
     return pl.pallas_call(
-        functools.partial(early_kernel, count),
-        out_shape=[jax.ShapeDtypeStruct((unit, width), FULL)] * count,
-        in_specs=[SMEM] + [VMEM] * (2 * count),
-        out_specs=[VMEM] * count,
-        scratch_shapes=[pltpu.VMEM((unit, count * unit), HALF)],
+        functools.partial(
+            sums_kernel, count, n_theirs, bool(starts), len(passed) + len(after), diagonal
+        ),
+        out_shape=[jax.ShapeDtypeStruct((unit, width), FULL)] * count
+        + [jax.ShapeDtypeStruct(array.shape, array.dtype) for array in passed],
+        in_specs=[SMEM] + [VMEM] * (before - 1) + [ANY] * (len(passed) + len(after)),
+        out_specs=[VMEM] * count + [ANY] * len(passed),
+        input_output_aliases={before + k: count + k for k in range(len(passed))},
+        scratch_shapes=[pltpu.VMEM((unit, n_theirs * unit), HALF)],
         cost_estimate=pl.CostEstimate(
-            flops=4 * (count * unit) ** 2 * width,
+            flops=4 * count * n_theirs * unit**2 * width,
             bytes_accessed=8 * count * unit * width,
-            transcendentals=(count * unit) ** 2,
+            transcendentals=count * n_theirs * unit**2,
         ),
         compiler_params=PARAMS,
-    )(affine, *mine, *theirs)
-
-
-def part_kernel(count, summed, n_after, affine, mine, *refs):
+    )(affine, *mine, *theirs, *starts, *passed, *after)
+
+
+def part_kernel(count, n_added, n_after, affine, mine, *refs):
     theirs, refs = refs[:count], refs[count:]
-    start = refs[0][...] if summed else None
+    start = None
+    for ref in refs[:n_added]:
+        start = ref[...].astype(FULL) if start is None else start + ref[...].astype(FULL)
     part, coupling = refs[-2:]
     part[...] = accumulate(affine, mine[...], theirs, coupling, start, False).astype(HALF)
 
 
-def part_of(affine, mine, theirs, start, after):
+def part_of(affine, mine, theirs, added=(), after=()):
     unit, width = mine.shape
     count = len(theirs)
-    starts = [] if start is None else [start]
     return pl.pallas_call(
-        functools.partial(part_kernel, count, len(starts), len(after)),
+        functools.partial(part_kernel, count, len(added), len(after)),
         out_shape=jax.ShapeDtypeStruct((unit, width), HALF),
-        in_specs=[SMEM] + [VMEM] * (1 + count + len(starts)) + [ANY] * len(after),
+        in_specs=[SMEM] + [VMEM] * (1 + count + len(added)) + [ANY] * len(after),
         out_specs=VMEM,
         scratch_shapes=[pltpu.VMEM((unit, count * unit), HALF)],
         cost_estimate=pl.CostEstimate(
@@ -142,7 +163,7 @@
             transcendentals=count * unit**2,
         ),
         compiler_params=PARAMS,
-    )(affine, mine, *theirs, *starts, *after)
+    )(affine, mine, *theirs, *added, *after)
 
 
 def finish_kernel(core, multiplier, raw, *refs):
@@ -173,8 +194,12 @@
     raw, own, own_theirs = pl.pallas_call(
         normalize_kernel,
         out_shape=[unit] * 3,
-        in_specs=[SMEM] + [VMEM] * 4,
+        in_specs=[SMEM] + [ANY] * 4,
         out_specs=[VMEM] * 3,
+        scratch_shapes=[
+            pltpu.VMEM((4, rows, width), HALF),
+            pltpu.SemaphoreType.DMA((16,)),
+        ],
         compiler_params=PARAMS,
     )(
         is_first.astype(FULL).reshape(1),
@@ -184,24 +209,44 @@
         other_core(caption_vectors_raw),
     )
 
-    mine, theirs = {(0, 0): own}, {(0, 0): own_theirs}
-    for steps, across in reversed(WAYS):
-        mine[steps, across] = sent(own, -steps, across)
-        theirs[steps, across] = other_core(mine[steps, across])
-    first = [(0, 0), *EARLY]
-    second = [way for way in mine if way not in first]
-    sums = early_sums(affine, [mine[w] for w in first], [theirs[w] for w in first])
-    sums = dict(zip(first, sums, strict=True))
-
-    arrived = []
-    for k, way in enumerate((*WAYS, (0, 0))):
-        after = arrived[k - 4 : k - 3] if k >= 4 else []
-        if way in sums:
-            part = part_of(affine, mine[way], [theirs[w] for w in second], sums[way], after)
-        else:
-            part = part_of(affine, mine[way], [theirs[w] for w in (*first, *second)], None, after)
-        if way != (0, 0):
-            arrived.append(sent(part, *way))
+    mine = {OWN: own}
+    for way in (RIGHT, LEFT, PARTNER, RIGHT_ACROSS, LEFT_ACROSS):
+        mine[way] = sent(own, -way[0], way[1])
+    mine[FAR] = sent(mine[RIGHT], -1, 0)
+    mine[FAR_ACROSS] = sent(mine[LEFT_ACROSS], 1, 0)
+    theirs = {OWN: own_theirs}
+    for way in (RIGHT, LEFT, PARTNER, RIGHT_ACROSS, LEFT_ACROSS):
+        theirs[way] = other_core(mine[way])
+
+    def pick(units, ways):
+        return [units[way] for way in ways]
+
+    one, two, three = (OWN, RIGHT, LEFT), (PARTNER, RIGHT_ACROSS, LEFT_ACROSS), (FAR, FAR_ACROSS)
+    sums = sums_of(affine, pick(mine, one), pick(theirs, one), diagonal=True)
+    sums = sums_of(affine, pick(mine, one), pick(theirs, two), sums)
+    sums += sums_of(affine, pick(mine, two[:1]), pick(theirs, one + two))
+    *more, mine[FAR], mine[FAR_ACROSS] = sums_of(
+        affine,
+        pick(mine, two[1:]),
+        pick(theirs, one + two),
+        passed=pick(mine, three),
+        after=[sums[0], sums[3]],
+    )
+    for way in three:
+        theirs[way] = other_core(mine[way])
+    sums = dict(zip(one + two, [*sums, *more], strict=True))
+
+    def part(way, added=(), after=()):
+        if way in three:
+            return part_of(affine, mine[way], pick(theirs, one + two + three), added, after)
+        return part_of(affine, mine[way], pick(theirs, three), [sums[way], *added], after)
+
+    far = sent(part(FAR), 1, 0)
+    far_across = sent(part(FAR_ACROSS), -1, 0)
+    arrived = [sent(part(way), *way) for way in (RIGHT_ACROSS, PARTNER, LEFT)]
+    arrived.append(sent(part(LEFT_ACROSS, [far_across]), *LEFT_ACROSS))
+    arrived.append(sent(part(RIGHT, [far], arrived[:1]), *RIGHT))
+    own_part = part(OWN, after=arrived[1:2])
 
     here, there = pl.pallas_call(
         finish_kernel,
@@ -210,7 +255,7 @@
         out_specs=[VMEM] * 2,
         scratch_shapes=[pltpu.VMEM((2 * rows, width), FULL)],
         compiler_params=PARAMS,
-    )(core.reshape(1), multiplier, raw, part, *arrived)
+    )(core.reshape(1), multiplier, raw, own_part, *arrived)
     back = other_core(there)
     return (jnp.where(is_first, here, back), jnp.where(is_first, back, here))
 

time: 105 us -> 103 us (0.981)
  starting transfers between devices: 54.5 us -> 36.5 us
  waiting for transfers between devices: 13.7 us -> 24.7 us
  Pallas kernels: 30.3 us -> 35.5 us
    ppermute x10, starting transfers between devices: 23.4 us -> 9.04 us  [other_core(): return lax.ppermute(value, 'core', [(0, 1), (1, 0)])]
    ppermute x14, waiting for transfers between devices: 8.53 us -> 19 us  [sent(): return lax.ppermute(value, FINE_AXES, pairs)]
    ppermute x14, starting transfers between devices: 31.1 us -> 27.4 us  [sent(): return lax.ppermute(value, FINE_AXES, pairs)]
    pallas_call x9 -> x12, Pallas kernels: 28.6 us -> 32.3 us  [the longest x8 16.2 us: part_of(): pl.pallas_call(functools.partial(part_kernel, count, len(added), len(afte...]
    pallas_call x1, Pallas kernels: 0.61 us -> 2.2 us  [on_device(): pl.pallas_call(normalize_kernel, out_shape=[unit] * 3, in_specs=[SMEM] +...]
  transfers between devices with their start and end apart: 24 -> 24, of which waited for: 9 -> 10; matrix products, arithmetic and copies ran while one was open for 0% -> 0% of each run, Pallas kernels for 24% -> 23%
where the time goes in v5:
time: 103 us; the launch traced here: 102 us
  starting transfers between devices  36.5 us (35%)
  Pallas kernels  35.5 us (34%)
  waiting for transfers between devices  24.7 us (24%)
  between operations  2.76 us (3%)
  local copies, waits for them, and re-layouts  1.92 us (2%)
  other arithmetic  1.16 us (1%)
    ppermute x14, starting transfers between devices, sent(): return lax.ppermute(value, FINE_AXES, pairs)  27.4 us
    ppermute x14, waiting for transfers between devices, sent(): return lax.ppermute(value, FINE_AXES, pairs)  19 us
    pallas_call x8, Pallas kernels, part_of(): pl.pallas_call(functools.partial(part_kernel, count, len(added), len(afte...  16.2 us
    pallas_call x4, Pallas kernels, sums_of(): pl.pallas_call(functools.partial(sums_kernel, count, n_theirs, bool(start...  16.1 us
    ppermute x10, starting transfers between devices, other_core(): return lax.ppermute(value, 'core', [(0, 1), (1, 0)])  9.04 us
    ppermute x10, waiting for transfers between devices, other_core(): return lax.ppermute(value, 'core', [(0, 1), (1, 0)])  5.73 us
    pallas_call x1, Pallas kernels, on_device(): pl.pallas_call(normalize_kernel, out_shape=[unit] * 3, in_specs=[SMEM] +...  2.2 us
  transfers between devices with their start and end apart: 24, of which 10 were waited for; matrix products, arithmetic and copies ran while one was open for 0% of the time, Pallas kernels for 23%

profile of v5, /device:TPU:1, one launch (start us, length us, event | category | flops | bytes accessed | tf_op | source)
XLA Modules:
  0.0 102.5 jit_solution(2794396195957846797)
XLA Ops:
  0.6 1.5 %collective-permute-start = (bf16[128,1152]{1,0:T(8,128)(2,1)}, bf16[128,1152]{1,0:T(8,128)(2,1)S(1)}, u32[]{:S(2)}, u32[]{:S(2)}) collective-permute-start(bf16[128,1152]{1,0:T(8,128)(2,1)} %refs_0_.1), channel_id=1, source_target_pairs={{0,32},{32,0},{1,33},{33,1},{2,34},{34,2},{3,35},{35,3},{4,36},{36... | collective-permute-start | bytes 884744 | tf_op jit(solution)/shard_map/ppermute | solution.py:51
  2.1 0.1 collective-permute-start.1
  2.2 1.3 %collective-permute-done.refs_2_ = bf16[128,1152]{1,0:T(8,128)(2,1)S(1)} collective-permute-done((bf16[128,1152]{1,0:T(8,128)(2,1)}, bf16[128,1152]{1,0:T(8,128)(2,1)S(1)}, u32[]{:S(2)}, u32[]{:S(2)}) %collective-permute-start) | collective-permute-done | bytes 294944 | tf_op jit(solution)/shard_map/ppermute | solution.py:51
  3.6 0.4 collective-permute-done.1.refs_3_
  4.0 1.0 copy-done
  4.9 1.0 copy-done.1
  5.9 2.2 %shard_map.68 = (bf16[256,1152]{1,0:T(8,128)(2,1)S(1)}, bf16[256,1152]{1,0:T(8,128)(2,1)S(1)}, bf16[256,1152]{1,0:T(8,128)(2,1)S(1)}) custom-call(f32[1]{0:T(128)} %bitcast.1.is_first, bf16[128,1152]{1,0:T(8,128)(2,1)S(1)} %copy-done, bf16[128,1152]{1,0:T(8,128)(2,1)S(1)} %copy-done.1, bf16[128,1152]{1,0:T(8,128)(2,1)S(1)} %collective-permute-done.refs_2_, ...), custom_call_target="tpu_custom_call" | custom-call | tf_op jit(solution)/shard_map/pallas_call | solution.py:194
  8.1 2.9 %collective-permute-start.8 = (bf16[256,1152]{1,0:T(8,128)(2,1)S(1)}, bf16[256,1152]{1,0:T(8,128)(2,1)S(1)}, u32[]{:S(2)}, u32[]{:S(2)}) collective-permute-start(bf16[256,1152]{1,0:T(8,128)(2,1)S(1)} %get-tuple-element.18.refs_0_.mine), channel_id=1, source_target_pairs={{0,64},{32,97},{2,66},{34,99},{4,68},{36,101},{6,70},{38,103},{64,... | collective-permute-start | bytes 1769480 | tf_op jit(solution)/shard_map/ppermute | solution.py:47
  11.0 1.6 %collective-permute-start.6 = (bf16[256,1152]{1,0:T(8,128)(2,1)S(1)}, bf16[256,1152]{1,0:T(8,128)(2,1)S(1)}, u32[]{:S(2)}, u32[]{:S(2)}) collective-permute-start(bf16[256,1152]{1,0:T(8,128)(2,1)S(1)} %get-tuple-element.18.refs_0_.mine), channel_id=1, source_target_pairs={{0,8},{32,34},{2,10},{34,36},{4,12},{36,38},{6,14},{38,32},{64,72}... | collective-permute-start | bytes 1769480 | tf_op jit(solution)/shard_map/ppermute | solution.py:47
  12.6 2.1 %collective-permute-start.4 = (bf16[256,1152]{1,0:T(8,128)(2,1)S(1)}, bf16[256,1152]{1,0:T(8,128)(2,1)S(1)}, u32[]{:S(2)}, u32[]{:S(2)}) collective-permute-start(bf16[256,1152]{1,0:T(8,128)(2,1)S(1)} %get-tuple-element.18.refs_0_.mine), channel_id=1, source_target_pairs={{0,24},{32,38},{2,26},{34,32},{4,28},{36,34},{6,30},{38,36},{64,88... | collective-permute-start | bytes 1769480 | tf_op jit(solution)/shard_map/ppermute | solution.py:47
  14.8 4.8 %collective-permute-start.2 = (bf16[256,1152]{1,0:T(8,128)(2,1)S(1)}, bf16[256,1152]{1,0:T(8,128)(2,1)S(1)}, u32[]{:S(2)}, u32[]{:S(2)}) collective-permute-start(bf16[256,1152]{1,0:T(8,128)(2,1)S(1)} %get-tuple-element.18.refs_0_.mine), channel_id=1, source_target_pairs={{0,88},{32,103},{2,90},{34,97},{4,92},{36,99},{6,94},{38,101},{64,... | collective-permute-start | bytes 1769480 | tf_op jit(solution)/shard_map/ppermute | solution.py:47
  19.6 9.1 %collective-permute-done.6.refs_2_.mine = bf16[256,1152]{1,0:T(8,128)(2,1)S(1)} collective-permute-done((bf16[256,1152]{1,0:T(8,128)(2,1)S(1)}, bf16[256,1152]{1,0:T(8,128)(2,1)S(1)}, u32[]{:S(2)}, u32[]{:S(2)}) %collective-permute-start.6) | collective-permute-done | bytes 589856 | tf_op jit(solution)/shard_map/ppermute | solution.py:47
  28.7 0.5 collective-permute-start.5
  29.2 2.4 %collective-permute-start.11 = (bf16[256,1152]{1,0:T(8,128)(2,1)S(1)}, bf16[256,1152]{1,0:T(8,128)(2,1)S(1)}, u32[]{:S(2)}, u32[]{:S(2)}) collective-permute-start(bf16[256,1152]{1,0:T(8,128)(2,1)S(1)} %collective-permute-done.3.refs_1_.mine), channel_id=1, source_target_pairs={{0,32},{32,0},{1,33},{33,1},{2,34},{34,2},{3,35},{35,3},{4,36},{36... | collective-permute-start | bytes 1769480 | tf_op jit(solution)/shard_map/ppermute | solution.py:51
  31.6 0.7 collective-permute-done.2.refs_0_.mine
  32.3 1.4 %collective-permute-start.10 = (bf16[256,1152]{1,0:T(8,128)(2,1)S(1)}, bf16[256,1152]{1,0:T(8,128)(2,1)S(1)}, u32[]{:S(2)}, u32[]{:S(2)}) collective-permute-start(bf16[256,1152]{1,0:T(8,128)(2,1)S(1)} %collective-permute-done.2.refs_0_.mine), channel_id=1, source_target_pairs={{0,32},{32,0},{1,33},{33,1},{2,34},{34,2},{3,35},{35,3},{4,36},{36... | collective-permute-start | bytes 1769480 | tf_op jit(solution)/shard_map/ppermute | solution.py:51
  35.1 0.1 pad_maximum_fusion.affine
  35.1 3.9 %collective-permute-start.12 = (bf16[256,1152]{1,0:T(8,128)(2,1)S(1)}, bf16[256,1152]{1,0:T(8,128)(2,1)S(1)}, u32[]{:S(2)}, u32[]{:S(2)}) collective-permute-start(bf16[256,1152]{1,0:T(8,128)(2,1)S(1)} %collective-permute-done.4.refs_1_.mine), channel_id=1, source_target_pairs={{0,24},{32,38},{2,26},{34,32},{4,28},{36,34},{6,30},{38,36},{64,88... | collective-permute-start | bytes 1769480 | tf_op jit(solution)/shard_map/ppermute | solution.py:47
  39.0 2.8 %shard_map.71.refs_11_.refs_2_ = f32[256,1152]{1,0:T(8,128)S(1)} custom-call(f32[2]{0:T(128)S(1)} %pad_maximum_fusion.affine, bf16[256,1152]{1,0:T(8,128)(2,1)S(1)} %collective-permute-done.8.refs_0_.mine, bf16[256,1152]{1,0:T(8,128)(2,1)S(1)} %get-tuple-element.19.refs_3_.refs_1_.refs_2_.refs_0_, ...), custom_call_target="tpu_custom_call" | custom-call | flops 1811939328 | bytes 2359296 | tf_op jit(solution)/shard_map/pallas_call | solution.py:123
  41.9 4.1 %shard_map.69 = (f32[256,1152]{1,0:T(8,128)S(1)}, f32[256,1152]{1,0:T(8,128)S(1)}, f32[256,1152]{1,0:T(8,128)S(1)}) custom-call(f32[2]{0:T(128)S(1)} %pad_maximum_fusion.affine, bf16[256,1152]{1,0:T(8,128)(2,1)S(1)} %get-tuple-element.18.refs_0_.mine, bf16[256,1152]{1,0:T(8,128)(2,1)S(1)} %collective-permute-done.4.refs_1_.mine, ...), custom_call_target="tpu_custom_call" | custom-call | flops 2717908992 | bytes 7077888 | tf_op jit(solution)/shard_map/pallas_call | solution.py:123
  46.0 4.3 %shard_map.70 = (f32[256,1152]{1,0:T(8,128)S(1)}, f32[256,1152]{1,0:T(8,128)S(1)}, f32[256,1152]{1,0:T(8,128)S(1)}) custom-call(f32[2]{0:T(128)S(1)} %pad_maximum_fusion.affine, bf16[256,1152]{1,0:T(8,128)(2,1)S(1)} %get-tuple-element.18.refs_0_.mine, bf16[256,1152]{1,0:T(8,128)(2,1)S(1)} %collective-permute-done.4.refs_1_.mine, ...), custom_call_target="tpu_custom_call" | custom-call | flops 2717908992 | bytes 7077888 | tf_op jit(solution)/shard_map/pallas_call | solution.py:123
  50.3 4.9 %shard_map.72 = (f32[256,1152]{1,0:T(8,128)S(1)}, f32[256,1152]{1,0:T(8,128)S(1)}, bf16[256,1152]{1,0:T(8,128)(2,1)S(1)}, bf16[256,1152]{1,0:T(8,128)(2,1)S(1)}) custom-call(f32[2]{0:T(128)S(1)} %pad_maximum_fusion.affine, bf16[256,1152]{1,0:T(8,128)(2,1)S(1)} %collective-permute-done.2.refs_0_.mine, ...), custom_call_target="tpu_custom_call", output_to_operand_aliasing={{2}: (9, {}), {3}: (10, {})} | custom-call | flops 3623878656 | bytes 4718592 | tf_op jit(solution)/shard_map/pallas_call | solution.py:123
  55.2 0.1 collective-permute-start.14
  55.3 0.5 collective-permute-start.15
  55.8 1.5 %collective-permute-done.14.refs_0_.refs_6_ = bf16[256,1152]{1,0:T(8,128)(2,1)S(1)} collective-permute-done((bf16[256,1152]{1,0:T(8,128)(2,1)S(1)}, bf16[256,1152]{1,0:T(8,128)(2,1)S(1)}, u32[]{:S(2)}, u32[]{:S(2)}) %collective-permute-start.14) | collective-permute-done | bytes 589856 | tf_op jit(solution)/shard_map/ppermute | solution.py:51
  57.2 0.8 collective-permute-done.15.refs_1_.refs_7_
  58.1 3.5 %shard_map.77 = bf16[256,1152]{1,0:T(8,128)(2,1)S(1)} custom-call(f32[2]{0:T(128)S(1)} %pad_maximum_fusion.affine, bf16[256,1152]{1,0:T(8,128)(2,1)S(1)} %get-tuple-element.25.mine, bf16[256,1152]{1,0:T(8,128)(2,1)S(1)} %get-tuple-element.19.refs_3_.refs_1_.refs_2_.refs_0_, bf16[256,1152]{1,0:T(8,128)(2,1)S(1)} %collective-permute-done.5.refs_4_.refs_2_.refs_3_.refs_1_, ...), custom_call_target="tpu_custom_call" | custom-call | flops 2415919104 | bytes 589824 | tf_op jit(solution)/shard_map/pallas_call | solution.py:154
  61.6 2.7 %collective-permute-start.19 = (bf16[256,1152]{1,0:T(8,128)(2,1)S(1)}, bf16[256,1152]{1,0:T(8,128)(2,1)S(1)}, u32[]{:S(2)}, u32[]{:S(2)}) collective-permute-start(bf16[256,1152]{1,0:T(8,128)(2,1)S(1)} %shard_map.77), channel_id=1, source_target_pairs={{0,24},{32,38},{2,26},{34,32},{4,28},{36,34},{6,30},{38,36},{64,88... | collective-permute-start | bytes 1769480 | tf_op jit(solution)/shard_map/ppermute | solution.py:47
  64.3 3.5 %shard_map.79 = bf16[256,1152]{1,0:T(8,128)(2,1)S(1)} custom-call(f32[2]{0:T(128)S(1)} %pad_maximum_fusion.affine, bf16[256,1152]{1,0:T(8,128)(2,1)S(1)} %get-tuple-element.24.mine, bf16[256,1152]{1,0:T(8,128)(2,1)S(1)} %get-tuple-element.19.refs_3_.refs_1_.refs_2_.refs_0_, bf16[256,1152]{1,0:T(8,128)(2,1)S(1)} %collective-permute-done.5.refs_4_.refs_2_.refs_3_.refs_1_, ...), custom_call_target="tpu_custom_call" | custom-call | flops 2415919104 | bytes 589824 | tf_op jit(solution)/shard_map/pallas_call | solution.py:154
  67.8 0.1 collective-permute-start.21
  67.9 1.5 %shard_map.75 = bf16[256,1152]{1,0:T(8,128)(2,1)S(1)} custom-call(f32[2]{0:T(128)S(1)} %pad_maximum_fusion.affine, bf16[256,1152]{1,0:T(8,128)(2,1)S(1)} %collective-permute-done.2.refs_0_.mine, bf16[256,1152]{1,0:T(8,128)(2,1)S(1)} %collective-permute-done.14.refs_0_.refs_6_, bf16[256,1152]{1,0:T(8,128)(2,1)S(1)} %collective-permute-done.15.refs_1_.refs_7_, ...), custom_call_target="tpu_custom_call" | custom-call | flops 603979776 | bytes 589824 | tf_op jit(solution)/shard_map/pallas_call | solution.py:154
  69.5 1.3 %collective-permute-start.17 = (bf16[256,1152]{1,0:T(8,128)(2,1)S(1)}, bf16[256,1152]{1,0:T(8,128)(2,1)S(1)}, u32[]{:S(2)}, u32[]{:S(2)}) collective-permute-start(bf16[256,1152]{1,0:T(8,128)(2,1)S(1)} %shard_map.75), channel_id=1, source_target_pairs={{0,72},{32,99},{2,74},{34,101},{4,76},{36,103},{6,78},{38,97},{64,... | collective-permute-start | bytes 1769480 | tf_op jit(solution)/shard_map/ppermute | solution.py:47
  70.8 1.5 %shard_map.73 = bf16[256,1152]{1,0:T(8,128)(2,1)S(1)} custom-call(f32[2]{0:T(128)S(1)} %pad_maximum_fusion.affine, bf16[256,1152]{1,0:T(8,128)(2,1)S(1)} %collective-permute-done.8.refs_0_.mine, bf16[256,1152]{1,0:T(8,128)(2,1)S(1)} %collective-permute-done.14.refs_0_.refs_6_, bf16[256,1152]{1,0:T(8,128)(2,1)S(1)} %collective-permute-done.15.refs_1_.refs_7_, ...), custom_call_target="tpu_custom_call" | custom-call | flops 603979776 | bytes 589824 | tf_op jit(solution)/shard_map/pallas_call | solution.py:154
  72.3 1.6 %collective-permute-start.16 = (bf16[256,1152]{1,0:T(8,128)(2,1)S(1)}, bf16[256,1152]{1,0:T(8,128)(2,1)S(1)}, u32[]{:S(2)}, u32[]{:S(2)}) collective-permute-start(bf16[256,1152]{1,0:T(8,128)(2,1)S(1)} %shard_map.73), channel_id=1, source_target_pairs={{0,64},{32,97},{2,66},{34,99},{4,68},{36,101},{6,70},{38,103},{64,... | collective-permute-start | bytes 1769480 | tf_op jit(solution)/shard_map/ppermute | solution.py:47
  73.9 1.5 %shard_map.76 = bf16[256,1152]{1,0:T(8,128)(2,1)S(1)} custom-call(f32[2]{0:T(128)S(1)} %pad_maximum_fusion.affine, bf16[256,1152]{1,0:T(8,128)(2,1)S(1)} %collective-permute-done.6.refs_2_.mine, bf16[256,1152]{1,0:T(8,128)(2,1)S(1)} %collective-permute-done.14.refs_0_.refs_6_, bf16[256,1152]{1,0:T(8,128)(2,1)S(1)} %collective-permute-done.15.refs_1_.refs_7_, ...), custom_call_target="tpu_custom_call" | custom-call | flops 603979776 | bytes 589824 | tf_op jit(solution)/shard_map/pallas_call | solution.py:154
  75.4 2.7 %collective-permute-start.18 = (bf16[256,1152]{1,0:T(8,128)(2,1)S(1)}, bf16[256,1152]{1,0:T(8,128)(2,1)S(1)}, u32[]{:S(2)}, u32[]{:S(2)}) collective-permute-start(bf16[256,1152]{1,0:T(8,128)(2,1)S(1)} %shard_map.76), channel_id=1, source_target_pairs={{0,24},{32,38},{2,26},{34,32},{4,28},{36,34},{6,30},{38,36},{64,88... | collective-permute-start | bytes 1769480 | tf_op jit(solution)/shard_map/ppermute | solution.py:47
  78.1 1.5 %shard_map.78 = bf16[256,1152]{1,0:T(8,128)(2,1)S(1)} custom-call(f32[2]{0:T(128)S(1)} %pad_maximum_fusion.affine, bf16[256,1152]{1,0:T(8,128)(2,1)S(1)} %collective-permute-done.3.refs_1_.mine, bf16[256,1152]{1,0:T(8,128)(2,1)S(1)} %collective-permute-done.14.refs_0_.refs_6_, bf16[256,1152]{1,0:T(8,128)(2,1)S(1)} %collective-permute-done.15.refs_1_.refs_7_, ...), custom_call_target="tpu_custom_call" | custom-call | flops 603979776 | bytes 589824 | tf_op jit(solution)/shard_map/pallas_call | solution.py:154
  79.7 3.6 %collective-permute-start.20 = (bf16[256,1152]{1,0:T(8,128)(2,1)S(1)}, bf16[256,1152]{1,0:T(8,128)(2,1)S(1)}, u32[]{:S(2)}, u32[]{:S(2)}) collective-permute-start(bf16[256,1152]{1,0:T(8,128)(2,1)S(1)} %shard_map.78), channel_id=1, source_target_pairs={{0,88},{32,103},{2,90},{34,97},{4,92},{36,99},{6,94},{38,101},{64,... | collective-permute-start | bytes 1769480 | tf_op jit(solution)/shard_map/ppermute | solution.py:47
  83.3 1.1 %collective-permute-done.21.refs_3_ = bf16[256,1152]{1,0:T(8,128)(2,1)S(1)} collective-permute-done((bf16[256,1152]{1,0:T(8,128)(2,1)S(1)}, bf16[256,1152]{1,0:T(8,128)(2,1)S(1)}, u32[]{:S(2)}, u32[]{:S(2)}) %collective-permute-start.21) | collective-permute-done | bytes 589856 | tf_op jit(solution)/shard_map/ppermute | solution.py:47
  84.5 1.5 %shard_map.80 = bf16[256,1152]{1,0:T(8,128)(2,1)S(1)} custom-call(f32[2]{0:T(128)S(1)} %pad_maximum_fusion.affine, bf16[256,1152]{1,0:T(8,128)(2,1)S(1)} %collective-permute-done.4.refs_1_.mine, bf16[256,1152]{1,0:T(8,128)(2,1)S(1)} %collective-permute-done.14.refs_0_.refs_6_, bf16[256,1152]{1,0:T(8,128)(2,1)S(1)} %collective-permute-done.15.refs_1_.refs_7_, ...), custom_call_target="tpu_custom_call" | custom-call | flops 603979776 | bytes 589824 | tf_op jit(solution)/shard_map/pallas_call | solution.py:154
  86.0 0.1 collective-permute-start.22
  86.7 1.5 %shard_map.74.refs_0_ = bf16[256,1152]{1,0:T(8,128)(2,1)S(1)} custom-call(f32[2]{0:T(128)S(1)} %pad_maximum_fusion.affine, bf16[256,1152]{1,0:T(8,128)(2,1)S(1)} %get-tuple-element.18.refs_0_.mine, bf16[256,1152]{1,0:T(8,128)(2,1)S(1)} %collective-permute-done.14.refs_0_.refs_6_, bf16[256,1152]{1,0:T(8,128)(2,1)S(1)} %collective-permute-done.15.refs_1_.refs_7_, ...), custom_call_target="tpu_custom_call" | custom-call | flops 603979776 | bytes 589824 | tf_op jit(solution)/shard_map/pallas_call | solution.py:154
  88.3 4.2 %collective-permute-done.20.refs_4_ = bf16[256,1152]{1,0:T(8,128)(2,1)S(1)} collective-permute-done((bf16[256,1152]{1,0:T(8,128)(2,1)S(1)}, bf16[256,1152]{1,0:T(8,128)(2,1)S(1)}, u32[]{:S(2)}, u32[]{:S(2)}) %collective-permute-start.20) | collective-permute-done | bytes 589856 | tf_op jit(solution)/shard_map/ppermute | solution.py:47
  92.4 3.9 %collective-permute-done.22.refs_5_ = bf16[256,1152]{1,0:T(8,128)(2,1)S(1)} collective-permute-done((bf16[256,1152]{1,0:T(8,128)(2,1)S(1)}, bf16[256,1152]{1,0:T(8,128)(2,1)S(1)}, u32[]{:S(2)}, u32[]{:S(2)}) %collective-permute-start.22) | collective-permute-done | bytes 589856 | tf_op jit(solution)/shard_map/ppermute | solution.py:47
  96.3 1.0 shard_map.81
  97.3 2.5 %collective-permute-start.23 = (f32[128,1152]{1,0:T(8,128)S(1)}, f32[128,1152]{1,0:T(8,128)S(1)}, u32[]{:S(2)}, u32[]{:S(2)}) collective-permute-start(f32[128,1152]{1,0:T(8,128)S(1)} %get-tuple-element.31), channel_id=1, source_target_pairs={{0,32},{32,0},{1,33},{33,1},{2,34},{34,2},{3,35},{35,3},{4,36},{36... | collective-permute-start | bytes 1769480 | tf_op jit(solution)/shard_map/ppermute | solution.py:51
  99.8 1.6 %collective-permute-done.23 = f32[128,1152]{1,0:T(8,128)S(1)} collective-permute-done((f32[128,1152]{1,0:T(8,128)S(1)}, f32[128,1152]{1,0:T(8,128)S(1)}, u32[]{:S(2)}, u32[]{:S(2)}) %collective-permute-start.23) | collective-permute-done | bytes 589856 | tf_op jit(solution)/shard_map/ppermute | solution.py:51
  101.4 1.1 %broadcast_select_fusion = (f32[128,1152]{1,0:T(8,128)}, f32[128,1152]{1,0:T(8,128)}) fusion(f32[128,1152]{1,0:T(8,128)S(1)} %collective-permute-done.23, f32[128,1152]{1,0:T(8,128)S(1)} %get-tuple-element.30, pred[]{:T(512)S(6)} %eq.3), kind=kLoop, calls=%fused_computation | loop fusion | flops 294912 | bytes 2359297 | tf_op jit(solution)/shard_map/jit(_where)/select_n | solution.py:260
  (20 shorter events, 0.1 us)
Async XLA Ops:
  0.6 2.9 %collective-permute-start = (bf16[128,1152]{1,0:T(8,128)(2,1)}, bf16[128,1152]{1,0:T(8,128)(2,1)S(1)}, u32[]{:S(2)}, u32[]{:S(2)}) collective-permute-start(bf16[128,1152]{1,0:T(8,128)(2,1)} %refs_0_.1), channel_id=1, source_target_pairs={{0,32},{32,0},{1,33},{33,1},{2,34},{34,2},{3,35},{35,3},{4,36},{36... | collective-permute-start | bytes 884744 | tf_op jit(solution)/shard_map/ppermute | solution.py:51
  2.1 1.8 %collective-permute-start.1 = (bf16[128,1152]{1,0:T(8,128)(2,1)}, bf16[128,1152]{1,0:T(8,128)(2,1)S(1)}, u32[]{:S(2)}, u32[]{:S(2)}) collective-permute-start(bf16[128,1152]{1,0:T(8,128)(2,1)} %refs_1_.1), channel_id=1, source_target_pairs={{0,32},{32,0},{1,33},{33,1},{2,34},{34,2},{3,35},{35,3},{4,36},{36... | collective-permute-start | bytes 884744 | tf_op jit(solution)/shard_map/ppermute | solution.py:51
  4.0 1.0 copy-start
  4.9 1.0 copy-start.1
  8.1 11.4 %collective-permute-start.8 = (bf16[256,1152]{1,0:T(8,128)(2,1)S(1)}, bf16[256,1152]{1,0:T(8,128)(2,1)S(1)}, u32[]{:S(2)}, u32[]{:S(2)}) collective-permute-start(bf16[256,1152]{1,0:T(8,128)(2,1)S(1)} %get-tuple-element.18.refs_0_.mine), channel_id=1, source_target_pairs={{0,64},{32,97},{2,66},{34,99},{4,68},{36,101},{6,70},{38,103},{64,... | collective-permute-start | bytes 1769480 | tf_op jit(solution)/shard_map/ppermute | solution.py:47
  11.0 17.6 %collective-permute-start.6 = (bf16[256,1152]{1,0:T(8,128)(2,1)S(1)}, bf16[256,1152]{1,0:T(8,128)(2,1)S(1)}, u32[]{:S(2)}, u32[]{:S(2)}) collective-permute-start(bf16[256,1152]{1,0:T(8,128)(2,1)S(1)} %get-tuple-element.18.refs_0_.mine), channel_id=1, source_target_pairs={{0,8},{32,34},{2,10},{34,36},{4,12},{36,38},{6,14},{38,32},{64,72}... | collective-permute-start | bytes 1769480 | tf_op jit(solution)/shard_map/ppermute | solution.py:47
  12.6 16.0 %collective-permute-start.4 = (bf16[256,1152]{1,0:T(8,128)(2,1)S(1)}, bf16[256,1152]{1,0:T(8,128)(2,1)S(1)}, u32[]{:S(2)}, u32[]{:S(2)}) collective-permute-start(bf16[256,1152]{1,0:T(8,128)(2,1)S(1)} %get-tuple-element.18.refs_0_.mine), channel_id=1, source_target_pairs={{0,24},{32,38},{2,26},{34,32},{4,28},{36,34},{6,30},{38,36},{64,88... | collective-permute-start | bytes 1769480 | tf_op jit(solution)/shard_map/ppermute | solution.py:47
  14.8 14.4 %collective-permute-start.3 = (bf16[256,1152]{1,0:T(8,128)(2,1)S(1)}, bf16[256,1152]{1,0:T(8,128)(2,1)S(1)}, u32[]{:S(2)}, u32[]{:S(2)}) collective-permute-start(bf16[256,1152]{1,0:T(8,128)(2,1)S(1)} %get-tuple-element.18.refs_0_.mine), channel_id=1, source_target_pairs={{0,72},{32,99},{2,74},{34,101},{4,76},{36,103},{6,78},{38,97},{64,... | collective-permute-start | bytes 1769480 | tf_op jit(solution)/shard_map/ppermute | solution.py:47
  14.8 17.5 %collective-permute-start.2 = (bf16[256,1152]{1,0:T(8,128)(2,1)S(1)}, bf16[256,1152]{1,0:T(8,128)(2,1)S(1)}, u32[]{:S(2)}, u32[]{:S(2)}) collective-permute-start(bf16[256,1152]{1,0:T(8,128)(2,1)S(1)} %get-tuple-element.18.refs_0_.mine), channel_id=1, source_target_pairs={{0,88},{32,103},{2,90},{34,97},{4,92},{36,99},{6,94},{38,101},{64,... | collective-permute-start | bytes 1769480 | tf_op jit(solution)/shard_map/ppermute | solution.py:47
  19.6 15.6 %collective-permute-start.9 = (bf16[256,1152]{1,0:T(8,128)(2,1)S(1)}, bf16[256,1152]{1,0:T(8,128)(2,1)S(1)}, u32[]{:S(2)}, u32[]{:S(2)}) collective-permute-start(bf16[256,1152]{1,0:T(8,128)(2,1)S(1)} %collective-permute-done.8.refs_0_.mine), channel_id=1, source_target_pairs={{0,32},{32,0},{1,33},{33,1},{2,34},{34,2},{3,35},{35,3},{4,36},{36... | collective-permute-start | bytes 1769480 | tf_op jit(solution)/shard_map/ppermute | solution.py:51
  28.6 10.3 %collective-permute-start.7 = (bf16[256,1152]{1,0:T(8,128)(2,1)S(1)}, bf16[256,1152]{1,0:T(8,128)(2,1)S(1)}, u32[]{:S(2)}, u32[]{:S(2)}) collective-permute-start(bf16[256,1152]{1,0:T(8,128)(2,1)S(1)} %collective-permute-done.6.refs_2_.mine), channel_id=1, source_target_pairs={{0,32},{32,0},{1,33},{33,1},{2,34},{34,2},{3,35},{35,3},{4,36},{36... | collective-permute-start | bytes 1769480 | tf_op jit(solution)/shard_map/ppermute | solution.py:51
  28.7 10.3 %collective-permute-start.5 = (bf16[256,1152]{1,0:T(8,128)(2,1)S(1)}, bf16[256,1152]{1,0:T(8,128)(2,1)S(1)}, u32[]{:S(2)}, u32[]{:S(2)}) collective-permute-start(bf16[256,1152]{1,0:T(8,128)(2,1)S(1)} %collective-permute-done.4.refs_1_.mine), channel_id=1, source_target_pairs={{0,32},{32,0},{1,33},{33,1},{2,34},{34,2},{3,35},{35,3},{4,36},{36... | collective-permute-start | bytes 1769480 | tf_op jit(solution)/shard_map/ppermute | solution.py:51
  29.2 9.8 %collective-permute-start.11 = (bf16[256,1152]{1,0:T(8,128)(2,1)S(1)}, bf16[256,1152]{1,0:T(8,128)(2,1)S(1)}, u32[]{:S(2)}, u32[]{:S(2)}) collective-permute-start(bf16[256,1152]{1,0:T(8,128)(2,1)S(1)} %collective-permute-done.3.refs_1_.mine), channel_id=1, source_target_pairs={{0,32},{32,0},{1,33},{33,1},{2,34},{34,2},{3,35},{35,3},{4,36},{36... | collective-permute-start | bytes 1769480 | tf_op jit(solution)/shard_map/ppermute | solution.py:51
  32.3 6.7 %collective-permute-start.10 = (bf16[256,1152]{1,0:T(8,128)(2,1)S(1)}, bf16[256,1152]{1,0:T(8,128)(2,1)S(1)}, u32[]{:S(2)}, u32[]{:S(2)}) collective-permute-start(bf16[256,1152]{1,0:T(8,128)(2,1)S(1)} %collective-permute-done.2.refs_0_.mine), channel_id=1, source_target_pairs={{0,32},{32,0},{1,33},{33,1},{2,34},{34,2},{3,35},{35,3},{4,36},{36... | collective-permute-start | bytes 1769480 | tf_op jit(solution)/shard_map/ppermute | solution.py:51
  35.1 15.1 %collective-permute-start.12 = (bf16[256,1152]{1,0:T(8,128)(2,1)S(1)}, bf16[256,1152]{1,0:T(8,128)(2,1)S(1)}, u32[]{:S(2)}, u32[]{:S(2)}) collective-permute-start(bf16[256,1152]{1,0:T(8,128)(2,1)S(1)} %collective-permute-done.4.refs_1_.mine), channel_id=1, source_target_pairs={{0,24},{32,38},{2,26},{34,32},{4,28},{36,34},{6,30},{38,36},{64,88... | collective-permute-start | bytes 1769480 | tf_op jit(solution)/shard_map/ppermute | solution.py:47
  39.0 11.3 %collective-permute-start.13 = (bf16[256,1152]{1,0:T(8,128)(2,1)S(1)}, bf16[256,1152]{1,0:T(8,128)(2,1)S(1)}, u32[]{:S(2)}, u32[]{:S(2)}) collective-permute-start(bf16[256,1152]{1,0:T(8,128)(2,1)S(1)} %collective-permute-done.3.refs_1_.mine), channel_id=1, source_target_pairs={{0,8},{32,34},{2,10},{34,36},{4,12},{36,38},{6,14},{38,32},{64,72}... | collective-permute-start | bytes 1769480 | tf_op jit(solution)/shard_map/ppermute | solution.py:47
  55.2 2.1 %collective-permute-start.14 = (bf16[256,1152]{1,0:T(8,128)(2,1)S(1)}, bf16[256,1152]{1,0:T(8,128)(2,1)S(1)}, u32[]{:S(2)}, u32[]{:S(2)}) collective-permute-start(bf16[256,1152]{1,0:T(8,128)(2,1)S(1)} %get-tuple-element.24.mine), channel_id=1, source_target_pairs={{0,32},{32,0},{1,33},{33,1},{2,34},{34,2},{3,35},{35,3},{4,36},{36... | collective-permute-start | bytes 1769480 | tf_op jit(solution)/shard_map/ppermute | solution.py:51
  55.3 2.8 %collective-permute-start.15 = (bf16[256,1152]{1,0:T(8,128)(2,1)S(1)}, bf16[256,1152]{1,0:T(8,128)(2,1)S(1)}, u32[]{:S(2)}, u32[]{:S(2)}) collective-permute-start(bf16[256,1152]{1,0:T(8,128)(2,1)S(1)} %get-tuple-element.25.mine), channel_id=1, source_target_pairs={{0,32},{32,0},{1,33},{33,1},{2,34},{34,2},{3,35},{35,3},{4,36},{36... | collective-permute-start | bytes 1769480 | tf_op jit(solution)/shard_map/ppermute | solution.py:51
  61.6 16.5 %collective-permute-start.19 = (bf16[256,1152]{1,0:T(8,128)(2,1)S(1)}, bf16[256,1152]{1,0:T(8,128)(2,1)S(1)}, u32[]{:S(2)}, u32[]{:S(2)}) collective-permute-start(bf16[256,1152]{1,0:T(8,128)(2,1)S(1)} %shard_map.77), channel_id=1, source_target_pairs={{0,24},{32,38},{2,26},{34,32},{4,28},{36,34},{6,30},{38,36},{64,88... | collective-permute-start | bytes 1769480 | tf_op jit(solution)/shard_map/ppermute | solution.py:47
  67.8 16.6 %collective-permute-start.21 = (bf16[256,1152]{1,0:T(8,128)(2,1)S(1)}, bf16[256,1152]{1,0:T(8,128)(2,1)S(1)}, u32[]{:S(2)}, u32[]{:S(2)}) collective-permute-start(bf16[256,1152]{1,0:T(8,128)(2,1)S(1)} %shard_map.79), channel_id=1, source_target_pairs={{0,8},{32,34},{2,10},{34,36},{4,12},{36,38},{6,14},{38,32},{64,72}... | collective-permute-start | bytes 1769480 | tf_op jit(solution)/shard_map/ppermute | solution.py:47
  69.5 15.0 %collective-permute-start.17 = (bf16[256,1152]{1,0:T(8,128)(2,1)S(1)}, bf16[256,1152]{1,0:T(8,128)(2,1)S(1)}, u32[]{:S(2)}, u32[]{:S(2)}) collective-permute-start(bf16[256,1152]{1,0:T(8,128)(2,1)S(1)} %shard_map.75), channel_id=1, source_target_pairs={{0,72},{32,99},{2,74},{34,101},{4,76},{36,103},{6,78},{38,97},{64,... | collective-permute-start | bytes 1769480 | tf_op jit(solution)/shard_map/ppermute | solution.py:47
  72.3 14.4 %collective-permute-start.16 = (bf16[256,1152]{1,0:T(8,128)(2,1)S(1)}, bf16[256,1152]{1,0:T(8,128)(2,1)S(1)}, u32[]{:S(2)}, u32[]{:S(2)}) collective-permute-start(bf16[256,1152]{1,0:T(8,128)(2,1)S(1)} %shard_map.73), channel_id=1, source_target_pairs={{0,64},{32,97},{2,66},{34,99},{4,68},{36,101},{6,70},{38,103},{64,... | collective-permute-start | bytes 1769480 | tf_op jit(solution)/shard_map/ppermute | solution.py:47
  75.4 12.9 %collective-permute-start.18 = (bf16[256,1152]{1,0:T(8,128)(2,1)S(1)}, bf16[256,1152]{1,0:T(8,128)(2,1)S(1)}, u32[]{:S(2)}, u32[]{:S(2)}) collective-permute-start(bf16[256,1152]{1,0:T(8,128)(2,1)S(1)} %shard_map.76), channel_id=1, source_target_pairs={{0,24},{32,38},{2,26},{34,32},{4,28},{36,34},{6,30},{38,36},{64,88... | collective-permute-start | bytes 1769480 | tf_op jit(solution)/shard_map/ppermute | solution.py:47
  79.7 12.8 %collective-permute-start.20 = (bf16[256,1152]{1,0:T(8,128)(2,1)S(1)}, bf16[256,1152]{1,0:T(8,128)(2,1)S(1)}, u32[]{:S(2)}, u32[]{:S(2)}) collective-permute-start(bf16[256,1152]{1,0:T(8,128)(2,1)S(1)} %shard_map.78), channel_id=1, source_target_pairs={{0,88},{32,103},{2,90},{34,97},{4,92},{36,99},{6,94},{38,101},{64,... | collective-permute-start | bytes 1769480 | tf_op jit(solution)/shard_map/ppermute | solution.py:47
  86.0 10.3 %collective-permute-start.22 = (bf16[256,1152]{1,0:T(8,128)(2,1)S(1)}, bf16[256,1152]{1,0:T(8,128)(2,1)S(1)}, u32[]{:S(2)}, u32[]{:S(2)}) collective-permute-start(bf16[256,1152]{1,0:T(8,128)(2,1)S(1)} %shard_map.80), channel_id=1, source_target_pairs={{0,8},{32,34},{2,10},{34,36},{4,12},{36,38},{6,14},{38,32},{64,72}... | collective-permute-start | bytes 1769480 | tf_op jit(solution)/shard_map/ppermute | solution.py:47
  97.3 4.1 %collective-permute-start.23 = (f32[128,1152]{1,0:T(8,128)S(1)}, f32[128,1152]{1,0:T(8,128)S(1)}, u32[]{:S(2)}, u32[]{:S(2)}) collective-permute-start(f32[128,1152]{1,0:T(8,128)S(1)} %get-tuple-element.31), channel_id=1, source_target_pairs={{0,32},{32,0},{1,33},{33,1},{2,34},{34,2},{3,35},{35,3},{4,36},{36... | collective-permute-start | bytes 1769480 | tf_op jit(solution)/shard_map/ppermute | solution.py:51

commit v6 on v4

v6 whole, which is shorter than its diff:
```python
import functools
import math

import jax
import jax.numpy as jnp
import numpy as np
from jax import lax
from jax.experimental import pallas as pl
from jax.experimental.pallas import tpu as pltpu
from jax.sharding import Mesh
from jax.sharding import PartitionSpec as P

FINE_AXES = ("y_lo", "core", "x", "z", "y_hi")
FINE_SIZES = (2, 2, 4, 4, 2)
RING = 4
VMEM_BYTES = 16 * 1024 * 1024
HALF = jnp.bfloat16
FULL = jnp.float32

VMEM = pl.BlockSpec(memory_space=pltpu.VMEM)
SMEM = pl.BlockSpec(memory_space=pltpu.SMEM)
ANY = pl.BlockSpec(memory_space=pl.ANY)
PARAMS = pltpu.CompilerParams(vmem_limit_bytes=VMEM_BYTES)

ONE = ("x", "y", "z")
TWO = ("xyz", "xy", "yz", "zx")


def place(core, x, y, z):
    return int(np.ravel_multi_index((y % 2, core, x, z, y // 2), FINE_SIZES))


def mate(core, k):
    if core == 0:
        return k ^ 1
    return (k + 1) % RING if k % 2 else (k - 1) % RING


def sent(value, way):
    pairs = []
    for at in np.ndindex(RING, RING, RING):
        for core in range(2):
            to = [mate(core, k) if axis in way else k for axis, k in zip("xyz", at, strict=True)]
            pairs.append((place(core, *at), place(core, *to)))
    return lax.ppermute(value, FINE_AXES, pairs)


def other_core(value):
    return lax.ppermute(value, "core", [(0, 1), (1, 0)])


def dot(a, b, contract):
    return lax.dot_general(a, b, ((contract[:1], contract[1:]), ((), ())), preferred_element_type=FULL)


def unit_rows(raw):
    values = raw.astype(FULL)
    scale = lax.rsqrt(jnp.mean(values * values, axis=1, keepdims=True) + 1e-06) / math.sqrt(
        values.shape[1]
    )
    return values * scale, scale


def local(body, outs, scalars, arrays, after=()):
    n_scalars, n_arrays = len(scalars), len(arrays)

    def kernel(*refs):
        given = refs[: n_scalars + n_arrays]
        results = refs[n_scalars + n_arrays + len(after) :]
        for ref, value in zip(results, body(given[:n_scalars], given[n_scalars:]), strict=True):
            ref[...] = value.astype(ref.dtype)

    return pl.pallas_call(
        kernel,
        out_shape=[jax.ShapeDtypeStruct(s, d) for s, d in outs],
        in_specs=[SMEM] * n_scalars + [VMEM] * n_arrays + [ANY] * len(after),
        out_specs=[VMEM] * len(outs),
        compiler_params=PARAMS,
    )(*scalars, *arrays, *after)


def accumulate(affine, mine, theirs, coupling, start, diagonal):
    unit = mine.shape[0]
    pieces = [(ref, k) for ref in theirs for k in range(0, ref.shape[0], unit)]
    for n, (ref, k) in enumerate(pieces):
        energies = dot(mine, ref[pl.ds(k, unit), :], (1, 1))
        tile = 0.5 * jnp.tanh(affine[0] * energies + affine[1]) + 0.5
        if diagonal and n == 0:
            row = lax.broadcasted_iota(jnp.int32, tile.shape, 0)
            column = lax.broadcasted_iota(jnp.int32, tile.shape, 1)
            tile = tile - jnp.where(row == column, 1.0, 0.0)
        coupling[:, pl.ds(n * unit, unit)] = tile.astype(HALF)
    total, first = start, 0
    for ref in theirs:
        count = ref.shape[0]
        term = dot(coupling[:, pl.ds(first, count)], ref[...], (1, 0))
        total = term if total is None else total + term
        first += count
    return total


def sums_kernel(count, n_theirs, n_after, diagonal, affine, *refs):
    mine, theirs = refs[:count], refs[count : count + n_theirs]
    sums, coupling = refs[count + n_theirs + n_after : -1], refs[-1]
    for k in range(count):
        total = accumulate(affine, mine[k][...], theirs, coupling, None, diagonal and k == 0)
        sums[k][...] = total


def sums_of(affine, mine, theirs, after=(), diagonal=False):
    count, n_theirs, n_after = len(mine), len(theirs), len(after)
    unit, width = mine[0].shape
    against = sum(array.shape[0] for array in theirs)
    return pl.pallas_call(
        functools.partial(sums_kernel, count, n_theirs, n_after, diagonal),
        out_shape=[jax.ShapeDtypeStruct((unit, width), FULL)] * count,
        in_specs=[SMEM] + [VMEM] * (count + n_theirs) + [ANY] * n_after,
        out_specs=[VMEM] * count,
        scratch_shapes=[pltpu.VMEM((unit, against), HALF)],
        cost_estimate=pl.CostEstimate(
            flops=4 * count * unit * against * width,
            bytes_accessed=8 * count * unit * width,
            transcendentals=count * unit * against,
        ),
        compiler_params=PARAMS,
    )(affine, *mine, *theirs, *after)


def part_kernel(n_added, affine, mine, theirs, *refs):
    start = refs[0][...]
    for ref in refs[1:n_added]:
        start = start + ref[...].astype(FULL)
    part, coupling = refs[-2:]
    part[...] = accumulate(affine, mine[...], [theirs], coupling, start, False).astype(HALF)


def part_of(affine, mine, theirs, added):
    unit, width = mine.shape
    against = theirs.shape[0]
    return pl.pallas_call(
        functools.partial(part_kernel, len(added)),
        out_shape=jax.ShapeDtypeStruct((unit, width), HALF),
        in_specs=[SMEM] + [VMEM] * (2 + len(added)),
        out_specs=VMEM,
        scratch_shapes=[pltpu.VMEM((unit, against), HALF)],
        cost_estimate=pl.CostEstimate(
            flops=4 * unit * against * width,
            bytes_accessed=2 * unit * width,
            transcendentals=unit * against,
        ),
        compiler_params=PARAMS,
    )(affine, mine, theirs, *added)


def finish_kernel(core, multiplier, raw, *refs):
    parts, (here, there, grads) = refs[:-3], refs[-3:]
    rows = here.shape[0]
    total = parts[0][...].astype(FULL)
    for part in parts[1:]:
        total = total + part[...].astype(FULL)
    unit, scale = unit_rows(raw[...])
    grad = multiplier[0] * total
    grads[...] = scale * (grad - unit * jnp.sum(unit * grad, axis=1, keepdims=True))
    here[...] = grads[pl.ds(core[0] * rows, rows), :]
    there[...] = grads[pl.ds((1 - core[0]) * rows, rows), :]


def on_device(
    picture_vectors_raw, caption_vectors_raw, logit_multiplier, offset_term, incoming_adjoint
):
    rows, width = picture_vectors_raw.shape
    pairs = rows * math.prod(FINE_SIZES)
    core = lax.axis_index("core").astype(jnp.int32)
    is_first = core == 0
    first_flag = is_first.astype(FULL).reshape(1)
    affine = jnp.concatenate([0.5 * logit_multiplier, 0.5 * offset_term])
    multiplier = incoming_adjoint * logit_multiplier / pairs
    shard, unit = ((rows, width), HALF), ((2 * rows, width), HALF)
    shard_full = jax.ShapeDtypeStruct((rows, width), FULL)

    image_there = other_core(picture_vectors_raw)
    text_there = other_core(caption_vectors_raw)
    image, text, raw_here = local(
        lambda scalars, refs: [
            unit_rows(refs[0][...])[0],
            unit_rows(refs[1][...])[0],
            jnp.where(scalars[0][0] > 0, refs[0][...].astype(FULL), refs[1][...].astype(FULL)),
        ],
        [shard] * 3,
        [first_flag],
        [picture_vectors_raw, caption_vectors_raw],
    )

    def own_units(scalars, refs):
        first = scalars[0][0] > 0
        image_there, text_there, image, text, raw_here = [ref[...].astype(FULL) for ref in refs]
        raw_there = jnp.where(first, image_there, text_there)
        images, texts = (image, unit_rows(image_there)[0]), (text, unit_rows(text_there)[0])
        results = [[], [], []]
        for k in range(2):
            of_image = jnp.where(first, images[k], images[1 - k])
            of_text = jnp.where(first, texts[k], texts[1 - k])
            results[0].append(jnp.where(first, of_image, of_text))
            results[1].append(jnp.where(first, of_text, of_image))
            raws = (raw_here, raw_there)
            results[2].append(jnp.where(first, raws[k], raws[1 - k]))
        return [jnp.concatenate(halves, 0) for halves in results]

    own, own_theirs, raw = local(
        own_units, [unit] * 3, [first_flag], [image_there, text_there, image, text, raw_here]
    )

    def stacked(ways, after=()):
        (stack,) = local(
            lambda _, refs: [jnp.concatenate([ref[...] for ref in refs], 0)],
            [((2 * rows * len(ways), width), HALF)],
            [],
            [mine[way] for way in ways],
            after,
        )
        return other_core(stack)

    mine = {"": own}
    for way in ONE:
        mine[way] = sent(own, way)
    mine["xyz"] = sent(mine["x"], "yz")
    mine["xy"] = sent(mine["x"], "y")
    mine["yz"] = sent(mine["y"], "z")
    mine["zx"] = sent(mine["z"], "x")
    theirs_one = [own_theirs, stacked(ONE)]
    sums = sums_of(affine, [mine[way] for way in ("", *ONE)], theirs_one, diagonal=True)
    theirs_two = stacked(TWO, sums[:1])
    sums += sums_of(affine, [mine[way] for way in TWO], theirs_one)
    sums = dict(zip(("", *ONE, *TWO), sums, strict=True))

    def part(way, *added):
        return part_of(affine, mine[way], theirs_two, [sums[way], *added])

    for_x = [sent(part("xyz"), "yz"), sent(part("xy"), "y")]
    for_y = sent(part("yz"), "z")
    for_z = sent(part("zx"), "x")
    arrived = [
        sent(part("x", *for_x), "x"),
        sent(part("y", for_y), "y"),
        sent(part("z", for_z), "z"),
    ]
    own_part = part("")

    here, there = pl.pallas_call(
        finish_kernel,
        out_shape=[shard_full, shard_full],
        in_specs=[SMEM, SMEM] + [VMEM] * (2 + len(arrived)),
        out_specs=[VMEM] * 2,
        scratch_shapes=[pltpu.VMEM((2 * rows, width), FULL)],
        compiler_params=PARAMS,
    )(core.reshape(1), multiplier, raw, own_part, *arrived)
    back = other_core(there)
    return (jnp.where(is_first, here, back), jnp.where(is_first, back, here))


def solution(mesh):
    fine = Mesh(mesh.devices.reshape(FINE_SIZES), FINE_AXES)
    rows = P(FINE_AXES, None)
    return jax.shard_map(
        on_device,
        mesh=fine,
        in_specs=(rows, rows, P(), P(), P()),
        out_specs=(rows, rows),
        check_vma=False,
    )
```

time: 105 us -> 90.5 us (0.86)
  starting transfers between devices: 54.5 us -> 24.7 us
  waiting for transfers between devices: 13.7 us -> 28.3 us
  Pallas kernels: 30.3 us -> 31.5 us
    ppermute x10 -> x5, starting transfers between devices: 23.4 us -> 2.03 us  [other_core(): return lax.ppermute(value, 'core', [(0, 1), (1, 0)])]
    ppermute x14, waiting for transfers between devices: 8.53 us -> 26.3 us  [sent(): return lax.ppermute(value, FINE_AXES, pairs)]
    ppermute x14, starting transfers between devices: 31.1 us -> 22.7 us  [sent(): return lax.ppermute(value, FINE_AXES, pairs)]
    ppermute x10 -> x5, waiting for transfers between devices: 5.16 us -> 2 us  [other_core(): return lax.ppermute(value, 'core', [(0, 1), (1, 0)])]
    pallas_call x10 -> x14, Pallas kernels: 29.2 us -> 30.6 us  [the longest x8 16.9 us: part_of(): pl.pallas_call(functools.partial(part_kernel, len(added)), out_shape=jax....]
  transfers between devices with their start and end apart: 24 -> 19, of which waited for: 9 -> 10; matrix products, arithmetic and copies ran while one was open for 0% -> 0% of each run, Pallas kernels for 24% -> 31%
where the time goes in v6:
time: 90.5 us; the launch traced here: 90.3 us
  Pallas kernels  31.5 us (35%)
  waiting for transfers between devices  28.3 us (31%)
  starting transfers between devices  24.7 us (27%)
  between operations  2.73 us (3%)
  local copies, waits for them, and re-layouts  1.92 us (2%)
  other arithmetic  1.16 us (1%)
    ppermute x14, waiting for transfers between devices, sent(): return lax.ppermute(value, FINE_AXES, pairs)  26.3 us
    ppermute x14, starting transfers between devices, sent(): return lax.ppermute(value, FINE_AXES, pairs)  22.7 us
    pallas_call x8, Pallas kernels, part_of(): pl.pallas_call(functools.partial(part_kernel, len(added)), out_shape=jax....  16.9 us
    pallas_call x2, Pallas kernels, sums_of(): pl.pallas_call(functools.partial(sums_kernel, count, n_theirs, n_after, d...  12.7 us
    ppermute x5, starting transfers between devices, other_core(): return lax.ppermute(value, 'core', [(0, 1), (1, 0)])  2.03 us
    ppermute x5, waiting for transfers between devices, other_core(): return lax.ppermute(value, 'core', [(0, 1), (1, 0)])  2 us
    unnamed x4, local copies, waits for them, and re-layouts  1.92 us
  transfers between devices with their start and end apart: 19, of which 10 were waited for; matrix products, arithmetic and copies ran while one was open for 0% of the time, Pallas kernels for 31%

profile of v6, /device:TPU:1, one launch (start us, length us, event | category | flops | bytes accessed | tf_op | source)
XLA Modules:
  0.0 90.3 jit_solution(5861580179743264793)
XLA Ops:
  0.6 1.5 %collective-permute-start = (bf16[128,1152]{1,0:T(8,128)(2,1)}, bf16[128,1152]{1,0:T(8,128)(2,1)S(1)}, u32[]{:S(2)}, u32[]{:S(2)}) collective-permute-start(bf16[128,1152]{1,0:T(8,128)(2,1)} %refs_1_.1), channel_id=1, source_target_pairs={{0,32},{32,0},{1,33},{33,1},{2,34},{34,2},{3,35},{35,3},{4,36},{36... | collective-permute-start | bytes 884744 | tf_op jit(solution)/shard_map/ppermute | solution.py:49
  2.1 0.1 collective-permute-start.1
  2.2 1.0 %copy-done = bf16[128,1152]{1,0:T(8,128)(2,1)S(1)} copy-done((bf16[128,1152]{1,0:T(8,128)(2,1)S(1)}, bf16[128,1152]{1,0:T(8,128)(2,1)}, u32[]{:S(2)}) %copy-start) | copy-done | bytes 294936
  3.2 1.0 %copy-done.1 = bf16[128,1152]{1,0:T(8,128)(2,1)S(1)} copy-done((bf16[128,1152]{1,0:T(8,128)(2,1)S(1)}, bf16[128,1152]{1,0:T(8,128)(2,1)}, u32[]{:S(2)}) %copy-start.1) | copy-done | bytes 294936
  4.1 0.2 shard_map.68
  4.4 0.5 shard_map.69
  4.9 2.6 %collective-permute-start.2 = (bf16[256,1152]{1,0:T(8,128)(2,1)S(1)}, bf16[256,1152]{1,0:T(8,128)(2,1)S(1)}, u32[]{:S(2)}, u32[]{:S(2)}) collective-permute-start(bf16[256,1152]{1,0:T(8,128)(2,1)S(1)} %get-tuple-element.22.refs_0_.mine), channel_id=1, source_target_pairs={{0,8},{32,56},{2,10},{34,58},{4,12},{36,60},{6,14},{38,62},{64,72}... | collective-permute-start | bytes 1769480 | tf_op jit(solution)/shard_map/ppermute | solution.py:45
  7.5 2.7 %collective-permute-start.5 = (bf16[256,1152]{1,0:T(8,128)(2,1)S(1)}, bf16[256,1152]{1,0:T(8,128)(2,1)S(1)}, u32[]{:S(2)}, u32[]{:S(2)}) collective-permute-start(bf16[256,1152]{1,0:T(8,128)(2,1)S(1)} %get-tuple-element.22.refs_0_.mine), channel_id=1, source_target_pairs={{0,64},{32,97},{2,66},{34,99},{4,68},{36,101},{6,70},{38,103},{64,... | collective-permute-start | bytes 1769480 | tf_op jit(solution)/shard_map/ppermute | solution.py:45
  10.3 3.8 %collective-permute-start.7 = (bf16[256,1152]{1,0:T(8,128)(2,1)S(1)}, bf16[256,1152]{1,0:T(8,128)(2,1)S(1)}, u32[]{:S(2)}, u32[]{:S(2)}) collective-permute-start(bf16[256,1152]{1,0:T(8,128)(2,1)S(1)} %get-tuple-element.22.refs_0_.mine), channel_id=1, source_target_pairs={{0,2},{32,38},{2,0},{34,36},{4,6},{36,34},{6,4},{38,32},{64,66},{9... | collective-permute-start | bytes 1769480 | tf_op jit(solution)/shard_map/ppermute | solution.py:45
  14.0 0.9 collective-permute-done.2.refs_0_.refs_1_.mine
  14.9 2.6 %collective-permute-done.5.refs_1_.refs_2_.mine = bf16[256,1152]{1,0:T(8,128)(2,1)S(1)} collective-permute-done((bf16[256,1152]{1,0:T(8,128)(2,1)S(1)}, bf16[256,1152]{1,0:T(8,128)(2,1)S(1)}, u32[]{:S(2)}, u32[]{:S(2)}) %collective-permute-start.5) | collective-permute-done | bytes 589856 | tf_op jit(solution)/shard_map/ppermute | solution.py:45
  17.6 3.8 %collective-permute-done.7.refs_2_.refs_3_.mine = bf16[256,1152]{1,0:T(8,128)(2,1)S(1)} collective-permute-done((bf16[256,1152]{1,0:T(8,128)(2,1)S(1)}, bf16[256,1152]{1,0:T(8,128)(2,1)S(1)}, u32[]{:S(2)}, u32[]{:S(2)}) %collective-permute-start.7) | collective-permute-done | bytes 589856 | tf_op jit(solution)/shard_map/ppermute | solution.py:45
  21.3 0.1 shard_map.70
  21.4 0.1 collective-permute-start.9
  21.5 2.5 %collective-permute-start.3 = (bf16[256,1152]{1,0:T(8,128)(2,1)S(1)}, bf16[256,1152]{1,0:T(8,128)(2,1)S(1)}, u32[]{:S(2)}, u32[]{:S(2)}) collective-permute-start(bf16[256,1152]{1,0:T(8,128)(2,1)S(1)} %collective-permute-done.2.refs_0_.refs_1_.mine), channel_id=1, source_target_pairs={{0,66},{32,103},{2,64},{34,101},{4,70},{36,99},{6,68},{38,97},{64,... | collective-permute-start | bytes 1769480 | tf_op jit(solution)/shard_map/ppermute | solution.py:45
  24.0 2.7 %collective-permute-start.4 = (bf16[256,1152]{1,0:T(8,128)(2,1)S(1)}, bf16[256,1152]{1,0:T(8,128)(2,1)S(1)}, u32[]{:S(2)}, u32[]{:S(2)}) collective-permute-start(bf16[256,1152]{1,0:T(8,128)(2,1)S(1)} %collective-permute-done.2.refs_0_.refs_1_.mine), channel_id=1, source_target_pairs={{0,64},{32,97},{2,66},{34,99},{4,68},{36,101},{6,70},{38,103},{64,... | collective-permute-start | bytes 1769480 | tf_op jit(solution)/shard_map/ppermute | solution.py:45
  26.7 0.0 collective-permute-start.6
  26.7 0.2 collective-permute-start.8
  28.2 0.1 pad_maximum_fusion.affine
  28.3 6.4 %shard_map.71 = (f32[256,1152]{1,0:T(8,128)S(1)}, f32[256,1152]{1,0:T(8,128)S(1)}, f32[256,1152]{1,0:T(8,128)S(1)}, f32[256,1152]{1,0:T(8,128)S(1)}) custom-call(f32[2]{0:T(128)S(1)} %pad_maximum_fusion.affine, bf16[256,1152]{1,0:T(8,128)(2,1)S(1)} %get-tuple-element.22.refs_0_.mine, bf16[256,1152]{1,0:T(8,128)(2,1)S(1)} %collective-permute-done.2.refs_0_.refs_1_.mine, ...), custom_call_target="tpu_custom_call" | custom-call | flops 4831838208 | bytes 9437184 | tf_op jit(solution)/shard_map/pallas_call | solution.py:114
  34.6 5.7 %collective-permute-done.4.refs_1_.mine = bf16[256,1152]{1,0:T(8,128)(2,1)S(1)} collective-permute-done((bf16[256,1152]{1,0:T(8,128)(2,1)S(1)}, bf16[256,1152]{1,0:T(8,128)(2,1)S(1)}, u32[]{:S(2)}, u32[]{:S(2)}) %collective-permute-start.4) | collective-permute-done | bytes 589856 | tf_op jit(solution)/shard_map/ppermute | solution.py:45
  40.3 0.2 shard_map.72
  40.5 0.3 collective-permute-start.10
  40.8 6.3 %shard_map.74 = (f32[256,1152]{1,0:T(8,128)S(1)}, f32[256,1152]{1,0:T(8,128)S(1)}, f32[256,1152]{1,0:T(8,128)S(1)}, f32[256,1152]{1,0:T(8,128)S(1)}) custom-call(f32[2]{0:T(128)S(1)} %pad_maximum_fusion.affine, bf16[256,1152]{1,0:T(8,128)(2,1)S(1)} %collective-permute-done.3.refs_0_.mine, bf16[256,1152]{1,0:T(8,128)(2,1)S(1)} %collective-permute-done.4.refs_1_.mine, ...), custom_call_target="tpu_custom_call" | custom-call | flops 4831838208 | bytes 9437184 | tf_op jit(solution)/shard_map/pallas_call | solution.py:114
  47.1 2.1 %shard_map.75 = bf16[256,1152]{1,0:T(8,128)(2,1)S(1)} custom-call(f32[2]{0:T(128)S(1)} %pad_maximum_fusion.affine, bf16[256,1152]{1,0:T(8,128)(2,1)S(1)} %collective-permute-done.3.refs_0_.mine, bf16[1024,1152]{1,0:T(8,128)(2,1)S(1)} %collective-permute-done.10.theirs, f32[256,1152]{1,0:T(8,128)S(1)} %get-tuple-element.26.refs_0_), custom_call_target="tpu_custom_call" | custom-call | flops 1207959552 | bytes 589824 | tf_op jit(solution)/shard_map/pallas_call | solution.py:140
  49.2 2.2 %collective-permute-start.11 = (bf16[256,1152]{1,0:T(8,128)(2,1)S(1)}, bf16[256,1152]{1,0:T(8,128)(2,1)S(1)}, u32[]{:S(2)}, u32[]{:S(2)}) collective-permute-start(bf16[256,1152]{1,0:T(8,128)(2,1)S(1)} %shard_map.75), channel_id=1, source_target_pairs={{0,66},{32,103},{2,64},{34,101},{4,70},{36,99},{6,68},{38,97},{64,... | collective-permute-start | bytes 1769480 | tf_op jit(solution)/shard_map/ppermute | solution.py:45
  51.4 2.1 %shard_map.76 = bf16[256,1152]{1,0:T(8,128)(2,1)S(1)} custom-call(f32[2]{0:T(128)S(1)} %pad_maximum_fusion.affine, bf16[256,1152]{1,0:T(8,128)(2,1)S(1)} %collective-permute-done.4.refs_1_.mine, bf16[1024,1152]{1,0:T(8,128)(2,1)S(1)} %collective-permute-done.10.theirs, f32[256,1152]{1,0:T(8,128)S(1)} %get-tuple-element.27.refs_0_), custom_call_target="tpu_custom_call" | custom-call | flops 1207959552 | bytes 589824 | tf_op jit(solution)/shard_map/pallas_call | solution.py:140
  53.5 2.7 %collective-permute-start.12 = (bf16[256,1152]{1,0:T(8,128)(2,1)S(1)}, bf16[256,1152]{1,0:T(8,128)(2,1)S(1)}, u32[]{:S(2)}, u32[]{:S(2)}) collective-permute-start(bf16[256,1152]{1,0:T(8,128)(2,1)S(1)} %shard_map.76), channel_id=1, source_target_pairs={{0,64},{32,97},{2,66},{34,99},{4,68},{36,101},{6,70},{38,103},{64,... | collective-permute-start | bytes 1769480 | tf_op jit(solution)/shard_map/ppermute | solution.py:45
  56.2 2.1 %shard_map.78 = bf16[256,1152]{1,0:T(8,128)(2,1)S(1)} custom-call(f32[2]{0:T(128)S(1)} %pad_maximum_fusion.affine, bf16[256,1152]{1,0:T(8,128)(2,1)S(1)} %collective-permute-done.6.refs_2_.mine, bf16[1024,1152]{1,0:T(8,128)(2,1)S(1)} %collective-permute-done.10.theirs, f32[256,1152]{1,0:T(8,128)S(1)} %get-tuple-element.29.refs_0_), custom_call_target="tpu_custom_call" | custom-call | flops 1207959552 | bytes 589824 | tf_op jit(solution)/shard_map/pallas_call | solution.py:140
  58.4 0.4 collective-permute-start.14
  58.8 2.1 %shard_map.80 = bf16[256,1152]{1,0:T(8,128)(2,1)S(1)} custom-call(f32[2]{0:T(128)S(1)} %pad_maximum_fusion.affine, bf16[256,1152]{1,0:T(8,128)(2,1)S(1)} %collective-permute-done.8.refs_3_.mine, bf16[1024,1152]{1,0:T(8,128)(2,1)S(1)} %collective-permute-done.10.theirs, f32[256,1152]{1,0:T(8,128)S(1)} %get-tuple-element.31.refs_0_), custom_call_target="tpu_custom_call" | custom-call | flops 1207959552 | bytes 589824 | tf_op jit(solution)/shard_map/pallas_call | solution.py:140
  60.9 0.3 collective-permute-start.16
  61.2 0.2 collective-permute-done.11.refs_1_
  61.4 6.3 %collective-permute-done.12.refs_2_ = bf16[256,1152]{1,0:T(8,128)(2,1)S(1)} collective-permute-done((bf16[256,1152]{1,0:T(8,128)(2,1)S(1)}, bf16[256,1152]{1,0:T(8,128)(2,1)S(1)}, u32[]{:S(2)}, u32[]{:S(2)}) %collective-permute-start.12) | collective-permute-done | bytes 589856 | tf_op jit(solution)/shard_map/ppermute | solution.py:45
  67.6 2.1 %shard_map.77 = bf16[256,1152]{1,0:T(8,128)(2,1)S(1)} custom-call(f32[2]{0:T(128)S(1)} %pad_maximum_fusion.affine, bf16[256,1152]{1,0:T(8,128)(2,1)S(1)} %collective-permute-done.2.refs_0_.refs_1_.mine, bf16[1024,1152]{1,0:T(8,128)(2,1)S(1)} %collective-permute-done.10.theirs, f32[256,1152]{1,0:T(8,128)S(1)} %get-tuple-element.25.refs_0_, ...), custom_call_target="tpu_custom_call" | custom-call | flops 1207959552 | bytes 589824 | tf_op jit(solution)/shard_map/pallas_call | solution.py:140
  69.8 0.5 collective-permute-start.13
  70.3 2.1 %shard_map.79 = bf16[256,1152]{1,0:T(8,128)(2,1)S(1)} custom-call(f32[2]{0:T(128)S(1)} %pad_maximum_fusion.affine, bf16[256,1152]{1,0:T(8,128)(2,1)S(1)} %collective-permute-done.5.refs_1_.refs_2_.mine, bf16[1024,1152]{1,0:T(8,128)(2,1)S(1)} %collective-permute-done.10.theirs, f32[256,1152]{1,0:T(8,128)S(1)} %get-tuple-element.28.refs_0_, ...), custom_call_target="tpu_custom_call" | custom-call | flops 1207959552 | bytes 589824 | tf_op jit(solution)/shard_map/pallas_call | solution.py:140
  72.4 1.7 %collective-permute-start.15 = (bf16[256,1152]{1,0:T(8,128)(2,1)S(1)}, bf16[256,1152]{1,0:T(8,128)(2,1)S(1)}, u32[]{:S(2)}, u32[]{:S(2)}) collective-permute-start(bf16[256,1152]{1,0:T(8,128)(2,1)S(1)} %shard_map.79), channel_id=1, source_target_pairs={{0,64},{32,97},{2,66},{34,99},{4,68},{36,101},{6,70},{38,103},{64,... | collective-permute-start | bytes 1769480 | tf_op jit(solution)/shard_map/ppermute | solution.py:45
  74.1 2.1 %shard_map.81 = bf16[256,1152]{1,0:T(8,128)(2,1)S(1)} custom-call(f32[2]{0:T(128)S(1)} %pad_maximum_fusion.affine, bf16[256,1152]{1,0:T(8,128)(2,1)S(1)} %collective-permute-done.7.refs_2_.refs_3_.mine, bf16[1024,1152]{1,0:T(8,128)(2,1)S(1)} %collective-permute-done.10.theirs, f32[256,1152]{1,0:T(8,128)S(1)} %get-tuple-element.30.refs_0_, ...), custom_call_target="tpu_custom_call" | custom-call | flops 1207959552 | bytes 589824 | tf_op jit(solution)/shard_map/pallas_call | solution.py:140
  76.2 0.4 collective-permute-start.17
  77.3 2.1 %shard_map.73.refs_0_ = bf16[256,1152]{1,0:T(8,128)(2,1)S(1)} custom-call(f32[2]{0:T(128)S(1)} %pad_maximum_fusion.affine, bf16[256,1152]{1,0:T(8,128)(2,1)S(1)} %get-tuple-element.22.refs_0_.mine, bf16[1024,1152]{1,0:T(8,128)(2,1)S(1)} %collective-permute-done.10.theirs, f32[256,1152]{1,0:T(8,128)S(1)} %get-tuple-element.24.refs_4_.refs_0_), custom_call_target="tpu_custom_call" | custom-call | flops 1207959552 | bytes 589824 | tf_op jit(solution)/shard_map/pallas_call | solution.py:140
  79.4 0.6 collective-permute-done.13.refs_1_
  80.0 2.4 %collective-permute-done.15.refs_2_ = bf16[256,1152]{1,0:T(8,128)(2,1)S(1)} collective-permute-done((bf16[256,1152]{1,0:T(8,128)(2,1)S(1)}, bf16[256,1152]{1,0:T(8,128)(2,1)S(1)}, u32[]{:S(2)}, u32[]{:S(2)}) %collective-permute-start.15) | collective-permute-done | bytes 589856 | tf_op jit(solution)/shard_map/ppermute | solution.py:45
  82.4 3.8 %collective-permute-done.17.refs_3_ = bf16[256,1152]{1,0:T(8,128)(2,1)S(1)} collective-permute-done((bf16[256,1152]{1,0:T(8,128)(2,1)S(1)}, bf16[256,1152]{1,0:T(8,128)(2,1)S(1)}, u32[]{:S(2)}, u32[]{:S(2)}) %collective-permute-start.17) | collective-permute-done | bytes 589856 | tf_op jit(solution)/shard_map/ppermute | solution.py:45
  86.3 0.9 shard_map.82
  87.1 0.1 collective-permute-start.18
  87.2 2.0 %collective-permute-done.18 = f32[128,1152]{1,0:T(8,128)S(1)} collective-permute-done((f32[128,1152]{1,0:T(8,128)S(1)}, f32[128,1152]{1,0:T(8,128)S(1)}, u32[]{:S(2)}, u32[]{:S(2)}) %collective-permute-start.18) | collective-permute-done | bytes 589856 | tf_op jit(solution)/shard_map/ppermute | solution.py:49
  89.2 1.1 %broadcast_select_fusion = (f32[128,1152]{1,0:T(8,128)}, f32[128,1152]{1,0:T(8,128)}) fusion(f32[128,1152]{1,0:T(8,128)S(1)} %collective-permute-done.18, f32[128,1152]{1,0:T(8,128)S(1)} %get-tuple-element.32, pred[]{:T(512)S(6)} %eq.3), kind=kLoop, calls=%fused_computation | loop fusion | flops 294912 | bytes 2359297 | tf_op jit(solution)/shard_map/jit(_where)/select_n | solution.py:258
  (11 shorter events, 0.0 us)
Async XLA Ops:
  0.6 3.8 %collective-permute-start = (bf16[128,1152]{1,0:T(8,128)(2,1)}, bf16[128,1152]{1,0:T(8,128)(2,1)S(1)}, u32[]{:S(2)}, u32[]{:S(2)}) collective-permute-start(bf16[128,1152]{1,0:T(8,128)(2,1)} %refs_1_.1), channel_id=1, source_target_pairs={{0,32},{32,0},{1,33},{33,1},{2,34},{34,2},{3,35},{35,3},{4,36},{36... | collective-permute-start | bytes 884744 | tf_op jit(solution)/shard_map/ppermute | solution.py:49
  2.1 2.3 %collective-permute-start.1 = (bf16[128,1152]{1,0:T(8,128)(2,1)}, bf16[128,1152]{1,0:T(8,128)(2,1)S(1)}, u32[]{:S(2)}, u32[]{:S(2)}) collective-permute-start(bf16[128,1152]{1,0:T(8,128)(2,1)} %refs_2_.1), channel_id=1, source_target_pairs={{0,32},{32,0},{1,33},{33,1},{2,34},{34,2},{3,35},{35,3},{4,36},{36... | collective-permute-start | bytes 884744 | tf_op jit(solution)/shard_map/ppermute | solution.py:49
  2.2 1.0 %copy-start = (bf16[128,1152]{1,0:T(8,128)(2,1)S(1)}, bf16[128,1152]{1,0:T(8,128)(2,1)}, u32[]{:S(2)}) copy-start(bf16[128,1152]{1,0:T(8,128)(2,1)} %refs_1_.1) | copy-start | bytes 884740
  3.2 1.0 %copy-start.1 = (bf16[128,1152]{1,0:T(8,128)(2,1)S(1)}, bf16[128,1152]{1,0:T(8,128)(2,1)}, u32[]{:S(2)}) copy-start(bf16[128,1152]{1,0:T(8,128)(2,1)} %refs_2_.1) | copy-start | bytes 884740
  4.9 10.0 %collective-permute-start.2 = (bf16[256,1152]{1,0:T(8,128)(2,1)S(1)}, bf16[256,1152]{1,0:T(8,128)(2,1)S(1)}, u32[]{:S(2)}, u32[]{:S(2)}) collective-permute-start(bf16[256,1152]{1,0:T(8,128)(2,1)S(1)} %get-tuple-element.22.refs_0_.mine), channel_id=1, source_target_pairs={{0,8},{32,56},{2,10},{34,58},{4,12},{36,60},{6,14},{38,62},{64,72}... | collective-permute-start | bytes 1769480 | tf_op jit(solution)/shard_map/ppermute | solution.py:45
  7.5 10.0 %collective-permute-start.5 = (bf16[256,1152]{1,0:T(8,128)(2,1)S(1)}, bf16[256,1152]{1,0:T(8,128)(2,1)S(1)}, u32[]{:S(2)}, u32[]{:S(2)}) collective-permute-start(bf16[256,1152]{1,0:T(8,128)(2,1)S(1)} %get-tuple-element.22.refs_0_.mine), channel_id=1, source_target_pairs={{0,64},{32,97},{2,66},{34,99},{4,68},{36,101},{6,70},{38,103},{64,... | collective-permute-start | bytes 1769480 | tf_op jit(solution)/shard_map/ppermute | solution.py:45
  10.3 11.0 %collective-permute-start.7 = (bf16[256,1152]{1,0:T(8,128)(2,1)S(1)}, bf16[256,1152]{1,0:T(8,128)(2,1)S(1)}, u32[]{:S(2)}, u32[]{:S(2)}) collective-permute-start(bf16[256,1152]{1,0:T(8,128)(2,1)S(1)} %get-tuple-element.22.refs_0_.mine), channel_id=1, source_target_pairs={{0,2},{32,38},{2,0},{34,36},{4,6},{36,34},{6,4},{38,32},{64,66},{9... | collective-permute-start | bytes 1769480 | tf_op jit(solution)/shard_map/ppermute | solution.py:45
  21.4 6.8 %collective-permute-start.9 = (bf16[768,1152]{1,0:T(8,128)(2,1)S(1)}, bf16[768,1152]{1,0:T(8,128)(2,1)S(1)}, u32[]{:S(2)}, u32[]{:S(2)}) collective-permute-start(bf16[768,1152]{1,0:T(8,128)(2,1)S(1)} %shard_map.70), channel_id=1, source_target_pairs={{0,32},{32,0},{1,33},{33,1},{2,34},{34,2},{3,35},{35,3},{4,36},{36... | collective-permute-start | bytes 5308424 | tf_op jit(solution)/shard_map/ppermute | solution.py:49
  21.5 13.1 %collective-permute-start.3 = (bf16[256,1152]{1,0:T(8,128)(2,1)S(1)}, bf16[256,1152]{1,0:T(8,128)(2,1)S(1)}, u32[]{:S(2)}, u32[]{:S(2)}) collective-permute-start(bf16[256,1152]{1,0:T(8,128)(2,1)S(1)} %collective-permute-done.2.refs_0_.refs_1_.mine), channel_id=1, source_target_pairs={{0,66},{32,103},{2,64},{34,101},{4,70},{36,99},{6,68},{38,97},{64,... | collective-permute-start | bytes 1769480 | tf_op jit(solution)/shard_map/ppermute | solution.py:45
  24.0 16.3 %collective-permute-start.4 = (bf16[256,1152]{1,0:T(8,128)(2,1)S(1)}, bf16[256,1152]{1,0:T(8,128)(2,1)S(1)}, u32[]{:S(2)}, u32[]{:S(2)}) collective-permute-start(bf16[256,1152]{1,0:T(8,128)(2,1)S(1)} %collective-permute-done.2.refs_0_.refs_1_.mine), channel_id=1, source_target_pairs={{0,64},{32,97},{2,66},{34,99},{4,68},{36,101},{6,70},{38,103},{64,... | collective-permute-start | bytes 1769480 | tf_op jit(solution)/shard_map/ppermute | solution.py:45
  26.7 13.6 %collective-permute-start.6 = (bf16[256,1152]{1,0:T(8,128)(2,1)S(1)}, bf16[256,1152]{1,0:T(8,128)(2,1)S(1)}, u32[]{:S(2)}, u32[]{:S(2)}) collective-permute-start(bf16[256,1152]{1,0:T(8,128)(2,1)S(1)} %collective-permute-done.5.refs_1_.refs_2_.mine), channel_id=1, source_target_pairs={{0,2},{32,38},{2,0},{34,36},{4,6},{36,34},{6,4},{38,32},{64,66},{9... | collective-permute-start | bytes 1769480 | tf_op jit(solution)/shard_map/ppermute | solution.py:45
  26.7 13.6 %collective-permute-start.8 = (bf16[256,1152]{1,0:T(8,128)(2,1)S(1)}, bf16[256,1152]{1,0:T(8,128)(2,1)S(1)}, u32[]{:S(2)}, u32[]{:S(2)}) collective-permute-start(bf16[256,1152]{1,0:T(8,128)(2,1)S(1)} %collective-permute-done.7.refs_2_.refs_3_.mine), channel_id=1, source_target_pairs={{0,8},{32,56},{2,10},{34,58},{4,12},{36,60},{6,14},{38,62},{64,72}... | collective-permute-start | bytes 1769480 | tf_op jit(solution)/shard_map/ppermute | solution.py:45
  40.5 6.6 %collective-permute-start.10 = (bf16[1024,1152]{1,0:T(8,128)(2,1)S(1)}, bf16[1024,1152]{1,0:T(8,128)(2,1)S(1)}, u32[]{:S(2)}, u32[]{:S(2)}) collective-permute-start(bf16[1024,1152]{1,0:T(8,128)(2,1)S(1)} %shard_map.72), channel_id=1, source_target_pairs={{0,32},{32,0},{1,33},{33,1},{2,34},{34,2},{3,35},{35,3},{4,36},{36... | collective-permute-start | bytes 7077896 | tf_op jit(solution)/shard_map/ppermute | solution.py:49
  49.2 12.1 %collective-permute-start.11 = (bf16[256,1152]{1,0:T(8,128)(2,1)S(1)}, bf16[256,1152]{1,0:T(8,128)(2,1)S(1)}, u32[]{:S(2)}, u32[]{:S(2)}) collective-permute-start(bf16[256,1152]{1,0:T(8,128)(2,1)S(1)} %shard_map.75), channel_id=1, source_target_pairs={{0,66},{32,103},{2,64},{34,101},{4,70},{36,99},{6,68},{38,97},{64,... | collective-permute-start | bytes 1769480 | tf_op jit(solution)/shard_map/ppermute | solution.py:45
  53.5 14.1 %collective-permute-start.12 = (bf16[256,1152]{1,0:T(8,128)(2,1)S(1)}, bf16[256,1152]{1,0:T(8,128)(2,1)S(1)}, u32[]{:S(2)}, u32[]{:S(2)}) collective-permute-start(bf16[256,1152]{1,0:T(8,128)(2,1)S(1)} %shard_map.76), channel_id=1, source_target_pairs={{0,64},{32,97},{2,66},{34,99},{4,68},{36,101},{6,70},{38,103},{64,... | collective-permute-start | bytes 1769480 | tf_op jit(solution)/shard_map/ppermute | solution.py:45
  58.4 11.9 %collective-permute-start.14 = (bf16[256,1152]{1,0:T(8,128)(2,1)S(1)}, bf16[256,1152]{1,0:T(8,128)(2,1)S(1)}, u32[]{:S(2)}, u32[]{:S(2)}) collective-permute-start(bf16[256,1152]{1,0:T(8,128)(2,1)S(1)} %shard_map.78), channel_id=1, source_target_pairs={{0,2},{32,38},{2,0},{34,36},{4,6},{36,34},{6,4},{38,32},{64,66},{9... | collective-permute-start | bytes 1769480 | tf_op jit(solution)/shard_map/ppermute | solution.py:45
  60.9 13.3 %collective-permute-start.16 = (bf16[256,1152]{1,0:T(8,128)(2,1)S(1)}, bf16[256,1152]{1,0:T(8,128)(2,1)S(1)}, u32[]{:S(2)}, u32[]{:S(2)}) collective-permute-start(bf16[256,1152]{1,0:T(8,128)(2,1)S(1)} %shard_map.80), channel_id=1, source_target_pairs={{0,8},{32,56},{2,10},{34,58},{4,12},{36,60},{6,14},{38,62},{64,72}... | collective-permute-start | bytes 1769480 | tf_op jit(solution)/shard_map/ppermute | solution.py:45
  69.8 10.2 %collective-permute-start.13 = (bf16[256,1152]{1,0:T(8,128)(2,1)S(1)}, bf16[256,1152]{1,0:T(8,128)(2,1)S(1)}, u32[]{:S(2)}, u32[]{:S(2)}) collective-permute-start(bf16[256,1152]{1,0:T(8,128)(2,1)S(1)} %shard_map.77), channel_id=1, source_target_pairs={{0,8},{32,56},{2,10},{34,58},{4,12},{36,60},{6,14},{38,62},{64,72}... | collective-permute-start | bytes 1769480 | tf_op jit(solution)/shard_map/ppermute | solution.py:45
  72.4 10.0 %collective-permute-start.15 = (bf16[256,1152]{1,0:T(8,128)(2,1)S(1)}, bf16[256,1152]{1,0:T(8,128)(2,1)S(1)}, u32[]{:S(2)}, u32[]{:S(2)}) collective-permute-start(bf16[256,1152]{1,0:T(8,128)(2,1)S(1)} %shard_map.79), channel_id=1, source_target_pairs={{0,64},{32,97},{2,66},{34,99},{4,68},{36,101},{6,70},{38,103},{64,... | collective-permute-start | bytes 1769480 | tf_op jit(solution)/shard_map/ppermute | solution.py:45
  76.2 10.0 %collective-permute-start.17 = (bf16[256,1152]{1,0:T(8,128)(2,1)S(1)}, bf16[256,1152]{1,0:T(8,128)(2,1)S(1)}, u32[]{:S(2)}, u32[]{:S(2)}) collective-permute-start(bf16[256,1152]{1,0:T(8,128)(2,1)S(1)} %shard_map.81), channel_id=1, source_target_pairs={{0,2},{32,38},{2,0},{34,36},{4,6},{36,34},{6,4},{38,32},{64,66},{9... | collective-permute-start | bytes 1769480 | tf_op jit(solution)/shard_map/ppermute | solution.py:45
  87.1 2.1 %collective-permute-start.18 = (f32[128,1152]{1,0:T(8,128)S(1)}, f32[128,1152]{1,0:T(8,128)S(1)}, u32[]{:S(2)}, u32[]{:S(2)}) collective-permute-start(f32[128,1152]{1,0:T(8,128)S(1)} %get-tuple-element.33), channel_id=1, source_target_pairs={{0,32},{32,0},{1,33},{33,1},{2,34},{34,2},{3,35},{35,3},{4,36},{36... | collective-permute-start | bytes 1769480 | tf_op jit(solution)/shard_map/ppermute | solution.py:49

commit v7 on v6

--- a/solution.py
+++ b/solution.py
@@ -30,8 +30,8 @@
     return int(np.ravel_multi_index((y % 2, core, x, z, y // 2), FINE_SIZES))
 
 
-def mate(core, k):
-    if core == 0:
+def mate(core, axis, k):
+    if (core == 0) != (axis == "z"):
         return k ^ 1
     return (k + 1) % RING if k % 2 else (k - 1) % RING
 
@@ -40,7 +40,7 @@
     pairs = []
     for at in np.ndindex(RING, RING, RING):
         for core in range(2):
-            to = [mate(core, k) if axis in way else k for axis, k in zip("xyz", at, strict=True)]
+            to = [mate(core, axis, k) if axis in way else k for axis, k in zip("xyz", at, strict=True)]
             pairs.append((place(core, *at), place(core, *to)))
     return lax.ppermute(value, FINE_AXES, pairs)
 
@@ -99,57 +99,35 @@
     return total
 
 
-def sums_kernel(count, n_theirs, n_after, diagonal, affine, *refs):
-    mine, theirs = refs[:count], refs[count : count + n_theirs]
-    sums, coupling = refs[count + n_theirs + n_after : -1], refs[-1]
+def sums_kernel(count, n_theirs, n_starts, n_after, diagonal, affine, *refs):
+    mine, refs = refs[:count], refs[count:]
+    theirs, refs = refs[:n_theirs], refs[n_theirs:]
+    starts, refs = refs[:n_starts], refs[n_starts + n_after :]
+    sums, coupling = refs[:-1], refs[-1]
     for k in range(count):
-        total = accumulate(affine, mine[k][...], theirs, coupling, None, diagonal and k == 0)
-        sums[k][...] = total
-
-
-def sums_of(affine, mine, theirs, after=(), diagonal=False):
-    count, n_theirs, n_after = len(mine), len(theirs), len(after)
+        start = starts[k][...] if starts else None
+        total = accumulate(affine, mine[k][...], theirs, coupling, start, diagonal and k == 0)
+        sums[k][...] = total.astype(sums[k].dtype)
+
+
+def sums_of(affine, mine, theirs, starts=(), after=(), kinds=None, diagonal=False, hides=True):
+    count, n_theirs, n_starts, n_after = len(mine), len(theirs), len(starts), len(after)
     unit, width = mine[0].shape
     against = sum(array.shape[0] for array in theirs)
+    kinds = kinds or [FULL] * count
     return pl.pallas_call(
-        functools.partial(sums_kernel, count, n_theirs, n_after, diagonal),
-        out_shape=[jax.ShapeDtypeStruct((unit, width), FULL)] * count,
-        in_specs=[SMEM] + [VMEM] * (count + n_theirs) + [ANY] * n_after,
+        functools.partial(sums_kernel, count, n_theirs, n_starts, n_after, diagonal),
+        out_shape=[jax.ShapeDtypeStruct((unit, width), kind) for kind in kinds],
+        in_specs=[SMEM] + [VMEM] * (count + n_theirs + n_starts) + [ANY] * n_after,
         out_specs=[VMEM] * count,
         scratch_shapes=[pltpu.VMEM((unit, against), HALF)],
         cost_estimate=pl.CostEstimate(
-            flops=4 * count * unit * against * width,
-            bytes_accessed=8 * count * unit * width,
-            transcendentals=count * unit * against,
+            flops=4 * count * unit * against * width if hides else 0,
+            bytes_accessed=8 * count * unit * width if hides else 0,
+            transcendentals=count * unit * against if hides else 0,
         ),
         compiler_params=PARAMS,
-    )(affine, *mine, *theirs, *after)
-
-
-def part_kernel(n_added, affine, mine, theirs, *refs):
-    start = refs[0][...]
-    for ref in refs[1:n_added]:
-        start = start + ref[...].astype(FULL)
-    part, coupling = refs[-2:]
-    part[...] = accumulate(affine, mine[...], [theirs], coupling, start, False).astype(HALF)
-
-
-def part_of(affine, mine, theirs, added):
-    unit, width = mine.shape
-    against = theirs.shape[0]
-    return pl.pallas_call(
-        functools.partial(part_kernel, len(added)),
-        out_shape=jax.ShapeDtypeStruct((unit, width), HALF),
-        in_specs=[SMEM] + [VMEM] * (2 + len(added)),
-        out_specs=VMEM,
-        scratch_shapes=[pltpu.VMEM((unit, against), HALF)],
-        cost_estimate=pl.CostEstimate(
-            flops=4 * unit * against * width,
-            bytes_accessed=2 * unit * width,
-            transcendentals=unit * against,
-        ),
-        compiler_params=PARAMS,
-    )(affine, mine, theirs, *added)
+    )(affine, *mine, *theirs, *starts, *after)
 
 
 def finish_kernel(core, multiplier, raw, *refs):
@@ -227,24 +205,40 @@
     mine["xy"] = sent(mine["x"], "y")
     mine["yz"] = sent(mine["y"], "z")
     mine["zx"] = sent(mine["z"], "x")
+    def pick(units, ways):
+        return [units[way] for way in ways]
+
     theirs_one = [own_theirs, stacked(ONE)]
-    sums = sums_of(affine, [mine[way] for way in ("", *ONE)], theirs_one, diagonal=True)
-    theirs_two = stacked(TWO, sums[:1])
-    sums += sums_of(affine, [mine[way] for way in TWO], theirs_one)
-    sums = dict(zip(("", *ONE, *TWO), sums, strict=True))
-
-    def part(way, *added):
-        return part_of(affine, mine[way], theirs_two, [sums[way], *added])
-
-    for_x = [sent(part("xyz"), "yz"), sent(part("xy"), "y")]
-    for_y = sent(part("yz"), "z")
-    for_z = sent(part("zx"), "x")
+    near = ("", *ONE)
+    sums = sums_of(affine, pick(mine, near), theirs_one, diagonal=True, hides=False)
+    theirs_two = [stacked(TWO, sums[:1])]
+    sums += sums_of(affine, pick(mine, TWO), theirs_one)
+    sums = dict(zip((*near, *TWO), sums, strict=True))
+
+    def parts_of(ways, kinds, after=()):
+        return sums_of(affine, pick(mine, ways), theirs_two, pick(sums, ways), after, kinds)
+
+    part_xyz, part_xy = parts_of(("xyz", "xy"), [HALF, HALF])
+    for_x = [sent(part_xyz, "yz"), sent(part_xy, "y")]
+    part_yz, part_zx = parts_of(("yz", "zx"), [HALF, HALF], [part_xy])
+    for_y = [sent(part_yz, "z")]
+    for_z = [sent(part_zx, "x")]
+    own_part, part_x, part_y, part_z = parts_of(near, [FULL] * 4, [part_zx])
+
+    def with_added(part, added, way):
+        (total,) = local(
+            lambda _, refs: [sum([ref[...].astype(FULL) for ref in refs[1:]], refs[0][...])],
+            [unit],
+            [],
+            [part, *added],
+        )
+        return sent(total, way)
+
     arrived = [
-        sent(part("x", *for_x), "x"),
-        sent(part("y", for_y), "y"),
-        sent(part("z", for_z), "z"),
+        with_added(part_x, for_x, "x"),
+        with_added(part_y, for_y, "y"),
+        with_added(part_z, for_z, "z"),
     ]
-    own_part = part("")
 
     here, there = pl.pallas_call(
         finish_kernel,

time: 90.5 us -> 84.9 us (0.938)
  waiting for transfers between devices: 28.3 us -> 20.4 us
  starting transfers between devices: 24.7 us -> 30.3 us
  Pallas kernels: 31.5 us -> 28.1 us
    ppermute x14, waiting for transfers between devices: 26.3 us -> 18.8 us  [sent(): return lax.ppermute(value, FINE_AXES, pairs)]
    ppermute x5, starting transfers between devices: 2.03 us -> 6.2 us  [other_core(): return lax.ppermute(value, 'core', [(0, 1), (1, 0)])]
    pallas_call x10 -> x5, Pallas kernels: 29.6 us -> 25.9 us  [sums_of(): pl.pallas_call(functools.partial(sums_kernel, count, n_theirs, n_starts,...]
    ppermute x14, starting transfers between devices: 22.7 us -> 24.1 us  [sent(): return lax.ppermute(value, FINE_AXES, pairs)]
  transfers between devices with their start and end apart: 19 -> 19, of which waited for: 10 -> 10; matrix products, arithmetic and copies ran while one was open for 0% -> 0% of each run, Pallas kernels for 31% -> 27%
where the time goes in v7:
time: 84.9 us; the launch traced here: 84.7 us
  starting transfers between devices  30.3 us (36%)
  Pallas kernels  28.1 us (33%)
  waiting for transfers between devices  20.4 us (24%)
  between operations  2.7 us (3%)
  local copies, waits for them, and re-layouts  1.92 us (2%)
  other arithmetic  1.16 us (1%)
    pallas_call x5, Pallas kernels, sums_of(): pl.pallas_call(functools.partial(sums_kernel, count, n_theirs, n_starts,...  25.9 us
    ppermute x14, starting transfers between devices, sent(): return lax.ppermute(value, FINE_AXES, pairs)  24.1 us
    ppermute x14, waiting for transfers between devices, sent(): return lax.ppermute(value, FINE_AXES, pairs)  18.8 us
    ppermute x5, starting transfers between devices, other_core(): return lax.ppermute(value, 'core', [(0, 1), (1, 0)])  6.2 us
    unnamed x4, local copies, waits for them, and re-layouts  1.92 us
  transfers between devices with their start and end apart: 19, of which 10 were waited for; matrix products, arithmetic and copies ran while one was open for 0% of the time, Pallas kernels for 27%

profile of v7, /device:TPU:1, one launch (start us, length us, event | category | flops | bytes accessed | tf_op | source)
XLA Modules:
  0.0 84.7 jit_solution(450877266553142314)
XLA Ops:
  0.6 1.5 %collective-permute-start = (bf16[128,1152]{1,0:T(8,128)(2,1)}, bf16[128,1152]{1,0:T(8,128)(2,1)S(1)}, u32[]{:S(2)}, u32[]{:S(2)}) collective-permute-start(bf16[128,1152]{1,0:T(8,128)(2,1)} %refs_1_.1), channel_id=1, source_target_pairs={{0,32},{32,0},{1,33},{33,1},{2,34},{34,2},{3,35},{35,3},{4,36},{36... | collective-permute-start | bytes 884744 | tf_op jit(solution)/shard_map/ppermute | solution.py:49
  2.1 0.1 collective-permute-start.1
  2.2 1.0 %copy-done = bf16[128,1152]{1,0:T(8,128)(2,1)S(1)} copy-done((bf16[128,1152]{1,0:T(8,128)(2,1)S(1)}, bf16[128,1152]{1,0:T(8,128)(2,1)}, u32[]{:S(2)}) %copy-start) | copy-done | bytes 294936
  3.2 1.0 %copy-done.1 = bf16[128,1152]{1,0:T(8,128)(2,1)S(1)} copy-done((bf16[128,1152]{1,0:T(8,128)(2,1)S(1)}, bf16[128,1152]{1,0:T(8,128)(2,1)}, u32[]{:S(2)}) %copy-start.1) | copy-done | bytes 294936
  4.1 0.2 shard_map.68
  4.4 0.0 collective-permute-done.refs_1_
  4.4 0.0 collective-permute-done.1.refs_2_
  4.4 0.5 shard_map.69
  4.9 2.6 %collective-permute-start.2 = (bf16[256,1152]{1,0:T(8,128)(2,1)S(1)}, bf16[256,1152]{1,0:T(8,128)(2,1)S(1)}, u32[]{:S(2)}, u32[]{:S(2)}) collective-permute-start(bf16[256,1152]{1,0:T(8,128)(2,1)S(1)} %get-tuple-element.30.refs_0_), channel_id=1, source_target_pairs={{0,8},{32,56},{2,10},{34,58},{4,12},{36,60},{6,14},{38,62},{64,72}... | collective-permute-start | bytes 1769480 | tf_op jit(solution)/shard_map/ppermute | solution.py:45
  7.5 2.7 %collective-permute-start.3 = (bf16[256,1152]{1,0:T(8,128)(2,1)S(1)}, bf16[256,1152]{1,0:T(8,128)(2,1)S(1)}, u32[]{:S(2)}, u32[]{:S(2)}) collective-permute-start(bf16[256,1152]{1,0:T(8,128)(2,1)S(1)} %get-tuple-element.30.refs_0_), channel_id=1, source_target_pairs={{0,64},{32,97},{2,66},{34,99},{4,68},{36,101},{6,70},{38,103},{64,... | collective-permute-start | bytes 1769480 | tf_op jit(solution)/shard_map/ppermute | solution.py:45
  10.3 1.6 %collective-permute-start.4 = (bf16[256,1152]{1,0:T(8,128)(2,1)S(1)}, bf16[256,1152]{1,0:T(8,128)(2,1)S(1)}, u32[]{:S(2)}, u32[]{:S(2)}) collective-permute-start(bf16[256,1152]{1,0:T(8,128)(2,1)S(1)} %get-tuple-element.30.refs_0_), channel_id=1, source_target_pairs={{0,6},{32,34},{2,4},{34,32},{4,2},{36,38},{6,0},{38,36},{64,70},{9... | collective-permute-start | bytes 1769480 | tf_op jit(solution)/shard_map/ppermute | solution.py:45
  11.9 3.3 %collective-permute-done.2.refs_0_.refs_1_ = bf16[256,1152]{1,0:T(8,128)(2,1)S(1)} collective-permute-done((bf16[256,1152]{1,0:T(8,128)(2,1)S(1)}, bf16[256,1152]{1,0:T(8,128)(2,1)S(1)}, u32[]{:S(2)}, u32[]{:S(2)}) %collective-permute-start.2) | collective-permute-done | bytes 589856 | tf_op jit(solution)/shard_map/ppermute | solution.py:45
  15.2 2.6 %collective-permute-done.3.refs_1_.refs_2_ = bf16[256,1152]{1,0:T(8,128)(2,1)S(1)} collective-permute-done((bf16[256,1152]{1,0:T(8,128)(2,1)S(1)}, bf16[256,1152]{1,0:T(8,128)(2,1)S(1)}, u32[]{:S(2)}, u32[]{:S(2)}) %collective-permute-start.3) | collective-permute-done | bytes 589856 | tf_op jit(solution)/shard_map/ppermute | solution.py:45
  17.8 1.6 %collective-permute-done.4.refs_2_.refs_3_ = bf16[256,1152]{1,0:T(8,128)(2,1)S(1)} collective-permute-done((bf16[256,1152]{1,0:T(8,128)(2,1)S(1)}, bf16[256,1152]{1,0:T(8,128)(2,1)S(1)}, u32[]{:S(2)}, u32[]{:S(2)}) %collective-permute-start.4) | collective-permute-done | bytes 589856 | tf_op jit(solution)/shard_map/ppermute | solution.py:45
  19.5 0.1 shard_map.70
  19.6 1.0 %collective-permute-start.9 = (bf16[768,1152]{1,0:T(8,128)(2,1)S(1)}, bf16[768,1152]{1,0:T(8,128)(2,1)S(1)}, u32[]{:S(2)}, u32[]{:S(2)}) collective-permute-start(bf16[768,1152]{1,0:T(8,128)(2,1)S(1)} %shard_map.70), channel_id=1, source_target_pairs={{0,32},{32,0},{1,33},{33,1},{2,34},{34,2},{3,35},{35,3},{4,36},{36... | collective-permute-start | bytes 5308424 | tf_op jit(solution)/shard_map/ppermute | solution.py:49
  20.7 1.2 %collective-permute-start.5 = (bf16[256,1152]{1,0:T(8,128)(2,1)S(1)}, bf16[256,1152]{1,0:T(8,128)(2,1)S(1)}, u32[]{:S(2)}, u32[]{:S(2)}) collective-permute-start(bf16[256,1152]{1,0:T(8,128)(2,1)S(1)} %collective-permute-done.2.refs_0_.refs_1_), channel_id=1, source_target_pairs={{0,70},{32,99},{2,68},{34,97},{4,66},{36,103},{6,64},{38,101},{64,... | collective-permute-start | bytes 1769480 | tf_op jit(solution)/shard_map/ppermute | solution.py:45
  21.9 1.4 %collective-permute-start.6 = (bf16[256,1152]{1,0:T(8,128)(2,1)S(1)}, bf16[256,1152]{1,0:T(8,128)(2,1)S(1)}, u32[]{:S(2)}, u32[]{:S(2)}) collective-permute-start(bf16[256,1152]{1,0:T(8,128)(2,1)S(1)} %collective-permute-done.2.refs_0_.refs_1_), channel_id=1, source_target_pairs={{0,64},{32,97},{2,66},{34,99},{4,68},{36,101},{6,70},{38,103},{64,... | collective-permute-start | bytes 1769480 | tf_op jit(solution)/shard_map/ppermute | solution.py:45
  23.4 1.2 %collective-permute-start.7 = (bf16[256,1152]{1,0:T(8,128)(2,1)S(1)}, bf16[256,1152]{1,0:T(8,128)(2,1)S(1)}, u32[]{:S(2)}, u32[]{:S(2)}) collective-permute-start(bf16[256,1152]{1,0:T(8,128)(2,1)S(1)} %collective-permute-done.3.refs_1_.refs_2_), channel_id=1, source_target_pairs={{0,6},{32,34},{2,4},{34,32},{4,2},{36,38},{6,0},{38,36},{64,70},{9... | collective-permute-start | bytes 1769480 | tf_op jit(solution)/shard_map/ppermute | solution.py:45
  24.5 1.8 %collective-permute-start.8 = (bf16[256,1152]{1,0:T(8,128)(2,1)S(1)}, bf16[256,1152]{1,0:T(8,128)(2,1)S(1)}, u32[]{:S(2)}, u32[]{:S(2)}) collective-permute-start(bf16[256,1152]{1,0:T(8,128)(2,1)S(1)} %collective-permute-done.4.refs_2_.refs_3_), channel_id=1, source_target_pairs={{0,8},{32,56},{2,10},{34,58},{4,12},{36,60},{6,14},{38,62},{64,72}... | collective-permute-start | bytes 1769480 | tf_op jit(solution)/shard_map/ppermute | solution.py:45
  27.6 0.1 pad_maximum_fusion.affine
  27.7 6.3 %shard_map.71 = (f32[256,1152]{1,0:T(8,128)S(1)}, f32[256,1152]{1,0:T(8,128)S(1)}, f32[256,1152]{1,0:T(8,128)S(1)}, f32[256,1152]{1,0:T(8,128)S(1)}) custom-call(f32[2]{0:T(128)S(1)} %pad_maximum_fusion.affine, bf16[256,1152]{1,0:T(8,128)(2,1)S(1)} %get-tuple-element.30.refs_0_, bf16[256,1152]{1,0:T(8,128)(2,1)S(1)} %collective-permute-done.2.refs_0_.refs_1_, ...), custom_call_target="tpu_custom_call" | custom-call | tf_op jit(solution)/shard_map/pallas_call | solution.py:118
  34.0 3.3 %collective-permute-done.6.refs_1_ = bf16[256,1152]{1,0:T(8,128)(2,1)S(1)} collective-permute-done((bf16[256,1152]{1,0:T(8,128)(2,1)S(1)}, bf16[256,1152]{1,0:T(8,128)(2,1)S(1)}, u32[]{:S(2)}, u32[]{:S(2)}) %collective-permute-start.6) | collective-permute-done | bytes 589856 | tf_op jit(solution)/shard_map/ppermute | solution.py:45
  37.3 0.8 %collective-permute-done.7.refs_2_.refs_0_ = bf16[256,1152]{1,0:T(8,128)(2,1)S(1)} collective-permute-done((bf16[256,1152]{1,0:T(8,128)(2,1)S(1)}, bf16[256,1152]{1,0:T(8,128)(2,1)S(1)}, u32[]{:S(2)}, u32[]{:S(2)}) %collective-permute-start.7) | collective-permute-done | bytes 589856 | tf_op jit(solution)/shard_map/ppermute | solution.py:45
  38.1 0.2 shard_map.72
  38.3 1.8 %collective-permute-start.10 = (bf16[1024,1152]{1,0:T(8,128)(2,1)S(1)}, bf16[1024,1152]{1,0:T(8,128)(2,1)S(1)}, u32[]{:S(2)}, u32[]{:S(2)}) collective-permute-start(bf16[1024,1152]{1,0:T(8,128)(2,1)S(1)} %shard_map.72), channel_id=1, source_target_pairs={{0,32},{32,0},{1,33},{33,1},{2,34},{34,2},{3,35},{35,3},{4,36},{36... | collective-permute-start | bytes 7077896 | tf_op jit(solution)/shard_map/ppermute | solution.py:49
  40.1 6.3 %shard_map.73 = (f32[256,1152]{1,0:T(8,128)S(1)}, f32[256,1152]{1,0:T(8,128)S(1)}, f32[256,1152]{1,0:T(8,128)S(1)}, f32[256,1152]{1,0:T(8,128)S(1)}) custom-call(f32[2]{0:T(128)S(1)} %pad_maximum_fusion.affine, bf16[256,1152]{1,0:T(8,128)(2,1)S(1)} %collective-permute-done.5.refs_0_, bf16[256,1152]{1,0:T(8,128)(2,1)S(1)} %collective-permute-done.6.refs_1_, ...), custom_call_target="tpu_custom_call" | custom-call | flops 4831838208 | bytes 9437184 | tf_op jit(solution)/shard_map/pallas_call | solution.py:118
  46.4 3.5 %shard_map.74 = (bf16[256,1152]{1,0:T(8,128)(2,1)S(1)}, bf16[256,1152]{1,0:T(8,128)(2,1)S(1)}) custom-call(f32[2]{0:T(128)S(1)} %pad_maximum_fusion.affine, bf16[256,1152]{1,0:T(8,128)(2,1)S(1)} %collective-permute-done.5.refs_0_, bf16[256,1152]{1,0:T(8,128)(2,1)S(1)} %collective-permute-done.6.refs_1_, ...), custom_call_target="tpu_custom_call" | custom-call | flops 2415919104 | bytes 4718592 | tf_op jit(solution)/shard_map/pallas_call | solution.py:118
  49.9 0.3 collective-permute-start.11
  50.2 1.8 %collective-permute-start.12 = (bf16[256,1152]{1,0:T(8,128)(2,1)S(1)}, bf16[256,1152]{1,0:T(8,128)(2,1)S(1)}, u32[]{:S(2)}, u32[]{:S(2)}) collective-permute-start(bf16[256,1152]{1,0:T(8,128)(2,1)S(1)} %get-tuple-element.40.refs_5_), channel_id=1, source_target_pairs={{0,64},{32,97},{2,66},{34,99},{4,68},{36,101},{6,70},{38,103},{64,... | collective-permute-start | bytes 1769480 | tf_op jit(solution)/shard_map/ppermute | solution.py:45
  52.0 3.5 %shard_map.75 = (bf16[256,1152]{1,0:T(8,128)(2,1)S(1)}, bf16[256,1152]{1,0:T(8,128)(2,1)S(1)}) custom-call(f32[2]{0:T(128)S(1)} %pad_maximum_fusion.affine, bf16[256,1152]{1,0:T(8,128)(2,1)S(1)} %collective-permute-done.7.refs_2_.refs_0_, bf16[256,1152]{1,0:T(8,128)(2,1)S(1)} %collective-permute-done.8.refs_3_.refs_1_, ...), custom_call_target="tpu_custom_call" | custom-call | flops 2415919104 | bytes 4718592 | tf_op jit(solution)/shard_map/pallas_call | solution.py:118
  55.5 2.0 %collective-permute-start.14 = (bf16[256,1152]{1,0:T(8,128)(2,1)S(1)}, bf16[256,1152]{1,0:T(8,128)(2,1)S(1)}, u32[]{:S(2)}, u32[]{:S(2)}) collective-permute-start(bf16[256,1152]{1,0:T(8,128)(2,1)S(1)} %get-tuple-element.46), channel_id=1, source_target_pairs={{0,6},{32,34},{2,4},{34,32},{4,2},{36,38},{6,0},{38,36},{64,70},{9... | collective-permute-start | bytes 1769480 | tf_op jit(solution)/shard_map/ppermute | solution.py:45
  57.5 1.8 %collective-permute-start.16 = (bf16[256,1152]{1,0:T(8,128)(2,1)S(1)}, bf16[256,1152]{1,0:T(8,128)(2,1)S(1)}, u32[]{:S(2)}, u32[]{:S(2)}) collective-permute-start(bf16[256,1152]{1,0:T(8,128)(2,1)S(1)} %get-tuple-element.41.refs_9_), channel_id=1, source_target_pairs={{0,8},{32,56},{2,10},{34,58},{4,12},{36,60},{6,14},{38,62},{64,72}... | collective-permute-start | bytes 1769480 | tf_op jit(solution)/shard_map/ppermute | solution.py:45
  59.3 6.3 %shard_map.76 = (f32[256,1152]{1,0:T(8,128)S(1)}, f32[256,1152]{1,0:T(8,128)S(1)}, f32[256,1152]{1,0:T(8,128)S(1)}, f32[256,1152]{1,0:T(8,128)S(1)}) custom-call(f32[2]{0:T(128)S(1)} %pad_maximum_fusion.affine, bf16[256,1152]{1,0:T(8,128)(2,1)S(1)} %get-tuple-element.30.refs_0_, bf16[256,1152]{1,0:T(8,128)(2,1)S(1)} %collective-permute-done.2.refs_0_.refs_1_, ...), custom_call_target="tpu_custom_call" | custom-call | flops 4831838208 | bytes 9437184 | tf_op jit(solution)/shard_map/pallas_call | solution.py:118
  65.6 0.2 collective-permute-done.12.refs_2_
  65.8 0.2 shard_map.77
  66.0 1.9 %collective-permute-start.13 = (bf16[256,1152]{1,0:T(8,128)(2,1)S(1)}, bf16[256,1152]{1,0:T(8,128)(2,1)S(1)}, u32[]{:S(2)}, u32[]{:S(2)}) collective-permute-start(bf16[256,1152]{1,0:T(8,128)(2,1)S(1)} %shard_map.77), channel_id=1, source_target_pairs={{0,8},{32,56},{2,10},{34,58},{4,12},{36,60},{6,14},{38,62},{64,72}... | collective-permute-start | bytes 1769480 | tf_op jit(solution)/shard_map/ppermute | solution.py:45
  67.9 0.1 shard_map.78
  68.0 1.6 %collective-permute-start.15 = (bf16[256,1152]{1,0:T(8,128)(2,1)S(1)}, bf16[256,1152]{1,0:T(8,128)(2,1)S(1)}, u32[]{:S(2)}, u32[]{:S(2)}) collective-permute-start(bf16[256,1152]{1,0:T(8,128)(2,1)S(1)} %shard_map.78), channel_id=1, source_target_pairs={{0,64},{32,97},{2,66},{34,99},{4,68},{36,101},{6,70},{38,103},{64,... | collective-permute-start | bytes 1769480 | tf_op jit(solution)/shard_map/ppermute | solution.py:45
  69.5 0.1 shard_map.79
  69.7 2.2 %collective-permute-start.17 = (bf16[256,1152]{1,0:T(8,128)(2,1)S(1)}, bf16[256,1152]{1,0:T(8,128)(2,1)S(1)}, u32[]{:S(2)}, u32[]{:S(2)}) collective-permute-start(bf16[256,1152]{1,0:T(8,128)(2,1)S(1)} %shard_map.79), channel_id=1, source_target_pairs={{0,6},{32,34},{2,4},{34,32},{4,2},{36,38},{6,0},{38,36},{64,70},{9... | collective-permute-start | bytes 1769480 | tf_op jit(solution)/shard_map/ppermute | solution.py:45
  72.5 3.8 %collective-permute-done.13.refs_1_ = bf16[256,1152]{1,0:T(8,128)(2,1)S(1)} collective-permute-done((bf16[256,1152]{1,0:T(8,128)(2,1)S(1)}, bf16[256,1152]{1,0:T(8,128)(2,1)S(1)}, u32[]{:S(2)}, u32[]{:S(2)}) %collective-permute-start.13) | collective-permute-done | bytes 589856 | tf_op jit(solution)/shard_map/ppermute | solution.py:45
  76.3 2.0 %collective-permute-done.15.refs_2_ = bf16[256,1152]{1,0:T(8,128)(2,1)S(1)} collective-permute-done((bf16[256,1152]{1,0:T(8,128)(2,1)S(1)}, bf16[256,1152]{1,0:T(8,128)(2,1)S(1)}, u32[]{:S(2)}, u32[]{:S(2)}) %collective-permute-start.15) | collective-permute-done | bytes 589856 | tf_op jit(solution)/shard_map/ppermute | solution.py:45
  78.3 1.1 %collective-permute-done.17.refs_3_ = bf16[256,1152]{1,0:T(8,128)(2,1)S(1)} collective-permute-done((bf16[256,1152]{1,0:T(8,128)(2,1)S(1)}, bf16[256,1152]{1,0:T(8,128)(2,1)S(1)}, u32[]{:S(2)}, u32[]{:S(2)}) %collective-permute-start.17) | collective-permute-done | bytes 589856 | tf_op jit(solution)/shard_map/ppermute | solution.py:45
  79.4 0.8 shard_map.80
  80.2 1.7 %collective-permute-start.18 = (f32[128,1152]{1,0:T(8,128)S(1)}, f32[128,1152]{1,0:T(8,128)S(1)}, u32[]{:S(2)}, u32[]{:S(2)}) collective-permute-start(f32[128,1152]{1,0:T(8,128)S(1)} %get-tuple-element.49), channel_id=1, source_target_pairs={{0,32},{32,0},{1,33},{33,1},{2,34},{34,2},{3,35},{35,3},{4,36},{36... | collective-permute-start | bytes 1769480 | tf_op jit(solution)/shard_map/ppermute | solution.py:49
  81.9 1.6 %collective-permute-done.18 = f32[128,1152]{1,0:T(8,128)S(1)} collective-permute-done((f32[128,1152]{1,0:T(8,128)S(1)}, f32[128,1152]{1,0:T(8,128)S(1)}, u32[]{:S(2)}, u32[]{:S(2)}) %collective-permute-start.18) | collective-permute-done | bytes 589856 | tf_op jit(solution)/shard_map/ppermute | solution.py:49
  83.6 1.1 %broadcast_select_fusion = (f32[128,1152]{1,0:T(8,128)}, f32[128,1152]{1,0:T(8,128)}) fusion(f32[128,1152]{1,0:T(8,128)S(1)} %collective-permute-done.18, f32[128,1152]{1,0:T(8,128)S(1)} %get-tuple-element.48, pred[]{:T(512)S(6)} %eq.3), kind=kLoop, calls=%fused_computation | loop fusion | flops 294912 | bytes 2359297 | tf_op jit(solution)/shard_map/jit(_where)/select_n | solution.py:252
  (9 shorter events, 0.0 us)
Async XLA Ops:
  0.6 3.8 %collective-permute-start = (bf16[128,1152]{1,0:T(8,128)(2,1)}, bf16[128,1152]{1,0:T(8,128)(2,1)S(1)}, u32[]{:S(2)}, u32[]{:S(2)}) collective-permute-start(bf16[128,1152]{1,0:T(8,128)(2,1)} %refs_1_.1), channel_id=1, source_target_pairs={{0,32},{32,0},{1,33},{33,1},{2,34},{34,2},{3,35},{35,3},{4,36},{36... | collective-permute-start | bytes 884744 | tf_op jit(solution)/shard_map/ppermute | solution.py:49
  2.1 2.3 %collective-permute-start.1 = (bf16[128,1152]{1,0:T(8,128)(2,1)}, bf16[128,1152]{1,0:T(8,128)(2,1)S(1)}, u32[]{:S(2)}, u32[]{:S(2)}) collective-permute-start(bf16[128,1152]{1,0:T(8,128)(2,1)} %refs_2_.1), channel_id=1, source_target_pairs={{0,32},{32,0},{1,33},{33,1},{2,34},{34,2},{3,35},{35,3},{4,36},{36... | collective-permute-start | bytes 884744 | tf_op jit(solution)/shard_map/ppermute | solution.py:49
  2.2 1.0 %copy-start = (bf16[128,1152]{1,0:T(8,128)(2,1)S(1)}, bf16[128,1152]{1,0:T(8,128)(2,1)}, u32[]{:S(2)}) copy-start(bf16[128,1152]{1,0:T(8,128)(2,1)} %refs_1_.1) | copy-start | bytes 884740
  3.2 1.0 %copy-start.1 = (bf16[128,1152]{1,0:T(8,128)(2,1)S(1)}, bf16[128,1152]{1,0:T(8,128)(2,1)}, u32[]{:S(2)}) copy-start(bf16[128,1152]{1,0:T(8,128)(2,1)} %refs_2_.1) | copy-start | bytes 884740
  4.9 10.3 %collective-permute-start.2 = (bf16[256,1152]{1,0:T(8,128)(2,1)S(1)}, bf16[256,1152]{1,0:T(8,128)(2,1)S(1)}, u32[]{:S(2)}, u32[]{:S(2)}) collective-permute-start(bf16[256,1152]{1,0:T(8,128)(2,1)S(1)} %get-tuple-element.30.refs_0_), channel_id=1, source_target_pairs={{0,8},{32,56},{2,10},{34,58},{4,12},{36,60},{6,14},{38,62},{64,72}... | collective-permute-start | bytes 1769480 | tf_op jit(solution)/shard_map/ppermute | solution.py:45
  7.5 10.3 %collective-permute-start.3 = (bf16[256,1152]{1,0:T(8,128)(2,1)S(1)}, bf16[256,1152]{1,0:T(8,128)(2,1)S(1)}, u32[]{:S(2)}, u32[]{:S(2)}) collective-permute-start(bf16[256,1152]{1,0:T(8,128)(2,1)S(1)} %get-tuple-element.30.refs_0_), channel_id=1, source_target_pairs={{0,64},{32,97},{2,66},{34,99},{4,68},{36,101},{6,70},{38,103},{64,... | collective-permute-start | bytes 1769480 | tf_op jit(solution)/shard_map/ppermute | solution.py:45
  10.3 9.2 %collective-permute-start.4 = (bf16[256,1152]{1,0:T(8,128)(2,1)S(1)}, bf16[256,1152]{1,0:T(8,128)(2,1)S(1)}, u32[]{:S(2)}, u32[]{:S(2)}) collective-permute-start(bf16[256,1152]{1,0:T(8,128)(2,1)S(1)} %get-tuple-element.30.refs_0_), channel_id=1, source_target_pairs={{0,6},{32,34},{2,4},{34,32},{4,2},{36,38},{6,0},{38,36},{64,70},{9... | collective-permute-start | bytes 1769480 | tf_op jit(solution)/shard_map/ppermute | solution.py:45
  19.6 8.1 %collective-permute-start.9 = (bf16[768,1152]{1,0:T(8,128)(2,1)S(1)}, bf16[768,1152]{1,0:T(8,128)(2,1)S(1)}, u32[]{:S(2)}, u32[]{:S(2)}) collective-permute-start(bf16[768,1152]{1,0:T(8,128)(2,1)S(1)} %shard_map.70), channel_id=1, source_target_pairs={{0,32},{32,0},{1,33},{33,1},{2,34},{34,2},{3,35},{35,3},{4,36},{36... | collective-permute-start | bytes 5308424 | tf_op jit(solution)/shard_map/ppermute | solution.py:49
  20.7 13.3 %collective-permute-start.5 = (bf16[256,1152]{1,0:T(8,128)(2,1)S(1)}, bf16[256,1152]{1,0:T(8,128)(2,1)S(1)}, u32[]{:S(2)}, u32[]{:S(2)}) collective-permute-start(bf16[256,1152]{1,0:T(8,128)(2,1)S(1)} %collective-permute-done.2.refs_0_.refs_1_), channel_id=1, source_target_pairs={{0,70},{32,99},{2,68},{34,97},{4,66},{36,103},{6,64},{38,101},{64,... | collective-permute-start | bytes 1769480 | tf_op jit(solution)/shard_map/ppermute | solution.py:45
  21.9 15.4 %collective-permute-start.6 = (bf16[256,1152]{1,0:T(8,128)(2,1)S(1)}, bf16[256,1152]{1,0:T(8,128)(2,1)S(1)}, u32[]{:S(2)}, u32[]{:S(2)}) collective-permute-start(bf16[256,1152]{1,0:T(8,128)(2,1)S(1)} %collective-permute-done.2.refs_0_.refs_1_), channel_id=1, source_target_pairs={{0,64},{32,97},{2,66},{34,99},{4,68},{36,101},{6,70},{38,103},{64,... | collective-permute-start | bytes 1769480 | tf_op jit(solution)/shard_map/ppermute | solution.py:45
  23.4 14.8 %collective-permute-start.7 = (bf16[256,1152]{1,0:T(8,128)(2,1)S(1)}, bf16[256,1152]{1,0:T(8,128)(2,1)S(1)}, u32[]{:S(2)}, u32[]{:S(2)}) collective-permute-start(bf16[256,1152]{1,0:T(8,128)(2,1)S(1)} %collective-permute-done.3.refs_1_.refs_2_), channel_id=1, source_target_pairs={{0,6},{32,34},{2,4},{34,32},{4,2},{36,38},{6,0},{38,36},{64,70},{9... | collective-permute-start | bytes 1769480 | tf_op jit(solution)/shard_map/ppermute | solution.py:45
  24.5 13.6 %collective-permute-start.8 = (bf16[256,1152]{1,0:T(8,128)(2,1)S(1)}, bf16[256,1152]{1,0:T(8,128)(2,1)S(1)}, u32[]{:S(2)}, u32[]{:S(2)}) collective-permute-start(bf16[256,1152]{1,0:T(8,128)(2,1)S(1)} %collective-permute-done.4.refs_2_.refs_3_), channel_id=1, source_target_pairs={{0,8},{32,56},{2,10},{34,58},{4,12},{36,60},{6,14},{38,62},{64,72}... | collective-permute-start | bytes 1769480 | tf_op jit(solution)/shard_map/ppermute | solution.py:45
  38.3 8.1 %collective-permute-start.10 = (bf16[1024,1152]{1,0:T(8,128)(2,1)S(1)}, bf16[1024,1152]{1,0:T(8,128)(2,1)S(1)}, u32[]{:S(2)}, u32[]{:S(2)}) collective-permute-start(bf16[1024,1152]{1,0:T(8,128)(2,1)S(1)} %shard_map.72), channel_id=1, source_target_pairs={{0,32},{32,0},{1,33},{33,1},{2,34},{34,2},{3,35},{35,3},{4,36},{36... | collective-permute-start | bytes 7077896 | tf_op jit(solution)/shard_map/ppermute | solution.py:49
  49.9 15.6 %collective-permute-start.11 = (bf16[256,1152]{1,0:T(8,128)(2,1)S(1)}, bf16[256,1152]{1,0:T(8,128)(2,1)S(1)}, u32[]{:S(2)}, u32[]{:S(2)}) collective-permute-start(bf16[256,1152]{1,0:T(8,128)(2,1)S(1)} %get-tuple-element.44), channel_id=1, source_target_pairs={{0,70},{32,99},{2,68},{34,97},{4,66},{36,103},{6,64},{38,101},{64,... | collective-permute-start | bytes 1769480 | tf_op jit(solution)/shard_map/ppermute | solution.py:45
  50.2 15.6 %collective-permute-start.12 = (bf16[256,1152]{1,0:T(8,128)(2,1)S(1)}, bf16[256,1152]{1,0:T(8,128)(2,1)S(1)}, u32[]{:S(2)}, u32[]{:S(2)}) collective-permute-start(bf16[256,1152]{1,0:T(8,128)(2,1)S(1)} %get-tuple-element.40.refs_5_), channel_id=1, source_target_pairs={{0,64},{32,97},{2,66},{34,99},{4,68},{36,101},{6,70},{38,103},{64,... | collective-permute-start | bytes 1769480 | tf_op jit(solution)/shard_map/ppermute | solution.py:45
  55.5 12.4 %collective-permute-start.14 = (bf16[256,1152]{1,0:T(8,128)(2,1)S(1)}, bf16[256,1152]{1,0:T(8,128)(2,1)S(1)}, u32[]{:S(2)}, u32[]{:S(2)}) collective-permute-start(bf16[256,1152]{1,0:T(8,128)(2,1)S(1)} %get-tuple-element.46), channel_id=1, source_target_pairs={{0,6},{32,34},{2,4},{34,32},{4,2},{36,38},{6,0},{38,36},{64,70},{9... | collective-permute-start | bytes 1769480 | tf_op jit(solution)/shard_map/ppermute | solution.py:45
  57.5 12.1 %collective-permute-start.16 = (bf16[256,1152]{1,0:T(8,128)(2,1)S(1)}, bf16[256,1152]{1,0:T(8,128)(2,1)S(1)}, u32[]{:S(2)}, u32[]{:S(2)}) collective-permute-start(bf16[256,1152]{1,0:T(8,128)(2,1)S(1)} %get-tuple-element.41.refs_9_), channel_id=1, source_target_pairs={{0,8},{32,56},{2,10},{34,58},{4,12},{36,60},{6,14},{38,62},{64,72}... | collective-permute-start | bytes 1769480 | tf_op jit(solution)/shard_map/ppermute | solution.py:45
  66.0 10.3 %collective-permute-start.13 = (bf16[256,1152]{1,0:T(8,128)(2,1)S(1)}, bf16[256,1152]{1,0:T(8,128)(2,1)S(1)}, u32[]{:S(2)}, u32[]{:S(2)}) collective-permute-start(bf16[256,1152]{1,0:T(8,128)(2,1)S(1)} %shard_map.77), channel_id=1, source_target_pairs={{0,8},{32,56},{2,10},{34,58},{4,12},{36,60},{6,14},{38,62},{64,72}... | collective-permute-start | bytes 1769480 | tf_op jit(solution)/shard_map/ppermute | solution.py:45
  68.0 10.3 %collective-permute-start.15 = (bf16[256,1152]{1,0:T(8,128)(2,1)S(1)}, bf16[256,1152]{1,0:T(8,128)(2,1)S(1)}, u32[]{:S(2)}, u32[]{:S(2)}) collective-permute-start(bf16[256,1152]{1,0:T(8,128)(2,1)S(1)} %shard_map.78), channel_id=1, source_target_pairs={{0,64},{32,97},{2,66},{34,99},{4,68},{36,101},{6,70},{38,103},{64,... | collective-permute-start | bytes 1769480 | tf_op jit(solution)/shard_map/ppermute | solution.py:45
  69.7 9.7 %collective-permute-start.17 = (bf16[256,1152]{1,0:T(8,128)(2,1)S(1)}, bf16[256,1152]{1,0:T(8,128)(2,1)S(1)}, u32[]{:S(2)}, u32[]{:S(2)}) collective-permute-start(bf16[256,1152]{1,0:T(8,128)(2,1)S(1)} %shard_map.79), channel_id=1, source_target_pairs={{0,6},{32,34},{2,4},{34,32},{4,2},{36,38},{6,0},{38,36},{64,70},{9... | collective-permute-start | bytes 1769480 | tf_op jit(solution)/shard_map/ppermute | solution.py:45
  80.2 3.4 %collective-permute-start.18 = (f32[128,1152]{1,0:T(8,128)S(1)}, f32[128,1152]{1,0:T(8,128)S(1)}, u32[]{:S(2)}, u32[]{:S(2)}) collective-permute-start(f32[128,1152]{1,0:T(8,128)S(1)} %get-tuple-element.49), channel_id=1, source_target_pairs={{0,32},{32,0},{1,33},{33,1},{2,34},{34,2},{3,35},{35,3},{4,36},{36... | collective-permute-start | bytes 1769480 | tf_op jit(solution)/shard_map/ppermute | solution.py:49

commit v8 on v7

--- a/solution.py
+++ b/solution.py
@@ -14,6 +14,8 @@
 FINE_SIZES = (2, 2, 4, 4, 2)
 RING = 4
 VMEM_BYTES = 16 * 1024 * 1024
+WIDE_VMEM_BYTES = 56 * 1024 * 1024
+CUTS = 4
 HALF = jnp.bfloat16
 FULL = jnp.float32
 
@@ -23,7 +25,8 @@
 PARAMS = pltpu.CompilerParams(vmem_limit_bytes=VMEM_BYTES)
 
 ONE = ("x", "y", "z")
-TWO = ("xyz", "xy", "yz", "zx")
+TWO = ("xy", "yz", "zx")
+CORNER = "xyz"
 
 
 def place(core, x, y, z):
@@ -130,6 +133,40 @@
     )(affine, *mine, *theirs, *starts, *after)
 
 
+def cut_copies(pairs, sems):
+    copies = []
+    for source, target in pairs:
+        rows = source.shape[0] // CUTS
+        for k in range(CUTS):
+            at = pl.ds(k * rows, rows)
+            copies.append(pltpu.make_async_copy(source.at[at], target.at[at], sems.at[len(copies)]))
+    return copies
+
+
+def first_kernel(is_first, image_raw, text_raw, image, text, raw_here, held, sems):
+    copies = cut_copies([(image_raw, held.at[0]), (text_raw, held.at[1])], sems)
+    for copy in copies:
+        copy.start()
+    for copy in copies:
+        copy.wait()
+    images, texts = held[0].astype(FULL), held[1].astype(FULL)
+    image[...] = unit_rows(images)[0].astype(HALF)
+    text[...] = unit_rows(texts)[0].astype(HALF)
+    raw_here[...] = jnp.where(is_first[0] > 0, images, texts).astype(HALF)
+
+
+def last_kernel(core, here, back, image_grad, text_grad, sems):
+    for mine, theirs, which in ((image_grad, text_grad, 0), (text_grad, image_grad, 1)):
+
+        @pl.when(core[0] == which)
+        def _(mine=mine, theirs=theirs):
+            copies = cut_copies([(here, mine), (back, theirs)], sems)
+            for copy in copies:
+                copy.start()
+            for copy in copies:
+                copy.wait()
+
+
 def finish_kernel(core, multiplier, raw, *refs):
     parts, (here, there, grads) = refs[:-3], refs[-3:]
     rows = here.shape[0]
@@ -158,16 +195,14 @@
 
     image_there = other_core(picture_vectors_raw)
     text_there = other_core(caption_vectors_raw)
-    image, text, raw_here = local(
-        lambda scalars, refs: [
-            unit_rows(refs[0][...])[0],
-            unit_rows(refs[1][...])[0],
-            jnp.where(scalars[0][0] > 0, refs[0][...].astype(FULL), refs[1][...].astype(FULL)),
-        ],
-        [shard] * 3,
-        [first_flag],
-        [picture_vectors_raw, caption_vectors_raw],
-    )
+    image, text, raw_here = pl.pallas_call(
+        first_kernel,
+        out_shape=[jax.ShapeDtypeStruct(*shard)] * 3,
+        in_specs=[SMEM, ANY, ANY],
+        out_specs=[VMEM] * 3,
+        scratch_shapes=[pltpu.VMEM((2, rows, width), HALF), pltpu.SemaphoreType.DMA((2 * CUTS,))],
+        compiler_params=pltpu.CompilerParams(vmem_limit_bytes=WIDE_VMEM_BYTES),
+    )(first_flag, picture_vectors_raw, caption_vectors_raw)
 
     def own_units(scalars, refs):
         first = scalars[0][0] > 0
@@ -201,29 +236,36 @@
     mine = {"": own}
     for way in ONE:
         mine[way] = sent(own, way)
-    mine["xyz"] = sent(mine["x"], "yz")
     mine["xy"] = sent(mine["x"], "y")
     mine["yz"] = sent(mine["y"], "z")
     mine["zx"] = sent(mine["z"], "x")
     def pick(units, ways):
         return [units[way] for way in ways]
 
+    mine[CORNER] = sent(mine["xy"], "z")
+
+    def pick(units, ways):
+        return [units[way] for way in ways]
+
     theirs_one = [own_theirs, stacked(ONE)]
     near = ("", *ONE)
-    sums = sums_of(affine, pick(mine, near), theirs_one, diagonal=True, hides=False)
-    theirs_two = [stacked(TWO, sums[:1])]
-    sums += sums_of(affine, pick(mine, TWO), theirs_one)
-    sums = dict(zip((*near, *TWO), sums, strict=True))
-
-    def parts_of(ways, kinds, after=()):
-        return sums_of(affine, pick(mine, ways), theirs_two, pick(sums, ways), after, kinds)
-
-    part_xyz, part_xy = parts_of(("xyz", "xy"), [HALF, HALF])
+    sums_near = sums_of(affine, pick(mine, near), theirs_one, diagonal=True, hides=False)
+    theirs_two = [stacked(TWO, sums_near[:1])]
+    sums_two = sums_of(affine, pick(mine, TWO), theirs_one)
+    sums_two = sums_of(affine, pick(mine, TWO), theirs_two, sums_two)
+    theirs_corner = [stacked([CORNER], sums_two[:1])]
+    sums_corner = sums_of(affine, [mine[CORNER]], theirs_one + theirs_two, after=sums_two[:1])
+
+    far = (CORNER, *TWO)
+    part_xyz, part_xy, part_yz, part_zx = sums_of(
+        affine, pick(mine, far), theirs_corner, [*sums_corner, *sums_two], kinds=[HALF] * 4
+    )
     for_x = [sent(part_xyz, "yz"), sent(part_xy, "y")]
-    part_yz, part_zx = parts_of(("yz", "zx"), [HALF, HALF], [part_xy])
     for_y = [sent(part_yz, "z")]
     for_z = [sent(part_zx, "x")]
-    own_part, part_x, part_y, part_z = parts_of(near, [FULL] * 4, [part_zx])
+    own_part, part_x, part_y, part_z = sums_of(
+        affine, pick(mine, near), theirs_two + theirs_corner, sums_near, after=[part_xyz]
+    )
 
     def with_added(part, added, way):
         (total,) = local(
@@ -249,7 +291,16 @@
         compiler_params=PARAMS,
     )(core.reshape(1), multiplier, raw, own_part, *arrived)
     back = other_core(there)
-    return (jnp.where(is_first, here, back), jnp.where(is_first, back, here))
+    return tuple(
+        pl.pallas_call(
+            last_kernel,
+            out_shape=[shard_full] * 2,
+            in_specs=[SMEM, VMEM, VMEM],
+            out_specs=[ANY] * 2,
+            scratch_shapes=[pltpu.SemaphoreType.DMA((2 * CUTS,))],
+            compiler_params=PARAMS,
+        )(core.reshape(1), here, back)
+    )
 
 
 def solution(mesh):

time: 84.9 us -> 90 us (1.060)
  Pallas kernels: 28.1 us -> 33 us
  waiting for transfers between devices: 20.4 us -> 23 us
  starting transfers between devices: 30.3 us -> 27.8 us
  other arithmetic: 1.16 us -> 0.08 us
  local copies, waits for them, and re-layouts: 1.92 us -> 2.88 us
    pallas_call x0 -> x2, Pallas kernels: none -> 3.37 us  [the longest x1 2.3 us: on_device(): pl.pallas_call(first_kernel, out_shape=[jax.ShapeDtypeStruct(*shard)] * 3...]
    ppermute x14, starting transfers between devices: 24.1 us -> 20.8 us  [sent(): return lax.ppermute(value, FINE_AXES, pairs)]
    ppermute x14, waiting for transfers between devices: 18.8 us -> 21 us  [sent(): return lax.ppermute(value, FINE_AXES, pairs)]
    pallas_call x5 -> x6, Pallas kernels: 25.9 us -> 27.6 us  [sums_of(): pl.pallas_call(functools.partial(sums_kernel, count, n_theirs, n_starts,...]
    select_n x1 -> x0, other arithmetic: 1.09 us -> none  [on_device(): return (jnp.where(is_first, here, back), jnp.where(is_first, back, here))]
    unnamed x4 -> x6, local copies, waits for them, and re-layouts: 1.92 us -> 2.88 us
    ppermute x5 -> x6, starting transfers between devices: 6.2 us -> 6.98 us  [other_core(): return lax.ppermute(value, 'core', [(0, 1), (1, 0)])]
    ppermute x5 -> x6, waiting for transfers between devices: 1.64 us -> 2 us  [other_core(): return lax.ppermute(value, 'core', [(0, 1), (1, 0)])]
  transfers between devices with their start and end apart: 19 -> 20, of which waited for: 10 -> 9; matrix products, arithmetic and copies ran while one was open for 0% -> 0% of each run, Pallas kernels for 27% -> 31%
where the time goes in v8:
time: 90 us; the launch traced here: 89.7 us
  Pallas kernels  33 us (37%)
  starting transfers between devices  27.8 us (31%)
  waiting for transfers between devices  23 us (26%)
  between operations  2.94 us (3%)
  local copies, waits for them, and re-layouts  2.88 us (3%)
    pallas_call x6, Pallas kernels, sums_of(): pl.pallas_call(functools.partial(sums_kernel, count, n_theirs, n_starts,...  27.6 us
    ppermute x14, waiting for transfers between devices, sent(): return lax.ppermute(value, FINE_AXES, pairs)  21 us
    ppermute x14, starting transfers between devices, sent(): return lax.ppermute(value, FINE_AXES, pairs)  20.8 us
    ppermute x6, starting transfers between devices, other_core(): return lax.ppermute(value, 'core', [(0, 1), (1, 0)])  6.98 us
    unnamed x6, local copies, waits for them, and re-layouts  2.88 us
    pallas_call x1, Pallas kernels, on_device(): pl.pallas_call(first_kernel, out_shape=[jax.ShapeDtypeStruct(*shard)] * 3...  2.3 us
    ppermute x6, waiting for transfers between devices, other_core(): return lax.ppermute(value, 'core', [(0, 1), (1, 0)])  2 us
  transfers between devices with their start and end apart: 20, of which 9 were waited for; matrix products, arithmetic and copies ran while one was open for 0% of the time, Pallas kernels for 31%

profile of v8, /device:TPU:1, one launch (start us, length us, event | category | flops | bytes accessed | tf_op | source)
XLA Modules:
  0.0 89.7 jit_solution(7280527652547086810)
XLA Ops:
  0.6 1.5 %collective-permute-start = (bf16[128,1152]{1,0:T(8,128)(2,1)}, bf16[128,1152]{1,0:T(8,128)(2,1)S(1)}, u32[]{:S(2)}, u32[]{:S(2)}) collective-permute-start(bf16[128,1152]{1,0:T(8,128)(2,1)} %image_raw.1), channel_id=1, source_target_pairs={{0,32},{32,0},{1,33},{33,1},{2,34},{34,2},{3,35},{35,3},{4,36},{36... | collective-permute-start | bytes 884744 | tf_op jit(solution)/shard_map/ppermute | solution.py:52
  2.1 0.1 collective-permute-start.1
  2.2 2.3 %shard_map.68 = (bf16[128,1152]{1,0:T(8,128)(2,1)}, bf16[128,1152]{1,0:T(8,128)(2,1)}, bf16[128,1152]{1,0:T(8,128)(2,1)}) custom-call(f32[1]{0:T(128)} %bitcast.1.is_first.refs_0_, bf16[128,1152]{1,0:T(8,128)(2,1)} %image_raw.1, bf16[128,1152]{1,0:T(8,128)(2,1)} %text_raw.1), custom_call_target="tpu_custom_call" | custom-call | tf_op jit(solution)/shard_map/pallas_call | solution.py:198
  4.5 0.0 copy-start
  4.6 1.0 %copy-done = bf16[128,1152]{1,0:T(8,128)(2,1)S(1)} copy-done((bf16[128,1152]{1,0:T(8,128)(2,1)S(1)}, bf16[128,1152]{1,0:T(8,128)(2,1)}, u32[]{:S(2)}) %copy-start) | copy-done | bytes 294936
  5.5 1.0 %copy-done.1 = bf16[128,1152]{1,0:T(8,128)(2,1)S(1)} copy-done((bf16[128,1152]{1,0:T(8,128)(2,1)S(1)}, bf16[128,1152]{1,0:T(8,128)(2,1)}, u32[]{:S(2)}) %copy-start.1) | copy-done | bytes 294936
  6.5 1.0 %copy-done.2 = bf16[128,1152]{1,0:T(8,128)(2,1)S(1)} copy-done((bf16[128,1152]{1,0:T(8,128)(2,1)S(1)}, bf16[128,1152]{1,0:T(8,128)(2,1)}, u32[]{:S(2)}) %copy-start.2) | copy-done | bytes 294936
  7.4 0.5 shard_map.69
  7.9 2.6 %collective-permute-start.2 = (bf16[256,1152]{1,0:T(8,128)(2,1)S(1)}, bf16[256,1152]{1,0:T(8,128)(2,1)S(1)}, u32[]{:S(2)}, u32[]{:S(2)}) collective-permute-start(bf16[256,1152]{1,0:T(8,128)(2,1)S(1)} %get-tuple-element.32.refs_0_), channel_id=1, source_target_pairs={{0,8},{32,56},{2,10},{34,58},{4,12},{36,60},{6,14},{38,62},{64,72}... | collective-permute-start | bytes 1769480 | tf_op jit(solution)/shard_map/ppermute | solution.py:48
  10.6 2.7 %collective-permute-start.3 = (bf16[256,1152]{1,0:T(8,128)(2,1)S(1)}, bf16[256,1152]{1,0:T(8,128)(2,1)S(1)}, u32[]{:S(2)}, u32[]{:S(2)}) collective-permute-start(bf16[256,1152]{1,0:T(8,128)(2,1)S(1)} %get-tuple-element.32.refs_0_), channel_id=1, source_target_pairs={{0,64},{32,97},{2,66},{34,99},{4,68},{36,101},{6,70},{38,103},{64,... | collective-permute-start | bytes 1769480 | tf_op jit(solution)/shard_map/ppermute | solution.py:48
  13.3 1.6 %collective-permute-start.4 = (bf16[256,1152]{1,0:T(8,128)(2,1)S(1)}, bf16[256,1152]{1,0:T(8,128)(2,1)S(1)}, u32[]{:S(2)}, u32[]{:S(2)}) collective-permute-start(bf16[256,1152]{1,0:T(8,128)(2,1)S(1)} %get-tuple-element.32.refs_0_), channel_id=1, source_target_pairs={{0,6},{32,34},{2,4},{34,32},{4,2},{36,38},{6,0},{38,36},{64,70},{9... | collective-permute-start | bytes 1769480 | tf_op jit(solution)/shard_map/ppermute | solution.py:48
  14.9 3.3 %collective-permute-done.2.refs_0_.refs_1_ = bf16[256,1152]{1,0:T(8,128)(2,1)S(1)} collective-permute-done((bf16[256,1152]{1,0:T(8,128)(2,1)S(1)}, bf16[256,1152]{1,0:T(8,128)(2,1)S(1)}, u32[]{:S(2)}, u32[]{:S(2)}) %collective-permute-start.2) | collective-permute-done | bytes 589856 | tf_op jit(solution)/shard_map/ppermute | solution.py:48
  18.2 2.6 %collective-permute-done.3.refs_1_.refs_2_ = bf16[256,1152]{1,0:T(8,128)(2,1)S(1)} collective-permute-done((bf16[256,1152]{1,0:T(8,128)(2,1)S(1)}, bf16[256,1152]{1,0:T(8,128)(2,1)S(1)}, u32[]{:S(2)}, u32[]{:S(2)}) %collective-permute-start.3) | collective-permute-done | bytes 589856 | tf_op jit(solution)/shard_map/ppermute | solution.py:48
  20.9 1.6 %collective-permute-done.4.refs_2_.refs_3_ = bf16[256,1152]{1,0:T(8,128)(2,1)S(1)} collective-permute-done((bf16[256,1152]{1,0:T(8,128)(2,1)S(1)}, bf16[256,1152]{1,0:T(8,128)(2,1)S(1)}, u32[]{:S(2)}, u32[]{:S(2)}) %collective-permute-start.4) | collective-permute-done | bytes 589856 | tf_op jit(solution)/shard_map/ppermute | solution.py:48
  22.5 0.1 shard_map.70
  22.6 1.0 %collective-permute-start.8 = (bf16[768,1152]{1,0:T(8,128)(2,1)S(1)}, bf16[768,1152]{1,0:T(8,128)(2,1)S(1)}, u32[]{:S(2)}, u32[]{:S(2)}) collective-permute-start(bf16[768,1152]{1,0:T(8,128)(2,1)S(1)} %shard_map.70), channel_id=1, source_target_pairs={{0,32},{32,0},{1,33},{33,1},{2,34},{34,2},{3,35},{35,3},{4,36},{36... | collective-permute-start | bytes 5308424 | tf_op jit(solution)/shard_map/ppermute | solution.py:52
  23.7 1.9 %collective-permute-start.5 = (bf16[256,1152]{1,0:T(8,128)(2,1)S(1)}, bf16[256,1152]{1,0:T(8,128)(2,1)S(1)}, u32[]{:S(2)}, u32[]{:S(2)}) collective-permute-start(bf16[256,1152]{1,0:T(8,128)(2,1)S(1)} %collective-permute-done.2.refs_0_.refs_1_), channel_id=1, source_target_pairs={{0,64},{32,97},{2,66},{34,99},{4,68},{36,101},{6,70},{38,103},{64,... | collective-permute-start | bytes 1769480 | tf_op jit(solution)/shard_map/ppermute | solution.py:48
  25.6 1.8 %collective-permute-start.7 = (bf16[256,1152]{1,0:T(8,128)(2,1)S(1)}, bf16[256,1152]{1,0:T(8,128)(2,1)S(1)}, u32[]{:S(2)}, u32[]{:S(2)}) collective-permute-start(bf16[256,1152]{1,0:T(8,128)(2,1)S(1)} %collective-permute-done.4.refs_2_.refs_3_), channel_id=1, source_target_pairs={{0,8},{32,56},{2,10},{34,58},{4,12},{36,60},{6,14},{38,62},{64,72}... | collective-permute-start | bytes 1769480 | tf_op jit(solution)/shard_map/ppermute | solution.py:48
  28.7 0.1 pad_maximum_fusion.affine
  28.8 6.3 %shard_map.71 = (f32[256,1152]{1,0:T(8,128)S(1)}, f32[256,1152]{1,0:T(8,128)S(1)}, f32[256,1152]{1,0:T(8,128)S(1)}, f32[256,1152]{1,0:T(8,128)S(1)}) custom-call(f32[2]{0:T(128)S(1)} %pad_maximum_fusion.affine, bf16[256,1152]{1,0:T(8,128)(2,1)S(1)} %get-tuple-element.32.refs_0_, bf16[256,1152]{1,0:T(8,128)(2,1)S(1)} %collective-permute-done.2.refs_0_.refs_1_, ...), custom_call_target="tpu_custom_call" | custom-call | tf_op jit(solution)/shard_map/pallas_call | solution.py:121
  35.1 0.5 collective-permute-done.7.refs_2_.refs_3_
  35.5 0.1 shard_map.72
  35.7 1.9 %collective-permute-start.9 = (bf16[768,1152]{1,0:T(8,128)(2,1)S(1)}, bf16[768,1152]{1,0:T(8,128)(2,1)S(1)}, u32[]{:S(2)}, u32[]{:S(2)}) collective-permute-start(bf16[768,1152]{1,0:T(8,128)(2,1)S(1)} %shard_map.72), channel_id=1, source_target_pairs={{0,32},{32,0},{1,33},{33,1},{2,34},{34,2},{3,35},{35,3},{4,36},{36... | collective-permute-start | bytes 5308424 | tf_op jit(solution)/shard_map/ppermute | solution.py:52
  37.6 0.0 collective-permute-start.10
  37.6 4.9 %shard_map.73 = (f32[256,1152]{1,0:T(8,128)S(1)}, f32[256,1152]{1,0:T(8,128)S(1)}, f32[256,1152]{1,0:T(8,128)S(1)}) custom-call(f32[2]{0:T(128)S(1)} %pad_maximum_fusion.affine, bf16[256,1152]{1,0:T(8,128)(2,1)S(1)} %collective-permute-done.5.refs_0_.refs_1_, bf16[256,1152]{1,0:T(8,128)(2,1)S(1)} %collective-permute-done.6.refs_1_.refs_2_, ...), custom_call_target="tpu_custom_call" | custom-call | flops 3623878656 | bytes 7077888 | tf_op jit(solution)/shard_map/pallas_call | solution.py:121
  42.4 4.2 %shard_map.74 = (f32[256,1152]{1,0:T(8,128)S(1)}, f32[256,1152]{1,0:T(8,128)S(1)}, f32[256,1152]{1,0:T(8,128)S(1)}) custom-call(f32[2]{0:T(128)S(1)} %pad_maximum_fusion.affine, bf16[256,1152]{1,0:T(8,128)(2,1)S(1)} %collective-permute-done.5.refs_0_.refs_1_, bf16[256,1152]{1,0:T(8,128)(2,1)S(1)} %collective-permute-done.6.refs_1_.refs_2_, ...), custom_call_target="tpu_custom_call" | custom-call | flops 2717908992 | bytes 7077888 | tf_op jit(solution)/shard_map/pallas_call | solution.py:121
  46.7 2.4 %collective-permute-start.11 = (bf16[256,1152]{1,0:T(8,128)(2,1)S(1)}, bf16[256,1152]{1,0:T(8,128)(2,1)S(1)}, u32[]{:S(2)}, u32[]{:S(2)}) collective-permute-start(bf16[256,1152]{1,0:T(8,128)(2,1)S(1)} %shard_map.75), channel_id=1, source_target_pairs={{0,32},{32,0},{1,33},{33,1},{2,34},{34,2},{3,35},{35,3},{4,36},{36... | collective-permute-start | bytes 1769480 | tf_op jit(solution)/shard_map/ppermute | solution.py:52
  49.0 3.2 %shard_map.76.refs_5_ = f32[256,1152]{1,0:T(8,128)S(1)} custom-call(f32[2]{0:T(128)S(1)} %pad_maximum_fusion.affine, bf16[256,1152]{1,0:T(8,128)(2,1)S(1)} %collective-permute-done.10.refs_0_, bf16[256,1152]{1,0:T(8,128)(2,1)S(1)} %get-tuple-element.33.refs_4_.refs_3_.refs_1_, bf16[768,1152]{1,0:T(8,128)(2,1)S(1)} %collective-permute-done.8.refs_5_.refs_4_.refs_2_, ...), custom_call_target="tpu_custom_call" | custom-call | flops 2113929216 | bytes 2359296 | tf_op jit(solution)/shard_map/pallas_call | solution.py:121
  52.2 2.9 %shard_map.77 = (bf16[256,1152]{1,0:T(8,128)(2,1)S(1)}, bf16[256,1152]{1,0:T(8,128)(2,1)S(1)}, bf16[256,1152]{1,0:T(8,128)(2,1)S(1)}, bf16[256,1152]{1,0:T(8,128)(2,1)S(1)}) custom-call(f32[2]{0:T(128)S(1)} %pad_maximum_fusion.affine, bf16[256,1152]{1,0:T(8,128)(2,1)S(1)} %collective-permute-done.10.refs_0_, ...), custom_call_target="tpu_custom_call" | custom-call | flops 1207959552 | bytes 9437184 | tf_op jit(solution)/shard_map/pallas_call | solution.py:121
  55.1 1.9 %collective-permute-start.17 = (bf16[256,1152]{1,0:T(8,128)(2,1)S(1)}, bf16[256,1152]{1,0:T(8,128)(2,1)S(1)}, u32[]{:S(2)}, u32[]{:S(2)}) collective-permute-start(bf16[256,1152]{1,0:T(8,128)(2,1)S(1)} %get-tuple-element.51), channel_id=1, source_target_pairs={{0,8},{32,56},{2,10},{34,58},{4,12},{36,60},{6,14},{38,62},{64,72}... | collective-permute-start | bytes 1769480 | tf_op jit(solution)/shard_map/ppermute | solution.py:48
  57.0 0.5 collective-permute-start.15
  57.5 3.4 %collective-permute-start.12 = (bf16[256,1152]{1,0:T(8,128)(2,1)S(1)}, bf16[256,1152]{1,0:T(8,128)(2,1)S(1)}, u32[]{:S(2)}, u32[]{:S(2)}) collective-permute-start(bf16[256,1152]{1,0:T(8,128)(2,1)S(1)} %get-tuple-element.44.refs_10_), channel_id=1, source_target_pairs={{0,70},{32,99},{2,68},{34,97},{4,66},{36,103},{6,64},{38,101},{64,... | collective-permute-start | bytes 1769480 | tf_op jit(solution)/shard_map/ppermute | solution.py:48
  60.9 0.0 collective-permute-start.13
  60.9 6.3 %shard_map.78 = (f32[256,1152]{1,0:T(8,128)S(1)}, f32[256,1152]{1,0:T(8,128)S(1)}, f32[256,1152]{1,0:T(8,128)S(1)}, f32[256,1152]{1,0:T(8,128)S(1)}) custom-call(f32[2]{0:T(128)S(1)} %pad_maximum_fusion.affine, bf16[256,1152]{1,0:T(8,128)(2,1)S(1)} %get-tuple-element.32.refs_0_, bf16[256,1152]{1,0:T(8,128)(2,1)S(1)} %collective-permute-done.2.refs_0_.refs_1_, ...), custom_call_target="tpu_custom_call" | custom-call | flops 4831838208 | bytes 9437184 | tf_op jit(solution)/shard_map/pallas_call | solution.py:121
  67.2 0.1 shard_map.81
  67.3 0.5 collective-permute-start.18
  67.9 4.5 %collective-permute-done.15.refs_1_ = bf16[256,1152]{1,0:T(8,128)(2,1)S(1)} collective-permute-done((bf16[256,1152]{1,0:T(8,128)(2,1)S(1)}, bf16[256,1152]{1,0:T(8,128)(2,1)S(1)}, u32[]{:S(2)}, u32[]{:S(2)}) %collective-permute-start.15) | collective-permute-done | bytes 589856 | tf_op jit(solution)/shard_map/ppermute | solution.py:48
  72.3 0.1 shard_map.80
  72.5 2.8 %collective-permute-start.16 = (bf16[256,1152]{1,0:T(8,128)(2,1)S(1)}, bf16[256,1152]{1,0:T(8,128)(2,1)S(1)}, u32[]{:S(2)}, u32[]{:S(2)}) collective-permute-start(bf16[256,1152]{1,0:T(8,128)(2,1)S(1)} %shard_map.80), channel_id=1, source_target_pairs={{0,64},{32,97},{2,66},{34,99},{4,68},{36,101},{6,70},{38,103},{64,... | collective-permute-start | bytes 1769480 | tf_op jit(solution)/shard_map/ppermute | solution.py:48
  75.3 0.2 shard_map.79
  75.5 0.9 %collective-permute-start.14 = (bf16[256,1152]{1,0:T(8,128)(2,1)S(1)}, bf16[256,1152]{1,0:T(8,128)(2,1)S(1)}, u32[]{:S(2)}, u32[]{:S(2)}) collective-permute-start(bf16[256,1152]{1,0:T(8,128)(2,1)S(1)} %shard_map.79), channel_id=1, source_target_pairs={{0,8},{32,56},{2,10},{34,58},{4,12},{36,60},{6,14},{38,62},{64,72}... | collective-permute-start | bytes 1769480 | tf_op jit(solution)/shard_map/ppermute | solution.py:48
  77.1 1.6 %collective-permute-done.18.refs_3_ = bf16[256,1152]{1,0:T(8,128)(2,1)S(1)} collective-permute-done((bf16[256,1152]{1,0:T(8,128)(2,1)S(1)}, bf16[256,1152]{1,0:T(8,128)(2,1)S(1)}, u32[]{:S(2)}, u32[]{:S(2)}) %collective-permute-start.18) | collective-permute-done | bytes 589856 | tf_op jit(solution)/shard_map/ppermute | solution.py:48
  78.7 3.9 %collective-permute-done.16.refs_2_ = bf16[256,1152]{1,0:T(8,128)(2,1)S(1)} collective-permute-done((bf16[256,1152]{1,0:T(8,128)(2,1)S(1)}, bf16[256,1152]{1,0:T(8,128)(2,1)S(1)}, u32[]{:S(2)}, u32[]{:S(2)}) %collective-permute-start.16) | collective-permute-done | bytes 589856 | tf_op jit(solution)/shard_map/ppermute | solution.py:48
  82.5 3.0 %collective-permute-done.14.refs_1_ = bf16[256,1152]{1,0:T(8,128)(2,1)S(1)} collective-permute-done((bf16[256,1152]{1,0:T(8,128)(2,1)S(1)}, bf16[256,1152]{1,0:T(8,128)(2,1)S(1)}, u32[]{:S(2)}, u32[]{:S(2)}) %collective-permute-start.14) | collective-permute-done | bytes 589856 | tf_op jit(solution)/shard_map/ppermute | solution.py:48
  85.5 0.8 shard_map.82
  86.3 0.1 collective-permute-start.19
  86.4 2.0 %collective-permute-done.19.back = f32[128,1152]{1,0:T(8,128)S(1)} collective-permute-done((f32[128,1152]{1,0:T(8,128)S(1)}, f32[128,1152]{1,0:T(8,128)S(1)}, u32[]{:S(2)}, u32[]{:S(2)}) %collective-permute-start.19) | collective-permute-done | bytes 589856 | tf_op jit(solution)/shard_map/ppermute | solution.py:52
  88.4 1.1 %shard_map.83 = (f32[128,1152]{1,0:T(8,128)}, f32[128,1152]{1,0:T(8,128)}) custom-call(s32[1]{0:T(128)} %bitcast.core, f32[128,1152]{1,0:T(8,128)S(1)} %get-tuple-element.52.here, f32[128,1152]{1,0:T(8,128)S(1)} %collective-permute-done.19.back), custom_call_target="tpu_custom_call" | custom-call | tf_op jit(solution)/shard_map/pallas_call | solution.py:295
  (15 shorter events, 0.1 us)
Async XLA Ops:
  0.6 3.9 %collective-permute-start = (bf16[128,1152]{1,0:T(8,128)(2,1)}, bf16[128,1152]{1,0:T(8,128)(2,1)S(1)}, u32[]{:S(2)}, u32[]{:S(2)}) collective-permute-start(bf16[128,1152]{1,0:T(8,128)(2,1)} %image_raw.1), channel_id=1, source_target_pairs={{0,32},{32,0},{1,33},{33,1},{2,34},{34,2},{3,35},{35,3},{4,36},{36... | collective-permute-start | bytes 884744 | tf_op jit(solution)/shard_map/ppermute | solution.py:52
  2.1 2.4 %collective-permute-start.1 = (bf16[128,1152]{1,0:T(8,128)(2,1)}, bf16[128,1152]{1,0:T(8,128)(2,1)S(1)}, u32[]{:S(2)}, u32[]{:S(2)}) collective-permute-start(bf16[128,1152]{1,0:T(8,128)(2,1)} %text_raw.1), channel_id=1, source_target_pairs={{0,32},{32,0},{1,33},{33,1},{2,34},{34,2},{3,35},{35,3},{4,36},{36... | collective-permute-start | bytes 884744 | tf_op jit(solution)/shard_map/ppermute | solution.py:52
  4.5 1.0 %copy-start = (bf16[128,1152]{1,0:T(8,128)(2,1)S(1)}, bf16[128,1152]{1,0:T(8,128)(2,1)}, u32[]{:S(2)}) copy-start(bf16[128,1152]{1,0:T(8,128)(2,1)} %get-tuple-element.28.refs_3_) | copy-start | bytes 884740
  5.5 1.0 %copy-start.1 = (bf16[128,1152]{1,0:T(8,128)(2,1)S(1)}, bf16[128,1152]{1,0:T(8,128)(2,1)}, u32[]{:S(2)}) copy-start(bf16[128,1152]{1,0:T(8,128)(2,1)} %get-tuple-element.29.refs_4_) | copy-start | bytes 884740
  6.5 1.0 %copy-start.2 = (bf16[128,1152]{1,0:T(8,128)(2,1)S(1)}, bf16[128,1152]{1,0:T(8,128)(2,1)}, u32[]{:S(2)}) copy-start(bf16[128,1152]{1,0:T(8,128)(2,1)} %get-tuple-element.30.refs_5_) | copy-start | bytes 884740
  7.9 10.3 %collective-permute-start.2 = (bf16[256,1152]{1,0:T(8,128)(2,1)S(1)}, bf16[256,1152]{1,0:T(8,128)(2,1)S(1)}, u32[]{:S(2)}, u32[]{:S(2)}) collective-permute-start(bf16[256,1152]{1,0:T(8,128)(2,1)S(1)} %get-tuple-element.32.refs_0_), channel_id=1, source_target_pairs={{0,8},{32,56},{2,10},{34,58},{4,12},{36,60},{6,14},{38,62},{64,72}... | collective-permute-start | bytes 1769480 | tf_op jit(solution)/shard_map/ppermute | solution.py:48
  10.6 10.3 %collective-permute-start.3 = (bf16[256,1152]{1,0:T(8,128)(2,1)S(1)}, bf16[256,1152]{1,0:T(8,128)(2,1)S(1)}, u32[]{:S(2)}, u32[]{:S(2)}) collective-permute-start(bf16[256,1152]{1,0:T(8,128)(2,1)S(1)} %get-tuple-element.32.refs_0_), channel_id=1, source_target_pairs={{0,64},{32,97},{2,66},{34,99},{4,68},{36,101},{6,70},{38,103},{64,... | collective-permute-start | bytes 1769480 | tf_op jit(solution)/shard_map/ppermute | solution.py:48
  13.3 9.2 %collective-permute-start.4 = (bf16[256,1152]{1,0:T(8,128)(2,1)S(1)}, bf16[256,1152]{1,0:T(8,128)(2,1)S(1)}, u32[]{:S(2)}, u32[]{:S(2)}) collective-permute-start(bf16[256,1152]{1,0:T(8,128)(2,1)S(1)} %get-tuple-element.32.refs_0_), channel_id=1, source_target_pairs={{0,6},{32,34},{2,4},{34,32},{4,2},{36,38},{6,0},{38,36},{64,70},{9... | collective-permute-start | bytes 1769480 | tf_op jit(solution)/shard_map/ppermute | solution.py:48
  22.6 6.1 %collective-permute-start.8 = (bf16[768,1152]{1,0:T(8,128)(2,1)S(1)}, bf16[768,1152]{1,0:T(8,128)(2,1)S(1)}, u32[]{:S(2)}, u32[]{:S(2)}) collective-permute-start(bf16[768,1152]{1,0:T(8,128)(2,1)S(1)} %shard_map.70), channel_id=1, source_target_pairs={{0,32},{32,0},{1,33},{33,1},{2,34},{34,2},{3,35},{35,3},{4,36},{36... | collective-permute-start | bytes 5308424 | tf_op jit(solution)/shard_map/ppermute | solution.py:52
  23.7 11.4 %collective-permute-start.5 = (bf16[256,1152]{1,0:T(8,128)(2,1)S(1)}, bf16[256,1152]{1,0:T(8,128)(2,1)S(1)}, u32[]{:S(2)}, u32[]{:S(2)}) collective-permute-start(bf16[256,1152]{1,0:T(8,128)(2,1)S(1)} %collective-permute-done.2.refs_0_.refs_1_), channel_id=1, source_target_pairs={{0,64},{32,97},{2,66},{34,99},{4,68},{36,101},{6,70},{38,103},{64,... | collective-permute-start | bytes 1769480 | tf_op jit(solution)/shard_map/ppermute | solution.py:48
  25.6 9.5 %collective-permute-start.6 = (bf16[256,1152]{1,0:T(8,128)(2,1)S(1)}, bf16[256,1152]{1,0:T(8,128)(2,1)S(1)}, u32[]{:S(2)}, u32[]{:S(2)}) collective-permute-start(bf16[256,1152]{1,0:T(8,128)(2,1)S(1)} %collective-permute-done.3.refs_1_.refs_2_), channel_id=1, source_target_pairs={{0,6},{32,34},{2,4},{34,32},{4,2},{36,38},{6,0},{38,36},{64,70},{9... | collective-permute-start | bytes 1769480 | tf_op jit(solution)/shard_map/ppermute | solution.py:48
  25.6 9.9 %collective-permute-start.7 = (bf16[256,1152]{1,0:T(8,128)(2,1)S(1)}, bf16[256,1152]{1,0:T(8,128)(2,1)S(1)}, u32[]{:S(2)}, u32[]{:S(2)}) collective-permute-start(bf16[256,1152]{1,0:T(8,128)(2,1)S(1)} %collective-permute-done.4.refs_2_.refs_3_), channel_id=1, source_target_pairs={{0,8},{32,56},{2,10},{34,58},{4,12},{36,60},{6,14},{38,62},{64,72}... | collective-permute-start | bytes 1769480 | tf_op jit(solution)/shard_map/ppermute | solution.py:48
  35.7 6.8 %collective-permute-start.9 = (bf16[768,1152]{1,0:T(8,128)(2,1)S(1)}, bf16[768,1152]{1,0:T(8,128)(2,1)S(1)}, u32[]{:S(2)}, u32[]{:S(2)}) collective-permute-start(bf16[768,1152]{1,0:T(8,128)(2,1)S(1)} %shard_map.72), channel_id=1, source_target_pairs={{0,32},{32,0},{1,33},{33,1},{2,34},{34,2},{3,35},{35,3},{4,36},{36... | collective-permute-start | bytes 5308424 | tf_op jit(solution)/shard_map/ppermute | solution.py:52
  37.6 9.1 %collective-permute-start.10 = (bf16[256,1152]{1,0:T(8,128)(2,1)S(1)}, bf16[256,1152]{1,0:T(8,128)(2,1)S(1)}, u32[]{:S(2)}, u32[]{:S(2)}) collective-permute-start(bf16[256,1152]{1,0:T(8,128)(2,1)S(1)} %collective-permute-done.5.refs_0_.refs_1_), channel_id=1, source_target_pairs={{0,6},{32,34},{2,4},{34,32},{4,2},{36,38},{6,0},{38,36},{64,70},{9... | collective-permute-start | bytes 1769480 | tf_op jit(solution)/shard_map/ppermute | solution.py:48
  46.7 5.5 %collective-permute-start.11 = (bf16[256,1152]{1,0:T(8,128)(2,1)S(1)}, bf16[256,1152]{1,0:T(8,128)(2,1)S(1)}, u32[]{:S(2)}, u32[]{:S(2)}) collective-permute-start(bf16[256,1152]{1,0:T(8,128)(2,1)S(1)} %shard_map.75), channel_id=1, source_target_pairs={{0,32},{32,0},{1,33},{33,1},{2,34},{34,2},{3,35},{35,3},{4,36},{36... | collective-permute-start | bytes 1769480 | tf_op jit(solution)/shard_map/ppermute | solution.py:52
  55.1 12.1 %collective-permute-start.17 = (bf16[256,1152]{1,0:T(8,128)(2,1)S(1)}, bf16[256,1152]{1,0:T(8,128)(2,1)S(1)}, u32[]{:S(2)}, u32[]{:S(2)}) collective-permute-start(bf16[256,1152]{1,0:T(8,128)(2,1)S(1)} %get-tuple-element.51), channel_id=1, source_target_pairs={{0,8},{32,56},{2,10},{34,58},{4,12},{36,60},{6,14},{38,62},{64,72}... | collective-permute-start | bytes 1769480 | tf_op jit(solution)/shard_map/ppermute | solution.py:48
  57.0 15.3 %collective-permute-start.15 = (bf16[256,1152]{1,0:T(8,128)(2,1)S(1)}, bf16[256,1152]{1,0:T(8,128)(2,1)S(1)}, u32[]{:S(2)}, u32[]{:S(2)}) collective-permute-start(bf16[256,1152]{1,0:T(8,128)(2,1)S(1)} %get-tuple-element.49), channel_id=1, source_target_pairs={{0,6},{32,34},{2,4},{34,32},{4,2},{36,38},{6,0},{38,36},{64,70},{9... | collective-permute-start | bytes 1769480 | tf_op jit(solution)/shard_map/ppermute | solution.py:48
  57.5 17.8 %collective-permute-start.12 = (bf16[256,1152]{1,0:T(8,128)(2,1)S(1)}, bf16[256,1152]{1,0:T(8,128)(2,1)S(1)}, u32[]{:S(2)}, u32[]{:S(2)}) collective-permute-start(bf16[256,1152]{1,0:T(8,128)(2,1)S(1)} %get-tuple-element.44.refs_10_), channel_id=1, source_target_pairs={{0,70},{32,99},{2,68},{34,97},{4,66},{36,103},{6,64},{38,101},{64,... | collective-permute-start | bytes 1769480 | tf_op jit(solution)/shard_map/ppermute | solution.py:48
  60.9 14.4 %collective-permute-start.13 = (bf16[256,1152]{1,0:T(8,128)(2,1)S(1)}, bf16[256,1152]{1,0:T(8,128)(2,1)S(1)}, u32[]{:S(2)}, u32[]{:S(2)}) collective-permute-start(bf16[256,1152]{1,0:T(8,128)(2,1)S(1)} %get-tuple-element.47), channel_id=1, source_target_pairs={{0,64},{32,97},{2,66},{34,99},{4,68},{36,101},{6,70},{38,103},{64,... | collective-permute-start | bytes 1769480 | tf_op jit(solution)/shard_map/ppermute | solution.py:48
  67.3 11.3 %collective-permute-start.18 = (bf16[256,1152]{1,0:T(8,128)(2,1)S(1)}, bf16[256,1152]{1,0:T(8,128)(2,1)S(1)}, u32[]{:S(2)}, u32[]{:S(2)}) collective-permute-start(bf16[256,1152]{1,0:T(8,128)(2,1)S(1)} %shard_map.81), channel_id=1, source_target_pairs={{0,6},{32,34},{2,4},{34,32},{4,2},{36,38},{6,0},{38,36},{64,70},{9... | collective-permute-start | bytes 1769480 | tf_op jit(solution)/shard_map/ppermute | solution.py:48
  72.5 10.1 %collective-permute-start.16 = (bf16[256,1152]{1,0:T(8,128)(2,1)S(1)}, bf16[256,1152]{1,0:T(8,128)(2,1)S(1)}, u32[]{:S(2)}, u32[]{:S(2)}) collective-permute-start(bf16[256,1152]{1,0:T(8,128)(2,1)S(1)} %shard_map.80), channel_id=1, source_target_pairs={{0,64},{32,97},{2,66},{34,99},{4,68},{36,101},{6,70},{38,103},{64,... | collective-permute-start | bytes 1769480 | tf_op jit(solution)/shard_map/ppermute | solution.py:48
  75.5 10.0 %collective-permute-start.14 = (bf16[256,1152]{1,0:T(8,128)(2,1)S(1)}, bf16[256,1152]{1,0:T(8,128)(2,1)S(1)}, u32[]{:S(2)}, u32[]{:S(2)}) collective-permute-start(bf16[256,1152]{1,0:T(8,128)(2,1)S(1)} %shard_map.79), channel_id=1, source_target_pairs={{0,8},{32,56},{2,10},{34,58},{4,12},{36,60},{6,14},{38,62},{64,72}... | collective-permute-start | bytes 1769480 | tf_op jit(solution)/shard_map/ppermute | solution.py:48
  86.3 2.1 %collective-permute-start.19 = (f32[128,1152]{1,0:T(8,128)S(1)}, f32[128,1152]{1,0:T(8,128)S(1)}, u32[]{:S(2)}, u32[]{:S(2)}) collective-permute-start(f32[128,1152]{1,0:T(8,128)S(1)} %get-tuple-element.53), channel_id=1, source_target_pairs={{0,32},{32,0},{1,33},{33,1},{2,34},{34,2},{3,35},{35,3},{4,36},{36... | collective-permute-start | bytes 1769480 | tf_op jit(solution)/shard_map/ppermute | solution.py:52

commit v9 on v7

--- a/solution.py
+++ b/solution.py
@@ -23,7 +23,8 @@
 PARAMS = pltpu.CompilerParams(vmem_limit_bytes=VMEM_BYTES)
 
 ONE = ("x", "y", "z")
-TWO = ("xyz", "xy", "yz", "zx")
+TWO = ("xy", "yz", "zx")
+CORNER = "xyz"
 
 
 def place(core, x, y, z):
@@ -201,29 +202,32 @@
     mine = {"": own}
     for way in ONE:
         mine[way] = sent(own, way)
-    mine["xyz"] = sent(mine["x"], "yz")
+    mine[CORNER] = sent(own, CORNER)
     mine["xy"] = sent(mine["x"], "y")
     mine["yz"] = sent(mine["y"], "z")
     mine["zx"] = sent(mine["z"], "x")
     def pick(units, ways):
         return [units[way] for way in ways]
 
-    theirs_one = [own_theirs, stacked(ONE)]
-    near = ("", *ONE)
-    sums = sums_of(affine, pick(mine, near), theirs_one, diagonal=True, hides=False)
-    theirs_two = [stacked(TWO, sums[:1])]
-    sums += sums_of(affine, pick(mine, TWO), theirs_one)
-    sums = dict(zip((*near, *TWO), sums, strict=True))
-
-    def parts_of(ways, kinds, after=()):
-        return sums_of(affine, pick(mine, ways), theirs_two, pick(sums, ways), after, kinds)
-
-    part_xyz, part_xy = parts_of(("xyz", "xy"), [HALF, HALF])
-    for_x = [sent(part_xyz, "yz"), sent(part_xy, "y")]
-    part_yz, part_zx = parts_of(("yz", "zx"), [HALF, HALF], [part_xy])
-    for_y = [sent(part_yz, "z")]
-    for_z = [sent(part_zx, "x")]
-    own_part, part_x, part_y, part_z = parts_of(near, [FULL] * 4, [part_zx])
+    first = (*ONE, CORNER)
+    theirs_one = [own_theirs, stacked(first)]
+    *sums_near, sum_corner = sums_of(
+        affine, pick(mine, ("", *first)), theirs_one, diagonal=True, hides=False
+    )
+    theirs_two = [stacked(TWO, sums_near[:1])]
+    sums_two = sums_of(affine, pick(mine, TWO), theirs_one)
+
+    part_xy, part_yz, part_zx = sums_of(
+        affine, pick(mine, TWO), theirs_two, sums_two, kinds=[HALF] * 3
+    )
+    for_x, for_y, for_z = sent(part_xy, "y"), sent(part_yz, "z"), sent(part_zx, "x")
+    (part_xyz,) = sums_of(
+        affine, [mine[CORNER]], theirs_two, [sum_corner], after=[part_xy], kinds=[HALF]
+    )
+    arrived = [sent(part_xyz, CORNER)]
+    part_x, part_y, part_z = sums_of(
+        affine, pick(mine, ONE), theirs_two, sums_near[1:], after=[part_xyz]
+    )
 
     def with_added(part, added, way):
         (total,) = local(
@@ -234,11 +238,10 @@
         )
         return sent(total, way)
 
-    arrived = [
-        with_added(part_x, for_x, "x"),
-        with_added(part_y, for_y, "y"),
-        with_added(part_z, for_z, "z"),
-    ]
+    arrived.append(with_added(part_x, [for_x], "x"))
+    arrived.append(with_added(part_y, [for_y], "y"))
+    arrived.append(with_added(part_z, [for_z], "z"))
+    (own_part,) = sums_of(affine, [own], theirs_two, sums_near[:1], after=[part_z])
 
     here, there = pl.pallas_call(
         finish_kernel,

time: 84.9 us -> 85.8 us (1.011)
  Pallas kernels: 28.1 us -> 30.2 us
  waiting for transfers between devices: 20.4 us -> 19.5 us
    ppermute x5, starting transfers between devices: 6.2 us -> 3.51 us  [other_core(): return lax.ppermute(value, 'core', [(0, 1), (1, 0)])]
    ppermute x14, starting transfers between devices: 24.1 us -> 26.6 us  [sent(): return lax.ppermute(value, FINE_AXES, pairs)]
    pallas_call x5 -> x6, Pallas kernels: 25.9 us -> 27.9 us  [sums_of(): pl.pallas_call(functools.partial(sums_kernel, count, n_theirs, n_starts,...]
    ppermute x14, waiting for transfers between devices: 18.8 us -> 17.8 us  [sent(): return lax.ppermute(value, FINE_AXES, pairs)]
  transfers between devices with their start and end apart: 19 -> 19, of which waited for: 10 -> 6; matrix products, arithmetic and copies ran while one was open for 0% -> 0% of each run, Pallas kernels for 27% -> 28%
where the time goes in v9:
time: 85.8 us; the launch traced here: 85.6 us
  Pallas kernels  30.2 us (35%)
  starting transfers between devices  30.1 us (35%)
  waiting for transfers between devices  19.5 us (23%)
  between operations  2.73 us (3%)
  local copies, waits for them, and re-layouts  1.92 us (2%)
  other arithmetic  1.16 us (1%)
    pallas_call x6, Pallas kernels, sums_of(): pl.pallas_call(functools.partial(sums_kernel, count, n_theirs, n_starts,...  27.9 us
    ppermute x14, starting transfers between devices, sent(): return lax.ppermute(value, FINE_AXES, pairs)  26.6 us
    ppermute x14, waiting for transfers between devices, sent(): return lax.ppermute(value, FINE_AXES, pairs)  17.8 us
    ppermute x5, starting transfers between devices, other_core(): return lax.ppermute(value, 'core', [(0, 1), (1, 0)])  3.51 us
    unnamed x4, local copies, waits for them, and re-layouts  1.92 us
  transfers between devices with their start and end apart: 19, of which 6 were waited for; matrix products, arithmetic and copies ran while one was open for 0% of the time, Pallas kernels for 28%

profile of v9, /device:TPU:1, one launch (start us, length us, event | category | flops | bytes accessed | tf_op | source)
XLA Modules:
  0.0 85.6 jit_solution(7990444720558719670)
XLA Ops:
  0.6 1.5 %collective-permute-start = (bf16[128,1152]{1,0:T(8,128)(2,1)}, bf16[128,1152]{1,0:T(8,128)(2,1)S(1)}, u32[]{:S(2)}, u32[]{:S(2)}) collective-permute-start(bf16[128,1152]{1,0:T(8,128)(2,1)} %refs_1_.1), channel_id=1, source_target_pairs={{0,32},{32,0},{1,33},{33,1},{2,34},{34,2},{3,35},{35,3},{4,36},{36... | collective-permute-start | bytes 884744 | tf_op jit(solution)/shard_map/ppermute | solution.py:50
  2.1 0.1 collective-permute-start.1
  2.2 1.0 %copy-done = bf16[128,1152]{1,0:T(8,128)(2,1)S(1)} copy-done((bf16[128,1152]{1,0:T(8,128)(2,1)S(1)}, bf16[128,1152]{1,0:T(8,128)(2,1)}, u32[]{:S(2)}) %copy-start) | copy-done | bytes 294936
  3.2 1.0 %copy-done.1 = bf16[128,1152]{1,0:T(8,128)(2,1)S(1)} copy-done((bf16[128,1152]{1,0:T(8,128)(2,1)S(1)}, bf16[128,1152]{1,0:T(8,128)(2,1)}, u32[]{:S(2)}) %copy-start.1) | copy-done | bytes 294936
  4.1 0.2 shard_map.68
  4.4 0.5 shard_map.69
  4.9 6.4 %collective-permute-start.8 = (bf16[256,1152]{1,0:T(8,128)(2,1)S(1)}, bf16[256,1152]{1,0:T(8,128)(2,1)S(1)}, u32[]{:S(2)}, u32[]{:S(2)}) collective-permute-start(bf16[256,1152]{1,0:T(8,128)(2,1)S(1)} %get-tuple-element.28.refs_0_), channel_id=1, source_target_pairs={{0,78},{32,123},{2,76},{34,121},{4,74},{36,127},{6,72},{38,125},{6... | collective-permute-start | bytes 1769480 | tf_op jit(solution)/shard_map/ppermute | solution.py:46
  11.4 0.0 collective-permute-start.6
  11.4 0.0 collective-permute-start.4
  11.4 0.7 collective-permute-start.2
  12.0 6.8 %collective-permute-done.8.refs_3_.refs_4_.refs_0_ = bf16[256,1152]{1,0:T(8,128)(2,1)S(1)} collective-permute-done((bf16[256,1152]{1,0:T(8,128)(2,1)S(1)}, bf16[256,1152]{1,0:T(8,128)(2,1)S(1)}, u32[]{:S(2)}, u32[]{:S(2)}) %collective-permute-start.8) | collective-permute-done | bytes 589856 | tf_op jit(solution)/shard_map/ppermute | solution.py:46
  18.8 6.5 %collective-permute-done.6.refs_2_.refs_3_ = bf16[256,1152]{1,0:T(8,128)(2,1)S(1)} collective-permute-done((bf16[256,1152]{1,0:T(8,128)(2,1)S(1)}, bf16[256,1152]{1,0:T(8,128)(2,1)S(1)}, u32[]{:S(2)}, u32[]{:S(2)}) %collective-permute-start.6) | collective-permute-done | bytes 589856 | tf_op jit(solution)/shard_map/ppermute | solution.py:46
  25.2 0.0 collective-permute-done.4.refs_1_.refs_2_
  25.2 0.0 collective-permute-done.2.refs_0_.refs_1_
  25.3 0.2 shard_map.70
  25.4 1.0 %collective-permute-start.9 = (bf16[1024,1152]{1,0:T(8,128)(2,1)S(1)}, bf16[1024,1152]{1,0:T(8,128)(2,1)S(1)}, u32[]{:S(2)}, u32[]{:S(2)}) collective-permute-start(bf16[1024,1152]{1,0:T(8,128)(2,1)S(1)} %shard_map.70), channel_id=1, source_target_pairs={{0,32},{32,0},{1,33},{33,1},{2,34},{34,2},{3,35},{35,3},{4,36},{36... | collective-permute-start | bytes 7077896 | tf_op jit(solution)/shard_map/ppermute | solution.py:50
  26.5 2.5 %collective-permute-start.7 = (bf16[256,1152]{1,0:T(8,128)(2,1)S(1)}, bf16[256,1152]{1,0:T(8,128)(2,1)S(1)}, u32[]{:S(2)}, u32[]{:S(2)}) collective-permute-start(bf16[256,1152]{1,0:T(8,128)(2,1)S(1)} %collective-permute-done.6.refs_2_.refs_3_), channel_id=1, source_target_pairs={{0,8},{32,56},{2,10},{34,58},{4,12},{36,60},{6,14},{38,62},{64,72}... | collective-permute-start | bytes 1769480 | tf_op jit(solution)/shard_map/ppermute | solution.py:46
  29.0 2.6 %collective-permute-start.3 = (bf16[256,1152]{1,0:T(8,128)(2,1)S(1)}, bf16[256,1152]{1,0:T(8,128)(2,1)S(1)}, u32[]{:S(2)}, u32[]{:S(2)}) collective-permute-start(bf16[256,1152]{1,0:T(8,128)(2,1)S(1)} %collective-permute-done.2.refs_0_.refs_1_), channel_id=1, source_target_pairs={{0,64},{32,97},{2,66},{34,99},{4,68},{36,101},{6,70},{38,103},{64,... | collective-permute-start | bytes 1769480 | tf_op jit(solution)/shard_map/ppermute | solution.py:46
  32.8 0.1 pad_maximum_fusion.affine
  32.9 9.5 %shard_map.71 = (f32[256,1152]{1,0:T(8,128)S(1)}, f32[256,1152]{1,0:T(8,128)S(1)}, f32[256,1152]{1,0:T(8,128)S(1)}, f32[256,1152]{1,0:T(8,128)S(1)}, f32[256,1152]{1,0:T(8,128)S(1)}) custom-call(f32[2]{0:T(128)S(1)} %pad_maximum_fusion.affine, bf16[256,1152]{1,0:T(8,128)(2,1)S(1)} %get-tuple-element.28.refs_0_, ...), custom_call_target="tpu_custom_call" | custom-call | tf_op jit(solution)/shard_map/pallas_call | solution.py:119
  42.5 0.0 collective-permute-done.3.refs_0_
  42.5 0.1 shard_map.72
  42.6 0.3 collective-permute-start.10
  42.9 6.1 %shard_map.73 = (f32[256,1152]{1,0:T(8,128)S(1)}, f32[256,1152]{1,0:T(8,128)S(1)}, f32[256,1152]{1,0:T(8,128)S(1)}) custom-call(f32[2]{0:T(128)S(1)} %pad_maximum_fusion.affine, bf16[256,1152]{1,0:T(8,128)(2,1)S(1)} %collective-permute-done.3.refs_0_, bf16[256,1152]{1,0:T(8,128)(2,1)S(1)} %collective-permute-done.5.refs_1_, ...), custom_call_target="tpu_custom_call" | custom-call | flops 4529848320 | bytes 7077888 | tf_op jit(solution)/shard_map/pallas_call | solution.py:119
  49.0 0.0 collective-permute-done.10.refs_3_.refs_1_
  49.0 4.1 %shard_map.74 = (bf16[256,1152]{1,0:T(8,128)(2,1)S(1)}, bf16[256,1152]{1,0:T(8,128)(2,1)S(1)}, bf16[256,1152]{1,0:T(8,128)(2,1)S(1)}) custom-call(f32[2]{0:T(128)S(1)} %pad_maximum_fusion.affine, bf16[256,1152]{1,0:T(8,128)(2,1)S(1)} %collective-permute-done.3.refs_0_, bf16[256,1152]{1,0:T(8,128)(2,1)S(1)} %collective-permute-done.5.refs_1_, ...), custom_call_target="tpu_custom_call" | custom-call | flops 2717908992 | bytes 7077888 | tf_op jit(solution)/shard_map/pallas_call | solution.py:119
  53.1 1.6 %collective-permute-start.14 = (bf16[256,1152]{1,0:T(8,128)(2,1)S(1)}, bf16[256,1152]{1,0:T(8,128)(2,1)S(1)}, u32[]{:S(2)}, u32[]{:S(2)}) collective-permute-start(bf16[256,1152]{1,0:T(8,128)(2,1)S(1)} %get-tuple-element.42), channel_id=1, source_target_pairs={{0,6},{32,34},{2,4},{34,32},{4,2},{36,38},{6,0},{38,36},{64,70},{9... | collective-permute-start | bytes 1769480 | tf_op jit(solution)/shard_map/ppermute | solution.py:46
  54.7 0.2 collective-permute-start.16
  54.8 2.3 %collective-permute-start.12 = (bf16[256,1152]{1,0:T(8,128)(2,1)S(1)}, bf16[256,1152]{1,0:T(8,128)(2,1)S(1)}, u32[]{:S(2)}, u32[]{:S(2)}) collective-permute-start(bf16[256,1152]{1,0:T(8,128)(2,1)S(1)} %get-tuple-element.38.refs_3_), channel_id=1, source_target_pairs={{0,64},{32,97},{2,66},{34,99},{4,68},{36,101},{6,70},{38,103},{64,... | collective-permute-start | bytes 1769480 | tf_op jit(solution)/shard_map/ppermute | solution.py:46
  57.2 2.0 %shard_map.75.refs_7_ = bf16[256,1152]{1,0:T(8,128)(2,1)S(1)} custom-call(f32[2]{0:T(128)S(1)} %pad_maximum_fusion.affine, bf16[256,1152]{1,0:T(8,128)(2,1)S(1)} %collective-permute-done.8.refs_3_.refs_4_.refs_0_, bf16[768,1152]{1,0:T(8,128)(2,1)S(1)} %collective-permute-done.10.refs_3_.refs_1_, f32[256,1152]{1,0:T(8,128)S(1)} %get-tuple-element.34.refs_2_, ...), custom_call_target="tpu_custom_call" | custom-call | flops 905969664 | bytes 2359296 | tf_op jit(solution)/shard_map/pallas_call | solution.py:119
  59.2 2.7 %collective-permute-start.11 = (bf16[256,1152]{1,0:T(8,128)(2,1)S(1)}, bf16[256,1152]{1,0:T(8,128)(2,1)S(1)}, u32[]{:S(2)}, u32[]{:S(2)}) collective-permute-start(bf16[256,1152]{1,0:T(8,128)(2,1)S(1)} %shard_map.75.refs_7_), channel_id=1, source_target_pairs={{0,78},{32,123},{2,76},{34,121},{4,74},{36,127},{6,72},{38,125},{6... | collective-permute-start | bytes 1769480 | tf_op jit(solution)/shard_map/ppermute | solution.py:46
  61.9 4.2 %shard_map.76 = (f32[256,1152]{1,0:T(8,128)S(1)}, f32[256,1152]{1,0:T(8,128)S(1)}, f32[256,1152]{1,0:T(8,128)S(1)}) custom-call(f32[2]{0:T(128)S(1)} %pad_maximum_fusion.affine, bf16[256,1152]{1,0:T(8,128)(2,1)S(1)} %collective-permute-done.2.refs_0_.refs_1_, bf16[256,1152]{1,0:T(8,128)(2,1)S(1)} %collective-permute-done.4.refs_1_.refs_2_, ...), custom_call_target="tpu_custom_call" | custom-call | flops 2717908992 | bytes 7077888 | tf_op jit(solution)/shard_map/pallas_call | solution.py:119
  66.0 0.0 collective-permute-done.14.refs_1_
  66.0 0.1 shard_map.79
  66.2 1.4 %collective-permute-start.15 = (bf16[256,1152]{1,0:T(8,128)(2,1)S(1)}, bf16[256,1152]{1,0:T(8,128)(2,1)S(1)}, u32[]{:S(2)}, u32[]{:S(2)}) collective-permute-start(bf16[256,1152]{1,0:T(8,128)(2,1)S(1)} %shard_map.79), channel_id=1, source_target_pairs={{0,64},{32,97},{2,66},{34,99},{4,68},{36,101},{6,70},{38,103},{64,... | collective-permute-start | bytes 1769480 | tf_op jit(solution)/shard_map/ppermute | solution.py:46
  67.6 0.0 collective-permute-done.16.refs_1_
  67.6 0.1 shard_map.80
  67.7 0.2 collective-permute-start.17
  67.9 0.1 shard_map.78
  68.0 6.1 %collective-permute-start.13 = (bf16[256,1152]{1,0:T(8,128)(2,1)S(1)}, bf16[256,1152]{1,0:T(8,128)(2,1)S(1)}, u32[]{:S(2)}, u32[]{:S(2)}) collective-permute-start(bf16[256,1152]{1,0:T(8,128)(2,1)S(1)} %shard_map.78), channel_id=1, source_target_pairs={{0,8},{32,56},{2,10},{34,58},{4,12},{36,60},{6,14},{38,62},{64,72}... | collective-permute-start | bytes 1769480 | tf_op jit(solution)/shard_map/ppermute | solution.py:46
  74.7 2.0 %shard_map.77.refs_0_ = f32[256,1152]{1,0:T(8,128)S(1)} custom-call(f32[2]{0:T(128)S(1)} %pad_maximum_fusion.affine, bf16[256,1152]{1,0:T(8,128)(2,1)S(1)} %get-tuple-element.28.refs_0_, bf16[768,1152]{1,0:T(8,128)(2,1)S(1)} %collective-permute-done.10.refs_3_.refs_1_, f32[256,1152]{1,0:T(8,128)S(1)} %get-tuple-element.30.refs_3_.refs_2_, ...), custom_call_target="tpu_custom_call" | custom-call | flops 905969664 | bytes 2359296 | tf_op jit(solution)/shard_map/pallas_call | solution.py:119
  76.8 2.2 %collective-permute-done.15.refs_3_ = bf16[256,1152]{1,0:T(8,128)(2,1)S(1)} collective-permute-done((bf16[256,1152]{1,0:T(8,128)(2,1)S(1)}, bf16[256,1152]{1,0:T(8,128)(2,1)S(1)}, u32[]{:S(2)}, u32[]{:S(2)}) %collective-permute-start.15) | collective-permute-done | bytes 589856 | tf_op jit(solution)/shard_map/ppermute | solution.py:46
  79.0 0.1 collective-permute-done.17.refs_4_
  79.1 2.3 %collective-permute-done.13.refs_2_ = bf16[256,1152]{1,0:T(8,128)(2,1)S(1)} collective-permute-done((bf16[256,1152]{1,0:T(8,128)(2,1)S(1)}, bf16[256,1152]{1,0:T(8,128)(2,1)S(1)}, u32[]{:S(2)}, u32[]{:S(2)}) %collective-permute-start.13) | collective-permute-done | bytes 589856 | tf_op jit(solution)/shard_map/ppermute | solution.py:46
  81.4 0.9 %shard_map.81 = (f32[128,1152]{1,0:T(8,128)S(1)}, f32[128,1152]{1,0:T(8,128)S(1)}) custom-call(s32[1]{0:T(128)} %bitcast.core, f32[1]{0:T(128)S(6)} %div.3.multiplier, bf16[256,1152]{1,0:T(8,128)(2,1)S(1)} %get-tuple-element.27.raw, f32[256,1152]{1,0:T(8,128)S(1)} %shard_map.77.refs_0_, bf16[256,1152]{1,0:T(8,128)(2,1)S(1)} %collective-permute-done.11.refs_1_, ...), custom_call_target="tpu_custom_call" | custom-call | tf_op jit(solution)/shard_map/pallas_call | solution.py:246
  82.3 0.6 collective-permute-start.18
  82.9 1.6 %collective-permute-done.18 = f32[128,1152]{1,0:T(8,128)S(1)} collective-permute-done((f32[128,1152]{1,0:T(8,128)S(1)}, f32[128,1152]{1,0:T(8,128)S(1)}, u32[]{:S(2)}, u32[]{:S(2)}) %collective-permute-start.18) | collective-permute-done | bytes 589856 | tf_op jit(solution)/shard_map/ppermute | solution.py:50
  84.5 1.1 %broadcast_select_fusion = (f32[128,1152]{1,0:T(8,128)}, f32[128,1152]{1,0:T(8,128)}) fusion(f32[128,1152]{1,0:T(8,128)S(1)} %collective-permute-done.18, f32[128,1152]{1,0:T(8,128)S(1)} %get-tuple-element.44, pred[]{:T(512)S(6)} %eq.3), kind=kLoop, calls=%fused_computation | loop fusion | flops 294912 | bytes 2359297 | tf_op jit(solution)/shard_map/jit(_where)/select_n | solution.py:255
  (10 shorter events, 0.0 us)
Async XLA Ops:
  0.6 3.8 %collective-permute-start = (bf16[128,1152]{1,0:T(8,128)(2,1)}, bf16[128,1152]{1,0:T(8,128)(2,1)S(1)}, u32[]{:S(2)}, u32[]{:S(2)}) collective-permute-start(bf16[128,1152]{1,0:T(8,128)(2,1)} %refs_1_.1), channel_id=1, source_target_pairs={{0,32},{32,0},{1,33},{33,1},{2,34},{34,2},{3,35},{35,3},{4,36},{36... | collective-permute-start | bytes 884744 | tf_op jit(solution)/shard_map/ppermute | solution.py:50
  2.1 2.3 %collective-permute-start.1 = (bf16[128,1152]{1,0:T(8,128)(2,1)}, bf16[128,1152]{1,0:T(8,128)(2,1)S(1)}, u32[]{:S(2)}, u32[]{:S(2)}) collective-permute-start(bf16[128,1152]{1,0:T(8,128)(2,1)} %refs_2_.1), channel_id=1, source_target_pairs={{0,32},{32,0},{1,33},{33,1},{2,34},{34,2},{3,35},{35,3},{4,36},{36... | collective-permute-start | bytes 884744 | tf_op jit(solution)/shard_map/ppermute | solution.py:50
  2.2 1.0 %copy-start = (bf16[128,1152]{1,0:T(8,128)(2,1)S(1)}, bf16[128,1152]{1,0:T(8,128)(2,1)}, u32[]{:S(2)}) copy-start(bf16[128,1152]{1,0:T(8,128)(2,1)} %refs_1_.1) | copy-start | bytes 884740
  3.2 1.0 %copy-start.1 = (bf16[128,1152]{1,0:T(8,128)(2,1)S(1)}, bf16[128,1152]{1,0:T(8,128)(2,1)}, u32[]{:S(2)}) copy-start(bf16[128,1152]{1,0:T(8,128)(2,1)} %refs_2_.1) | copy-start | bytes 884740
  4.9 13.9 %collective-permute-start.8 = (bf16[256,1152]{1,0:T(8,128)(2,1)S(1)}, bf16[256,1152]{1,0:T(8,128)(2,1)S(1)}, u32[]{:S(2)}, u32[]{:S(2)}) collective-permute-start(bf16[256,1152]{1,0:T(8,128)(2,1)S(1)} %get-tuple-element.28.refs_0_), channel_id=1, source_target_pairs={{0,78},{32,123},{2,76},{34,121},{4,74},{36,127},{6,72},{38,125},{6... | collective-permute-start | bytes 1769480 | tf_op jit(solution)/shard_map/ppermute | solution.py:46
  11.4 13.9 %collective-permute-start.6 = (bf16[256,1152]{1,0:T(8,128)(2,1)S(1)}, bf16[256,1152]{1,0:T(8,128)(2,1)S(1)}, u32[]{:S(2)}, u32[]{:S(2)}) collective-permute-start(bf16[256,1152]{1,0:T(8,128)(2,1)S(1)} %get-tuple-element.28.refs_0_), channel_id=1, source_target_pairs={{0,6},{32,34},{2,4},{34,32},{4,2},{36,38},{6,0},{38,36},{64,70},{9... | collective-permute-start | bytes 1769480 | tf_op jit(solution)/shard_map/ppermute | solution.py:46
  11.4 13.9 %collective-permute-start.4 = (bf16[256,1152]{1,0:T(8,128)(2,1)S(1)}, bf16[256,1152]{1,0:T(8,128)(2,1)S(1)}, u32[]{:S(2)}, u32[]{:S(2)}) collective-permute-start(bf16[256,1152]{1,0:T(8,128)(2,1)S(1)} %get-tuple-element.28.refs_0_), channel_id=1, source_target_pairs={{0,64},{32,97},{2,66},{34,99},{4,68},{36,101},{6,70},{38,103},{64,... | collective-permute-start | bytes 1769480 | tf_op jit(solution)/shard_map/ppermute | solution.py:46
  11.4 13.9 %collective-permute-start.2 = (bf16[256,1152]{1,0:T(8,128)(2,1)S(1)}, bf16[256,1152]{1,0:T(8,128)(2,1)S(1)}, u32[]{:S(2)}, u32[]{:S(2)}) collective-permute-start(bf16[256,1152]{1,0:T(8,128)(2,1)S(1)} %get-tuple-element.28.refs_0_), channel_id=1, source_target_pairs={{0,8},{32,56},{2,10},{34,58},{4,12},{36,60},{6,14},{38,62},{64,72}... | collective-permute-start | bytes 1769480 | tf_op jit(solution)/shard_map/ppermute | solution.py:46
  25.4 7.5 %collective-permute-start.9 = (bf16[1024,1152]{1,0:T(8,128)(2,1)S(1)}, bf16[1024,1152]{1,0:T(8,128)(2,1)S(1)}, u32[]{:S(2)}, u32[]{:S(2)}) collective-permute-start(bf16[1024,1152]{1,0:T(8,128)(2,1)S(1)} %shard_map.70), channel_id=1, source_target_pairs={{0,32},{32,0},{1,33},{33,1},{2,34},{34,2},{3,35},{35,3},{4,36},{36... | collective-permute-start | bytes 7077896 | tf_op jit(solution)/shard_map/ppermute | solution.py:50
  26.5 16.0 %collective-permute-start.7 = (bf16[256,1152]{1,0:T(8,128)(2,1)S(1)}, bf16[256,1152]{1,0:T(8,128)(2,1)S(1)}, u32[]{:S(2)}, u32[]{:S(2)}) collective-permute-start(bf16[256,1152]{1,0:T(8,128)(2,1)S(1)} %collective-permute-done.6.refs_2_.refs_3_), channel_id=1, source_target_pairs={{0,8},{32,56},{2,10},{34,58},{4,12},{36,60},{6,14},{38,62},{64,72}... | collective-permute-start | bytes 1769480 | tf_op jit(solution)/shard_map/ppermute | solution.py:46
  29.0 13.5 %collective-permute-start.5 = (bf16[256,1152]{1,0:T(8,128)(2,1)S(1)}, bf16[256,1152]{1,0:T(8,128)(2,1)S(1)}, u32[]{:S(2)}, u32[]{:S(2)}) collective-permute-start(bf16[256,1152]{1,0:T(8,128)(2,1)S(1)} %collective-permute-done.4.refs_1_.refs_2_), channel_id=1, source_target_pairs={{0,6},{32,34},{2,4},{34,32},{4,2},{36,38},{6,0},{38,36},{64,70},{9... | collective-permute-start | bytes 1769480 | tf_op jit(solution)/shard_map/ppermute | solution.py:46
  29.0 13.5 %collective-permute-start.3 = (bf16[256,1152]{1,0:T(8,128)(2,1)S(1)}, bf16[256,1152]{1,0:T(8,128)(2,1)S(1)}, u32[]{:S(2)}, u32[]{:S(2)}) collective-permute-start(bf16[256,1152]{1,0:T(8,128)(2,1)S(1)} %collective-permute-done.2.refs_0_.refs_1_), channel_id=1, source_target_pairs={{0,64},{32,97},{2,66},{34,99},{4,68},{36,101},{6,70},{38,103},{64,... | collective-permute-start | bytes 1769480 | tf_op jit(solution)/shard_map/ppermute | solution.py:46
  42.6 6.4 %collective-permute-start.10 = (bf16[768,1152]{1,0:T(8,128)(2,1)S(1)}, bf16[768,1152]{1,0:T(8,128)(2,1)S(1)}, u32[]{:S(2)}, u32[]{:S(2)}) collective-permute-start(bf16[768,1152]{1,0:T(8,128)(2,1)S(1)} %shard_map.72), channel_id=1, source_target_pairs={{0,32},{32,0},{1,33},{33,1},{2,34},{34,2},{3,35},{35,3},{4,36},{36... | collective-permute-start | bytes 5308424 | tf_op jit(solution)/shard_map/ppermute | solution.py:50
  53.1 12.9 %collective-permute-start.14 = (bf16[256,1152]{1,0:T(8,128)(2,1)S(1)}, bf16[256,1152]{1,0:T(8,128)(2,1)S(1)}, u32[]{:S(2)}, u32[]{:S(2)}) collective-permute-start(bf16[256,1152]{1,0:T(8,128)(2,1)S(1)} %get-tuple-element.42), channel_id=1, source_target_pairs={{0,6},{32,34},{2,4},{34,32},{4,2},{36,38},{6,0},{38,36},{64,70},{9... | collective-permute-start | bytes 1769480 | tf_op jit(solution)/shard_map/ppermute | solution.py:46
  54.7 12.9 %collective-permute-start.16 = (bf16[256,1152]{1,0:T(8,128)(2,1)S(1)}, bf16[256,1152]{1,0:T(8,128)(2,1)S(1)}, u32[]{:S(2)}, u32[]{:S(2)}) collective-permute-start(bf16[256,1152]{1,0:T(8,128)(2,1)S(1)} %get-tuple-element.43), channel_id=1, source_target_pairs={{0,8},{32,56},{2,10},{34,58},{4,12},{36,60},{6,14},{38,62},{64,72}... | collective-permute-start | bytes 1769480 | tf_op jit(solution)/shard_map/ppermute | solution.py:46
  54.8 13.1 %collective-permute-start.12 = (bf16[256,1152]{1,0:T(8,128)(2,1)S(1)}, bf16[256,1152]{1,0:T(8,128)(2,1)S(1)}, u32[]{:S(2)}, u32[]{:S(2)}) collective-permute-start(bf16[256,1152]{1,0:T(8,128)(2,1)S(1)} %get-tuple-element.38.refs_3_), channel_id=1, source_target_pairs={{0,64},{32,97},{2,66},{34,99},{4,68},{36,101},{6,70},{38,103},{64,... | collective-permute-start | bytes 1769480 | tf_op jit(solution)/shard_map/ppermute | solution.py:46
  59.2 17.6 %collective-permute-start.11 = (bf16[256,1152]{1,0:T(8,128)(2,1)S(1)}, bf16[256,1152]{1,0:T(8,128)(2,1)S(1)}, u32[]{:S(2)}, u32[]{:S(2)}) collective-permute-start(bf16[256,1152]{1,0:T(8,128)(2,1)S(1)} %shard_map.75.refs_7_), channel_id=1, source_target_pairs={{0,78},{32,123},{2,76},{34,121},{4,74},{36,127},{6,72},{38,125},{6... | collective-permute-start | bytes 1769480 | tf_op jit(solution)/shard_map/ppermute | solution.py:46
  66.2 12.8 %collective-permute-start.15 = (bf16[256,1152]{1,0:T(8,128)(2,1)S(1)}, bf16[256,1152]{1,0:T(8,128)(2,1)S(1)}, u32[]{:S(2)}, u32[]{:S(2)}) collective-permute-start(bf16[256,1152]{1,0:T(8,128)(2,1)S(1)} %shard_map.79), channel_id=1, source_target_pairs={{0,64},{32,97},{2,66},{34,99},{4,68},{36,101},{6,70},{38,103},{64,... | collective-permute-start | bytes 1769480 | tf_op jit(solution)/shard_map/ppermute | solution.py:46
  67.7 11.4 %collective-permute-start.17 = (bf16[256,1152]{1,0:T(8,128)(2,1)S(1)}, bf16[256,1152]{1,0:T(8,128)(2,1)S(1)}, u32[]{:S(2)}, u32[]{:S(2)}) collective-permute-start(bf16[256,1152]{1,0:T(8,128)(2,1)S(1)} %shard_map.80), channel_id=1, source_target_pairs={{0,6},{32,34},{2,4},{34,32},{4,2},{36,38},{6,0},{38,36},{64,70},{9... | collective-permute-start | bytes 1769480 | tf_op jit(solution)/shard_map/ppermute | solution.py:46
  68.0 13.3 %collective-permute-start.13 = (bf16[256,1152]{1,0:T(8,128)(2,1)S(1)}, bf16[256,1152]{1,0:T(8,128)(2,1)S(1)}, u32[]{:S(2)}, u32[]{:S(2)}) collective-permute-start(bf16[256,1152]{1,0:T(8,128)(2,1)S(1)} %shard_map.78), channel_id=1, source_target_pairs={{0,8},{32,56},{2,10},{34,58},{4,12},{36,60},{6,14},{38,62},{64,72}... | collective-permute-start | bytes 1769480 | tf_op jit(solution)/shard_map/ppermute | solution.py:46
  82.3 2.2 %collective-permute-start.18 = (f32[128,1152]{1,0:T(8,128)S(1)}, f32[128,1152]{1,0:T(8,128)S(1)}, u32[]{:S(2)}, u32[]{:S(2)}) collective-permute-start(f32[128,1152]{1,0:T(8,128)S(1)} %get-tuple-element.45), channel_id=1, source_target_pairs={{0,32},{32,0},{1,33},{33,1},{2,34},{34,2},{3,35},{35,3},{4,36},{36... | collective-permute-start | bytes 1769480 | tf_op jit(solution)/shard_map/ppermute | solution.py:50

commit v10 on v9

--- a/solution.py
+++ b/solution.py
@@ -202,31 +202,33 @@
     mine = {"": own}
     for way in ONE:
         mine[way] = sent(own, way)
-    mine[CORNER] = sent(own, CORNER)
     mine["xy"] = sent(mine["x"], "y")
     mine["yz"] = sent(mine["y"], "z")
     mine["zx"] = sent(mine["z"], "x")
     def pick(units, ways):
         return [units[way] for way in ways]
 
-    first = (*ONE, CORNER)
-    theirs_one = [own_theirs, stacked(first)]
-    *sums_near, sum_corner = sums_of(
-        affine, pick(mine, ("", *first)), theirs_one, diagonal=True, hides=False
-    )
-    theirs_two = [stacked(TWO, sums_near[:1])]
-    sums_two = sums_of(affine, pick(mine, TWO), theirs_one)
+    mine[CORNER] = sent(mine["xy"], "z")
+    near = ("", *ONE)
+    theirs = [own_theirs, stacked(ONE)]
+    sums_near = sums_of(affine, pick(mine, near), theirs, diagonal=True, hides=False)
+    theirs_two = stacked(TWO, sums_near[:1])
+    sums_two = sums_of(affine, pick(mine, TWO), theirs)
+    sums_two = sums_of(affine, pick(mine, TWO), [theirs_two], sums_two)
+    theirs_corner = stacked([CORNER], sums_two[:1])
+    sum_corner = sums_of(affine, [mine[CORNER]], [*theirs, theirs_two], after=sums_two[:1])
 
     part_xy, part_yz, part_zx = sums_of(
-        affine, pick(mine, TWO), theirs_two, sums_two, kinds=[HALF] * 3
+        affine, pick(mine, TWO), [theirs_corner], sums_two, sum_corner, [HALF] * 3
     )
     for_x, for_y, for_z = sent(part_xy, "y"), sent(part_yz, "z"), sent(part_zx, "x")
     (part_xyz,) = sums_of(
-        affine, [mine[CORNER]], theirs_two, [sum_corner], after=[part_xy], kinds=[HALF]
+        affine, [mine[CORNER]], [theirs_corner], sum_corner, [part_xy], [HALF]
     )
     arrived = [sent(part_xyz, CORNER)]
+    theirs = [theirs_two, theirs_corner]
     part_x, part_y, part_z = sums_of(
-        affine, pick(mine, ONE), theirs_two, sums_near[1:], after=[part_xyz]
+        affine, pick(mine, ONE), theirs, sums_near[1:], [part_xyz]
     )
 
     def with_added(part, added, way):
@@ -241,7 +243,7 @@
     arrived.append(with_added(part_x, [for_x], "x"))
     arrived.append(with_added(part_y, [for_y], "y"))
     arrived.append(with_added(part_z, [for_z], "z"))
-    (own_part,) = sums_of(affine, [own], theirs_two, sums_near[:1], after=[part_z])
+    (own_part,) = sums_of(affine, [own], theirs, sums_near[:1], [part_z])
 
     here, there = pl.pallas_call(
         finish_kernel,

time: 85.8 us -> 85.5 us (level)
  waiting for transfers between devices: 19.5 us -> 17.6 us
  Pallas kernels: 30.2 us -> 31.6 us
    ppermute x5 -> x6, starting transfers between devices: 3.51 us -> 9.01 us  [other_core(): return lax.ppermute(value, 'core', [(0, 1), (1, 0)])]
    ppermute x14, starting transfers between devices: 26.6 us -> 21.2 us  [sent(): return lax.ppermute(value, FINE_AXES, pairs)]
    ppermute x14, waiting for transfers between devices: 17.8 us -> 16 us  [sent(): return lax.ppermute(value, FINE_AXES, pairs)]
    pallas_call x6 -> x8, Pallas kernels: 27.9 us -> 29.4 us  [sums_of(): pl.pallas_call(functools.partial(sums_kernel, count, n_theirs, n_starts,...]
  transfers between devices with their start and end apart: 19 -> 20, of which waited for: 6 -> 8; matrix products, arithmetic and copies ran while one was open for 0% -> 0% of each run, Pallas kernels for 28% -> 32%
where the time goes in v10:
time: 85.5 us; the launch traced here: 85.3 us
  Pallas kernels  31.6 us (37%)
  starting transfers between devices  30.2 us (35%)
  waiting for transfers between devices  17.6 us (21%)
  between operations  2.75 us (3%)
  local copies, waits for them, and re-layouts  1.92 us (2%)
  other arithmetic  1.16 us (1%)
    pallas_call x8, Pallas kernels, sums_of(): pl.pallas_call(functools.partial(sums_kernel, count, n_theirs, n_starts,...  29.4 us
    ppermute x14, starting transfers between devices, sent(): return lax.ppermute(value, FINE_AXES, pairs)  21.2 us
    ppermute x14, waiting for transfers between devices, sent(): return lax.ppermute(value, FINE_AXES, pairs)  16 us
    ppermute x6, starting transfers between devices, other_core(): return lax.ppermute(value, 'core', [(0, 1), (1, 0)])  9.01 us
    unnamed x4, local copies, waits for them, and re-layouts  1.92 us
  transfers between devices with their start and end apart: 20, of which 8 were waited for; matrix products, arithmetic and copies ran while one was open for 0% of the time, Pallas kernels for 32%

profile of v10, /device:TPU:1, one launch (start us, length us, event | category | flops | bytes accessed | tf_op | source)
XLA Modules:
  0.0 85.3 jit_solution(11842239807992076128)
XLA Ops:
  0.6 1.5 %collective-permute-start = (bf16[128,1152]{1,0:T(8,128)(2,1)}, bf16[128,1152]{1,0:T(8,128)(2,1)S(1)}, u32[]{:S(2)}, u32[]{:S(2)}) collective-permute-start(bf16[128,1152]{1,0:T(8,128)(2,1)} %refs_1_.1), channel_id=1, source_target_pairs={{0,32},{32,0},{1,33},{33,1},{2,34},{34,2},{3,35},{35,3},{4,36},{36... | collective-permute-start | bytes 884744 | tf_op jit(solution)/shard_map/ppermute | solution.py:50
  2.1 0.1 collective-permute-start.1
  2.2 1.0 %copy-done = bf16[128,1152]{1,0:T(8,128)(2,1)S(1)} copy-done((bf16[128,1152]{1,0:T(8,128)(2,1)S(1)}, bf16[128,1152]{1,0:T(8,128)(2,1)}, u32[]{:S(2)}) %copy-start) | copy-done | bytes 294936
  3.2 1.0 %copy-done.1 = bf16[128,1152]{1,0:T(8,128)(2,1)S(1)} copy-done((bf16[128,1152]{1,0:T(8,128)(2,1)S(1)}, bf16[128,1152]{1,0:T(8,128)(2,1)}, u32[]{:S(2)}) %copy-start.1) | copy-done | bytes 294936
  4.1 0.2 shard_map.68
  4.4 0.5 shard_map.69
  4.9 2.6 %collective-permute-start.2 = (bf16[256,1152]{1,0:T(8,128)(2,1)S(1)}, bf16[256,1152]{1,0:T(8,128)(2,1)S(1)}, u32[]{:S(2)}, u32[]{:S(2)}) collective-permute-start(bf16[256,1152]{1,0:T(8,128)(2,1)S(1)} %get-tuple-element.30.refs_0_), channel_id=1, source_target_pairs={{0,8},{32,56},{2,10},{34,58},{4,12},{36,60},{6,14},{38,62},{64,72}... | collective-permute-start | bytes 1769480 | tf_op jit(solution)/shard_map/ppermute | solution.py:46
  7.5 2.7 %collective-permute-start.4 = (bf16[256,1152]{1,0:T(8,128)(2,1)S(1)}, bf16[256,1152]{1,0:T(8,128)(2,1)S(1)}, u32[]{:S(2)}, u32[]{:S(2)}) collective-permute-start(bf16[256,1152]{1,0:T(8,128)(2,1)S(1)} %get-tuple-element.30.refs_0_), channel_id=1, source_target_pairs={{0,64},{32,97},{2,66},{34,99},{4,68},{36,101},{6,70},{38,103},{64,... | collective-permute-start | bytes 1769480 | tf_op jit(solution)/shard_map/ppermute | solution.py:46
  10.3 1.6 %collective-permute-start.6 = (bf16[256,1152]{1,0:T(8,128)(2,1)S(1)}, bf16[256,1152]{1,0:T(8,128)(2,1)S(1)}, u32[]{:S(2)}, u32[]{:S(2)}) collective-permute-start(bf16[256,1152]{1,0:T(8,128)(2,1)S(1)} %get-tuple-element.30.refs_0_), channel_id=1, source_target_pairs={{0,6},{32,34},{2,4},{34,32},{4,2},{36,38},{6,0},{38,36},{64,70},{9... | collective-permute-start | bytes 1769480 | tf_op jit(solution)/shard_map/ppermute | solution.py:46
  11.9 3.3 %collective-permute-done.2.refs_0_.refs_1_ = bf16[256,1152]{1,0:T(8,128)(2,1)S(1)} collective-permute-done((bf16[256,1152]{1,0:T(8,128)(2,1)S(1)}, bf16[256,1152]{1,0:T(8,128)(2,1)S(1)}, u32[]{:S(2)}, u32[]{:S(2)}) %collective-permute-start.2) | collective-permute-done | bytes 589856 | tf_op jit(solution)/shard_map/ppermute | solution.py:46
  15.2 2.6 %collective-permute-done.4.refs_1_.refs_2_ = bf16[256,1152]{1,0:T(8,128)(2,1)S(1)} collective-permute-done((bf16[256,1152]{1,0:T(8,128)(2,1)S(1)}, bf16[256,1152]{1,0:T(8,128)(2,1)S(1)}, u32[]{:S(2)}, u32[]{:S(2)}) %collective-permute-start.4) | collective-permute-done | bytes 589856 | tf_op jit(solution)/shard_map/ppermute | solution.py:46
  17.8 1.6 %collective-permute-done.6.refs_2_.refs_3_ = bf16[256,1152]{1,0:T(8,128)(2,1)S(1)} collective-permute-done((bf16[256,1152]{1,0:T(8,128)(2,1)S(1)}, bf16[256,1152]{1,0:T(8,128)(2,1)S(1)}, u32[]{:S(2)}, u32[]{:S(2)}) %collective-permute-start.6) | collective-permute-done | bytes 589856 | tf_op jit(solution)/shard_map/ppermute | solution.py:46
  19.5 0.1 shard_map.70
  19.6 1.0 %collective-permute-start.8 = (bf16[768,1152]{1,0:T(8,128)(2,1)S(1)}, bf16[768,1152]{1,0:T(8,128)(2,1)S(1)}, u32[]{:S(2)}, u32[]{:S(2)}) collective-permute-start(bf16[768,1152]{1,0:T(8,128)(2,1)S(1)} %shard_map.70), channel_id=1, source_target_pairs={{0,32},{32,0},{1,33},{33,1},{2,34},{34,2},{3,35},{35,3},{4,36},{36... | collective-permute-start | bytes 5308424 | tf_op jit(solution)/shard_map/ppermute | solution.py:50
  20.7 1.9 %collective-permute-start.3 = (bf16[256,1152]{1,0:T(8,128)(2,1)S(1)}, bf16[256,1152]{1,0:T(8,128)(2,1)S(1)}, u32[]{:S(2)}, u32[]{:S(2)}) collective-permute-start(bf16[256,1152]{1,0:T(8,128)(2,1)S(1)} %collective-permute-done.2.refs_0_.refs_1_), channel_id=1, source_target_pairs={{0,64},{32,97},{2,66},{34,99},{4,68},{36,101},{6,70},{38,103},{64,... | collective-permute-start | bytes 1769480 | tf_op jit(solution)/shard_map/ppermute | solution.py:46
  22.6 1.8 %collective-permute-start.7 = (bf16[256,1152]{1,0:T(8,128)(2,1)S(1)}, bf16[256,1152]{1,0:T(8,128)(2,1)S(1)}, u32[]{:S(2)}, u32[]{:S(2)}) collective-permute-start(bf16[256,1152]{1,0:T(8,128)(2,1)S(1)} %collective-permute-done.6.refs_2_.refs_3_), channel_id=1, source_target_pairs={{0,8},{32,56},{2,10},{34,58},{4,12},{36,60},{6,14},{38,62},{64,72}... | collective-permute-start | bytes 1769480 | tf_op jit(solution)/shard_map/ppermute | solution.py:46
  25.7 0.1 pad_maximum_fusion.affine
  25.8 6.3 %shard_map.71 = (f32[256,1152]{1,0:T(8,128)S(1)}, f32[256,1152]{1,0:T(8,128)S(1)}, f32[256,1152]{1,0:T(8,128)S(1)}, f32[256,1152]{1,0:T(8,128)S(1)}) custom-call(f32[2]{0:T(128)S(1)} %pad_maximum_fusion.affine, bf16[256,1152]{1,0:T(8,128)(2,1)S(1)} %get-tuple-element.30.refs_0_, bf16[256,1152]{1,0:T(8,128)(2,1)S(1)} %collective-permute-done.2.refs_0_.refs_1_, ...), custom_call_target="tpu_custom_call" | custom-call | tf_op jit(solution)/shard_map/pallas_call | solution.py:119
  32.1 0.5 collective-permute-done.7.refs_2_
  32.5 0.1 shard_map.72
  32.6 1.9 %collective-permute-start.9 = (bf16[768,1152]{1,0:T(8,128)(2,1)S(1)}, bf16[768,1152]{1,0:T(8,128)(2,1)S(1)}, u32[]{:S(2)}, u32[]{:S(2)}) collective-permute-start(bf16[768,1152]{1,0:T(8,128)(2,1)S(1)} %shard_map.72), channel_id=1, source_target_pairs={{0,32},{32,0},{1,33},{33,1},{2,34},{34,2},{3,35},{35,3},{4,36},{36... | collective-permute-start | bytes 5308424 | tf_op jit(solution)/shard_map/ppermute | solution.py:50
  34.5 0.0 collective-permute-start.10
  34.5 4.9 %shard_map.73 = (f32[256,1152]{1,0:T(8,128)S(1)}, f32[256,1152]{1,0:T(8,128)S(1)}, f32[256,1152]{1,0:T(8,128)S(1)}) custom-call(f32[2]{0:T(128)S(1)} %pad_maximum_fusion.affine, bf16[256,1152]{1,0:T(8,128)(2,1)S(1)} %collective-permute-done.3.refs_0_, bf16[256,1152]{1,0:T(8,128)(2,1)S(1)} %collective-permute-done.5.refs_1_, ...), custom_call_target="tpu_custom_call" | custom-call | flops 3623878656 | bytes 7077888 | tf_op jit(solution)/shard_map/pallas_call | solution.py:119
  39.4 4.1 %shard_map.74 = (f32[256,1152]{1,0:T(8,128)S(1)}, f32[256,1152]{1,0:T(8,128)S(1)}, f32[256,1152]{1,0:T(8,128)S(1)}) custom-call(f32[2]{0:T(128)S(1)} %pad_maximum_fusion.affine, bf16[256,1152]{1,0:T(8,128)(2,1)S(1)} %collective-permute-done.3.refs_0_, bf16[256,1152]{1,0:T(8,128)(2,1)S(1)} %collective-permute-done.5.refs_1_, ...), custom_call_target="tpu_custom_call" | custom-call | flops 2717908992 | bytes 7077888 | tf_op jit(solution)/shard_map/pallas_call | solution.py:119
  43.6 0.0 collective-permute-done.10.refs_0_
  43.6 2.4 %collective-permute-start.11 = (bf16[256,1152]{1,0:T(8,128)(2,1)S(1)}, bf16[256,1152]{1,0:T(8,128)(2,1)S(1)}, u32[]{:S(2)}, u32[]{:S(2)}) collective-permute-start(bf16[256,1152]{1,0:T(8,128)(2,1)S(1)} %shard_map.75), channel_id=1, source_target_pairs={{0,32},{32,0},{1,33},{33,1},{2,34},{34,2},{3,35},{35,3},{4,36},{36... | collective-permute-start | bytes 1769480 | tf_op jit(solution)/shard_map/ppermute | solution.py:50
  46.0 3.1 %shard_map.76.refs_7_.refs_2_ = f32[256,1152]{1,0:T(8,128)S(1)} custom-call(f32[2]{0:T(128)S(1)} %pad_maximum_fusion.affine, bf16[256,1152]{1,0:T(8,128)(2,1)S(1)} %collective-permute-done.10.refs_0_, bf16[256,1152]{1,0:T(8,128)(2,1)S(1)} %get-tuple-element.31.refs_4_.refs_3_.refs_1_, bf16[768,1152]{1,0:T(8,128)(2,1)S(1)} %collective-permute-done.8.refs_5_.refs_4_.refs_2_, ...), custom_call_target="tpu_custom_call" | custom-call | flops 2113929216 | bytes 2359296 | tf_op jit(solution)/shard_map/pallas_call | solution.py:119
  49.2 2.5 %shard_map.77 = (bf16[256,1152]{1,0:T(8,128)(2,1)S(1)}, bf16[256,1152]{1,0:T(8,128)(2,1)S(1)}, bf16[256,1152]{1,0:T(8,128)(2,1)S(1)}) custom-call(f32[2]{0:T(128)S(1)} %pad_maximum_fusion.affine, bf16[256,1152]{1,0:T(8,128)(2,1)S(1)} %collective-permute-done.3.refs_0_, bf16[256,1152]{1,0:T(8,128)(2,1)S(1)} %collective-permute-done.5.refs_1_, ...), custom_call_target="tpu_custom_call" | custom-call | flops 905969664 | bytes 7077888 | tf_op jit(solution)/shard_map/pallas_call | solution.py:119
  51.7 1.9 %collective-permute-start.17 = (bf16[256,1152]{1,0:T(8,128)(2,1)S(1)}, bf16[256,1152]{1,0:T(8,128)(2,1)S(1)}, u32[]{:S(2)}, u32[]{:S(2)}) collective-permute-start(bf16[256,1152]{1,0:T(8,128)(2,1)S(1)} %get-tuple-element.47), channel_id=1, source_target_pairs={{0,8},{32,56},{2,10},{34,58},{4,12},{36,60},{6,14},{38,62},{64,72}... | collective-permute-start | bytes 1769480 | tf_op jit(solution)/shard_map/ppermute | solution.py:46
  53.6 0.4 collective-permute-start.15
  54.1 2.3 %collective-permute-start.13 = (bf16[256,1152]{1,0:T(8,128)(2,1)S(1)}, bf16[256,1152]{1,0:T(8,128)(2,1)S(1)}, u32[]{:S(2)}, u32[]{:S(2)}) collective-permute-start(bf16[256,1152]{1,0:T(8,128)(2,1)S(1)} %get-tuple-element.42.refs_3_), channel_id=1, source_target_pairs={{0,64},{32,97},{2,66},{34,99},{4,68},{36,101},{6,70},{38,103},{64,... | collective-permute-start | bytes 1769480 | tf_op jit(solution)/shard_map/ppermute | solution.py:46
  56.4 1.5 %shard_map.78.refs_8_ = bf16[256,1152]{1,0:T(8,128)(2,1)S(1)} custom-call(f32[2]{0:T(128)S(1)} %pad_maximum_fusion.affine, bf16[256,1152]{1,0:T(8,128)(2,1)S(1)} %collective-permute-done.10.refs_0_, bf16[256,1152]{1,0:T(8,128)(2,1)S(1)} %collective-permute-done.11.refs_3_.refs_1_.refs_4_.refs_2_, f32[256,1152]{1,0:T(8,128)S(1)} %shard_map.76.refs_7_.refs_2_, ...), custom_call_target="tpu_custom_call" | custom-call | flops 301989888 | bytes 2359296 | tf_op jit(solution)/shard_map/pallas_call | solution.py:119
  57.8 2.1 %collective-permute-start.12 = (bf16[256,1152]{1,0:T(8,128)(2,1)S(1)}, bf16[256,1152]{1,0:T(8,128)(2,1)S(1)}, u32[]{:S(2)}, u32[]{:S(2)}) collective-permute-start(bf16[256,1152]{1,0:T(8,128)(2,1)S(1)} %shard_map.78.refs_8_), channel_id=1, source_target_pairs={{0,78},{32,123},{2,76},{34,121},{4,74},{36,127},{6,72},{38,125},{6... | collective-permute-start | bytes 1769480 | tf_op jit(solution)/shard_map/ppermute | solution.py:46
  59.9 4.9 %shard_map.79 = (f32[256,1152]{1,0:T(8,128)S(1)}, f32[256,1152]{1,0:T(8,128)S(1)}, f32[256,1152]{1,0:T(8,128)S(1)}) custom-call(f32[2]{0:T(128)S(1)} %pad_maximum_fusion.affine, bf16[256,1152]{1,0:T(8,128)(2,1)S(1)} %collective-permute-done.2.refs_0_.refs_1_, bf16[256,1152]{1,0:T(8,128)(2,1)S(1)} %collective-permute-done.4.refs_1_.refs_2_, ...), custom_call_target="tpu_custom_call" | custom-call | flops 3623878656 | bytes 7077888 | tf_op jit(solution)/shard_map/pallas_call | solution.py:119
  64.8 0.1 shard_map.83
  64.9 0.5 collective-permute-start.18
  65.3 0.1 shard_map.82
  65.5 2.4 %collective-permute-start.16 = (bf16[256,1152]{1,0:T(8,128)(2,1)S(1)}, bf16[256,1152]{1,0:T(8,128)(2,1)S(1)}, u32[]{:S(2)}, u32[]{:S(2)}) collective-permute-start(bf16[256,1152]{1,0:T(8,128)(2,1)S(1)} %shard_map.82), channel_id=1, source_target_pairs={{0,64},{32,97},{2,66},{34,99},{4,68},{36,101},{6,70},{38,103},{64,... | collective-permute-start | bytes 1769480 | tf_op jit(solution)/shard_map/ppermute | solution.py:46
  67.9 1.6 %collective-permute-done.13.refs_1_ = bf16[256,1152]{1,0:T(8,128)(2,1)S(1)} collective-permute-done((bf16[256,1152]{1,0:T(8,128)(2,1)S(1)}, bf16[256,1152]{1,0:T(8,128)(2,1)S(1)}, u32[]{:S(2)}, u32[]{:S(2)}) %collective-permute-start.13) | collective-permute-done | bytes 589856 | tf_op jit(solution)/shard_map/ppermute | solution.py:46
  69.5 0.1 shard_map.81
  69.6 0.9 %collective-permute-start.14 = (bf16[256,1152]{1,0:T(8,128)(2,1)S(1)}, bf16[256,1152]{1,0:T(8,128)(2,1)S(1)}, u32[]{:S(2)}, u32[]{:S(2)}) collective-permute-start(bf16[256,1152]{1,0:T(8,128)(2,1)S(1)} %shard_map.81), channel_id=1, source_target_pairs={{0,8},{32,56},{2,10},{34,58},{4,12},{36,60},{6,14},{38,62},{64,72}... | collective-permute-start | bytes 1769480 | tf_op jit(solution)/shard_map/ppermute | solution.py:46
  71.2 2.1 %shard_map.80.refs_0_ = f32[256,1152]{1,0:T(8,128)S(1)} custom-call(f32[2]{0:T(128)S(1)} %pad_maximum_fusion.affine, bf16[256,1152]{1,0:T(8,128)(2,1)S(1)} %get-tuple-element.30.refs_0_, bf16[768,1152]{1,0:T(8,128)(2,1)S(1)} %collective-permute-done.9.refs_3_.refs_1_, bf16[256,1152]{1,0:T(8,128)(2,1)S(1)} %collective-permute-done.11.refs_3_.refs_1_.refs_4_.refs_2_, ...), custom_call_target="tpu_custom_call" | custom-call | flops 1207959552 | bytes 2359296 | tf_op jit(solution)/shard_map/pallas_call | solution.py:119
  73.3 4.4 %collective-permute-done.18.refs_4_ = bf16[256,1152]{1,0:T(8,128)(2,1)S(1)} collective-permute-done((bf16[256,1152]{1,0:T(8,128)(2,1)S(1)}, bf16[256,1152]{1,0:T(8,128)(2,1)S(1)}, u32[]{:S(2)}, u32[]{:S(2)}) %collective-permute-start.18) | collective-permute-done | bytes 589856 | tf_op jit(solution)/shard_map/ppermute | solution.py:46
  77.7 1.9 %collective-permute-done.14.refs_2_ = bf16[256,1152]{1,0:T(8,128)(2,1)S(1)} collective-permute-done((bf16[256,1152]{1,0:T(8,128)(2,1)S(1)}, bf16[256,1152]{1,0:T(8,128)(2,1)S(1)}, u32[]{:S(2)}, u32[]{:S(2)}) %collective-permute-start.14) | collective-permute-done | bytes 589856 | tf_op jit(solution)/shard_map/ppermute | solution.py:46
  79.6 0.9 %shard_map.84 = (f32[128,1152]{1,0:T(8,128)S(1)}, f32[128,1152]{1,0:T(8,128)S(1)}) custom-call(s32[1]{0:T(128)} %bitcast.core, f32[1]{0:T(128)S(6)} %div.3.multiplier, bf16[256,1152]{1,0:T(8,128)(2,1)S(1)} %get-tuple-element.29.raw, f32[256,1152]{1,0:T(8,128)S(1)} %shard_map.80.refs_0_, bf16[256,1152]{1,0:T(8,128)(2,1)S(1)} %collective-permute-done.12.refs_1_, ...), custom_call_target="tpu_custom_call" | custom-call | tf_op jit(solution)/shard_map/pallas_call | solution.py:248
  80.5 2.1 %collective-permute-start.19 = (f32[128,1152]{1,0:T(8,128)S(1)}, f32[128,1152]{1,0:T(8,128)S(1)}, u32[]{:S(2)}, u32[]{:S(2)}) collective-permute-start(f32[128,1152]{1,0:T(8,128)S(1)} %get-tuple-element.49), channel_id=1, source_target_pairs={{0,32},{32,0},{1,33},{33,1},{2,34},{34,2},{3,35},{35,3},{4,36},{36... | collective-permute-start | bytes 1769480 | tf_op jit(solution)/shard_map/ppermute | solution.py:50
  82.6 1.6 %collective-permute-done.19 = f32[128,1152]{1,0:T(8,128)S(1)} collective-permute-done((f32[128,1152]{1,0:T(8,128)S(1)}, f32[128,1152]{1,0:T(8,128)S(1)}, u32[]{:S(2)}, u32[]{:S(2)}) %collective-permute-start.19) | collective-permute-done | bytes 589856 | tf_op jit(solution)/shard_map/ppermute | solution.py:50
  84.2 1.1 %broadcast_select_fusion = (f32[128,1152]{1,0:T(8,128)}, f32[128,1152]{1,0:T(8,128)}) fusion(f32[128,1152]{1,0:T(8,128)S(1)} %collective-permute-done.19, f32[128,1152]{1,0:T(8,128)S(1)} %get-tuple-element.48, pred[]{:T(512)S(6)} %eq.3), kind=kLoop, calls=%fused_computation | loop fusion | flops 294912 | bytes 2359297 | tf_op jit(solution)/shard_map/jit(_where)/select_n | solution.py:257
  (15 shorter events, 0.1 us)
Async XLA Ops:
  0.6 3.8 %collective-permute-start = (bf16[128,1152]{1,0:T(8,128)(2,1)}, bf16[128,1152]{1,0:T(8,128)(2,1)S(1)}, u32[]{:S(2)}, u32[]{:S(2)}) collective-permute-start(bf16[128,1152]{1,0:T(8,128)(2,1)} %refs_1_.1), channel_id=1, source_target_pairs={{0,32},{32,0},{1,33},{33,1},{2,34},{34,2},{3,35},{35,3},{4,36},{36... | collective-permute-start | bytes 884744 | tf_op jit(solution)/shard_map/ppermute | solution.py:50
  2.1 2.3 %collective-permute-start.1 = (bf16[128,1152]{1,0:T(8,128)(2,1)}, bf16[128,1152]{1,0:T(8,128)(2,1)S(1)}, u32[]{:S(2)}, u32[]{:S(2)}) collective-permute-start(bf16[128,1152]{1,0:T(8,128)(2,1)} %refs_2_.1), channel_id=1, source_target_pairs={{0,32},{32,0},{1,33},{33,1},{2,34},{34,2},{3,35},{35,3},{4,36},{36... | collective-permute-start | bytes 884744 | tf_op jit(solution)/shard_map/ppermute | solution.py:50
  2.2 1.0 %copy-start = (bf16[128,1152]{1,0:T(8,128)(2,1)S(1)}, bf16[128,1152]{1,0:T(8,128)(2,1)}, u32[]{:S(2)}) copy-start(bf16[128,1152]{1,0:T(8,128)(2,1)} %refs_1_.1) | copy-start | bytes 884740
  3.2 1.0 %copy-start.1 = (bf16[128,1152]{1,0:T(8,128)(2,1)S(1)}, bf16[128,1152]{1,0:T(8,128)(2,1)}, u32[]{:S(2)}) copy-start(bf16[128,1152]{1,0:T(8,128)(2,1)} %refs_2_.1) | copy-start | bytes 884740
  4.9 10.3 %collective-permute-start.2 = (bf16[256,1152]{1,0:T(8,128)(2,1)S(1)}, bf16[256,1152]{1,0:T(8,128)(2,1)S(1)}, u32[]{:S(2)}, u32[]{:S(2)}) collective-permute-start(bf16[256,1152]{1,0:T(8,128)(2,1)S(1)} %get-tuple-element.30.refs_0_), channel_id=1, source_target_pairs={{0,8},{32,56},{2,10},{34,58},{4,12},{36,60},{6,14},{38,62},{64,72}... | collective-permute-start | bytes 1769480 | tf_op jit(solution)/shard_map/ppermute | solution.py:46
  7.5 10.3 %collective-permute-start.4 = (bf16[256,1152]{1,0:T(8,128)(2,1)S(1)}, bf16[256,1152]{1,0:T(8,128)(2,1)S(1)}, u32[]{:S(2)}, u32[]{:S(2)}) collective-permute-start(bf16[256,1152]{1,0:T(8,128)(2,1)S(1)} %get-tuple-element.30.refs_0_), channel_id=1, source_target_pairs={{0,64},{32,97},{2,66},{34,99},{4,68},{36,101},{6,70},{38,103},{64,... | collective-permute-start | bytes 1769480 | tf_op jit(solution)/shard_map/ppermute | solution.py:46
  10.3 9.2 %collective-permute-start.6 = (bf16[256,1152]{1,0:T(8,128)(2,1)S(1)}, bf16[256,1152]{1,0:T(8,128)(2,1)S(1)}, u32[]{:S(2)}, u32[]{:S(2)}) collective-permute-start(bf16[256,1152]{1,0:T(8,128)(2,1)S(1)} %get-tuple-element.30.refs_0_), channel_id=1, source_target_pairs={{0,6},{32,34},{2,4},{34,32},{4,2},{36,38},{6,0},{38,36},{64,70},{9... | collective-permute-start | bytes 1769480 | tf_op jit(solution)/shard_map/ppermute | solution.py:46
  19.6 6.1 %collective-permute-start.8 = (bf16[768,1152]{1,0:T(8,128)(2,1)S(1)}, bf16[768,1152]{1,0:T(8,128)(2,1)S(1)}, u32[]{:S(2)}, u32[]{:S(2)}) collective-permute-start(bf16[768,1152]{1,0:T(8,128)(2,1)S(1)} %shard_map.70), channel_id=1, source_target_pairs={{0,32},{32,0},{1,33},{33,1},{2,34},{34,2},{3,35},{35,3},{4,36},{36... | collective-permute-start | bytes 5308424 | tf_op jit(solution)/shard_map/ppermute | solution.py:50
  20.7 11.4 %collective-permute-start.3 = (bf16[256,1152]{1,0:T(8,128)(2,1)S(1)}, bf16[256,1152]{1,0:T(8,128)(2,1)S(1)}, u32[]{:S(2)}, u32[]{:S(2)}) collective-permute-start(bf16[256,1152]{1,0:T(8,128)(2,1)S(1)} %collective-permute-done.2.refs_0_.refs_1_), channel_id=1, source_target_pairs={{0,64},{32,97},{2,66},{34,99},{4,68},{36,101},{6,70},{38,103},{64,... | collective-permute-start | bytes 1769480 | tf_op jit(solution)/shard_map/ppermute | solution.py:46
  22.6 9.5 %collective-permute-start.5 = (bf16[256,1152]{1,0:T(8,128)(2,1)S(1)}, bf16[256,1152]{1,0:T(8,128)(2,1)S(1)}, u32[]{:S(2)}, u32[]{:S(2)}) collective-permute-start(bf16[256,1152]{1,0:T(8,128)(2,1)S(1)} %collective-permute-done.4.refs_1_.refs_2_), channel_id=1, source_target_pairs={{0,6},{32,34},{2,4},{34,32},{4,2},{36,38},{6,0},{38,36},{64,70},{9... | collective-permute-start | bytes 1769480 | tf_op jit(solution)/shard_map/ppermute | solution.py:46
  22.6 9.9 %collective-permute-start.7 = (bf16[256,1152]{1,0:T(8,128)(2,1)S(1)}, bf16[256,1152]{1,0:T(8,128)(2,1)S(1)}, u32[]{:S(2)}, u32[]{:S(2)}) collective-permute-start(bf16[256,1152]{1,0:T(8,128)(2,1)S(1)} %collective-permute-done.6.refs_2_.refs_3_), channel_id=1, source_target_pairs={{0,8},{32,56},{2,10},{34,58},{4,12},{36,60},{6,14},{38,62},{64,72}... | collective-permute-start | bytes 1769480 | tf_op jit(solution)/shard_map/ppermute | solution.py:46
  32.6 6.8 %collective-permute-start.9 = (bf16[768,1152]{1,0:T(8,128)(2,1)S(1)}, bf16[768,1152]{1,0:T(8,128)(2,1)S(1)}, u32[]{:S(2)}, u32[]{:S(2)}) collective-permute-start(bf16[768,1152]{1,0:T(8,128)(2,1)S(1)} %shard_map.72), channel_id=1, source_target_pairs={{0,32},{32,0},{1,33},{33,1},{2,34},{34,2},{3,35},{35,3},{4,36},{36... | collective-permute-start | bytes 5308424 | tf_op jit(solution)/shard_map/ppermute | solution.py:50
  34.5 9.0 %collective-permute-start.10 = (bf16[256,1152]{1,0:T(8,128)(2,1)S(1)}, bf16[256,1152]{1,0:T(8,128)(2,1)S(1)}, u32[]{:S(2)}, u32[]{:S(2)}) collective-permute-start(bf16[256,1152]{1,0:T(8,128)(2,1)S(1)} %collective-permute-done.3.refs_0_), channel_id=1, source_target_pairs={{0,6},{32,34},{2,4},{34,32},{4,2},{36,38},{6,0},{38,36},{64,70},{9... | collective-permute-start | bytes 1769480 | tf_op jit(solution)/shard_map/ppermute | solution.py:46
  43.6 5.6 %collective-permute-start.11 = (bf16[256,1152]{1,0:T(8,128)(2,1)S(1)}, bf16[256,1152]{1,0:T(8,128)(2,1)S(1)}, u32[]{:S(2)}, u32[]{:S(2)}) collective-permute-start(bf16[256,1152]{1,0:T(8,128)(2,1)S(1)} %shard_map.75), channel_id=1, source_target_pairs={{0,32},{32,0},{1,33},{33,1},{2,34},{34,2},{3,35},{35,3},{4,36},{36... | collective-permute-start | bytes 1769480 | tf_op jit(solution)/shard_map/ppermute | solution.py:50
  51.7 13.0 %collective-permute-start.17 = (bf16[256,1152]{1,0:T(8,128)(2,1)S(1)}, bf16[256,1152]{1,0:T(8,128)(2,1)S(1)}, u32[]{:S(2)}, u32[]{:S(2)}) collective-permute-start(bf16[256,1152]{1,0:T(8,128)(2,1)S(1)} %get-tuple-element.47), channel_id=1, source_target_pairs={{0,8},{32,56},{2,10},{34,58},{4,12},{36,60},{6,14},{38,62},{64,72}... | collective-permute-start | bytes 1769480 | tf_op jit(solution)/shard_map/ppermute | solution.py:46
  53.6 11.7 %collective-permute-start.15 = (bf16[256,1152]{1,0:T(8,128)(2,1)S(1)}, bf16[256,1152]{1,0:T(8,128)(2,1)S(1)}, u32[]{:S(2)}, u32[]{:S(2)}) collective-permute-start(bf16[256,1152]{1,0:T(8,128)(2,1)S(1)} %get-tuple-element.46), channel_id=1, source_target_pairs={{0,6},{32,34},{2,4},{34,32},{4,2},{36,38},{6,0},{38,36},{64,70},{9... | collective-permute-start | bytes 1769480 | tf_op jit(solution)/shard_map/ppermute | solution.py:46
  54.1 15.4 %collective-permute-start.13 = (bf16[256,1152]{1,0:T(8,128)(2,1)S(1)}, bf16[256,1152]{1,0:T(8,128)(2,1)S(1)}, u32[]{:S(2)}, u32[]{:S(2)}) collective-permute-start(bf16[256,1152]{1,0:T(8,128)(2,1)S(1)} %get-tuple-element.42.refs_3_), channel_id=1, source_target_pairs={{0,64},{32,97},{2,66},{34,99},{4,68},{36,101},{6,70},{38,103},{64,... | collective-permute-start | bytes 1769480 | tf_op jit(solution)/shard_map/ppermute | solution.py:46
  57.8 15.5 %collective-permute-start.12 = (bf16[256,1152]{1,0:T(8,128)(2,1)S(1)}, bf16[256,1152]{1,0:T(8,128)(2,1)S(1)}, u32[]{:S(2)}, u32[]{:S(2)}) collective-permute-start(bf16[256,1152]{1,0:T(8,128)(2,1)S(1)} %shard_map.78.refs_8_), channel_id=1, source_target_pairs={{0,78},{32,123},{2,76},{34,121},{4,74},{36,127},{6,72},{38,125},{6... | collective-permute-start | bytes 1769480 | tf_op jit(solution)/shard_map/ppermute | solution.py:46
  64.9 12.9 %collective-permute-start.18 = (bf16[256,1152]{1,0:T(8,128)(2,1)S(1)}, bf16[256,1152]{1,0:T(8,128)(2,1)S(1)}, u32[]{:S(2)}, u32[]{:S(2)}) collective-permute-start(bf16[256,1152]{1,0:T(8,128)(2,1)S(1)} %shard_map.83), channel_id=1, source_target_pairs={{0,6},{32,34},{2,4},{34,32},{4,2},{36,38},{6,0},{38,36},{64,70},{9... | collective-permute-start | bytes 1769480 | tf_op jit(solution)/shard_map/ppermute | solution.py:46
  65.5 12.3 %collective-permute-start.16 = (bf16[256,1152]{1,0:T(8,128)(2,1)S(1)}, bf16[256,1152]{1,0:T(8,128)(2,1)S(1)}, u32[]{:S(2)}, u32[]{:S(2)}) collective-permute-start(bf16[256,1152]{1,0:T(8,128)(2,1)S(1)} %shard_map.82), channel_id=1, source_target_pairs={{0,64},{32,97},{2,66},{34,99},{4,68},{36,101},{6,70},{38,103},{64,... | collective-permute-start | bytes 1769480 | tf_op jit(solution)/shard_map/ppermute | solution.py:46
  69.6 10.0 %collective-permute-start.14 = (bf16[256,1152]{1,0:T(8,128)(2,1)S(1)}, bf16[256,1152]{1,0:T(8,128)(2,1)S(1)}, u32[]{:S(2)}, u32[]{:S(2)}) collective-permute-start(bf16[256,1152]{1,0:T(8,128)(2,1)S(1)} %shard_map.81), channel_id=1, source_target_pairs={{0,8},{32,56},{2,10},{34,58},{4,12},{36,60},{6,14},{38,62},{64,72}... | collective-permute-start | bytes 1769480 | tf_op jit(solution)/shard_map/ppermute | solution.py:46
  80.5 3.7 %collective-permute-start.19 = (f32[128,1152]{1,0:T(8,128)S(1)}, f32[128,1152]{1,0:T(8,128)S(1)}, u32[]{:S(2)}, u32[]{:S(2)}) collective-permute-start(f32[128,1152]{1,0:T(8,128)S(1)} %get-tuple-element.49), channel_id=1, source_target_pairs={{0,32},{32,0},{1,33},{33,1},{2,34},{34,2},{3,35},{35,3},{4,36},{36... | collective-permute-start | bytes 1769480 | tf_op jit(solution)/shard_map/ppermute | solution.py:50

commit v11 on v7

--- a/solution.py
+++ b/solution.py
@@ -36,12 +36,12 @@
     return (k + 1) % RING if k % 2 else (k - 1) % RING
 
 
-def sent(value, way):
+def sent(value, way, crossing=False):
     pairs = []
     for at in np.ndindex(RING, RING, RING):
         for core in range(2):
             to = [mate(core, axis, k) if axis in way else k for axis, k in zip("xyz", at, strict=True)]
-            pairs.append((place(core, *at), place(core, *to)))
+            pairs.append((place(core, *at), place(1 - core if crossing else core, *to)))
     return lax.ppermute(value, FINE_AXES, pairs)
 
 
@@ -130,19 +130,6 @@
     )(affine, *mine, *theirs, *starts, *after)
 
 
-def finish_kernel(core, multiplier, raw, *refs):
-    parts, (here, there, grads) = refs[:-3], refs[-3:]
-    rows = here.shape[0]
-    total = parts[0][...].astype(FULL)
-    for part in parts[1:]:
-        total = total + part[...].astype(FULL)
-    unit, scale = unit_rows(raw[...])
-    grad = multiplier[0] * total
-    grads[...] = scale * (grad - unit * jnp.sum(unit * grad, axis=1, keepdims=True))
-    here[...] = grads[pl.ds(core[0] * rows, rows), :]
-    there[...] = grads[pl.ds((1 - core[0]) * rows, rows), :]
-
-
 def on_device(
     picture_vectors_raw, caption_vectors_raw, logit_multiplier, offset_term, incoming_adjoint
 ):
@@ -154,38 +141,31 @@
     affine = jnp.concatenate([0.5 * logit_multiplier, 0.5 * offset_term])
     multiplier = incoming_adjoint * logit_multiplier / pairs
     shard, unit = ((rows, width), HALF), ((2 * rows, width), HALF)
-    shard_full = jax.ShapeDtypeStruct((rows, width), FULL)
+    shard_full = ((rows, width), FULL)
 
     image_there = other_core(picture_vectors_raw)
     text_there = other_core(caption_vectors_raw)
-    image, text, raw_here = local(
-        lambda scalars, refs: [
-            unit_rows(refs[0][...])[0],
-            unit_rows(refs[1][...])[0],
-            jnp.where(scalars[0][0] > 0, refs[0][...].astype(FULL), refs[1][...].astype(FULL)),
-        ],
-        [shard] * 3,
-        [first_flag],
+    image, text = local(
+        lambda _, refs: [unit_rows(ref[...])[0] for ref in refs],
+        [shard] * 2,
+        [],
         [picture_vectors_raw, caption_vectors_raw],
     )
 
     def own_units(scalars, refs):
         first = scalars[0][0] > 0
-        image_there, text_there, image, text, raw_here = [ref[...].astype(FULL) for ref in refs]
-        raw_there = jnp.where(first, image_there, text_there)
+        image_there, text_there, image, text = [ref[...].astype(FULL) for ref in refs]
         images, texts = (image, unit_rows(image_there)[0]), (text, unit_rows(text_there)[0])
-        results = [[], [], []]
+        results = [[], []]
         for k in range(2):
             of_image = jnp.where(first, images[k], images[1 - k])
             of_text = jnp.where(first, texts[k], texts[1 - k])
             results[0].append(jnp.where(first, of_image, of_text))
             results[1].append(jnp.where(first, of_text, of_image))
-            raws = (raw_here, raw_there)
-            results[2].append(jnp.where(first, raws[k], raws[1 - k]))
         return [jnp.concatenate(halves, 0) for halves in results]
 
-    own, own_theirs, raw = local(
-        own_units, [unit] * 3, [first_flag], [image_there, text_there, image, text, raw_here]
+    own, own_theirs = local(
+        own_units, [unit] * 2, [first_flag], [image_there, text_there, image, text]
     )
 
     def stacked(ways, after=()):
@@ -219,37 +199,52 @@
         return sums_of(affine, pick(mine, ways), theirs_two, pick(sums, ways), after, kinds)
 
     part_xyz, part_xy = parts_of(("xyz", "xy"), [HALF, HALF])
-    for_x = [sent(part_xyz, "yz"), sent(part_xy, "y")]
+    for_x = [sent(part_xy, "y")]
     part_yz, part_zx = parts_of(("yz", "zx"), [HALF, HALF], [part_xy])
-    for_y = [sent(part_yz, "z")]
+    for_y = [sent(part_xyz, "zx"), sent(part_yz, "z")]
     for_z = [sent(part_zx, "x")]
     own_part, part_x, part_y, part_z = parts_of(near, [FULL] * 4, [part_zx])
 
-    def with_added(part, added, way):
-        (total,) = local(
-            lambda _, refs: [sum([ref[...].astype(FULL) for ref in refs[1:]], refs[0][...])],
-            [unit],
-            [],
-            [part, *added],
+    def halves(scalars, refs):
+        core, total = scalars[0][0], refs[0]
+        found = []
+        for which in (core, 1 - core):
+            at = pl.ds(pl.multiple_of(which * rows, rows), rows)
+            half = total[at, :]
+            for ref in refs[1:]:
+                half = half + ref[at, :].astype(FULL)
+            found.append(half)
+        return found
+
+    which = core.reshape(1)
+    own_here, own_there = local(halves, [shard_full, shard], [which], [own_part])
+    here, there = [own_here], [other_core(own_there)]
+    for way, part, added in (("x", part_x, for_x), ("y", part_y, for_y), ("z", part_z, for_z)):
+        mine_half, other_half = local(halves, [shard] * 2, [which], [part, *added])
+        here.append(sent(mine_half, way))
+        there.append(sent(other_half, way, True))
+
+    def finish(scalars, refs):
+        first, multiplier = scalars[0][0] > 0, scalars[1][0]
+        raws, refs = refs[:2], refs[2:]
+        totals = []
+        for parts in (refs[: len(here)], refs[len(here) :]):
+            totals.append(sum([ref[...].astype(FULL) for ref in parts[1:]], parts[0][...].astype(FULL)))
+        results = []
+        for k, raw in enumerate(raws):
+            unit, scale = unit_rows(raw[...])
+            grad = multiplier * jnp.where(first, totals[k], totals[1 - k])
+            results.append(scale * (grad - unit * jnp.sum(unit * grad, axis=1, keepdims=True)))
+        return results
+
+    return tuple(
+        local(
+            finish,
+            [shard_full] * 2,
+            [first_flag, multiplier],
+            [picture_vectors_raw, caption_vectors_raw, *here, *there],
         )
-        return sent(total, way)
-
-    arrived = [
-        with_added(part_x, for_x, "x"),
-        with_added(part_y, for_y, "y"),
-        with_added(part_z, for_z, "z"),
-    ]
-
-    here, there = pl.pallas_call(
-        finish_kernel,
-        out_shape=[shard_full, shard_full],
-        in_specs=[SMEM, SMEM] + [VMEM] * (2 + len(arrived)),
-        out_specs=[VMEM] * 2,
-        scratch_shapes=[pltpu.VMEM((2 * rows, width), FULL)],
-        compiler_params=PARAMS,
-    )(core.reshape(1), multiplier, raw, own_part, *arrived)
-    back = other_core(there)
-    return (jnp.where(is_first, here, back), jnp.where(is_first, back, here))
+    )
 
 
 def solution(mesh):

time: 84.9 us -> 84.4 us (level)
  other arithmetic: 1.16 us -> 0.08 us
  Pallas kernels: 28.1 us -> 29 us
    ppermute x14 -> x17, starting transfers between devices: 24.1 us -> 26.3 us  [sent(): return lax.ppermute(value, FINE_AXES, pairs)]
    pallas_call x7 -> x9, Pallas kernels: 1.43 us -> 3.1 us  [local(): pl.pallas_call(kernel, out_shape=[jax.ShapeDtypeStruct(s, d) for s, d in...]
    ppermute x5, starting transfers between devices: 6.2 us -> 4.56 us  [other_core(): return lax.ppermute(value, 'core', [(0, 1), (1, 0)])]
    ppermute x5, waiting for transfers between devices: 1.64 us -> 0.01 us  [other_core(): return lax.ppermute(value, 'core', [(0, 1), (1, 0)])]
    select_n x1 -> x0, other arithmetic: 1.09 us -> none  [on_device(): return (jnp.where(is_first, here, back), jnp.where(is_first, back, here))]
    ppermute x14 -> x17, waiting for transfers between devices: 18.8 us -> 19.6 us  [sent(): return lax.ppermute(value, FINE_AXES, pairs)]
    unnamed x4 -> x8, local copies, waits for them, and re-layouts: 1.92 us -> 1.93 us
  transfers between devices with their start and end apart: 19 -> 22, of which waited for: 10 -> 11; matrix products, arithmetic and copies ran while one was open for 0% -> 0% of each run, Pallas kernels for 27% -> 27%
where the time goes in v11:
time: 84.4 us; the launch traced here: 84.2 us
  starting transfers between devices  30.9 us (37%)
  Pallas kernels  29 us (34%)
  waiting for transfers between devices  19.6 us (23%)
  between operations  2.75 us (3%)
  local copies, waits for them, and re-layouts  1.93 us (2%)
    ppermute x17, starting transfers between devices, sent(): return lax.ppermute(value, FINE_AXES, pairs)  26.3 us
    pallas_call x5, Pallas kernels, sums_of(): pl.pallas_call(functools.partial(sums_kernel, count, n_theirs, n_starts,...  25.9 us
    ppermute x17, waiting for transfers between devices, sent(): return lax.ppermute(value, FINE_AXES, pairs)  19.6 us
    ppermute x5, starting transfers between devices, other_core(): return lax.ppermute(value, 'core', [(0, 1), (1, 0)])  4.56 us
    pallas_call x9, Pallas kernels, local(): pl.pallas_call(kernel, out_shape=[jax.ShapeDtypeStruct(s, d) for s, d in...  3.1 us
    unnamed x8, local copies, waits for them, and re-layouts  1.93 us
  transfers between devices with their start and end apart: 22, of which 11 were waited for; matrix products, arithmetic and copies ran while one was open for 0% of the time, Pallas kernels for 27%

profile of v11, /device:TPU:1, one launch (start us, length us, event | category | flops | bytes accessed | tf_op | source)
XLA Modules:
  0.0 84.2 jit_solution(4567885442482654190)
XLA Ops:
  0.6 1.5 %collective-permute-start = (bf16[128,1152]{1,0:T(8,128)(2,1)}, bf16[128,1152]{1,0:T(8,128)(2,1)S(1)}, u32[]{:S(2)}, u32[]{:S(2)}) collective-permute-start(bf16[128,1152]{1,0:T(8,128)(2,1)} %refs_2_.1), channel_id=1, source_target_pairs={{0,32},{32,0},{1,33},{33,1},{2,34},{34,2},{3,35},{35,3},{4,36},{36... | collective-permute-start | bytes 884744 | tf_op jit(solution)/shard_map/ppermute | solution.py:49
  2.1 0.1 collective-permute-start.1
  2.2 1.0 %copy-done = bf16[128,1152]{1,0:T(8,128)(2,1)S(1)} copy-done((bf16[128,1152]{1,0:T(8,128)(2,1)S(1)}, bf16[128,1152]{1,0:T(8,128)(2,1)}, u32[]{:S(2)}) %copy-start) | copy-done | bytes 294936
  3.2 1.0 %copy-done.2 = bf16[128,1152]{1,0:T(8,128)(2,1)S(1)} copy-done((bf16[128,1152]{1,0:T(8,128)(2,1)S(1)}, bf16[128,1152]{1,0:T(8,128)(2,1)}, u32[]{:S(2)}) %copy-start.2) | copy-done | bytes 294936
  4.1 0.2 shard_map.68
  4.4 0.4 shard_map.69
  4.8 2.6 %collective-permute-start.2 = (bf16[256,1152]{1,0:T(8,128)(2,1)S(1)}, bf16[256,1152]{1,0:T(8,128)(2,1)S(1)}, u32[]{:S(2)}, u32[]{:S(2)}) collective-permute-start(bf16[256,1152]{1,0:T(8,128)(2,1)S(1)} %get-tuple-element.32.refs_0_), channel_id=1, source_target_pairs={{0,8},{32,56},{2,10},{34,58},{4,12},{36,60},{6,14},{38,62},{64,72}... | collective-permute-start | bytes 1769480 | tf_op jit(solution)/shard_map/ppermute | solution.py:45
  7.4 2.7 %collective-permute-start.3 = (bf16[256,1152]{1,0:T(8,128)(2,1)S(1)}, bf16[256,1152]{1,0:T(8,128)(2,1)S(1)}, u32[]{:S(2)}, u32[]{:S(2)}) collective-permute-start(bf16[256,1152]{1,0:T(8,128)(2,1)S(1)} %get-tuple-element.32.refs_0_), channel_id=1, source_target_pairs={{0,64},{32,97},{2,66},{34,99},{4,68},{36,101},{6,70},{38,103},{64,... | collective-permute-start | bytes 1769480 | tf_op jit(solution)/shard_map/ppermute | solution.py:45
  10.1 1.6 %collective-permute-start.4 = (bf16[256,1152]{1,0:T(8,128)(2,1)S(1)}, bf16[256,1152]{1,0:T(8,128)(2,1)S(1)}, u32[]{:S(2)}, u32[]{:S(2)}) collective-permute-start(bf16[256,1152]{1,0:T(8,128)(2,1)S(1)} %get-tuple-element.32.refs_0_), channel_id=1, source_target_pairs={{0,6},{32,34},{2,4},{34,32},{4,2},{36,38},{6,0},{38,36},{64,70},{9... | collective-permute-start | bytes 1769480 | tf_op jit(solution)/shard_map/ppermute | solution.py:45
  11.8 3.3 %collective-permute-done.2.refs_0_.refs_1_ = bf16[256,1152]{1,0:T(8,128)(2,1)S(1)} collective-permute-done((bf16[256,1152]{1,0:T(8,128)(2,1)S(1)}, bf16[256,1152]{1,0:T(8,128)(2,1)S(1)}, u32[]{:S(2)}, u32[]{:S(2)}) %collective-permute-start.2) | collective-permute-done | bytes 589856 | tf_op jit(solution)/shard_map/ppermute | solution.py:45
  15.1 2.6 %collective-permute-done.3.refs_1_.refs_2_ = bf16[256,1152]{1,0:T(8,128)(2,1)S(1)} collective-permute-done((bf16[256,1152]{1,0:T(8,128)(2,1)S(1)}, bf16[256,1152]{1,0:T(8,128)(2,1)S(1)}, u32[]{:S(2)}, u32[]{:S(2)}) %collective-permute-start.3) | collective-permute-done | bytes 589856 | tf_op jit(solution)/shard_map/ppermute | solution.py:45
  17.7 1.6 %collective-permute-done.4.refs_2_.refs_3_ = bf16[256,1152]{1,0:T(8,128)(2,1)S(1)} collective-permute-done((bf16[256,1152]{1,0:T(8,128)(2,1)S(1)}, bf16[256,1152]{1,0:T(8,128)(2,1)S(1)}, u32[]{:S(2)}, u32[]{:S(2)}) %collective-permute-start.4) | collective-permute-done | bytes 589856 | tf_op jit(solution)/shard_map/ppermute | solution.py:45
  19.3 0.1 shard_map.70
  19.5 1.0 %collective-permute-start.9 = (bf16[768,1152]{1,0:T(8,128)(2,1)S(1)}, bf16[768,1152]{1,0:T(8,128)(2,1)S(1)}, u32[]{:S(2)}, u32[]{:S(2)}) collective-permute-start(bf16[768,1152]{1,0:T(8,128)(2,1)S(1)} %shard_map.70), channel_id=1, source_target_pairs={{0,32},{32,0},{1,33},{33,1},{2,34},{34,2},{3,35},{35,3},{4,36},{36... | collective-permute-start | bytes 5308424 | tf_op jit(solution)/shard_map/ppermute | solution.py:49
  20.5 1.2 %collective-permute-start.5 = (bf16[256,1152]{1,0:T(8,128)(2,1)S(1)}, bf16[256,1152]{1,0:T(8,128)(2,1)S(1)}, u32[]{:S(2)}, u32[]{:S(2)}) collective-permute-start(bf16[256,1152]{1,0:T(8,128)(2,1)S(1)} %collective-permute-done.2.refs_0_.refs_1_), channel_id=1, source_target_pairs={{0,70},{32,99},{2,68},{34,97},{4,66},{36,103},{6,64},{38,101},{64,... | collective-permute-start | bytes 1769480 | tf_op jit(solution)/shard_map/ppermute | solution.py:45
  21.8 1.4 %collective-permute-start.6 = (bf16[256,1152]{1,0:T(8,128)(2,1)S(1)}, bf16[256,1152]{1,0:T(8,128)(2,1)S(1)}, u32[]{:S(2)}, u32[]{:S(2)}) collective-permute-start(bf16[256,1152]{1,0:T(8,128)(2,1)S(1)} %collective-permute-done.2.refs_0_.refs_1_), channel_id=1, source_target_pairs={{0,64},{32,97},{2,66},{34,99},{4,68},{36,101},{6,70},{38,103},{64,... | collective-permute-start | bytes 1769480 | tf_op jit(solution)/shard_map/ppermute | solution.py:45
  23.2 1.2 %collective-permute-start.7 = (bf16[256,1152]{1,0:T(8,128)(2,1)S(1)}, bf16[256,1152]{1,0:T(8,128)(2,1)S(1)}, u32[]{:S(2)}, u32[]{:S(2)}) collective-permute-start(bf16[256,1152]{1,0:T(8,128)(2,1)S(1)} %collective-permute-done.3.refs_1_.refs_2_), channel_id=1, source_target_pairs={{0,6},{32,34},{2,4},{34,32},{4,2},{36,38},{6,0},{38,36},{64,70},{9... | collective-permute-start | bytes 1769480 | tf_op jit(solution)/shard_map/ppermute | solution.py:45
  24.4 1.8 %collective-permute-start.8 = (bf16[256,1152]{1,0:T(8,128)(2,1)S(1)}, bf16[256,1152]{1,0:T(8,128)(2,1)S(1)}, u32[]{:S(2)}, u32[]{:S(2)}) collective-permute-start(bf16[256,1152]{1,0:T(8,128)(2,1)S(1)} %collective-permute-done.4.refs_2_.refs_3_), channel_id=1, source_target_pairs={{0,8},{32,56},{2,10},{34,58},{4,12},{36,60},{6,14},{38,62},{64,72}... | collective-permute-start | bytes 1769480 | tf_op jit(solution)/shard_map/ppermute | solution.py:45
  27.5 0.1 pad_maximum_fusion.affine
  27.6 6.3 %shard_map.71 = (f32[256,1152]{1,0:T(8,128)S(1)}, f32[256,1152]{1,0:T(8,128)S(1)}, f32[256,1152]{1,0:T(8,128)S(1)}, f32[256,1152]{1,0:T(8,128)S(1)}) custom-call(f32[2]{0:T(128)S(1)} %pad_maximum_fusion.affine, bf16[256,1152]{1,0:T(8,128)(2,1)S(1)} %get-tuple-element.32.refs_0_, bf16[256,1152]{1,0:T(8,128)(2,1)S(1)} %collective-permute-done.2.refs_0_.refs_1_, ...), custom_call_target="tpu_custom_call" | custom-call | tf_op jit(solution)/shard_map/pallas_call | solution.py:118
  33.9 3.3 %collective-permute-done.6.refs_1_ = bf16[256,1152]{1,0:T(8,128)(2,1)S(1)} collective-permute-done((bf16[256,1152]{1,0:T(8,128)(2,1)S(1)}, bf16[256,1152]{1,0:T(8,128)(2,1)S(1)}, u32[]{:S(2)}, u32[]{:S(2)}) %collective-permute-start.6) | collective-permute-done | bytes 589856 | tf_op jit(solution)/shard_map/ppermute | solution.py:45
  37.1 0.8 %collective-permute-done.7.refs_2_.refs_0_ = bf16[256,1152]{1,0:T(8,128)(2,1)S(1)} collective-permute-done((bf16[256,1152]{1,0:T(8,128)(2,1)S(1)}, bf16[256,1152]{1,0:T(8,128)(2,1)S(1)}, u32[]{:S(2)}, u32[]{:S(2)}) %collective-permute-start.7) | collective-permute-done | bytes 589856 | tf_op jit(solution)/shard_map/ppermute | solution.py:45
  38.0 0.2 shard_map.72
  38.2 1.8 %collective-permute-start.10 = (bf16[1024,1152]{1,0:T(8,128)(2,1)S(1)}, bf16[1024,1152]{1,0:T(8,128)(2,1)S(1)}, u32[]{:S(2)}, u32[]{:S(2)}) collective-permute-start(bf16[1024,1152]{1,0:T(8,128)(2,1)S(1)} %shard_map.72), channel_id=1, source_target_pairs={{0,32},{32,0},{1,33},{33,1},{2,34},{34,2},{3,35},{35,3},{4,36},{36... | collective-permute-start | bytes 7077896 | tf_op jit(solution)/shard_map/ppermute | solution.py:49
  40.0 6.3 %shard_map.73 = (f32[256,1152]{1,0:T(8,128)S(1)}, f32[256,1152]{1,0:T(8,128)S(1)}, f32[256,1152]{1,0:T(8,128)S(1)}, f32[256,1152]{1,0:T(8,128)S(1)}) custom-call(f32[2]{0:T(128)S(1)} %pad_maximum_fusion.affine, bf16[256,1152]{1,0:T(8,128)(2,1)S(1)} %collective-permute-done.5.refs_0_, bf16[256,1152]{1,0:T(8,128)(2,1)S(1)} %collective-permute-done.6.refs_1_, ...), custom_call_target="tpu_custom_call" | custom-call | flops 4831838208 | bytes 9437184 | tf_op jit(solution)/shard_map/pallas_call | solution.py:118
  46.3 3.5 %shard_map.74 = (bf16[256,1152]{1,0:T(8,128)(2,1)S(1)}, bf16[256,1152]{1,0:T(8,128)(2,1)S(1)}) custom-call(f32[2]{0:T(128)S(1)} %pad_maximum_fusion.affine, bf16[256,1152]{1,0:T(8,128)(2,1)S(1)} %collective-permute-done.5.refs_0_, bf16[256,1152]{1,0:T(8,128)(2,1)S(1)} %collective-permute-done.6.refs_1_, ...), custom_call_target="tpu_custom_call" | custom-call | flops 2415919104 | bytes 4718592 | tf_op jit(solution)/shard_map/pallas_call | solution.py:118
  49.8 2.0 %collective-permute-start.11 = (bf16[256,1152]{1,0:T(8,128)(2,1)S(1)}, bf16[256,1152]{1,0:T(8,128)(2,1)S(1)}, u32[]{:S(2)}, u32[]{:S(2)}) collective-permute-start(bf16[256,1152]{1,0:T(8,128)(2,1)S(1)} %get-tuple-element.42.refs_5_), channel_id=1, source_target_pairs={{0,64},{32,97},{2,66},{34,99},{4,68},{36,101},{6,70},{38,103},{64,... | collective-permute-start | bytes 1769480 | tf_op jit(solution)/shard_map/ppermute | solution.py:45
  51.8 3.5 %shard_map.75 = (bf16[256,1152]{1,0:T(8,128)(2,1)S(1)}, bf16[256,1152]{1,0:T(8,128)(2,1)S(1)}) custom-call(f32[2]{0:T(128)S(1)} %pad_maximum_fusion.affine, bf16[256,1152]{1,0:T(8,128)(2,1)S(1)} %collective-permute-done.7.refs_2_.refs_0_, bf16[256,1152]{1,0:T(8,128)(2,1)S(1)} %collective-permute-done.8.refs_3_.refs_1_, ...), custom_call_target="tpu_custom_call" | custom-call | flops 2415919104 | bytes 4718592 | tf_op jit(solution)/shard_map/pallas_call | solution.py:118
  55.3 3.1 %collective-permute-start.14 = (bf16[256,1152]{1,0:T(8,128)(2,1)S(1)}, bf16[256,1152]{1,0:T(8,128)(2,1)S(1)}, u32[]{:S(2)}, u32[]{:S(2)}) collective-permute-start(bf16[256,1152]{1,0:T(8,128)(2,1)S(1)} %get-tuple-element.50), channel_id=1, source_target_pairs={{0,6},{32,34},{2,4},{34,32},{4,2},{36,38},{6,0},{38,36},{64,70},{9... | collective-permute-start | bytes 1769480 | tf_op jit(solution)/shard_map/ppermute | solution.py:45
  58.3 0.9 %collective-permute-start.16 = (bf16[256,1152]{1,0:T(8,128)(2,1)S(1)}, bf16[256,1152]{1,0:T(8,128)(2,1)S(1)}, u32[]{:S(2)}, u32[]{:S(2)}) collective-permute-start(bf16[256,1152]{1,0:T(8,128)(2,1)S(1)} %get-tuple-element.43.refs_9_), channel_id=1, source_target_pairs={{0,8},{32,56},{2,10},{34,58},{4,12},{36,60},{6,14},{38,62},{64,72}... | collective-permute-start | bytes 1769480 | tf_op jit(solution)/shard_map/ppermute | solution.py:45
  59.2 6.3 %shard_map.76 = (f32[256,1152]{1,0:T(8,128)S(1)}, f32[256,1152]{1,0:T(8,128)S(1)}, f32[256,1152]{1,0:T(8,128)S(1)}, f32[256,1152]{1,0:T(8,128)S(1)}) custom-call(f32[2]{0:T(128)S(1)} %pad_maximum_fusion.affine, bf16[256,1152]{1,0:T(8,128)(2,1)S(1)} %get-tuple-element.32.refs_0_, bf16[256,1152]{1,0:T(8,128)(2,1)S(1)} %collective-permute-done.2.refs_0_.refs_1_, ...), custom_call_target="tpu_custom_call" | custom-call | flops 4831838208 | bytes 9437184 | tf_op jit(solution)/shard_map/pallas_call | solution.py:118
  65.5 0.1 shard_map.77
  65.6 0.1 collective-permute-start.18
  65.7 0.1 shard_map.78
  65.8 1.9 %collective-permute-start.12 = (bf16[128,1152]{1,0:T(8,128)(2,1)S(1)}, bf16[128,1152]{1,0:T(8,128)(2,1)S(1)}, u32[]{:S(2)}, u32[]{:S(2)}) collective-permute-start(bf16[128,1152]{1,0:T(8,128)(2,1)S(1)} %get-tuple-element.47), channel_id=1, source_target_pairs={{0,8},{32,56},{2,10},{34,58},{4,12},{36,60},{6,14},{38,62},{64,72}... | collective-permute-start | bytes 884744 | tf_op jit(solution)/shard_map/ppermute | solution.py:45
  67.7 1.2 %collective-permute-done.14.refs_3_ = bf16[256,1152]{1,0:T(8,128)(2,1)S(1)} collective-permute-done((bf16[256,1152]{1,0:T(8,128)(2,1)S(1)}, bf16[256,1152]{1,0:T(8,128)(2,1)S(1)}, u32[]{:S(2)}, u32[]{:S(2)}) %collective-permute-start.14) | collective-permute-done | bytes 589856 | tf_op jit(solution)/shard_map/ppermute | solution.py:45
  68.9 0.2 shard_map.79
  69.1 1.2 %collective-permute-start.15 = (bf16[128,1152]{1,0:T(8,128)(2,1)S(1)}, bf16[128,1152]{1,0:T(8,128)(2,1)S(1)}, u32[]{:S(2)}, u32[]{:S(2)}) collective-permute-start(bf16[128,1152]{1,0:T(8,128)(2,1)S(1)} %get-tuple-element.51), channel_id=1, source_target_pairs={{0,64},{32,97},{2,66},{34,99},{4,68},{36,101},{6,70},{38,103},{64,... | collective-permute-start | bytes 884744 | tf_op jit(solution)/shard_map/ppermute | solution.py:45
  70.3 0.1 shard_map.80
  70.4 0.1 collective-permute-start.17
  70.5 4.5 %collective-permute-start.19 = (bf16[128,1152]{1,0:T(8,128)(2,1)S(1)}, bf16[128,1152]{1,0:T(8,128)(2,1)S(1)}, u32[]{:S(2)}, u32[]{:S(2)}) collective-permute-start(bf16[128,1152]{1,0:T(8,128)(2,1)S(1)} %get-tuple-element.55), channel_id=1, source_target_pairs={{0,40},{32,24},{2,42},{34,26},{4,44},{36,28},{6,46},{38,30},{64,10... | collective-permute-start | bytes 884744 | tf_op jit(solution)/shard_map/ppermute | solution.py:45
  75.0 0.1 collective-permute-start.20
  75.8 0.5 collective-permute-done.15.refs_6_
  76.3 0.1 collective-permute-done.17.refs_7_
  76.3 2.3 %collective-permute-done.19.refs_9_ = bf16[128,1152]{1,0:T(8,128)(2,1)S(1)} collective-permute-done((bf16[128,1152]{1,0:T(8,128)(2,1)S(1)}, bf16[128,1152]{1,0:T(8,128)(2,1)S(1)}, u32[]{:S(2)}, u32[]{:S(2)}) %collective-permute-start.19) | collective-permute-done | bytes 294944 | tf_op jit(solution)/shard_map/ppermute | solution.py:45
  78.7 2.7 %collective-permute-done.20.refs_10_ = bf16[128,1152]{1,0:T(8,128)(2,1)S(1)} collective-permute-done((bf16[128,1152]{1,0:T(8,128)(2,1)S(1)}, bf16[128,1152]{1,0:T(8,128)(2,1)S(1)}, u32[]{:S(2)}, u32[]{:S(2)}) %collective-permute-start.20) | collective-permute-done | bytes 294944 | tf_op jit(solution)/shard_map/ppermute | solution.py:45
  81.3 1.1 %collective-permute-done.21.refs_11_ = bf16[128,1152]{1,0:T(8,128)(2,1)S(1)} collective-permute-done((bf16[128,1152]{1,0:T(8,128)(2,1)S(1)}, bf16[128,1152]{1,0:T(8,128)(2,1)S(1)}, u32[]{:S(2)}, u32[]{:S(2)}) %collective-permute-start.21) | collective-permute-done | bytes 294944 | tf_op jit(solution)/shard_map/ppermute | solution.py:45
  82.5 1.8 %shard_map.81 = (f32[128,1152]{1,0:T(8,128)}, f32[128,1152]{1,0:T(8,128)}) custom-call(f32[1]{0:T(128)} %bitcast.refs_0_, f32[1]{0:T(128)S(6)} %div.3.refs_1_, bf16[128,1152]{1,0:T(8,128)(2,1)S(1)} %copy-done.1, bf16[128,1152]{1,0:T(8,128)(2,1)S(1)} %copy-done.3, f32[128,1152]{1,0:T(8,128)S(1)} %get-tuple-element.45.refs_4_, ...), custom_call_target="tpu_custom_call" | custom-call | tf_op jit(solution)/shard_map/pallas_call | solution.py:73
  (19 shorter events, 0.1 us)
Async XLA Ops:
  0.6 3.7 %collective-permute-start = (bf16[128,1152]{1,0:T(8,128)(2,1)}, bf16[128,1152]{1,0:T(8,128)(2,1)S(1)}, u32[]{:S(2)}, u32[]{:S(2)}) collective-permute-start(bf16[128,1152]{1,0:T(8,128)(2,1)} %refs_2_.1), channel_id=1, source_target_pairs={{0,32},{32,0},{1,33},{33,1},{2,34},{34,2},{3,35},{35,3},{4,36},{36... | collective-permute-start | bytes 884744 | tf_op jit(solution)/shard_map/ppermute | solution.py:49
  2.1 2.3 %collective-permute-start.1 = (bf16[128,1152]{1,0:T(8,128)(2,1)}, bf16[128,1152]{1,0:T(8,128)(2,1)S(1)}, u32[]{:S(2)}, u32[]{:S(2)}) collective-permute-start(bf16[128,1152]{1,0:T(8,128)(2,1)} %refs_3_.1), channel_id=1, source_target_pairs={{0,32},{32,0},{1,33},{33,1},{2,34},{34,2},{3,35},{35,3},{4,36},{36... | collective-permute-start | bytes 884744 | tf_op jit(solution)/shard_map/ppermute | solution.py:49
  2.2 1.0 %copy-start = (bf16[128,1152]{1,0:T(8,128)(2,1)S(1)}, bf16[128,1152]{1,0:T(8,128)(2,1)}, u32[]{:S(2)}) copy-start(bf16[128,1152]{1,0:T(8,128)(2,1)} %refs_2_.1) | copy-start | bytes 884740
  3.2 1.0 %copy-start.2 = (bf16[128,1152]{1,0:T(8,128)(2,1)S(1)}, bf16[128,1152]{1,0:T(8,128)(2,1)}, u32[]{:S(2)}) copy-start(bf16[128,1152]{1,0:T(8,128)(2,1)} %refs_3_.1) | copy-start | bytes 884740
  4.8 10.3 %collective-permute-start.2 = (bf16[256,1152]{1,0:T(8,128)(2,1)S(1)}, bf16[256,1152]{1,0:T(8,128)(2,1)S(1)}, u32[]{:S(2)}, u32[]{:S(2)}) collective-permute-start(bf16[256,1152]{1,0:T(8,128)(2,1)S(1)} %get-tuple-element.32.refs_0_), channel_id=1, source_target_pairs={{0,8},{32,56},{2,10},{34,58},{4,12},{36,60},{6,14},{38,62},{64,72}... | collective-permute-start | bytes 1769480 | tf_op jit(solution)/shard_map/ppermute | solution.py:45
  7.4 10.3 %collective-permute-start.3 = (bf16[256,1152]{1,0:T(8,128)(2,1)S(1)}, bf16[256,1152]{1,0:T(8,128)(2,1)S(1)}, u32[]{:S(2)}, u32[]{:S(2)}) collective-permute-start(bf16[256,1152]{1,0:T(8,128)(2,1)S(1)} %get-tuple-element.32.refs_0_), channel_id=1, source_target_pairs={{0,64},{32,97},{2,66},{34,99},{4,68},{36,101},{6,70},{38,103},{64,... | collective-permute-start | bytes 1769480 | tf_op jit(solution)/shard_map/ppermute | solution.py:45
  10.1 9.2 %collective-permute-start.4 = (bf16[256,1152]{1,0:T(8,128)(2,1)S(1)}, bf16[256,1152]{1,0:T(8,128)(2,1)S(1)}, u32[]{:S(2)}, u32[]{:S(2)}) collective-permute-start(bf16[256,1152]{1,0:T(8,128)(2,1)S(1)} %get-tuple-element.32.refs_0_), channel_id=1, source_target_pairs={{0,6},{32,34},{2,4},{34,32},{4,2},{36,38},{6,0},{38,36},{64,70},{9... | collective-permute-start | bytes 1769480 | tf_op jit(solution)/shard_map/ppermute | solution.py:45
  19.5 8.1 %collective-permute-start.9 = (bf16[768,1152]{1,0:T(8,128)(2,1)S(1)}, bf16[768,1152]{1,0:T(8,128)(2,1)S(1)}, u32[]{:S(2)}, u32[]{:S(2)}) collective-permute-start(bf16[768,1152]{1,0:T(8,128)(2,1)S(1)} %shard_map.70), channel_id=1, source_target_pairs={{0,32},{32,0},{1,33},{33,1},{2,34},{34,2},{3,35},{35,3},{4,36},{36... | collective-permute-start | bytes 5308424 | tf_op jit(solution)/shard_map/ppermute | solution.py:49
  20.5 13.3 %collective-permute-start.5 = (bf16[256,1152]{1,0:T(8,128)(2,1)S(1)}, bf16[256,1152]{1,0:T(8,128)(2,1)S(1)}, u32[]{:S(2)}, u32[]{:S(2)}) collective-permute-start(bf16[256,1152]{1,0:T(8,128)(2,1)S(1)} %collective-permute-done.2.refs_0_.refs_1_), channel_id=1, source_target_pairs={{0,70},{32,99},{2,68},{34,97},{4,66},{36,103},{6,64},{38,101},{64,... | collective-permute-start | bytes 1769480 | tf_op jit(solution)/shard_map/ppermute | solution.py:45
  21.8 15.4 %collective-permute-start.6 = (bf16[256,1152]{1,0:T(8,128)(2,1)S(1)}, bf16[256,1152]{1,0:T(8,128)(2,1)S(1)}, u32[]{:S(2)}, u32[]{:S(2)}) collective-permute-start(bf16[256,1152]{1,0:T(8,128)(2,1)S(1)} %collective-permute-done.2.refs_0_.refs_1_), channel_id=1, source_target_pairs={{0,64},{32,97},{2,66},{34,99},{4,68},{36,101},{6,70},{38,103},{64,... | collective-permute-start | bytes 1769480 | tf_op jit(solution)/shard_map/ppermute | solution.py:45
  23.2 14.8 %collective-permute-start.7 = (bf16[256,1152]{1,0:T(8,128)(2,1)S(1)}, bf16[256,1152]{1,0:T(8,128)(2,1)S(1)}, u32[]{:S(2)}, u32[]{:S(2)}) collective-permute-start(bf16[256,1152]{1,0:T(8,128)(2,1)S(1)} %collective-permute-done.3.refs_1_.refs_2_), channel_id=1, source_target_pairs={{0,6},{32,34},{2,4},{34,32},{4,2},{36,38},{6,0},{38,36},{64,70},{9... | collective-permute-start | bytes 1769480 | tf_op jit(solution)/shard_map/ppermute | solution.py:45
  24.4 13.6 %collective-permute-start.8 = (bf16[256,1152]{1,0:T(8,128)(2,1)S(1)}, bf16[256,1152]{1,0:T(8,128)(2,1)S(1)}, u32[]{:S(2)}, u32[]{:S(2)}) collective-permute-start(bf16[256,1152]{1,0:T(8,128)(2,1)S(1)} %collective-permute-done.4.refs_2_.refs_3_), channel_id=1, source_target_pairs={{0,8},{32,56},{2,10},{34,58},{4,12},{36,60},{6,14},{38,62},{64,72}... | collective-permute-start | bytes 1769480 | tf_op jit(solution)/shard_map/ppermute | solution.py:45
  38.2 8.1 %collective-permute-start.10 = (bf16[1024,1152]{1,0:T(8,128)(2,1)S(1)}, bf16[1024,1152]{1,0:T(8,128)(2,1)S(1)}, u32[]{:S(2)}, u32[]{:S(2)}) collective-permute-start(bf16[1024,1152]{1,0:T(8,128)(2,1)S(1)} %shard_map.72), channel_id=1, source_target_pairs={{0,32},{32,0},{1,33},{33,1},{2,34},{34,2},{3,35},{35,3},{4,36},{36... | collective-permute-start | bytes 7077896 | tf_op jit(solution)/shard_map/ppermute | solution.py:49
  49.8 15.9 %collective-permute-start.11 = (bf16[256,1152]{1,0:T(8,128)(2,1)S(1)}, bf16[256,1152]{1,0:T(8,128)(2,1)S(1)}, u32[]{:S(2)}, u32[]{:S(2)}) collective-permute-start(bf16[256,1152]{1,0:T(8,128)(2,1)S(1)} %get-tuple-element.42.refs_5_), channel_id=1, source_target_pairs={{0,64},{32,97},{2,66},{34,99},{4,68},{36,101},{6,70},{38,103},{64,... | collective-permute-start | bytes 1769480 | tf_op jit(solution)/shard_map/ppermute | solution.py:45
  51.8 16.0 %collective-permute-start.13 = (bf16[256,1152]{1,0:T(8,128)(2,1)S(1)}, bf16[256,1152]{1,0:T(8,128)(2,1)S(1)}, u32[]{:S(2)}, u32[]{:S(2)}) collective-permute-start(bf16[256,1152]{1,0:T(8,128)(2,1)S(1)} %get-tuple-element.49), channel_id=1, source_target_pairs={{0,14},{32,58},{2,12},{34,56},{4,10},{36,62},{6,8},{38,60},{64,78}... | collective-permute-start | bytes 1769480 | tf_op jit(solution)/shard_map/ppermute | solution.py:45
  55.3 13.6 %collective-permute-start.14 = (bf16[256,1152]{1,0:T(8,128)(2,1)S(1)}, bf16[256,1152]{1,0:T(8,128)(2,1)S(1)}, u32[]{:S(2)}, u32[]{:S(2)}) collective-permute-start(bf16[256,1152]{1,0:T(8,128)(2,1)S(1)} %get-tuple-element.50), channel_id=1, source_target_pairs={{0,6},{32,34},{2,4},{34,32},{4,2},{36,38},{6,0},{38,36},{64,70},{9... | collective-permute-start | bytes 1769480 | tf_op jit(solution)/shard_map/ppermute | solution.py:45
  58.3 11.9 %collective-permute-start.16 = (bf16[256,1152]{1,0:T(8,128)(2,1)S(1)}, bf16[256,1152]{1,0:T(8,128)(2,1)S(1)}, u32[]{:S(2)}, u32[]{:S(2)}) collective-permute-start(bf16[256,1152]{1,0:T(8,128)(2,1)S(1)} %get-tuple-element.43.refs_9_), channel_id=1, source_target_pairs={{0,8},{32,56},{2,10},{34,58},{4,12},{36,60},{6,14},{38,62},{64,72}... | collective-permute-start | bytes 1769480 | tf_op jit(solution)/shard_map/ppermute | solution.py:45
  65.6 9.4 %collective-permute-start.18 = (bf16[128,1152]{1,0:T(8,128)(2,1)S(1)}, bf16[128,1152]{1,0:T(8,128)(2,1)S(1)}, u32[]{:S(2)}, u32[]{:S(2)}) collective-permute-start(bf16[128,1152]{1,0:T(8,128)(2,1)S(1)} %get-tuple-element.54), channel_id=1, source_target_pairs={{0,32},{32,0},{1,33},{33,1},{2,34},{34,2},{3,35},{35,3},{4,36},{36... | collective-permute-start | bytes 884744 | tf_op jit(solution)/shard_map/ppermute | solution.py:49
  65.8 9.3 %collective-permute-start.12 = (bf16[128,1152]{1,0:T(8,128)(2,1)S(1)}, bf16[128,1152]{1,0:T(8,128)(2,1)S(1)}, u32[]{:S(2)}, u32[]{:S(2)}) collective-permute-start(bf16[128,1152]{1,0:T(8,128)(2,1)S(1)} %get-tuple-element.47), channel_id=1, source_target_pairs={{0,8},{32,56},{2,10},{34,58},{4,12},{36,60},{6,14},{38,62},{64,72}... | collective-permute-start | bytes 884744 | tf_op jit(solution)/shard_map/ppermute | solution.py:45
  69.1 13.4 %copy-start.1 = (bf16[128,1152]{1,0:T(8,128)(2,1)S(1)}, bf16[128,1152]{1,0:T(8,128)(2,1)}, u32[]{:S(2)}) copy-start(bf16[128,1152]{1,0:T(8,128)(2,1)} %refs_2_.1) | copy-start | bytes 884740
  69.1 13.4 %copy-start.3 = (bf16[128,1152]{1,0:T(8,128)(2,1)S(1)}, bf16[128,1152]{1,0:T(8,128)(2,1)}, u32[]{:S(2)}) copy-start(bf16[128,1152]{1,0:T(8,128)(2,1)} %refs_3_.1) | copy-start | bytes 884740
  69.1 7.2 %collective-permute-start.15 = (bf16[128,1152]{1,0:T(8,128)(2,1)S(1)}, bf16[128,1152]{1,0:T(8,128)(2,1)S(1)}, u32[]{:S(2)}, u32[]{:S(2)}) collective-permute-start(bf16[128,1152]{1,0:T(8,128)(2,1)S(1)} %get-tuple-element.51), channel_id=1, source_target_pairs={{0,64},{32,97},{2,66},{34,99},{4,68},{36,101},{6,70},{38,103},{64,... | collective-permute-start | bytes 884744 | tf_op jit(solution)/shard_map/ppermute | solution.py:45
  70.4 5.9 %collective-permute-start.17 = (bf16[128,1152]{1,0:T(8,128)(2,1)S(1)}, bf16[128,1152]{1,0:T(8,128)(2,1)S(1)}, u32[]{:S(2)}, u32[]{:S(2)}) collective-permute-start(bf16[128,1152]{1,0:T(8,128)(2,1)S(1)} %get-tuple-element.53), channel_id=1, source_target_pairs={{0,6},{32,34},{2,4},{34,32},{4,2},{36,38},{6,0},{38,36},{64,70},{9... | collective-permute-start | bytes 884744 | tf_op jit(solution)/shard_map/ppermute | solution.py:45
  70.5 8.2 %collective-permute-start.19 = (bf16[128,1152]{1,0:T(8,128)(2,1)S(1)}, bf16[128,1152]{1,0:T(8,128)(2,1)S(1)}, u32[]{:S(2)}, u32[]{:S(2)}) collective-permute-start(bf16[128,1152]{1,0:T(8,128)(2,1)S(1)} %get-tuple-element.55), channel_id=1, source_target_pairs={{0,40},{32,24},{2,42},{34,26},{4,44},{36,28},{6,46},{38,30},{64,10... | collective-permute-start | bytes 884744 | tf_op jit(solution)/shard_map/ppermute | solution.py:45
  75.0 6.3 %collective-permute-start.20 = (bf16[128,1152]{1,0:T(8,128)(2,1)S(1)}, bf16[128,1152]{1,0:T(8,128)(2,1)S(1)}, u32[]{:S(2)}, u32[]{:S(2)}) collective-permute-start(bf16[128,1152]{1,0:T(8,128)(2,1)S(1)} %get-tuple-element.56), channel_id=1, source_target_pairs={{0,96},{32,65},{2,98},{34,67},{4,100},{36,69},{6,102},{38,71},{64,... | collective-permute-start | bytes 884744 | tf_op jit(solution)/shard_map/ppermute | solution.py:45
  75.1 7.4 %collective-permute-start.21 = (bf16[128,1152]{1,0:T(8,128)(2,1)S(1)}, bf16[128,1152]{1,0:T(8,128)(2,1)S(1)}, u32[]{:S(2)}, u32[]{:S(2)}) collective-permute-start(bf16[128,1152]{1,0:T(8,128)(2,1)S(1)} %get-tuple-element.57), channel_id=1, source_target_pairs={{0,38},{32,2},{2,36},{34,0},{4,34},{36,6},{6,32},{38,4},{64,102},{... | collective-permute-start | bytes 884744 | tf_op jit(solution)/shard_map/ppermute | solution.py:45

commit v12 on v11

--- a/solution.py
+++ b/solution.py
@@ -99,35 +99,46 @@
     return total
 
 
-def sums_kernel(count, n_theirs, n_starts, n_after, diagonal, affine, *refs):
-    mine, refs = refs[:count], refs[count:]
-    theirs, refs = refs[:n_theirs], refs[n_theirs:]
-    starts, refs = refs[:n_starts], refs[n_starts + n_after :]
-    sums, coupling = refs[:-1], refs[-1]
-    for k in range(count):
-        start = starts[k][...] if starts else None
-        total = accumulate(affine, mine[k][...], theirs, coupling, start, diagonal and k == 0)
-        sums[k][...] = total.astype(sums[k].dtype)
-
-
-def sums_of(affine, mine, theirs, starts=(), after=(), kinds=None, diagonal=False, hides=True):
-    count, n_theirs, n_starts, n_after = len(mine), len(theirs), len(starts), len(after)
-    unit, width = mine[0].shape
-    against = sum(array.shape[0] for array in theirs)
-    kinds = kinds or [FULL] * count
+def sums_kernel(plan, n_inputs, n_after, diagonal, affine, *refs):
+    inputs, results, coupling = refs[:n_inputs], refs[n_inputs + n_after : -1], refs[-1]
+    for k, (mine, theirs, start) in enumerate(plan):
+        begin = None if start is None else inputs[start][...]
+        total = accumulate(
+            affine, inputs[mine][...], [inputs[n] for n in theirs], coupling, begin, diagonal and k == 0
+        )
+        results[k][...] = total.astype(results[k].dtype)
+
+
+def sums_of(affine, jobs, after=(), kind=FULL, diagonal=False, hides=True):
+    inputs, plan, tiles, widest = [], [], 0, 0
+
+    def index(array):
+        for n, known in enumerate(inputs):
+            if known is array:
+                return n
+        inputs.append(array)
+        return len(inputs) - 1
+
+    unit, width = jobs[0][0].shape
+    for mine, theirs, start in jobs:
+        against = sum(array.shape[0] for array in theirs)
+        tiles, widest = tiles + against // unit, max(widest, against)
+        plan.append(
+            (index(mine), [index(array) for array in theirs], None if start is None else index(start))
+        )
     return pl.pallas_call(
-        functools.partial(sums_kernel, count, n_theirs, n_starts, n_after, diagonal),
-        out_shape=[jax.ShapeDtypeStruct((unit, width), kind) for kind in kinds],
-        in_specs=[SMEM] + [VMEM] * (count + n_theirs + n_starts) + [ANY] * n_after,
-        out_specs=[VMEM] * count,
-        scratch_shapes=[pltpu.VMEM((unit, against), HALF)],
+        functools.partial(sums_kernel, plan, len(inputs), len(after), diagonal),
+        out_shape=[jax.ShapeDtypeStruct((unit, width), kind)] * len(jobs),
+        in_specs=[SMEM] + [VMEM] * len(inputs) + [ANY] * len(after),
+        out_specs=[VMEM] * len(jobs),
+        scratch_shapes=[pltpu.VMEM((unit, widest), HALF)],
         cost_estimate=pl.CostEstimate(
-            flops=4 * count * unit * against * width if hides else 0,
-            bytes_accessed=8 * count * unit * width if hides else 0,
-            transcendentals=count * unit * against if hides else 0,
+            flops=4 * tiles * unit**2 * width if hides else 0,
+            bytes_accessed=8 * len(jobs) * unit * width if hides else 0,
+            transcendentals=tiles * unit**2 if hides else 0,
         ),
         compiler_params=PARAMS,
-    )(affine, *mine, *theirs, *starts, *after)
+    )(affine, *inputs, *after)
 
 
 def on_device(
@@ -185,25 +196,32 @@
     mine["xy"] = sent(mine["x"], "y")
     mine["yz"] = sent(mine["y"], "z")
     mine["zx"] = sent(mine["z"], "x")
-    def pick(units, ways):
-        return [units[way] for way in ways]
-
-    theirs_one = [own_theirs, stacked(ONE)]
     near = ("", *ONE)
-    sums = sums_of(affine, pick(mine, near), theirs_one, diagonal=True, hides=False)
-    theirs_two = [stacked(TWO, sums[:1])]
-    sums += sums_of(affine, pick(mine, TWO), theirs_one)
-    sums = dict(zip((*near, *TWO), sums, strict=True))
-
-    def parts_of(ways, kinds, after=()):
-        return sums_of(affine, pick(mine, ways), theirs_two, pick(sums, ways), after, kinds)
-
-    part_xyz, part_xy = parts_of(("xyz", "xy"), [HALF, HALF])
-    for_x = [sent(part_xy, "y")]
-    part_yz, part_zx = parts_of(("yz", "zx"), [HALF, HALF], [part_xy])
-    for_y = [sent(part_xyz, "zx"), sent(part_yz, "z")]
-    for_z = [sent(part_zx, "x")]
-    own_part, part_x, part_y, part_z = parts_of(near, [FULL] * 4, [part_zx])
+    one = [own_theirs, stacked(ONE)]
+    sums = sums_of(affine, [(mine[way], one, None) for way in near], diagonal=True, hides=False)
+    sums = dict(zip(near, sums, strict=True))
+    two = [stacked(TWO, [sums[""]])]
+    sums |= zip(TWO, sums_of(affine, [(mine[way], one, None) for way in TWO]), strict=True)
+
+    def parts_of(ways, after, kind=FULL):
+        return sums_of(affine, [(mine[way], two, sums[way]) for way in ways], after, kind)
+
+    def added(part, other):
+        (total,) = local(
+            lambda _, refs: [refs[0][...] + refs[1][...].astype(FULL)], [unit], [], [part, other]
+        )
+        return total
+
+    (part_xyz,) = parts_of(["xyz"], [], HALF)
+    for_yz = sent(part_xyz, "x")
+    part_xy, part_zx = parts_of(["xy", "zx"], [part_xyz], HALF)
+    for_x, for_z = sent(part_xy, "y"), sent(part_zx, "x")
+    (part_yz,) = parts_of(["yz"], [part_xy])
+    part_yz = added(part_yz, for_yz)
+    for_y = sent(part_yz, "z")
+    part_x, part_y, part_z = parts_of(ONE, [part_yz])
+    part_x, part_z = added(part_x, for_x), added(part_z, for_z)
+    from_x, from_z = sent(part_x, "x"), sent(part_z, "z")
 
     def halves(scalars, refs):
         core, total = scalars[0][0], refs[0]
@@ -217,21 +235,20 @@
         return found
 
     which = core.reshape(1)
-    own_here, own_there = local(halves, [shard_full, shard], [which], [own_part])
-    here, there = [own_here], [other_core(own_there)]
-    for way, part, added in (("x", part_x, for_x), ("y", part_y, for_y), ("z", part_z, for_z)):
-        mine_half, other_half = local(halves, [shard] * 2, [which], [part, *added])
-        here.append(sent(mine_half, way))
-        there.append(sent(other_half, way, True))
+    y_here, y_there = local(halves, [shard] * 2, [which], [part_y, for_y], [part_x, part_z])
+    (own_part,) = parts_of([""], [y_here])
+    y_here, y_there = sent(y_here, "y"), sent(y_there, "y", True)
+    here, there = local(
+        halves, [shard_full, shard], [which], [own_part, from_x, from_z], [y_there]
+    )
+    there = other_core(there)
 
     def finish(scalars, refs):
         first, multiplier = scalars[0][0] > 0, scalars[1][0]
-        raws, refs = refs[:2], refs[2:]
-        totals = []
-        for parts in (refs[: len(here)], refs[len(here) :]):
-            totals.append(sum([ref[...].astype(FULL) for ref in parts[1:]], parts[0][...].astype(FULL)))
+        here, there, y_here, y_there = [ref[...].astype(FULL) for ref in refs[2:]]
+        totals = (here + y_here, there + y_there)
         results = []
-        for k, raw in enumerate(raws):
+        for k, raw in enumerate(refs[:2]):
             unit, scale = unit_rows(raw[...])
             grad = multiplier * jnp.where(first, totals[k], totals[1 - k])
             results.append(scale * (grad - unit * jnp.sum(unit * grad, axis=1, keepdims=True)))
@@ -242,7 +259,7 @@
             finish,
             [shard_full] * 2,
             [first_flag, multiplier],
-            [picture_vectors_raw, caption_vectors_raw, *here, *there],
+            [picture_vectors_raw, caption_vectors_raw, here, there, y_here, y_there],
         )
     )
 

time: 84.4 us -> 81.8 us (0.969)
  waiting for transfers between devices: 19.6 us -> 13.5 us
  starting transfers between devices: 30.9 us -> 32.8 us
  Pallas kernels: 29 us -> 30.5 us
    ppermute x17 -> x15, waiting for transfers between devices: 19.6 us -> 13.5 us  [sent(): return lax.ppermute(value, FINE_AXES, pairs)]
    ppermute x5, starting transfers between devices: 4.56 us -> 7.38 us  [other_core(): return lax.ppermute(value, 'core', [(0, 1), (1, 0)])]
    pallas_call x5 -> x7, Pallas kernels: 25.9 us -> 27.4 us  [sums_of(): pl.pallas_call(functools.partial(sums_kernel, plan, len(inputs), len(afte...]
    ppermute x17 -> x15, starting transfers between devices: 26.3 us -> 25.5 us  [sent(): return lax.ppermute(value, FINE_AXES, pairs)]
    pallas_call x9 -> x10, Pallas kernels: 3.1 us -> 3.1 us  [local(): pl.pallas_call(kernel, out_shape=[jax.ShapeDtypeStruct(s, d) for s, d in...]
  transfers between devices with their start and end apart: 22 -> 20, of which waited for: 11 -> 9; matrix products, arithmetic and copies ran while one was open for 0% -> 0% of each run, Pallas kernels for 27% -> 32%
where the time goes in v12:
time: 81.8 us; the launch traced here: 81.6 us
  starting transfers between devices  32.8 us (40%)
  Pallas kernels  30.5 us (37%)
  waiting for transfers between devices  13.5 us (17%)
  between operations  2.75 us (3%)
  local copies, waits for them, and re-layouts  1.93 us (2%)
    pallas_call x7, Pallas kernels, sums_of(): pl.pallas_call(functools.partial(sums_kernel, plan, len(inputs), len(afte...  27.4 us
    ppermute x15, starting transfers between devices, sent(): return lax.ppermute(value, FINE_AXES, pairs)  25.5 us
    ppermute x15, waiting for transfers between devices, sent(): return lax.ppermute(value, FINE_AXES, pairs)  13.5 us
    ppermute x5, starting transfers between devices, other_core(): return lax.ppermute(value, 'core', [(0, 1), (1, 0)])  7.38 us
    pallas_call x10, Pallas kernels, local(): pl.pallas_call(kernel, out_shape=[jax.ShapeDtypeStruct(s, d) for s, d in...  3.1 us
    unnamed x8, local copies, waits for them, and re-layouts  1.93 us
  transfers between devices with their start and end apart: 20, of which 9 were waited for; matrix products, arithmetic and copies ran while one was open for 0% of the time, Pallas kernels for 32%

profile of v12, /device:TPU:1, one launch (start us, length us, event | category | flops | bytes accessed | tf_op | source)
XLA Modules:
  0.0 81.6 jit_solution(15885911607251563240)
XLA Ops:
  0.6 1.5 %collective-permute-start = (bf16[128,1152]{1,0:T(8,128)(2,1)}, bf16[128,1152]{1,0:T(8,128)(2,1)S(1)}, u32[]{:S(2)}, u32[]{:S(2)}) collective-permute-start(bf16[128,1152]{1,0:T(8,128)(2,1)} %refs_2_.1), channel_id=1, source_target_pairs={{0,32},{32,0},{1,33},{33,1},{2,34},{34,2},{3,35},{35,3},{4,36},{36... | collective-permute-start | bytes 884744 | tf_op jit(solution)/shard_map/ppermute | solution.py:49
  2.1 0.1 collective-permute-start.1
  2.2 1.0 %copy-done = bf16[128,1152]{1,0:T(8,128)(2,1)S(1)} copy-done((bf16[128,1152]{1,0:T(8,128)(2,1)S(1)}, bf16[128,1152]{1,0:T(8,128)(2,1)}, u32[]{:S(2)}) %copy-start) | copy-done | bytes 294936
  3.2 1.0 %copy-done.2 = bf16[128,1152]{1,0:T(8,128)(2,1)S(1)} copy-done((bf16[128,1152]{1,0:T(8,128)(2,1)S(1)}, bf16[128,1152]{1,0:T(8,128)(2,1)}, u32[]{:S(2)}) %copy-start.2) | copy-done | bytes 294936
  4.1 0.2 shard_map.68
  4.4 0.4 shard_map.69
  4.8 2.6 %collective-permute-start.2 = (bf16[256,1152]{1,0:T(8,128)(2,1)S(1)}, bf16[256,1152]{1,0:T(8,128)(2,1)S(1)}, u32[]{:S(2)}, u32[]{:S(2)}) collective-permute-start(bf16[256,1152]{1,0:T(8,128)(2,1)S(1)} %get-tuple-element.25.refs_0_), channel_id=1, source_target_pairs={{0,8},{32,56},{2,10},{34,58},{4,12},{36,60},{6,14},{38,62},{64,72}... | collective-permute-start | bytes 1769480 | tf_op jit(solution)/shard_map/ppermute | solution.py:45
  7.4 2.7 %collective-permute-start.5 = (bf16[256,1152]{1,0:T(8,128)(2,1)S(1)}, bf16[256,1152]{1,0:T(8,128)(2,1)S(1)}, u32[]{:S(2)}, u32[]{:S(2)}) collective-permute-start(bf16[256,1152]{1,0:T(8,128)(2,1)S(1)} %get-tuple-element.25.refs_0_), channel_id=1, source_target_pairs={{0,64},{32,97},{2,66},{34,99},{4,68},{36,101},{6,70},{38,103},{64,... | collective-permute-start | bytes 1769480 | tf_op jit(solution)/shard_map/ppermute | solution.py:45
  10.1 1.6 %collective-permute-start.7 = (bf16[256,1152]{1,0:T(8,128)(2,1)S(1)}, bf16[256,1152]{1,0:T(8,128)(2,1)S(1)}, u32[]{:S(2)}, u32[]{:S(2)}) collective-permute-start(bf16[256,1152]{1,0:T(8,128)(2,1)S(1)} %get-tuple-element.25.refs_0_), channel_id=1, source_target_pairs={{0,6},{32,34},{2,4},{34,32},{4,2},{36,38},{6,0},{38,36},{64,70},{9... | collective-permute-start | bytes 1769480 | tf_op jit(solution)/shard_map/ppermute | solution.py:45
  11.8 3.3 %collective-permute-done.2.refs_0_.refs_3_ = bf16[256,1152]{1,0:T(8,128)(2,1)S(1)} collective-permute-done((bf16[256,1152]{1,0:T(8,128)(2,1)S(1)}, bf16[256,1152]{1,0:T(8,128)(2,1)S(1)}, u32[]{:S(2)}, u32[]{:S(2)}) %collective-permute-start.2) | collective-permute-done | bytes 589856 | tf_op jit(solution)/shard_map/ppermute | solution.py:45
  15.1 2.6 %collective-permute-done.5.refs_1_.refs_4_.refs_3_ = bf16[256,1152]{1,0:T(8,128)(2,1)S(1)} collective-permute-done((bf16[256,1152]{1,0:T(8,128)(2,1)S(1)}, bf16[256,1152]{1,0:T(8,128)(2,1)S(1)}, u32[]{:S(2)}, u32[]{:S(2)}) %collective-permute-start.5) | collective-permute-done | bytes 589856 | tf_op jit(solution)/shard_map/ppermute | solution.py:45
  17.7 1.6 %collective-permute-done.7.refs_2_.refs_5_ = bf16[256,1152]{1,0:T(8,128)(2,1)S(1)} collective-permute-done((bf16[256,1152]{1,0:T(8,128)(2,1)S(1)}, bf16[256,1152]{1,0:T(8,128)(2,1)S(1)}, u32[]{:S(2)}, u32[]{:S(2)}) %collective-permute-start.7) | collective-permute-done | bytes 589856 | tf_op jit(solution)/shard_map/ppermute | solution.py:45
  19.3 0.1 shard_map.70
  19.5 1.0 %collective-permute-start.9 = (bf16[768,1152]{1,0:T(8,128)(2,1)S(1)}, bf16[768,1152]{1,0:T(8,128)(2,1)S(1)}, u32[]{:S(2)}, u32[]{:S(2)}) collective-permute-start(bf16[768,1152]{1,0:T(8,128)(2,1)S(1)} %shard_map.70), channel_id=1, source_target_pairs={{0,32},{32,0},{1,33},{33,1},{2,34},{34,2},{3,35},{35,3},{4,36},{36... | collective-permute-start | bytes 5308424 | tf_op jit(solution)/shard_map/ppermute | solution.py:49
  20.5 1.2 %collective-permute-start.3 = (bf16[256,1152]{1,0:T(8,128)(2,1)S(1)}, bf16[256,1152]{1,0:T(8,128)(2,1)S(1)}, u32[]{:S(2)}, u32[]{:S(2)}) collective-permute-start(bf16[256,1152]{1,0:T(8,128)(2,1)S(1)} %collective-permute-done.2.refs_0_.refs_3_), channel_id=1, source_target_pairs={{0,70},{32,99},{2,68},{34,97},{4,66},{36,103},{6,64},{38,101},{64,... | collective-permute-start | bytes 1769480 | tf_op jit(solution)/shard_map/ppermute | solution.py:45
  21.8 1.4 %collective-permute-start.4 = (bf16[256,1152]{1,0:T(8,128)(2,1)S(1)}, bf16[256,1152]{1,0:T(8,128)(2,1)S(1)}, u32[]{:S(2)}, u32[]{:S(2)}) collective-permute-start(bf16[256,1152]{1,0:T(8,128)(2,1)S(1)} %collective-permute-done.2.refs_0_.refs_3_), channel_id=1, source_target_pairs={{0,64},{32,97},{2,66},{34,99},{4,68},{36,101},{6,70},{38,103},{64,... | collective-permute-start | bytes 1769480 | tf_op jit(solution)/shard_map/ppermute | solution.py:45
  23.2 1.2 %collective-permute-start.6 = (bf16[256,1152]{1,0:T(8,128)(2,1)S(1)}, bf16[256,1152]{1,0:T(8,128)(2,1)S(1)}, u32[]{:S(2)}, u32[]{:S(2)}) collective-permute-start(bf16[256,1152]{1,0:T(8,128)(2,1)S(1)} %collective-permute-done.5.refs_1_.refs_4_.refs_3_), channel_id=1, source_target_pairs={{0,6},{32,34},{2,4},{34,32},{4,2},{36,38},{6,0},{38,36},{64,70},{9... | collective-permute-start | bytes 1769480 | tf_op jit(solution)/shard_map/ppermute | solution.py:45
  24.4 1.8 %collective-permute-start.8 = (bf16[256,1152]{1,0:T(8,128)(2,1)S(1)}, bf16[256,1152]{1,0:T(8,128)(2,1)S(1)}, u32[]{:S(2)}, u32[]{:S(2)}) collective-permute-start(bf16[256,1152]{1,0:T(8,128)(2,1)S(1)} %collective-permute-done.7.refs_2_.refs_5_), channel_id=1, source_target_pairs={{0,8},{32,56},{2,10},{34,58},{4,12},{36,60},{6,14},{38,62},{64,72}... | collective-permute-start | bytes 1769480 | tf_op jit(solution)/shard_map/ppermute | solution.py:45
  27.6 6.4 %shard_map.71 = (f32[256,1152]{1,0:T(8,128)S(1)}, f32[256,1152]{1,0:T(8,128)S(1)}, f32[256,1152]{1,0:T(8,128)S(1)}, f32[256,1152]{1,0:T(8,128)S(1)}) custom-call(f32[2]{0:T(128)S(1)} %pad_maximum_fusion.affine, bf16[256,1152]{1,0:T(8,128)(2,1)S(1)} %get-tuple-element.25.refs_0_, bf16[256,1152]{1,0:T(8,128)(2,1)S(1)} %get-tuple-element.26.refs_1_, ...), custom_call_target="tpu_custom_call" | custom-call | tf_op jit(solution)/shard_map/pallas_call | solution.py:129
  33.9 3.2 %collective-permute-done.4.refs_1_.refs_3_.refs_0_ = bf16[256,1152]{1,0:T(8,128)(2,1)S(1)} collective-permute-done((bf16[256,1152]{1,0:T(8,128)(2,1)S(1)}, bf16[256,1152]{1,0:T(8,128)(2,1)S(1)}, u32[]{:S(2)}, u32[]{:S(2)}) %collective-permute-start.4) | collective-permute-done | bytes 589856 | tf_op jit(solution)/shard_map/ppermute | solution.py:45
  37.1 0.8 %collective-permute-done.6.refs_2_.refs_4_.refs_0_ = bf16[256,1152]{1,0:T(8,128)(2,1)S(1)} collective-permute-done((bf16[256,1152]{1,0:T(8,128)(2,1)S(1)}, bf16[256,1152]{1,0:T(8,128)(2,1)S(1)}, u32[]{:S(2)}, u32[]{:S(2)}) %collective-permute-start.6) | collective-permute-done | bytes 589856 | tf_op jit(solution)/shard_map/ppermute | solution.py:45
  38.0 0.2 shard_map.72
  38.2 1.8 %collective-permute-start.10 = (bf16[1024,1152]{1,0:T(8,128)(2,1)S(1)}, bf16[1024,1152]{1,0:T(8,128)(2,1)S(1)}, u32[]{:S(2)}, u32[]{:S(2)}) collective-permute-start(bf16[1024,1152]{1,0:T(8,128)(2,1)S(1)} %shard_map.72), channel_id=1, source_target_pairs={{0,32},{32,0},{1,33},{33,1},{2,34},{34,2},{3,35},{35,3},{4,36},{36... | collective-permute-start | bytes 7077896 | tf_op jit(solution)/shard_map/ppermute | solution.py:49
  40.0 6.3 %shard_map.73 = (f32[256,1152]{1,0:T(8,128)S(1)}, f32[256,1152]{1,0:T(8,128)S(1)}, f32[256,1152]{1,0:T(8,128)S(1)}, f32[256,1152]{1,0:T(8,128)S(1)}) custom-call(f32[2]{0:T(128)S(1)} %pad_maximum_fusion.affine, bf16[256,1152]{1,0:T(8,128)(2,1)S(1)} %collective-permute-done.3.refs_0_, bf16[256,1152]{1,0:T(8,128)(2,1)S(1)} %get-tuple-element.26.refs_1_, ...), custom_call_target="tpu_custom_call" | custom-call | flops 4831838208 | bytes 9437184 | tf_op jit(solution)/shard_map/pallas_call | solution.py:129
  46.3 2.1 %shard_map.74.refs_5_ = bf16[256,1152]{1,0:T(8,128)(2,1)S(1)} custom-call(f32[2]{0:T(128)S(1)} %pad_maximum_fusion.affine, bf16[256,1152]{1,0:T(8,128)(2,1)S(1)} %collective-permute-done.3.refs_0_, bf16[1024,1152]{1,0:T(8,128)(2,1)S(1)} %collective-permute-done.10.refs_1_, f32[256,1152]{1,0:T(8,128)S(1)} %get-tuple-element.34.refs_2_), custom_call_target="tpu_custom_call" | custom-call | flops 1207959552 | bytes 2359296 | tf_op jit(solution)/shard_map/pallas_call | solution.py:129
  48.5 1.9 %collective-permute-start.11 = (bf16[256,1152]{1,0:T(8,128)(2,1)S(1)}, bf16[256,1152]{1,0:T(8,128)(2,1)S(1)}, u32[]{:S(2)}, u32[]{:S(2)}) collective-permute-start(bf16[256,1152]{1,0:T(8,128)(2,1)S(1)} %shard_map.74.refs_5_), channel_id=1, source_target_pairs={{0,8},{32,56},{2,10},{34,58},{4,12},{36,60},{6,14},{38,62},{64,72}... | collective-permute-start | bytes 1769480 | tf_op jit(solution)/shard_map/ppermute | solution.py:45
  50.3 3.5 %shard_map.75 = (bf16[256,1152]{1,0:T(8,128)(2,1)S(1)}, bf16[256,1152]{1,0:T(8,128)(2,1)S(1)}) custom-call(f32[2]{0:T(128)S(1)} %pad_maximum_fusion.affine, bf16[256,1152]{1,0:T(8,128)(2,1)S(1)} %collective-permute-done.4.refs_1_.refs_3_.refs_0_, bf16[1024,1152]{1,0:T(8,128)(2,1)S(1)} %collective-permute-done.10.refs_1_, ...), custom_call_target="tpu_custom_call" | custom-call | flops 2415919104 | bytes 4718592 | tf_op jit(solution)/shard_map/pallas_call | solution.py:129
  53.8 2.0 %collective-permute-start.13 = (bf16[256,1152]{1,0:T(8,128)(2,1)S(1)}, bf16[256,1152]{1,0:T(8,128)(2,1)S(1)}, u32[]{:S(2)}, u32[]{:S(2)}) collective-permute-start(bf16[256,1152]{1,0:T(8,128)(2,1)S(1)} %get-tuple-element.35.refs_3_), channel_id=1, source_target_pairs={{0,64},{32,97},{2,66},{34,99},{4,68},{36,101},{6,70},{38,103},{64,... | collective-permute-start | bytes 1769480 | tf_op jit(solution)/shard_map/ppermute | solution.py:45
  55.8 0.9 %collective-permute-start.14 = (bf16[256,1152]{1,0:T(8,128)(2,1)S(1)}, bf16[256,1152]{1,0:T(8,128)(2,1)S(1)}, u32[]{:S(2)}, u32[]{:S(2)}) collective-permute-start(bf16[256,1152]{1,0:T(8,128)(2,1)S(1)} %get-tuple-element.39), channel_id=1, source_target_pairs={{0,8},{32,56},{2,10},{34,58},{4,12},{36,60},{6,14},{38,62},{64,72}... | collective-permute-start | bytes 1769480 | tf_op jit(solution)/shard_map/ppermute | solution.py:45
  56.7 2.1 %shard_map.76.refs_0_ = f32[256,1152]{1,0:T(8,128)S(1)} custom-call(f32[2]{0:T(128)S(1)} %pad_maximum_fusion.affine, bf16[256,1152]{1,0:T(8,128)(2,1)S(1)} %collective-permute-done.6.refs_2_.refs_4_.refs_0_, bf16[1024,1152]{1,0:T(8,128)(2,1)S(1)} %collective-permute-done.10.refs_1_, f32[256,1152]{1,0:T(8,128)S(1)} %get-tuple-element.31.refs_2_, ...), custom_call_target="tpu_custom_call" | custom-call | flops 1207959552 | bytes 2359296 | tf_op jit(solution)/shard_map/pallas_call | solution.py:129
  58.8 0.1 shard_map.77.refs_7_
  58.9 0.3 collective-permute-start.12
  59.2 4.9 %shard_map.78 = (f32[256,1152]{1,0:T(8,128)S(1)}, f32[256,1152]{1,0:T(8,128)S(1)}, f32[256,1152]{1,0:T(8,128)S(1)}) custom-call(f32[2]{0:T(128)S(1)} %pad_maximum_fusion.affine, bf16[256,1152]{1,0:T(8,128)(2,1)S(1)} %collective-permute-done.2.refs_0_.refs_3_, bf16[1024,1152]{1,0:T(8,128)(2,1)S(1)} %collective-permute-done.10.refs_1_, ...), custom_call_target="tpu_custom_call" | custom-call | flops 3623878656 | bytes 7077888 | tf_op jit(solution)/shard_map/pallas_call | solution.py:129
  64.1 0.1 shard_map.79.refs_3_
  64.3 1.9 %collective-permute-start.15 = (bf16[256,1152]{1,0:T(8,128)(2,1)S(1)}, bf16[256,1152]{1,0:T(8,128)(2,1)S(1)}, u32[]{:S(2)}, u32[]{:S(2)}) collective-permute-start(bf16[256,1152]{1,0:T(8,128)(2,1)S(1)} %shard_map.79.refs_3_), channel_id=1, source_target_pairs={{0,8},{32,56},{2,10},{34,58},{4,12},{36,60},{6,14},{38,62},{64,72}... | collective-permute-start | bytes 1769480 | tf_op jit(solution)/shard_map/ppermute | solution.py:45
  66.2 0.1 shard_map.80.refs_4_
  66.3 1.5 %collective-permute-start.16 = (bf16[256,1152]{1,0:T(8,128)(2,1)S(1)}, bf16[256,1152]{1,0:T(8,128)(2,1)S(1)}, u32[]{:S(2)}, u32[]{:S(2)}) collective-permute-start(bf16[256,1152]{1,0:T(8,128)(2,1)S(1)} %shard_map.80.refs_4_), channel_id=1, source_target_pairs={{0,6},{32,34},{2,4},{34,32},{4,2},{36,38},{6,0},{38,36},{64,70},{9... | collective-permute-start | bytes 1769480 | tf_op jit(solution)/shard_map/ppermute | solution.py:45
  67.8 0.5 collective-permute-done.12.refs_2_
  68.3 0.1 shard_map.81
  68.4 3.5 %collective-permute-start.17 = (bf16[128,1152]{1,0:T(8,128)(2,1)S(1)}, bf16[128,1152]{1,0:T(8,128)(2,1)S(1)}, u32[]{:S(2)}, u32[]{:S(2)}) collective-permute-start(bf16[128,1152]{1,0:T(8,128)(2,1)S(1)} %get-tuple-element.41), channel_id=1, source_target_pairs={{0,96},{32,65},{2,98},{34,67},{4,100},{36,69},{6,102},{38,71},{64,... | collective-permute-start | bytes 884744 | tf_op jit(solution)/shard_map/ppermute | solution.py:45
  71.9 0.8 collective-permute-start.19
  72.7 2.1 %shard_map.82.refs_1_ = f32[256,1152]{1,0:T(8,128)S(1)} custom-call(f32[2]{0:T(128)S(1)} %pad_maximum_fusion.affine, bf16[256,1152]{1,0:T(8,128)(2,1)S(1)} %get-tuple-element.25.refs_0_, bf16[1024,1152]{1,0:T(8,128)(2,1)S(1)} %collective-permute-done.10.refs_1_, f32[256,1152]{1,0:T(8,128)S(1)} %get-tuple-element.27.refs_4_.refs_2_, ...), custom_call_target="tpu_custom_call" | custom-call | flops 1207959552 | bytes 2359296 | tf_op jit(solution)/shard_map/pallas_call | solution.py:129
  74.9 0.5 collective-permute-done.16.refs_3_
  75.4 0.2 collective-permute-done.17.refs_4_.refs_7_
  75.6 0.2 shard_map.83
  75.7 2.9 %collective-permute-start.18 = (bf16[128,1152]{1,0:T(8,128)(2,1)S(1)}, bf16[128,1152]{1,0:T(8,128)(2,1)S(1)}, u32[]{:S(2)}, u32[]{:S(2)}) collective-permute-start(bf16[128,1152]{1,0:T(8,128)(2,1)S(1)} %get-tuple-element.43), channel_id=1, source_target_pairs={{0,32},{32,0},{1,33},{33,1},{2,34},{34,2},{3,35},{35,3},{4,36},{36... | collective-permute-start | bytes 884744 | tf_op jit(solution)/shard_map/ppermute | solution.py:49
  79.3 0.7 collective-permute-done.19.refs_6_
  80.0 1.6 %shard_map.84 = (f32[128,1152]{1,0:T(8,128)}, f32[128,1152]{1,0:T(8,128)}) custom-call(f32[1]{0:T(128)} %bitcast.refs_0_, f32[1]{0:T(128)S(6)} %div.3.refs_1_, bf16[128,1152]{1,0:T(8,128)(2,1)S(1)} %copy-done.1, bf16[128,1152]{1,0:T(8,128)(2,1)S(1)} %copy-done.3, f32[128,1152]{1,0:T(8,128)S(1)} %get-tuple-element.42.refs_4_, ...), custom_call_target="tpu_custom_call" | custom-call | tf_op jit(solution)/shard_map/pallas_call | solution.py:73
  (18 shorter events, 0.2 us)
Async XLA Ops:
  0.6 3.7 %collective-permute-start = (bf16[128,1152]{1,0:T(8,128)(2,1)}, bf16[128,1152]{1,0:T(8,128)(2,1)S(1)}, u32[]{:S(2)}, u32[]{:S(2)}) collective-permute-start(bf16[128,1152]{1,0:T(8,128)(2,1)} %refs_2_.1), channel_id=1, source_target_pairs={{0,32},{32,0},{1,33},{33,1},{2,34},{34,2},{3,35},{35,3},{4,36},{36... | collective-permute-start | bytes 884744 | tf_op jit(solution)/shard_map/ppermute | solution.py:49
  2.1 2.3 %collective-permute-start.1 = (bf16[128,1152]{1,0:T(8,128)(2,1)}, bf16[128,1152]{1,0:T(8,128)(2,1)S(1)}, u32[]{:S(2)}, u32[]{:S(2)}) collective-permute-start(bf16[128,1152]{1,0:T(8,128)(2,1)} %refs_3_.1), channel_id=1, source_target_pairs={{0,32},{32,0},{1,33},{33,1},{2,34},{34,2},{3,35},{35,3},{4,36},{36... | collective-permute-start | bytes 884744 | tf_op jit(solution)/shard_map/ppermute | solution.py:49
  2.2 1.0 %copy-start = (bf16[128,1152]{1,0:T(8,128)(2,1)S(1)}, bf16[128,1152]{1,0:T(8,128)(2,1)}, u32[]{:S(2)}) copy-start(bf16[128,1152]{1,0:T(8,128)(2,1)} %refs_2_.1) | copy-start | bytes 884740
  3.2 1.0 %copy-start.2 = (bf16[128,1152]{1,0:T(8,128)(2,1)S(1)}, bf16[128,1152]{1,0:T(8,128)(2,1)}, u32[]{:S(2)}) copy-start(bf16[128,1152]{1,0:T(8,128)(2,1)} %refs_3_.1) | copy-start | bytes 884740
  4.8 10.3 %collective-permute-start.2 = (bf16[256,1152]{1,0:T(8,128)(2,1)S(1)}, bf16[256,1152]{1,0:T(8,128)(2,1)S(1)}, u32[]{:S(2)}, u32[]{:S(2)}) collective-permute-start(bf16[256,1152]{1,0:T(8,128)(2,1)S(1)} %get-tuple-element.25.refs_0_), channel_id=1, source_target_pairs={{0,8},{32,56},{2,10},{34,58},{4,12},{36,60},{6,14},{38,62},{64,72}... | collective-permute-start | bytes 1769480 | tf_op jit(solution)/shard_map/ppermute | solution.py:45
  7.4 10.3 %collective-permute-start.5 = (bf16[256,1152]{1,0:T(8,128)(2,1)S(1)}, bf16[256,1152]{1,0:T(8,128)(2,1)S(1)}, u32[]{:S(2)}, u32[]{:S(2)}) collective-permute-start(bf16[256,1152]{1,0:T(8,128)(2,1)S(1)} %get-tuple-element.25.refs_0_), channel_id=1, source_target_pairs={{0,64},{32,97},{2,66},{34,99},{4,68},{36,101},{6,70},{38,103},{64,... | collective-permute-start | bytes 1769480 | tf_op jit(solution)/shard_map/ppermute | solution.py:45
  10.1 9.2 %collective-permute-start.7 = (bf16[256,1152]{1,0:T(8,128)(2,1)S(1)}, bf16[256,1152]{1,0:T(8,128)(2,1)S(1)}, u32[]{:S(2)}, u32[]{:S(2)}) collective-permute-start(bf16[256,1152]{1,0:T(8,128)(2,1)S(1)} %get-tuple-element.25.refs_0_), channel_id=1, source_target_pairs={{0,6},{32,34},{2,4},{34,32},{4,2},{36,38},{6,0},{38,36},{64,70},{9... | collective-permute-start | bytes 1769480 | tf_op jit(solution)/shard_map/ppermute | solution.py:45
  19.5 8.1 %collective-permute-start.9 = (bf16[768,1152]{1,0:T(8,128)(2,1)S(1)}, bf16[768,1152]{1,0:T(8,128)(2,1)S(1)}, u32[]{:S(2)}, u32[]{:S(2)}) collective-permute-start(bf16[768,1152]{1,0:T(8,128)(2,1)S(1)} %shard_map.70), channel_id=1, source_target_pairs={{0,32},{32,0},{1,33},{33,1},{2,34},{34,2},{3,35},{35,3},{4,36},{36... | collective-permute-start | bytes 5308424 | tf_op jit(solution)/shard_map/ppermute | solution.py:49
  20.5 13.4 %collective-permute-start.3 = (bf16[256,1152]{1,0:T(8,128)(2,1)S(1)}, bf16[256,1152]{1,0:T(8,128)(2,1)S(1)}, u32[]{:S(2)}, u32[]{:S(2)}) collective-permute-start(bf16[256,1152]{1,0:T(8,128)(2,1)S(1)} %collective-permute-done.2.refs_0_.refs_3_), channel_id=1, source_target_pairs={{0,70},{32,99},{2,68},{34,97},{4,66},{36,103},{6,64},{38,101},{64,... | collective-permute-start | bytes 1769480 | tf_op jit(solution)/shard_map/ppermute | solution.py:45
  21.8 15.4 %collective-permute-start.4 = (bf16[256,1152]{1,0:T(8,128)(2,1)S(1)}, bf16[256,1152]{1,0:T(8,128)(2,1)S(1)}, u32[]{:S(2)}, u32[]{:S(2)}) collective-permute-start(bf16[256,1152]{1,0:T(8,128)(2,1)S(1)} %collective-permute-done.2.refs_0_.refs_3_), channel_id=1, source_target_pairs={{0,64},{32,97},{2,66},{34,99},{4,68},{36,101},{6,70},{38,103},{64,... | collective-permute-start | bytes 1769480 | tf_op jit(solution)/shard_map/ppermute | solution.py:45
  23.2 14.8 %collective-permute-start.6 = (bf16[256,1152]{1,0:T(8,128)(2,1)S(1)}, bf16[256,1152]{1,0:T(8,128)(2,1)S(1)}, u32[]{:S(2)}, u32[]{:S(2)}) collective-permute-start(bf16[256,1152]{1,0:T(8,128)(2,1)S(1)} %collective-permute-done.5.refs_1_.refs_4_.refs_3_), channel_id=1, source_target_pairs={{0,6},{32,34},{2,4},{34,32},{4,2},{36,38},{6,0},{38,36},{64,70},{9... | collective-permute-start | bytes 1769480 | tf_op jit(solution)/shard_map/ppermute | solution.py:45
  24.4 13.6 %collective-permute-start.8 = (bf16[256,1152]{1,0:T(8,128)(2,1)S(1)}, bf16[256,1152]{1,0:T(8,128)(2,1)S(1)}, u32[]{:S(2)}, u32[]{:S(2)}) collective-permute-start(bf16[256,1152]{1,0:T(8,128)(2,1)S(1)} %collective-permute-done.7.refs_2_.refs_5_), channel_id=1, source_target_pairs={{0,8},{32,56},{2,10},{34,58},{4,12},{36,60},{6,14},{38,62},{64,72}... | collective-permute-start | bytes 1769480 | tf_op jit(solution)/shard_map/ppermute | solution.py:45
  38.2 8.2 %collective-permute-start.10 = (bf16[1024,1152]{1,0:T(8,128)(2,1)S(1)}, bf16[1024,1152]{1,0:T(8,128)(2,1)S(1)}, u32[]{:S(2)}, u32[]{:S(2)}) collective-permute-start(bf16[1024,1152]{1,0:T(8,128)(2,1)S(1)} %shard_map.72), channel_id=1, source_target_pairs={{0,32},{32,0},{1,33},{33,1},{2,34},{34,2},{3,35},{35,3},{4,36},{36... | collective-permute-start | bytes 7077896 | tf_op jit(solution)/shard_map/ppermute | solution.py:49
  48.5 10.3 %collective-permute-start.11 = (bf16[256,1152]{1,0:T(8,128)(2,1)S(1)}, bf16[256,1152]{1,0:T(8,128)(2,1)S(1)}, u32[]{:S(2)}, u32[]{:S(2)}) collective-permute-start(bf16[256,1152]{1,0:T(8,128)(2,1)S(1)} %shard_map.74.refs_5_), channel_id=1, source_target_pairs={{0,8},{32,56},{2,10},{34,58},{4,12},{36,60},{6,14},{38,62},{64,72}... | collective-permute-start | bytes 1769480 | tf_op jit(solution)/shard_map/ppermute | solution.py:45
  53.8 10.3 %collective-permute-start.13 = (bf16[256,1152]{1,0:T(8,128)(2,1)S(1)}, bf16[256,1152]{1,0:T(8,128)(2,1)S(1)}, u32[]{:S(2)}, u32[]{:S(2)}) collective-permute-start(bf16[256,1152]{1,0:T(8,128)(2,1)S(1)} %get-tuple-element.35.refs_3_), channel_id=1, source_target_pairs={{0,64},{32,97},{2,66},{34,99},{4,68},{36,101},{6,70},{38,103},{64,... | collective-permute-start | bytes 1769480 | tf_op jit(solution)/shard_map/ppermute | solution.py:45
  55.8 10.4 %collective-permute-start.14 = (bf16[256,1152]{1,0:T(8,128)(2,1)S(1)}, bf16[256,1152]{1,0:T(8,128)(2,1)S(1)}, u32[]{:S(2)}, u32[]{:S(2)}) collective-permute-start(bf16[256,1152]{1,0:T(8,128)(2,1)S(1)} %get-tuple-element.39), channel_id=1, source_target_pairs={{0,8},{32,56},{2,10},{34,58},{4,12},{36,60},{6,14},{38,62},{64,72}... | collective-permute-start | bytes 1769480 | tf_op jit(solution)/shard_map/ppermute | solution.py:45
  58.9 9.3 %collective-permute-start.12 = (bf16[256,1152]{1,0:T(8,128)(2,1)S(1)}, bf16[256,1152]{1,0:T(8,128)(2,1)S(1)}, u32[]{:S(2)}, u32[]{:S(2)}) collective-permute-start(bf16[256,1152]{1,0:T(8,128)(2,1)S(1)} %shard_map.77.refs_7_), channel_id=1, source_target_pairs={{0,6},{32,34},{2,4},{34,32},{4,2},{36,38},{6,0},{38,36},{64,70},{9... | collective-permute-start | bytes 1769480 | tf_op jit(solution)/shard_map/ppermute | solution.py:45
  64.3 10.6 %collective-permute-start.15 = (bf16[256,1152]{1,0:T(8,128)(2,1)S(1)}, bf16[256,1152]{1,0:T(8,128)(2,1)S(1)}, u32[]{:S(2)}, u32[]{:S(2)}) collective-permute-start(bf16[256,1152]{1,0:T(8,128)(2,1)S(1)} %shard_map.79.refs_3_), channel_id=1, source_target_pairs={{0,8},{32,56},{2,10},{34,58},{4,12},{36,60},{6,14},{38,62},{64,72}... | collective-permute-start | bytes 1769480 | tf_op jit(solution)/shard_map/ppermute | solution.py:45
  66.3 9.1 %collective-permute-start.16 = (bf16[256,1152]{1,0:T(8,128)(2,1)S(1)}, bf16[256,1152]{1,0:T(8,128)(2,1)S(1)}, u32[]{:S(2)}, u32[]{:S(2)}) collective-permute-start(bf16[256,1152]{1,0:T(8,128)(2,1)S(1)} %shard_map.80.refs_4_), channel_id=1, source_target_pairs={{0,6},{32,34},{2,4},{34,32},{4,2},{36,38},{6,0},{38,36},{64,70},{9... | collective-permute-start | bytes 1769480 | tf_op jit(solution)/shard_map/ppermute | solution.py:45
  68.4 7.2 %collective-permute-start.17 = (bf16[128,1152]{1,0:T(8,128)(2,1)S(1)}, bf16[128,1152]{1,0:T(8,128)(2,1)S(1)}, u32[]{:S(2)}, u32[]{:S(2)}) collective-permute-start(bf16[128,1152]{1,0:T(8,128)(2,1)S(1)} %get-tuple-element.41), channel_id=1, source_target_pairs={{0,96},{32,65},{2,98},{34,67},{4,100},{36,69},{6,102},{38,71},{64,... | collective-permute-start | bytes 884744 | tf_op jit(solution)/shard_map/ppermute | solution.py:45
  71.9 8.1 %collective-permute-start.19 = (bf16[128,1152]{1,0:T(8,128)(2,1)S(1)}, bf16[128,1152]{1,0:T(8,128)(2,1)S(1)}, u32[]{:S(2)}, u32[]{:S(2)}) collective-permute-start(bf16[128,1152]{1,0:T(8,128)(2,1)S(1)} %get-tuple-element.40.refs_3_), channel_id=1, source_target_pairs={{0,64},{32,97},{2,66},{34,99},{4,68},{36,101},{6,70},{38,103},{64,... | collective-permute-start | bytes 884744 | tf_op jit(solution)/shard_map/ppermute | solution.py:45
  74.8 5.2 %copy-start.1 = (bf16[128,1152]{1,0:T(8,128)(2,1)S(1)}, bf16[128,1152]{1,0:T(8,128)(2,1)}, u32[]{:S(2)}) copy-start(bf16[128,1152]{1,0:T(8,128)(2,1)} %refs_2_.1) | copy-start | bytes 884740
  74.8 5.2 %copy-start.3 = (bf16[128,1152]{1,0:T(8,128)(2,1)S(1)}, bf16[128,1152]{1,0:T(8,128)(2,1)}, u32[]{:S(2)}) copy-start(bf16[128,1152]{1,0:T(8,128)(2,1)} %refs_3_.1) | copy-start | bytes 884740
  75.7 4.2 %collective-permute-start.18 = (bf16[128,1152]{1,0:T(8,128)(2,1)S(1)}, bf16[128,1152]{1,0:T(8,128)(2,1)S(1)}, u32[]{:S(2)}, u32[]{:S(2)}) collective-permute-start(bf16[128,1152]{1,0:T(8,128)(2,1)S(1)} %get-tuple-element.43), channel_id=1, source_target_pairs={{0,32},{32,0},{1,33},{33,1},{2,34},{34,2},{3,35},{35,3},{4,36},{36... | collective-permute-start | bytes 884744 | tf_op jit(solution)/shard_map/ppermute | solution.py:49

commit v13 on v12

--- a/solution.py
+++ b/solution.py
@@ -22,8 +22,7 @@
 ANY = pl.BlockSpec(memory_space=pl.ANY)
 PARAMS = pltpu.CompilerParams(vmem_limit_bytes=VMEM_BYTES)
 
-ONE = ("x", "y", "z")
-TWO = ("xyz", "xy", "yz", "zx")
+ONE = ("x", "z", "y")
 
 
 def place(core, x, y, z):
@@ -200,8 +199,11 @@
     one = [own_theirs, stacked(ONE)]
     sums = sums_of(affine, [(mine[way], one, None) for way in near], diagonal=True, hides=False)
     sums = dict(zip(near, sums, strict=True))
-    two = [stacked(TWO, [sums[""]])]
-    sums |= zip(TWO, sums_of(affine, [(mine[way], one, None) for way in TWO]), strict=True)
+    zx_there = stacked(["zx"], [sums[""]])
+    (sums["zx"],) = sums_of(affine, [(mine["zx"], one, None)], [sums[""]])
+    two = [zx_there, stacked(("xyz", "xy", "yz"), [sums["zx"], zx_there])]
+    jobs = [(mine["xyz"], one, None), (mine["xy"], one, None)]
+    sums["xyz"], sums["xy"] = sums_of(affine, jobs, [sums["zx"]])
 
     def parts_of(ways, after, kind=FULL):
         return sums_of(affine, [(mine[way], two, sums[way]) for way in ways], after, kind)
@@ -216,10 +218,10 @@
     for_yz = sent(part_xyz, "x")
     part_xy, part_zx = parts_of(["xy", "zx"], [part_xyz], HALF)
     for_x, for_z = sent(part_xy, "y"), sent(part_zx, "x")
-    (part_yz,) = parts_of(["yz"], [part_xy])
+    (part_yz,) = sums_of(affine, [(mine["yz"], one + two, None)], [part_xy])
     part_yz = added(part_yz, for_yz)
     for_y = sent(part_yz, "z")
-    part_x, part_y, part_z = parts_of(ONE, [part_yz])
+    part_x, part_z, part_y = parts_of(ONE, [part_yz])
     part_x, part_z = added(part_x, for_x), added(part_z, for_z)
     from_x, from_z = sent(part_x, "x"), sent(part_z, "z")
 

time: 81.8 us -> 82.4 us (level)
  waiting for transfers between devices: 13.5 us -> 15.6 us
  starting transfers between devices: 32.8 us -> 30.7 us
    ppermute x15, waiting for transfers between devices: 13.5 us -> 15.1 us  [sent(): return lax.ppermute(value, FINE_AXES, pairs)]
    ppermute x5 -> x6, starting transfers between devices: 7.38 us -> 6.03 us  [other_core(): return lax.ppermute(value, 'core', [(0, 1), (1, 0)])]
    pallas_call x7 -> x8, Pallas kernels: 27.4 us -> 28 us  [sums_of(): pl.pallas_call(functools.partial(sums_kernel, plan, len(inputs), len(afte...]
    pallas_call x10 -> x11, Pallas kernels: 3.1 us -> 3.06 us  [local(): pl.pallas_call(kernel, out_shape=[jax.ShapeDtypeStruct(s, d) for s, d in...]
  transfers between devices with their start and end apart: 20 -> 21, of which waited for: 9 -> 7; matrix products, arithmetic and copies ran while one was open for 0% -> 0% of each run, Pallas kernels for 32% -> 33%
where the time goes in v13:
time: 82.4 us; the launch traced here: 82.2 us
  Pallas kernels  31.1 us (38%)
  starting transfers between devices  30.7 us (37%)
  waiting for transfers between devices  15.6 us (19%)
  between operations  2.81 us (3%)
  local copies, waits for them, and re-layouts  1.93 us (2%)
    pallas_call x8, Pallas kernels, sums_of(): pl.pallas_call(functools.partial(sums_kernel, plan, len(inputs), len(afte...  28 us
    ppermute x15, starting transfers between devices, sent(): return lax.ppermute(value, FINE_AXES, pairs)  24.7 us
    ppermute x15, waiting for transfers between devices, sent(): return lax.ppermute(value, FINE_AXES, pairs)  15.1 us
    ppermute x6, starting transfers between devices, other_core(): return lax.ppermute(value, 'core', [(0, 1), (1, 0)])  6.03 us
    pallas_call x11, Pallas kernels, local(): pl.pallas_call(kernel, out_shape=[jax.ShapeDtypeStruct(s, d) for s, d in...  3.06 us
    unnamed x8, local copies, waits for them, and re-layouts  1.93 us
  transfers between devices with their start and end apart: 21, of which 7 were waited for; matrix products, arithmetic and copies ran while one was open for 0% of the time, Pallas kernels for 33%

profile of v13, /device:TPU:1, one launch (start us, length us, event | category | flops | bytes accessed | tf_op | source)
XLA Modules:
  0.0 82.2 jit_solution(6219720037155775779)
XLA Ops:
  0.6 1.5 %collective-permute-start = (bf16[128,1152]{1,0:T(8,128)(2,1)}, bf16[128,1152]{1,0:T(8,128)(2,1)S(1)}, u32[]{:S(2)}, u32[]{:S(2)}) collective-permute-start(bf16[128,1152]{1,0:T(8,128)(2,1)} %refs_2_.1), channel_id=1, source_target_pairs={{0,32},{32,0},{1,33},{33,1},{2,34},{34,2},{3,35},{35,3},{4,36},{36... | collective-permute-start | bytes 884744 | tf_op jit(solution)/shard_map/ppermute | solution.py:48
  2.1 0.1 collective-permute-start.1
  2.2 1.0 %copy-done = bf16[128,1152]{1,0:T(8,128)(2,1)S(1)} copy-done((bf16[128,1152]{1,0:T(8,128)(2,1)S(1)}, bf16[128,1152]{1,0:T(8,128)(2,1)}, u32[]{:S(2)}) %copy-start) | copy-done | bytes 294936
  3.2 1.0 %copy-done.2 = bf16[128,1152]{1,0:T(8,128)(2,1)S(1)} copy-done((bf16[128,1152]{1,0:T(8,128)(2,1)S(1)}, bf16[128,1152]{1,0:T(8,128)(2,1)}, u32[]{:S(2)}) %copy-start.2) | copy-done | bytes 294936
  4.1 0.2 shard_map.68
  4.4 0.4 shard_map.69
  4.8 2.9 %collective-permute-start.5 = (bf16[256,1152]{1,0:T(8,128)(2,1)S(1)}, bf16[256,1152]{1,0:T(8,128)(2,1)S(1)}, u32[]{:S(2)}, u32[]{:S(2)}) collective-permute-start(bf16[256,1152]{1,0:T(8,128)(2,1)S(1)} %get-tuple-element.23.refs_0_), channel_id=1, source_target_pairs={{0,64},{32,97},{2,66},{34,99},{4,68},{36,101},{6,70},{38,103},{64,... | collective-permute-start | bytes 1769480 | tf_op jit(solution)/shard_map/ppermute | solution.py:44
  7.7 2.5 %collective-permute-start.4 = (bf16[256,1152]{1,0:T(8,128)(2,1)S(1)}, bf16[256,1152]{1,0:T(8,128)(2,1)S(1)}, u32[]{:S(2)}, u32[]{:S(2)}) collective-permute-start(bf16[256,1152]{1,0:T(8,128)(2,1)S(1)} %get-tuple-element.23.refs_0_), channel_id=1, source_target_pairs={{0,8},{32,56},{2,10},{34,58},{4,12},{36,60},{6,14},{38,62},{64,72}... | collective-permute-start | bytes 1769480 | tf_op jit(solution)/shard_map/ppermute | solution.py:44
  10.1 1.6 %collective-permute-start.2 = (bf16[256,1152]{1,0:T(8,128)(2,1)S(1)}, bf16[256,1152]{1,0:T(8,128)(2,1)S(1)}, u32[]{:S(2)}, u32[]{:S(2)}) collective-permute-start(bf16[256,1152]{1,0:T(8,128)(2,1)S(1)} %get-tuple-element.23.refs_0_), channel_id=1, source_target_pairs={{0,6},{32,34},{2,4},{34,32},{4,2},{36,38},{6,0},{38,36},{64,70},{9... | collective-permute-start | bytes 1769480 | tf_op jit(solution)/shard_map/ppermute | solution.py:44
  11.8 3.5 %collective-permute-done.5.refs_2_.refs_5_.refs_6_ = bf16[256,1152]{1,0:T(8,128)(2,1)S(1)} collective-permute-done((bf16[256,1152]{1,0:T(8,128)(2,1)S(1)}, bf16[256,1152]{1,0:T(8,128)(2,1)S(1)}, u32[]{:S(2)}, u32[]{:S(2)}) %collective-permute-start.5) | collective-permute-done | bytes 589856 | tf_op jit(solution)/shard_map/ppermute | solution.py:44
  15.2 2.7 %collective-permute-done.4.refs_0_.refs_3_ = bf16[256,1152]{1,0:T(8,128)(2,1)S(1)} collective-permute-done((bf16[256,1152]{1,0:T(8,128)(2,1)S(1)}, bf16[256,1152]{1,0:T(8,128)(2,1)S(1)}, u32[]{:S(2)}, u32[]{:S(2)}) %collective-permute-start.4) | collective-permute-done | bytes 589856 | tf_op jit(solution)/shard_map/ppermute | solution.py:44
  17.9 1.4 %collective-permute-done.2.refs_1_.refs_4_ = bf16[256,1152]{1,0:T(8,128)(2,1)S(1)} collective-permute-done((bf16[256,1152]{1,0:T(8,128)(2,1)S(1)}, bf16[256,1152]{1,0:T(8,128)(2,1)S(1)}, u32[]{:S(2)}, u32[]{:S(2)}) %collective-permute-start.2) | collective-permute-done | bytes 589856 | tf_op jit(solution)/shard_map/ppermute | solution.py:44
  19.3 0.1 shard_map.70
  19.5 1.0 %collective-permute-start.6 = (bf16[768,1152]{1,0:T(8,128)(2,1)S(1)}, bf16[768,1152]{1,0:T(8,128)(2,1)S(1)}, u32[]{:S(2)}, u32[]{:S(2)}) collective-permute-start(bf16[768,1152]{1,0:T(8,128)(2,1)S(1)} %shard_map.70), channel_id=1, source_target_pairs={{0,32},{32,0},{1,33},{33,1},{2,34},{34,2},{3,35},{35,3},{4,36},{36... | collective-permute-start | bytes 5308424 | tf_op jit(solution)/shard_map/ppermute | solution.py:48
  20.5 1.8 %collective-permute-start.3 = (bf16[256,1152]{1,0:T(8,128)(2,1)S(1)}, bf16[256,1152]{1,0:T(8,128)(2,1)S(1)}, u32[]{:S(2)}, u32[]{:S(2)}) collective-permute-start(bf16[256,1152]{1,0:T(8,128)(2,1)S(1)} %collective-permute-done.2.refs_1_.refs_4_), channel_id=1, source_target_pairs={{0,8},{32,56},{2,10},{34,58},{4,12},{36,60},{6,14},{38,62},{64,72}... | collective-permute-start | bytes 1769480 | tf_op jit(solution)/shard_map/ppermute | solution.py:44
  23.6 0.1 pad_maximum_fusion.affine
  23.7 2.0 %collective-permute-start.9 = (bf16[256,1152]{1,0:T(8,128)(2,1)S(1)}, bf16[256,1152]{1,0:T(8,128)(2,1)S(1)}, u32[]{:S(2)}, u32[]{:S(2)}) collective-permute-start(bf16[256,1152]{1,0:T(8,128)(2,1)S(1)} %collective-permute-done.4.refs_0_.refs_3_), channel_id=1, source_target_pairs={{0,64},{32,97},{2,66},{34,99},{4,68},{36,101},{6,70},{38,103},{64,... | collective-permute-start | bytes 1769480 | tf_op jit(solution)/shard_map/ppermute | solution.py:44
  25.7 1.9 %collective-permute-start.8 = (bf16[256,1152]{1,0:T(8,128)(2,1)S(1)}, bf16[256,1152]{1,0:T(8,128)(2,1)S(1)}, u32[]{:S(2)}, u32[]{:S(2)}) collective-permute-start(bf16[256,1152]{1,0:T(8,128)(2,1)S(1)} %collective-permute-done.4.refs_0_.refs_3_), channel_id=1, source_target_pairs={{0,70},{32,99},{2,68},{34,97},{4,66},{36,103},{6,64},{38,101},{64,... | collective-permute-start | bytes 1769480 | tf_op jit(solution)/shard_map/ppermute | solution.py:44
  27.6 6.3 %shard_map.71 = (f32[256,1152]{1,0:T(8,128)S(1)}, f32[256,1152]{1,0:T(8,128)S(1)}, f32[256,1152]{1,0:T(8,128)S(1)}, f32[256,1152]{1,0:T(8,128)S(1)}) custom-call(f32[2]{0:T(128)S(1)} %pad_maximum_fusion.affine, bf16[256,1152]{1,0:T(8,128)(2,1)S(1)} %get-tuple-element.23.refs_0_, bf16[256,1152]{1,0:T(8,128)(2,1)S(1)} %get-tuple-element.24.refs_1_, ...), custom_call_target="tpu_custom_call" | custom-call | tf_op jit(solution)/shard_map/pallas_call | solution.py:128
  33.9 0.1 collective-permute-start.7
  34.0 2.1 %shard_map.73.refs_3_.refs_4_.refs_5_ = f32[256,1152]{1,0:T(8,128)S(1)} custom-call(f32[2]{0:T(128)S(1)} %pad_maximum_fusion.affine, bf16[256,1152]{1,0:T(8,128)(2,1)S(1)} %collective-permute-done.3.refs_0_.refs_4_, bf16[256,1152]{1,0:T(8,128)(2,1)S(1)} %get-tuple-element.24.refs_1_, bf16[768,1152]{1,0:T(8,128)(2,1)S(1)} %collective-permute-done.6.refs_2_, ...), custom_call_target="tpu_custom_call" | custom-call | flops 1207959552 | bytes 2359296 | tf_op jit(solution)/shard_map/pallas_call | solution.py:128
  36.2 5.0 %collective-permute-done.8.refs_0_ = bf16[256,1152]{1,0:T(8,128)(2,1)S(1)} collective-permute-done((bf16[256,1152]{1,0:T(8,128)(2,1)S(1)}, bf16[256,1152]{1,0:T(8,128)(2,1)S(1)}, u32[]{:S(2)}, u32[]{:S(2)}) %collective-permute-start.8) | collective-permute-done | bytes 589856 | tf_op jit(solution)/shard_map/ppermute | solution.py:44
  41.2 0.1 shard_map.74
  41.3 0.6 collective-permute-start.11
  41.9 3.5 %shard_map.75 = (f32[256,1152]{1,0:T(8,128)S(1)}, f32[256,1152]{1,0:T(8,128)S(1)}) custom-call(f32[2]{0:T(128)S(1)} %pad_maximum_fusion.affine, bf16[256,1152]{1,0:T(8,128)(2,1)S(1)} %collective-permute-done.8.refs_0_, bf16[256,1152]{1,0:T(8,128)(2,1)S(1)} %get-tuple-element.24.refs_1_, bf16[768,1152]{1,0:T(8,128)(2,1)S(1)} %collective-permute-done.6.refs_2_, ...), custom_call_target="tpu_custom_call" | custom-call | flops 2415919104 | bytes 4718592 | tf_op jit(solution)/shard_map/pallas_call | solution.py:128
  45.4 2.1 %shard_map.76.refs_6_ = bf16[256,1152]{1,0:T(8,128)(2,1)S(1)} custom-call(f32[2]{0:T(128)S(1)} %pad_maximum_fusion.affine, bf16[256,1152]{1,0:T(8,128)(2,1)S(1)} %collective-permute-done.8.refs_0_, bf16[256,1152]{1,0:T(8,128)(2,1)S(1)} %collective-permute-done.7.refs_4_.refs_1_.refs_3_, bf16[768,1152]{1,0:T(8,128)(2,1)S(1)} %collective-permute-done.11.refs_2_.refs_4_, ...), custom_call_target="tpu_custom_call" | custom-call | flops 1207959552 | bytes 2359296 | tf_op jit(solution)/shard_map/pallas_call | solution.py:128
  47.5 2.6 %collective-permute-start.12 = (bf16[256,1152]{1,0:T(8,128)(2,1)S(1)}, bf16[256,1152]{1,0:T(8,128)(2,1)S(1)}, u32[]{:S(2)}, u32[]{:S(2)}) collective-permute-start(bf16[256,1152]{1,0:T(8,128)(2,1)S(1)} %shard_map.76.refs_6_), channel_id=1, source_target_pairs={{0,8},{32,56},{2,10},{34,58},{4,12},{36,60},{6,14},{38,62},{64,72}... | collective-permute-start | bytes 1769480 | tf_op jit(solution)/shard_map/ppermute | solution.py:44
  50.1 3.5 %shard_map.77 = (bf16[256,1152]{1,0:T(8,128)(2,1)S(1)}, bf16[256,1152]{1,0:T(8,128)(2,1)S(1)}) custom-call(f32[2]{0:T(128)S(1)} %pad_maximum_fusion.affine, bf16[256,1152]{1,0:T(8,128)(2,1)S(1)} %collective-permute-done.9.refs_1_.refs_3_.refs_0_, bf16[256,1152]{1,0:T(8,128)(2,1)S(1)} %collective-permute-done.7.refs_4_.refs_1_.refs_3_, ...), custom_call_target="tpu_custom_call" | custom-call | flops 2415919104 | bytes 4718592 | tf_op jit(solution)/shard_map/pallas_call | solution.py:128
  53.6 2.0 %collective-permute-start.14 = (bf16[256,1152]{1,0:T(8,128)(2,1)S(1)}, bf16[256,1152]{1,0:T(8,128)(2,1)S(1)}, u32[]{:S(2)}, u32[]{:S(2)}) collective-permute-start(bf16[256,1152]{1,0:T(8,128)(2,1)S(1)} %get-tuple-element.31.refs_5_), channel_id=1, source_target_pairs={{0,64},{32,97},{2,66},{34,99},{4,68},{36,101},{6,70},{38,103},{64,... | collective-permute-start | bytes 1769480 | tf_op jit(solution)/shard_map/ppermute | solution.py:44
  55.6 0.2 collective-permute-start.15
  55.8 3.5 %shard_map.78.refs_0_ = f32[256,1152]{1,0:T(8,128)S(1)} custom-call(f32[2]{0:T(128)S(1)} %pad_maximum_fusion.affine, bf16[256,1152]{1,0:T(8,128)(2,1)S(1)} %collective-permute-done.10.refs_2_.refs_0_, bf16[256,1152]{1,0:T(8,128)(2,1)S(1)} %get-tuple-element.24.refs_1_, bf16[768,1152]{1,0:T(8,128)(2,1)S(1)} %collective-permute-done.6.refs_2_, ...), custom_call_target="tpu_custom_call" | custom-call | flops 2415919104 | bytes 2359296 | tf_op jit(solution)/shard_map/pallas_call | solution.py:128
  59.3 0.1 shard_map.79.refs_8_
  59.4 0.3 collective-permute-start.13
  59.7 4.9 %shard_map.80 = (f32[256,1152]{1,0:T(8,128)S(1)}, f32[256,1152]{1,0:T(8,128)S(1)}, f32[256,1152]{1,0:T(8,128)S(1)}) custom-call(f32[2]{0:T(128)S(1)} %pad_maximum_fusion.affine, bf16[256,1152]{1,0:T(8,128)(2,1)S(1)} %collective-permute-done.4.refs_0_.refs_3_, bf16[256,1152]{1,0:T(8,128)(2,1)S(1)} %collective-permute-done.7.refs_4_.refs_1_.refs_3_, ...), custom_call_target="tpu_custom_call" | custom-call | flops 3623878656 | bytes 7077888 | tf_op jit(solution)/shard_map/pallas_call | solution.py:128
  64.6 0.1 shard_map.81.refs_3_
  64.8 2.6 %collective-permute-start.16 = (bf16[256,1152]{1,0:T(8,128)(2,1)S(1)}, bf16[256,1152]{1,0:T(8,128)(2,1)S(1)}, u32[]{:S(2)}, u32[]{:S(2)}) collective-permute-start(bf16[256,1152]{1,0:T(8,128)(2,1)S(1)} %shard_map.81.refs_3_), channel_id=1, source_target_pairs={{0,8},{32,56},{2,10},{34,58},{4,12},{36,60},{6,14},{38,62},{64,72}... | collective-permute-start | bytes 1769480 | tf_op jit(solution)/shard_map/ppermute | solution.py:44
  67.3 0.1 shard_map.82.refs_4_
  67.4 1.5 %collective-permute-start.17 = (bf16[256,1152]{1,0:T(8,128)(2,1)S(1)}, bf16[256,1152]{1,0:T(8,128)(2,1)S(1)}, u32[]{:S(2)}, u32[]{:S(2)}) collective-permute-start(bf16[256,1152]{1,0:T(8,128)(2,1)S(1)} %shard_map.82.refs_4_), channel_id=1, source_target_pairs={{0,6},{32,34},{2,4},{34,32},{4,2},{36,38},{6,0},{38,36},{64,70},{9... | collective-permute-start | bytes 1769480 | tf_op jit(solution)/shard_map/ppermute | solution.py:44
  69.0 0.1 shard_map.83
  69.1 2.6 %collective-permute-start.18 = (bf16[128,1152]{1,0:T(8,128)(2,1)S(1)}, bf16[128,1152]{1,0:T(8,128)(2,1)S(1)}, u32[]{:S(2)}, u32[]{:S(2)}) collective-permute-start(bf16[128,1152]{1,0:T(8,128)(2,1)S(1)} %get-tuple-element.37), channel_id=1, source_target_pairs={{0,96},{32,65},{2,98},{34,67},{4,100},{36,69},{6,102},{38,71},{64,... | collective-permute-start | bytes 884744 | tf_op jit(solution)/shard_map/ppermute | solution.py:44
  71.6 0.3 collective-permute-start.20
  71.9 2.1 %shard_map.84.refs_1_ = f32[256,1152]{1,0:T(8,128)S(1)} custom-call(f32[2]{0:T(128)S(1)} %pad_maximum_fusion.affine, bf16[256,1152]{1,0:T(8,128)(2,1)S(1)} %get-tuple-element.23.refs_0_, bf16[256,1152]{1,0:T(8,128)(2,1)S(1)} %collective-permute-done.7.refs_4_.refs_1_.refs_3_, bf16[768,1152]{1,0:T(8,128)(2,1)S(1)} %collective-permute-done.11.refs_2_.refs_4_, ...), custom_call_target="tpu_custom_call" | custom-call | flops 1207959552 | bytes 2359296 | tf_op jit(solution)/shard_map/pallas_call | solution.py:128
  74.1 1.0 %collective-permute-done.16.refs_2_ = bf16[256,1152]{1,0:T(8,128)(2,1)S(1)} collective-permute-done((bf16[256,1152]{1,0:T(8,128)(2,1)S(1)}, bf16[256,1152]{1,0:T(8,128)(2,1)S(1)}, u32[]{:S(2)}, u32[]{:S(2)}) %collective-permute-start.16) | collective-permute-done | bytes 589856 | tf_op jit(solution)/shard_map/ppermute | solution.py:44
  75.1 1.5 %collective-permute-done.17.refs_3_ = bf16[256,1152]{1,0:T(8,128)(2,1)S(1)} collective-permute-done((bf16[256,1152]{1,0:T(8,128)(2,1)S(1)}, bf16[256,1152]{1,0:T(8,128)(2,1)S(1)}, u32[]{:S(2)}, u32[]{:S(2)}) %collective-permute-start.17) | collective-permute-done | bytes 589856 | tf_op jit(solution)/shard_map/ppermute | solution.py:44
  76.5 0.2 shard_map.85
  76.7 2.7 %collective-permute-start.19 = (bf16[128,1152]{1,0:T(8,128)(2,1)S(1)}, bf16[128,1152]{1,0:T(8,128)(2,1)S(1)}, u32[]{:S(2)}, u32[]{:S(2)}) collective-permute-start(bf16[128,1152]{1,0:T(8,128)(2,1)S(1)} %get-tuple-element.39), channel_id=1, source_target_pairs={{0,32},{32,0},{1,33},{33,1},{2,34},{34,2},{3,35},{35,3},{4,36},{36... | collective-permute-start | bytes 884744 | tf_op jit(solution)/shard_map/ppermute | solution.py:48
  80.1 0.5 collective-permute-done.19.refs_5_
  80.6 1.6 %shard_map.86 = (f32[128,1152]{1,0:T(8,128)}, f32[128,1152]{1,0:T(8,128)}) custom-call(f32[1]{0:T(128)} %bitcast.refs_0_, f32[1]{0:T(128)S(6)} %div.3.refs_1_, bf16[128,1152]{1,0:T(8,128)(2,1)S(1)} %copy-done.1, bf16[128,1152]{1,0:T(8,128)(2,1)S(1)} %copy-done.3, f32[128,1152]{1,0:T(8,128)S(1)} %get-tuple-element.38.refs_4_, ...), custom_call_target="tpu_custom_call" | custom-call | tf_op jit(solution)/shard_map/pallas_call | solution.py:72
  (22 shorter events, 0.1 us)
Async XLA Ops:
  0.6 3.7 %collective-permute-start = (bf16[128,1152]{1,0:T(8,128)(2,1)}, bf16[128,1152]{1,0:T(8,128)(2,1)S(1)}, u32[]{:S(2)}, u32[]{:S(2)}) collective-permute-start(bf16[128,1152]{1,0:T(8,128)(2,1)} %refs_2_.1), channel_id=1, source_target_pairs={{0,32},{32,0},{1,33},{33,1},{2,34},{34,2},{3,35},{35,3},{4,36},{36... | collective-permute-start | bytes 884744 | tf_op jit(solution)/shard_map/ppermute | solution.py:48
  2.1 2.3 %collective-permute-start.1 = (bf16[128,1152]{1,0:T(8,128)(2,1)}, bf16[128,1152]{1,0:T(8,128)(2,1)S(1)}, u32[]{:S(2)}, u32[]{:S(2)}) collective-permute-start(bf16[128,1152]{1,0:T(8,128)(2,1)} %refs_3_.1), channel_id=1, source_target_pairs={{0,32},{32,0},{1,33},{33,1},{2,34},{34,2},{3,35},{35,3},{4,36},{36... | collective-permute-start | bytes 884744 | tf_op jit(solution)/shard_map/ppermute | solution.py:48
  2.2 1.0 %copy-start = (bf16[128,1152]{1,0:T(8,128)(2,1)S(1)}, bf16[128,1152]{1,0:T(8,128)(2,1)}, u32[]{:S(2)}) copy-start(bf16[128,1152]{1,0:T(8,128)(2,1)} %refs_2_.1) | copy-start | bytes 884740
  3.2 1.0 %copy-start.2 = (bf16[128,1152]{1,0:T(8,128)(2,1)S(1)}, bf16[128,1152]{1,0:T(8,128)(2,1)}, u32[]{:S(2)}) copy-start(bf16[128,1152]{1,0:T(8,128)(2,1)} %refs_3_.1) | copy-start | bytes 884740
  4.8 10.5 %collective-permute-start.5 = (bf16[256,1152]{1,0:T(8,128)(2,1)S(1)}, bf16[256,1152]{1,0:T(8,128)(2,1)S(1)}, u32[]{:S(2)}, u32[]{:S(2)}) collective-permute-start(bf16[256,1152]{1,0:T(8,128)(2,1)S(1)} %get-tuple-element.23.refs_0_), channel_id=1, source_target_pairs={{0,64},{32,97},{2,66},{34,99},{4,68},{36,101},{6,70},{38,103},{64,... | collective-permute-start | bytes 1769480 | tf_op jit(solution)/shard_map/ppermute | solution.py:44
  7.7 10.2 %collective-permute-start.4 = (bf16[256,1152]{1,0:T(8,128)(2,1)S(1)}, bf16[256,1152]{1,0:T(8,128)(2,1)S(1)}, u32[]{:S(2)}, u32[]{:S(2)}) collective-permute-start(bf16[256,1152]{1,0:T(8,128)(2,1)S(1)} %get-tuple-element.23.refs_0_), channel_id=1, source_target_pairs={{0,8},{32,56},{2,10},{34,58},{4,12},{36,60},{6,14},{38,62},{64,72}... | collective-permute-start | bytes 1769480 | tf_op jit(solution)/shard_map/ppermute | solution.py:44
  10.1 9.2 %collective-permute-start.2 = (bf16[256,1152]{1,0:T(8,128)(2,1)S(1)}, bf16[256,1152]{1,0:T(8,128)(2,1)S(1)}, u32[]{:S(2)}, u32[]{:S(2)}) collective-permute-start(bf16[256,1152]{1,0:T(8,128)(2,1)S(1)} %get-tuple-element.23.refs_0_), channel_id=1, source_target_pairs={{0,6},{32,34},{2,4},{34,32},{4,2},{36,38},{6,0},{38,36},{64,70},{9... | collective-permute-start | bytes 1769480 | tf_op jit(solution)/shard_map/ppermute | solution.py:44
  19.5 8.1 %collective-permute-start.6 = (bf16[768,1152]{1,0:T(8,128)(2,1)S(1)}, bf16[768,1152]{1,0:T(8,128)(2,1)S(1)}, u32[]{:S(2)}, u32[]{:S(2)}) collective-permute-start(bf16[768,1152]{1,0:T(8,128)(2,1)S(1)} %shard_map.70), channel_id=1, source_target_pairs={{0,32},{32,0},{1,33},{33,1},{2,34},{34,2},{3,35},{35,3},{4,36},{36... | collective-permute-start | bytes 5308424 | tf_op jit(solution)/shard_map/ppermute | solution.py:48
  20.5 13.4 %collective-permute-start.3 = (bf16[256,1152]{1,0:T(8,128)(2,1)S(1)}, bf16[256,1152]{1,0:T(8,128)(2,1)S(1)}, u32[]{:S(2)}, u32[]{:S(2)}) collective-permute-start(bf16[256,1152]{1,0:T(8,128)(2,1)S(1)} %collective-permute-done.2.refs_1_.refs_4_), channel_id=1, source_target_pairs={{0,8},{32,56},{2,10},{34,58},{4,12},{36,60},{6,14},{38,62},{64,72}... | collective-permute-start | bytes 1769480 | tf_op jit(solution)/shard_map/ppermute | solution.py:44
  23.7 12.4 %collective-permute-start.10 = (bf16[256,1152]{1,0:T(8,128)(2,1)S(1)}, bf16[256,1152]{1,0:T(8,128)(2,1)S(1)}, u32[]{:S(2)}, u32[]{:S(2)}) collective-permute-start(bf16[256,1152]{1,0:T(8,128)(2,1)S(1)} %collective-permute-done.5.refs_2_.refs_5_.refs_6_), channel_id=1, source_target_pairs={{0,6},{32,34},{2,4},{34,32},{4,2},{36,38},{6,0},{38,36},{64,70},{9... | collective-permute-start | bytes 1769480 | tf_op jit(solution)/shard_map/ppermute | solution.py:44
  23.7 12.4 %collective-permute-start.9 = (bf16[256,1152]{1,0:T(8,128)(2,1)S(1)}, bf16[256,1152]{1,0:T(8,128)(2,1)S(1)}, u32[]{:S(2)}, u32[]{:S(2)}) collective-permute-start(bf16[256,1152]{1,0:T(8,128)(2,1)S(1)} %collective-permute-done.4.refs_0_.refs_3_), channel_id=1, source_target_pairs={{0,64},{32,97},{2,66},{34,99},{4,68},{36,101},{6,70},{38,103},{64,... | collective-permute-start | bytes 1769480 | tf_op jit(solution)/shard_map/ppermute | solution.py:44
  25.7 15.5 %collective-permute-start.8 = (bf16[256,1152]{1,0:T(8,128)(2,1)S(1)}, bf16[256,1152]{1,0:T(8,128)(2,1)S(1)}, u32[]{:S(2)}, u32[]{:S(2)}) collective-permute-start(bf16[256,1152]{1,0:T(8,128)(2,1)S(1)} %collective-permute-done.4.refs_0_.refs_3_), channel_id=1, source_target_pairs={{0,70},{32,99},{2,68},{34,97},{4,66},{36,103},{6,64},{38,101},{64,... | collective-permute-start | bytes 1769480 | tf_op jit(solution)/shard_map/ppermute | solution.py:44
  33.9 7.2 %collective-permute-start.7 = (bf16[256,1152]{1,0:T(8,128)(2,1)S(1)}, bf16[256,1152]{1,0:T(8,128)(2,1)S(1)}, u32[]{:S(2)}, u32[]{:S(2)}) collective-permute-start(bf16[256,1152]{1,0:T(8,128)(2,1)S(1)} %shard_map.72), channel_id=1, source_target_pairs={{0,32},{32,0},{1,33},{33,1},{2,34},{34,2},{3,35},{35,3},{4,36},{36... | collective-permute-start | bytes 1769480 | tf_op jit(solution)/shard_map/ppermute | solution.py:48
  41.3 4.1 %collective-permute-start.11 = (bf16[768,1152]{1,0:T(8,128)(2,1)S(1)}, bf16[768,1152]{1,0:T(8,128)(2,1)S(1)}, u32[]{:S(2)}, u32[]{:S(2)}) collective-permute-start(bf16[768,1152]{1,0:T(8,128)(2,1)S(1)} %shard_map.74), channel_id=1, source_target_pairs={{0,32},{32,0},{1,33},{33,1},{2,34},{34,2},{3,35},{35,3},{4,36},{36... | collective-permute-start | bytes 5308424 | tf_op jit(solution)/shard_map/ppermute | solution.py:48
  47.5 11.7 %collective-permute-start.12 = (bf16[256,1152]{1,0:T(8,128)(2,1)S(1)}, bf16[256,1152]{1,0:T(8,128)(2,1)S(1)}, u32[]{:S(2)}, u32[]{:S(2)}) collective-permute-start(bf16[256,1152]{1,0:T(8,128)(2,1)S(1)} %shard_map.76.refs_6_), channel_id=1, source_target_pairs={{0,8},{32,56},{2,10},{34,58},{4,12},{36,60},{6,14},{38,62},{64,72}... | collective-permute-start | bytes 1769480 | tf_op jit(solution)/shard_map/ppermute | solution.py:44
  53.6 11.0 %collective-permute-start.14 = (bf16[256,1152]{1,0:T(8,128)(2,1)S(1)}, bf16[256,1152]{1,0:T(8,128)(2,1)S(1)}, u32[]{:S(2)}, u32[]{:S(2)}) collective-permute-start(bf16[256,1152]{1,0:T(8,128)(2,1)S(1)} %get-tuple-element.31.refs_5_), channel_id=1, source_target_pairs={{0,64},{32,97},{2,66},{34,99},{4,68},{36,101},{6,70},{38,103},{64,... | collective-permute-start | bytes 1769480 | tf_op jit(solution)/shard_map/ppermute | solution.py:44
  55.6 11.7 %collective-permute-start.15 = (bf16[256,1152]{1,0:T(8,128)(2,1)S(1)}, bf16[256,1152]{1,0:T(8,128)(2,1)S(1)}, u32[]{:S(2)}, u32[]{:S(2)}) collective-permute-start(bf16[256,1152]{1,0:T(8,128)(2,1)S(1)} %get-tuple-element.35), channel_id=1, source_target_pairs={{0,8},{32,56},{2,10},{34,58},{4,12},{36,60},{6,14},{38,62},{64,72}... | collective-permute-start | bytes 1769480 | tf_op jit(solution)/shard_map/ppermute | solution.py:44
  59.4 9.6 %collective-permute-start.13 = (bf16[256,1152]{1,0:T(8,128)(2,1)S(1)}, bf16[256,1152]{1,0:T(8,128)(2,1)S(1)}, u32[]{:S(2)}, u32[]{:S(2)}) collective-permute-start(bf16[256,1152]{1,0:T(8,128)(2,1)S(1)} %shard_map.79.refs_8_), channel_id=1, source_target_pairs={{0,6},{32,34},{2,4},{34,32},{4,2},{36,38},{6,0},{38,36},{64,70},{9... | collective-permute-start | bytes 1769480 | tf_op jit(solution)/shard_map/ppermute | solution.py:44
  64.8 10.3 %collective-permute-start.16 = (bf16[256,1152]{1,0:T(8,128)(2,1)S(1)}, bf16[256,1152]{1,0:T(8,128)(2,1)S(1)}, u32[]{:S(2)}, u32[]{:S(2)}) collective-permute-start(bf16[256,1152]{1,0:T(8,128)(2,1)S(1)} %shard_map.81.refs_3_), channel_id=1, source_target_pairs={{0,8},{32,56},{2,10},{34,58},{4,12},{36,60},{6,14},{38,62},{64,72}... | collective-permute-start | bytes 1769480 | tf_op jit(solution)/shard_map/ppermute | solution.py:44
  67.4 9.1 %collective-permute-start.17 = (bf16[256,1152]{1,0:T(8,128)(2,1)S(1)}, bf16[256,1152]{1,0:T(8,128)(2,1)S(1)}, u32[]{:S(2)}, u32[]{:S(2)}) collective-permute-start(bf16[256,1152]{1,0:T(8,128)(2,1)S(1)} %shard_map.82.refs_4_), channel_id=1, source_target_pairs={{0,6},{32,34},{2,4},{34,32},{4,2},{36,38},{6,0},{38,36},{64,70},{9... | collective-permute-start | bytes 1769480 | tf_op jit(solution)/shard_map/ppermute | solution.py:44
  69.1 7.5 %collective-permute-start.18 = (bf16[128,1152]{1,0:T(8,128)(2,1)S(1)}, bf16[128,1152]{1,0:T(8,128)(2,1)S(1)}, u32[]{:S(2)}, u32[]{:S(2)}) collective-permute-start(bf16[128,1152]{1,0:T(8,128)(2,1)S(1)} %get-tuple-element.37), channel_id=1, source_target_pairs={{0,96},{32,65},{2,98},{34,67},{4,100},{36,69},{6,102},{38,71},{64,... | collective-permute-start | bytes 884744 | tf_op jit(solution)/shard_map/ppermute | solution.py:44
  71.6 8.4 %collective-permute-start.20 = (bf16[128,1152]{1,0:T(8,128)(2,1)S(1)}, bf16[128,1152]{1,0:T(8,128)(2,1)S(1)}, u32[]{:S(2)}, u32[]{:S(2)}) collective-permute-start(bf16[128,1152]{1,0:T(8,128)(2,1)S(1)} %get-tuple-element.36.refs_4_), channel_id=1, source_target_pairs={{0,64},{32,97},{2,66},{34,99},{4,68},{36,101},{6,70},{38,103},{64,... | collective-permute-start | bytes 884744 | tf_op jit(solution)/shard_map/ppermute | solution.py:44
  74.0 6.6 %copy-start.1 = (bf16[128,1152]{1,0:T(8,128)(2,1)S(1)}, bf16[128,1152]{1,0:T(8,128)(2,1)}, u32[]{:S(2)}) copy-start(bf16[128,1152]{1,0:T(8,128)(2,1)} %refs_2_.1) | copy-start | bytes 884740
  74.0 6.6 %copy-start.3 = (bf16[128,1152]{1,0:T(8,128)(2,1)S(1)}, bf16[128,1152]{1,0:T(8,128)(2,1)}, u32[]{:S(2)}) copy-start(bf16[128,1152]{1,0:T(8,128)(2,1)} %refs_3_.1) | copy-start | bytes 884740
  76.7 3.9 %collective-permute-start.19 = (bf16[128,1152]{1,0:T(8,128)(2,1)S(1)}, bf16[128,1152]{1,0:T(8,128)(2,1)S(1)}, u32[]{:S(2)}, u32[]{:S(2)}) collective-permute-start(bf16[128,1152]{1,0:T(8,128)(2,1)S(1)} %get-tuple-element.39), channel_id=1, source_target_pairs={{0,32},{32,0},{1,33},{33,1},{2,34},{34,2},{3,35},{35,3},{4,36},{36... | collective-permute-start | bytes 884744 | tf_op jit(solution)/shard_map/ppermute | solution.py:48

commit v14 on v12

--- a/solution.py
+++ b/solution.py
@@ -14,6 +14,7 @@
 FINE_SIZES = (2, 2, 4, 4, 2)
 RING = 4
 VMEM_BYTES = 16 * 1024 * 1024
+CUTS = 4
 HALF = jnp.bfloat16
 FULL = jnp.float32
 
@@ -141,6 +142,24 @@
     )(affine, *inputs, *after)
 
 
+def finish_kernel(is_first, multiplier, *refs):
+    raws, (here, there, y_here, y_there), outs, (held, sems) = refs[:2], refs[2:6], refs[6:8], refs[8:]
+    first = is_first[0] > 0
+    cut = raws[0].shape[0] // CUTS
+    copies = []
+    for n in range(CUTS):
+        at = pl.ds(n * cut, cut)
+        totals = (here[at, :] + y_here[at, :].astype(FULL), there[at, :].astype(FULL) + y_there[at, :].astype(FULL))
+        for k, raw in enumerate(raws):
+            unit, scale = unit_rows(raw[at, :])
+            grad = multiplier[0] * jnp.where(first, totals[k], totals[1 - k])
+            held[k, at, :] = scale * (grad - unit * jnp.sum(unit * grad, axis=1, keepdims=True))
+            copies.append(pltpu.make_async_copy(held.at[k, at], outs[k].at[at], sems.at[len(copies)]))
+            copies[-1].start()
+    for copy in copies:
+        copy.wait()
+
+
 def on_device(
     picture_vectors_raw, caption_vectors_raw, logit_multiplier, offset_term, incoming_adjoint
 ):
@@ -201,7 +220,8 @@
     sums = sums_of(affine, [(mine[way], one, None) for way in near], diagonal=True, hides=False)
     sums = dict(zip(near, sums, strict=True))
     two = [stacked(TWO, [sums[""]])]
-    sums |= zip(TWO, sums_of(affine, [(mine[way], one, None) for way in TWO]), strict=True)
+    ways = ("xyz", "xy", "zx")
+    sums |= zip(ways, sums_of(affine, [(mine[way], one, None) for way in ways]), strict=True)
 
     def parts_of(ways, after, kind=FULL):
         return sums_of(affine, [(mine[way], two, sums[way]) for way in ways], after, kind)
@@ -216,7 +236,7 @@
     for_yz = sent(part_xyz, "x")
     part_xy, part_zx = parts_of(["xy", "zx"], [part_xyz], HALF)
     for_x, for_z = sent(part_xy, "y"), sent(part_zx, "x")
-    (part_yz,) = parts_of(["yz"], [part_xy])
+    (part_yz,) = sums_of(affine, [(mine["yz"], one + two, None)], [part_xy])
     part_yz = added(part_yz, for_yz)
     for_y = sent(part_yz, "z")
     part_x, part_y, part_z = parts_of(ONE, [part_yz])
@@ -243,23 +263,26 @@
     )
     there = other_core(there)
 
-    def finish(scalars, refs):
-        first, multiplier = scalars[0][0] > 0, scalars[1][0]
-        here, there, y_here, y_there = [ref[...].astype(FULL) for ref in refs[2:]]
-        totals = (here + y_here, there + y_there)
-        results = []
-        for k, raw in enumerate(refs[:2]):
-            unit, scale = unit_rows(raw[...])
-            grad = multiplier * jnp.where(first, totals[k], totals[1 - k])
-            results.append(scale * (grad - unit * jnp.sum(unit * grad, axis=1, keepdims=True)))
-        return results
-
     return tuple(
-        local(
-            finish,
-            [shard_full] * 2,
-            [first_flag, multiplier],
-            [picture_vectors_raw, caption_vectors_raw, here, there, y_here, y_there],
+        pl.pallas_call(
+            finish_kernel,
+            out_shape=[jax.ShapeDtypeStruct(*shard_full)] * 2,
+            in_specs=[SMEM] * 2 + [VMEM] * 6,
+            out_specs=[ANY] * 2,
+            scratch_shapes=[
+                pltpu.VMEM((2, rows, width), FULL),
+                pltpu.SemaphoreType.DMA((2 * CUTS,)),
+            ],
+            compiler_params=PARAMS,
+        )(
+            first_flag,
+            multiplier,
+            picture_vectors_raw,
+            caption_vectors_raw,
+            here,
+            there,
+            y_here,
+            y_there,
         )
     )
 

time: 81.8 us -> 80.4 us (0.983)
  starting transfers between devices: 32.8 us -> 30.4 us
  waiting for transfers between devices: 13.5 us -> 14.7 us
    pallas_call x10 -> x9, Pallas kernels: 3.1 us -> 1.48 us  [local(): pl.pallas_call(kernel, out_shape=[jax.ShapeDtypeStruct(s, d) for s, d in...]
    pallas_call x0 -> x1, Pallas kernels: none -> 1.58 us  [on_device(): pl.pallas_call(finish_kernel, out_shape=[jax.ShapeDtypeStruct(*shard_full...]
    ppermute x15, starting transfers between devices: 25.5 us -> 24.2 us  [sent(): return lax.ppermute(value, FINE_AXES, pairs)]
    ppermute x5, starting transfers between devices: 7.38 us -> 6.22 us  [other_core(): return lax.ppermute(value, 'core', [(0, 1), (1, 0)])]
    ppermute x15, waiting for transfers between devices: 13.5 us -> 14.7 us  [sent(): return lax.ppermute(value, FINE_AXES, pairs)]
where the time goes in v14:
time: 80.4 us; the launch traced here: 80.2 us
  starting transfers between devices  30.4 us (38%)
  Pallas kernels  30.2 us (38%)
  waiting for transfers between devices  14.7 us (18%)
  between operations  2.94 us (4%)
  local copies, waits for them, and re-layouts  1.93 us (2%)
    pallas_call x7, Pallas kernels, sums_of(): pl.pallas_call(functools.partial(sums_kernel, plan, len(inputs), len(afte...  27.2 us
    ppermute x15, starting transfers between devices, sent(): return lax.ppermute(value, FINE_AXES, pairs)  24.2 us
    ppermute x15, waiting for transfers between devices, sent(): return lax.ppermute(value, FINE_AXES, pairs)  14.7 us
    ppermute x5, starting transfers between devices, other_core(): return lax.ppermute(value, 'core', [(0, 1), (1, 0)])  6.22 us
    unnamed x8, local copies, waits for them, and re-layouts  1.93 us
  transfers between devices with their start and end apart: 20, of which 9 were waited for; matrix products, arithmetic and copies ran while one was open for 0% of the time, Pallas kernels for 32%

profile of v14, /device:TPU:1, one launch (start us, length us, event | category | flops | bytes accessed | tf_op | source)
XLA Modules:
  0.0 80.2 jit_solution(17437214132514238399)
XLA Ops:
  0.6 1.5 %collective-permute-start = (bf16[128,1152]{1,0:T(8,128)(2,1)}, bf16[128,1152]{1,0:T(8,128)(2,1)S(1)}, u32[]{:S(2)}, u32[]{:S(2)}) collective-permute-start(bf16[128,1152]{1,0:T(8,128)(2,1)} %refs_0_.3), channel_id=1, source_target_pairs={{0,32},{32,0},{1,33},{33,1},{2,34},{34,2},{3,35},{35,3},{4,36},{36... | collective-permute-start | bytes 884744 | tf_op jit(solution)/shard_map/ppermute | solution.py:50
  2.1 0.1 collective-permute-start.1
  2.2 1.0 %copy-done = bf16[128,1152]{1,0:T(8,128)(2,1)S(1)} copy-done((bf16[128,1152]{1,0:T(8,128)(2,1)S(1)}, bf16[128,1152]{1,0:T(8,128)(2,1)}, u32[]{:S(2)}) %copy-start) | copy-done | bytes 294936
  3.2 1.0 %copy-done.2 = bf16[128,1152]{1,0:T(8,128)(2,1)S(1)} copy-done((bf16[128,1152]{1,0:T(8,128)(2,1)S(1)}, bf16[128,1152]{1,0:T(8,128)(2,1)}, u32[]{:S(2)}) %copy-start.2) | copy-done | bytes 294936
  4.1 0.2 shard_map.68
  4.4 0.4 shard_map.69
  4.8 2.6 %collective-permute-start.2 = (bf16[256,1152]{1,0:T(8,128)(2,1)S(1)}, bf16[256,1152]{1,0:T(8,128)(2,1)S(1)}, u32[]{:S(2)}, u32[]{:S(2)}) collective-permute-start(bf16[256,1152]{1,0:T(8,128)(2,1)S(1)} %get-tuple-element.24.refs_0_), channel_id=1, source_target_pairs={{0,8},{32,56},{2,10},{34,58},{4,12},{36,60},{6,14},{38,62},{64,72}... | collective-permute-start | bytes 1769480 | tf_op jit(solution)/shard_map/ppermute | solution.py:46
  7.4 2.7 %collective-permute-start.5 = (bf16[256,1152]{1,0:T(8,128)(2,1)S(1)}, bf16[256,1152]{1,0:T(8,128)(2,1)S(1)}, u32[]{:S(2)}, u32[]{:S(2)}) collective-permute-start(bf16[256,1152]{1,0:T(8,128)(2,1)S(1)} %get-tuple-element.24.refs_0_), channel_id=1, source_target_pairs={{0,64},{32,97},{2,66},{34,99},{4,68},{36,101},{6,70},{38,103},{64,... | collective-permute-start | bytes 1769480 | tf_op jit(solution)/shard_map/ppermute | solution.py:46
  10.1 1.6 %collective-permute-start.7 = (bf16[256,1152]{1,0:T(8,128)(2,1)S(1)}, bf16[256,1152]{1,0:T(8,128)(2,1)S(1)}, u32[]{:S(2)}, u32[]{:S(2)}) collective-permute-start(bf16[256,1152]{1,0:T(8,128)(2,1)S(1)} %get-tuple-element.24.refs_0_), channel_id=1, source_target_pairs={{0,6},{32,34},{2,4},{34,32},{4,2},{36,38},{6,0},{38,36},{64,70},{9... | collective-permute-start | bytes 1769480 | tf_op jit(solution)/shard_map/ppermute | solution.py:46
  11.8 3.3 %collective-permute-done.2.refs_0_.refs_3_ = bf16[256,1152]{1,0:T(8,128)(2,1)S(1)} collective-permute-done((bf16[256,1152]{1,0:T(8,128)(2,1)S(1)}, bf16[256,1152]{1,0:T(8,128)(2,1)S(1)}, u32[]{:S(2)}, u32[]{:S(2)}) %collective-permute-start.2) | collective-permute-done | bytes 589856 | tf_op jit(solution)/shard_map/ppermute | solution.py:46
  15.1 2.6 %collective-permute-done.5.refs_1_.refs_4_.refs_3_ = bf16[256,1152]{1,0:T(8,128)(2,1)S(1)} collective-permute-done((bf16[256,1152]{1,0:T(8,128)(2,1)S(1)}, bf16[256,1152]{1,0:T(8,128)(2,1)S(1)}, u32[]{:S(2)}, u32[]{:S(2)}) %collective-permute-start.5) | collective-permute-done | bytes 589856 | tf_op jit(solution)/shard_map/ppermute | solution.py:46
  17.7 1.6 %collective-permute-done.7.refs_2_.refs_5_ = bf16[256,1152]{1,0:T(8,128)(2,1)S(1)} collective-permute-done((bf16[256,1152]{1,0:T(8,128)(2,1)S(1)}, bf16[256,1152]{1,0:T(8,128)(2,1)S(1)}, u32[]{:S(2)}, u32[]{:S(2)}) %collective-permute-start.7) | collective-permute-done | bytes 589856 | tf_op jit(solution)/shard_map/ppermute | solution.py:46
  19.3 0.1 shard_map.70
  19.5 1.0 %collective-permute-start.9 = (bf16[768,1152]{1,0:T(8,128)(2,1)S(1)}, bf16[768,1152]{1,0:T(8,128)(2,1)S(1)}, u32[]{:S(2)}, u32[]{:S(2)}) collective-permute-start(bf16[768,1152]{1,0:T(8,128)(2,1)S(1)} %shard_map.70), channel_id=1, source_target_pairs={{0,32},{32,0},{1,33},{33,1},{2,34},{34,2},{3,35},{35,3},{4,36},{36... | collective-permute-start | bytes 5308424 | tf_op jit(solution)/shard_map/ppermute | solution.py:50
  20.5 1.2 %collective-permute-start.3 = (bf16[256,1152]{1,0:T(8,128)(2,1)S(1)}, bf16[256,1152]{1,0:T(8,128)(2,1)S(1)}, u32[]{:S(2)}, u32[]{:S(2)}) collective-permute-start(bf16[256,1152]{1,0:T(8,128)(2,1)S(1)} %collective-permute-done.2.refs_0_.refs_3_), channel_id=1, source_target_pairs={{0,70},{32,99},{2,68},{34,97},{4,66},{36,103},{6,64},{38,101},{64,... | collective-permute-start | bytes 1769480 | tf_op jit(solution)/shard_map/ppermute | solution.py:46
  21.8 1.4 %collective-permute-start.4 = (bf16[256,1152]{1,0:T(8,128)(2,1)S(1)}, bf16[256,1152]{1,0:T(8,128)(2,1)S(1)}, u32[]{:S(2)}, u32[]{:S(2)}) collective-permute-start(bf16[256,1152]{1,0:T(8,128)(2,1)S(1)} %collective-permute-done.2.refs_0_.refs_3_), channel_id=1, source_target_pairs={{0,64},{32,97},{2,66},{34,99},{4,68},{36,101},{6,70},{38,103},{64,... | collective-permute-start | bytes 1769480 | tf_op jit(solution)/shard_map/ppermute | solution.py:46
  23.2 1.2 %collective-permute-start.6 = (bf16[256,1152]{1,0:T(8,128)(2,1)S(1)}, bf16[256,1152]{1,0:T(8,128)(2,1)S(1)}, u32[]{:S(2)}, u32[]{:S(2)}) collective-permute-start(bf16[256,1152]{1,0:T(8,128)(2,1)S(1)} %collective-permute-done.5.refs_1_.refs_4_.refs_3_), channel_id=1, source_target_pairs={{0,6},{32,34},{2,4},{34,32},{4,2},{36,38},{6,0},{38,36},{64,70},{9... | collective-permute-start | bytes 1769480 | tf_op jit(solution)/shard_map/ppermute | solution.py:46
  24.4 1.8 %collective-permute-start.8 = (bf16[256,1152]{1,0:T(8,128)(2,1)S(1)}, bf16[256,1152]{1,0:T(8,128)(2,1)S(1)}, u32[]{:S(2)}, u32[]{:S(2)}) collective-permute-start(bf16[256,1152]{1,0:T(8,128)(2,1)S(1)} %collective-permute-done.7.refs_2_.refs_5_), channel_id=1, source_target_pairs={{0,8},{32,56},{2,10},{34,58},{4,12},{36,60},{6,14},{38,62},{64,72}... | collective-permute-start | bytes 1769480 | tf_op jit(solution)/shard_map/ppermute | solution.py:46
  27.6 6.3 %shard_map.71 = (f32[256,1152]{1,0:T(8,128)S(1)}, f32[256,1152]{1,0:T(8,128)S(1)}, f32[256,1152]{1,0:T(8,128)S(1)}, f32[256,1152]{1,0:T(8,128)S(1)}) custom-call(f32[2]{0:T(128)S(1)} %pad_maximum_fusion.affine, bf16[256,1152]{1,0:T(8,128)(2,1)S(1)} %get-tuple-element.24.refs_0_, bf16[256,1152]{1,0:T(8,128)(2,1)S(1)} %get-tuple-element.25.refs_1_, ...), custom_call_target="tpu_custom_call" | custom-call | tf_op jit(solution)/shard_map/pallas_call | solution.py:130
  33.9 3.3 %collective-permute-done.4.refs_1_.refs_3_.refs_0_ = bf16[256,1152]{1,0:T(8,128)(2,1)S(1)} collective-permute-done((bf16[256,1152]{1,0:T(8,128)(2,1)S(1)}, bf16[256,1152]{1,0:T(8,128)(2,1)S(1)}, u32[]{:S(2)}, u32[]{:S(2)}) %collective-permute-start.4) | collective-permute-done | bytes 589856 | tf_op jit(solution)/shard_map/ppermute | solution.py:46
  37.1 0.8 %collective-permute-done.6.refs_2_.refs_0_ = bf16[256,1152]{1,0:T(8,128)(2,1)S(1)} collective-permute-done((bf16[256,1152]{1,0:T(8,128)(2,1)S(1)}, bf16[256,1152]{1,0:T(8,128)(2,1)S(1)}, u32[]{:S(2)}, u32[]{:S(2)}) %collective-permute-start.6) | collective-permute-done | bytes 589856 | tf_op jit(solution)/shard_map/ppermute | solution.py:46
  38.0 0.2 shard_map.72
  38.2 1.8 %collective-permute-start.10 = (bf16[1024,1152]{1,0:T(8,128)(2,1)S(1)}, bf16[1024,1152]{1,0:T(8,128)(2,1)S(1)}, u32[]{:S(2)}, u32[]{:S(2)}) collective-permute-start(bf16[1024,1152]{1,0:T(8,128)(2,1)S(1)} %shard_map.72), channel_id=1, source_target_pairs={{0,32},{32,0},{1,33},{33,1},{2,34},{34,2},{3,35},{35,3},{4,36},{36... | collective-permute-start | bytes 7077896 | tf_op jit(solution)/shard_map/ppermute | solution.py:50
  40.0 4.9 %shard_map.73 = (f32[256,1152]{1,0:T(8,128)S(1)}, f32[256,1152]{1,0:T(8,128)S(1)}, f32[256,1152]{1,0:T(8,128)S(1)}) custom-call(f32[2]{0:T(128)S(1)} %pad_maximum_fusion.affine, bf16[256,1152]{1,0:T(8,128)(2,1)S(1)} %collective-permute-done.3.refs_0_, bf16[256,1152]{1,0:T(8,128)(2,1)S(1)} %get-tuple-element.25.refs_1_, ...), custom_call_target="tpu_custom_call" | custom-call | flops 3623878656 | bytes 7077888 | tf_op jit(solution)/shard_map/pallas_call | solution.py:130
  44.9 2.1 %shard_map.74.refs_5_ = bf16[256,1152]{1,0:T(8,128)(2,1)S(1)} custom-call(f32[2]{0:T(128)S(1)} %pad_maximum_fusion.affine, bf16[256,1152]{1,0:T(8,128)(2,1)S(1)} %collective-permute-done.3.refs_0_, bf16[1024,1152]{1,0:T(8,128)(2,1)S(1)} %collective-permute-done.10.refs_1_.refs_3_, f32[256,1152]{1,0:T(8,128)S(1)} %get-tuple-element.32.refs_2_), custom_call_target="tpu_custom_call" | custom-call | flops 1207959552 | bytes 2359296 | tf_op jit(solution)/shard_map/pallas_call | solution.py:130
  47.0 1.9 %collective-permute-start.11 = (bf16[256,1152]{1,0:T(8,128)(2,1)S(1)}, bf16[256,1152]{1,0:T(8,128)(2,1)S(1)}, u32[]{:S(2)}, u32[]{:S(2)}) collective-permute-start(bf16[256,1152]{1,0:T(8,128)(2,1)S(1)} %shard_map.74.refs_5_), channel_id=1, source_target_pairs={{0,8},{32,56},{2,10},{34,58},{4,12},{36,60},{6,14},{38,62},{64,72}... | collective-permute-start | bytes 1769480 | tf_op jit(solution)/shard_map/ppermute | solution.py:46
  48.9 3.5 %shard_map.75 = (bf16[256,1152]{1,0:T(8,128)(2,1)S(1)}, bf16[256,1152]{1,0:T(8,128)(2,1)S(1)}) custom-call(f32[2]{0:T(128)S(1)} %pad_maximum_fusion.affine, bf16[256,1152]{1,0:T(8,128)(2,1)S(1)} %collective-permute-done.4.refs_1_.refs_3_.refs_0_, bf16[1024,1152]{1,0:T(8,128)(2,1)S(1)} %collective-permute-done.10.refs_1_.refs_3_, ...), custom_call_target="tpu_custom_call" | custom-call | flops 2415919104 | bytes 4718592 | tf_op jit(solution)/shard_map/pallas_call | solution.py:130
  52.4 2.0 %collective-permute-start.13 = (bf16[256,1152]{1,0:T(8,128)(2,1)S(1)}, bf16[256,1152]{1,0:T(8,128)(2,1)S(1)}, u32[]{:S(2)}, u32[]{:S(2)}) collective-permute-start(bf16[256,1152]{1,0:T(8,128)(2,1)S(1)} %get-tuple-element.33.refs_4_), channel_id=1, source_target_pairs={{0,64},{32,97},{2,66},{34,99},{4,68},{36,101},{6,70},{38,103},{64,... | collective-permute-start | bytes 1769480 | tf_op jit(solution)/shard_map/ppermute | solution.py:46
  54.3 0.9 %collective-permute-start.14 = (bf16[256,1152]{1,0:T(8,128)(2,1)S(1)}, bf16[256,1152]{1,0:T(8,128)(2,1)S(1)}, u32[]{:S(2)}, u32[]{:S(2)}) collective-permute-start(bf16[256,1152]{1,0:T(8,128)(2,1)S(1)} %get-tuple-element.37), channel_id=1, source_target_pairs={{0,8},{32,56},{2,10},{34,58},{4,12},{36,60},{6,14},{38,62},{64,72}... | collective-permute-start | bytes 1769480 | tf_op jit(solution)/shard_map/ppermute | solution.py:46
  55.2 3.5 %shard_map.76.refs_0_ = f32[256,1152]{1,0:T(8,128)S(1)} custom-call(f32[2]{0:T(128)S(1)} %pad_maximum_fusion.affine, bf16[256,1152]{1,0:T(8,128)(2,1)S(1)} %collective-permute-done.6.refs_2_.refs_0_, bf16[256,1152]{1,0:T(8,128)(2,1)S(1)} %get-tuple-element.25.refs_1_, bf16[768,1152]{1,0:T(8,128)(2,1)S(1)} %collective-permute-done.9.refs_2_, ...), custom_call_target="tpu_custom_call" | custom-call | flops 2415919104 | bytes 2359296 | tf_op jit(solution)/shard_map/pallas_call | solution.py:130
  58.7 0.1 shard_map.77.refs_7_
  58.8 0.3 collective-permute-start.12
  59.1 4.9 %shard_map.78 = (f32[256,1152]{1,0:T(8,128)S(1)}, f32[256,1152]{1,0:T(8,128)S(1)}, f32[256,1152]{1,0:T(8,128)S(1)}) custom-call(f32[2]{0:T(128)S(1)} %pad_maximum_fusion.affine, bf16[256,1152]{1,0:T(8,128)(2,1)S(1)} %collective-permute-done.2.refs_0_.refs_3_, bf16[1024,1152]{1,0:T(8,128)(2,1)S(1)} %collective-permute-done.10.refs_1_.refs_3_, ...), custom_call_target="tpu_custom_call" | custom-call | flops 3623878656 | bytes 7077888 | tf_op jit(solution)/shard_map/pallas_call | solution.py:130
  64.0 0.1 shard_map.79.refs_3_
  64.1 1.9 %collective-permute-start.15 = (bf16[256,1152]{1,0:T(8,128)(2,1)S(1)}, bf16[256,1152]{1,0:T(8,128)(2,1)S(1)}, u32[]{:S(2)}, u32[]{:S(2)}) collective-permute-start(bf16[256,1152]{1,0:T(8,128)(2,1)S(1)} %shard_map.79.refs_3_), channel_id=1, source_target_pairs={{0,8},{32,56},{2,10},{34,58},{4,12},{36,60},{6,14},{38,62},{64,72}... | collective-permute-start | bytes 1769480 | tf_op jit(solution)/shard_map/ppermute | solution.py:46
  66.0 0.1 shard_map.80.refs_4_
  66.2 1.5 %collective-permute-start.16 = (bf16[256,1152]{1,0:T(8,128)(2,1)S(1)}, bf16[256,1152]{1,0:T(8,128)(2,1)S(1)}, u32[]{:S(2)}, u32[]{:S(2)}) collective-permute-start(bf16[256,1152]{1,0:T(8,128)(2,1)S(1)} %shard_map.80.refs_4_), channel_id=1, source_target_pairs={{0,6},{32,34},{2,4},{34,32},{4,2},{36,38},{6,0},{38,36},{64,70},{9... | collective-permute-start | bytes 1769480 | tf_op jit(solution)/shard_map/ppermute | solution.py:46
  67.7 0.4 collective-permute-done.12.refs_2_
  68.1 0.1 shard_map.81
  68.2 2.7 %collective-permute-start.17 = (bf16[128,1152]{1,0:T(8,128)(2,1)S(1)}, bf16[128,1152]{1,0:T(8,128)(2,1)S(1)}, u32[]{:S(2)}, u32[]{:S(2)}) collective-permute-start(bf16[128,1152]{1,0:T(8,128)(2,1)S(1)} %get-tuple-element.39), channel_id=1, source_target_pairs={{0,96},{32,65},{2,98},{34,67},{4,100},{36,69},{6,102},{38,71},{64,... | collective-permute-start | bytes 884744 | tf_op jit(solution)/shard_map/ppermute | solution.py:46
  70.9 0.3 collective-permute-start.19
  71.2 2.1 %shard_map.82.refs_1_ = f32[256,1152]{1,0:T(8,128)S(1)} custom-call(f32[2]{0:T(128)S(1)} %pad_maximum_fusion.affine, bf16[256,1152]{1,0:T(8,128)(2,1)S(1)} %get-tuple-element.24.refs_0_, bf16[1024,1152]{1,0:T(8,128)(2,1)S(1)} %collective-permute-done.10.refs_1_.refs_3_, f32[256,1152]{1,0:T(8,128)S(1)} %get-tuple-element.26.refs_4_.refs_2_, ...), custom_call_target="tpu_custom_call" | custom-call | flops 1207959552 | bytes 2359296 | tf_op jit(solution)/shard_map/pallas_call | solution.py:130
  73.3 1.1 %collective-permute-done.15.refs_2_ = bf16[256,1152]{1,0:T(8,128)(2,1)S(1)} collective-permute-done((bf16[256,1152]{1,0:T(8,128)(2,1)S(1)}, bf16[256,1152]{1,0:T(8,128)(2,1)S(1)}, u32[]{:S(2)}, u32[]{:S(2)}) %collective-permute-start.15) | collective-permute-done | bytes 589856 | tf_op jit(solution)/shard_map/ppermute | solution.py:46
  74.5 0.8 collective-permute-done.16.refs_3_
  75.3 0.2 shard_map.83
  75.4 1.7 %collective-permute-start.18 = (bf16[128,1152]{1,0:T(8,128)(2,1)S(1)}, bf16[128,1152]{1,0:T(8,128)(2,1)S(1)}, u32[]{:S(2)}, u32[]{:S(2)}) collective-permute-start(bf16[128,1152]{1,0:T(8,128)(2,1)S(1)} %get-tuple-element.41), channel_id=1, source_target_pairs={{0,32},{32,0},{1,33},{33,1},{2,34},{34,2},{3,35},{35,3},{4,36},{36... | collective-permute-start | bytes 884744 | tf_op jit(solution)/shard_map/ppermute | solution.py:50
  77.8 0.6 collective-permute-done.19.refs_4_
  78.5 1.6 %shard_map.84 = (f32[128,1152]{1,0:T(8,128)}, f32[128,1152]{1,0:T(8,128)}) custom-call(f32[1]{0:T(128)} %bitcast.refs_0_.is_first, f32[1]{0:T(128)S(6)} %div.3.multiplier, bf16[128,1152]{1,0:T(8,128)(2,1)S(1)} %copy-done.1, bf16[128,1152]{1,0:T(8,128)(2,1)S(1)} %copy-done.3, f32[128,1152]{1,0:T(8,128)S(1)} %get-tuple-element.40.refs_2_, ...), custom_call_target="tpu_custom_call" | custom-call | tf_op jit(solution)/shard_map/pallas_call | solution.py:267
  (18 shorter events, 0.1 us)
Async XLA Ops:
  0.6 3.7 %collective-permute-start = (bf16[128,1152]{1,0:T(8,128)(2,1)}, bf16[128,1152]{1,0:T(8,128)(2,1)S(1)}, u32[]{:S(2)}, u32[]{:S(2)}) collective-permute-start(bf16[128,1152]{1,0:T(8,128)(2,1)} %refs_0_.3), channel_id=1, source_target_pairs={{0,32},{32,0},{1,33},{33,1},{2,34},{34,2},{3,35},{35,3},{4,36},{36... | collective-permute-start | bytes 884744 | tf_op jit(solution)/shard_map/ppermute | solution.py:50
  2.1 2.3 %collective-permute-start.1 = (bf16[128,1152]{1,0:T(8,128)(2,1)}, bf16[128,1152]{1,0:T(8,128)(2,1)S(1)}, u32[]{:S(2)}, u32[]{:S(2)}) collective-permute-start(bf16[128,1152]{1,0:T(8,128)(2,1)} %refs_1_.3), channel_id=1, source_target_pairs={{0,32},{32,0},{1,33},{33,1},{2,34},{34,2},{3,35},{35,3},{4,36},{36... | collective-permute-start | bytes 884744 | tf_op jit(solution)/shard_map/ppermute | solution.py:50
  2.2 1.0 %copy-start = (bf16[128,1152]{1,0:T(8,128)(2,1)S(1)}, bf16[128,1152]{1,0:T(8,128)(2,1)}, u32[]{:S(2)}) copy-start(bf16[128,1152]{1,0:T(8,128)(2,1)} %refs_0_.3) | copy-start | bytes 884740
  3.2 1.0 %copy-start.2 = (bf16[128,1152]{1,0:T(8,128)(2,1)S(1)}, bf16[128,1152]{1,0:T(8,128)(2,1)}, u32[]{:S(2)}) copy-start(bf16[128,1152]{1,0:T(8,128)(2,1)} %refs_1_.3) | copy-start | bytes 884740
  4.8 10.3 %collective-permute-start.2 = (bf16[256,1152]{1,0:T(8,128)(2,1)S(1)}, bf16[256,1152]{1,0:T(8,128)(2,1)S(1)}, u32[]{:S(2)}, u32[]{:S(2)}) collective-permute-start(bf16[256,1152]{1,0:T(8,128)(2,1)S(1)} %get-tuple-element.24.refs_0_), channel_id=1, source_target_pairs={{0,8},{32,56},{2,10},{34,58},{4,12},{36,60},{6,14},{38,62},{64,72}... | collective-permute-start | bytes 1769480 | tf_op jit(solution)/shard_map/ppermute | solution.py:46
  7.4 10.3 %collective-permute-start.5 = (bf16[256,1152]{1,0:T(8,128)(2,1)S(1)}, bf16[256,1152]{1,0:T(8,128)(2,1)S(1)}, u32[]{:S(2)}, u32[]{:S(2)}) collective-permute-start(bf16[256,1152]{1,0:T(8,128)(2,1)S(1)} %get-tuple-element.24.refs_0_), channel_id=1, source_target_pairs={{0,64},{32,97},{2,66},{34,99},{4,68},{36,101},{6,70},{38,103},{64,... | collective-permute-start | bytes 1769480 | tf_op jit(solution)/shard_map/ppermute | solution.py:46
  10.1 9.2 %collective-permute-start.7 = (bf16[256,1152]{1,0:T(8,128)(2,1)S(1)}, bf16[256,1152]{1,0:T(8,128)(2,1)S(1)}, u32[]{:S(2)}, u32[]{:S(2)}) collective-permute-start(bf16[256,1152]{1,0:T(8,128)(2,1)S(1)} %get-tuple-element.24.refs_0_), channel_id=1, source_target_pairs={{0,6},{32,34},{2,4},{34,32},{4,2},{36,38},{6,0},{38,36},{64,70},{9... | collective-permute-start | bytes 1769480 | tf_op jit(solution)/shard_map/ppermute | solution.py:46
  19.5 8.1 %collective-permute-start.9 = (bf16[768,1152]{1,0:T(8,128)(2,1)S(1)}, bf16[768,1152]{1,0:T(8,128)(2,1)S(1)}, u32[]{:S(2)}, u32[]{:S(2)}) collective-permute-start(bf16[768,1152]{1,0:T(8,128)(2,1)S(1)} %shard_map.70), channel_id=1, source_target_pairs={{0,32},{32,0},{1,33},{33,1},{2,34},{34,2},{3,35},{35,3},{4,36},{36... | collective-permute-start | bytes 5308424 | tf_op jit(solution)/shard_map/ppermute | solution.py:50
  20.5 13.3 %collective-permute-start.3 = (bf16[256,1152]{1,0:T(8,128)(2,1)S(1)}, bf16[256,1152]{1,0:T(8,128)(2,1)S(1)}, u32[]{:S(2)}, u32[]{:S(2)}) collective-permute-start(bf16[256,1152]{1,0:T(8,128)(2,1)S(1)} %collective-permute-done.2.refs_0_.refs_3_), channel_id=1, source_target_pairs={{0,70},{32,99},{2,68},{34,97},{4,66},{36,103},{6,64},{38,101},{64,... | collective-permute-start | bytes 1769480 | tf_op jit(solution)/shard_map/ppermute | solution.py:46
  21.8 15.4 %collective-permute-start.4 = (bf16[256,1152]{1,0:T(8,128)(2,1)S(1)}, bf16[256,1152]{1,0:T(8,128)(2,1)S(1)}, u32[]{:S(2)}, u32[]{:S(2)}) collective-permute-start(bf16[256,1152]{1,0:T(8,128)(2,1)S(1)} %collective-permute-done.2.refs_0_.refs_3_), channel_id=1, source_target_pairs={{0,64},{32,97},{2,66},{34,99},{4,68},{36,101},{6,70},{38,103},{64,... | collective-permute-start | bytes 1769480 | tf_op jit(solution)/shard_map/ppermute | solution.py:46
  23.2 14.8 %collective-permute-start.6 = (bf16[256,1152]{1,0:T(8,128)(2,1)S(1)}, bf16[256,1152]{1,0:T(8,128)(2,1)S(1)}, u32[]{:S(2)}, u32[]{:S(2)}) collective-permute-start(bf16[256,1152]{1,0:T(8,128)(2,1)S(1)} %collective-permute-done.5.refs_1_.refs_4_.refs_3_), channel_id=1, source_target_pairs={{0,6},{32,34},{2,4},{34,32},{4,2},{36,38},{6,0},{38,36},{64,70},{9... | collective-permute-start | bytes 1769480 | tf_op jit(solution)/shard_map/ppermute | solution.py:46
  24.4 13.6 %collective-permute-start.8 = (bf16[256,1152]{1,0:T(8,128)(2,1)S(1)}, bf16[256,1152]{1,0:T(8,128)(2,1)S(1)}, u32[]{:S(2)}, u32[]{:S(2)}) collective-permute-start(bf16[256,1152]{1,0:T(8,128)(2,1)S(1)} %collective-permute-done.7.refs_2_.refs_5_), channel_id=1, source_target_pairs={{0,8},{32,56},{2,10},{34,58},{4,12},{36,60},{6,14},{38,62},{64,72}... | collective-permute-start | bytes 1769480 | tf_op jit(solution)/shard_map/ppermute | solution.py:46
  38.2 6.7 %collective-permute-start.10 = (bf16[1024,1152]{1,0:T(8,128)(2,1)S(1)}, bf16[1024,1152]{1,0:T(8,128)(2,1)S(1)}, u32[]{:S(2)}, u32[]{:S(2)}) collective-permute-start(bf16[1024,1152]{1,0:T(8,128)(2,1)S(1)} %shard_map.72), channel_id=1, source_target_pairs={{0,32},{32,0},{1,33},{33,1},{2,34},{34,2},{3,35},{35,3},{4,36},{36... | collective-permute-start | bytes 7077896 | tf_op jit(solution)/shard_map/ppermute | solution.py:50
  47.0 11.7 %collective-permute-start.11 = (bf16[256,1152]{1,0:T(8,128)(2,1)S(1)}, bf16[256,1152]{1,0:T(8,128)(2,1)S(1)}, u32[]{:S(2)}, u32[]{:S(2)}) collective-permute-start(bf16[256,1152]{1,0:T(8,128)(2,1)S(1)} %shard_map.74.refs_5_), channel_id=1, source_target_pairs={{0,8},{32,56},{2,10},{34,58},{4,12},{36,60},{6,14},{38,62},{64,72}... | collective-permute-start | bytes 1769480 | tf_op jit(solution)/shard_map/ppermute | solution.py:46
  52.4 11.6 %collective-permute-start.13 = (bf16[256,1152]{1,0:T(8,128)(2,1)S(1)}, bf16[256,1152]{1,0:T(8,128)(2,1)S(1)}, u32[]{:S(2)}, u32[]{:S(2)}) collective-permute-start(bf16[256,1152]{1,0:T(8,128)(2,1)S(1)} %get-tuple-element.33.refs_4_), channel_id=1, source_target_pairs={{0,64},{32,97},{2,66},{34,99},{4,68},{36,101},{6,70},{38,103},{64,... | collective-permute-start | bytes 1769480 | tf_op jit(solution)/shard_map/ppermute | solution.py:46
  54.3 11.7 %collective-permute-start.14 = (bf16[256,1152]{1,0:T(8,128)(2,1)S(1)}, bf16[256,1152]{1,0:T(8,128)(2,1)S(1)}, u32[]{:S(2)}, u32[]{:S(2)}) collective-permute-start(bf16[256,1152]{1,0:T(8,128)(2,1)S(1)} %get-tuple-element.37), channel_id=1, source_target_pairs={{0,8},{32,56},{2,10},{34,58},{4,12},{36,60},{6,14},{38,62},{64,72}... | collective-permute-start | bytes 1769480 | tf_op jit(solution)/shard_map/ppermute | solution.py:46
  58.8 9.3 %collective-permute-start.12 = (bf16[256,1152]{1,0:T(8,128)(2,1)S(1)}, bf16[256,1152]{1,0:T(8,128)(2,1)S(1)}, u32[]{:S(2)}, u32[]{:S(2)}) collective-permute-start(bf16[256,1152]{1,0:T(8,128)(2,1)S(1)} %shard_map.77.refs_7_), channel_id=1, source_target_pairs={{0,6},{32,34},{2,4},{34,32},{4,2},{36,38},{6,0},{38,36},{64,70},{9... | collective-permute-start | bytes 1769480 | tf_op jit(solution)/shard_map/ppermute | solution.py:46
  64.1 10.3 %collective-permute-start.15 = (bf16[256,1152]{1,0:T(8,128)(2,1)S(1)}, bf16[256,1152]{1,0:T(8,128)(2,1)S(1)}, u32[]{:S(2)}, u32[]{:S(2)}) collective-permute-start(bf16[256,1152]{1,0:T(8,128)(2,1)S(1)} %shard_map.79.refs_3_), channel_id=1, source_target_pairs={{0,8},{32,56},{2,10},{34,58},{4,12},{36,60},{6,14},{38,62},{64,72}... | collective-permute-start | bytes 1769480 | tf_op jit(solution)/shard_map/ppermute | solution.py:46
  66.2 9.1 %collective-permute-start.16 = (bf16[256,1152]{1,0:T(8,128)(2,1)S(1)}, bf16[256,1152]{1,0:T(8,128)(2,1)S(1)}, u32[]{:S(2)}, u32[]{:S(2)}) collective-permute-start(bf16[256,1152]{1,0:T(8,128)(2,1)S(1)} %shard_map.80.refs_4_), channel_id=1, source_target_pairs={{0,6},{32,34},{2,4},{34,32},{4,2},{36,38},{6,0},{38,36},{64,70},{9... | collective-permute-start | bytes 1769480 | tf_op jit(solution)/shard_map/ppermute | solution.py:46
  68.2 7.1 %collective-permute-start.17 = (bf16[128,1152]{1,0:T(8,128)(2,1)S(1)}, bf16[128,1152]{1,0:T(8,128)(2,1)S(1)}, u32[]{:S(2)}, u32[]{:S(2)}) collective-permute-start(bf16[128,1152]{1,0:T(8,128)(2,1)S(1)} %get-tuple-element.39), channel_id=1, source_target_pairs={{0,96},{32,65},{2,98},{34,67},{4,100},{36,69},{6,102},{38,71},{64,... | collective-permute-start | bytes 884744 | tf_op jit(solution)/shard_map/ppermute | solution.py:46
  70.9 7.6 %collective-permute-start.19 = (bf16[128,1152]{1,0:T(8,128)(2,1)S(1)}, bf16[128,1152]{1,0:T(8,128)(2,1)S(1)}, u32[]{:S(2)}, u32[]{:S(2)}) collective-permute-start(bf16[128,1152]{1,0:T(8,128)(2,1)S(1)} %get-tuple-element.38.refs_3_), channel_id=1, source_target_pairs={{0,64},{32,97},{2,66},{34,99},{4,68},{36,101},{6,70},{38,103},{64,... | collective-permute-start | bytes 884744 | tf_op jit(solution)/shard_map/ppermute | solution.py:46
  73.3 5.2 %copy-start.1 = (bf16[128,1152]{1,0:T(8,128)(2,1)S(1)}, bf16[128,1152]{1,0:T(8,128)(2,1)}, u32[]{:S(2)}) copy-start(bf16[128,1152]{1,0:T(8,128)(2,1)} %refs_0_.3) | copy-start | bytes 884740
  73.3 5.2 %copy-start.3 = (bf16[128,1152]{1,0:T(8,128)(2,1)S(1)}, bf16[128,1152]{1,0:T(8,128)(2,1)}, u32[]{:S(2)}) copy-start(bf16[128,1152]{1,0:T(8,128)(2,1)} %refs_1_.3) | copy-start | bytes 884740
  75.4 3.0 %collective-permute-start.18 = (bf16[128,1152]{1,0:T(8,128)(2,1)S(1)}, bf16[128,1152]{1,0:T(8,128)(2,1)S(1)}, u32[]{:S(2)}, u32[]{:S(2)}) collective-permute-start(bf16[128,1152]{1,0:T(8,128)(2,1)S(1)} %get-tuple-element.41), channel_id=1, source_target_pairs={{0,32},{32,0},{1,33},{33,1},{2,34},{34,2},{3,35},{35,3},{4,36},{36... | collective-permute-start | bytes 884744 | tf_op jit(solution)/shard_map/ppermute | solution.py:50

commit v15 on v14

--- a/solution.py
+++ b/solution.py
@@ -24,7 +24,7 @@
 PARAMS = pltpu.CompilerParams(vmem_limit_bytes=VMEM_BYTES)
 
 ONE = ("x", "y", "z")
-TWO = ("xyz", "xy", "yz", "zx")
+TWO = ("xy", "yz", "zx")
 
 
 def place(core, x, y, z):
@@ -219,9 +219,11 @@
     one = [own_theirs, stacked(ONE)]
     sums = sums_of(affine, [(mine[way], one, None) for way in near], diagonal=True, hides=False)
     sums = dict(zip(near, sums, strict=True))
-    two = [stacked(TWO, [sums[""]])]
-    ways = ("xyz", "xy", "zx")
-    sums |= zip(ways, sums_of(affine, [(mine[way], one, None) for way in ways]), strict=True)
+    corner_there = stacked(["xyz"], [sums[""]])
+    (sums["xyz"],) = sums_of(affine, [(mine["xyz"], one, None)], [sums[""]])
+    two = [corner_there, stacked(TWO, [sums["xyz"], corner_there])]
+    jobs = [(mine["xy"], one, None), (mine["zx"], one, None)]
+    sums["xy"], sums["zx"] = sums_of(affine, jobs, [sums["xyz"]])
 
     def parts_of(ways, after, kind=FULL):
         return sums_of(affine, [(mine[way], two, sums[way]) for way in ways], after, kind)
@@ -232,7 +234,7 @@
         )
         return total
 
-    (part_xyz,) = parts_of(["xyz"], [], HALF)
+    (part_xyz,) = parts_of(["xyz"], [sums["xy"]], HALF)
     for_yz = sent(part_xyz, "x")
     part_xy, part_zx = parts_of(["xy", "zx"], [part_xyz], HALF)
     for_x, for_z = sent(part_xy, "y"), sent(part_zx, "x")

time: 80.4 us -> 79.2 us (0.985)
  waiting for transfers between devices: 14.7 us -> 12.3 us
    ppermute x15, waiting for transfers between devices: 14.7 us -> 12.3 us  [sent(): return lax.ppermute(value, FINE_AXES, pairs)]
    pallas_call x7 -> x8, Pallas kernels: 27.2 us -> 28 us  [sums_of(): pl.pallas_call(functools.partial(sums_kernel, plan, len(inputs), len(afte...]
    ppermute x5 -> x6, starting transfers between devices: 6.22 us -> 6.44 us  [other_core(): return lax.ppermute(value, 'core', [(0, 1), (1, 0)])]
  transfers between devices with their start and end apart: 20 -> 21, of which waited for: 9 -> 9; matrix products, arithmetic and copies ran while one was open for 0% -> 0% of each run, Pallas kernels for 32% -> 34%
where the time goes in v15:
time: 79.2 us; the launch traced here: 79 us
  Pallas kernels  31 us (39%)
  starting transfers between devices  30.7 us (39%)
  waiting for transfers between devices  12.3 us (16%)
  between operations  2.96 us (4%)
  local copies, waits for them, and re-layouts  1.93 us (2%)
    pallas_call x8, Pallas kernels, sums_of(): pl.pallas_call(functools.partial(sums_kernel, plan, len(inputs), len(afte...  28 us
    ppermute x15, starting transfers between devices, sent(): return lax.ppermute(value, FINE_AXES, pairs)  24.3 us
    ppermute x15, waiting for transfers between devices, sent(): return lax.ppermute(value, FINE_AXES, pairs)  12.3 us
    ppermute x6, starting transfers between devices, other_core(): return lax.ppermute(value, 'core', [(0, 1), (1, 0)])  6.44 us
    unnamed x8, local copies, waits for them, and re-layouts  1.93 us
  transfers between devices with their start and end apart: 21, of which 9 were waited for; matrix products, arithmetic and copies ran while one was open for 0% of the time, Pallas kernels for 34%

profile of v15, /device:TPU:1, one launch (start us, length us, event | category | flops | bytes accessed | tf_op | source)
XLA Modules:
  0.0 79.0 jit_solution(18012413235675065660)
XLA Ops:
  0.6 1.5 %collective-permute-start = (bf16[128,1152]{1,0:T(8,128)(2,1)}, bf16[128,1152]{1,0:T(8,128)(2,1)S(1)}, u32[]{:S(2)}, u32[]{:S(2)}) collective-permute-start(bf16[128,1152]{1,0:T(8,128)(2,1)} %refs_0_.3), channel_id=1, source_target_pairs={{0,32},{32,0},{1,33},{33,1},{2,34},{34,2},{3,35},{35,3},{4,36},{36... | collective-permute-start | bytes 884744 | tf_op jit(solution)/shard_map/ppermute | solution.py:50
  2.2 1.0 %copy-done = bf16[128,1152]{1,0:T(8,128)(2,1)S(1)} copy-done((bf16[128,1152]{1,0:T(8,128)(2,1)S(1)}, bf16[128,1152]{1,0:T(8,128)(2,1)}, u32[]{:S(2)}) %copy-start) | copy-done | bytes 294936
  3.2 1.0 %copy-done.2 = bf16[128,1152]{1,0:T(8,128)(2,1)S(1)} copy-done((bf16[128,1152]{1,0:T(8,128)(2,1)S(1)}, bf16[128,1152]{1,0:T(8,128)(2,1)}, u32[]{:S(2)}) %copy-start.2) | copy-done | bytes 294936
  4.1 0.2 shard_map.68
  4.4 0.4 shard_map.69
  4.8 2.6 %collective-permute-start.2 = (bf16[256,1152]{1,0:T(8,128)(2,1)S(1)}, bf16[256,1152]{1,0:T(8,128)(2,1)S(1)}, u32[]{:S(2)}, u32[]{:S(2)}) collective-permute-start(bf16[256,1152]{1,0:T(8,128)(2,1)S(1)} %get-tuple-element.23.refs_0_), channel_id=1, source_target_pairs={{0,8},{32,56},{2,10},{34,58},{4,12},{36,60},{6,14},{38,62},{64,72}... | collective-permute-start | bytes 1769480 | tf_op jit(solution)/shard_map/ppermute | solution.py:46
  7.4 2.7 %collective-permute-start.4 = (bf16[256,1152]{1,0:T(8,128)(2,1)S(1)}, bf16[256,1152]{1,0:T(8,128)(2,1)S(1)}, u32[]{:S(2)}, u32[]{:S(2)}) collective-permute-start(bf16[256,1152]{1,0:T(8,128)(2,1)S(1)} %get-tuple-element.23.refs_0_), channel_id=1, source_target_pairs={{0,64},{32,97},{2,66},{34,99},{4,68},{36,101},{6,70},{38,103},{64,... | collective-permute-start | bytes 1769480 | tf_op jit(solution)/shard_map/ppermute | solution.py:46
  10.1 1.6 %collective-permute-start.5 = (bf16[256,1152]{1,0:T(8,128)(2,1)S(1)}, bf16[256,1152]{1,0:T(8,128)(2,1)S(1)}, u32[]{:S(2)}, u32[]{:S(2)}) collective-permute-start(bf16[256,1152]{1,0:T(8,128)(2,1)S(1)} %get-tuple-element.23.refs_0_), channel_id=1, source_target_pairs={{0,6},{32,34},{2,4},{34,32},{4,2},{36,38},{6,0},{38,36},{64,70},{9... | collective-permute-start | bytes 1769480 | tf_op jit(solution)/shard_map/ppermute | solution.py:46
  11.8 3.3 %collective-permute-done.2.refs_0_.refs_3_ = bf16[256,1152]{1,0:T(8,128)(2,1)S(1)} collective-permute-done((bf16[256,1152]{1,0:T(8,128)(2,1)S(1)}, bf16[256,1152]{1,0:T(8,128)(2,1)S(1)}, u32[]{:S(2)}, u32[]{:S(2)}) %collective-permute-start.2) | collective-permute-done | bytes 589856 | tf_op jit(solution)/shard_map/ppermute | solution.py:46
  15.1 2.6 %collective-permute-done.4.refs_1_.refs_4_ = bf16[256,1152]{1,0:T(8,128)(2,1)S(1)} collective-permute-done((bf16[256,1152]{1,0:T(8,128)(2,1)S(1)}, bf16[256,1152]{1,0:T(8,128)(2,1)S(1)}, u32[]{:S(2)}, u32[]{:S(2)}) %collective-permute-start.4) | collective-permute-done | bytes 589856 | tf_op jit(solution)/shard_map/ppermute | solution.py:46
  17.7 1.6 %collective-permute-done.5.refs_2_.refs_5_.refs_6_ = bf16[256,1152]{1,0:T(8,128)(2,1)S(1)} collective-permute-done((bf16[256,1152]{1,0:T(8,128)(2,1)S(1)}, bf16[256,1152]{1,0:T(8,128)(2,1)S(1)}, u32[]{:S(2)}, u32[]{:S(2)}) %collective-permute-start.5) | collective-permute-done | bytes 589856 | tf_op jit(solution)/shard_map/ppermute | solution.py:46
  19.3 0.1 shard_map.70
  19.5 1.0 %collective-permute-start.6 = (bf16[768,1152]{1,0:T(8,128)(2,1)S(1)}, bf16[768,1152]{1,0:T(8,128)(2,1)S(1)}, u32[]{:S(2)}, u32[]{:S(2)}) collective-permute-start(bf16[768,1152]{1,0:T(8,128)(2,1)S(1)} %shard_map.70), channel_id=1, source_target_pairs={{0,32},{32,0},{1,33},{33,1},{2,34},{34,2},{3,35},{35,3},{4,36},{36... | collective-permute-start | bytes 5308424 | tf_op jit(solution)/shard_map/ppermute | solution.py:50
  20.5 1.2 %collective-permute-start.3 = (bf16[256,1152]{1,0:T(8,128)(2,1)S(1)}, bf16[256,1152]{1,0:T(8,128)(2,1)S(1)}, u32[]{:S(2)}, u32[]{:S(2)}) collective-permute-start(bf16[256,1152]{1,0:T(8,128)(2,1)S(1)} %collective-permute-done.2.refs_0_.refs_3_), channel_id=1, source_target_pairs={{0,70},{32,99},{2,68},{34,97},{4,66},{36,103},{6,64},{38,101},{64,... | collective-permute-start | bytes 1769480 | tf_op jit(solution)/shard_map/ppermute | solution.py:46
  23.1 1.5 %collective-permute-start.8 = (bf16[256,1152]{1,0:T(8,128)(2,1)S(1)}, bf16[256,1152]{1,0:T(8,128)(2,1)S(1)}, u32[]{:S(2)}, u32[]{:S(2)}) collective-permute-start(bf16[256,1152]{1,0:T(8,128)(2,1)S(1)} %collective-permute-done.2.refs_0_.refs_3_), channel_id=1, source_target_pairs={{0,64},{32,97},{2,66},{34,99},{4,68},{36,101},{6,70},{38,103},{64,... | collective-permute-start | bytes 1769480 | tf_op jit(solution)/shard_map/ppermute | solution.py:46
  24.6 1.2 %collective-permute-start.9 = (bf16[256,1152]{1,0:T(8,128)(2,1)S(1)}, bf16[256,1152]{1,0:T(8,128)(2,1)S(1)}, u32[]{:S(2)}, u32[]{:S(2)}) collective-permute-start(bf16[256,1152]{1,0:T(8,128)(2,1)S(1)} %collective-permute-done.4.refs_1_.refs_4_), channel_id=1, source_target_pairs={{0,6},{32,34},{2,4},{34,32},{4,2},{36,38},{6,0},{38,36},{64,70},{9... | collective-permute-start | bytes 1769480 | tf_op jit(solution)/shard_map/ppermute | solution.py:46
  25.8 1.8 %collective-permute-start.10 = (bf16[256,1152]{1,0:T(8,128)(2,1)S(1)}, bf16[256,1152]{1,0:T(8,128)(2,1)S(1)}, u32[]{:S(2)}, u32[]{:S(2)}) collective-permute-start(bf16[256,1152]{1,0:T(8,128)(2,1)S(1)} %collective-permute-done.5.refs_2_.refs_5_.refs_6_), channel_id=1, source_target_pairs={{0,8},{32,56},{2,10},{34,58},{4,12},{36,60},{6,14},{38,62},{64,72}... | collective-permute-start | bytes 1769480 | tf_op jit(solution)/shard_map/ppermute | solution.py:46
  27.6 6.3 %shard_map.71 = (f32[256,1152]{1,0:T(8,128)S(1)}, f32[256,1152]{1,0:T(8,128)S(1)}, f32[256,1152]{1,0:T(8,128)S(1)}, f32[256,1152]{1,0:T(8,128)S(1)}) custom-call(f32[2]{0:T(128)S(1)} %pad_maximum_fusion.affine, bf16[256,1152]{1,0:T(8,128)(2,1)S(1)} %get-tuple-element.23.refs_0_, bf16[256,1152]{1,0:T(8,128)(2,1)S(1)} %get-tuple-element.24.refs_1_, ...), custom_call_target="tpu_custom_call" | custom-call | tf_op jit(solution)/shard_map/pallas_call | solution.py:130
  34.0 2.1 %shard_map.73.refs_3_.refs_4_ = f32[256,1152]{1,0:T(8,128)S(1)} custom-call(f32[2]{0:T(128)S(1)} %pad_maximum_fusion.affine, bf16[256,1152]{1,0:T(8,128)(2,1)S(1)} %collective-permute-done.3.refs_0_, bf16[256,1152]{1,0:T(8,128)(2,1)S(1)} %get-tuple-element.24.refs_1_, bf16[768,1152]{1,0:T(8,128)(2,1)S(1)} %collective-permute-done.6.refs_2_, ...), custom_call_target="tpu_custom_call" | custom-call | flops 1207959552 | bytes 2359296 | tf_op jit(solution)/shard_map/pallas_call | solution.py:130
  36.1 1.0 %collective-permute-done.8.refs_0_ = bf16[256,1152]{1,0:T(8,128)(2,1)S(1)} collective-permute-done((bf16[256,1152]{1,0:T(8,128)(2,1)S(1)}, bf16[256,1152]{1,0:T(8,128)(2,1)S(1)}, u32[]{:S(2)}, u32[]{:S(2)}) %collective-permute-start.8) | collective-permute-done | bytes 589856 | tf_op jit(solution)/shard_map/ppermute | solution.py:46
  37.1 0.8 %collective-permute-done.9.refs_1_.refs_0_ = bf16[256,1152]{1,0:T(8,128)(2,1)S(1)} collective-permute-done((bf16[256,1152]{1,0:T(8,128)(2,1)S(1)}, bf16[256,1152]{1,0:T(8,128)(2,1)S(1)}, u32[]{:S(2)}, u32[]{:S(2)}) %collective-permute-start.9) | collective-permute-done | bytes 589856 | tf_op jit(solution)/shard_map/ppermute | solution.py:46
  38.0 0.1 shard_map.74
  38.1 1.8 %collective-permute-start.11 = (bf16[768,1152]{1,0:T(8,128)(2,1)S(1)}, bf16[768,1152]{1,0:T(8,128)(2,1)S(1)}, u32[]{:S(2)}, u32[]{:S(2)}) collective-permute-start(bf16[768,1152]{1,0:T(8,128)(2,1)S(1)} %shard_map.74), channel_id=1, source_target_pairs={{0,32},{32,0},{1,33},{33,1},{2,34},{34,2},{3,35},{35,3},{4,36},{36... | collective-permute-start | bytes 5308424 | tf_op jit(solution)/shard_map/ppermute | solution.py:50
  40.0 3.5 %shard_map.75 = (f32[256,1152]{1,0:T(8,128)S(1)}, f32[256,1152]{1,0:T(8,128)S(1)}) custom-call(f32[2]{0:T(128)S(1)} %pad_maximum_fusion.affine, bf16[256,1152]{1,0:T(8,128)(2,1)S(1)} %collective-permute-done.8.refs_0_, bf16[256,1152]{1,0:T(8,128)(2,1)S(1)} %get-tuple-element.24.refs_1_, bf16[768,1152]{1,0:T(8,128)(2,1)S(1)} %collective-permute-done.6.refs_2_, ...), custom_call_target="tpu_custom_call" | custom-call | flops 2415919104 | bytes 4718592 | tf_op jit(solution)/shard_map/pallas_call | solution.py:130
  43.5 2.1 %shard_map.76.refs_6_ = bf16[256,1152]{1,0:T(8,128)(2,1)S(1)} custom-call(f32[2]{0:T(128)S(1)} %pad_maximum_fusion.affine, bf16[256,1152]{1,0:T(8,128)(2,1)S(1)} %collective-permute-done.3.refs_0_, bf16[256,1152]{1,0:T(8,128)(2,1)S(1)} %collective-permute-done.7.refs_4_.refs_1_.refs_3_, bf16[768,1152]{1,0:T(8,128)(2,1)S(1)} %collective-permute-done.11.refs_2_.refs_4_, ...), custom_call_target="tpu_custom_call" | custom-call | flops 1207959552 | bytes 2359296 | tf_op jit(solution)/shard_map/pallas_call | solution.py:130
  45.6 1.9 %collective-permute-start.12 = (bf16[256,1152]{1,0:T(8,128)(2,1)S(1)}, bf16[256,1152]{1,0:T(8,128)(2,1)S(1)}, u32[]{:S(2)}, u32[]{:S(2)}) collective-permute-start(bf16[256,1152]{1,0:T(8,128)(2,1)S(1)} %shard_map.76.refs_6_), channel_id=1, source_target_pairs={{0,8},{32,56},{2,10},{34,58},{4,12},{36,60},{6,14},{38,62},{64,72}... | collective-permute-start | bytes 1769480 | tf_op jit(solution)/shard_map/ppermute | solution.py:46
  47.5 3.5 %shard_map.77 = (bf16[256,1152]{1,0:T(8,128)(2,1)S(1)}, bf16[256,1152]{1,0:T(8,128)(2,1)S(1)}) custom-call(f32[2]{0:T(128)S(1)} %pad_maximum_fusion.affine, bf16[256,1152]{1,0:T(8,128)(2,1)S(1)} %collective-permute-done.8.refs_0_, bf16[256,1152]{1,0:T(8,128)(2,1)S(1)} %collective-permute-done.7.refs_4_.refs_1_.refs_3_, ...), custom_call_target="tpu_custom_call" | custom-call | flops 2415919104 | bytes 4718592 | tf_op jit(solution)/shard_map/pallas_call | solution.py:130
  51.0 2.0 %collective-permute-start.14 = (bf16[256,1152]{1,0:T(8,128)(2,1)S(1)}, bf16[256,1152]{1,0:T(8,128)(2,1)S(1)}, u32[]{:S(2)}, u32[]{:S(2)}) collective-permute-start(bf16[256,1152]{1,0:T(8,128)(2,1)S(1)} %get-tuple-element.31.refs_5_), channel_id=1, source_target_pairs={{0,64},{32,97},{2,66},{34,99},{4,68},{36,101},{6,70},{38,103},{64,... | collective-permute-start | bytes 1769480 | tf_op jit(solution)/shard_map/ppermute | solution.py:46
  53.0 0.9 %collective-permute-start.15 = (bf16[256,1152]{1,0:T(8,128)(2,1)S(1)}, bf16[256,1152]{1,0:T(8,128)(2,1)S(1)}, u32[]{:S(2)}, u32[]{:S(2)}) collective-permute-start(bf16[256,1152]{1,0:T(8,128)(2,1)S(1)} %get-tuple-element.35), channel_id=1, source_target_pairs={{0,8},{32,56},{2,10},{34,58},{4,12},{36,60},{6,14},{38,62},{64,72}... | collective-permute-start | bytes 1769480 | tf_op jit(solution)/shard_map/ppermute | solution.py:46
  53.8 3.5 %shard_map.78.refs_0_ = f32[256,1152]{1,0:T(8,128)S(1)} custom-call(f32[2]{0:T(128)S(1)} %pad_maximum_fusion.affine, bf16[256,1152]{1,0:T(8,128)(2,1)S(1)} %collective-permute-done.9.refs_1_.refs_0_, bf16[256,1152]{1,0:T(8,128)(2,1)S(1)} %get-tuple-element.24.refs_1_, bf16[768,1152]{1,0:T(8,128)(2,1)S(1)} %collective-permute-done.6.refs_2_, ...), custom_call_target="tpu_custom_call" | custom-call | flops 2415919104 | bytes 2359296 | tf_op jit(solution)/shard_map/pallas_call | solution.py:130
  57.3 0.1 shard_map.79.refs_8_
  57.4 0.3 collective-permute-start.13
  57.7 4.9 %shard_map.80 = (f32[256,1152]{1,0:T(8,128)S(1)}, f32[256,1152]{1,0:T(8,128)S(1)}, f32[256,1152]{1,0:T(8,128)S(1)}) custom-call(f32[2]{0:T(128)S(1)} %pad_maximum_fusion.affine, bf16[256,1152]{1,0:T(8,128)(2,1)S(1)} %collective-permute-done.2.refs_0_.refs_3_, bf16[256,1152]{1,0:T(8,128)(2,1)S(1)} %collective-permute-done.7.refs_4_.refs_1_.refs_3_, ...), custom_call_target="tpu_custom_call" | custom-call | flops 3623878656 | bytes 7077888 | tf_op jit(solution)/shard_map/pallas_call | solution.py:130
  62.6 0.1 shard_map.81.refs_3_
  62.8 1.9 %collective-permute-start.16 = (bf16[256,1152]{1,0:T(8,128)(2,1)S(1)}, bf16[256,1152]{1,0:T(8,128)(2,1)S(1)}, u32[]{:S(2)}, u32[]{:S(2)}) collective-permute-start(bf16[256,1152]{1,0:T(8,128)(2,1)S(1)} %shard_map.81.refs_3_), channel_id=1, source_target_pairs={{0,8},{32,56},{2,10},{34,58},{4,12},{36,60},{6,14},{38,62},{64,72}... | collective-permute-start | bytes 1769480 | tf_op jit(solution)/shard_map/ppermute | solution.py:46
  64.7 0.1 shard_map.82.refs_4_
  64.8 1.5 %collective-permute-start.17 = (bf16[256,1152]{1,0:T(8,128)(2,1)S(1)}, bf16[256,1152]{1,0:T(8,128)(2,1)S(1)}, u32[]{:S(2)}, u32[]{:S(2)}) collective-permute-start(bf16[256,1152]{1,0:T(8,128)(2,1)S(1)} %shard_map.82.refs_4_), channel_id=1, source_target_pairs={{0,6},{32,34},{2,4},{34,32},{4,2},{36,38},{6,0},{38,36},{64,70},{9... | collective-permute-start | bytes 1769480 | tf_op jit(solution)/shard_map/ppermute | solution.py:46
  66.3 0.5 collective-permute-done.13.refs_2_
  66.8 0.1 shard_map.83
  66.9 2.8 %collective-permute-start.18 = (bf16[128,1152]{1,0:T(8,128)(2,1)S(1)}, bf16[128,1152]{1,0:T(8,128)(2,1)S(1)}, u32[]{:S(2)}, u32[]{:S(2)}) collective-permute-start(bf16[128,1152]{1,0:T(8,128)(2,1)S(1)} %get-tuple-element.37), channel_id=1, source_target_pairs={{0,96},{32,65},{2,98},{34,67},{4,100},{36,69},{6,102},{38,71},{64,... | collective-permute-start | bytes 884744 | tf_op jit(solution)/shard_map/ppermute | solution.py:46
  69.7 0.3 collective-permute-start.20
  70.0 2.1 %shard_map.84.refs_1_ = f32[256,1152]{1,0:T(8,128)S(1)} custom-call(f32[2]{0:T(128)S(1)} %pad_maximum_fusion.affine, bf16[256,1152]{1,0:T(8,128)(2,1)S(1)} %get-tuple-element.23.refs_0_, bf16[256,1152]{1,0:T(8,128)(2,1)S(1)} %collective-permute-done.7.refs_4_.refs_1_.refs_3_, bf16[768,1152]{1,0:T(8,128)(2,1)S(1)} %collective-permute-done.11.refs_2_.refs_4_, ...), custom_call_target="tpu_custom_call" | custom-call | flops 1207959552 | bytes 2359296 | tf_op jit(solution)/shard_map/pallas_call | solution.py:130
  72.1 1.0 %collective-permute-done.16.refs_2_ = bf16[256,1152]{1,0:T(8,128)(2,1)S(1)} collective-permute-done((bf16[256,1152]{1,0:T(8,128)(2,1)S(1)}, bf16[256,1152]{1,0:T(8,128)(2,1)S(1)}, u32[]{:S(2)}, u32[]{:S(2)}) %collective-permute-start.16) | collective-permute-done | bytes 589856 | tf_op jit(solution)/shard_map/ppermute | solution.py:46
  73.1 0.8 collective-permute-done.17.refs_3_
  73.9 0.2 shard_map.85
  74.0 1.9 %collective-permute-start.19 = (bf16[128,1152]{1,0:T(8,128)(2,1)S(1)}, bf16[128,1152]{1,0:T(8,128)(2,1)S(1)}, u32[]{:S(2)}, u32[]{:S(2)}) collective-permute-start(bf16[128,1152]{1,0:T(8,128)(2,1)S(1)} %get-tuple-element.39), channel_id=1, source_target_pairs={{0,32},{32,0},{1,33},{33,1},{2,34},{34,2},{3,35},{35,3},{4,36},{36... | collective-permute-start | bytes 884744 | tf_op jit(solution)/shard_map/ppermute | solution.py:50
  76.6 0.7 collective-permute-done.20.refs_4_
  77.2 1.6 %shard_map.86 = (f32[128,1152]{1,0:T(8,128)}, f32[128,1152]{1,0:T(8,128)}) custom-call(f32[1]{0:T(128)} %bitcast.refs_0_.is_first, f32[1]{0:T(128)S(6)} %div.3.multiplier, bf16[128,1152]{1,0:T(8,128)(2,1)S(1)} %copy-done.1, bf16[128,1152]{1,0:T(8,128)(2,1)S(1)} %copy-done.3, f32[128,1152]{1,0:T(8,128)S(1)} %get-tuple-element.38.refs_2_, ...), custom_call_target="tpu_custom_call" | custom-call | tf_op jit(solution)/shard_map/pallas_call | solution.py:269
  (22 shorter events, 0.3 us)
Async XLA Ops:
  0.6 3.7 %collective-permute-start = (bf16[128,1152]{1,0:T(8,128)(2,1)}, bf16[128,1152]{1,0:T(8,128)(2,1)S(1)}, u32[]{:S(2)}, u32[]{:S(2)}) collective-permute-start(bf16[128,1152]{1,0:T(8,128)(2,1)} %refs_0_.3), channel_id=1, source_target_pairs={{0,32},{32,0},{1,33},{33,1},{2,34},{34,2},{3,35},{35,3},{4,36},{36... | collective-permute-start | bytes 884744 | tf_op jit(solution)/shard_map/ppermute | solution.py:50
  2.1 2.3 %collective-permute-start.1 = (bf16[128,1152]{1,0:T(8,128)(2,1)}, bf16[128,1152]{1,0:T(8,128)(2,1)S(1)}, u32[]{:S(2)}, u32[]{:S(2)}) collective-permute-start(bf16[128,1152]{1,0:T(8,128)(2,1)} %refs_1_.3), channel_id=1, source_target_pairs={{0,32},{32,0},{1,33},{33,1},{2,34},{34,2},{3,35},{35,3},{4,36},{36... | collective-permute-start | bytes 884744 | tf_op jit(solution)/shard_map/ppermute | solution.py:50
  2.2 1.0 %copy-start = (bf16[128,1152]{1,0:T(8,128)(2,1)S(1)}, bf16[128,1152]{1,0:T(8,128)(2,1)}, u32[]{:S(2)}) copy-start(bf16[128,1152]{1,0:T(8,128)(2,1)} %refs_0_.3) | copy-start | bytes 884740
  3.2 1.0 %copy-start.2 = (bf16[128,1152]{1,0:T(8,128)(2,1)S(1)}, bf16[128,1152]{1,0:T(8,128)(2,1)}, u32[]{:S(2)}) copy-start(bf16[128,1152]{1,0:T(8,128)(2,1)} %refs_1_.3) | copy-start | bytes 884740
  4.8 10.3 %collective-permute-start.2 = (bf16[256,1152]{1,0:T(8,128)(2,1)S(1)}, bf16[256,1152]{1,0:T(8,128)(2,1)S(1)}, u32[]{:S(2)}, u32[]{:S(2)}) collective-permute-start(bf16[256,1152]{1,0:T(8,128)(2,1)S(1)} %get-tuple-element.23.refs_0_), channel_id=1, source_target_pairs={{0,8},{32,56},{2,10},{34,58},{4,12},{36,60},{6,14},{38,62},{64,72}... | collective-permute-start | bytes 1769480 | tf_op jit(solution)/shard_map/ppermute | solution.py:46
  7.4 10.3 %collective-permute-start.4 = (bf16[256,1152]{1,0:T(8,128)(2,1)S(1)}, bf16[256,1152]{1,0:T(8,128)(2,1)S(1)}, u32[]{:S(2)}, u32[]{:S(2)}) collective-permute-start(bf16[256,1152]{1,0:T(8,128)(2,1)S(1)} %get-tuple-element.23.refs_0_), channel_id=1, source_target_pairs={{0,64},{32,97},{2,66},{34,99},{4,68},{36,101},{6,70},{38,103},{64,... | collective-permute-start | bytes 1769480 | tf_op jit(solution)/shard_map/ppermute | solution.py:46
  10.1 9.2 %collective-permute-start.5 = (bf16[256,1152]{1,0:T(8,128)(2,1)S(1)}, bf16[256,1152]{1,0:T(8,128)(2,1)S(1)}, u32[]{:S(2)}, u32[]{:S(2)}) collective-permute-start(bf16[256,1152]{1,0:T(8,128)(2,1)S(1)} %get-tuple-element.23.refs_0_), channel_id=1, source_target_pairs={{0,6},{32,34},{2,4},{34,32},{4,2},{36,38},{6,0},{38,36},{64,70},{9... | collective-permute-start | bytes 1769480 | tf_op jit(solution)/shard_map/ppermute | solution.py:46
  19.5 8.1 %collective-permute-start.6 = (bf16[768,1152]{1,0:T(8,128)(2,1)S(1)}, bf16[768,1152]{1,0:T(8,128)(2,1)S(1)}, u32[]{:S(2)}, u32[]{:S(2)}) collective-permute-start(bf16[768,1152]{1,0:T(8,128)(2,1)S(1)} %shard_map.70), channel_id=1, source_target_pairs={{0,32},{32,0},{1,33},{33,1},{2,34},{34,2},{3,35},{35,3},{4,36},{36... | collective-permute-start | bytes 5308424 | tf_op jit(solution)/shard_map/ppermute | solution.py:50
  20.5 13.4 %collective-permute-start.3 = (bf16[256,1152]{1,0:T(8,128)(2,1)S(1)}, bf16[256,1152]{1,0:T(8,128)(2,1)S(1)}, u32[]{:S(2)}, u32[]{:S(2)}) collective-permute-start(bf16[256,1152]{1,0:T(8,128)(2,1)S(1)} %collective-permute-done.2.refs_0_.refs_3_), channel_id=1, source_target_pairs={{0,70},{32,99},{2,68},{34,97},{4,66},{36,103},{6,64},{38,101},{64,... | collective-permute-start | bytes 1769480 | tf_op jit(solution)/shard_map/ppermute | solution.py:46
  23.1 14.0 %collective-permute-start.8 = (bf16[256,1152]{1,0:T(8,128)(2,1)S(1)}, bf16[256,1152]{1,0:T(8,128)(2,1)S(1)}, u32[]{:S(2)}, u32[]{:S(2)}) collective-permute-start(bf16[256,1152]{1,0:T(8,128)(2,1)S(1)} %collective-permute-done.2.refs_0_.refs_3_), channel_id=1, source_target_pairs={{0,64},{32,97},{2,66},{34,99},{4,68},{36,101},{6,70},{38,103},{64,... | collective-permute-start | bytes 1769480 | tf_op jit(solution)/shard_map/ppermute | solution.py:46
  24.6 13.4 %collective-permute-start.9 = (bf16[256,1152]{1,0:T(8,128)(2,1)S(1)}, bf16[256,1152]{1,0:T(8,128)(2,1)S(1)}, u32[]{:S(2)}, u32[]{:S(2)}) collective-permute-start(bf16[256,1152]{1,0:T(8,128)(2,1)S(1)} %collective-permute-done.4.refs_1_.refs_4_), channel_id=1, source_target_pairs={{0,6},{32,34},{2,4},{34,32},{4,2},{36,38},{6,0},{38,36},{64,70},{9... | collective-permute-start | bytes 1769480 | tf_op jit(solution)/shard_map/ppermute | solution.py:46
  25.8 12.2 %collective-permute-start.10 = (bf16[256,1152]{1,0:T(8,128)(2,1)S(1)}, bf16[256,1152]{1,0:T(8,128)(2,1)S(1)}, u32[]{:S(2)}, u32[]{:S(2)}) collective-permute-start(bf16[256,1152]{1,0:T(8,128)(2,1)S(1)} %collective-permute-done.5.refs_2_.refs_5_.refs_6_), channel_id=1, source_target_pairs={{0,8},{32,56},{2,10},{34,58},{4,12},{36,60},{6,14},{38,62},{64,72}... | collective-permute-start | bytes 1769480 | tf_op jit(solution)/shard_map/ppermute | solution.py:46
  33.9 4.1 %collective-permute-start.7 = (bf16[256,1152]{1,0:T(8,128)(2,1)S(1)}, bf16[256,1152]{1,0:T(8,128)(2,1)S(1)}, u32[]{:S(2)}, u32[]{:S(2)}) collective-permute-start(bf16[256,1152]{1,0:T(8,128)(2,1)S(1)} %shard_map.72), channel_id=1, source_target_pairs={{0,32},{32,0},{1,33},{33,1},{2,34},{34,2},{3,35},{35,3},{4,36},{36... | collective-permute-start | bytes 1769480 | tf_op jit(solution)/shard_map/ppermute | solution.py:50
  38.1 5.4 %collective-permute-start.11 = (bf16[768,1152]{1,0:T(8,128)(2,1)S(1)}, bf16[768,1152]{1,0:T(8,128)(2,1)S(1)}, u32[]{:S(2)}, u32[]{:S(2)}) collective-permute-start(bf16[768,1152]{1,0:T(8,128)(2,1)S(1)} %shard_map.74), channel_id=1, source_target_pairs={{0,32},{32,0},{1,33},{33,1},{2,34},{34,2},{3,35},{35,3},{4,36},{36... | collective-permute-start | bytes 5308424 | tf_op jit(solution)/shard_map/ppermute | solution.py:50
  45.6 11.7 %collective-permute-start.12 = (bf16[256,1152]{1,0:T(8,128)(2,1)S(1)}, bf16[256,1152]{1,0:T(8,128)(2,1)S(1)}, u32[]{:S(2)}, u32[]{:S(2)}) collective-permute-start(bf16[256,1152]{1,0:T(8,128)(2,1)S(1)} %shard_map.76.refs_6_), channel_id=1, source_target_pairs={{0,8},{32,56},{2,10},{34,58},{4,12},{36,60},{6,14},{38,62},{64,72}... | collective-permute-start | bytes 1769480 | tf_op jit(solution)/shard_map/ppermute | solution.py:46
  51.0 11.6 %collective-permute-start.14 = (bf16[256,1152]{1,0:T(8,128)(2,1)S(1)}, bf16[256,1152]{1,0:T(8,128)(2,1)S(1)}, u32[]{:S(2)}, u32[]{:S(2)}) collective-permute-start(bf16[256,1152]{1,0:T(8,128)(2,1)S(1)} %get-tuple-element.31.refs_5_), channel_id=1, source_target_pairs={{0,64},{32,97},{2,66},{34,99},{4,68},{36,101},{6,70},{38,103},{64,... | collective-permute-start | bytes 1769480 | tf_op jit(solution)/shard_map/ppermute | solution.py:46
  53.0 11.7 %collective-permute-start.15 = (bf16[256,1152]{1,0:T(8,128)(2,1)S(1)}, bf16[256,1152]{1,0:T(8,128)(2,1)S(1)}, u32[]{:S(2)}, u32[]{:S(2)}) collective-permute-start(bf16[256,1152]{1,0:T(8,128)(2,1)S(1)} %get-tuple-element.35), channel_id=1, source_target_pairs={{0,8},{32,56},{2,10},{34,58},{4,12},{36,60},{6,14},{38,62},{64,72}... | collective-permute-start | bytes 1769480 | tf_op jit(solution)/shard_map/ppermute | solution.py:46
  57.4 9.3 %collective-permute-start.13 = (bf16[256,1152]{1,0:T(8,128)(2,1)S(1)}, bf16[256,1152]{1,0:T(8,128)(2,1)S(1)}, u32[]{:S(2)}, u32[]{:S(2)}) collective-permute-start(bf16[256,1152]{1,0:T(8,128)(2,1)S(1)} %shard_map.79.refs_8_), channel_id=1, source_target_pairs={{0,6},{32,34},{2,4},{34,32},{4,2},{36,38},{6,0},{38,36},{64,70},{9... | collective-permute-start | bytes 1769480 | tf_op jit(solution)/shard_map/ppermute | solution.py:46
  62.8 10.3 %collective-permute-start.16 = (bf16[256,1152]{1,0:T(8,128)(2,1)S(1)}, bf16[256,1152]{1,0:T(8,128)(2,1)S(1)}, u32[]{:S(2)}, u32[]{:S(2)}) collective-permute-start(bf16[256,1152]{1,0:T(8,128)(2,1)S(1)} %shard_map.81.refs_3_), channel_id=1, source_target_pairs={{0,8},{32,56},{2,10},{34,58},{4,12},{36,60},{6,14},{38,62},{64,72}... | collective-permute-start | bytes 1769480 | tf_op jit(solution)/shard_map/ppermute | solution.py:46
  64.8 9.1 %collective-permute-start.17 = (bf16[256,1152]{1,0:T(8,128)(2,1)S(1)}, bf16[256,1152]{1,0:T(8,128)(2,1)S(1)}, u32[]{:S(2)}, u32[]{:S(2)}) collective-permute-start(bf16[256,1152]{1,0:T(8,128)(2,1)S(1)} %shard_map.82.refs_4_), channel_id=1, source_target_pairs={{0,6},{32,34},{2,4},{34,32},{4,2},{36,38},{6,0},{38,36},{64,70},{9... | collective-permute-start | bytes 1769480 | tf_op jit(solution)/shard_map/ppermute | solution.py:46
  66.9 7.0 %collective-permute-start.18 = (bf16[128,1152]{1,0:T(8,128)(2,1)S(1)}, bf16[128,1152]{1,0:T(8,128)(2,1)S(1)}, u32[]{:S(2)}, u32[]{:S(2)}) collective-permute-start(bf16[128,1152]{1,0:T(8,128)(2,1)S(1)} %get-tuple-element.37), channel_id=1, source_target_pairs={{0,96},{32,65},{2,98},{34,67},{4,100},{36,69},{6,102},{38,71},{64,... | collective-permute-start | bytes 884744 | tf_op jit(solution)/shard_map/ppermute | solution.py:46
  69.7 7.6 %collective-permute-start.20 = (bf16[128,1152]{1,0:T(8,128)(2,1)S(1)}, bf16[128,1152]{1,0:T(8,128)(2,1)S(1)}, u32[]{:S(2)}, u32[]{:S(2)}) collective-permute-start(bf16[128,1152]{1,0:T(8,128)(2,1)S(1)} %get-tuple-element.36.refs_4_), channel_id=1, source_target_pairs={{0,64},{32,97},{2,66},{34,99},{4,68},{36,101},{6,70},{38,103},{64,... | collective-permute-start | bytes 884744 | tf_op jit(solution)/shard_map/ppermute | solution.py:46
  72.1 5.2 %copy-start.1 = (bf16[128,1152]{1,0:T(8,128)(2,1)S(1)}, bf16[128,1152]{1,0:T(8,128)(2,1)}, u32[]{:S(2)}) copy-start(bf16[128,1152]{1,0:T(8,128)(2,1)} %refs_0_.3) | copy-start | bytes 884740
  72.1 5.2 %copy-start.3 = (bf16[128,1152]{1,0:T(8,128)(2,1)S(1)}, bf16[128,1152]{1,0:T(8,128)(2,1)}, u32[]{:S(2)}) copy-start(bf16[128,1152]{1,0:T(8,128)(2,1)} %refs_1_.3) | copy-start | bytes 884740
  74.0 3.2 %collective-permute-start.19 = (bf16[128,1152]{1,0:T(8,128)(2,1)S(1)}, bf16[128,1152]{1,0:T(8,128)(2,1)S(1)}, u32[]{:S(2)}, u32[]{:S(2)}) collective-permute-start(bf16[128,1152]{1,0:T(8,128)(2,1)S(1)} %get-tuple-element.39), channel_id=1, source_target_pairs={{0,32},{32,0},{1,33},{33,1},{2,34},{34,2},{3,35},{35,3},{4,36},{36... | collective-permute-start | bytes 884744 | tf_op jit(solution)/shard_map/ppermute | solution.py:50

commit v16 on v15

--- a/solution.py
+++ b/solution.py
@@ -82,10 +82,11 @@
 
 def accumulate(affine, mine, theirs, coupling, start, diagonal):
     unit = mine.shape[0]
+    slope, shift = 0.5 * affine[0][0], 0.5 * affine[1][0]
     pieces = [(ref, k) for ref in theirs for k in range(0, ref.shape[0], unit)]
     for n, (ref, k) in enumerate(pieces):
         energies = dot(mine, ref[pl.ds(k, unit), :], (1, 1))
-        tile = 0.5 * jnp.tanh(affine[0] * energies + affine[1]) + 0.5
+        tile = 0.5 * jnp.tanh(slope * energies + shift) + 0.5
         if diagonal and n == 0:
             row = lax.broadcasted_iota(jnp.int32, tile.shape, 0)
             column = lax.broadcasted_iota(jnp.int32, tile.shape, 1)
@@ -100,7 +101,8 @@
     return total
 
 
-def sums_kernel(plan, n_inputs, n_after, diagonal, affine, *refs):
+def sums_kernel(plan, n_inputs, n_after, diagonal, *refs):
+    affine, refs = refs[:2], refs[2:]
     inputs, results, coupling = refs[:n_inputs], refs[n_inputs + n_after : -1], refs[-1]
     for k, (mine, theirs, start) in enumerate(plan):
         begin = None if start is None else inputs[start][...]
@@ -130,7 +132,7 @@
     return pl.pallas_call(
         functools.partial(sums_kernel, plan, len(inputs), len(after), diagonal),
         out_shape=[jax.ShapeDtypeStruct((unit, width), kind)] * len(jobs),
-        in_specs=[SMEM] + [VMEM] * len(inputs) + [ANY] * len(after),
+        in_specs=[SMEM] * 2 + [VMEM] * len(inputs) + [ANY] * len(after),
         out_specs=[VMEM] * len(jobs),
         scratch_shapes=[pltpu.VMEM((unit, widest), HALF)],
         cost_estimate=pl.CostEstimate(
@@ -139,7 +141,7 @@
             transcendentals=tiles * unit**2 if hides else 0,
         ),
         compiler_params=PARAMS,
-    )(affine, *inputs, *after)
+    )(*affine, *inputs, *after)
 
 
 def finish_kernel(is_first, multiplier, *refs):
@@ -168,7 +170,7 @@
     core = lax.axis_index("core").astype(jnp.int32)
     is_first = core == 0
     first_flag = is_first.astype(FULL).reshape(1)
-    affine = jnp.concatenate([0.5 * logit_multiplier, 0.5 * offset_term])
+    affine = (logit_multiplier, offset_term)
     multiplier = incoming_adjoint * logit_multiplier / pairs
     shard, unit = ((rows, width), HALF), ((2 * rows, width), HALF)
     shard_full = ((rows, width), FULL)
@@ -198,11 +200,11 @@
         own_units, [unit] * 2, [first_flag], [image_there, text_there, image, text]
     )
 
-    def stacked(ways, after=()):
+    def stacked(ways, after=(), scalars=()):
         (stack,) = local(
             lambda _, refs: [jnp.concatenate([ref[...] for ref in refs], 0)],
             [((2 * rows * len(ways), width), HALF)],
-            [],
+            scalars,
             [mine[way] for way in ways],
             after,
         )
@@ -216,7 +218,7 @@
     mine["yz"] = sent(mine["y"], "z")
     mine["zx"] = sent(mine["z"], "x")
     near = ("", *ONE)
-    one = [own_theirs, stacked(ONE)]
+    one = [own_theirs, stacked(ONE, scalars=affine)]
     sums = sums_of(affine, [(mine[way], one, None) for way in near], diagonal=True, hides=False)
     sums = dict(zip(near, sums, strict=True))
     corner_there = stacked(["xyz"], [sums[""]])

time: 79.2 us -> 78.7 us (level)
  Pallas kernels: 31 us -> 26.5 us
  starting transfers between devices: 30.7 us -> 33.2 us
  waiting for transfers between devices: 12.3 us -> 13.8 us
    pallas_call x8, Pallas kernels: 28 us -> 23.4 us  [sums_of(): pl.pallas_call(functools.partial(sums_kernel, plan, len(inputs), len(afte...]
    ppermute x15, starting transfers between devices: 24.3 us -> 25.6 us  [sent(): return lax.ppermute(value, FINE_AXES, pairs)]
    ppermute x6, starting transfers between devices: 6.44 us -> 7.65 us  [other_core(): return lax.ppermute(value, 'core', [(0, 1), (1, 0)])]
    ppermute x15, waiting for transfers between devices: 12.3 us -> 13.5 us  [sent(): return lax.ppermute(value, FINE_AXES, pairs)]
  transfers between devices with their start and end apart: 21 -> 21, of which waited for: 9 -> 10; matrix products, arithmetic and copies ran while one was open for 0% -> 0% of each run, Pallas kernels for 34% -> 29%
where the time goes in v16:
time: 78.7 us; the launch traced here: 78.5 us
  starting transfers between devices  33.2 us (42%)
  Pallas kernels  26.5 us (34%)
  waiting for transfers between devices  13.8 us (18%)
  between operations  2.96 us (4%)
  local copies, waits for them, and re-layouts  1.93 us (2%)
    ppermute x15, starting transfers between devices, sent(): return lax.ppermute(value, FINE_AXES, pairs)  25.6 us
    pallas_call x8, Pallas kernels, sums_of(): pl.pallas_call(functools.partial(sums_kernel, plan, len(inputs), len(afte...  23.4 us
    ppermute x15, waiting for transfers between devices, sent(): return lax.ppermute(value, FINE_AXES, pairs)  13.5 us
    ppermute x6, starting transfers between devices, other_core(): return lax.ppermute(value, 'core', [(0, 1), (1, 0)])  7.65 us
    unnamed x8, local copies, waits for them, and re-layouts  1.93 us
    pallas_call x1, Pallas kernels, on_device(): pl.pallas_call(finish_kernel, out_shape=[jax.ShapeDtypeStruct(*shard_full...  1.58 us
  transfers between devices with their start and end apart: 21, of which 10 were waited for; matrix products, arithmetic and copies ran while one was open for 0% of the time, Pallas kernels for 29%

profile of v16, /device:TPU:1, one launch (start us, length us, event | category | flops | bytes accessed | tf_op | source)
XLA Modules:
  0.0 78.5 jit_solution(13030839460269732999)
XLA Ops:
  0.6 1.5 %collective-permute-start = (bf16[128,1152]{1,0:T(8,128)(2,1)}, bf16[128,1152]{1,0:T(8,128)(2,1)S(1)}, u32[]{:S(2)}, u32[]{:S(2)}) collective-permute-start(bf16[128,1152]{1,0:T(8,128)(2,1)} %refs_0_.12), channel_id=1, source_target_pairs={{0,32},{32,0},{1,33},{33,1},{2,34},{34,2},{3,35},{35,3},{4,36},{36... | collective-permute-start | bytes 884744 | tf_op jit(solution)/shard_map/ppermute | solution.py:50
  2.2 1.0 %copy-done = bf16[128,1152]{1,0:T(8,128)(2,1)S(1)} copy-done((bf16[128,1152]{1,0:T(8,128)(2,1)S(1)}, bf16[128,1152]{1,0:T(8,128)(2,1)}, u32[]{:S(2)}) %copy-start) | copy-done | bytes 294936
  3.2 1.0 %copy-done.2 = bf16[128,1152]{1,0:T(8,128)(2,1)S(1)} copy-done((bf16[128,1152]{1,0:T(8,128)(2,1)S(1)}, bf16[128,1152]{1,0:T(8,128)(2,1)}, u32[]{:S(2)}) %copy-start.2) | copy-done | bytes 294936
  4.1 0.2 shard_map.68
  4.4 0.4 shard_map.69
  4.8 2.6 %collective-permute-start.2 = (bf16[256,1152]{1,0:T(8,128)(2,1)S(1)}, bf16[256,1152]{1,0:T(8,128)(2,1)S(1)}, u32[]{:S(2)}, u32[]{:S(2)}) collective-permute-start(bf16[256,1152]{1,0:T(8,128)(2,1)S(1)} %get-tuple-element.23.refs_2_), channel_id=1, source_target_pairs={{0,8},{32,56},{2,10},{34,58},{4,12},{36,60},{6,14},{38,62},{64,72}... | collective-permute-start | bytes 1769480 | tf_op jit(solution)/shard_map/ppermute | solution.py:46
  7.4 2.7 %collective-permute-start.4 = (bf16[256,1152]{1,0:T(8,128)(2,1)S(1)}, bf16[256,1152]{1,0:T(8,128)(2,1)S(1)}, u32[]{:S(2)}, u32[]{:S(2)}) collective-permute-start(bf16[256,1152]{1,0:T(8,128)(2,1)S(1)} %get-tuple-element.23.refs_2_), channel_id=1, source_target_pairs={{0,64},{32,97},{2,66},{34,99},{4,68},{36,101},{6,70},{38,103},{64,... | collective-permute-start | bytes 1769480 | tf_op jit(solution)/shard_map/ppermute | solution.py:46
  10.1 1.6 %collective-permute-start.5 = (bf16[256,1152]{1,0:T(8,128)(2,1)S(1)}, bf16[256,1152]{1,0:T(8,128)(2,1)S(1)}, u32[]{:S(2)}, u32[]{:S(2)}) collective-permute-start(bf16[256,1152]{1,0:T(8,128)(2,1)S(1)} %get-tuple-element.23.refs_2_), channel_id=1, source_target_pairs={{0,6},{32,34},{2,4},{34,32},{4,2},{36,38},{6,0},{38,36},{64,70},{9... | collective-permute-start | bytes 1769480 | tf_op jit(solution)/shard_map/ppermute | solution.py:46
  13.1 2.0 %collective-permute-done.2.refs_2_.refs_5_ = bf16[256,1152]{1,0:T(8,128)(2,1)S(1)} collective-permute-done((bf16[256,1152]{1,0:T(8,128)(2,1)S(1)}, bf16[256,1152]{1,0:T(8,128)(2,1)S(1)}, u32[]{:S(2)}, u32[]{:S(2)}) %collective-permute-start.2) | collective-permute-done | bytes 589856 | tf_op jit(solution)/shard_map/ppermute | solution.py:46
  15.1 2.6 %collective-permute-done.4.refs_3_.refs_6_ = bf16[256,1152]{1,0:T(8,128)(2,1)S(1)} collective-permute-done((bf16[256,1152]{1,0:T(8,128)(2,1)S(1)}, bf16[256,1152]{1,0:T(8,128)(2,1)S(1)}, u32[]{:S(2)}, u32[]{:S(2)}) %collective-permute-start.4) | collective-permute-done | bytes 589856 | tf_op jit(solution)/shard_map/ppermute | solution.py:46
  17.7 1.6 %collective-permute-done.5.refs_4_.refs_7_.refs_8_ = bf16[256,1152]{1,0:T(8,128)(2,1)S(1)} collective-permute-done((bf16[256,1152]{1,0:T(8,128)(2,1)S(1)}, bf16[256,1152]{1,0:T(8,128)(2,1)S(1)}, u32[]{:S(2)}, u32[]{:S(2)}) %collective-permute-start.5) | collective-permute-done | bytes 589856 | tf_op jit(solution)/shard_map/ppermute | solution.py:46
  19.3 0.1 shard_map.70
  19.5 1.0 %collective-permute-start.6 = (bf16[768,1152]{1,0:T(8,128)(2,1)S(1)}, bf16[768,1152]{1,0:T(8,128)(2,1)S(1)}, u32[]{:S(2)}, u32[]{:S(2)}) collective-permute-start(bf16[768,1152]{1,0:T(8,128)(2,1)S(1)} %shard_map.70), channel_id=1, source_target_pairs={{0,32},{32,0},{1,33},{33,1},{2,34},{34,2},{3,35},{35,3},{4,36},{36... | collective-permute-start | bytes 5308424 | tf_op jit(solution)/shard_map/ppermute | solution.py:50
  20.5 1.2 %collective-permute-start.3 = (bf16[256,1152]{1,0:T(8,128)(2,1)S(1)}, bf16[256,1152]{1,0:T(8,128)(2,1)S(1)}, u32[]{:S(2)}, u32[]{:S(2)}) collective-permute-start(bf16[256,1152]{1,0:T(8,128)(2,1)S(1)} %collective-permute-done.2.refs_2_.refs_5_), channel_id=1, source_target_pairs={{0,70},{32,99},{2,68},{34,97},{4,66},{36,103},{6,64},{38,101},{64,... | collective-permute-start | bytes 1769480 | tf_op jit(solution)/shard_map/ppermute | solution.py:46
  21.8 1.4 %collective-permute-start.8 = (bf16[256,1152]{1,0:T(8,128)(2,1)S(1)}, bf16[256,1152]{1,0:T(8,128)(2,1)S(1)}, u32[]{:S(2)}, u32[]{:S(2)}) collective-permute-start(bf16[256,1152]{1,0:T(8,128)(2,1)S(1)} %collective-permute-done.2.refs_2_.refs_5_), channel_id=1, source_target_pairs={{0,64},{32,97},{2,66},{34,99},{4,68},{36,101},{6,70},{38,103},{64,... | collective-permute-start | bytes 1769480 | tf_op jit(solution)/shard_map/ppermute | solution.py:46
  23.2 1.2 %collective-permute-start.9 = (bf16[256,1152]{1,0:T(8,128)(2,1)S(1)}, bf16[256,1152]{1,0:T(8,128)(2,1)S(1)}, u32[]{:S(2)}, u32[]{:S(2)}) collective-permute-start(bf16[256,1152]{1,0:T(8,128)(2,1)S(1)} %collective-permute-done.4.refs_3_.refs_6_), channel_id=1, source_target_pairs={{0,6},{32,34},{2,4},{34,32},{4,2},{36,38},{6,0},{38,36},{64,70},{9... | collective-permute-start | bytes 1769480 | tf_op jit(solution)/shard_map/ppermute | solution.py:46
  24.4 1.8 %collective-permute-start.10 = (bf16[256,1152]{1,0:T(8,128)(2,1)S(1)}, bf16[256,1152]{1,0:T(8,128)(2,1)S(1)}, u32[]{:S(2)}, u32[]{:S(2)}) collective-permute-start(bf16[256,1152]{1,0:T(8,128)(2,1)S(1)} %collective-permute-done.5.refs_4_.refs_7_.refs_8_), channel_id=1, source_target_pairs={{0,8},{32,56},{2,10},{34,58},{4,12},{36,60},{6,14},{38,62},{64,72}... | collective-permute-start | bytes 1769480 | tf_op jit(solution)/shard_map/ppermute | solution.py:46
  26.2 5.7 %shard_map.71 = (f32[256,1152]{1,0:T(8,128)S(1)}, f32[256,1152]{1,0:T(8,128)S(1)}, f32[256,1152]{1,0:T(8,128)S(1)}, f32[256,1152]{1,0:T(8,128)S(1)}) custom-call(f32[1]{0:T(128)S(6)} %copy.7.refs_0_, f32[1]{0:T(128)S(6)} %copy.8.refs_1_, bf16[256,1152]{1,0:T(8,128)(2,1)S(1)} %get-tuple-element.23.refs_2_, bf16[256,1152]{1,0:T(8,128)(2,1)S(1)} %get-tuple-element.24.refs_3_, ...), custom_call_target="tpu_custom_call" | custom-call | tf_op jit(solution)/shard_map/pallas_call | solution.py:132
  32.0 0.9 %collective-permute-start.7 = (bf16[256,1152]{1,0:T(8,128)(2,1)S(1)}, bf16[256,1152]{1,0:T(8,128)(2,1)S(1)}, u32[]{:S(2)}, u32[]{:S(2)}) collective-permute-start(bf16[256,1152]{1,0:T(8,128)(2,1)S(1)} %shard_map.72), channel_id=1, source_target_pairs={{0,32},{32,0},{1,33},{33,1},{2,34},{34,2},{3,35},{35,3},{4,36},{36... | collective-permute-start | bytes 1769480 | tf_op jit(solution)/shard_map/ppermute | solution.py:50
  32.8 1.6 %shard_map.73.refs_3_.refs_6_.refs_5_ = f32[256,1152]{1,0:T(8,128)S(1)} custom-call(f32[1]{0:T(128)S(6)} %copy.7.refs_0_, f32[1]{0:T(128)S(6)} %copy.8.refs_1_, bf16[256,1152]{1,0:T(8,128)(2,1)S(1)} %collective-permute-done.3.refs_0_.refs_2_, bf16[256,1152]{1,0:T(8,128)(2,1)S(1)} %get-tuple-element.24.refs_3_, ...), custom_call_target="tpu_custom_call" | custom-call | flops 1207959552 | bytes 2359296 | tf_op jit(solution)/shard_map/pallas_call | solution.py:132
  34.4 2.7 %collective-permute-done.8.refs_0_.refs_2_ = bf16[256,1152]{1,0:T(8,128)(2,1)S(1)} collective-permute-done((bf16[256,1152]{1,0:T(8,128)(2,1)S(1)}, bf16[256,1152]{1,0:T(8,128)(2,1)S(1)}, u32[]{:S(2)}, u32[]{:S(2)}) %collective-permute-start.8) | collective-permute-done | bytes 589856 | tf_op jit(solution)/shard_map/ppermute | solution.py:46
  37.1 0.8 %collective-permute-done.9.refs_1_.refs_2_ = bf16[256,1152]{1,0:T(8,128)(2,1)S(1)} collective-permute-done((bf16[256,1152]{1,0:T(8,128)(2,1)S(1)}, bf16[256,1152]{1,0:T(8,128)(2,1)S(1)}, u32[]{:S(2)}, u32[]{:S(2)}) %collective-permute-start.9) | collective-permute-done | bytes 589856 | tf_op jit(solution)/shard_map/ppermute | solution.py:46
  38.0 0.1 shard_map.74
  38.1 1.8 %collective-permute-start.11 = (bf16[768,1152]{1,0:T(8,128)(2,1)S(1)}, bf16[768,1152]{1,0:T(8,128)(2,1)S(1)}, u32[]{:S(2)}, u32[]{:S(2)}) collective-permute-start(bf16[768,1152]{1,0:T(8,128)(2,1)S(1)} %shard_map.74), channel_id=1, source_target_pairs={{0,32},{32,0},{1,33},{33,1},{2,34},{34,2},{3,35},{35,3},{4,36},{36... | collective-permute-start | bytes 5308424 | tf_op jit(solution)/shard_map/ppermute | solution.py:50
  40.0 2.9 %shard_map.75 = (f32[256,1152]{1,0:T(8,128)S(1)}, f32[256,1152]{1,0:T(8,128)S(1)}) custom-call(f32[1]{0:T(128)S(6)} %copy.7.refs_0_, f32[1]{0:T(128)S(6)} %copy.8.refs_1_, bf16[256,1152]{1,0:T(8,128)(2,1)S(1)} %collective-permute-done.8.refs_0_.refs_2_, bf16[256,1152]{1,0:T(8,128)(2,1)S(1)} %get-tuple-element.24.refs_3_, ...), custom_call_target="tpu_custom_call" | custom-call | flops 2415919104 | bytes 4718592 | tf_op jit(solution)/shard_map/pallas_call | solution.py:132
  42.9 0.4 collective-permute-done.11.refs_4_.refs_6_
  43.3 1.6 %shard_map.76.refs_8_ = bf16[256,1152]{1,0:T(8,128)(2,1)S(1)} custom-call(f32[1]{0:T(128)S(6)} %copy.7.refs_0_, f32[1]{0:T(128)S(6)} %copy.8.refs_1_, bf16[256,1152]{1,0:T(8,128)(2,1)S(1)} %collective-permute-done.3.refs_0_.refs_2_, bf16[256,1152]{1,0:T(8,128)(2,1)S(1)} %collective-permute-done.7.refs_4_.refs_3_.refs_5_, ...), custom_call_target="tpu_custom_call" | custom-call | flops 1207959552 | bytes 2359296 | tf_op jit(solution)/shard_map/pallas_call | solution.py:132
  44.8 1.9 %collective-permute-start.12 = (bf16[256,1152]{1,0:T(8,128)(2,1)S(1)}, bf16[256,1152]{1,0:T(8,128)(2,1)S(1)}, u32[]{:S(2)}, u32[]{:S(2)}) collective-permute-start(bf16[256,1152]{1,0:T(8,128)(2,1)S(1)} %shard_map.76.refs_8_), channel_id=1, source_target_pairs={{0,8},{32,56},{2,10},{34,58},{4,12},{36,60},{6,14},{38,62},{64,72}... | collective-permute-start | bytes 1769480 | tf_op jit(solution)/shard_map/ppermute | solution.py:46
  46.7 2.9 %shard_map.77 = (bf16[256,1152]{1,0:T(8,128)(2,1)S(1)}, bf16[256,1152]{1,0:T(8,128)(2,1)S(1)}) custom-call(f32[1]{0:T(128)S(6)} %copy.7.refs_0_, f32[1]{0:T(128)S(6)} %copy.8.refs_1_, bf16[256,1152]{1,0:T(8,128)(2,1)S(1)} %collective-permute-done.8.refs_0_.refs_2_, bf16[256,1152]{1,0:T(8,128)(2,1)S(1)} %collective-permute-done.7.refs_4_.refs_3_.refs_5_, ...), custom_call_target="tpu_custom_call" | custom-call | flops 2415919104 | bytes 4718592 | tf_op jit(solution)/shard_map/pallas_call | solution.py:132
  49.6 2.0 %collective-permute-start.14 = (bf16[256,1152]{1,0:T(8,128)(2,1)S(1)}, bf16[256,1152]{1,0:T(8,128)(2,1)S(1)}, u32[]{:S(2)}, u32[]{:S(2)}) collective-permute-start(bf16[256,1152]{1,0:T(8,128)(2,1)S(1)} %get-tuple-element.31.refs_7_), channel_id=1, source_target_pairs={{0,64},{32,97},{2,66},{34,99},{4,68},{36,101},{6,70},{38,103},{64,... | collective-permute-start | bytes 1769480 | tf_op jit(solution)/shard_map/ppermute | solution.py:46
  51.6 0.9 %collective-permute-start.15 = (bf16[256,1152]{1,0:T(8,128)(2,1)S(1)}, bf16[256,1152]{1,0:T(8,128)(2,1)S(1)}, u32[]{:S(2)}, u32[]{:S(2)}) collective-permute-start(bf16[256,1152]{1,0:T(8,128)(2,1)S(1)} %get-tuple-element.35), channel_id=1, source_target_pairs={{0,8},{32,56},{2,10},{34,58},{4,12},{36,60},{6,14},{38,62},{64,72}... | collective-permute-start | bytes 1769480 | tf_op jit(solution)/shard_map/ppermute | solution.py:46
  52.5 2.9 %shard_map.78.refs_0_ = f32[256,1152]{1,0:T(8,128)S(1)} custom-call(f32[1]{0:T(128)S(6)} %copy.7.refs_0_, f32[1]{0:T(128)S(6)} %copy.8.refs_1_, bf16[256,1152]{1,0:T(8,128)(2,1)S(1)} %collective-permute-done.9.refs_1_.refs_2_, bf16[256,1152]{1,0:T(8,128)(2,1)S(1)} %get-tuple-element.24.refs_3_, bf16[768,1152]{1,0:T(8,128)(2,1)S(1)} %collective-permute-done.6.refs_4_, ...), custom_call_target="tpu_custom_call" | custom-call | flops 2415919104 | bytes 2359296 | tf_op jit(solution)/shard_map/pallas_call | solution.py:132
  55.4 0.1 shard_map.79.refs_10_
  55.5 0.3 collective-permute-start.13
  55.8 4.3 %shard_map.80 = (f32[256,1152]{1,0:T(8,128)S(1)}, f32[256,1152]{1,0:T(8,128)S(1)}, f32[256,1152]{1,0:T(8,128)S(1)}) custom-call(f32[1]{0:T(128)S(6)} %copy.7.refs_0_, f32[1]{0:T(128)S(6)} %copy.8.refs_1_, bf16[256,1152]{1,0:T(8,128)(2,1)S(1)} %collective-permute-done.2.refs_2_.refs_5_, bf16[256,1152]{1,0:T(8,128)(2,1)S(1)} %collective-permute-done.7.refs_4_.refs_3_.refs_5_, ...), custom_call_target="tpu_custom_call" | custom-call | flops 3623878656 | bytes 7077888 | tf_op jit(solution)/shard_map/pallas_call | solution.py:132
  60.1 0.1 shard_map.81.refs_3_
  60.3 1.9 %collective-permute-start.16 = (bf16[256,1152]{1,0:T(8,128)(2,1)S(1)}, bf16[256,1152]{1,0:T(8,128)(2,1)S(1)}, u32[]{:S(2)}, u32[]{:S(2)}) collective-permute-start(bf16[256,1152]{1,0:T(8,128)(2,1)S(1)} %shard_map.81.refs_3_), channel_id=1, source_target_pairs={{0,8},{32,56},{2,10},{34,58},{4,12},{36,60},{6,14},{38,62},{64,72}... | collective-permute-start | bytes 1769480 | tf_op jit(solution)/shard_map/ppermute | solution.py:46
  62.2 1.5 %collective-permute-start.17 = (bf16[256,1152]{1,0:T(8,128)(2,1)S(1)}, bf16[256,1152]{1,0:T(8,128)(2,1)S(1)}, u32[]{:S(2)}, u32[]{:S(2)}) collective-permute-start(bf16[256,1152]{1,0:T(8,128)(2,1)S(1)} %shard_map.82.refs_4_), channel_id=1, source_target_pairs={{0,6},{32,34},{2,4},{34,32},{4,2},{36,38},{6,0},{38,36},{64,70},{9... | collective-permute-start | bytes 1769480 | tf_op jit(solution)/shard_map/ppermute | solution.py:46
  63.8 1.1 %collective-permute-done.13.refs_2_ = bf16[256,1152]{1,0:T(8,128)(2,1)S(1)} collective-permute-done((bf16[256,1152]{1,0:T(8,128)(2,1)S(1)}, bf16[256,1152]{1,0:T(8,128)(2,1)S(1)}, u32[]{:S(2)}, u32[]{:S(2)}) %collective-permute-start.13) | collective-permute-done | bytes 589856 | tf_op jit(solution)/shard_map/ppermute | solution.py:46
  65.0 3.7 %collective-permute-start.18 = (bf16[128,1152]{1,0:T(8,128)(2,1)S(1)}, bf16[128,1152]{1,0:T(8,128)(2,1)S(1)}, u32[]{:S(2)}, u32[]{:S(2)}) collective-permute-start(bf16[128,1152]{1,0:T(8,128)(2,1)S(1)} %get-tuple-element.37), channel_id=1, source_target_pairs={{0,96},{32,65},{2,98},{34,67},{4,100},{36,69},{6,102},{38,71},{64,... | collective-permute-start | bytes 884744 | tf_op jit(solution)/shard_map/ppermute | solution.py:46
  68.6 0.8 %collective-permute-start.20 = (bf16[128,1152]{1,0:T(8,128)(2,1)S(1)}, bf16[128,1152]{1,0:T(8,128)(2,1)S(1)}, u32[]{:S(2)}, u32[]{:S(2)}) collective-permute-start(bf16[128,1152]{1,0:T(8,128)(2,1)S(1)} %get-tuple-element.36.refs_6_), channel_id=1, source_target_pairs={{0,64},{32,97},{2,66},{34,99},{4,68},{36,101},{6,70},{38,103},{64,... | collective-permute-start | bytes 884744 | tf_op jit(solution)/shard_map/ppermute | solution.py:46
  69.4 1.6 %shard_map.84.refs_1_ = f32[256,1152]{1,0:T(8,128)S(1)} custom-call(f32[1]{0:T(128)S(6)} %copy.7.refs_0_, f32[1]{0:T(128)S(6)} %copy.8.refs_1_, bf16[256,1152]{1,0:T(8,128)(2,1)S(1)} %get-tuple-element.23.refs_2_, bf16[256,1152]{1,0:T(8,128)(2,1)S(1)} %collective-permute-done.7.refs_4_.refs_3_.refs_5_, ...), custom_call_target="tpu_custom_call" | custom-call | flops 1207959552 | bytes 2359296 | tf_op jit(solution)/shard_map/pallas_call | solution.py:132
  71.0 0.3 collective-permute-done.17.refs_3_
  71.4 0.9 %collective-permute-done.18.refs_4_.refs_5_ = bf16[128,1152]{1,0:T(8,128)(2,1)S(1)} collective-permute-done((bf16[128,1152]{1,0:T(8,128)(2,1)S(1)}, bf16[128,1152]{1,0:T(8,128)(2,1)S(1)}, u32[]{:S(2)}, u32[]{:S(2)}) %collective-permute-start.18) | collective-permute-done | bytes 294944 | tf_op jit(solution)/shard_map/ppermute | solution.py:46
  72.3 0.2 shard_map.85
  72.5 2.3 %collective-permute-start.19 = (bf16[128,1152]{1,0:T(8,128)(2,1)S(1)}, bf16[128,1152]{1,0:T(8,128)(2,1)S(1)}, u32[]{:S(2)}, u32[]{:S(2)}) collective-permute-start(bf16[128,1152]{1,0:T(8,128)(2,1)S(1)} %get-tuple-element.39), channel_id=1, source_target_pairs={{0,32},{32,0},{1,33},{33,1},{2,34},{34,2},{3,35},{35,3},{4,36},{36... | collective-permute-start | bytes 884744 | tf_op jit(solution)/shard_map/ppermute | solution.py:50
  75.4 1.3 %collective-permute-done.20.refs_4_ = bf16[128,1152]{1,0:T(8,128)(2,1)S(1)} collective-permute-done((bf16[128,1152]{1,0:T(8,128)(2,1)S(1)}, bf16[128,1152]{1,0:T(8,128)(2,1)S(1)}, u32[]{:S(2)}, u32[]{:S(2)}) %collective-permute-start.20) | collective-permute-done | bytes 294944 | tf_op jit(solution)/shard_map/ppermute | solution.py:46
  76.7 1.6 %shard_map.86 = (f32[128,1152]{1,0:T(8,128)}, f32[128,1152]{1,0:T(8,128)}) custom-call(f32[1]{0:T(128)} %bitcast.refs_0_.is_first, f32[1]{0:T(128)S(6)} %div.3.multiplier, bf16[128,1152]{1,0:T(8,128)(2,1)S(1)} %copy-done.1, bf16[128,1152]{1,0:T(8,128)(2,1)S(1)} %copy-done.3, f32[128,1152]{1,0:T(8,128)S(1)} %get-tuple-element.38.refs_2_, ...), custom_call_target="tpu_custom_call" | custom-call | tf_op jit(solution)/shard_map/pallas_call | solution.py:271
  (21 shorter events, 0.4 us)
Async XLA Ops:
  0.6 3.7 %collective-permute-start = (bf16[128,1152]{1,0:T(8,128)(2,1)}, bf16[128,1152]{1,0:T(8,128)(2,1)S(1)}, u32[]{:S(2)}, u32[]{:S(2)}) collective-permute-start(bf16[128,1152]{1,0:T(8,128)(2,1)} %refs_0_.12), channel_id=1, source_target_pairs={{0,32},{32,0},{1,33},{33,1},{2,34},{34,2},{3,35},{35,3},{4,36},{36... | collective-permute-start | bytes 884744 | tf_op jit(solution)/shard_map/ppermute | solution.py:50
  2.1 2.3 %collective-permute-start.1 = (bf16[128,1152]{1,0:T(8,128)(2,1)}, bf16[128,1152]{1,0:T(8,128)(2,1)S(1)}, u32[]{:S(2)}, u32[]{:S(2)}) collective-permute-start(bf16[128,1152]{1,0:T(8,128)(2,1)} %refs_1_.12), channel_id=1, source_target_pairs={{0,32},{32,0},{1,33},{33,1},{2,34},{34,2},{3,35},{35,3},{4,36},{36... | collective-permute-start | bytes 884744 | tf_op jit(solution)/shard_map/ppermute | solution.py:50
  2.2 1.0 %copy-start = (bf16[128,1152]{1,0:T(8,128)(2,1)S(1)}, bf16[128,1152]{1,0:T(8,128)(2,1)}, u32[]{:S(2)}) copy-start(bf16[128,1152]{1,0:T(8,128)(2,1)} %refs_0_.12) | copy-start | bytes 884740
  3.2 1.0 %copy-start.2 = (bf16[128,1152]{1,0:T(8,128)(2,1)S(1)}, bf16[128,1152]{1,0:T(8,128)(2,1)}, u32[]{:S(2)}) copy-start(bf16[128,1152]{1,0:T(8,128)(2,1)} %refs_1_.12) | copy-start | bytes 884740
  4.8 10.3 %collective-permute-start.2 = (bf16[256,1152]{1,0:T(8,128)(2,1)S(1)}, bf16[256,1152]{1,0:T(8,128)(2,1)S(1)}, u32[]{:S(2)}, u32[]{:S(2)}) collective-permute-start(bf16[256,1152]{1,0:T(8,128)(2,1)S(1)} %get-tuple-element.23.refs_2_), channel_id=1, source_target_pairs={{0,8},{32,56},{2,10},{34,58},{4,12},{36,60},{6,14},{38,62},{64,72}... | collective-permute-start | bytes 1769480 | tf_op jit(solution)/shard_map/ppermute | solution.py:46
  7.4 10.3 %collective-permute-start.4 = (bf16[256,1152]{1,0:T(8,128)(2,1)S(1)}, bf16[256,1152]{1,0:T(8,128)(2,1)S(1)}, u32[]{:S(2)}, u32[]{:S(2)}) collective-permute-start(bf16[256,1152]{1,0:T(8,128)(2,1)S(1)} %get-tuple-element.23.refs_2_), channel_id=1, source_target_pairs={{0,64},{32,97},{2,66},{34,99},{4,68},{36,101},{6,70},{38,103},{64,... | collective-permute-start | bytes 1769480 | tf_op jit(solution)/shard_map/ppermute | solution.py:46
  10.1 9.2 %collective-permute-start.5 = (bf16[256,1152]{1,0:T(8,128)(2,1)S(1)}, bf16[256,1152]{1,0:T(8,128)(2,1)S(1)}, u32[]{:S(2)}, u32[]{:S(2)}) collective-permute-start(bf16[256,1152]{1,0:T(8,128)(2,1)S(1)} %get-tuple-element.23.refs_2_), channel_id=1, source_target_pairs={{0,6},{32,34},{2,4},{34,32},{4,2},{36,38},{6,0},{38,36},{64,70},{9... | collective-permute-start | bytes 1769480 | tf_op jit(solution)/shard_map/ppermute | solution.py:46
  19.5 6.7 %collective-permute-start.6 = (bf16[768,1152]{1,0:T(8,128)(2,1)S(1)}, bf16[768,1152]{1,0:T(8,128)(2,1)S(1)}, u32[]{:S(2)}, u32[]{:S(2)}) collective-permute-start(bf16[768,1152]{1,0:T(8,128)(2,1)S(1)} %shard_map.70), channel_id=1, source_target_pairs={{0,32},{32,0},{1,33},{33,1},{2,34},{34,2},{3,35},{35,3},{4,36},{36... | collective-permute-start | bytes 5308424 | tf_op jit(solution)/shard_map/ppermute | solution.py:50
  20.5 11.4 %collective-permute-start.3 = (bf16[256,1152]{1,0:T(8,128)(2,1)S(1)}, bf16[256,1152]{1,0:T(8,128)(2,1)S(1)}, u32[]{:S(2)}, u32[]{:S(2)}) collective-permute-start(bf16[256,1152]{1,0:T(8,128)(2,1)S(1)} %collective-permute-done.2.refs_2_.refs_5_), channel_id=1, source_target_pairs={{0,70},{32,99},{2,68},{34,97},{4,66},{36,103},{6,64},{38,101},{64,... | collective-permute-start | bytes 1769480 | tf_op jit(solution)/shard_map/ppermute | solution.py:46
  21.8 15.4 %collective-permute-start.8 = (bf16[256,1152]{1,0:T(8,128)(2,1)S(1)}, bf16[256,1152]{1,0:T(8,128)(2,1)S(1)}, u32[]{:S(2)}, u32[]{:S(2)}) collective-permute-start(bf16[256,1152]{1,0:T(8,128)(2,1)S(1)} %collective-permute-done.2.refs_2_.refs_5_), channel_id=1, source_target_pairs={{0,64},{32,97},{2,66},{34,99},{4,68},{36,101},{6,70},{38,103},{64,... | collective-permute-start | bytes 1769480 | tf_op jit(solution)/shard_map/ppermute | solution.py:46
  23.2 14.8 %collective-permute-start.9 = (bf16[256,1152]{1,0:T(8,128)(2,1)S(1)}, bf16[256,1152]{1,0:T(8,128)(2,1)S(1)}, u32[]{:S(2)}, u32[]{:S(2)}) collective-permute-start(bf16[256,1152]{1,0:T(8,128)(2,1)S(1)} %collective-permute-done.4.refs_3_.refs_6_), channel_id=1, source_target_pairs={{0,6},{32,34},{2,4},{34,32},{4,2},{36,38},{6,0},{38,36},{64,70},{9... | collective-permute-start | bytes 1769480 | tf_op jit(solution)/shard_map/ppermute | solution.py:46
  24.4 13.6 %collective-permute-start.10 = (bf16[256,1152]{1,0:T(8,128)(2,1)S(1)}, bf16[256,1152]{1,0:T(8,128)(2,1)S(1)}, u32[]{:S(2)}, u32[]{:S(2)}) collective-permute-start(bf16[256,1152]{1,0:T(8,128)(2,1)S(1)} %collective-permute-done.5.refs_4_.refs_7_.refs_8_), channel_id=1, source_target_pairs={{0,8},{32,56},{2,10},{34,58},{4,12},{36,60},{6,14},{38,62},{64,72}... | collective-permute-start | bytes 1769480 | tf_op jit(solution)/shard_map/ppermute | solution.py:46
  32.0 6.0 %collective-permute-start.7 = (bf16[256,1152]{1,0:T(8,128)(2,1)S(1)}, bf16[256,1152]{1,0:T(8,128)(2,1)S(1)}, u32[]{:S(2)}, u32[]{:S(2)}) collective-permute-start(bf16[256,1152]{1,0:T(8,128)(2,1)S(1)} %shard_map.72), channel_id=1, source_target_pairs={{0,32},{32,0},{1,33},{33,1},{2,34},{34,2},{3,35},{35,3},{4,36},{36... | collective-permute-start | bytes 1769480 | tf_op jit(solution)/shard_map/ppermute | solution.py:50
  38.1 5.2 %collective-permute-start.11 = (bf16[768,1152]{1,0:T(8,128)(2,1)S(1)}, bf16[768,1152]{1,0:T(8,128)(2,1)S(1)}, u32[]{:S(2)}, u32[]{:S(2)}) collective-permute-start(bf16[768,1152]{1,0:T(8,128)(2,1)S(1)} %shard_map.74), channel_id=1, source_target_pairs={{0,32},{32,0},{1,33},{33,1},{2,34},{34,2},{3,35},{35,3},{4,36},{36... | collective-permute-start | bytes 5308424 | tf_op jit(solution)/shard_map/ppermute | solution.py:50
  44.8 10.6 %collective-permute-start.12 = (bf16[256,1152]{1,0:T(8,128)(2,1)S(1)}, bf16[256,1152]{1,0:T(8,128)(2,1)S(1)}, u32[]{:S(2)}, u32[]{:S(2)}) collective-permute-start(bf16[256,1152]{1,0:T(8,128)(2,1)S(1)} %shard_map.76.refs_8_), channel_id=1, source_target_pairs={{0,8},{32,56},{2,10},{34,58},{4,12},{36,60},{6,14},{38,62},{64,72}... | collective-permute-start | bytes 1769480 | tf_op jit(solution)/shard_map/ppermute | solution.py:46
  49.6 10.5 %collective-permute-start.14 = (bf16[256,1152]{1,0:T(8,128)(2,1)S(1)}, bf16[256,1152]{1,0:T(8,128)(2,1)S(1)}, u32[]{:S(2)}, u32[]{:S(2)}) collective-permute-start(bf16[256,1152]{1,0:T(8,128)(2,1)S(1)} %get-tuple-element.31.refs_7_), channel_id=1, source_target_pairs={{0,64},{32,97},{2,66},{34,99},{4,68},{36,101},{6,70},{38,103},{64,... | collective-permute-start | bytes 1769480 | tf_op jit(solution)/shard_map/ppermute | solution.py:46
  51.6 10.5 %collective-permute-start.15 = (bf16[256,1152]{1,0:T(8,128)(2,1)S(1)}, bf16[256,1152]{1,0:T(8,128)(2,1)S(1)}, u32[]{:S(2)}, u32[]{:S(2)}) collective-permute-start(bf16[256,1152]{1,0:T(8,128)(2,1)S(1)} %get-tuple-element.35), channel_id=1, source_target_pairs={{0,8},{32,56},{2,10},{34,58},{4,12},{36,60},{6,14},{38,62},{64,72}... | collective-permute-start | bytes 1769480 | tf_op jit(solution)/shard_map/ppermute | solution.py:46
  55.5 9.3 %collective-permute-start.13 = (bf16[256,1152]{1,0:T(8,128)(2,1)S(1)}, bf16[256,1152]{1,0:T(8,128)(2,1)S(1)}, u32[]{:S(2)}, u32[]{:S(2)}) collective-permute-start(bf16[256,1152]{1,0:T(8,128)(2,1)S(1)} %shard_map.79.refs_10_), channel_id=1, source_target_pairs={{0,6},{32,34},{2,4},{34,32},{4,2},{36,38},{6,0},{38,36},{64,70},{9... | collective-permute-start | bytes 1769480 | tf_op jit(solution)/shard_map/ppermute | solution.py:46
  60.3 10.8 %collective-permute-start.16 = (bf16[256,1152]{1,0:T(8,128)(2,1)S(1)}, bf16[256,1152]{1,0:T(8,128)(2,1)S(1)}, u32[]{:S(2)}, u32[]{:S(2)}) collective-permute-start(bf16[256,1152]{1,0:T(8,128)(2,1)S(1)} %shard_map.81.refs_3_), channel_id=1, source_target_pairs={{0,8},{32,56},{2,10},{34,58},{4,12},{36,60},{6,14},{38,62},{64,72}... | collective-permute-start | bytes 1769480 | tf_op jit(solution)/shard_map/ppermute | solution.py:46
  62.2 9.1 %collective-permute-start.17 = (bf16[256,1152]{1,0:T(8,128)(2,1)S(1)}, bf16[256,1152]{1,0:T(8,128)(2,1)S(1)}, u32[]{:S(2)}, u32[]{:S(2)}) collective-permute-start(bf16[256,1152]{1,0:T(8,128)(2,1)S(1)} %shard_map.82.refs_4_), channel_id=1, source_target_pairs={{0,6},{32,34},{2,4},{34,32},{4,2},{36,38},{6,0},{38,36},{64,70},{9... | collective-permute-start | bytes 1769480 | tf_op jit(solution)/shard_map/ppermute | solution.py:46
  65.0 7.3 %collective-permute-start.18 = (bf16[128,1152]{1,0:T(8,128)(2,1)S(1)}, bf16[128,1152]{1,0:T(8,128)(2,1)S(1)}, u32[]{:S(2)}, u32[]{:S(2)}) collective-permute-start(bf16[128,1152]{1,0:T(8,128)(2,1)S(1)} %get-tuple-element.37), channel_id=1, source_target_pairs={{0,96},{32,65},{2,98},{34,67},{4,100},{36,69},{6,102},{38,71},{64,... | collective-permute-start | bytes 884744 | tf_op jit(solution)/shard_map/ppermute | solution.py:46
  68.6 8.1 %collective-permute-start.20 = (bf16[128,1152]{1,0:T(8,128)(2,1)S(1)}, bf16[128,1152]{1,0:T(8,128)(2,1)S(1)}, u32[]{:S(2)}, u32[]{:S(2)}) collective-permute-start(bf16[128,1152]{1,0:T(8,128)(2,1)S(1)} %get-tuple-element.36.refs_6_), channel_id=1, source_target_pairs={{0,64},{32,97},{2,66},{34,99},{4,68},{36,101},{6,70},{38,103},{64,... | collective-permute-start | bytes 884744 | tf_op jit(solution)/shard_map/ppermute | solution.py:46
  71.0 5.7 %copy-start.1 = (bf16[128,1152]{1,0:T(8,128)(2,1)S(1)}, bf16[128,1152]{1,0:T(8,128)(2,1)}, u32[]{:S(2)}) copy-start(bf16[128,1152]{1,0:T(8,128)(2,1)} %refs_0_.12) | copy-start | bytes 884740
  71.0 5.7 %copy-start.3 = (bf16[128,1152]{1,0:T(8,128)(2,1)S(1)}, bf16[128,1152]{1,0:T(8,128)(2,1)}, u32[]{:S(2)}) copy-start(bf16[128,1152]{1,0:T(8,128)(2,1)} %refs_1_.12) | copy-start | bytes 884740
  72.5 4.2 %collective-permute-start.19 = (bf16[128,1152]{1,0:T(8,128)(2,1)S(1)}, bf16[128,1152]{1,0:T(8,128)(2,1)S(1)}, u32[]{:S(2)}, u32[]{:S(2)}) collective-permute-start(bf16[128,1152]{1,0:T(8,128)(2,1)S(1)} %get-tuple-element.39), channel_id=1, source_target_pairs={{0,32},{32,0},{1,33},{33,1},{2,34},{34,2},{3,35},{35,3},{4,36},{36... | collective-permute-start | bytes 884744 | tf_op jit(solution)/shard_map/ppermute | solution.py:50

commit v17 on v16

--- a/solution.py
+++ b/solution.py
@@ -177,12 +177,12 @@
 
     image_there = other_core(picture_vectors_raw)
     text_there = other_core(caption_vectors_raw)
-    image, text = local(
-        lambda _, refs: [unit_rows(ref[...])[0] for ref in refs],
-        [shard] * 2,
-        [],
-        [picture_vectors_raw, caption_vectors_raw],
-    )
+    def own_shards(_, refs):
+        units = unit_rows(refs[0][...])[0]
+        return [units[:rows], units[rows:]]
+
+    both = jnp.concatenate([picture_vectors_raw, caption_vectors_raw], 0)
+    image, text = local(own_shards, [shard] * 2, [], [both])
 
     def own_units(scalars, refs):
         first = scalars[0][0] > 0

time: 78.7 us -> 78.1 us (level)
  local copies, waits for them, and re-layouts: 1.93 us -> 0.01 us
  other arithmetic: 0 us -> 1.1 us
    unnamed x8 -> x4, local copies, waits for them, and re-layouts: 1.93 us -> 0.01 us
    concatenate x0 -> x1, other arithmetic: none -> 1.1 us  [on_device(): both = jnp.concatenate([picture_vectors_raw, caption_vectors_raw], 0)]
  transfers between devices with their start and end apart: 21 -> 21, of which waited for: 10 -> 11; matrix products, arithmetic and copies ran while one was open for 0% -> 1% of each run, Pallas kernels for 29% -> 29%
where the time goes in v17:
time: 78.1 us; the launch traced here: 78 us
  starting transfers between devices  33.2 us (43%)
  Pallas kernels  26.5 us (34%)
  waiting for transfers between devices  14.3 us (18%)
  between operations  2.94 us (4%)
  other arithmetic  1.1 us (1%)
    ppermute x15, starting transfers between devices, sent(): return lax.ppermute(value, FINE_AXES, pairs)  25.6 us
    pallas_call x8, Pallas kernels, sums_of(): pl.pallas_call(functools.partial(sums_kernel, plan, len(inputs), len(afte...  23.4 us
    ppermute x15, waiting for transfers between devices, sent(): return lax.ppermute(value, FINE_AXES, pairs)  13.4 us
    ppermute x6, starting transfers between devices, other_core(): return lax.ppermute(value, 'core', [(0, 1), (1, 0)])  7.6 us
    pallas_call x1, Pallas kernels, on_device(): pl.pallas_call(finish_kernel, out_shape=[jax.ShapeDtypeStruct(*shard_full...  1.58 us
  transfers between devices with their start and end apart: 21, of which 11 were waited for; matrix products, arithmetic and copies ran while one was open for 1% of the time, Pallas kernels for 29%

profile of v17, /device:TPU:1, one launch (start us, length us, event | category | flops | bytes accessed | tf_op | source)
XLA Modules:
  0.0 78.0 jit_solution(10532723390711420183)
XLA Ops:
  0.6 1.5 %collective-permute-start = (bf16[128,1152]{1,0:T(8,128)(2,1)}, bf16[128,1152]{1,0:T(8,128)(2,1)S(1)}, u32[]{:S(2)}, u32[]{:S(2)}) collective-permute-start(bf16[128,1152]{1,0:T(8,128)(2,1)} %refs_0_.10), channel_id=1, source_target_pairs={{0,32},{32,0},{1,33},{33,1},{2,34},{34,2},{3,35},{35,3},{4,36},{36... | collective-permute-start | bytes 884744 | tf_op jit(solution)/shard_map/ppermute | solution.py:50
  2.2 1.1 %pad_maximum_fusion.refs_0_ = bf16[256,1152]{1,0:T(8,128)(2,1)S(1)} fusion(bf16[128,1152]{1,0:T(8,128)(2,1)} %refs_1_.10, bf16[128,1152]{1,0:T(8,128)(2,1)} %refs_0_.10), kind=kLoop, calls=%fused_computation | loop fusion | flops 1179648 | bytes 1179648 | tf_op jit(solution)/shard_map/concatenate | solution.py:184
  3.3 0.2 shard_map.68
  3.5 0.4 collective-permute-done.1.refs_2_
  4.0 0.4 shard_map.69
  4.3 2.6 %collective-permute-start.2 = (bf16[256,1152]{1,0:T(8,128)(2,1)S(1)}, bf16[256,1152]{1,0:T(8,128)(2,1)S(1)}, u32[]{:S(2)}, u32[]{:S(2)}) collective-permute-start(bf16[256,1152]{1,0:T(8,128)(2,1)S(1)} %get-tuple-element.23.refs_2_), channel_id=1, source_target_pairs={{0,8},{32,56},{2,10},{34,58},{4,12},{36,60},{6,14},{38,62},{64,72}... | collective-permute-start | bytes 1769480 | tf_op jit(solution)/shard_map/ppermute | solution.py:46
  7.0 2.7 %collective-permute-start.4 = (bf16[256,1152]{1,0:T(8,128)(2,1)S(1)}, bf16[256,1152]{1,0:T(8,128)(2,1)S(1)}, u32[]{:S(2)}, u32[]{:S(2)}) collective-permute-start(bf16[256,1152]{1,0:T(8,128)(2,1)S(1)} %get-tuple-element.23.refs_2_), channel_id=1, source_target_pairs={{0,64},{32,97},{2,66},{34,99},{4,68},{36,101},{6,70},{38,103},{64,... | collective-permute-start | bytes 1769480 | tf_op jit(solution)/shard_map/ppermute | solution.py:46
  9.7 1.6 %collective-permute-start.5 = (bf16[256,1152]{1,0:T(8,128)(2,1)S(1)}, bf16[256,1152]{1,0:T(8,128)(2,1)S(1)}, u32[]{:S(2)}, u32[]{:S(2)}) collective-permute-start(bf16[256,1152]{1,0:T(8,128)(2,1)S(1)} %get-tuple-element.23.refs_2_), channel_id=1, source_target_pairs={{0,6},{32,34},{2,4},{34,32},{4,2},{36,38},{6,0},{38,36},{64,70},{9... | collective-permute-start | bytes 1769480 | tf_op jit(solution)/shard_map/ppermute | solution.py:46
  12.7 2.0 %collective-permute-done.2.refs_2_.refs_5_ = bf16[256,1152]{1,0:T(8,128)(2,1)S(1)} collective-permute-done((bf16[256,1152]{1,0:T(8,128)(2,1)S(1)}, bf16[256,1152]{1,0:T(8,128)(2,1)S(1)}, u32[]{:S(2)}, u32[]{:S(2)}) %collective-permute-start.2) | collective-permute-done | bytes 589856 | tf_op jit(solution)/shard_map/ppermute | solution.py:46
  14.7 2.6 %collective-permute-done.4.refs_3_.refs_6_ = bf16[256,1152]{1,0:T(8,128)(2,1)S(1)} collective-permute-done((bf16[256,1152]{1,0:T(8,128)(2,1)S(1)}, bf16[256,1152]{1,0:T(8,128)(2,1)S(1)}, u32[]{:S(2)}, u32[]{:S(2)}) %collective-permute-start.4) | collective-permute-done | bytes 589856 | tf_op jit(solution)/shard_map/ppermute | solution.py:46
  17.3 1.6 %collective-permute-done.5.refs_4_.refs_7_.refs_8_ = bf16[256,1152]{1,0:T(8,128)(2,1)S(1)} collective-permute-done((bf16[256,1152]{1,0:T(8,128)(2,1)S(1)}, bf16[256,1152]{1,0:T(8,128)(2,1)S(1)}, u32[]{:S(2)}, u32[]{:S(2)}) %collective-permute-start.5) | collective-permute-done | bytes 589856 | tf_op jit(solution)/shard_map/ppermute | solution.py:46
  18.9 0.1 shard_map.70
  19.1 1.0 %collective-permute-start.6 = (bf16[768,1152]{1,0:T(8,128)(2,1)S(1)}, bf16[768,1152]{1,0:T(8,128)(2,1)S(1)}, u32[]{:S(2)}, u32[]{:S(2)}) collective-permute-start(bf16[768,1152]{1,0:T(8,128)(2,1)S(1)} %shard_map.70), channel_id=1, source_target_pairs={{0,32},{32,0},{1,33},{33,1},{2,34},{34,2},{3,35},{35,3},{4,36},{36... | collective-permute-start | bytes 5308424 | tf_op jit(solution)/shard_map/ppermute | solution.py:50
  20.1 1.3 %collective-permute-start.3 = (bf16[256,1152]{1,0:T(8,128)(2,1)S(1)}, bf16[256,1152]{1,0:T(8,128)(2,1)S(1)}, u32[]{:S(2)}, u32[]{:S(2)}) collective-permute-start(bf16[256,1152]{1,0:T(8,128)(2,1)S(1)} %collective-permute-done.2.refs_2_.refs_5_), channel_id=1, source_target_pairs={{0,70},{32,99},{2,68},{34,97},{4,66},{36,103},{6,64},{38,101},{64,... | collective-permute-start | bytes 1769480 | tf_op jit(solution)/shard_map/ppermute | solution.py:46
  21.3 1.5 %collective-permute-start.8 = (bf16[256,1152]{1,0:T(8,128)(2,1)S(1)}, bf16[256,1152]{1,0:T(8,128)(2,1)S(1)}, u32[]{:S(2)}, u32[]{:S(2)}) collective-permute-start(bf16[256,1152]{1,0:T(8,128)(2,1)S(1)} %collective-permute-done.2.refs_2_.refs_5_), channel_id=1, source_target_pairs={{0,64},{32,97},{2,66},{34,99},{4,68},{36,101},{6,70},{38,103},{64,... | collective-permute-start | bytes 1769480 | tf_op jit(solution)/shard_map/ppermute | solution.py:46
  22.8 1.1 %collective-permute-start.9 = (bf16[256,1152]{1,0:T(8,128)(2,1)S(1)}, bf16[256,1152]{1,0:T(8,128)(2,1)S(1)}, u32[]{:S(2)}, u32[]{:S(2)}) collective-permute-start(bf16[256,1152]{1,0:T(8,128)(2,1)S(1)} %collective-permute-done.4.refs_3_.refs_6_), channel_id=1, source_target_pairs={{0,6},{32,34},{2,4},{34,32},{4,2},{36,38},{6,0},{38,36},{64,70},{9... | collective-permute-start | bytes 1769480 | tf_op jit(solution)/shard_map/ppermute | solution.py:46
  23.9 1.8 %collective-permute-start.10 = (bf16[256,1152]{1,0:T(8,128)(2,1)S(1)}, bf16[256,1152]{1,0:T(8,128)(2,1)S(1)}, u32[]{:S(2)}, u32[]{:S(2)}) collective-permute-start(bf16[256,1152]{1,0:T(8,128)(2,1)S(1)} %collective-permute-done.5.refs_4_.refs_7_.refs_8_), channel_id=1, source_target_pairs={{0,8},{32,56},{2,10},{34,58},{4,12},{36,60},{6,14},{38,62},{64,72}... | collective-permute-start | bytes 1769480 | tf_op jit(solution)/shard_map/ppermute | solution.py:46
  25.7 5.7 %shard_map.71 = (f32[256,1152]{1,0:T(8,128)S(1)}, f32[256,1152]{1,0:T(8,128)S(1)}, f32[256,1152]{1,0:T(8,128)S(1)}, f32[256,1152]{1,0:T(8,128)S(1)}) custom-call(f32[1]{0:T(128)S(6)} %copy.7.refs_0_, f32[1]{0:T(128)S(6)} %copy.8.refs_1_, bf16[256,1152]{1,0:T(8,128)(2,1)S(1)} %get-tuple-element.23.refs_2_, bf16[256,1152]{1,0:T(8,128)(2,1)S(1)} %get-tuple-element.24.refs_3_, ...), custom_call_target="tpu_custom_call" | custom-call | tf_op jit(solution)/shard_map/pallas_call | solution.py:132
  31.5 0.9 %collective-permute-start.7 = (bf16[256,1152]{1,0:T(8,128)(2,1)S(1)}, bf16[256,1152]{1,0:T(8,128)(2,1)S(1)}, u32[]{:S(2)}, u32[]{:S(2)}) collective-permute-start(bf16[256,1152]{1,0:T(8,128)(2,1)S(1)} %shard_map.72), channel_id=1, source_target_pairs={{0,32},{32,0},{1,33},{33,1},{2,34},{34,2},{3,35},{35,3},{4,36},{36... | collective-permute-start | bytes 1769480 | tf_op jit(solution)/shard_map/ppermute | solution.py:50
  32.4 1.6 %shard_map.73.refs_3_.refs_6_.refs_5_ = f32[256,1152]{1,0:T(8,128)S(1)} custom-call(f32[1]{0:T(128)S(6)} %copy.7.refs_0_, f32[1]{0:T(128)S(6)} %copy.8.refs_1_, bf16[256,1152]{1,0:T(8,128)(2,1)S(1)} %collective-permute-done.3.refs_0_.refs_2_, bf16[256,1152]{1,0:T(8,128)(2,1)S(1)} %get-tuple-element.24.refs_3_, ...), custom_call_target="tpu_custom_call" | custom-call | flops 1207959552 | bytes 2359296 | tf_op jit(solution)/shard_map/pallas_call | solution.py:132
  33.9 2.8 %collective-permute-done.8.refs_0_.refs_2_ = bf16[256,1152]{1,0:T(8,128)(2,1)S(1)} collective-permute-done((bf16[256,1152]{1,0:T(8,128)(2,1)S(1)}, bf16[256,1152]{1,0:T(8,128)(2,1)S(1)}, u32[]{:S(2)}, u32[]{:S(2)}) %collective-permute-start.8) | collective-permute-done | bytes 589856 | tf_op jit(solution)/shard_map/ppermute | solution.py:46
  36.7 0.8 %collective-permute-done.9.refs_1_.refs_2_ = bf16[256,1152]{1,0:T(8,128)(2,1)S(1)} collective-permute-done((bf16[256,1152]{1,0:T(8,128)(2,1)S(1)}, bf16[256,1152]{1,0:T(8,128)(2,1)S(1)}, u32[]{:S(2)}, u32[]{:S(2)}) %collective-permute-start.9) | collective-permute-done | bytes 589856 | tf_op jit(solution)/shard_map/ppermute | solution.py:46
  37.5 0.1 shard_map.74
  37.7 1.8 %collective-permute-start.11 = (bf16[768,1152]{1,0:T(8,128)(2,1)S(1)}, bf16[768,1152]{1,0:T(8,128)(2,1)S(1)}, u32[]{:S(2)}, u32[]{:S(2)}) collective-permute-start(bf16[768,1152]{1,0:T(8,128)(2,1)S(1)} %shard_map.74), channel_id=1, source_target_pairs={{0,32},{32,0},{1,33},{33,1},{2,34},{34,2},{3,35},{35,3},{4,36},{36... | collective-permute-start | bytes 5308424 | tf_op jit(solution)/shard_map/ppermute | solution.py:50
  39.5 2.9 %shard_map.75 = (f32[256,1152]{1,0:T(8,128)S(1)}, f32[256,1152]{1,0:T(8,128)S(1)}) custom-call(f32[1]{0:T(128)S(6)} %copy.7.refs_0_, f32[1]{0:T(128)S(6)} %copy.8.refs_1_, bf16[256,1152]{1,0:T(8,128)(2,1)S(1)} %collective-permute-done.8.refs_0_.refs_2_, bf16[256,1152]{1,0:T(8,128)(2,1)S(1)} %get-tuple-element.24.refs_3_, ...), custom_call_target="tpu_custom_call" | custom-call | flops 2415919104 | bytes 4718592 | tf_op jit(solution)/shard_map/pallas_call | solution.py:132
  42.4 0.4 collective-permute-done.11.refs_4_.refs_6_
  42.8 1.6 %shard_map.76.refs_8_ = bf16[256,1152]{1,0:T(8,128)(2,1)S(1)} custom-call(f32[1]{0:T(128)S(6)} %copy.7.refs_0_, f32[1]{0:T(128)S(6)} %copy.8.refs_1_, bf16[256,1152]{1,0:T(8,128)(2,1)S(1)} %collective-permute-done.3.refs_0_.refs_2_, bf16[256,1152]{1,0:T(8,128)(2,1)S(1)} %collective-permute-done.7.refs_4_.refs_3_.refs_5_, ...), custom_call_target="tpu_custom_call" | custom-call | flops 1207959552 | bytes 2359296 | tf_op jit(solution)/shard_map/pallas_call | solution.py:132
  44.4 1.9 %collective-permute-start.12 = (bf16[256,1152]{1,0:T(8,128)(2,1)S(1)}, bf16[256,1152]{1,0:T(8,128)(2,1)S(1)}, u32[]{:S(2)}, u32[]{:S(2)}) collective-permute-start(bf16[256,1152]{1,0:T(8,128)(2,1)S(1)} %shard_map.76.refs_8_), channel_id=1, source_target_pairs={{0,8},{32,56},{2,10},{34,58},{4,12},{36,60},{6,14},{38,62},{64,72}... | collective-permute-start | bytes 1769480 | tf_op jit(solution)/shard_map/ppermute | solution.py:46
  46.2 2.9 %shard_map.77 = (bf16[256,1152]{1,0:T(8,128)(2,1)S(1)}, bf16[256,1152]{1,0:T(8,128)(2,1)S(1)}) custom-call(f32[1]{0:T(128)S(6)} %copy.7.refs_0_, f32[1]{0:T(128)S(6)} %copy.8.refs_1_, bf16[256,1152]{1,0:T(8,128)(2,1)S(1)} %collective-permute-done.8.refs_0_.refs_2_, bf16[256,1152]{1,0:T(8,128)(2,1)S(1)} %collective-permute-done.7.refs_4_.refs_3_.refs_5_, ...), custom_call_target="tpu_custom_call" | custom-call | flops 2415919104 | bytes 4718592 | tf_op jit(solution)/shard_map/pallas_call | solution.py:132
  49.2 2.0 %collective-permute-start.14 = (bf16[256,1152]{1,0:T(8,128)(2,1)S(1)}, bf16[256,1152]{1,0:T(8,128)(2,1)S(1)}, u32[]{:S(2)}, u32[]{:S(2)}) collective-permute-start(bf16[256,1152]{1,0:T(8,128)(2,1)S(1)} %get-tuple-element.31.refs_7_), channel_id=1, source_target_pairs={{0,64},{32,97},{2,66},{34,99},{4,68},{36,101},{6,70},{38,103},{64,... | collective-permute-start | bytes 1769480 | tf_op jit(solution)/shard_map/ppermute | solution.py:46
  51.2 0.9 %collective-permute-start.15 = (bf16[256,1152]{1,0:T(8,128)(2,1)S(1)}, bf16[256,1152]{1,0:T(8,128)(2,1)S(1)}, u32[]{:S(2)}, u32[]{:S(2)}) collective-permute-start(bf16[256,1152]{1,0:T(8,128)(2,1)S(1)} %get-tuple-element.35), channel_id=1, source_target_pairs={{0,8},{32,56},{2,10},{34,58},{4,12},{36,60},{6,14},{38,62},{64,72}... | collective-permute-start | bytes 1769480 | tf_op jit(solution)/shard_map/ppermute | solution.py:46
  52.0 2.9 %shard_map.78.refs_0_ = f32[256,1152]{1,0:T(8,128)S(1)} custom-call(f32[1]{0:T(128)S(6)} %copy.7.refs_0_, f32[1]{0:T(128)S(6)} %copy.8.refs_1_, bf16[256,1152]{1,0:T(8,128)(2,1)S(1)} %collective-permute-done.9.refs_1_.refs_2_, bf16[256,1152]{1,0:T(8,128)(2,1)S(1)} %get-tuple-element.24.refs_3_, bf16[768,1152]{1,0:T(8,128)(2,1)S(1)} %collective-permute-done.6.refs_4_, ...), custom_call_target="tpu_custom_call" | custom-call | flops 2415919104 | bytes 2359296 | tf_op jit(solution)/shard_map/pallas_call | solution.py:132
  55.0 0.1 shard_map.79.refs_10_
  55.1 0.3 collective-permute-start.13
  55.4 4.3 %shard_map.80 = (f32[256,1152]{1,0:T(8,128)S(1)}, f32[256,1152]{1,0:T(8,128)S(1)}, f32[256,1152]{1,0:T(8,128)S(1)}) custom-call(f32[1]{0:T(128)S(6)} %copy.7.refs_0_, f32[1]{0:T(128)S(6)} %copy.8.refs_1_, bf16[256,1152]{1,0:T(8,128)(2,1)S(1)} %collective-permute-done.2.refs_2_.refs_5_, bf16[256,1152]{1,0:T(8,128)(2,1)S(1)} %collective-permute-done.7.refs_4_.refs_3_.refs_5_, ...), custom_call_target="tpu_custom_call" | custom-call | flops 3623878656 | bytes 7077888 | tf_op jit(solution)/shard_map/pallas_call | solution.py:132
  59.7 0.1 shard_map.81.refs_3_
  59.8 1.9 %collective-permute-start.16 = (bf16[256,1152]{1,0:T(8,128)(2,1)S(1)}, bf16[256,1152]{1,0:T(8,128)(2,1)S(1)}, u32[]{:S(2)}, u32[]{:S(2)}) collective-permute-start(bf16[256,1152]{1,0:T(8,128)(2,1)S(1)} %shard_map.81.refs_3_), channel_id=1, source_target_pairs={{0,8},{32,56},{2,10},{34,58},{4,12},{36,60},{6,14},{38,62},{64,72}... | collective-permute-start | bytes 1769480 | tf_op jit(solution)/shard_map/ppermute | solution.py:46
  61.8 1.5 %collective-permute-start.17 = (bf16[256,1152]{1,0:T(8,128)(2,1)S(1)}, bf16[256,1152]{1,0:T(8,128)(2,1)S(1)}, u32[]{:S(2)}, u32[]{:S(2)}) collective-permute-start(bf16[256,1152]{1,0:T(8,128)(2,1)S(1)} %shard_map.82.refs_4_), channel_id=1, source_target_pairs={{0,6},{32,34},{2,4},{34,32},{4,2},{36,38},{6,0},{38,36},{64,70},{9... | collective-permute-start | bytes 1769480 | tf_op jit(solution)/shard_map/ppermute | solution.py:46
  63.3 1.1 %collective-permute-done.13.refs_2_ = bf16[256,1152]{1,0:T(8,128)(2,1)S(1)} collective-permute-done((bf16[256,1152]{1,0:T(8,128)(2,1)S(1)}, bf16[256,1152]{1,0:T(8,128)(2,1)S(1)}, u32[]{:S(2)}, u32[]{:S(2)}) %collective-permute-start.13) | collective-permute-done | bytes 589856 | tf_op jit(solution)/shard_map/ppermute | solution.py:46
  64.5 3.7 %collective-permute-start.18 = (bf16[128,1152]{1,0:T(8,128)(2,1)S(1)}, bf16[128,1152]{1,0:T(8,128)(2,1)S(1)}, u32[]{:S(2)}, u32[]{:S(2)}) collective-permute-start(bf16[128,1152]{1,0:T(8,128)(2,1)S(1)} %get-tuple-element.37), channel_id=1, source_target_pairs={{0,96},{32,65},{2,98},{34,67},{4,100},{36,69},{6,102},{38,71},{64,... | collective-permute-start | bytes 884744 | tf_op jit(solution)/shard_map/ppermute | solution.py:46
  68.1 0.8 %collective-permute-start.20 = (bf16[128,1152]{1,0:T(8,128)(2,1)S(1)}, bf16[128,1152]{1,0:T(8,128)(2,1)S(1)}, u32[]{:S(2)}, u32[]{:S(2)}) collective-permute-start(bf16[128,1152]{1,0:T(8,128)(2,1)S(1)} %get-tuple-element.36.refs_6_), channel_id=1, source_target_pairs={{0,64},{32,97},{2,66},{34,99},{4,68},{36,101},{6,70},{38,103},{64,... | collective-permute-start | bytes 884744 | tf_op jit(solution)/shard_map/ppermute | solution.py:46
  68.9 1.6 %shard_map.84.refs_1_ = f32[256,1152]{1,0:T(8,128)S(1)} custom-call(f32[1]{0:T(128)S(6)} %copy.7.refs_0_, f32[1]{0:T(128)S(6)} %copy.8.refs_1_, bf16[256,1152]{1,0:T(8,128)(2,1)S(1)} %get-tuple-element.23.refs_2_, bf16[256,1152]{1,0:T(8,128)(2,1)S(1)} %collective-permute-done.7.refs_4_.refs_3_.refs_5_, ...), custom_call_target="tpu_custom_call" | custom-call | flops 1207959552 | bytes 2359296 | tf_op jit(solution)/shard_map/pallas_call | solution.py:132
  70.5 0.4 collective-permute-done.17.refs_3_
  70.9 0.9 %collective-permute-done.18.refs_4_.refs_5_ = bf16[128,1152]{1,0:T(8,128)(2,1)S(1)} collective-permute-done((bf16[128,1152]{1,0:T(8,128)(2,1)S(1)}, bf16[128,1152]{1,0:T(8,128)(2,1)S(1)}, u32[]{:S(2)}, u32[]{:S(2)}) %collective-permute-start.18) | collective-permute-done | bytes 294944 | tf_op jit(solution)/shard_map/ppermute | solution.py:46
  71.8 0.2 shard_map.85
  72.0 2.3 %collective-permute-start.19 = (bf16[128,1152]{1,0:T(8,128)(2,1)S(1)}, bf16[128,1152]{1,0:T(8,128)(2,1)S(1)}, u32[]{:S(2)}, u32[]{:S(2)}) collective-permute-start(bf16[128,1152]{1,0:T(8,128)(2,1)S(1)} %get-tuple-element.39), channel_id=1, source_target_pairs={{0,32},{32,0},{1,33},{33,1},{2,34},{34,2},{3,35},{35,3},{4,36},{36... | collective-permute-start | bytes 884744 | tf_op jit(solution)/shard_map/ppermute | solution.py:50
  75.0 1.3 %collective-permute-done.20.refs_4_ = bf16[128,1152]{1,0:T(8,128)(2,1)S(1)} collective-permute-done((bf16[128,1152]{1,0:T(8,128)(2,1)S(1)}, bf16[128,1152]{1,0:T(8,128)(2,1)S(1)}, u32[]{:S(2)}, u32[]{:S(2)}) %collective-permute-start.20) | collective-permute-done | bytes 294944 | tf_op jit(solution)/shard_map/ppermute | solution.py:46
  76.2 1.6 %shard_map.86 = (f32[128,1152]{1,0:T(8,128)}, f32[128,1152]{1,0:T(8,128)}) custom-call(f32[1]{0:T(128)} %bitcast.refs_0_.is_first, f32[1]{0:T(128)S(6)} %div.3.multiplier, bf16[128,1152]{1,0:T(8,128)(2,1)S(1)} %copy-done, bf16[128,1152]{1,0:T(8,128)(2,1)S(1)} %copy-done.1, f32[128,1152]{1,0:T(8,128)S(1)} %get-tuple-element.38.refs_2_, ...), custom_call_target="tpu_custom_call" | custom-call | tf_op jit(solution)/shard_map/pallas_call | solution.py:271
  (18 shorter events, 0.4 us)
Async XLA Ops:
  0.6 2.9 %collective-permute-start = (bf16[128,1152]{1,0:T(8,128)(2,1)}, bf16[128,1152]{1,0:T(8,128)(2,1)S(1)}, u32[]{:S(2)}, u32[]{:S(2)}) collective-permute-start(bf16[128,1152]{1,0:T(8,128)(2,1)} %refs_0_.10), channel_id=1, source_target_pairs={{0,32},{32,0},{1,33},{33,1},{2,34},{34,2},{3,35},{35,3},{4,36},{36... | collective-permute-start | bytes 884744 | tf_op jit(solution)/shard_map/ppermute | solution.py:50
  2.1 1.8 %collective-permute-start.1 = (bf16[128,1152]{1,0:T(8,128)(2,1)}, bf16[128,1152]{1,0:T(8,128)(2,1)S(1)}, u32[]{:S(2)}, u32[]{:S(2)}) collective-permute-start(bf16[128,1152]{1,0:T(8,128)(2,1)} %refs_1_.10), channel_id=1, source_target_pairs={{0,32},{32,0},{1,33},{33,1},{2,34},{34,2},{3,35},{35,3},{4,36},{36... | collective-permute-start | bytes 884744 | tf_op jit(solution)/shard_map/ppermute | solution.py:50
  4.3 10.3 %collective-permute-start.2 = (bf16[256,1152]{1,0:T(8,128)(2,1)S(1)}, bf16[256,1152]{1,0:T(8,128)(2,1)S(1)}, u32[]{:S(2)}, u32[]{:S(2)}) collective-permute-start(bf16[256,1152]{1,0:T(8,128)(2,1)S(1)} %get-tuple-element.23.refs_2_), channel_id=1, source_target_pairs={{0,8},{32,56},{2,10},{34,58},{4,12},{36,60},{6,14},{38,62},{64,72}... | collective-permute-start | bytes 1769480 | tf_op jit(solution)/shard_map/ppermute | solution.py:46
  7.0 10.3 %collective-permute-start.4 = (bf16[256,1152]{1,0:T(8,128)(2,1)S(1)}, bf16[256,1152]{1,0:T(8,128)(2,1)S(1)}, u32[]{:S(2)}, u32[]{:S(2)}) collective-permute-start(bf16[256,1152]{1,0:T(8,128)(2,1)S(1)} %get-tuple-element.23.refs_2_), channel_id=1, source_target_pairs={{0,64},{32,97},{2,66},{34,99},{4,68},{36,101},{6,70},{38,103},{64,... | collective-permute-start | bytes 1769480 | tf_op jit(solution)/shard_map/ppermute | solution.py:46
  9.7 9.2 %collective-permute-start.5 = (bf16[256,1152]{1,0:T(8,128)(2,1)S(1)}, bf16[256,1152]{1,0:T(8,128)(2,1)S(1)}, u32[]{:S(2)}, u32[]{:S(2)}) collective-permute-start(bf16[256,1152]{1,0:T(8,128)(2,1)S(1)} %get-tuple-element.23.refs_2_), channel_id=1, source_target_pairs={{0,6},{32,34},{2,4},{34,32},{4,2},{36,38},{6,0},{38,36},{64,70},{9... | collective-permute-start | bytes 1769480 | tf_op jit(solution)/shard_map/ppermute | solution.py:46
  19.1 6.7 %collective-permute-start.6 = (bf16[768,1152]{1,0:T(8,128)(2,1)S(1)}, bf16[768,1152]{1,0:T(8,128)(2,1)S(1)}, u32[]{:S(2)}, u32[]{:S(2)}) collective-permute-start(bf16[768,1152]{1,0:T(8,128)(2,1)S(1)} %shard_map.70), channel_id=1, source_target_pairs={{0,32},{32,0},{1,33},{33,1},{2,34},{34,2},{3,35},{35,3},{4,36},{36... | collective-permute-start | bytes 5308424 | tf_op jit(solution)/shard_map/ppermute | solution.py:50
  20.1 11.4 %collective-permute-start.3 = (bf16[256,1152]{1,0:T(8,128)(2,1)S(1)}, bf16[256,1152]{1,0:T(8,128)(2,1)S(1)}, u32[]{:S(2)}, u32[]{:S(2)}) collective-permute-start(bf16[256,1152]{1,0:T(8,128)(2,1)S(1)} %collective-permute-done.2.refs_2_.refs_5_), channel_id=1, source_target_pairs={{0,70},{32,99},{2,68},{34,97},{4,66},{36,103},{6,64},{38,101},{64,... | collective-permute-start | bytes 1769480 | tf_op jit(solution)/shard_map/ppermute | solution.py:46
  21.3 15.4 %collective-permute-start.8 = (bf16[256,1152]{1,0:T(8,128)(2,1)S(1)}, bf16[256,1152]{1,0:T(8,128)(2,1)S(1)}, u32[]{:S(2)}, u32[]{:S(2)}) collective-permute-start(bf16[256,1152]{1,0:T(8,128)(2,1)S(1)} %collective-permute-done.2.refs_2_.refs_5_), channel_id=1, source_target_pairs={{0,64},{32,97},{2,66},{34,99},{4,68},{36,101},{6,70},{38,103},{64,... | collective-permute-start | bytes 1769480 | tf_op jit(solution)/shard_map/ppermute | solution.py:46
  22.8 14.7 %collective-permute-start.9 = (bf16[256,1152]{1,0:T(8,128)(2,1)S(1)}, bf16[256,1152]{1,0:T(8,128)(2,1)S(1)}, u32[]{:S(2)}, u32[]{:S(2)}) collective-permute-start(bf16[256,1152]{1,0:T(8,128)(2,1)S(1)} %collective-permute-done.4.refs_3_.refs_6_), channel_id=1, source_target_pairs={{0,6},{32,34},{2,4},{34,32},{4,2},{36,38},{6,0},{38,36},{64,70},{9... | collective-permute-start | bytes 1769480 | tf_op jit(solution)/shard_map/ppermute | solution.py:46
  23.9 13.6 %collective-permute-start.10 = (bf16[256,1152]{1,0:T(8,128)(2,1)S(1)}, bf16[256,1152]{1,0:T(8,128)(2,1)S(1)}, u32[]{:S(2)}, u32[]{:S(2)}) collective-permute-start(bf16[256,1152]{1,0:T(8,128)(2,1)S(1)} %collective-permute-done.5.refs_4_.refs_7_.refs_8_), channel_id=1, source_target_pairs={{0,8},{32,56},{2,10},{34,58},{4,12},{36,60},{6,14},{38,62},{64,72}... | collective-permute-start | bytes 1769480 | tf_op jit(solution)/shard_map/ppermute | solution.py:46
  31.5 6.0 %collective-permute-start.7 = (bf16[256,1152]{1,0:T(8,128)(2,1)S(1)}, bf16[256,1152]{1,0:T(8,128)(2,1)S(1)}, u32[]{:S(2)}, u32[]{:S(2)}) collective-permute-start(bf16[256,1152]{1,0:T(8,128)(2,1)S(1)} %shard_map.72), channel_id=1, source_target_pairs={{0,32},{32,0},{1,33},{33,1},{2,34},{34,2},{3,35},{35,3},{4,36},{36... | collective-permute-start | bytes 1769480 | tf_op jit(solution)/shard_map/ppermute | solution.py:50
  37.7 5.2 %collective-permute-start.11 = (bf16[768,1152]{1,0:T(8,128)(2,1)S(1)}, bf16[768,1152]{1,0:T(8,128)(2,1)S(1)}, u32[]{:S(2)}, u32[]{:S(2)}) collective-permute-start(bf16[768,1152]{1,0:T(8,128)(2,1)S(1)} %shard_map.74), channel_id=1, source_target_pairs={{0,32},{32,0},{1,33},{33,1},{2,34},{34,2},{3,35},{35,3},{4,36},{36... | collective-permute-start | bytes 5308424 | tf_op jit(solution)/shard_map/ppermute | solution.py:50
  44.4 10.6 %collective-permute-start.12 = (bf16[256,1152]{1,0:T(8,128)(2,1)S(1)}, bf16[256,1152]{1,0:T(8,128)(2,1)S(1)}, u32[]{:S(2)}, u32[]{:S(2)}) collective-permute-start(bf16[256,1152]{1,0:T(8,128)(2,1)S(1)} %shard_map.76.refs_8_), channel_id=1, source_target_pairs={{0,8},{32,56},{2,10},{34,58},{4,12},{36,60},{6,14},{38,62},{64,72}... | collective-permute-start | bytes 1769480 | tf_op jit(solution)/shard_map/ppermute | solution.py:46
  49.2 10.5 %collective-permute-start.14 = (bf16[256,1152]{1,0:T(8,128)(2,1)S(1)}, bf16[256,1152]{1,0:T(8,128)(2,1)S(1)}, u32[]{:S(2)}, u32[]{:S(2)}) collective-permute-start(bf16[256,1152]{1,0:T(8,128)(2,1)S(1)} %get-tuple-element.31.refs_7_), channel_id=1, source_target_pairs={{0,64},{32,97},{2,66},{34,99},{4,68},{36,101},{6,70},{38,103},{64,... | collective-permute-start | bytes 1769480 | tf_op jit(solution)/shard_map/ppermute | solution.py:46
  51.2 10.5 %collective-permute-start.15 = (bf16[256,1152]{1,0:T(8,128)(2,1)S(1)}, bf16[256,1152]{1,0:T(8,128)(2,1)S(1)}, u32[]{:S(2)}, u32[]{:S(2)}) collective-permute-start(bf16[256,1152]{1,0:T(8,128)(2,1)S(1)} %get-tuple-element.35), channel_id=1, source_target_pairs={{0,8},{32,56},{2,10},{34,58},{4,12},{36,60},{6,14},{38,62},{64,72}... | collective-permute-start | bytes 1769480 | tf_op jit(solution)/shard_map/ppermute | solution.py:46
  55.1 9.3 %collective-permute-start.13 = (bf16[256,1152]{1,0:T(8,128)(2,1)S(1)}, bf16[256,1152]{1,0:T(8,128)(2,1)S(1)}, u32[]{:S(2)}, u32[]{:S(2)}) collective-permute-start(bf16[256,1152]{1,0:T(8,128)(2,1)S(1)} %shard_map.79.refs_10_), channel_id=1, source_target_pairs={{0,6},{32,34},{2,4},{34,32},{4,2},{36,38},{6,0},{38,36},{64,70},{9... | collective-permute-start | bytes 1769480 | tf_op jit(solution)/shard_map/ppermute | solution.py:46
  59.8 10.7 %collective-permute-start.16 = (bf16[256,1152]{1,0:T(8,128)(2,1)S(1)}, bf16[256,1152]{1,0:T(8,128)(2,1)S(1)}, u32[]{:S(2)}, u32[]{:S(2)}) collective-permute-start(bf16[256,1152]{1,0:T(8,128)(2,1)S(1)} %shard_map.81.refs_3_), channel_id=1, source_target_pairs={{0,8},{32,56},{2,10},{34,58},{4,12},{36,60},{6,14},{38,62},{64,72}... | collective-permute-start | bytes 1769480 | tf_op jit(solution)/shard_map/ppermute | solution.py:46
  61.8 9.1 %collective-permute-start.17 = (bf16[256,1152]{1,0:T(8,128)(2,1)S(1)}, bf16[256,1152]{1,0:T(8,128)(2,1)S(1)}, u32[]{:S(2)}, u32[]{:S(2)}) collective-permute-start(bf16[256,1152]{1,0:T(8,128)(2,1)S(1)} %shard_map.82.refs_4_), channel_id=1, source_target_pairs={{0,6},{32,34},{2,4},{34,32},{4,2},{36,38},{6,0},{38,36},{64,70},{9... | collective-permute-start | bytes 1769480 | tf_op jit(solution)/shard_map/ppermute | solution.py:46
  64.5 7.3 %collective-permute-start.18 = (bf16[128,1152]{1,0:T(8,128)(2,1)S(1)}, bf16[128,1152]{1,0:T(8,128)(2,1)S(1)}, u32[]{:S(2)}, u32[]{:S(2)}) collective-permute-start(bf16[128,1152]{1,0:T(8,128)(2,1)S(1)} %get-tuple-element.37), channel_id=1, source_target_pairs={{0,96},{32,65},{2,98},{34,67},{4,100},{36,69},{6,102},{38,71},{64,... | collective-permute-start | bytes 884744 | tf_op jit(solution)/shard_map/ppermute | solution.py:46
  68.1 8.1 %collective-permute-start.20 = (bf16[128,1152]{1,0:T(8,128)(2,1)S(1)}, bf16[128,1152]{1,0:T(8,128)(2,1)S(1)}, u32[]{:S(2)}, u32[]{:S(2)}) collective-permute-start(bf16[128,1152]{1,0:T(8,128)(2,1)S(1)} %get-tuple-element.36.refs_6_), channel_id=1, source_target_pairs={{0,64},{32,97},{2,66},{34,99},{4,68},{36,101},{6,70},{38,103},{64,... | collective-permute-start | bytes 884744 | tf_op jit(solution)/shard_map/ppermute | solution.py:46
  70.5 5.7 %copy-start = (bf16[128,1152]{1,0:T(8,128)(2,1)S(1)}, bf16[128,1152]{1,0:T(8,128)(2,1)}, u32[]{:S(2)}) copy-start(bf16[128,1152]{1,0:T(8,128)(2,1)} %refs_0_.10) | copy-start | bytes 884740
  70.5 5.7 %copy-start.1 = (bf16[128,1152]{1,0:T(8,128)(2,1)S(1)}, bf16[128,1152]{1,0:T(8,128)(2,1)}, u32[]{:S(2)}) copy-start(bf16[128,1152]{1,0:T(8,128)(2,1)} %refs_1_.10) | copy-start | bytes 884740
  72.0 4.2 %collective-permute-start.19 = (bf16[128,1152]{1,0:T(8,128)(2,1)S(1)}, bf16[128,1152]{1,0:T(8,128)(2,1)S(1)}, u32[]{:S(2)}, u32[]{:S(2)}) collective-permute-start(bf16[128,1152]{1,0:T(8,128)(2,1)S(1)} %get-tuple-element.39), channel_id=1, source_target_pairs={{0,32},{32,0},{1,33},{33,1},{2,34},{34,2},{3,35},{35,3},{4,36},{36... | collective-permute-start | bytes 884744 | tf_op jit(solution)/shard_map/ppermute | solution.py:50

commit v18 on v17

--- a/solution.py
+++ b/solution.py
@@ -213,7 +213,7 @@
     mine = {"": own}
     for way in ONE:
         mine[way] = sent(own, way)
-    mine["xyz"] = sent(mine["x"], "yz")
+    mine["xyz"] = sent(mine["z"], "xy")
     mine["xy"] = sent(mine["x"], "y")
     mine["yz"] = sent(mine["y"], "z")
     mine["zx"] = sent(mine["z"], "x")

time: 78.1 us -> 78.4 us (level)
  waiting for transfers between devices: 14.3 us -> 17.6 us
  starting transfers between devices: 33.2 us -> 30.1 us
    ppermute x15, waiting for transfers between devices: 13.4 us -> 16.5 us  [sent(): return lax.ppermute(value, FINE_AXES, pairs)]
    ppermute x6, starting transfers between devices: 7.6 us -> 5.78 us  [other_core(): return lax.ppermute(value, 'core', [(0, 1), (1, 0)])]
    ppermute x15, starting transfers between devices: 25.6 us -> 24.3 us  [sent(): return lax.ppermute(value, FINE_AXES, pairs)]
  transfers between devices with their start and end apart: 21 -> 21, of which waited for: 11 -> 12; matrix products, arithmetic and copies ran while one was open for 1% -> 1% of each run, Pallas kernels for 29% -> 29%
where the time goes in v18:
time: 78.4 us; the launch traced here: 78.3 us
  starting transfers between devices  30.1 us (38%)
  Pallas kernels  26.5 us (34%)
  waiting for transfers between devices  17.6 us (22%)
  between operations  2.94 us (4%)
  other arithmetic  1.1 us (1%)
    ppermute x15, starting transfers between devices, sent(): return lax.ppermute(value, FINE_AXES, pairs)  24.3 us
    pallas_call x8, Pallas kernels, sums_of(): pl.pallas_call(functools.partial(sums_kernel, plan, len(inputs), len(afte...  23.4 us
    ppermute x15, waiting for transfers between devices, sent(): return lax.ppermute(value, FINE_AXES, pairs)  16.5 us
    ppermute x6, starting transfers between devices, other_core(): return lax.ppermute(value, 'core', [(0, 1), (1, 0)])  5.78 us
    pallas_call x1, Pallas kernels, on_device(): pl.pallas_call(finish_kernel, out_shape=[jax.ShapeDtypeStruct(*shard_full...  1.58 us
  transfers between devices with their start and end apart: 21, of which 12 were waited for; matrix products, arithmetic and copies ran while one was open for 1% of the time, Pallas kernels for 29%

profile of v18, /device:TPU:1, one launch (start us, length us, event | category | flops | bytes accessed | tf_op | source)
XLA Modules:
  0.0 78.3 jit_solution(16023806737646133825)
XLA Ops:
  0.6 1.5 %collective-permute-start = (bf16[128,1152]{1,0:T(8,128)(2,1)}, bf16[128,1152]{1,0:T(8,128)(2,1)S(1)}, u32[]{:S(2)}, u32[]{:S(2)}) collective-permute-start(bf16[128,1152]{1,0:T(8,128)(2,1)} %refs_0_.10), channel_id=1, source_target_pairs={{0,32},{32,0},{1,33},{33,1},{2,34},{34,2},{3,35},{35,3},{4,36},{36... | collective-permute-start | bytes 884744 | tf_op jit(solution)/shard_map/ppermute | solution.py:50
  2.2 1.1 %pad_maximum_fusion.refs_0_ = bf16[256,1152]{1,0:T(8,128)(2,1)S(1)} fusion(bf16[128,1152]{1,0:T(8,128)(2,1)} %refs_1_.10, bf16[128,1152]{1,0:T(8,128)(2,1)} %refs_0_.10), kind=kLoop, calls=%fused_computation | loop fusion | flops 1179648 | bytes 1179648 | tf_op jit(solution)/shard_map/concatenate | solution.py:184
  3.3 0.2 shard_map.68
  3.5 0.4 collective-permute-done.1.refs_2_
  4.0 0.4 shard_map.69
  4.3 1.8 %collective-permute-start.2 = (bf16[256,1152]{1,0:T(8,128)(2,1)S(1)}, bf16[256,1152]{1,0:T(8,128)(2,1)S(1)}, u32[]{:S(2)}, u32[]{:S(2)}) collective-permute-start(bf16[256,1152]{1,0:T(8,128)(2,1)S(1)} %get-tuple-element.23.refs_2_), channel_id=1, source_target_pairs={{0,6},{32,34},{2,4},{34,32},{4,2},{36,38},{6,0},{38,36},{64,70},{9... | collective-permute-start | bytes 1769480 | tf_op jit(solution)/shard_map/ppermute | solution.py:46
  6.1 2.5 %collective-permute-start.4 = (bf16[256,1152]{1,0:T(8,128)(2,1)S(1)}, bf16[256,1152]{1,0:T(8,128)(2,1)S(1)}, u32[]{:S(2)}, u32[]{:S(2)}) collective-permute-start(bf16[256,1152]{1,0:T(8,128)(2,1)S(1)} %get-tuple-element.23.refs_2_), channel_id=1, source_target_pairs={{0,8},{32,56},{2,10},{34,58},{4,12},{36,60},{6,14},{38,62},{64,72}... | collective-permute-start | bytes 1769480 | tf_op jit(solution)/shard_map/ppermute | solution.py:46
  8.6 2.7 %collective-permute-start.5 = (bf16[256,1152]{1,0:T(8,128)(2,1)S(1)}, bf16[256,1152]{1,0:T(8,128)(2,1)S(1)}, u32[]{:S(2)}, u32[]{:S(2)}) collective-permute-start(bf16[256,1152]{1,0:T(8,128)(2,1)S(1)} %get-tuple-element.23.refs_2_), channel_id=1, source_target_pairs={{0,64},{32,97},{2,66},{34,99},{4,68},{36,101},{6,70},{38,103},{64,... | collective-permute-start | bytes 1769480 | tf_op jit(solution)/shard_map/ppermute | solution.py:46
  12.7 1.1 %collective-permute-done.2.refs_4_.refs_7_.refs_8_ = bf16[256,1152]{1,0:T(8,128)(2,1)S(1)} collective-permute-done((bf16[256,1152]{1,0:T(8,128)(2,1)S(1)}, bf16[256,1152]{1,0:T(8,128)(2,1)S(1)}, u32[]{:S(2)}, u32[]{:S(2)}) %collective-permute-start.2) | collective-permute-done | bytes 589856 | tf_op jit(solution)/shard_map/ppermute | solution.py:46
  13.7 2.7 %collective-permute-done.4.refs_2_.refs_5_ = bf16[256,1152]{1,0:T(8,128)(2,1)S(1)} collective-permute-done((bf16[256,1152]{1,0:T(8,128)(2,1)S(1)}, bf16[256,1152]{1,0:T(8,128)(2,1)S(1)}, u32[]{:S(2)}, u32[]{:S(2)}) %collective-permute-start.4) | collective-permute-done | bytes 589856 | tf_op jit(solution)/shard_map/ppermute | solution.py:46
  16.4 2.2 %collective-permute-done.5.refs_3_.refs_6_ = bf16[256,1152]{1,0:T(8,128)(2,1)S(1)} collective-permute-done((bf16[256,1152]{1,0:T(8,128)(2,1)S(1)}, bf16[256,1152]{1,0:T(8,128)(2,1)S(1)}, u32[]{:S(2)}, u32[]{:S(2)}) %collective-permute-start.5) | collective-permute-done | bytes 589856 | tf_op jit(solution)/shard_map/ppermute | solution.py:46
  18.6 0.1 shard_map.70
  18.8 1.7 %collective-permute-start.6 = (bf16[768,1152]{1,0:T(8,128)(2,1)S(1)}, bf16[768,1152]{1,0:T(8,128)(2,1)S(1)}, u32[]{:S(2)}, u32[]{:S(2)}) collective-permute-start(bf16[768,1152]{1,0:T(8,128)(2,1)S(1)} %shard_map.70), channel_id=1, source_target_pairs={{0,32},{32,0},{1,33},{33,1},{2,34},{34,2},{3,35},{35,3},{4,36},{36... | collective-permute-start | bytes 5308424 | tf_op jit(solution)/shard_map/ppermute | solution.py:50
  20.5 4.3 %collective-permute-start.3 = (bf16[256,1152]{1,0:T(8,128)(2,1)S(1)}, bf16[256,1152]{1,0:T(8,128)(2,1)S(1)}, u32[]{:S(2)}, u32[]{:S(2)}) collective-permute-start(bf16[256,1152]{1,0:T(8,128)(2,1)S(1)} %collective-permute-done.2.refs_4_.refs_7_.refs_8_), channel_id=1, source_target_pairs={{0,72},{32,121},{2,74},{34,123},{4,76},{36,125},{6,78},{38,127},{6... | collective-permute-start | bytes 1769480 | tf_op jit(solution)/shard_map/ppermute | solution.py:46
  24.8 0.9 %collective-permute-start.10 = (bf16[256,1152]{1,0:T(8,128)(2,1)S(1)}, bf16[256,1152]{1,0:T(8,128)(2,1)S(1)}, u32[]{:S(2)}, u32[]{:S(2)}) collective-permute-start(bf16[256,1152]{1,0:T(8,128)(2,1)S(1)} %collective-permute-done.2.refs_4_.refs_7_.refs_8_), channel_id=1, source_target_pairs={{0,8},{32,56},{2,10},{34,58},{4,12},{36,60},{6,14},{38,62},{64,72}... | collective-permute-start | bytes 1769480 | tf_op jit(solution)/shard_map/ppermute | solution.py:46
  25.6 5.7 %shard_map.71 = (f32[256,1152]{1,0:T(8,128)S(1)}, f32[256,1152]{1,0:T(8,128)S(1)}, f32[256,1152]{1,0:T(8,128)S(1)}, f32[256,1152]{1,0:T(8,128)S(1)}) custom-call(f32[1]{0:T(128)S(6)} %copy.7.refs_0_, f32[1]{0:T(128)S(6)} %copy.8.refs_1_, bf16[256,1152]{1,0:T(8,128)(2,1)S(1)} %get-tuple-element.23.refs_2_, bf16[256,1152]{1,0:T(8,128)(2,1)S(1)} %get-tuple-element.24.refs_3_, ...), custom_call_target="tpu_custom_call" | custom-call | tf_op jit(solution)/shard_map/pallas_call | solution.py:132
  31.3 1.3 %collective-permute-done.3.refs_0_.refs_2_ = bf16[256,1152]{1,0:T(8,128)(2,1)S(1)} collective-permute-done((bf16[256,1152]{1,0:T(8,128)(2,1)S(1)}, bf16[256,1152]{1,0:T(8,128)(2,1)S(1)}, u32[]{:S(2)}, u32[]{:S(2)}) %collective-permute-start.3) | collective-permute-done | bytes 589856 | tf_op jit(solution)/shard_map/ppermute | solution.py:46
  32.8 1.6 %shard_map.73.refs_3_.refs_6_.refs_5_ = f32[256,1152]{1,0:T(8,128)S(1)} custom-call(f32[1]{0:T(128)S(6)} %copy.7.refs_0_, f32[1]{0:T(128)S(6)} %copy.8.refs_1_, bf16[256,1152]{1,0:T(8,128)(2,1)S(1)} %collective-permute-done.3.refs_0_.refs_2_, bf16[256,1152]{1,0:T(8,128)(2,1)S(1)} %get-tuple-element.24.refs_3_, ...), custom_call_target="tpu_custom_call" | custom-call | flops 1207959552 | bytes 2359296 | tf_op jit(solution)/shard_map/pallas_call | solution.py:132
  34.4 4.5 %collective-permute-done.8.refs_0_.refs_2_ = bf16[256,1152]{1,0:T(8,128)(2,1)S(1)} collective-permute-done((bf16[256,1152]{1,0:T(8,128)(2,1)S(1)}, bf16[256,1152]{1,0:T(8,128)(2,1)S(1)}, u32[]{:S(2)}, u32[]{:S(2)}) %collective-permute-start.8) | collective-permute-done | bytes 589856 | tf_op jit(solution)/shard_map/ppermute | solution.py:46
  38.9 0.4 collective-permute-done.10.refs_2_.refs_5_.refs_6_
  39.3 0.1 shard_map.74
  39.4 0.3 collective-permute-start.11
  39.7 2.9 %shard_map.75 = (f32[256,1152]{1,0:T(8,128)S(1)}, f32[256,1152]{1,0:T(8,128)S(1)}) custom-call(f32[1]{0:T(128)S(6)} %copy.7.refs_0_, f32[1]{0:T(128)S(6)} %copy.8.refs_1_, bf16[256,1152]{1,0:T(8,128)(2,1)S(1)} %collective-permute-done.8.refs_0_.refs_2_, bf16[256,1152]{1,0:T(8,128)(2,1)S(1)} %get-tuple-element.24.refs_3_, ...), custom_call_target="tpu_custom_call" | custom-call | flops 2415919104 | bytes 4718592 | tf_op jit(solution)/shard_map/pallas_call | solution.py:132
  42.6 0.7 collective-permute-done.11.refs_4_.refs_6_
  43.3 1.6 %shard_map.76.refs_8_ = bf16[256,1152]{1,0:T(8,128)(2,1)S(1)} custom-call(f32[1]{0:T(128)S(6)} %copy.7.refs_0_, f32[1]{0:T(128)S(6)} %copy.8.refs_1_, bf16[256,1152]{1,0:T(8,128)(2,1)S(1)} %collective-permute-done.3.refs_0_.refs_2_, bf16[256,1152]{1,0:T(8,128)(2,1)S(1)} %collective-permute-done.7.refs_4_.refs_3_.refs_5_, ...), custom_call_target="tpu_custom_call" | custom-call | flops 1207959552 | bytes 2359296 | tf_op jit(solution)/shard_map/pallas_call | solution.py:132
  44.9 1.9 %collective-permute-start.12 = (bf16[256,1152]{1,0:T(8,128)(2,1)S(1)}, bf16[256,1152]{1,0:T(8,128)(2,1)S(1)}, u32[]{:S(2)}, u32[]{:S(2)}) collective-permute-start(bf16[256,1152]{1,0:T(8,128)(2,1)S(1)} %shard_map.76.refs_8_), channel_id=1, source_target_pairs={{0,8},{32,56},{2,10},{34,58},{4,12},{36,60},{6,14},{38,62},{64,72}... | collective-permute-start | bytes 1769480 | tf_op jit(solution)/shard_map/ppermute | solution.py:46
  46.8 2.9 %shard_map.77 = (bf16[256,1152]{1,0:T(8,128)(2,1)S(1)}, bf16[256,1152]{1,0:T(8,128)(2,1)S(1)}) custom-call(f32[1]{0:T(128)S(6)} %copy.7.refs_0_, f32[1]{0:T(128)S(6)} %copy.8.refs_1_, bf16[256,1152]{1,0:T(8,128)(2,1)S(1)} %collective-permute-done.8.refs_0_.refs_2_, bf16[256,1152]{1,0:T(8,128)(2,1)S(1)} %collective-permute-done.7.refs_4_.refs_3_.refs_5_, ...), custom_call_target="tpu_custom_call" | custom-call | flops 2415919104 | bytes 4718592 | tf_op jit(solution)/shard_map/pallas_call | solution.py:132
  49.7 0.9 %collective-permute-start.14 = (bf16[256,1152]{1,0:T(8,128)(2,1)S(1)}, bf16[256,1152]{1,0:T(8,128)(2,1)S(1)}, u32[]{:S(2)}, u32[]{:S(2)}) collective-permute-start(bf16[256,1152]{1,0:T(8,128)(2,1)S(1)} %get-tuple-element.31.refs_7_), channel_id=1, source_target_pairs={{0,64},{32,97},{2,66},{34,99},{4,68},{36,101},{6,70},{38,103},{64,... | collective-permute-start | bytes 1769480 | tf_op jit(solution)/shard_map/ppermute | solution.py:46
  50.6 1.8 %collective-permute-start.15 = (bf16[256,1152]{1,0:T(8,128)(2,1)S(1)}, bf16[256,1152]{1,0:T(8,128)(2,1)S(1)}, u32[]{:S(2)}, u32[]{:S(2)}) collective-permute-start(bf16[256,1152]{1,0:T(8,128)(2,1)S(1)} %get-tuple-element.35), channel_id=1, source_target_pairs={{0,8},{32,56},{2,10},{34,58},{4,12},{36,60},{6,14},{38,62},{64,72}... | collective-permute-start | bytes 1769480 | tf_op jit(solution)/shard_map/ppermute | solution.py:46
  52.5 2.9 %shard_map.78.refs_0_ = f32[256,1152]{1,0:T(8,128)S(1)} custom-call(f32[1]{0:T(128)S(6)} %copy.7.refs_0_, f32[1]{0:T(128)S(6)} %copy.8.refs_1_, bf16[256,1152]{1,0:T(8,128)(2,1)S(1)} %collective-permute-done.9.refs_1_.refs_2_, bf16[256,1152]{1,0:T(8,128)(2,1)S(1)} %get-tuple-element.24.refs_3_, bf16[768,1152]{1,0:T(8,128)(2,1)S(1)} %collective-permute-done.6.refs_4_, ...), custom_call_target="tpu_custom_call" | custom-call | flops 2415919104 | bytes 2359296 | tf_op jit(solution)/shard_map/pallas_call | solution.py:132
  55.4 0.1 shard_map.79.refs_10_
  55.5 0.3 collective-permute-start.13
  55.8 4.3 %shard_map.80 = (f32[256,1152]{1,0:T(8,128)S(1)}, f32[256,1152]{1,0:T(8,128)S(1)}, f32[256,1152]{1,0:T(8,128)S(1)}) custom-call(f32[1]{0:T(128)S(6)} %copy.7.refs_0_, f32[1]{0:T(128)S(6)} %copy.8.refs_1_, bf16[256,1152]{1,0:T(8,128)(2,1)S(1)} %collective-permute-done.4.refs_2_.refs_5_, bf16[256,1152]{1,0:T(8,128)(2,1)S(1)} %collective-permute-done.7.refs_4_.refs_3_.refs_5_, ...), custom_call_target="tpu_custom_call" | custom-call | flops 3623878656 | bytes 7077888 | tf_op jit(solution)/shard_map/pallas_call | solution.py:132
  60.1 0.1 shard_map.81.refs_3_
  60.2 1.4 %collective-permute-start.16 = (bf16[256,1152]{1,0:T(8,128)(2,1)S(1)}, bf16[256,1152]{1,0:T(8,128)(2,1)S(1)}, u32[]{:S(2)}, u32[]{:S(2)}) collective-permute-start(bf16[256,1152]{1,0:T(8,128)(2,1)S(1)} %shard_map.81.refs_3_), channel_id=1, source_target_pairs={{0,8},{32,56},{2,10},{34,58},{4,12},{36,60},{6,14},{38,62},{64,72}... | collective-permute-start | bytes 1769480 | tf_op jit(solution)/shard_map/ppermute | solution.py:46
  61.7 0.1 shard_map.82.refs_4_
  61.8 1.5 %collective-permute-start.17 = (bf16[256,1152]{1,0:T(8,128)(2,1)S(1)}, bf16[256,1152]{1,0:T(8,128)(2,1)S(1)}, u32[]{:S(2)}, u32[]{:S(2)}) collective-permute-start(bf16[256,1152]{1,0:T(8,128)(2,1)S(1)} %shard_map.82.refs_4_), channel_id=1, source_target_pairs={{0,6},{32,34},{2,4},{34,32},{4,2},{36,38},{6,0},{38,36},{64,70},{9... | collective-permute-start | bytes 1769480 | tf_op jit(solution)/shard_map/ppermute | solution.py:46
  63.3 1.5 %collective-permute-done.13.refs_2_ = bf16[256,1152]{1,0:T(8,128)(2,1)S(1)} collective-permute-done((bf16[256,1152]{1,0:T(8,128)(2,1)S(1)}, bf16[256,1152]{1,0:T(8,128)(2,1)S(1)}, u32[]{:S(2)}, u32[]{:S(2)}) %collective-permute-start.13) | collective-permute-done | bytes 589856 | tf_op jit(solution)/shard_map/ppermute | solution.py:46
  64.8 0.1 shard_map.83
  64.9 3.4 %collective-permute-start.18 = (bf16[128,1152]{1,0:T(8,128)(2,1)S(1)}, bf16[128,1152]{1,0:T(8,128)(2,1)S(1)}, u32[]{:S(2)}, u32[]{:S(2)}) collective-permute-start(bf16[128,1152]{1,0:T(8,128)(2,1)S(1)} %get-tuple-element.37), channel_id=1, source_target_pairs={{0,96},{32,65},{2,98},{34,67},{4,100},{36,69},{6,102},{38,71},{64,... | collective-permute-start | bytes 884744 | tf_op jit(solution)/shard_map/ppermute | solution.py:46
  68.4 0.9 %collective-permute-start.20 = (bf16[128,1152]{1,0:T(8,128)(2,1)S(1)}, bf16[128,1152]{1,0:T(8,128)(2,1)S(1)}, u32[]{:S(2)}, u32[]{:S(2)}) collective-permute-start(bf16[128,1152]{1,0:T(8,128)(2,1)S(1)} %get-tuple-element.36.refs_6_), channel_id=1, source_target_pairs={{0,64},{32,97},{2,66},{34,99},{4,68},{36,101},{6,70},{38,103},{64,... | collective-permute-start | bytes 884744 | tf_op jit(solution)/shard_map/ppermute | solution.py:46
  69.2 1.6 %shard_map.84.refs_1_ = f32[256,1152]{1,0:T(8,128)S(1)} custom-call(f32[1]{0:T(128)S(6)} %copy.7.refs_0_, f32[1]{0:T(128)S(6)} %copy.8.refs_1_, bf16[256,1152]{1,0:T(8,128)(2,1)S(1)} %get-tuple-element.23.refs_2_, bf16[256,1152]{1,0:T(8,128)(2,1)S(1)} %collective-permute-done.7.refs_4_.refs_3_.refs_5_, ...), custom_call_target="tpu_custom_call" | custom-call | flops 1207959552 | bytes 2359296 | tf_op jit(solution)/shard_map/pallas_call | solution.py:132
  70.8 0.3 collective-permute-done.17.refs_3_
  71.2 0.9 %collective-permute-done.18.refs_4_.refs_5_ = bf16[128,1152]{1,0:T(8,128)(2,1)S(1)} collective-permute-done((bf16[128,1152]{1,0:T(8,128)(2,1)S(1)}, bf16[128,1152]{1,0:T(8,128)(2,1)S(1)}, u32[]{:S(2)}, u32[]{:S(2)}) %collective-permute-start.18) | collective-permute-done | bytes 294944 | tf_op jit(solution)/shard_map/ppermute | solution.py:46
  72.0 0.2 shard_map.85
  72.2 2.1 %collective-permute-start.19 = (bf16[128,1152]{1,0:T(8,128)(2,1)S(1)}, bf16[128,1152]{1,0:T(8,128)(2,1)S(1)}, u32[]{:S(2)}, u32[]{:S(2)}) collective-permute-start(bf16[128,1152]{1,0:T(8,128)(2,1)S(1)} %get-tuple-element.39), channel_id=1, source_target_pairs={{0,32},{32,0},{1,33},{33,1},{2,34},{34,2},{3,35},{35,3},{4,36},{36... | collective-permute-start | bytes 884744 | tf_op jit(solution)/shard_map/ppermute | solution.py:50
  75.0 1.5 %collective-permute-done.20.refs_4_ = bf16[128,1152]{1,0:T(8,128)(2,1)S(1)} collective-permute-done((bf16[128,1152]{1,0:T(8,128)(2,1)S(1)}, bf16[128,1152]{1,0:T(8,128)(2,1)S(1)}, u32[]{:S(2)}, u32[]{:S(2)}) %collective-permute-start.20) | collective-permute-done | bytes 294944 | tf_op jit(solution)/shard_map/ppermute | solution.py:46
  76.5 1.6 %shard_map.86 = (f32[128,1152]{1,0:T(8,128)}, f32[128,1152]{1,0:T(8,128)}) custom-call(f32[1]{0:T(128)} %bitcast.refs_0_.is_first, f32[1]{0:T(128)S(6)} %div.3.multiplier, bf16[128,1152]{1,0:T(8,128)(2,1)S(1)} %copy-done, bf16[128,1152]{1,0:T(8,128)(2,1)S(1)} %copy-done.1, f32[128,1152]{1,0:T(8,128)S(1)} %get-tuple-element.38.refs_2_, ...), custom_call_target="tpu_custom_call" | custom-call | tf_op jit(solution)/shard_map/pallas_call | solution.py:271
  (18 shorter events, 0.3 us)
Async XLA Ops:
  0.6 2.9 %collective-permute-start = (bf16[128,1152]{1,0:T(8,128)(2,1)}, bf16[128,1152]{1,0:T(8,128)(2,1)S(1)}, u32[]{:S(2)}, u32[]{:S(2)}) collective-permute-start(bf16[128,1152]{1,0:T(8,128)(2,1)} %refs_0_.10), channel_id=1, source_target_pairs={{0,32},{32,0},{1,33},{33,1},{2,34},{34,2},{3,35},{35,3},{4,36},{36... | collective-permute-start | bytes 884744 | tf_op jit(solution)/shard_map/ppermute | solution.py:50
  2.1 1.8 %collective-permute-start.1 = (bf16[128,1152]{1,0:T(8,128)(2,1)}, bf16[128,1152]{1,0:T(8,128)(2,1)S(1)}, u32[]{:S(2)}, u32[]{:S(2)}) collective-permute-start(bf16[128,1152]{1,0:T(8,128)(2,1)} %refs_1_.10), channel_id=1, source_target_pairs={{0,32},{32,0},{1,33},{33,1},{2,34},{34,2},{3,35},{35,3},{4,36},{36... | collective-permute-start | bytes 884744 | tf_op jit(solution)/shard_map/ppermute | solution.py:50
  4.3 9.4 %collective-permute-start.2 = (bf16[256,1152]{1,0:T(8,128)(2,1)S(1)}, bf16[256,1152]{1,0:T(8,128)(2,1)S(1)}, u32[]{:S(2)}, u32[]{:S(2)}) collective-permute-start(bf16[256,1152]{1,0:T(8,128)(2,1)S(1)} %get-tuple-element.23.refs_2_), channel_id=1, source_target_pairs={{0,6},{32,34},{2,4},{34,32},{4,2},{36,38},{6,0},{38,36},{64,70},{9... | collective-permute-start | bytes 1769480 | tf_op jit(solution)/shard_map/ppermute | solution.py:46
  6.1 10.2 %collective-permute-start.4 = (bf16[256,1152]{1,0:T(8,128)(2,1)S(1)}, bf16[256,1152]{1,0:T(8,128)(2,1)S(1)}, u32[]{:S(2)}, u32[]{:S(2)}) collective-permute-start(bf16[256,1152]{1,0:T(8,128)(2,1)S(1)} %get-tuple-element.23.refs_2_), channel_id=1, source_target_pairs={{0,8},{32,56},{2,10},{34,58},{4,12},{36,60},{6,14},{38,62},{64,72}... | collective-permute-start | bytes 1769480 | tf_op jit(solution)/shard_map/ppermute | solution.py:46
  8.6 10.0 %collective-permute-start.5 = (bf16[256,1152]{1,0:T(8,128)(2,1)S(1)}, bf16[256,1152]{1,0:T(8,128)(2,1)S(1)}, u32[]{:S(2)}, u32[]{:S(2)}) collective-permute-start(bf16[256,1152]{1,0:T(8,128)(2,1)S(1)} %get-tuple-element.23.refs_2_), channel_id=1, source_target_pairs={{0,64},{32,97},{2,66},{34,99},{4,68},{36,101},{6,70},{38,103},{64,... | collective-permute-start | bytes 1769480 | tf_op jit(solution)/shard_map/ppermute | solution.py:46
  18.8 6.9 %collective-permute-start.6 = (bf16[768,1152]{1,0:T(8,128)(2,1)S(1)}, bf16[768,1152]{1,0:T(8,128)(2,1)S(1)}, u32[]{:S(2)}, u32[]{:S(2)}) collective-permute-start(bf16[768,1152]{1,0:T(8,128)(2,1)S(1)} %shard_map.70), channel_id=1, source_target_pairs={{0,32},{32,0},{1,33},{33,1},{2,34},{34,2},{3,35},{35,3},{4,36},{36... | collective-permute-start | bytes 5308424 | tf_op jit(solution)/shard_map/ppermute | solution.py:50
  20.5 12.2 %collective-permute-start.3 = (bf16[256,1152]{1,0:T(8,128)(2,1)S(1)}, bf16[256,1152]{1,0:T(8,128)(2,1)S(1)}, u32[]{:S(2)}, u32[]{:S(2)}) collective-permute-start(bf16[256,1152]{1,0:T(8,128)(2,1)S(1)} %collective-permute-done.2.refs_4_.refs_7_.refs_8_), channel_id=1, source_target_pairs={{0,72},{32,121},{2,74},{34,123},{4,76},{36,125},{6,78},{38,127},{6... | collective-permute-start | bytes 1769480 | tf_op jit(solution)/shard_map/ppermute | solution.py:46
  24.8 14.1 %collective-permute-start.8 = (bf16[256,1152]{1,0:T(8,128)(2,1)S(1)}, bf16[256,1152]{1,0:T(8,128)(2,1)S(1)}, u32[]{:S(2)}, u32[]{:S(2)}) collective-permute-start(bf16[256,1152]{1,0:T(8,128)(2,1)S(1)} %collective-permute-done.4.refs_2_.refs_5_), channel_id=1, source_target_pairs={{0,64},{32,97},{2,66},{34,99},{4,68},{36,101},{6,70},{38,103},{64,... | collective-permute-start | bytes 1769480 | tf_op jit(solution)/shard_map/ppermute | solution.py:46
  24.8 14.1 %collective-permute-start.9 = (bf16[256,1152]{1,0:T(8,128)(2,1)S(1)}, bf16[256,1152]{1,0:T(8,128)(2,1)S(1)}, u32[]{:S(2)}, u32[]{:S(2)}) collective-permute-start(bf16[256,1152]{1,0:T(8,128)(2,1)S(1)} %collective-permute-done.5.refs_3_.refs_6_), channel_id=1, source_target_pairs={{0,6},{32,34},{2,4},{34,32},{4,2},{36,38},{6,0},{38,36},{64,70},{9... | collective-permute-start | bytes 1769480 | tf_op jit(solution)/shard_map/ppermute | solution.py:46
  24.8 14.5 %collective-permute-start.10 = (bf16[256,1152]{1,0:T(8,128)(2,1)S(1)}, bf16[256,1152]{1,0:T(8,128)(2,1)S(1)}, u32[]{:S(2)}, u32[]{:S(2)}) collective-permute-start(bf16[256,1152]{1,0:T(8,128)(2,1)S(1)} %collective-permute-done.2.refs_4_.refs_7_.refs_8_), channel_id=1, source_target_pairs={{0,8},{32,56},{2,10},{34,58},{4,12},{36,60},{6,14},{38,62},{64,72}... | collective-permute-start | bytes 1769480 | tf_op jit(solution)/shard_map/ppermute | solution.py:46
  32.7 6.6 %collective-permute-start.7 = (bf16[256,1152]{1,0:T(8,128)(2,1)S(1)}, bf16[256,1152]{1,0:T(8,128)(2,1)S(1)}, u32[]{:S(2)}, u32[]{:S(2)}) collective-permute-start(bf16[256,1152]{1,0:T(8,128)(2,1)S(1)} %shard_map.72), channel_id=1, source_target_pairs={{0,32},{32,0},{1,33},{33,1},{2,34},{34,2},{3,35},{35,3},{4,36},{36... | collective-permute-start | bytes 1769480 | tf_op jit(solution)/shard_map/ppermute | solution.py:50
  39.4 4.0 %collective-permute-start.11 = (bf16[768,1152]{1,0:T(8,128)(2,1)S(1)}, bf16[768,1152]{1,0:T(8,128)(2,1)S(1)}, u32[]{:S(2)}, u32[]{:S(2)}) collective-permute-start(bf16[768,1152]{1,0:T(8,128)(2,1)S(1)} %shard_map.74), channel_id=1, source_target_pairs={{0,32},{32,0},{1,33},{33,1},{2,34},{34,2},{3,35},{35,3},{4,36},{36... | collective-permute-start | bytes 5308424 | tf_op jit(solution)/shard_map/ppermute | solution.py:50
  44.9 10.5 %collective-permute-start.12 = (bf16[256,1152]{1,0:T(8,128)(2,1)S(1)}, bf16[256,1152]{1,0:T(8,128)(2,1)S(1)}, u32[]{:S(2)}, u32[]{:S(2)}) collective-permute-start(bf16[256,1152]{1,0:T(8,128)(2,1)S(1)} %shard_map.76.refs_8_), channel_id=1, source_target_pairs={{0,8},{32,56},{2,10},{34,58},{4,12},{36,60},{6,14},{38,62},{64,72}... | collective-permute-start | bytes 1769480 | tf_op jit(solution)/shard_map/ppermute | solution.py:46
  49.7 10.4 %collective-permute-start.14 = (bf16[256,1152]{1,0:T(8,128)(2,1)S(1)}, bf16[256,1152]{1,0:T(8,128)(2,1)S(1)}, u32[]{:S(2)}, u32[]{:S(2)}) collective-permute-start(bf16[256,1152]{1,0:T(8,128)(2,1)S(1)} %get-tuple-element.31.refs_7_), channel_id=1, source_target_pairs={{0,64},{32,97},{2,66},{34,99},{4,68},{36,101},{6,70},{38,103},{64,... | collective-permute-start | bytes 1769480 | tf_op jit(solution)/shard_map/ppermute | solution.py:46
  50.6 11.0 %collective-permute-start.15 = (bf16[256,1152]{1,0:T(8,128)(2,1)S(1)}, bf16[256,1152]{1,0:T(8,128)(2,1)S(1)}, u32[]{:S(2)}, u32[]{:S(2)}) collective-permute-start(bf16[256,1152]{1,0:T(8,128)(2,1)S(1)} %get-tuple-element.35), channel_id=1, source_target_pairs={{0,8},{32,56},{2,10},{34,58},{4,12},{36,60},{6,14},{38,62},{64,72}... | collective-permute-start | bytes 1769480 | tf_op jit(solution)/shard_map/ppermute | solution.py:46
  55.5 9.3 %collective-permute-start.13 = (bf16[256,1152]{1,0:T(8,128)(2,1)S(1)}, bf16[256,1152]{1,0:T(8,128)(2,1)S(1)}, u32[]{:S(2)}, u32[]{:S(2)}) collective-permute-start(bf16[256,1152]{1,0:T(8,128)(2,1)S(1)} %shard_map.79.refs_10_), channel_id=1, source_target_pairs={{0,6},{32,34},{2,4},{34,32},{4,2},{36,38},{6,0},{38,36},{64,70},{9... | collective-permute-start | bytes 1769480 | tf_op jit(solution)/shard_map/ppermute | solution.py:46
  60.2 10.6 %collective-permute-start.16 = (bf16[256,1152]{1,0:T(8,128)(2,1)S(1)}, bf16[256,1152]{1,0:T(8,128)(2,1)S(1)}, u32[]{:S(2)}, u32[]{:S(2)}) collective-permute-start(bf16[256,1152]{1,0:T(8,128)(2,1)S(1)} %shard_map.81.refs_3_), channel_id=1, source_target_pairs={{0,8},{32,56},{2,10},{34,58},{4,12},{36,60},{6,14},{38,62},{64,72}... | collective-permute-start | bytes 1769480 | tf_op jit(solution)/shard_map/ppermute | solution.py:46
  61.8 9.4 %collective-permute-start.17 = (bf16[256,1152]{1,0:T(8,128)(2,1)S(1)}, bf16[256,1152]{1,0:T(8,128)(2,1)S(1)}, u32[]{:S(2)}, u32[]{:S(2)}) collective-permute-start(bf16[256,1152]{1,0:T(8,128)(2,1)S(1)} %shard_map.82.refs_4_), channel_id=1, source_target_pairs={{0,6},{32,34},{2,4},{34,32},{4,2},{36,38},{6,0},{38,36},{64,70},{9... | collective-permute-start | bytes 1769480 | tf_op jit(solution)/shard_map/ppermute | solution.py:46
  64.9 7.1 %collective-permute-start.18 = (bf16[128,1152]{1,0:T(8,128)(2,1)S(1)}, bf16[128,1152]{1,0:T(8,128)(2,1)S(1)}, u32[]{:S(2)}, u32[]{:S(2)}) collective-permute-start(bf16[128,1152]{1,0:T(8,128)(2,1)S(1)} %get-tuple-element.37), channel_id=1, source_target_pairs={{0,96},{32,65},{2,98},{34,67},{4,100},{36,69},{6,102},{38,71},{64,... | collective-permute-start | bytes 884744 | tf_op jit(solution)/shard_map/ppermute | solution.py:46
  68.4 8.2 %collective-permute-start.20 = (bf16[128,1152]{1,0:T(8,128)(2,1)S(1)}, bf16[128,1152]{1,0:T(8,128)(2,1)S(1)}, u32[]{:S(2)}, u32[]{:S(2)}) collective-permute-start(bf16[128,1152]{1,0:T(8,128)(2,1)S(1)} %get-tuple-element.36.refs_6_), channel_id=1, source_target_pairs={{0,64},{32,97},{2,66},{34,99},{4,68},{36,101},{6,70},{38,103},{64,... | collective-permute-start | bytes 884744 | tf_op jit(solution)/shard_map/ppermute | solution.py:46
  70.8 5.7 %copy-start = (bf16[128,1152]{1,0:T(8,128)(2,1)S(1)}, bf16[128,1152]{1,0:T(8,128)(2,1)}, u32[]{:S(2)}) copy-start(bf16[128,1152]{1,0:T(8,128)(2,1)} %refs_0_.10) | copy-start | bytes 884740
  70.8 5.7 %copy-start.1 = (bf16[128,1152]{1,0:T(8,128)(2,1)S(1)}, bf16[128,1152]{1,0:T(8,128)(2,1)}, u32[]{:S(2)}) copy-start(bf16[128,1152]{1,0:T(8,128)(2,1)} %refs_1_.10) | copy-start | bytes 884740
  72.2 4.3 %collective-permute-start.19 = (bf16[128,1152]{1,0:T(8,128)(2,1)S(1)}, bf16[128,1152]{1,0:T(8,128)(2,1)S(1)}, u32[]{:S(2)}, u32[]{:S(2)}) collective-permute-start(bf16[128,1152]{1,0:T(8,128)(2,1)S(1)} %get-tuple-element.39), channel_id=1, source_target_pairs={{0,32},{32,0},{1,33},{33,1},{2,34},{34,2},{3,35},{35,3},{4,36},{36... | collective-permute-start | bytes 884744 | tf_op jit(solution)/shard_map/ppermute | solution.py:50

commit v19 on v18

--- a/solution.py
+++ b/solution.py
@@ -23,6 +23,7 @@
 ANY = pl.BlockSpec(memory_space=pl.ANY)
 PARAMS = pltpu.CompilerParams(vmem_limit_bytes=VMEM_BYTES)
 
+NAMES = ({"x": "x", "y": "y", "z": "z"}, {"x": "z", "y": "y", "z": "x"})
 ONE = ("x", "y", "z")
 TWO = ("xy", "yz", "zx")
 
@@ -41,7 +42,10 @@
     pairs = []
     for at in np.ndindex(RING, RING, RING):
         for core in range(2):
-            to = [mate(core, axis, k) if axis in way else k for axis, k in zip("xyz", at, strict=True)]
+            to = [
+                mate(core, axis, k) if NAMES[core][axis] in way else k
+                for axis, k in zip("xyz", at, strict=True)
+            ]
             pairs.append((place(core, *at), place(1 - core if crossing else core, *to)))
     return lax.ppermute(value, FINE_AXES, pairs)
 

time: 78.4 us -> 76.9 us (0.981)
  starting transfers between devices: 30.1 us -> 29.1 us
  transfers between devices with their start and end apart: 21 -> 21, of which waited for: 12 -> 11; matrix products, arithmetic and copies ran while one was open for 1% -> 1% of each run, Pallas kernels for 29% -> 30%
where the time goes in v19:
time: 76.9 us; the launch traced here: 76.7 us
  starting transfers between devices  29.1 us (38%)
  Pallas kernels  26.5 us (34%)
  waiting for transfers between devices  17.1 us (22%)
  between operations  2.93 us (4%)
  other arithmetic  1.1 us (1%)
    ppermute x15, starting transfers between devices, sent(): return lax.ppermute(value, FINE_AXES, pairs)  24 us
    pallas_call x8, Pallas kernels, sums_of(): pl.pallas_call(functools.partial(sums_kernel, plan, len(inputs), len(afte...  23.4 us
    ppermute x15, waiting for transfers between devices, sent(): return lax.ppermute(value, FINE_AXES, pairs)  16.1 us
    ppermute x6, starting transfers between devices, other_core(): return lax.ppermute(value, 'core', [(0, 1), (1, 0)])  5.09 us
    pallas_call x1, Pallas kernels, on_device(): pl.pallas_call(finish_kernel, out_shape=[jax.ShapeDtypeStruct(*shard_full...  1.58 us
  transfers between devices with their start and end apart: 21, of which 11 were waited for; matrix products, arithmetic and copies ran while one was open for 1% of the time, Pallas kernels for 30%

profile of v19, /device:TPU:1, one launch (start us, length us, event | category | flops | bytes accessed | tf_op | source)
XLA Modules:
  0.0 76.7 jit_solution(7116632480046800650)
XLA Ops:
  0.6 1.5 %collective-permute-start = (bf16[128,1152]{1,0:T(8,128)(2,1)}, bf16[128,1152]{1,0:T(8,128)(2,1)S(1)}, u32[]{:S(2)}, u32[]{:S(2)}) collective-permute-start(bf16[128,1152]{1,0:T(8,128)(2,1)} %refs_0_.10), channel_id=1, source_target_pairs={{0,32},{32,0},{1,33},{33,1},{2,34},{34,2},{3,35},{35,3},{4,36},{36... | collective-permute-start | bytes 884744 | tf_op jit(solution)/shard_map/ppermute | solution.py:54
  2.2 1.1 %pad_maximum_fusion.refs_0_ = bf16[256,1152]{1,0:T(8,128)(2,1)S(1)} fusion(bf16[128,1152]{1,0:T(8,128)(2,1)} %refs_1_.10, bf16[128,1152]{1,0:T(8,128)(2,1)} %refs_0_.10), kind=kLoop, calls=%fused_computation | loop fusion | flops 1179648 | bytes 1179648 | tf_op jit(solution)/shard_map/concatenate | solution.py:188
  3.3 0.2 shard_map.68
  3.5 0.4 collective-permute-done.1.refs_2_
  4.0 0.4 shard_map.69
  4.3 2.6 %collective-permute-start.2 = (bf16[256,1152]{1,0:T(8,128)(2,1)S(1)}, bf16[256,1152]{1,0:T(8,128)(2,1)S(1)}, u32[]{:S(2)}, u32[]{:S(2)}) collective-permute-start(bf16[256,1152]{1,0:T(8,128)(2,1)S(1)} %get-tuple-element.23.refs_2_), channel_id=1, source_target_pairs={{0,6},{32,56},{2,4},{34,58},{4,2},{36,60},{6,0},{38,62},{64,70},{9... | collective-permute-start | bytes 1769480 | tf_op jit(solution)/shard_map/ppermute | solution.py:50
  7.0 1.6 %collective-permute-start.4 = (bf16[256,1152]{1,0:T(8,128)(2,1)S(1)}, bf16[256,1152]{1,0:T(8,128)(2,1)S(1)}, u32[]{:S(2)}, u32[]{:S(2)}) collective-permute-start(bf16[256,1152]{1,0:T(8,128)(2,1)S(1)} %get-tuple-element.23.refs_2_), channel_id=1, source_target_pairs={{0,8},{32,34},{2,10},{34,32},{4,12},{36,38},{6,14},{38,36},{64,72}... | collective-permute-start | bytes 1769480 | tf_op jit(solution)/shard_map/ppermute | solution.py:50
  8.6 2.7 %collective-permute-start.5 = (bf16[256,1152]{1,0:T(8,128)(2,1)S(1)}, bf16[256,1152]{1,0:T(8,128)(2,1)S(1)}, u32[]{:S(2)}, u32[]{:S(2)}) collective-permute-start(bf16[256,1152]{1,0:T(8,128)(2,1)S(1)} %get-tuple-element.23.refs_2_), channel_id=1, source_target_pairs={{0,64},{32,97},{2,66},{34,99},{4,68},{36,101},{6,70},{38,103},{64,... | collective-permute-start | bytes 1769480 | tf_op jit(solution)/shard_map/ppermute | solution.py:50
  12.7 2.0 %collective-permute-done.2.refs_4_.refs_7_.refs_8_ = bf16[256,1152]{1,0:T(8,128)(2,1)S(1)} collective-permute-done((bf16[256,1152]{1,0:T(8,128)(2,1)S(1)}, bf16[256,1152]{1,0:T(8,128)(2,1)S(1)}, u32[]{:S(2)}, u32[]{:S(2)}) %collective-permute-start.2) | collective-permute-done | bytes 589856 | tf_op jit(solution)/shard_map/ppermute | solution.py:50
  14.7 1.5 %collective-permute-done.4.refs_2_.refs_5_ = bf16[256,1152]{1,0:T(8,128)(2,1)S(1)} collective-permute-done((bf16[256,1152]{1,0:T(8,128)(2,1)S(1)}, bf16[256,1152]{1,0:T(8,128)(2,1)S(1)}, u32[]{:S(2)}, u32[]{:S(2)}) %collective-permute-start.4) | collective-permute-done | bytes 589856 | tf_op jit(solution)/shard_map/ppermute | solution.py:50
  16.2 2.4 %collective-permute-done.5.refs_3_.refs_6_ = bf16[256,1152]{1,0:T(8,128)(2,1)S(1)} collective-permute-done((bf16[256,1152]{1,0:T(8,128)(2,1)S(1)}, bf16[256,1152]{1,0:T(8,128)(2,1)S(1)}, u32[]{:S(2)}, u32[]{:S(2)}) %collective-permute-start.5) | collective-permute-done | bytes 589856 | tf_op jit(solution)/shard_map/ppermute | solution.py:50
  18.6 0.1 shard_map.70
  18.8 1.7 %collective-permute-start.6 = (bf16[768,1152]{1,0:T(8,128)(2,1)S(1)}, bf16[768,1152]{1,0:T(8,128)(2,1)S(1)}, u32[]{:S(2)}, u32[]{:S(2)}) collective-permute-start(bf16[768,1152]{1,0:T(8,128)(2,1)S(1)} %shard_map.70), channel_id=1, source_target_pairs={{0,32},{32,0},{1,33},{33,1},{2,34},{34,2},{3,35},{35,3},{4,36},{36... | collective-permute-start | bytes 5308424 | tf_op jit(solution)/shard_map/ppermute | solution.py:54
  20.5 2.0 %collective-permute-start.3 = (bf16[256,1152]{1,0:T(8,128)(2,1)S(1)}, bf16[256,1152]{1,0:T(8,128)(2,1)S(1)}, u32[]{:S(2)}, u32[]{:S(2)}) collective-permute-start(bf16[256,1152]{1,0:T(8,128)(2,1)S(1)} %collective-permute-done.2.refs_4_.refs_7_.refs_8_), channel_id=1, source_target_pairs={{0,72},{32,99},{2,74},{34,97},{4,76},{36,103},{6,78},{38,101},{64,... | collective-permute-start | bytes 1769480 | tf_op jit(solution)/shard_map/ppermute | solution.py:50
  22.5 0.8 %collective-permute-start.8 = (bf16[256,1152]{1,0:T(8,128)(2,1)S(1)}, bf16[256,1152]{1,0:T(8,128)(2,1)S(1)}, u32[]{:S(2)}, u32[]{:S(2)}) collective-permute-start(bf16[256,1152]{1,0:T(8,128)(2,1)S(1)} %collective-permute-done.4.refs_2_.refs_5_), channel_id=1, source_target_pairs={{0,64},{32,97},{2,66},{34,99},{4,68},{36,101},{6,70},{38,103},{64,... | collective-permute-start | bytes 1769480 | tf_op jit(solution)/shard_map/ppermute | solution.py:50
  23.2 1.8 %collective-permute-start.9 = (bf16[256,1152]{1,0:T(8,128)(2,1)S(1)}, bf16[256,1152]{1,0:T(8,128)(2,1)S(1)}, u32[]{:S(2)}, u32[]{:S(2)}) collective-permute-start(bf16[256,1152]{1,0:T(8,128)(2,1)S(1)} %collective-permute-done.5.refs_3_.refs_6_), channel_id=1, source_target_pairs={{0,6},{32,56},{2,4},{34,58},{4,2},{36,60},{6,0},{38,62},{64,70},{9... | collective-permute-start | bytes 1769480 | tf_op jit(solution)/shard_map/ppermute | solution.py:50
  25.1 1.2 %collective-permute-start.10 = (bf16[256,1152]{1,0:T(8,128)(2,1)S(1)}, bf16[256,1152]{1,0:T(8,128)(2,1)S(1)}, u32[]{:S(2)}, u32[]{:S(2)}) collective-permute-start(bf16[256,1152]{1,0:T(8,128)(2,1)S(1)} %collective-permute-done.2.refs_4_.refs_7_.refs_8_), channel_id=1, source_target_pairs={{0,8},{32,34},{2,10},{34,32},{4,12},{36,38},{6,14},{38,36},{64,72}... | collective-permute-start | bytes 1769480 | tf_op jit(solution)/shard_map/ppermute | solution.py:50
  26.2 5.7 %shard_map.71 = (f32[256,1152]{1,0:T(8,128)S(1)}, f32[256,1152]{1,0:T(8,128)S(1)}, f32[256,1152]{1,0:T(8,128)S(1)}, f32[256,1152]{1,0:T(8,128)S(1)}) custom-call(f32[1]{0:T(128)S(6)} %copy.7.refs_0_, f32[1]{0:T(128)S(6)} %copy.8.refs_1_, bf16[256,1152]{1,0:T(8,128)(2,1)S(1)} %get-tuple-element.23.refs_2_, bf16[256,1152]{1,0:T(8,128)(2,1)S(1)} %get-tuple-element.24.refs_3_, ...), custom_call_target="tpu_custom_call" | custom-call | tf_op jit(solution)/shard_map/pallas_call | solution.py:136
  32.1 1.6 %shard_map.73.refs_3_.refs_6_.refs_5_ = f32[256,1152]{1,0:T(8,128)S(1)} custom-call(f32[1]{0:T(128)S(6)} %copy.7.refs_0_, f32[1]{0:T(128)S(6)} %copy.8.refs_1_, bf16[256,1152]{1,0:T(8,128)(2,1)S(1)} %collective-permute-done.3.refs_0_.refs_2_, bf16[256,1152]{1,0:T(8,128)(2,1)S(1)} %get-tuple-element.24.refs_3_, ...), custom_call_target="tpu_custom_call" | custom-call | flops 1207959552 | bytes 2359296 | tf_op jit(solution)/shard_map/pallas_call | solution.py:136
  33.7 3.2 %collective-permute-done.8.refs_0_.refs_2_ = bf16[256,1152]{1,0:T(8,128)(2,1)S(1)} collective-permute-done((bf16[256,1152]{1,0:T(8,128)(2,1)S(1)}, bf16[256,1152]{1,0:T(8,128)(2,1)S(1)}, u32[]{:S(2)}, u32[]{:S(2)}) %collective-permute-start.8) | collective-permute-done | bytes 589856 | tf_op jit(solution)/shard_map/ppermute | solution.py:50
  36.9 0.8 %collective-permute-done.10.refs_2_.refs_5_.refs_6_ = bf16[256,1152]{1,0:T(8,128)(2,1)S(1)} collective-permute-done((bf16[256,1152]{1,0:T(8,128)(2,1)S(1)}, bf16[256,1152]{1,0:T(8,128)(2,1)S(1)}, u32[]{:S(2)}, u32[]{:S(2)}) %collective-permute-start.10) | collective-permute-done | bytes 589856 | tf_op jit(solution)/shard_map/ppermute | solution.py:50
  37.7 0.1 shard_map.74
  37.8 0.5 collective-permute-start.11
  38.3 2.9 %shard_map.75 = (f32[256,1152]{1,0:T(8,128)S(1)}, f32[256,1152]{1,0:T(8,128)S(1)}) custom-call(f32[1]{0:T(128)S(6)} %copy.7.refs_0_, f32[1]{0:T(128)S(6)} %copy.8.refs_1_, bf16[256,1152]{1,0:T(8,128)(2,1)S(1)} %collective-permute-done.8.refs_0_.refs_2_, bf16[256,1152]{1,0:T(8,128)(2,1)S(1)} %get-tuple-element.24.refs_3_, ...), custom_call_target="tpu_custom_call" | custom-call | flops 2415919104 | bytes 4718592 | tf_op jit(solution)/shard_map/pallas_call | solution.py:136
  41.2 0.6 collective-permute-done.11.refs_4_.refs_6_
  41.8 1.6 %shard_map.76.refs_8_ = bf16[256,1152]{1,0:T(8,128)(2,1)S(1)} custom-call(f32[1]{0:T(128)S(6)} %copy.7.refs_0_, f32[1]{0:T(128)S(6)} %copy.8.refs_1_, bf16[256,1152]{1,0:T(8,128)(2,1)S(1)} %collective-permute-done.3.refs_0_.refs_2_, bf16[256,1152]{1,0:T(8,128)(2,1)S(1)} %collective-permute-done.7.refs_4_.refs_3_.refs_5_, ...), custom_call_target="tpu_custom_call" | custom-call | flops 1207959552 | bytes 2359296 | tf_op jit(solution)/shard_map/pallas_call | solution.py:136
  43.3 0.4 collective-permute-start.12
  43.7 2.9 %shard_map.77 = (bf16[256,1152]{1,0:T(8,128)(2,1)S(1)}, bf16[256,1152]{1,0:T(8,128)(2,1)S(1)}) custom-call(f32[1]{0:T(128)S(6)} %copy.7.refs_0_, f32[1]{0:T(128)S(6)} %copy.8.refs_1_, bf16[256,1152]{1,0:T(8,128)(2,1)S(1)} %collective-permute-done.8.refs_0_.refs_2_, bf16[256,1152]{1,0:T(8,128)(2,1)S(1)} %collective-permute-done.7.refs_4_.refs_3_.refs_5_, ...), custom_call_target="tpu_custom_call" | custom-call | flops 2415919104 | bytes 4718592 | tf_op jit(solution)/shard_map/pallas_call | solution.py:136
  46.7 2.8 %collective-permute-start.14 = (bf16[256,1152]{1,0:T(8,128)(2,1)S(1)}, bf16[256,1152]{1,0:T(8,128)(2,1)S(1)}, u32[]{:S(2)}, u32[]{:S(2)}) collective-permute-start(bf16[256,1152]{1,0:T(8,128)(2,1)S(1)} %get-tuple-element.31.refs_7_), channel_id=1, source_target_pairs={{0,64},{32,97},{2,66},{34,99},{4,68},{36,101},{6,70},{38,103},{64,... | collective-permute-start | bytes 1769480 | tf_op jit(solution)/shard_map/ppermute | solution.py:50
  49.5 1.1 %collective-permute-start.15 = (bf16[256,1152]{1,0:T(8,128)(2,1)S(1)}, bf16[256,1152]{1,0:T(8,128)(2,1)S(1)}, u32[]{:S(2)}, u32[]{:S(2)}) collective-permute-start(bf16[256,1152]{1,0:T(8,128)(2,1)S(1)} %get-tuple-element.35), channel_id=1, source_target_pairs={{0,8},{32,34},{2,10},{34,32},{4,12},{36,38},{6,14},{38,36},{64,72}... | collective-permute-start | bytes 1769480 | tf_op jit(solution)/shard_map/ppermute | solution.py:50
  50.6 2.9 %shard_map.78.refs_0_ = f32[256,1152]{1,0:T(8,128)S(1)} custom-call(f32[1]{0:T(128)S(6)} %copy.7.refs_0_, f32[1]{0:T(128)S(6)} %copy.8.refs_1_, bf16[256,1152]{1,0:T(8,128)(2,1)S(1)} %collective-permute-done.9.refs_1_.refs_2_, bf16[256,1152]{1,0:T(8,128)(2,1)S(1)} %get-tuple-element.24.refs_3_, bf16[768,1152]{1,0:T(8,128)(2,1)S(1)} %collective-permute-done.6.refs_4_, ...), custom_call_target="tpu_custom_call" | custom-call | flops 2415919104 | bytes 2359296 | tf_op jit(solution)/shard_map/pallas_call | solution.py:136
  53.5 0.1 shard_map.79.refs_10_
  53.6 2.1 %collective-permute-start.13 = (bf16[256,1152]{1,0:T(8,128)(2,1)S(1)}, bf16[256,1152]{1,0:T(8,128)(2,1)S(1)}, u32[]{:S(2)}, u32[]{:S(2)}) collective-permute-start(bf16[256,1152]{1,0:T(8,128)(2,1)S(1)} %shard_map.79.refs_10_), channel_id=1, source_target_pairs={{0,6},{32,56},{2,4},{34,58},{4,2},{36,60},{6,0},{38,62},{64,70},{9... | collective-permute-start | bytes 1769480 | tf_op jit(solution)/shard_map/ppermute | solution.py:50
  55.8 4.3 %shard_map.80 = (f32[256,1152]{1,0:T(8,128)S(1)}, f32[256,1152]{1,0:T(8,128)S(1)}, f32[256,1152]{1,0:T(8,128)S(1)}) custom-call(f32[1]{0:T(128)S(6)} %copy.7.refs_0_, f32[1]{0:T(128)S(6)} %copy.8.refs_1_, bf16[256,1152]{1,0:T(8,128)(2,1)S(1)} %collective-permute-done.4.refs_2_.refs_5_, bf16[256,1152]{1,0:T(8,128)(2,1)S(1)} %collective-permute-done.7.refs_4_.refs_3_.refs_5_, ...), custom_call_target="tpu_custom_call" | custom-call | flops 3623878656 | bytes 7077888 | tf_op jit(solution)/shard_map/pallas_call | solution.py:136
  60.1 0.1 shard_map.81.refs_3_
  60.2 0.4 collective-permute-start.16
  60.6 0.1 shard_map.82.refs_4_
  60.7 0.9 %collective-permute-start.17 = (bf16[256,1152]{1,0:T(8,128)(2,1)S(1)}, bf16[256,1152]{1,0:T(8,128)(2,1)S(1)}, u32[]{:S(2)}, u32[]{:S(2)}) collective-permute-start(bf16[256,1152]{1,0:T(8,128)(2,1)S(1)} %shard_map.82.refs_4_), channel_id=1, source_target_pairs={{0,6},{32,56},{2,4},{34,58},{4,2},{36,60},{6,0},{38,62},{64,70},{9... | collective-permute-start | bytes 1769480 | tf_op jit(solution)/shard_map/ppermute | solution.py:50
  61.6 2.5 %collective-permute-done.13.refs_2_ = bf16[256,1152]{1,0:T(8,128)(2,1)S(1)} collective-permute-done((bf16[256,1152]{1,0:T(8,128)(2,1)S(1)}, bf16[256,1152]{1,0:T(8,128)(2,1)S(1)}, u32[]{:S(2)}, u32[]{:S(2)}) %collective-permute-start.13) | collective-permute-done | bytes 589856 | tf_op jit(solution)/shard_map/ppermute | solution.py:50
  64.2 0.1 shard_map.83
  64.3 3.4 %collective-permute-start.18 = (bf16[128,1152]{1,0:T(8,128)(2,1)S(1)}, bf16[128,1152]{1,0:T(8,128)(2,1)S(1)}, u32[]{:S(2)}, u32[]{:S(2)}) collective-permute-start(bf16[128,1152]{1,0:T(8,128)(2,1)S(1)} %get-tuple-element.37), channel_id=1, source_target_pairs={{0,96},{32,65},{2,98},{34,67},{4,100},{36,69},{6,102},{38,71},{64,... | collective-permute-start | bytes 884744 | tf_op jit(solution)/shard_map/ppermute | solution.py:50
  67.7 1.6 %shard_map.84.refs_1_ = f32[256,1152]{1,0:T(8,128)S(1)} custom-call(f32[1]{0:T(128)S(6)} %copy.7.refs_0_, f32[1]{0:T(128)S(6)} %copy.8.refs_1_, bf16[256,1152]{1,0:T(8,128)(2,1)S(1)} %get-tuple-element.23.refs_2_, bf16[256,1152]{1,0:T(8,128)(2,1)S(1)} %collective-permute-done.7.refs_4_.refs_3_.refs_5_, ...), custom_call_target="tpu_custom_call" | custom-call | flops 1207959552 | bytes 2359296 | tf_op jit(solution)/shard_map/pallas_call | solution.py:136
  69.3 1.7 %collective-permute-done.17.refs_3_ = bf16[256,1152]{1,0:T(8,128)(2,1)S(1)} collective-permute-done((bf16[256,1152]{1,0:T(8,128)(2,1)S(1)}, bf16[256,1152]{1,0:T(8,128)(2,1)S(1)}, u32[]{:S(2)}, u32[]{:S(2)}) %collective-permute-start.17) | collective-permute-done | bytes 589856 | tf_op jit(solution)/shard_map/ppermute | solution.py:50
  71.0 0.4 collective-permute-done.18.refs_4_.refs_5_
  71.4 0.2 shard_map.85
  71.6 1.2 %collective-permute-start.19 = (bf16[128,1152]{1,0:T(8,128)(2,1)S(1)}, bf16[128,1152]{1,0:T(8,128)(2,1)S(1)}, u32[]{:S(2)}, u32[]{:S(2)}) collective-permute-start(bf16[128,1152]{1,0:T(8,128)(2,1)S(1)} %get-tuple-element.39), channel_id=1, source_target_pairs={{0,32},{32,0},{1,33},{33,1},{2,34},{34,2},{3,35},{35,3},{4,36},{36... | collective-permute-start | bytes 884744 | tf_op jit(solution)/shard_map/ppermute | solution.py:54
  73.4 1.5 %collective-permute-done.20.refs_4_ = bf16[128,1152]{1,0:T(8,128)(2,1)S(1)} collective-permute-done((bf16[128,1152]{1,0:T(8,128)(2,1)S(1)}, bf16[128,1152]{1,0:T(8,128)(2,1)S(1)}, u32[]{:S(2)}, u32[]{:S(2)}) %collective-permute-start.20) | collective-permute-done | bytes 294944 | tf_op jit(solution)/shard_map/ppermute | solution.py:50
  75.0 1.6 %shard_map.86 = (f32[128,1152]{1,0:T(8,128)}, f32[128,1152]{1,0:T(8,128)}) custom-call(f32[1]{0:T(128)} %bitcast.refs_0_.is_first, f32[1]{0:T(128)S(6)} %div.3.multiplier, bf16[128,1152]{1,0:T(8,128)(2,1)S(1)} %copy-done, bf16[128,1152]{1,0:T(8,128)(2,1)S(1)} %copy-done.1, f32[128,1152]{1,0:T(8,128)S(1)} %get-tuple-element.38.refs_2_, ...), custom_call_target="tpu_custom_call" | custom-call | tf_op jit(solution)/shard_map/pallas_call | solution.py:275
  (18 shorter events, 0.3 us)
Async XLA Ops:
  0.6 2.9 %collective-permute-start = (bf16[128,1152]{1,0:T(8,128)(2,1)}, bf16[128,1152]{1,0:T(8,128)(2,1)S(1)}, u32[]{:S(2)}, u32[]{:S(2)}) collective-permute-start(bf16[128,1152]{1,0:T(8,128)(2,1)} %refs_0_.10), channel_id=1, source_target_pairs={{0,32},{32,0},{1,33},{33,1},{2,34},{34,2},{3,35},{35,3},{4,36},{36... | collective-permute-start | bytes 884744 | tf_op jit(solution)/shard_map/ppermute | solution.py:54
  2.1 1.8 %collective-permute-start.1 = (bf16[128,1152]{1,0:T(8,128)(2,1)}, bf16[128,1152]{1,0:T(8,128)(2,1)S(1)}, u32[]{:S(2)}, u32[]{:S(2)}) collective-permute-start(bf16[128,1152]{1,0:T(8,128)(2,1)} %refs_1_.10), channel_id=1, source_target_pairs={{0,32},{32,0},{1,33},{33,1},{2,34},{34,2},{3,35},{35,3},{4,36},{36... | collective-permute-start | bytes 884744 | tf_op jit(solution)/shard_map/ppermute | solution.py:54
  4.3 10.3 %collective-permute-start.2 = (bf16[256,1152]{1,0:T(8,128)(2,1)S(1)}, bf16[256,1152]{1,0:T(8,128)(2,1)S(1)}, u32[]{:S(2)}, u32[]{:S(2)}) collective-permute-start(bf16[256,1152]{1,0:T(8,128)(2,1)S(1)} %get-tuple-element.23.refs_2_), channel_id=1, source_target_pairs={{0,6},{32,56},{2,4},{34,58},{4,2},{36,60},{6,0},{38,62},{64,70},{9... | collective-permute-start | bytes 1769480 | tf_op jit(solution)/shard_map/ppermute | solution.py:50
  7.0 9.2 %collective-permute-start.4 = (bf16[256,1152]{1,0:T(8,128)(2,1)S(1)}, bf16[256,1152]{1,0:T(8,128)(2,1)S(1)}, u32[]{:S(2)}, u32[]{:S(2)}) collective-permute-start(bf16[256,1152]{1,0:T(8,128)(2,1)S(1)} %get-tuple-element.23.refs_2_), channel_id=1, source_target_pairs={{0,8},{32,34},{2,10},{34,32},{4,12},{36,38},{6,14},{38,36},{64,72}... | collective-permute-start | bytes 1769480 | tf_op jit(solution)/shard_map/ppermute | solution.py:50
  8.6 10.0 %collective-permute-start.5 = (bf16[256,1152]{1,0:T(8,128)(2,1)S(1)}, bf16[256,1152]{1,0:T(8,128)(2,1)S(1)}, u32[]{:S(2)}, u32[]{:S(2)}) collective-permute-start(bf16[256,1152]{1,0:T(8,128)(2,1)S(1)} %get-tuple-element.23.refs_2_), channel_id=1, source_target_pairs={{0,64},{32,97},{2,66},{34,99},{4,68},{36,101},{6,70},{38,103},{64,... | collective-permute-start | bytes 1769480 | tf_op jit(solution)/shard_map/ppermute | solution.py:50
  18.8 7.5 %collective-permute-start.6 = (bf16[768,1152]{1,0:T(8,128)(2,1)S(1)}, bf16[768,1152]{1,0:T(8,128)(2,1)S(1)}, u32[]{:S(2)}, u32[]{:S(2)}) collective-permute-start(bf16[768,1152]{1,0:T(8,128)(2,1)S(1)} %shard_map.70), channel_id=1, source_target_pairs={{0,32},{32,0},{1,33},{33,1},{2,34},{34,2},{3,35},{35,3},{4,36},{36... | collective-permute-start | bytes 5308424 | tf_op jit(solution)/shard_map/ppermute | solution.py:54
  20.5 11.4 %collective-permute-start.3 = (bf16[256,1152]{1,0:T(8,128)(2,1)S(1)}, bf16[256,1152]{1,0:T(8,128)(2,1)S(1)}, u32[]{:S(2)}, u32[]{:S(2)}) collective-permute-start(bf16[256,1152]{1,0:T(8,128)(2,1)S(1)} %collective-permute-done.2.refs_4_.refs_7_.refs_8_), channel_id=1, source_target_pairs={{0,72},{32,99},{2,74},{34,97},{4,76},{36,103},{6,78},{38,101},{64,... | collective-permute-start | bytes 1769480 | tf_op jit(solution)/shard_map/ppermute | solution.py:50
  22.5 14.4 %collective-permute-start.8 = (bf16[256,1152]{1,0:T(8,128)(2,1)S(1)}, bf16[256,1152]{1,0:T(8,128)(2,1)S(1)}, u32[]{:S(2)}, u32[]{:S(2)}) collective-permute-start(bf16[256,1152]{1,0:T(8,128)(2,1)S(1)} %collective-permute-done.4.refs_2_.refs_5_), channel_id=1, source_target_pairs={{0,64},{32,97},{2,66},{34,99},{4,68},{36,101},{6,70},{38,103},{64,... | collective-permute-start | bytes 1769480 | tf_op jit(solution)/shard_map/ppermute | solution.py:50
  23.2 13.6 %collective-permute-start.9 = (bf16[256,1152]{1,0:T(8,128)(2,1)S(1)}, bf16[256,1152]{1,0:T(8,128)(2,1)S(1)}, u32[]{:S(2)}, u32[]{:S(2)}) collective-permute-start(bf16[256,1152]{1,0:T(8,128)(2,1)S(1)} %collective-permute-done.5.refs_3_.refs_6_), channel_id=1, source_target_pairs={{0,6},{32,56},{2,4},{34,58},{4,2},{36,60},{6,0},{38,62},{64,70},{9... | collective-permute-start | bytes 1769480 | tf_op jit(solution)/shard_map/ppermute | solution.py:50
  25.1 12.6 %collective-permute-start.10 = (bf16[256,1152]{1,0:T(8,128)(2,1)S(1)}, bf16[256,1152]{1,0:T(8,128)(2,1)S(1)}, u32[]{:S(2)}, u32[]{:S(2)}) collective-permute-start(bf16[256,1152]{1,0:T(8,128)(2,1)S(1)} %collective-permute-done.2.refs_4_.refs_7_.refs_8_), channel_id=1, source_target_pairs={{0,8},{32,34},{2,10},{34,32},{4,12},{36,38},{6,14},{38,36},{64,72}... | collective-permute-start | bytes 1769480 | tf_op jit(solution)/shard_map/ppermute | solution.py:50
  32.0 5.7 %collective-permute-start.7 = (bf16[256,1152]{1,0:T(8,128)(2,1)S(1)}, bf16[256,1152]{1,0:T(8,128)(2,1)S(1)}, u32[]{:S(2)}, u32[]{:S(2)}) collective-permute-start(bf16[256,1152]{1,0:T(8,128)(2,1)S(1)} %shard_map.72), channel_id=1, source_target_pairs={{0,32},{32,0},{1,33},{33,1},{2,34},{34,2},{3,35},{35,3},{4,36},{36... | collective-permute-start | bytes 1769480 | tf_op jit(solution)/shard_map/ppermute | solution.py:54
  37.8 4.0 %collective-permute-start.11 = (bf16[768,1152]{1,0:T(8,128)(2,1)S(1)}, bf16[768,1152]{1,0:T(8,128)(2,1)S(1)}, u32[]{:S(2)}, u32[]{:S(2)}) collective-permute-start(bf16[768,1152]{1,0:T(8,128)(2,1)S(1)} %shard_map.74), channel_id=1, source_target_pairs={{0,32},{32,0},{1,33},{33,1},{2,34},{34,2},{3,35},{35,3},{4,36},{36... | collective-permute-start | bytes 5308424 | tf_op jit(solution)/shard_map/ppermute | solution.py:54
  43.3 10.2 %collective-permute-start.12 = (bf16[256,1152]{1,0:T(8,128)(2,1)S(1)}, bf16[256,1152]{1,0:T(8,128)(2,1)S(1)}, u32[]{:S(2)}, u32[]{:S(2)}) collective-permute-start(bf16[256,1152]{1,0:T(8,128)(2,1)S(1)} %shard_map.76.refs_8_), channel_id=1, source_target_pairs={{0,8},{32,34},{2,10},{34,32},{4,12},{36,38},{6,14},{38,36},{64,72}... | collective-permute-start | bytes 1769480 | tf_op jit(solution)/shard_map/ppermute | solution.py:50
  46.7 13.4 %collective-permute-start.14 = (bf16[256,1152]{1,0:T(8,128)(2,1)S(1)}, bf16[256,1152]{1,0:T(8,128)(2,1)S(1)}, u32[]{:S(2)}, u32[]{:S(2)}) collective-permute-start(bf16[256,1152]{1,0:T(8,128)(2,1)S(1)} %get-tuple-element.31.refs_7_), channel_id=1, source_target_pairs={{0,64},{32,97},{2,66},{34,99},{4,68},{36,101},{6,70},{38,103},{64,... | collective-permute-start | bytes 1769480 | tf_op jit(solution)/shard_map/ppermute | solution.py:50
  49.5 11.1 %collective-permute-start.15 = (bf16[256,1152]{1,0:T(8,128)(2,1)S(1)}, bf16[256,1152]{1,0:T(8,128)(2,1)S(1)}, u32[]{:S(2)}, u32[]{:S(2)}) collective-permute-start(bf16[256,1152]{1,0:T(8,128)(2,1)S(1)} %get-tuple-element.35), channel_id=1, source_target_pairs={{0,8},{32,34},{2,10},{34,32},{4,12},{36,38},{6,14},{38,36},{64,72}... | collective-permute-start | bytes 1769480 | tf_op jit(solution)/shard_map/ppermute | solution.py:50
  53.6 10.5 %collective-permute-start.13 = (bf16[256,1152]{1,0:T(8,128)(2,1)S(1)}, bf16[256,1152]{1,0:T(8,128)(2,1)S(1)}, u32[]{:S(2)}, u32[]{:S(2)}) collective-permute-start(bf16[256,1152]{1,0:T(8,128)(2,1)S(1)} %shard_map.79.refs_10_), channel_id=1, source_target_pairs={{0,6},{32,56},{2,4},{34,58},{4,2},{36,60},{6,0},{38,62},{64,70},{9... | collective-permute-start | bytes 1769480 | tf_op jit(solution)/shard_map/ppermute | solution.py:50
  60.2 9.2 %collective-permute-start.16 = (bf16[256,1152]{1,0:T(8,128)(2,1)S(1)}, bf16[256,1152]{1,0:T(8,128)(2,1)S(1)}, u32[]{:S(2)}, u32[]{:S(2)}) collective-permute-start(bf16[256,1152]{1,0:T(8,128)(2,1)S(1)} %shard_map.81.refs_3_), channel_id=1, source_target_pairs={{0,8},{32,34},{2,10},{34,32},{4,12},{36,38},{6,14},{38,36},{64,72}... | collective-permute-start | bytes 1769480 | tf_op jit(solution)/shard_map/ppermute | solution.py:50
  60.7 10.3 %collective-permute-start.17 = (bf16[256,1152]{1,0:T(8,128)(2,1)S(1)}, bf16[256,1152]{1,0:T(8,128)(2,1)S(1)}, u32[]{:S(2)}, u32[]{:S(2)}) collective-permute-start(bf16[256,1152]{1,0:T(8,128)(2,1)S(1)} %shard_map.82.refs_4_), channel_id=1, source_target_pairs={{0,6},{32,56},{2,4},{34,58},{4,2},{36,60},{6,0},{38,62},{64,70},{9... | collective-permute-start | bytes 1769480 | tf_op jit(solution)/shard_map/ppermute | solution.py:50
  64.3 7.1 %collective-permute-start.18 = (bf16[128,1152]{1,0:T(8,128)(2,1)S(1)}, bf16[128,1152]{1,0:T(8,128)(2,1)S(1)}, u32[]{:S(2)}, u32[]{:S(2)}) collective-permute-start(bf16[128,1152]{1,0:T(8,128)(2,1)S(1)} %get-tuple-element.37), channel_id=1, source_target_pairs={{0,96},{32,65},{2,98},{34,67},{4,100},{36,69},{6,102},{38,71},{64,... | collective-permute-start | bytes 884744 | tf_op jit(solution)/shard_map/ppermute | solution.py:50
  67.7 7.3 %collective-permute-start.20 = (bf16[128,1152]{1,0:T(8,128)(2,1)S(1)}, bf16[128,1152]{1,0:T(8,128)(2,1)S(1)}, u32[]{:S(2)}, u32[]{:S(2)}) collective-permute-start(bf16[128,1152]{1,0:T(8,128)(2,1)S(1)} %get-tuple-element.36.refs_6_), channel_id=1, source_target_pairs={{0,64},{32,97},{2,66},{34,99},{4,68},{36,101},{6,70},{38,103},{64,... | collective-permute-start | bytes 884744 | tf_op jit(solution)/shard_map/ppermute | solution.py:50
  69.3 5.7 %copy-start = (bf16[128,1152]{1,0:T(8,128)(2,1)S(1)}, bf16[128,1152]{1,0:T(8,128)(2,1)}, u32[]{:S(2)}) copy-start(bf16[128,1152]{1,0:T(8,128)(2,1)} %refs_0_.10) | copy-start | bytes 884740
  69.3 5.7 %copy-start.1 = (bf16[128,1152]{1,0:T(8,128)(2,1)S(1)}, bf16[128,1152]{1,0:T(8,128)(2,1)}, u32[]{:S(2)}) copy-start(bf16[128,1152]{1,0:T(8,128)(2,1)} %refs_1_.10) | copy-start | bytes 884740
  71.6 3.4 %collective-permute-start.19 = (bf16[128,1152]{1,0:T(8,128)(2,1)S(1)}, bf16[128,1152]{1,0:T(8,128)(2,1)S(1)}, u32[]{:S(2)}, u32[]{:S(2)}) collective-permute-start(bf16[128,1152]{1,0:T(8,128)(2,1)S(1)} %get-tuple-element.39), channel_id=1, source_target_pairs={{0,32},{32,0},{1,33},{33,1},{2,34},{34,2},{3,35},{35,3},{4,36},{36... | collective-permute-start | bytes 884744 | tf_op jit(solution)/shard_map/ppermute | solution.py:54

commit v20 on v19

--- a/solution.py
+++ b/solution.py
@@ -23,7 +23,7 @@
 ANY = pl.BlockSpec(memory_space=pl.ANY)
 PARAMS = pltpu.CompilerParams(vmem_limit_bytes=VMEM_BYTES)
 
-NAMES = ({"x": "x", "y": "y", "z": "z"}, {"x": "z", "y": "y", "z": "x"})
+NAMES = ({"x": "x", "y": "y", "z": "z"}, {"x": "x", "y": "z", "z": "y"})
 ONE = ("x", "y", "z")
 TWO = ("xy", "yz", "zx")
 

time: 76.9 us -> 76.4 us (level)
    ppermute x6, starting transfers between devices: 5.09 us -> 3.93 us  [other_core(): return lax.ppermute(value, 'core', [(0, 1), (1, 0)])]
  transfers between devices with their start and end apart: 21 -> 21, of which waited for: 11 -> 12; matrix products, arithmetic and copies ran while one was open for 1% -> 1% of each run, Pallas kernels for 30% -> 30%
where the time goes in v20:
time: 76.4 us; the launch traced here: 76.2 us
  starting transfers between devices  28.4 us (37%)
  Pallas kernels  26.5 us (35%)
  waiting for transfers between devices  17.3 us (23%)
  between operations  2.92 us (4%)
  other arithmetic  1.1 us (1%)
    ppermute x15, starting transfers between devices, sent(): return lax.ppermute(value, FINE_AXES, pairs)  24.5 us
    pallas_call x8, Pallas kernels, sums_of(): pl.pallas_call(functools.partial(sums_kernel, plan, len(inputs), len(afte...  23.4 us
    ppermute x15, waiting for transfers between devices, sent(): return lax.ppermute(value, FINE_AXES, pairs)  15.8 us
    ppermute x6, starting transfers between devices, other_core(): return lax.ppermute(value, 'core', [(0, 1), (1, 0)])  3.93 us
    pallas_call x1, Pallas kernels, on_device(): pl.pallas_call(finish_kernel, out_shape=[jax.ShapeDtypeStruct(*shard_full...  1.57 us
  transfers between devices with their start and end apart: 21, of which 12 were waited for; matrix products, arithmetic and copies ran while one was open for 1% of the time, Pallas kernels for 30%

profile of v20, /device:TPU:1, one launch (start us, length us, event | category | flops | bytes accessed | tf_op | source)
XLA Modules:
  0.0 76.2 jit_solution(3529671832123118647)
XLA Ops:
  0.6 1.5 %collective-permute-start = (bf16[128,1152]{1,0:T(8,128)(2,1)}, bf16[128,1152]{1,0:T(8,128)(2,1)S(1)}, u32[]{:S(2)}, u32[]{:S(2)}) collective-permute-start(bf16[128,1152]{1,0:T(8,128)(2,1)} %refs_0_.10), channel_id=1, source_target_pairs={{0,32},{32,0},{1,33},{33,1},{2,34},{34,2},{3,35},{35,3},{4,36},{36... | collective-permute-start | bytes 884744 | tf_op jit(solution)/shard_map/ppermute | solution.py:54
  2.2 1.1 %pad_maximum_fusion.refs_0_ = bf16[256,1152]{1,0:T(8,128)(2,1)S(1)} fusion(bf16[128,1152]{1,0:T(8,128)(2,1)} %refs_1_.10, bf16[128,1152]{1,0:T(8,128)(2,1)} %refs_0_.10), kind=kLoop, calls=%fused_computation | loop fusion | flops 1179648 | bytes 1179648 | tf_op jit(solution)/shard_map/concatenate | solution.py:188
  3.3 0.2 shard_map.68
  3.5 0.4 collective-permute-done.1.refs_2_
  4.0 0.4 shard_map.69
  4.3 2.9 %collective-permute-start.2 = (bf16[256,1152]{1,0:T(8,128)(2,1)S(1)}, bf16[256,1152]{1,0:T(8,128)(2,1)S(1)}, u32[]{:S(2)}, u32[]{:S(2)}) collective-permute-start(bf16[256,1152]{1,0:T(8,128)(2,1)S(1)} %get-tuple-element.23.refs_2_), channel_id=1, source_target_pairs={{0,6},{32,97},{2,4},{34,99},{4,2},{36,101},{6,0},{38,103},{64,70},... | collective-permute-start | bytes 1769480 | tf_op jit(solution)/shard_map/ppermute | solution.py:50
  7.2 2.5 %collective-permute-start.4 = (bf16[256,1152]{1,0:T(8,128)(2,1)S(1)}, bf16[256,1152]{1,0:T(8,128)(2,1)S(1)}, u32[]{:S(2)}, u32[]{:S(2)}) collective-permute-start(bf16[256,1152]{1,0:T(8,128)(2,1)S(1)} %get-tuple-element.23.refs_2_), channel_id=1, source_target_pairs={{0,8},{32,56},{2,10},{34,58},{4,12},{36,60},{6,14},{38,62},{64,72}... | collective-permute-start | bytes 1769480 | tf_op jit(solution)/shard_map/ppermute | solution.py:50
  9.7 1.6 %collective-permute-start.5 = (bf16[256,1152]{1,0:T(8,128)(2,1)S(1)}, bf16[256,1152]{1,0:T(8,128)(2,1)S(1)}, u32[]{:S(2)}, u32[]{:S(2)}) collective-permute-start(bf16[256,1152]{1,0:T(8,128)(2,1)S(1)} %get-tuple-element.23.refs_2_), channel_id=1, source_target_pairs={{0,64},{32,34},{2,66},{34,32},{4,68},{36,38},{6,70},{38,36},{64,0}... | collective-permute-start | bytes 1769480 | tf_op jit(solution)/shard_map/ppermute | solution.py:50
  12.7 2.2 %collective-permute-done.2.refs_4_.refs_7_.refs_8_ = bf16[256,1152]{1,0:T(8,128)(2,1)S(1)} collective-permute-done((bf16[256,1152]{1,0:T(8,128)(2,1)S(1)}, bf16[256,1152]{1,0:T(8,128)(2,1)S(1)}, u32[]{:S(2)}, u32[]{:S(2)}) %collective-permute-start.2) | collective-permute-done | bytes 589856 | tf_op jit(solution)/shard_map/ppermute | solution.py:50
  14.8 2.4 %collective-permute-done.4.refs_2_.refs_5_ = bf16[256,1152]{1,0:T(8,128)(2,1)S(1)} collective-permute-done((bf16[256,1152]{1,0:T(8,128)(2,1)S(1)}, bf16[256,1152]{1,0:T(8,128)(2,1)S(1)}, u32[]{:S(2)}, u32[]{:S(2)}) %collective-permute-start.4) | collective-permute-done | bytes 589856 | tf_op jit(solution)/shard_map/ppermute | solution.py:50
  17.2 1.7 %collective-permute-done.5.refs_3_.refs_6_ = bf16[256,1152]{1,0:T(8,128)(2,1)S(1)} collective-permute-done((bf16[256,1152]{1,0:T(8,128)(2,1)S(1)}, bf16[256,1152]{1,0:T(8,128)(2,1)S(1)}, u32[]{:S(2)}, u32[]{:S(2)}) %collective-permute-start.5) | collective-permute-done | bytes 589856 | tf_op jit(solution)/shard_map/ppermute | solution.py:50
  18.9 0.1 shard_map.70
  19.1 1.4 %collective-permute-start.6 = (bf16[768,1152]{1,0:T(8,128)(2,1)S(1)}, bf16[768,1152]{1,0:T(8,128)(2,1)S(1)}, u32[]{:S(2)}, u32[]{:S(2)}) collective-permute-start(bf16[768,1152]{1,0:T(8,128)(2,1)S(1)} %shard_map.70), channel_id=1, source_target_pairs={{0,32},{32,0},{1,33},{33,1},{2,34},{34,2},{3,35},{35,3},{4,36},{36... | collective-permute-start | bytes 5308424 | tf_op jit(solution)/shard_map/ppermute | solution.py:54
  20.5 1.1 %collective-permute-start.3 = (bf16[256,1152]{1,0:T(8,128)(2,1)S(1)}, bf16[256,1152]{1,0:T(8,128)(2,1)S(1)}, u32[]{:S(2)}, u32[]{:S(2)}) collective-permute-start(bf16[256,1152]{1,0:T(8,128)(2,1)S(1)} %collective-permute-done.2.refs_4_.refs_7_.refs_8_), channel_id=1, source_target_pairs={{0,72},{32,58},{2,74},{34,56},{4,76},{36,62},{6,78},{38,60},{64,8}... | collective-permute-start | bytes 1769480 | tf_op jit(solution)/shard_map/ppermute | solution.py:50
  21.6 1.9 %collective-permute-start.8 = (bf16[256,1152]{1,0:T(8,128)(2,1)S(1)}, bf16[256,1152]{1,0:T(8,128)(2,1)S(1)}, u32[]{:S(2)}, u32[]{:S(2)}) collective-permute-start(bf16[256,1152]{1,0:T(8,128)(2,1)S(1)} %collective-permute-done.4.refs_2_.refs_5_), channel_id=1, source_target_pairs={{0,64},{32,34},{2,66},{34,32},{4,68},{36,38},{6,70},{38,36},{64,0}... | collective-permute-start | bytes 1769480 | tf_op jit(solution)/shard_map/ppermute | solution.py:50
  23.5 2.7 %collective-permute-start.9 = (bf16[256,1152]{1,0:T(8,128)(2,1)S(1)}, bf16[256,1152]{1,0:T(8,128)(2,1)S(1)}, u32[]{:S(2)}, u32[]{:S(2)}) collective-permute-start(bf16[256,1152]{1,0:T(8,128)(2,1)S(1)} %collective-permute-done.5.refs_3_.refs_6_), channel_id=1, source_target_pairs={{0,6},{32,97},{2,4},{34,99},{4,2},{36,101},{6,0},{38,103},{64,70},... | collective-permute-start | bytes 1769480 | tf_op jit(solution)/shard_map/ppermute | solution.py:50
  26.2 0.9 %collective-permute-start.10 = (bf16[256,1152]{1,0:T(8,128)(2,1)S(1)}, bf16[256,1152]{1,0:T(8,128)(2,1)S(1)}, u32[]{:S(2)}, u32[]{:S(2)}) collective-permute-start(bf16[256,1152]{1,0:T(8,128)(2,1)S(1)} %collective-permute-done.2.refs_4_.refs_7_.refs_8_), channel_id=1, source_target_pairs={{0,8},{32,56},{2,10},{34,58},{4,12},{36,60},{6,14},{38,62},{64,72}... | collective-permute-start | bytes 1769480 | tf_op jit(solution)/shard_map/ppermute | solution.py:50
  27.1 5.7 %shard_map.71 = (f32[256,1152]{1,0:T(8,128)S(1)}, f32[256,1152]{1,0:T(8,128)S(1)}, f32[256,1152]{1,0:T(8,128)S(1)}, f32[256,1152]{1,0:T(8,128)S(1)}) custom-call(f32[1]{0:T(128)S(6)} %copy.7.refs_0_, f32[1]{0:T(128)S(6)} %copy.8.refs_1_, bf16[256,1152]{1,0:T(8,128)(2,1)S(1)} %get-tuple-element.23.refs_2_, bf16[256,1152]{1,0:T(8,128)(2,1)S(1)} %get-tuple-element.24.refs_3_, ...), custom_call_target="tpu_custom_call" | custom-call | tf_op jit(solution)/shard_map/pallas_call | solution.py:136
  33.0 1.6 %shard_map.73.refs_3_.refs_6_.refs_5_ = f32[256,1152]{1,0:T(8,128)S(1)} custom-call(f32[1]{0:T(128)S(6)} %copy.7.refs_0_, f32[1]{0:T(128)S(6)} %copy.8.refs_1_, bf16[256,1152]{1,0:T(8,128)(2,1)S(1)} %collective-permute-done.3.refs_0_.refs_2_, bf16[256,1152]{1,0:T(8,128)(2,1)S(1)} %get-tuple-element.24.refs_3_, ...), custom_call_target="tpu_custom_call" | custom-call | flops 1207959552 | bytes 2359296 | tf_op jit(solution)/shard_map/pallas_call | solution.py:136
  34.5 2.8 %collective-permute-done.8.refs_0_.refs_2_ = bf16[256,1152]{1,0:T(8,128)(2,1)S(1)} collective-permute-done((bf16[256,1152]{1,0:T(8,128)(2,1)S(1)}, bf16[256,1152]{1,0:T(8,128)(2,1)S(1)}, u32[]{:S(2)}, u32[]{:S(2)}) %collective-permute-start.8) | collective-permute-done | bytes 589856 | tf_op jit(solution)/shard_map/ppermute | solution.py:50
  37.4 0.1 shard_map.74
  37.5 0.7 collective-permute-start.11
  38.3 2.9 %shard_map.75 = (f32[256,1152]{1,0:T(8,128)S(1)}, f32[256,1152]{1,0:T(8,128)S(1)}) custom-call(f32[1]{0:T(128)S(6)} %copy.7.refs_0_, f32[1]{0:T(128)S(6)} %copy.8.refs_1_, bf16[256,1152]{1,0:T(8,128)(2,1)S(1)} %collective-permute-done.8.refs_0_.refs_2_, bf16[256,1152]{1,0:T(8,128)(2,1)S(1)} %get-tuple-element.24.refs_3_, ...), custom_call_target="tpu_custom_call" | custom-call | flops 2415919104 | bytes 4718592 | tf_op jit(solution)/shard_map/pallas_call | solution.py:136
  41.2 0.4 collective-permute-done.11.refs_4_.refs_6_
  41.6 1.6 %shard_map.76.refs_8_ = bf16[256,1152]{1,0:T(8,128)(2,1)S(1)} custom-call(f32[1]{0:T(128)S(6)} %copy.7.refs_0_, f32[1]{0:T(128)S(6)} %copy.8.refs_1_, bf16[256,1152]{1,0:T(8,128)(2,1)S(1)} %collective-permute-done.3.refs_0_.refs_2_, bf16[256,1152]{1,0:T(8,128)(2,1)S(1)} %collective-permute-done.7.refs_4_.refs_3_.refs_5_, ...), custom_call_target="tpu_custom_call" | custom-call | flops 1207959552 | bytes 2359296 | tf_op jit(solution)/shard_map/pallas_call | solution.py:136
  43.1 1.9 %collective-permute-start.12 = (bf16[256,1152]{1,0:T(8,128)(2,1)S(1)}, bf16[256,1152]{1,0:T(8,128)(2,1)S(1)}, u32[]{:S(2)}, u32[]{:S(2)}) collective-permute-start(bf16[256,1152]{1,0:T(8,128)(2,1)S(1)} %shard_map.76.refs_8_), channel_id=1, source_target_pairs={{0,8},{32,56},{2,10},{34,58},{4,12},{36,60},{6,14},{38,62},{64,72}... | collective-permute-start | bytes 1769480 | tf_op jit(solution)/shard_map/ppermute | solution.py:50
  45.0 2.9 %shard_map.77 = (bf16[256,1152]{1,0:T(8,128)(2,1)S(1)}, bf16[256,1152]{1,0:T(8,128)(2,1)S(1)}) custom-call(f32[1]{0:T(128)S(6)} %copy.7.refs_0_, f32[1]{0:T(128)S(6)} %copy.8.refs_1_, bf16[256,1152]{1,0:T(8,128)(2,1)S(1)} %collective-permute-done.8.refs_0_.refs_2_, bf16[256,1152]{1,0:T(8,128)(2,1)S(1)} %collective-permute-done.7.refs_4_.refs_3_.refs_5_, ...), custom_call_target="tpu_custom_call" | custom-call | flops 2415919104 | bytes 4718592 | tf_op jit(solution)/shard_map/pallas_call | solution.py:136
  47.9 0.6 collective-permute-start.14
  48.5 0.9 %collective-permute-start.15 = (bf16[256,1152]{1,0:T(8,128)(2,1)S(1)}, bf16[256,1152]{1,0:T(8,128)(2,1)S(1)}, u32[]{:S(2)}, u32[]{:S(2)}) collective-permute-start(bf16[256,1152]{1,0:T(8,128)(2,1)S(1)} %get-tuple-element.35), channel_id=1, source_target_pairs={{0,8},{32,56},{2,10},{34,58},{4,12},{36,60},{6,14},{38,62},{64,72}... | collective-permute-start | bytes 1769480 | tf_op jit(solution)/shard_map/ppermute | solution.py:50
  49.4 2.9 %shard_map.78.refs_0_ = f32[256,1152]{1,0:T(8,128)S(1)} custom-call(f32[1]{0:T(128)S(6)} %copy.7.refs_0_, f32[1]{0:T(128)S(6)} %copy.8.refs_1_, bf16[256,1152]{1,0:T(8,128)(2,1)S(1)} %collective-permute-done.9.refs_1_.refs_2_, bf16[256,1152]{1,0:T(8,128)(2,1)S(1)} %get-tuple-element.24.refs_3_, bf16[768,1152]{1,0:T(8,128)(2,1)S(1)} %collective-permute-done.6.refs_4_, ...), custom_call_target="tpu_custom_call" | custom-call | flops 2415919104 | bytes 2359296 | tf_op jit(solution)/shard_map/pallas_call | solution.py:136
  52.3 0.8 %collective-permute-done.12.refs_1_ = bf16[256,1152]{1,0:T(8,128)(2,1)S(1)} collective-permute-done((bf16[256,1152]{1,0:T(8,128)(2,1)S(1)}, bf16[256,1152]{1,0:T(8,128)(2,1)S(1)}, u32[]{:S(2)}, u32[]{:S(2)}) %collective-permute-start.12) | collective-permute-done | bytes 589856 | tf_op jit(solution)/shard_map/ppermute | solution.py:50
  53.2 0.1 shard_map.79.refs_10_
  53.3 2.7 %collective-permute-start.13 = (bf16[256,1152]{1,0:T(8,128)(2,1)S(1)}, bf16[256,1152]{1,0:T(8,128)(2,1)S(1)}, u32[]{:S(2)}, u32[]{:S(2)}) collective-permute-start(bf16[256,1152]{1,0:T(8,128)(2,1)S(1)} %shard_map.79.refs_10_), channel_id=1, source_target_pairs={{0,6},{32,97},{2,4},{34,99},{4,2},{36,101},{6,0},{38,103},{64,70},... | collective-permute-start | bytes 1769480 | tf_op jit(solution)/shard_map/ppermute | solution.py:50
  56.0 4.3 %shard_map.80 = (f32[256,1152]{1,0:T(8,128)S(1)}, f32[256,1152]{1,0:T(8,128)S(1)}, f32[256,1152]{1,0:T(8,128)S(1)}) custom-call(f32[1]{0:T(128)S(6)} %copy.7.refs_0_, f32[1]{0:T(128)S(6)} %copy.8.refs_1_, bf16[256,1152]{1,0:T(8,128)(2,1)S(1)} %collective-permute-done.4.refs_2_.refs_5_, bf16[256,1152]{1,0:T(8,128)(2,1)S(1)} %collective-permute-done.7.refs_4_.refs_3_.refs_5_, ...), custom_call_target="tpu_custom_call" | custom-call | flops 3623878656 | bytes 7077888 | tf_op jit(solution)/shard_map/pallas_call | solution.py:136
  60.3 0.1 shard_map.81.refs_3_
  60.4 2.1 %collective-permute-start.16 = (bf16[256,1152]{1,0:T(8,128)(2,1)S(1)}, bf16[256,1152]{1,0:T(8,128)(2,1)S(1)}, u32[]{:S(2)}, u32[]{:S(2)}) collective-permute-start(bf16[256,1152]{1,0:T(8,128)(2,1)S(1)} %shard_map.81.refs_3_), channel_id=1, source_target_pairs={{0,8},{32,56},{2,10},{34,58},{4,12},{36,60},{6,14},{38,62},{64,72}... | collective-permute-start | bytes 1769480 | tf_op jit(solution)/shard_map/ppermute | solution.py:50
  62.5 0.1 shard_map.82.refs_4_
  62.6 0.2 collective-permute-start.17
  62.7 1.1 %collective-permute-done.13.refs_2_ = bf16[256,1152]{1,0:T(8,128)(2,1)S(1)} collective-permute-done((bf16[256,1152]{1,0:T(8,128)(2,1)S(1)}, bf16[256,1152]{1,0:T(8,128)(2,1)S(1)}, u32[]{:S(2)}, u32[]{:S(2)}) %collective-permute-start.13) | collective-permute-done | bytes 589856 | tf_op jit(solution)/shard_map/ppermute | solution.py:50
  63.9 0.2 collective-permute-start.18
  64.1 2.4 %collective-permute-start.20 = (bf16[128,1152]{1,0:T(8,128)(2,1)S(1)}, bf16[128,1152]{1,0:T(8,128)(2,1)S(1)}, u32[]{:S(2)}, u32[]{:S(2)}) collective-permute-start(bf16[128,1152]{1,0:T(8,128)(2,1)S(1)} %get-tuple-element.36.refs_6_), channel_id=1, source_target_pairs={{0,64},{32,34},{2,66},{34,32},{4,68},{36,38},{6,70},{38,36},{64,0}... | collective-permute-start | bytes 884744 | tf_op jit(solution)/shard_map/ppermute | solution.py:50
  66.5 1.6 %shard_map.84.refs_1_ = f32[256,1152]{1,0:T(8,128)S(1)} custom-call(f32[1]{0:T(128)S(6)} %copy.7.refs_0_, f32[1]{0:T(128)S(6)} %copy.8.refs_1_, bf16[256,1152]{1,0:T(8,128)(2,1)S(1)} %get-tuple-element.23.refs_2_, bf16[256,1152]{1,0:T(8,128)(2,1)S(1)} %collective-permute-done.7.refs_4_.refs_3_.refs_5_, ...), custom_call_target="tpu_custom_call" | custom-call | flops 1207959552 | bytes 2359296 | tf_op jit(solution)/shard_map/pallas_call | solution.py:136
  68.1 2.6 %collective-permute-done.16.refs_2_ = bf16[256,1152]{1,0:T(8,128)(2,1)S(1)} collective-permute-done((bf16[256,1152]{1,0:T(8,128)(2,1)S(1)}, bf16[256,1152]{1,0:T(8,128)(2,1)S(1)}, u32[]{:S(2)}, u32[]{:S(2)}) %collective-permute-start.16) | collective-permute-done | bytes 589856 | tf_op jit(solution)/shard_map/ppermute | solution.py:50
  70.7 1.9 %collective-permute-done.17.refs_3_ = bf16[256,1152]{1,0:T(8,128)(2,1)S(1)} collective-permute-done((bf16[256,1152]{1,0:T(8,128)(2,1)S(1)}, bf16[256,1152]{1,0:T(8,128)(2,1)S(1)}, u32[]{:S(2)}, u32[]{:S(2)}) %collective-permute-start.17) | collective-permute-done | bytes 589856 | tf_op jit(solution)/shard_map/ppermute | solution.py:50
  72.6 0.2 shard_map.85
  73.5 0.2 collective-permute-done.20.refs_4_
  73.8 0.7 collective-permute-done.19.refs_3_
  74.5 1.6 %shard_map.86 = (f32[128,1152]{1,0:T(8,128)}, f32[128,1152]{1,0:T(8,128)}) custom-call(f32[1]{0:T(128)} %bitcast.refs_0_.is_first, f32[1]{0:T(128)S(6)} %div.3.multiplier, bf16[128,1152]{1,0:T(8,128)(2,1)S(1)} %copy-done, bf16[128,1152]{1,0:T(8,128)(2,1)S(1)} %copy-done.1, f32[128,1152]{1,0:T(8,128)S(1)} %get-tuple-element.38.refs_2_, ...), custom_call_target="tpu_custom_call" | custom-call | tf_op jit(solution)/shard_map/pallas_call | solution.py:275
  (18 shorter events, 0.5 us)
Async XLA Ops:
  0.6 2.9 %collective-permute-start = (bf16[128,1152]{1,0:T(8,128)(2,1)}, bf16[128,1152]{1,0:T(8,128)(2,1)S(1)}, u32[]{:S(2)}, u32[]{:S(2)}) collective-permute-start(bf16[128,1152]{1,0:T(8,128)(2,1)} %refs_0_.10), channel_id=1, source_target_pairs={{0,32},{32,0},{1,33},{33,1},{2,34},{34,2},{3,35},{35,3},{4,36},{36... | collective-permute-start | bytes 884744 | tf_op jit(solution)/shard_map/ppermute | solution.py:54
  2.1 1.8 %collective-permute-start.1 = (bf16[128,1152]{1,0:T(8,128)(2,1)}, bf16[128,1152]{1,0:T(8,128)(2,1)S(1)}, u32[]{:S(2)}, u32[]{:S(2)}) collective-permute-start(bf16[128,1152]{1,0:T(8,128)(2,1)} %refs_1_.10), channel_id=1, source_target_pairs={{0,32},{32,0},{1,33},{33,1},{2,34},{34,2},{3,35},{35,3},{4,36},{36... | collective-permute-start | bytes 884744 | tf_op jit(solution)/shard_map/ppermute | solution.py:54
  4.3 10.5 %collective-permute-start.2 = (bf16[256,1152]{1,0:T(8,128)(2,1)S(1)}, bf16[256,1152]{1,0:T(8,128)(2,1)S(1)}, u32[]{:S(2)}, u32[]{:S(2)}) collective-permute-start(bf16[256,1152]{1,0:T(8,128)(2,1)S(1)} %get-tuple-element.23.refs_2_), channel_id=1, source_target_pairs={{0,6},{32,97},{2,4},{34,99},{4,2},{36,101},{6,0},{38,103},{64,70},... | collective-permute-start | bytes 1769480 | tf_op jit(solution)/shard_map/ppermute | solution.py:50
  7.2 9.9 %collective-permute-start.4 = (bf16[256,1152]{1,0:T(8,128)(2,1)S(1)}, bf16[256,1152]{1,0:T(8,128)(2,1)S(1)}, u32[]{:S(2)}, u32[]{:S(2)}) collective-permute-start(bf16[256,1152]{1,0:T(8,128)(2,1)S(1)} %get-tuple-element.23.refs_2_), channel_id=1, source_target_pairs={{0,8},{32,56},{2,10},{34,58},{4,12},{36,60},{6,14},{38,62},{64,72}... | collective-permute-start | bytes 1769480 | tf_op jit(solution)/shard_map/ppermute | solution.py:50
  9.7 9.2 %collective-permute-start.5 = (bf16[256,1152]{1,0:T(8,128)(2,1)S(1)}, bf16[256,1152]{1,0:T(8,128)(2,1)S(1)}, u32[]{:S(2)}, u32[]{:S(2)}) collective-permute-start(bf16[256,1152]{1,0:T(8,128)(2,1)S(1)} %get-tuple-element.23.refs_2_), channel_id=1, source_target_pairs={{0,64},{32,34},{2,66},{34,32},{4,68},{36,38},{6,70},{38,36},{64,0}... | collective-permute-start | bytes 1769480 | tf_op jit(solution)/shard_map/ppermute | solution.py:50
  19.1 8.0 %collective-permute-start.6 = (bf16[768,1152]{1,0:T(8,128)(2,1)S(1)}, bf16[768,1152]{1,0:T(8,128)(2,1)S(1)}, u32[]{:S(2)}, u32[]{:S(2)}) collective-permute-start(bf16[768,1152]{1,0:T(8,128)(2,1)S(1)} %shard_map.70), channel_id=1, source_target_pairs={{0,32},{32,0},{1,33},{33,1},{2,34},{34,2},{3,35},{35,3},{4,36},{36... | collective-permute-start | bytes 5308424 | tf_op jit(solution)/shard_map/ppermute | solution.py:54
  20.5 12.3 %collective-permute-start.3 = (bf16[256,1152]{1,0:T(8,128)(2,1)S(1)}, bf16[256,1152]{1,0:T(8,128)(2,1)S(1)}, u32[]{:S(2)}, u32[]{:S(2)}) collective-permute-start(bf16[256,1152]{1,0:T(8,128)(2,1)S(1)} %collective-permute-done.2.refs_4_.refs_7_.refs_8_), channel_id=1, source_target_pairs={{0,72},{32,58},{2,74},{34,56},{4,76},{36,62},{6,78},{38,60},{64,8}... | collective-permute-start | bytes 1769480 | tf_op jit(solution)/shard_map/ppermute | solution.py:50
  21.6 15.8 %collective-permute-start.8 = (bf16[256,1152]{1,0:T(8,128)(2,1)S(1)}, bf16[256,1152]{1,0:T(8,128)(2,1)S(1)}, u32[]{:S(2)}, u32[]{:S(2)}) collective-permute-start(bf16[256,1152]{1,0:T(8,128)(2,1)S(1)} %collective-permute-done.4.refs_2_.refs_5_), channel_id=1, source_target_pairs={{0,64},{32,34},{2,66},{34,32},{4,68},{36,38},{6,70},{38,36},{64,0}... | collective-permute-start | bytes 1769480 | tf_op jit(solution)/shard_map/ppermute | solution.py:50
  23.5 13.9 %collective-permute-start.9 = (bf16[256,1152]{1,0:T(8,128)(2,1)S(1)}, bf16[256,1152]{1,0:T(8,128)(2,1)S(1)}, u32[]{:S(2)}, u32[]{:S(2)}) collective-permute-start(bf16[256,1152]{1,0:T(8,128)(2,1)S(1)} %collective-permute-done.5.refs_3_.refs_6_), channel_id=1, source_target_pairs={{0,6},{32,97},{2,4},{34,99},{4,2},{36,101},{6,0},{38,103},{64,70},... | collective-permute-start | bytes 1769480 | tf_op jit(solution)/shard_map/ppermute | solution.py:50
  26.2 11.2 %collective-permute-start.10 = (bf16[256,1152]{1,0:T(8,128)(2,1)S(1)}, bf16[256,1152]{1,0:T(8,128)(2,1)S(1)}, u32[]{:S(2)}, u32[]{:S(2)}) collective-permute-start(bf16[256,1152]{1,0:T(8,128)(2,1)S(1)} %collective-permute-done.2.refs_4_.refs_7_.refs_8_), channel_id=1, source_target_pairs={{0,8},{32,56},{2,10},{34,58},{4,12},{36,60},{6,14},{38,62},{64,72}... | collective-permute-start | bytes 1769480 | tf_op jit(solution)/shard_map/ppermute | solution.py:50
  32.9 4.5 %collective-permute-start.7 = (bf16[256,1152]{1,0:T(8,128)(2,1)S(1)}, bf16[256,1152]{1,0:T(8,128)(2,1)S(1)}, u32[]{:S(2)}, u32[]{:S(2)}) collective-permute-start(bf16[256,1152]{1,0:T(8,128)(2,1)S(1)} %shard_map.72), channel_id=1, source_target_pairs={{0,32},{32,0},{1,33},{33,1},{2,34},{34,2},{3,35},{35,3},{4,36},{36... | collective-permute-start | bytes 1769480 | tf_op jit(solution)/shard_map/ppermute | solution.py:54
  37.5 4.0 %collective-permute-start.11 = (bf16[768,1152]{1,0:T(8,128)(2,1)S(1)}, bf16[768,1152]{1,0:T(8,128)(2,1)S(1)}, u32[]{:S(2)}, u32[]{:S(2)}) collective-permute-start(bf16[768,1152]{1,0:T(8,128)(2,1)S(1)} %shard_map.74), channel_id=1, source_target_pairs={{0,32},{32,0},{1,33},{33,1},{2,34},{34,2},{3,35},{35,3},{4,36},{36... | collective-permute-start | bytes 5308424 | tf_op jit(solution)/shard_map/ppermute | solution.py:54
  43.1 10.0 %collective-permute-start.12 = (bf16[256,1152]{1,0:T(8,128)(2,1)S(1)}, bf16[256,1152]{1,0:T(8,128)(2,1)S(1)}, u32[]{:S(2)}, u32[]{:S(2)}) collective-permute-start(bf16[256,1152]{1,0:T(8,128)(2,1)S(1)} %shard_map.76.refs_8_), channel_id=1, source_target_pairs={{0,8},{32,56},{2,10},{34,58},{4,12},{36,60},{6,14},{38,62},{64,72}... | collective-permute-start | bytes 1769480 | tf_op jit(solution)/shard_map/ppermute | solution.py:50
  47.9 12.3 %collective-permute-start.14 = (bf16[256,1152]{1,0:T(8,128)(2,1)S(1)}, bf16[256,1152]{1,0:T(8,128)(2,1)S(1)}, u32[]{:S(2)}, u32[]{:S(2)}) collective-permute-start(bf16[256,1152]{1,0:T(8,128)(2,1)S(1)} %get-tuple-element.31.refs_7_), channel_id=1, source_target_pairs={{0,64},{32,34},{2,66},{34,32},{4,68},{36,38},{6,70},{38,36},{64,0}... | collective-permute-start | bytes 1769480 | tf_op jit(solution)/shard_map/ppermute | solution.py:50
  48.5 13.9 %collective-permute-start.15 = (bf16[256,1152]{1,0:T(8,128)(2,1)S(1)}, bf16[256,1152]{1,0:T(8,128)(2,1)S(1)}, u32[]{:S(2)}, u32[]{:S(2)}) collective-permute-start(bf16[256,1152]{1,0:T(8,128)(2,1)S(1)} %get-tuple-element.35), channel_id=1, source_target_pairs={{0,8},{32,56},{2,10},{34,58},{4,12},{36,60},{6,14},{38,62},{64,72}... | collective-permute-start | bytes 1769480 | tf_op jit(solution)/shard_map/ppermute | solution.py:50
  53.3 10.5 %collective-permute-start.13 = (bf16[256,1152]{1,0:T(8,128)(2,1)S(1)}, bf16[256,1152]{1,0:T(8,128)(2,1)S(1)}, u32[]{:S(2)}, u32[]{:S(2)}) collective-permute-start(bf16[256,1152]{1,0:T(8,128)(2,1)S(1)} %shard_map.79.refs_10_), channel_id=1, source_target_pairs={{0,6},{32,97},{2,4},{34,99},{4,2},{36,101},{6,0},{38,103},{64,70},... | collective-permute-start | bytes 1769480 | tf_op jit(solution)/shard_map/ppermute | solution.py:50
  60.4 10.3 %collective-permute-start.16 = (bf16[256,1152]{1,0:T(8,128)(2,1)S(1)}, bf16[256,1152]{1,0:T(8,128)(2,1)S(1)}, u32[]{:S(2)}, u32[]{:S(2)}) collective-permute-start(bf16[256,1152]{1,0:T(8,128)(2,1)S(1)} %shard_map.81.refs_3_), channel_id=1, source_target_pairs={{0,8},{32,56},{2,10},{34,58},{4,12},{36,60},{6,14},{38,62},{64,72}... | collective-permute-start | bytes 1769480 | tf_op jit(solution)/shard_map/ppermute | solution.py:50
  62.6 10.0 %collective-permute-start.17 = (bf16[256,1152]{1,0:T(8,128)(2,1)S(1)}, bf16[256,1152]{1,0:T(8,128)(2,1)S(1)}, u32[]{:S(2)}, u32[]{:S(2)}) collective-permute-start(bf16[256,1152]{1,0:T(8,128)(2,1)S(1)} %shard_map.82.refs_4_), channel_id=1, source_target_pairs={{0,6},{32,97},{2,4},{34,99},{4,2},{36,101},{6,0},{38,103},{64,70},... | collective-permute-start | bytes 1769480 | tf_op jit(solution)/shard_map/ppermute | solution.py:50
  63.9 8.7 %collective-permute-start.18 = (bf16[128,1152]{1,0:T(8,128)(2,1)S(1)}, bf16[128,1152]{1,0:T(8,128)(2,1)S(1)}, u32[]{:S(2)}, u32[]{:S(2)}) collective-permute-start(bf16[128,1152]{1,0:T(8,128)(2,1)S(1)} %get-tuple-element.37), channel_id=1, source_target_pairs={{0,96},{32,2},{2,98},{34,0},{4,100},{36,6},{6,102},{38,4},{64,32},... | collective-permute-start | bytes 884744 | tf_op jit(solution)/shard_map/ppermute | solution.py:50
  64.1 9.7 %collective-permute-start.20 = (bf16[128,1152]{1,0:T(8,128)(2,1)S(1)}, bf16[128,1152]{1,0:T(8,128)(2,1)S(1)}, u32[]{:S(2)}, u32[]{:S(2)}) collective-permute-start(bf16[128,1152]{1,0:T(8,128)(2,1)S(1)} %get-tuple-element.36.refs_6_), channel_id=1, source_target_pairs={{0,64},{32,34},{2,66},{34,32},{4,68},{36,38},{6,70},{38,36},{64,0}... | collective-permute-start | bytes 884744 | tf_op jit(solution)/shard_map/ppermute | solution.py:50
  68.1 6.4 %copy-start = (bf16[128,1152]{1,0:T(8,128)(2,1)S(1)}, bf16[128,1152]{1,0:T(8,128)(2,1)}, u32[]{:S(2)}) copy-start(bf16[128,1152]{1,0:T(8,128)(2,1)} %refs_0_.10) | copy-start | bytes 884740
  68.1 6.4 %copy-start.1 = (bf16[128,1152]{1,0:T(8,128)(2,1)S(1)}, bf16[128,1152]{1,0:T(8,128)(2,1)}, u32[]{:S(2)}) copy-start(bf16[128,1152]{1,0:T(8,128)(2,1)} %refs_1_.10) | copy-start | bytes 884740
  72.8 1.7 %collective-permute-start.19 = (bf16[128,1152]{1,0:T(8,128)(2,1)S(1)}, bf16[128,1152]{1,0:T(8,128)(2,1)S(1)}, u32[]{:S(2)}, u32[]{:S(2)}) collective-permute-start(bf16[128,1152]{1,0:T(8,128)(2,1)S(1)} %get-tuple-element.39), channel_id=1, source_target_pairs={{0,32},{32,0},{1,33},{33,1},{2,34},{34,2},{3,35},{35,3},{4,36},{36... | collective-permute-start | bytes 884744 | tf_op jit(solution)/shard_map/ppermute | solution.py:54

commit v21 on v19

--- a/solution.py
+++ b/solution.py
@@ -247,8 +247,9 @@
     (part_yz,) = sums_of(affine, [(mine["yz"], one + two, None)], [part_xy])
     part_yz = added(part_yz, for_yz)
     for_y = sent(part_yz, "z")
-    part_x, part_y, part_z = parts_of(ONE, [part_yz])
+    part_x, part_z = parts_of(["x", "z"], [part_yz])
     part_x, part_z = added(part_x, for_x), added(part_z, for_z)
+    (part_y,) = parts_of(["y"], [part_x, part_z])
     from_x, from_z = sent(part_x, "x"), sent(part_z, "z")
 
     def halves(scalars, refs):

time: 76.9 us -> 76.7 us (level)
  waiting for transfers between devices: 17.1 us -> 16 us
    ppermute x15, waiting for transfers between devices: 16.1 us -> 15 us  [sent(): return lax.ppermute(value, FINE_AXES, pairs)]
    pallas_call x8 -> x9, Pallas kernels: 23.4 us -> 23.6 us  [sums_of(): pl.pallas_call(functools.partial(sums_kernel, plan, len(inputs), len(afte...]
where the time goes in v21:
time: 76.7 us; the launch traced here: 76.6 us
  starting transfers between devices  29.8 us (39%)
  Pallas kernels  26.7 us (35%)
  waiting for transfers between devices  16 us (21%)
  between operations  2.94 us (4%)
  other arithmetic  1.1 us (1%)
    ppermute x15, starting transfers between devices, sent(): return lax.ppermute(value, FINE_AXES, pairs)  24.7 us
    pallas_call x9, Pallas kernels, sums_of(): pl.pallas_call(functools.partial(sums_kernel, plan, len(inputs), len(afte...  23.6 us
    ppermute x15, waiting for transfers between devices, sent(): return lax.ppermute(value, FINE_AXES, pairs)  15 us
    ppermute x6, starting transfers between devices, other_core(): return lax.ppermute(value, 'core', [(0, 1), (1, 0)])  5.09 us
    pallas_call x1, Pallas kernels, on_device(): pl.pallas_call(finish_kernel, out_shape=[jax.ShapeDtypeStruct(*shard_full...  1.58 us
  transfers between devices with their start and end apart: 21, of which 11 were waited for; matrix products, arithmetic and copies ran while one was open for 1% of the time, Pallas kernels for 30%

profile of v21, /device:TPU:1, one launch (start us, length us, event | category | flops | bytes accessed | tf_op | source)
XLA Modules:
  0.0 76.6 jit_solution(12291037639566392664)
XLA Ops:
  0.6 1.5 %collective-permute-start = (bf16[128,1152]{1,0:T(8,128)(2,1)}, bf16[128,1152]{1,0:T(8,128)(2,1)S(1)}, u32[]{:S(2)}, u32[]{:S(2)}) collective-permute-start(bf16[128,1152]{1,0:T(8,128)(2,1)} %refs_0_.11), channel_id=1, source_target_pairs={{0,32},{32,0},{1,33},{33,1},{2,34},{34,2},{3,35},{35,3},{4,36},{36... | collective-permute-start | bytes 884744 | tf_op jit(solution)/shard_map/ppermute | solution.py:54
  2.2 1.1 %pad_maximum_fusion.refs_0_ = bf16[256,1152]{1,0:T(8,128)(2,1)S(1)} fusion(bf16[128,1152]{1,0:T(8,128)(2,1)} %refs_1_.11, bf16[128,1152]{1,0:T(8,128)(2,1)} %refs_0_.11), kind=kLoop, calls=%fused_computation | loop fusion | flops 1179648 | bytes 1179648 | tf_op jit(solution)/shard_map/concatenate | solution.py:188
  3.3 0.2 shard_map.68
  3.5 0.4 collective-permute-done.1.refs_2_
  4.0 0.4 shard_map.69
  4.3 2.6 %collective-permute-start.2 = (bf16[256,1152]{1,0:T(8,128)(2,1)S(1)}, bf16[256,1152]{1,0:T(8,128)(2,1)S(1)}, u32[]{:S(2)}, u32[]{:S(2)}) collective-permute-start(bf16[256,1152]{1,0:T(8,128)(2,1)S(1)} %get-tuple-element.22.refs_2_), channel_id=1, source_target_pairs={{0,6},{32,56},{2,4},{34,58},{4,2},{36,60},{6,0},{38,62},{64,70},{9... | collective-permute-start | bytes 1769480 | tf_op jit(solution)/shard_map/ppermute | solution.py:50
  7.0 1.6 %collective-permute-start.4 = (bf16[256,1152]{1,0:T(8,128)(2,1)S(1)}, bf16[256,1152]{1,0:T(8,128)(2,1)S(1)}, u32[]{:S(2)}, u32[]{:S(2)}) collective-permute-start(bf16[256,1152]{1,0:T(8,128)(2,1)S(1)} %get-tuple-element.22.refs_2_), channel_id=1, source_target_pairs={{0,8},{32,34},{2,10},{34,32},{4,12},{36,38},{6,14},{38,36},{64,72}... | collective-permute-start | bytes 1769480 | tf_op jit(solution)/shard_map/ppermute | solution.py:50
  8.6 2.7 %collective-permute-start.5 = (bf16[256,1152]{1,0:T(8,128)(2,1)S(1)}, bf16[256,1152]{1,0:T(8,128)(2,1)S(1)}, u32[]{:S(2)}, u32[]{:S(2)}) collective-permute-start(bf16[256,1152]{1,0:T(8,128)(2,1)S(1)} %get-tuple-element.22.refs_2_), channel_id=1, source_target_pairs={{0,64},{32,97},{2,66},{34,99},{4,68},{36,101},{6,70},{38,103},{64,... | collective-permute-start | bytes 1769480 | tf_op jit(solution)/shard_map/ppermute | solution.py:50
  12.7 2.0 %collective-permute-done.2.refs_4_.refs_7_.refs_6_ = bf16[256,1152]{1,0:T(8,128)(2,1)S(1)} collective-permute-done((bf16[256,1152]{1,0:T(8,128)(2,1)S(1)}, bf16[256,1152]{1,0:T(8,128)(2,1)S(1)}, u32[]{:S(2)}, u32[]{:S(2)}) %collective-permute-start.2) | collective-permute-done | bytes 589856 | tf_op jit(solution)/shard_map/ppermute | solution.py:50
  14.7 1.5 %collective-permute-done.4.refs_2_.refs_5_ = bf16[256,1152]{1,0:T(8,128)(2,1)S(1)} collective-permute-done((bf16[256,1152]{1,0:T(8,128)(2,1)S(1)}, bf16[256,1152]{1,0:T(8,128)(2,1)S(1)}, u32[]{:S(2)}, u32[]{:S(2)}) %collective-permute-start.4) | collective-permute-done | bytes 589856 | tf_op jit(solution)/shard_map/ppermute | solution.py:50
  16.2 2.4 %collective-permute-done.5.refs_3_.refs_6_.refs_2_ = bf16[256,1152]{1,0:T(8,128)(2,1)S(1)} collective-permute-done((bf16[256,1152]{1,0:T(8,128)(2,1)S(1)}, bf16[256,1152]{1,0:T(8,128)(2,1)S(1)}, u32[]{:S(2)}, u32[]{:S(2)}) %collective-permute-start.5) | collective-permute-done | bytes 589856 | tf_op jit(solution)/shard_map/ppermute | solution.py:50
  18.6 0.1 shard_map.70
  18.8 1.7 %collective-permute-start.6 = (bf16[768,1152]{1,0:T(8,128)(2,1)S(1)}, bf16[768,1152]{1,0:T(8,128)(2,1)S(1)}, u32[]{:S(2)}, u32[]{:S(2)}) collective-permute-start(bf16[768,1152]{1,0:T(8,128)(2,1)S(1)} %shard_map.70), channel_id=1, source_target_pairs={{0,32},{32,0},{1,33},{33,1},{2,34},{34,2},{3,35},{35,3},{4,36},{36... | collective-permute-start | bytes 5308424 | tf_op jit(solution)/shard_map/ppermute | solution.py:54
  20.5 2.0 %collective-permute-start.3 = (bf16[256,1152]{1,0:T(8,128)(2,1)S(1)}, bf16[256,1152]{1,0:T(8,128)(2,1)S(1)}, u32[]{:S(2)}, u32[]{:S(2)}) collective-permute-start(bf16[256,1152]{1,0:T(8,128)(2,1)S(1)} %collective-permute-done.2.refs_4_.refs_7_.refs_6_), channel_id=1, source_target_pairs={{0,72},{32,99},{2,74},{34,97},{4,76},{36,103},{6,78},{38,101},{64,... | collective-permute-start | bytes 1769480 | tf_op jit(solution)/shard_map/ppermute | solution.py:50
  22.5 0.8 %collective-permute-start.8 = (bf16[256,1152]{1,0:T(8,128)(2,1)S(1)}, bf16[256,1152]{1,0:T(8,128)(2,1)S(1)}, u32[]{:S(2)}, u32[]{:S(2)}) collective-permute-start(bf16[256,1152]{1,0:T(8,128)(2,1)S(1)} %collective-permute-done.4.refs_2_.refs_5_), channel_id=1, source_target_pairs={{0,64},{32,97},{2,66},{34,99},{4,68},{36,101},{6,70},{38,103},{64,... | collective-permute-start | bytes 1769480 | tf_op jit(solution)/shard_map/ppermute | solution.py:50
  23.2 1.8 %collective-permute-start.9 = (bf16[256,1152]{1,0:T(8,128)(2,1)S(1)}, bf16[256,1152]{1,0:T(8,128)(2,1)S(1)}, u32[]{:S(2)}, u32[]{:S(2)}) collective-permute-start(bf16[256,1152]{1,0:T(8,128)(2,1)S(1)} %collective-permute-done.5.refs_3_.refs_6_.refs_2_), channel_id=1, source_target_pairs={{0,6},{32,56},{2,4},{34,58},{4,2},{36,60},{6,0},{38,62},{64,70},{9... | collective-permute-start | bytes 1769480 | tf_op jit(solution)/shard_map/ppermute | solution.py:50
  25.1 1.2 %collective-permute-start.10 = (bf16[256,1152]{1,0:T(8,128)(2,1)S(1)}, bf16[256,1152]{1,0:T(8,128)(2,1)S(1)}, u32[]{:S(2)}, u32[]{:S(2)}) collective-permute-start(bf16[256,1152]{1,0:T(8,128)(2,1)S(1)} %collective-permute-done.2.refs_4_.refs_7_.refs_6_), channel_id=1, source_target_pairs={{0,8},{32,34},{2,10},{34,32},{4,12},{36,38},{6,14},{38,36},{64,72}... | collective-permute-start | bytes 1769480 | tf_op jit(solution)/shard_map/ppermute | solution.py:50
  26.2 5.7 %shard_map.71 = (f32[256,1152]{1,0:T(8,128)S(1)}, f32[256,1152]{1,0:T(8,128)S(1)}, f32[256,1152]{1,0:T(8,128)S(1)}, f32[256,1152]{1,0:T(8,128)S(1)}) custom-call(f32[1]{0:T(128)S(6)} %copy.7.refs_0_, f32[1]{0:T(128)S(6)} %copy.8.refs_1_, bf16[256,1152]{1,0:T(8,128)(2,1)S(1)} %get-tuple-element.22.refs_2_, bf16[256,1152]{1,0:T(8,128)(2,1)S(1)} %get-tuple-element.23.refs_3_, ...), custom_call_target="tpu_custom_call" | custom-call | tf_op jit(solution)/shard_map/pallas_call | solution.py:136
  32.1 1.6 %shard_map.73.refs_3_.refs_6_.refs_5_ = f32[256,1152]{1,0:T(8,128)S(1)} custom-call(f32[1]{0:T(128)S(6)} %copy.7.refs_0_, f32[1]{0:T(128)S(6)} %copy.8.refs_1_, bf16[256,1152]{1,0:T(8,128)(2,1)S(1)} %collective-permute-done.3.refs_0_.refs_2_, bf16[256,1152]{1,0:T(8,128)(2,1)S(1)} %get-tuple-element.23.refs_3_, ...), custom_call_target="tpu_custom_call" | custom-call | flops 1207959552 | bytes 2359296 | tf_op jit(solution)/shard_map/pallas_call | solution.py:136
  33.7 3.2 %collective-permute-done.8.refs_0_.refs_2_ = bf16[256,1152]{1,0:T(8,128)(2,1)S(1)} collective-permute-done((bf16[256,1152]{1,0:T(8,128)(2,1)S(1)}, bf16[256,1152]{1,0:T(8,128)(2,1)S(1)}, u32[]{:S(2)}, u32[]{:S(2)}) %collective-permute-start.8) | collective-permute-done | bytes 589856 | tf_op jit(solution)/shard_map/ppermute | solution.py:50
  36.9 0.8 %collective-permute-done.10.refs_2_.refs_5_.refs_6_ = bf16[256,1152]{1,0:T(8,128)(2,1)S(1)} collective-permute-done((bf16[256,1152]{1,0:T(8,128)(2,1)S(1)}, bf16[256,1152]{1,0:T(8,128)(2,1)S(1)}, u32[]{:S(2)}, u32[]{:S(2)}) %collective-permute-start.10) | collective-permute-done | bytes 589856 | tf_op jit(solution)/shard_map/ppermute | solution.py:50
  37.7 0.1 shard_map.74
  37.8 0.5 collective-permute-start.11
  38.3 2.9 %shard_map.75 = (f32[256,1152]{1,0:T(8,128)S(1)}, f32[256,1152]{1,0:T(8,128)S(1)}) custom-call(f32[1]{0:T(128)S(6)} %copy.7.refs_0_, f32[1]{0:T(128)S(6)} %copy.8.refs_1_, bf16[256,1152]{1,0:T(8,128)(2,1)S(1)} %collective-permute-done.8.refs_0_.refs_2_, bf16[256,1152]{1,0:T(8,128)(2,1)S(1)} %get-tuple-element.23.refs_3_, ...), custom_call_target="tpu_custom_call" | custom-call | flops 2415919104 | bytes 4718592 | tf_op jit(solution)/shard_map/pallas_call | solution.py:136
  41.2 0.6 collective-permute-done.11.refs_4_.refs_6_
  41.8 1.6 %shard_map.76.refs_8_ = bf16[256,1152]{1,0:T(8,128)(2,1)S(1)} custom-call(f32[1]{0:T(128)S(6)} %copy.7.refs_0_, f32[1]{0:T(128)S(6)} %copy.8.refs_1_, bf16[256,1152]{1,0:T(8,128)(2,1)S(1)} %collective-permute-done.3.refs_0_.refs_2_, bf16[256,1152]{1,0:T(8,128)(2,1)S(1)} %collective-permute-done.7.refs_4_.refs_3_.refs_5_, ...), custom_call_target="tpu_custom_call" | custom-call | flops 1207959552 | bytes 2359296 | tf_op jit(solution)/shard_map/pallas_call | solution.py:136
  43.3 0.4 collective-permute-start.12
  43.7 2.9 %shard_map.77 = (bf16[256,1152]{1,0:T(8,128)(2,1)S(1)}, bf16[256,1152]{1,0:T(8,128)(2,1)S(1)}) custom-call(f32[1]{0:T(128)S(6)} %copy.7.refs_0_, f32[1]{0:T(128)S(6)} %copy.8.refs_1_, bf16[256,1152]{1,0:T(8,128)(2,1)S(1)} %collective-permute-done.8.refs_0_.refs_2_, bf16[256,1152]{1,0:T(8,128)(2,1)S(1)} %collective-permute-done.7.refs_4_.refs_3_.refs_5_, ...), custom_call_target="tpu_custom_call" | custom-call | flops 2415919104 | bytes 4718592 | tf_op jit(solution)/shard_map/pallas_call | solution.py:136
  46.7 2.8 %collective-permute-start.13 = (bf16[256,1152]{1,0:T(8,128)(2,1)S(1)}, bf16[256,1152]{1,0:T(8,128)(2,1)S(1)}, u32[]{:S(2)}, u32[]{:S(2)}) collective-permute-start(bf16[256,1152]{1,0:T(8,128)(2,1)S(1)} %get-tuple-element.30.refs_7_), channel_id=1, source_target_pairs={{0,64},{32,97},{2,66},{34,99},{4,68},{36,101},{6,70},{38,103},{64,... | collective-permute-start | bytes 1769480 | tf_op jit(solution)/shard_map/ppermute | solution.py:50
  49.5 1.1 %collective-permute-start.14 = (bf16[256,1152]{1,0:T(8,128)(2,1)S(1)}, bf16[256,1152]{1,0:T(8,128)(2,1)S(1)}, u32[]{:S(2)}, u32[]{:S(2)}) collective-permute-start(bf16[256,1152]{1,0:T(8,128)(2,1)S(1)} %get-tuple-element.33), channel_id=1, source_target_pairs={{0,8},{32,34},{2,10},{34,32},{4,12},{36,38},{6,14},{38,36},{64,72}... | collective-permute-start | bytes 1769480 | tf_op jit(solution)/shard_map/ppermute | solution.py:50
  50.6 2.9 %shard_map.78.refs_0_ = f32[256,1152]{1,0:T(8,128)S(1)} custom-call(f32[1]{0:T(128)S(6)} %copy.7.refs_0_, f32[1]{0:T(128)S(6)} %copy.8.refs_1_, bf16[256,1152]{1,0:T(8,128)(2,1)S(1)} %collective-permute-done.9.refs_1_.refs_2_, bf16[256,1152]{1,0:T(8,128)(2,1)S(1)} %get-tuple-element.23.refs_3_, bf16[768,1152]{1,0:T(8,128)(2,1)S(1)} %collective-permute-done.6.refs_4_, ...), custom_call_target="tpu_custom_call" | custom-call | flops 2415919104 | bytes 2359296 | tf_op jit(solution)/shard_map/pallas_call | solution.py:136
  53.5 0.1 shard_map.79.refs_8_
  53.6 1.9 %collective-permute-start.15 = (bf16[256,1152]{1,0:T(8,128)(2,1)S(1)}, bf16[256,1152]{1,0:T(8,128)(2,1)S(1)}, u32[]{:S(2)}, u32[]{:S(2)}) collective-permute-start(bf16[256,1152]{1,0:T(8,128)(2,1)S(1)} %shard_map.79.refs_8_), channel_id=1, source_target_pairs={{0,6},{32,56},{2,4},{34,58},{4,2},{36,60},{6,0},{38,62},{64,70},{9... | collective-permute-start | bytes 1769480 | tf_op jit(solution)/shard_map/ppermute | solution.py:50
  55.5 2.9 %shard_map.80 = (f32[256,1152]{1,0:T(8,128)S(1)}, f32[256,1152]{1,0:T(8,128)S(1)}) custom-call(f32[1]{0:T(128)S(6)} %copy.7.refs_0_, f32[1]{0:T(128)S(6)} %copy.8.refs_1_, bf16[256,1152]{1,0:T(8,128)(2,1)S(1)} %collective-permute-done.4.refs_2_.refs_5_, bf16[256,1152]{1,0:T(8,128)(2,1)S(1)} %collective-permute-done.7.refs_4_.refs_3_.refs_5_, ...), custom_call_target="tpu_custom_call" | custom-call | flops 2415919104 | bytes 4718592 | tf_op jit(solution)/shard_map/pallas_call | solution.py:136
  58.5 0.1 shard_map.81.refs_6_.refs_3_
  58.6 0.4 collective-permute-start.16
  59.1 1.8 %collective-permute-start.17 = (bf16[256,1152]{1,0:T(8,128)(2,1)S(1)}, bf16[256,1152]{1,0:T(8,128)(2,1)S(1)}, u32[]{:S(2)}, u32[]{:S(2)}) collective-permute-start(bf16[256,1152]{1,0:T(8,128)(2,1)S(1)} %shard_map.82.refs_7_.refs_4_), channel_id=1, source_target_pairs={{0,6},{32,56},{2,4},{34,58},{4,2},{36,60},{6,0},{38,62},{64,70},{9... | collective-permute-start | bytes 1769480 | tf_op jit(solution)/shard_map/ppermute | solution.py:50
  61.0 1.6 %shard_map.83.refs_1_ = f32[256,1152]{1,0:T(8,128)S(1)} custom-call(f32[1]{0:T(128)S(6)} %copy.7.refs_0_, f32[1]{0:T(128)S(6)} %copy.8.refs_1_, bf16[256,1152]{1,0:T(8,128)(2,1)S(1)} %collective-permute-done.5.refs_3_.refs_6_.refs_2_, bf16[256,1152]{1,0:T(8,128)(2,1)S(1)} %collective-permute-done.7.refs_4_.refs_3_.refs_5_, ...), custom_call_target="tpu_custom_call" | custom-call | flops 1207959552 | bytes 2359296 | tf_op jit(solution)/shard_map/pallas_call | solution.py:136
  62.5 1.4 %collective-permute-done.15.refs_2_ = bf16[256,1152]{1,0:T(8,128)(2,1)S(1)} collective-permute-done((bf16[256,1152]{1,0:T(8,128)(2,1)S(1)}, bf16[256,1152]{1,0:T(8,128)(2,1)S(1)}, u32[]{:S(2)}, u32[]{:S(2)}) %collective-permute-start.15) | collective-permute-done | bytes 589856 | tf_op jit(solution)/shard_map/ppermute | solution.py:50
  64.0 0.1 shard_map.84
  64.1 3.4 %collective-permute-start.18 = (bf16[128,1152]{1,0:T(8,128)(2,1)S(1)}, bf16[128,1152]{1,0:T(8,128)(2,1)S(1)}, u32[]{:S(2)}, u32[]{:S(2)}) collective-permute-start(bf16[128,1152]{1,0:T(8,128)(2,1)S(1)} %get-tuple-element.35), channel_id=1, source_target_pairs={{0,96},{32,65},{2,98},{34,67},{4,100},{36,69},{6,102},{38,71},{64,... | collective-permute-start | bytes 884744 | tf_op jit(solution)/shard_map/ppermute | solution.py:50
  67.6 1.6 %shard_map.85.refs_1_ = f32[256,1152]{1,0:T(8,128)S(1)} custom-call(f32[1]{0:T(128)S(6)} %copy.7.refs_0_, f32[1]{0:T(128)S(6)} %copy.8.refs_1_, bf16[256,1152]{1,0:T(8,128)(2,1)S(1)} %get-tuple-element.22.refs_2_, bf16[256,1152]{1,0:T(8,128)(2,1)S(1)} %collective-permute-done.7.refs_4_.refs_3_.refs_5_, ...), custom_call_target="tpu_custom_call" | custom-call | flops 1207959552 | bytes 2359296 | tf_op jit(solution)/shard_map/pallas_call | solution.py:136
  69.1 1.1 %collective-permute-done.17.refs_3_ = bf16[256,1152]{1,0:T(8,128)(2,1)S(1)} collective-permute-done((bf16[256,1152]{1,0:T(8,128)(2,1)S(1)}, bf16[256,1152]{1,0:T(8,128)(2,1)S(1)}, u32[]{:S(2)}, u32[]{:S(2)}) %collective-permute-start.17) | collective-permute-done | bytes 589856 | tf_op jit(solution)/shard_map/ppermute | solution.py:50
  70.3 0.9 %collective-permute-done.18.refs_4_.refs_5_ = bf16[128,1152]{1,0:T(8,128)(2,1)S(1)} collective-permute-done((bf16[128,1152]{1,0:T(8,128)(2,1)S(1)}, bf16[128,1152]{1,0:T(8,128)(2,1)S(1)}, u32[]{:S(2)}, u32[]{:S(2)}) %collective-permute-start.18) | collective-permute-done | bytes 294944 | tf_op jit(solution)/shard_map/ppermute | solution.py:50
  71.2 0.2 shard_map.86
  71.4 1.2 %collective-permute-start.19 = (bf16[128,1152]{1,0:T(8,128)(2,1)S(1)}, bf16[128,1152]{1,0:T(8,128)(2,1)S(1)}, u32[]{:S(2)}, u32[]{:S(2)}) collective-permute-start(bf16[128,1152]{1,0:T(8,128)(2,1)S(1)} %get-tuple-element.37), channel_id=1, source_target_pairs={{0,32},{32,0},{1,33},{33,1},{2,34},{34,2},{3,35},{35,3},{4,36},{36... | collective-permute-start | bytes 884744 | tf_op jit(solution)/shard_map/ppermute | solution.py:54
  73.3 1.5 %collective-permute-done.20.refs_4_ = bf16[128,1152]{1,0:T(8,128)(2,1)S(1)} collective-permute-done((bf16[128,1152]{1,0:T(8,128)(2,1)S(1)}, bf16[128,1152]{1,0:T(8,128)(2,1)S(1)}, u32[]{:S(2)}, u32[]{:S(2)}) %collective-permute-start.20) | collective-permute-done | bytes 294944 | tf_op jit(solution)/shard_map/ppermute | solution.py:50
  74.8 1.6 %shard_map.87 = (f32[128,1152]{1,0:T(8,128)}, f32[128,1152]{1,0:T(8,128)}) custom-call(f32[1]{0:T(128)} %bitcast.refs_0_.is_first, f32[1]{0:T(128)S(6)} %div.3.multiplier, bf16[128,1152]{1,0:T(8,128)(2,1)S(1)} %copy-done, bf16[128,1152]{1,0:T(8,128)(2,1)S(1)} %copy-done.1, f32[128,1152]{1,0:T(8,128)S(1)} %get-tuple-element.36.refs_2_, ...), custom_call_target="tpu_custom_call" | custom-call | tf_op jit(solution)/shard_map/pallas_call | solution.py:276
  (19 shorter events, 0.4 us)
Async XLA Ops:
  0.6 2.9 %collective-permute-start = (bf16[128,1152]{1,0:T(8,128)(2,1)}, bf16[128,1152]{1,0:T(8,128)(2,1)S(1)}, u32[]{:S(2)}, u32[]{:S(2)}) collective-permute-start(bf16[128,1152]{1,0:T(8,128)(2,1)} %refs_0_.11), channel_id=1, source_target_pairs={{0,32},{32,0},{1,33},{33,1},{2,34},{34,2},{3,35},{35,3},{4,36},{36... | collective-permute-start | bytes 884744 | tf_op jit(solution)/shard_map/ppermute | solution.py:54
  2.1 1.8 %collective-permute-start.1 = (bf16[128,1152]{1,0:T(8,128)(2,1)}, bf16[128,1152]{1,0:T(8,128)(2,1)S(1)}, u32[]{:S(2)}, u32[]{:S(2)}) collective-permute-start(bf16[128,1152]{1,0:T(8,128)(2,1)} %refs_1_.11), channel_id=1, source_target_pairs={{0,32},{32,0},{1,33},{33,1},{2,34},{34,2},{3,35},{35,3},{4,36},{36... | collective-permute-start | bytes 884744 | tf_op jit(solution)/shard_map/ppermute | solution.py:54
  4.3 10.3 %collective-permute-start.2 = (bf16[256,1152]{1,0:T(8,128)(2,1)S(1)}, bf16[256,1152]{1,0:T(8,128)(2,1)S(1)}, u32[]{:S(2)}, u32[]{:S(2)}) collective-permute-start(bf16[256,1152]{1,0:T(8,128)(2,1)S(1)} %get-tuple-element.22.refs_2_), channel_id=1, source_target_pairs={{0,6},{32,56},{2,4},{34,58},{4,2},{36,60},{6,0},{38,62},{64,70},{9... | collective-permute-start | bytes 1769480 | tf_op jit(solution)/shard_map/ppermute | solution.py:50
  7.0 9.2 %collective-permute-start.4 = (bf16[256,1152]{1,0:T(8,128)(2,1)S(1)}, bf16[256,1152]{1,0:T(8,128)(2,1)S(1)}, u32[]{:S(2)}, u32[]{:S(2)}) collective-permute-start(bf16[256,1152]{1,0:T(8,128)(2,1)S(1)} %get-tuple-element.22.refs_2_), channel_id=1, source_target_pairs={{0,8},{32,34},{2,10},{34,32},{4,12},{36,38},{6,14},{38,36},{64,72}... | collective-permute-start | bytes 1769480 | tf_op jit(solution)/shard_map/ppermute | solution.py:50
  8.6 10.0 %collective-permute-start.5 = (bf16[256,1152]{1,0:T(8,128)(2,1)S(1)}, bf16[256,1152]{1,0:T(8,128)(2,1)S(1)}, u32[]{:S(2)}, u32[]{:S(2)}) collective-permute-start(bf16[256,1152]{1,0:T(8,128)(2,1)S(1)} %get-tuple-element.22.refs_2_), channel_id=1, source_target_pairs={{0,64},{32,97},{2,66},{34,99},{4,68},{36,101},{6,70},{38,103},{64,... | collective-permute-start | bytes 1769480 | tf_op jit(solution)/shard_map/ppermute | solution.py:50
  18.8 7.5 %collective-permute-start.6 = (bf16[768,1152]{1,0:T(8,128)(2,1)S(1)}, bf16[768,1152]{1,0:T(8,128)(2,1)S(1)}, u32[]{:S(2)}, u32[]{:S(2)}) collective-permute-start(bf16[768,1152]{1,0:T(8,128)(2,1)S(1)} %shard_map.70), channel_id=1, source_target_pairs={{0,32},{32,0},{1,33},{33,1},{2,34},{34,2},{3,35},{35,3},{4,36},{36... | collective-permute-start | bytes 5308424 | tf_op jit(solution)/shard_map/ppermute | solution.py:54
  20.5 11.4 %collective-permute-start.3 = (bf16[256,1152]{1,0:T(8,128)(2,1)S(1)}, bf16[256,1152]{1,0:T(8,128)(2,1)S(1)}, u32[]{:S(2)}, u32[]{:S(2)}) collective-permute-start(bf16[256,1152]{1,0:T(8,128)(2,1)S(1)} %collective-permute-done.2.refs_4_.refs_7_.refs_6_), channel_id=1, source_target_pairs={{0,72},{32,99},{2,74},{34,97},{4,76},{36,103},{6,78},{38,101},{64,... | collective-permute-start | bytes 1769480 | tf_op jit(solution)/shard_map/ppermute | solution.py:50
  22.5 14.4 %collective-permute-start.8 = (bf16[256,1152]{1,0:T(8,128)(2,1)S(1)}, bf16[256,1152]{1,0:T(8,128)(2,1)S(1)}, u32[]{:S(2)}, u32[]{:S(2)}) collective-permute-start(bf16[256,1152]{1,0:T(8,128)(2,1)S(1)} %collective-permute-done.4.refs_2_.refs_5_), channel_id=1, source_target_pairs={{0,64},{32,97},{2,66},{34,99},{4,68},{36,101},{6,70},{38,103},{64,... | collective-permute-start | bytes 1769480 | tf_op jit(solution)/shard_map/ppermute | solution.py:50
  23.2 13.6 %collective-permute-start.9 = (bf16[256,1152]{1,0:T(8,128)(2,1)S(1)}, bf16[256,1152]{1,0:T(8,128)(2,1)S(1)}, u32[]{:S(2)}, u32[]{:S(2)}) collective-permute-start(bf16[256,1152]{1,0:T(8,128)(2,1)S(1)} %collective-permute-done.5.refs_3_.refs_6_.refs_2_), channel_id=1, source_target_pairs={{0,6},{32,56},{2,4},{34,58},{4,2},{36,60},{6,0},{38,62},{64,70},{9... | collective-permute-start | bytes 1769480 | tf_op jit(solution)/shard_map/ppermute | solution.py:50
  25.1 12.6 %collective-permute-start.10 = (bf16[256,1152]{1,0:T(8,128)(2,1)S(1)}, bf16[256,1152]{1,0:T(8,128)(2,1)S(1)}, u32[]{:S(2)}, u32[]{:S(2)}) collective-permute-start(bf16[256,1152]{1,0:T(8,128)(2,1)S(1)} %collective-permute-done.2.refs_4_.refs_7_.refs_6_), channel_id=1, source_target_pairs={{0,8},{32,34},{2,10},{34,32},{4,12},{36,38},{6,14},{38,36},{64,72}... | collective-permute-start | bytes 1769480 | tf_op jit(solution)/shard_map/ppermute | solution.py:50
  32.0 5.7 %collective-permute-start.7 = (bf16[256,1152]{1,0:T(8,128)(2,1)S(1)}, bf16[256,1152]{1,0:T(8,128)(2,1)S(1)}, u32[]{:S(2)}, u32[]{:S(2)}) collective-permute-start(bf16[256,1152]{1,0:T(8,128)(2,1)S(1)} %shard_map.72), channel_id=1, source_target_pairs={{0,32},{32,0},{1,33},{33,1},{2,34},{34,2},{3,35},{35,3},{4,36},{36... | collective-permute-start | bytes 1769480 | tf_op jit(solution)/shard_map/ppermute | solution.py:54
  37.8 4.0 %collective-permute-start.11 = (bf16[768,1152]{1,0:T(8,128)(2,1)S(1)}, bf16[768,1152]{1,0:T(8,128)(2,1)S(1)}, u32[]{:S(2)}, u32[]{:S(2)}) collective-permute-start(bf16[768,1152]{1,0:T(8,128)(2,1)S(1)} %shard_map.74), channel_id=1, source_target_pairs={{0,32},{32,0},{1,33},{33,1},{2,34},{34,2},{3,35},{35,3},{4,36},{36... | collective-permute-start | bytes 5308424 | tf_op jit(solution)/shard_map/ppermute | solution.py:54
  43.3 10.2 %collective-permute-start.12 = (bf16[256,1152]{1,0:T(8,128)(2,1)S(1)}, bf16[256,1152]{1,0:T(8,128)(2,1)S(1)}, u32[]{:S(2)}, u32[]{:S(2)}) collective-permute-start(bf16[256,1152]{1,0:T(8,128)(2,1)S(1)} %shard_map.76.refs_8_), channel_id=1, source_target_pairs={{0,8},{32,34},{2,10},{34,32},{4,12},{36,38},{6,14},{38,36},{64,72}... | collective-permute-start | bytes 1769480 | tf_op jit(solution)/shard_map/ppermute | solution.py:50
  46.7 11.8 %collective-permute-start.13 = (bf16[256,1152]{1,0:T(8,128)(2,1)S(1)}, bf16[256,1152]{1,0:T(8,128)(2,1)S(1)}, u32[]{:S(2)}, u32[]{:S(2)}) collective-permute-start(bf16[256,1152]{1,0:T(8,128)(2,1)S(1)} %get-tuple-element.30.refs_7_), channel_id=1, source_target_pairs={{0,64},{32,97},{2,66},{34,99},{4,68},{36,101},{6,70},{38,103},{64,... | collective-permute-start | bytes 1769480 | tf_op jit(solution)/shard_map/ppermute | solution.py:50
  49.5 9.5 %collective-permute-start.14 = (bf16[256,1152]{1,0:T(8,128)(2,1)S(1)}, bf16[256,1152]{1,0:T(8,128)(2,1)S(1)}, u32[]{:S(2)}, u32[]{:S(2)}) collective-permute-start(bf16[256,1152]{1,0:T(8,128)(2,1)S(1)} %get-tuple-element.33), channel_id=1, source_target_pairs={{0,8},{32,34},{2,10},{34,32},{4,12},{36,38},{6,14},{38,36},{64,72}... | collective-permute-start | bytes 1769480 | tf_op jit(solution)/shard_map/ppermute | solution.py:50
  53.6 10.3 %collective-permute-start.15 = (bf16[256,1152]{1,0:T(8,128)(2,1)S(1)}, bf16[256,1152]{1,0:T(8,128)(2,1)S(1)}, u32[]{:S(2)}, u32[]{:S(2)}) collective-permute-start(bf16[256,1152]{1,0:T(8,128)(2,1)S(1)} %shard_map.79.refs_8_), channel_id=1, source_target_pairs={{0,6},{32,56},{2,4},{34,58},{4,2},{36,60},{6,0},{38,62},{64,70},{9... | collective-permute-start | bytes 1769480 | tf_op jit(solution)/shard_map/ppermute | solution.py:50
  58.6 10.6 %collective-permute-start.16 = (bf16[256,1152]{1,0:T(8,128)(2,1)S(1)}, bf16[256,1152]{1,0:T(8,128)(2,1)S(1)}, u32[]{:S(2)}, u32[]{:S(2)}) collective-permute-start(bf16[256,1152]{1,0:T(8,128)(2,1)S(1)} %shard_map.81.refs_6_.refs_3_), channel_id=1, source_target_pairs={{0,8},{32,34},{2,10},{34,32},{4,12},{36,38},{6,14},{38,36},{64,72}... | collective-permute-start | bytes 1769480 | tf_op jit(solution)/shard_map/ppermute | solution.py:50
  59.1 11.2 %collective-permute-start.17 = (bf16[256,1152]{1,0:T(8,128)(2,1)S(1)}, bf16[256,1152]{1,0:T(8,128)(2,1)S(1)}, u32[]{:S(2)}, u32[]{:S(2)}) collective-permute-start(bf16[256,1152]{1,0:T(8,128)(2,1)S(1)} %shard_map.82.refs_7_.refs_4_), channel_id=1, source_target_pairs={{0,6},{32,56},{2,4},{34,58},{4,2},{36,60},{6,0},{38,62},{64,70},{9... | collective-permute-start | bytes 1769480 | tf_op jit(solution)/shard_map/ppermute | solution.py:50
  64.1 7.1 %collective-permute-start.18 = (bf16[128,1152]{1,0:T(8,128)(2,1)S(1)}, bf16[128,1152]{1,0:T(8,128)(2,1)S(1)}, u32[]{:S(2)}, u32[]{:S(2)}) collective-permute-start(bf16[128,1152]{1,0:T(8,128)(2,1)S(1)} %get-tuple-element.35), channel_id=1, source_target_pairs={{0,96},{32,65},{2,98},{34,67},{4,100},{36,69},{6,102},{38,71},{64,... | collective-permute-start | bytes 884744 | tf_op jit(solution)/shard_map/ppermute | solution.py:50
  67.5 7.3 %collective-permute-start.20 = (bf16[128,1152]{1,0:T(8,128)(2,1)S(1)}, bf16[128,1152]{1,0:T(8,128)(2,1)S(1)}, u32[]{:S(2)}, u32[]{:S(2)}) collective-permute-start(bf16[128,1152]{1,0:T(8,128)(2,1)S(1)} %get-tuple-element.34.refs_6_), channel_id=1, source_target_pairs={{0,64},{32,97},{2,66},{34,99},{4,68},{36,101},{6,70},{38,103},{64,... | collective-permute-start | bytes 884744 | tf_op jit(solution)/shard_map/ppermute | solution.py:50
  69.1 5.7 %copy-start = (bf16[128,1152]{1,0:T(8,128)(2,1)S(1)}, bf16[128,1152]{1,0:T(8,128)(2,1)}, u32[]{:S(2)}) copy-start(bf16[128,1152]{1,0:T(8,128)(2,1)} %refs_0_.11) | copy-start | bytes 884740
  69.1 5.7 %copy-start.1 = (bf16[128,1152]{1,0:T(8,128)(2,1)S(1)}, bf16[128,1152]{1,0:T(8,128)(2,1)}, u32[]{:S(2)}) copy-start(bf16[128,1152]{1,0:T(8,128)(2,1)} %refs_1_.11) | copy-start | bytes 884740
  71.4 3.4 %collective-permute-start.19 = (bf16[128,1152]{1,0:T(8,128)(2,1)S(1)}, bf16[128,1152]{1,0:T(8,128)(2,1)S(1)}, u32[]{:S(2)}, u32[]{:S(2)}) collective-permute-start(bf16[128,1152]{1,0:T(8,128)(2,1)S(1)} %get-tuple-element.37), channel_id=1, source_target_pairs={{0,32},{32,0},{1,33},{33,1},{2,34},{34,2},{3,35},{35,3},{4,36},{36... | collective-permute-start | bytes 884744 | tf_op jit(solution)/shard_map/ppermute | solution.py:54

commit v22 on v20

--- a/solution.py
+++ b/solution.py
@@ -23,7 +23,7 @@
 ANY = pl.BlockSpec(memory_space=pl.ANY)
 PARAMS = pltpu.CompilerParams(vmem_limit_bytes=VMEM_BYTES)
 
-NAMES = ({"x": "x", "y": "y", "z": "z"}, {"x": "x", "y": "z", "z": "y"})
+NAMES = ({"x": "x", "y": "y", "z": "z"}, {"x": "y", "y": "z", "z": "x"})
 ONE = ("x", "y", "z")
 TWO = ("xy", "yz", "zx")
 

time: 76.4 us -> 76.9 us (level)
  starting transfers between devices: 28.4 us -> 31 us
  waiting for transfers between devices: 17.3 us -> 15.2 us
    ppermute x15, waiting for transfers between devices: 15.8 us -> 14.2 us  [sent(): return lax.ppermute(value, FINE_AXES, pairs)]
    ppermute x6, starting transfers between devices: 3.93 us -> 5.26 us  [other_core(): return lax.ppermute(value, 'core', [(0, 1), (1, 0)])]
    ppermute x15, starting transfers between devices: 24.5 us -> 25.7 us  [sent(): return lax.ppermute(value, FINE_AXES, pairs)]
  transfers between devices with their start and end apart: 21 -> 21, of which waited for: 12 -> 10; matrix products, arithmetic and copies ran while one was open for 1% -> 1% of each run, Pallas kernels for 30% -> 30%
where the time goes in v22:
time: 76.9 us; the launch traced here: 76.7 us
  starting transfers between devices  31 us (40%)
  Pallas kernels  26.5 us (34%)
  waiting for transfers between devices  15.2 us (20%)
  between operations  2.94 us (4%)
  other arithmetic  1.1 us (1%)
    ppermute x15, starting transfers between devices, sent(): return lax.ppermute(value, FINE_AXES, pairs)  25.7 us
    pallas_call x8, Pallas kernels, sums_of(): pl.pallas_call(functools.partial(sums_kernel, plan, len(inputs), len(afte...  23.5 us
    ppermute x15, waiting for transfers between devices, sent(): return lax.ppermute(value, FINE_AXES, pairs)  14.2 us
    ppermute x6, starting transfers between devices, other_core(): return lax.ppermute(value, 'core', [(0, 1), (1, 0)])  5.26 us
    pallas_call x1, Pallas kernels, on_device(): pl.pallas_call(finish_kernel, out_shape=[jax.ShapeDtypeStruct(*shard_full...  1.58 us
  transfers between devices with their start and end apart: 21, of which 10 were waited for; matrix products, arithmetic and copies ran while one was open for 1% of the time, Pallas kernels for 30%

profile of v22, /device:TPU:1, one launch (start us, length us, event | category | flops | bytes accessed | tf_op | source)
XLA Modules:
  0.0 76.7 jit_solution(203378051926743747)
XLA Ops:
  0.6 1.5 %collective-permute-start = (bf16[128,1152]{1,0:T(8,128)(2,1)}, bf16[128,1152]{1,0:T(8,128)(2,1)S(1)}, u32[]{:S(2)}, u32[]{:S(2)}) collective-permute-start(bf16[128,1152]{1,0:T(8,128)(2,1)} %refs_0_.10), channel_id=1, source_target_pairs={{0,32},{32,0},{1,33},{33,1},{2,34},{34,2},{3,35},{35,3},{4,36},{36... | collective-permute-start | bytes 884744 | tf_op jit(solution)/shard_map/ppermute | solution.py:54
  2.2 1.1 %pad_maximum_fusion.refs_0_ = bf16[256,1152]{1,0:T(8,128)(2,1)S(1)} fusion(bf16[128,1152]{1,0:T(8,128)(2,1)} %refs_1_.10, bf16[128,1152]{1,0:T(8,128)(2,1)} %refs_0_.10), kind=kLoop, calls=%fused_computation | loop fusion | flops 1179648 | bytes 1179648 | tf_op jit(solution)/shard_map/concatenate | solution.py:188
  3.3 0.2 shard_map.68
  3.5 0.4 collective-permute-done.1.refs_2_
  4.0 0.4 shard_map.69
  4.3 2.9 %collective-permute-start.2 = (bf16[256,1152]{1,0:T(8,128)(2,1)S(1)}, bf16[256,1152]{1,0:T(8,128)(2,1)S(1)}, u32[]{:S(2)}, u32[]{:S(2)}) collective-permute-start(bf16[256,1152]{1,0:T(8,128)(2,1)S(1)} %get-tuple-element.23.refs_2_), channel_id=1, source_target_pairs={{0,6},{32,97},{2,4},{34,99},{4,2},{36,101},{6,0},{38,103},{64,70},... | collective-permute-start | bytes 1769480 | tf_op jit(solution)/shard_map/ppermute | solution.py:50
  7.2 1.6 %collective-permute-start.4 = (bf16[256,1152]{1,0:T(8,128)(2,1)S(1)}, bf16[256,1152]{1,0:T(8,128)(2,1)S(1)}, u32[]{:S(2)}, u32[]{:S(2)}) collective-permute-start(bf16[256,1152]{1,0:T(8,128)(2,1)S(1)} %get-tuple-element.23.refs_2_), channel_id=1, source_target_pairs={{0,8},{32,34},{2,10},{34,32},{4,12},{36,38},{6,14},{38,36},{64,72}... | collective-permute-start | bytes 1769480 | tf_op jit(solution)/shard_map/ppermute | solution.py:50
  8.9 2.5 %collective-permute-start.5 = (bf16[256,1152]{1,0:T(8,128)(2,1)S(1)}, bf16[256,1152]{1,0:T(8,128)(2,1)S(1)}, u32[]{:S(2)}, u32[]{:S(2)}) collective-permute-start(bf16[256,1152]{1,0:T(8,128)(2,1)S(1)} %get-tuple-element.23.refs_2_), channel_id=1, source_target_pairs={{0,64},{32,56},{2,66},{34,58},{4,68},{36,60},{6,70},{38,62},{64,0}... | collective-permute-start | bytes 1769480 | tf_op jit(solution)/shard_map/ppermute | solution.py:50
  12.7 2.2 %collective-permute-done.2.refs_4_.refs_7_.refs_8_ = bf16[256,1152]{1,0:T(8,128)(2,1)S(1)} collective-permute-done((bf16[256,1152]{1,0:T(8,128)(2,1)S(1)}, bf16[256,1152]{1,0:T(8,128)(2,1)S(1)}, u32[]{:S(2)}, u32[]{:S(2)}) %collective-permute-start.2) | collective-permute-done | bytes 589856 | tf_op jit(solution)/shard_map/ppermute | solution.py:50
  14.8 1.6 %collective-permute-done.4.refs_2_.refs_5_ = bf16[256,1152]{1,0:T(8,128)(2,1)S(1)} collective-permute-done((bf16[256,1152]{1,0:T(8,128)(2,1)S(1)}, bf16[256,1152]{1,0:T(8,128)(2,1)S(1)}, u32[]{:S(2)}, u32[]{:S(2)}) %collective-permute-start.4) | collective-permute-done | bytes 589856 | tf_op jit(solution)/shard_map/ppermute | solution.py:50
  16.4 2.4 %collective-permute-done.5.refs_3_.refs_6_ = bf16[256,1152]{1,0:T(8,128)(2,1)S(1)} collective-permute-done((bf16[256,1152]{1,0:T(8,128)(2,1)S(1)}, bf16[256,1152]{1,0:T(8,128)(2,1)S(1)}, u32[]{:S(2)}, u32[]{:S(2)}) %collective-permute-start.5) | collective-permute-done | bytes 589856 | tf_op jit(solution)/shard_map/ppermute | solution.py:50
  18.8 0.1 shard_map.70
  19.0 1.5 %collective-permute-start.6 = (bf16[768,1152]{1,0:T(8,128)(2,1)S(1)}, bf16[768,1152]{1,0:T(8,128)(2,1)S(1)}, u32[]{:S(2)}, u32[]{:S(2)}) collective-permute-start(bf16[768,1152]{1,0:T(8,128)(2,1)S(1)} %shard_map.70), channel_id=1, source_target_pairs={{0,32},{32,0},{1,33},{33,1},{2,34},{34,2},{3,35},{35,3},{4,36},{36... | collective-permute-start | bytes 5308424 | tf_op jit(solution)/shard_map/ppermute | solution.py:54
  20.5 1.1 %collective-permute-start.3 = (bf16[256,1152]{1,0:T(8,128)(2,1)S(1)}, bf16[256,1152]{1,0:T(8,128)(2,1)S(1)}, u32[]{:S(2)}, u32[]{:S(2)}) collective-permute-start(bf16[256,1152]{1,0:T(8,128)(2,1)S(1)} %collective-permute-done.2.refs_4_.refs_7_.refs_8_), channel_id=1, source_target_pairs={{0,72},{32,58},{2,74},{34,56},{4,76},{36,62},{6,78},{38,60},{64,8}... | collective-permute-start | bytes 1769480 | tf_op jit(solution)/shard_map/ppermute | solution.py:50
  21.6 0.9 %collective-permute-start.8 = (bf16[256,1152]{1,0:T(8,128)(2,1)S(1)}, bf16[256,1152]{1,0:T(8,128)(2,1)S(1)}, u32[]{:S(2)}, u32[]{:S(2)}) collective-permute-start(bf16[256,1152]{1,0:T(8,128)(2,1)S(1)} %collective-permute-done.4.refs_2_.refs_5_), channel_id=1, source_target_pairs={{0,64},{32,56},{2,66},{34,58},{4,68},{36,60},{6,70},{38,62},{64,0}... | collective-permute-start | bytes 1769480 | tf_op jit(solution)/shard_map/ppermute | solution.py:50
  22.4 2.7 %collective-permute-start.9 = (bf16[256,1152]{1,0:T(8,128)(2,1)S(1)}, bf16[256,1152]{1,0:T(8,128)(2,1)S(1)}, u32[]{:S(2)}, u32[]{:S(2)}) collective-permute-start(bf16[256,1152]{1,0:T(8,128)(2,1)S(1)} %collective-permute-done.5.refs_3_.refs_6_), channel_id=1, source_target_pairs={{0,6},{32,97},{2,4},{34,99},{4,2},{36,101},{6,0},{38,103},{64,70},... | collective-permute-start | bytes 1769480 | tf_op jit(solution)/shard_map/ppermute | solution.py:50
  25.1 1.9 %collective-permute-start.10 = (bf16[256,1152]{1,0:T(8,128)(2,1)S(1)}, bf16[256,1152]{1,0:T(8,128)(2,1)S(1)}, u32[]{:S(2)}, u32[]{:S(2)}) collective-permute-start(bf16[256,1152]{1,0:T(8,128)(2,1)S(1)} %collective-permute-done.2.refs_4_.refs_7_.refs_8_), channel_id=1, source_target_pairs={{0,8},{32,34},{2,10},{34,32},{4,12},{36,38},{6,14},{38,36},{64,72}... | collective-permute-start | bytes 1769480 | tf_op jit(solution)/shard_map/ppermute | solution.py:50
  27.1 5.7 %shard_map.71 = (f32[256,1152]{1,0:T(8,128)S(1)}, f32[256,1152]{1,0:T(8,128)S(1)}, f32[256,1152]{1,0:T(8,128)S(1)}, f32[256,1152]{1,0:T(8,128)S(1)}) custom-call(f32[1]{0:T(128)S(6)} %copy.7.refs_0_, f32[1]{0:T(128)S(6)} %copy.8.refs_1_, bf16[256,1152]{1,0:T(8,128)(2,1)S(1)} %get-tuple-element.23.refs_2_, bf16[256,1152]{1,0:T(8,128)(2,1)S(1)} %get-tuple-element.24.refs_3_, ...), custom_call_target="tpu_custom_call" | custom-call | tf_op jit(solution)/shard_map/pallas_call | solution.py:136
  33.0 1.6 %shard_map.73.refs_3_.refs_6_.refs_5_ = f32[256,1152]{1,0:T(8,128)S(1)} custom-call(f32[1]{0:T(128)S(6)} %copy.7.refs_0_, f32[1]{0:T(128)S(6)} %copy.8.refs_1_, bf16[256,1152]{1,0:T(8,128)(2,1)S(1)} %collective-permute-done.3.refs_0_.refs_2_, bf16[256,1152]{1,0:T(8,128)(2,1)S(1)} %get-tuple-element.24.refs_3_, ...), custom_call_target="tpu_custom_call" | custom-call | flops 1207959552 | bytes 2359296 | tf_op jit(solution)/shard_map/pallas_call | solution.py:136
  34.5 1.5 %collective-permute-done.8.refs_0_.refs_2_ = bf16[256,1152]{1,0:T(8,128)(2,1)S(1)} collective-permute-done((bf16[256,1152]{1,0:T(8,128)(2,1)S(1)}, bf16[256,1152]{1,0:T(8,128)(2,1)S(1)}, u32[]{:S(2)}, u32[]{:S(2)}) %collective-permute-start.8) | collective-permute-done | bytes 589856 | tf_op jit(solution)/shard_map/ppermute | solution.py:50
  36.0 1.7 %collective-permute-done.10.refs_2_.refs_5_.refs_6_ = bf16[256,1152]{1,0:T(8,128)(2,1)S(1)} collective-permute-done((bf16[256,1152]{1,0:T(8,128)(2,1)S(1)}, bf16[256,1152]{1,0:T(8,128)(2,1)S(1)}, u32[]{:S(2)}, u32[]{:S(2)}) %collective-permute-start.10) | collective-permute-done | bytes 589856 | tf_op jit(solution)/shard_map/ppermute | solution.py:50
  37.7 0.1 shard_map.74
  37.8 0.5 collective-permute-start.11
  38.3 2.9 %shard_map.75 = (f32[256,1152]{1,0:T(8,128)S(1)}, f32[256,1152]{1,0:T(8,128)S(1)}) custom-call(f32[1]{0:T(128)S(6)} %copy.7.refs_0_, f32[1]{0:T(128)S(6)} %copy.8.refs_1_, bf16[256,1152]{1,0:T(8,128)(2,1)S(1)} %collective-permute-done.8.refs_0_.refs_2_, bf16[256,1152]{1,0:T(8,128)(2,1)S(1)} %get-tuple-element.24.refs_3_, ...), custom_call_target="tpu_custom_call" | custom-call | flops 2415919104 | bytes 4718592 | tf_op jit(solution)/shard_map/pallas_call | solution.py:136
  41.2 0.6 collective-permute-done.11.refs_4_.refs_6_
  41.8 1.6 %shard_map.76.refs_8_ = bf16[256,1152]{1,0:T(8,128)(2,1)S(1)} custom-call(f32[1]{0:T(128)S(6)} %copy.7.refs_0_, f32[1]{0:T(128)S(6)} %copy.8.refs_1_, bf16[256,1152]{1,0:T(8,128)(2,1)S(1)} %collective-permute-done.3.refs_0_.refs_2_, bf16[256,1152]{1,0:T(8,128)(2,1)S(1)} %collective-permute-done.7.refs_4_.refs_3_.refs_5_, ...), custom_call_target="tpu_custom_call" | custom-call | flops 1207959552 | bytes 2359296 | tf_op jit(solution)/shard_map/pallas_call | solution.py:136
  43.3 0.4 collective-permute-start.12
  43.7 2.9 %shard_map.77 = (bf16[256,1152]{1,0:T(8,128)(2,1)S(1)}, bf16[256,1152]{1,0:T(8,128)(2,1)S(1)}) custom-call(f32[1]{0:T(128)S(6)} %copy.7.refs_0_, f32[1]{0:T(128)S(6)} %copy.8.refs_1_, bf16[256,1152]{1,0:T(8,128)(2,1)S(1)} %collective-permute-done.8.refs_0_.refs_2_, bf16[256,1152]{1,0:T(8,128)(2,1)S(1)} %collective-permute-done.7.refs_4_.refs_3_.refs_5_, ...), custom_call_target="tpu_custom_call" | custom-call | flops 2415919104 | bytes 4718592 | tf_op jit(solution)/shard_map/pallas_call | solution.py:136
  46.7 1.9 %collective-permute-start.14 = (bf16[256,1152]{1,0:T(8,128)(2,1)S(1)}, bf16[256,1152]{1,0:T(8,128)(2,1)S(1)}, u32[]{:S(2)}, u32[]{:S(2)}) collective-permute-start(bf16[256,1152]{1,0:T(8,128)(2,1)S(1)} %get-tuple-element.31.refs_7_), channel_id=1, source_target_pairs={{0,64},{32,56},{2,66},{34,58},{4,68},{36,60},{6,70},{38,62},{64,0}... | collective-permute-start | bytes 1769480 | tf_op jit(solution)/shard_map/ppermute | solution.py:50
  48.6 1.1 %collective-permute-start.15 = (bf16[256,1152]{1,0:T(8,128)(2,1)S(1)}, bf16[256,1152]{1,0:T(8,128)(2,1)S(1)}, u32[]{:S(2)}, u32[]{:S(2)}) collective-permute-start(bf16[256,1152]{1,0:T(8,128)(2,1)S(1)} %get-tuple-element.35), channel_id=1, source_target_pairs={{0,8},{32,34},{2,10},{34,32},{4,12},{36,38},{6,14},{38,36},{64,72}... | collective-permute-start | bytes 1769480 | tf_op jit(solution)/shard_map/ppermute | solution.py:50
  49.7 2.9 %shard_map.78.refs_0_ = f32[256,1152]{1,0:T(8,128)S(1)} custom-call(f32[1]{0:T(128)S(6)} %copy.7.refs_0_, f32[1]{0:T(128)S(6)} %copy.8.refs_1_, bf16[256,1152]{1,0:T(8,128)(2,1)S(1)} %collective-permute-done.9.refs_1_.refs_2_, bf16[256,1152]{1,0:T(8,128)(2,1)S(1)} %get-tuple-element.24.refs_3_, bf16[768,1152]{1,0:T(8,128)(2,1)S(1)} %collective-permute-done.6.refs_4_, ...), custom_call_target="tpu_custom_call" | custom-call | flops 2415919104 | bytes 2359296 | tf_op jit(solution)/shard_map/pallas_call | solution.py:136
  52.6 0.1 shard_map.79.refs_10_
  52.7 3.0 %collective-permute-start.13 = (bf16[256,1152]{1,0:T(8,128)(2,1)S(1)}, bf16[256,1152]{1,0:T(8,128)(2,1)S(1)}, u32[]{:S(2)}, u32[]{:S(2)}) collective-permute-start(bf16[256,1152]{1,0:T(8,128)(2,1)S(1)} %shard_map.79.refs_10_), channel_id=1, source_target_pairs={{0,6},{32,97},{2,4},{34,99},{4,2},{36,101},{6,0},{38,103},{64,70},... | collective-permute-start | bytes 1769480 | tf_op jit(solution)/shard_map/ppermute | solution.py:50
  55.8 4.3 %shard_map.80 = (f32[256,1152]{1,0:T(8,128)S(1)}, f32[256,1152]{1,0:T(8,128)S(1)}, f32[256,1152]{1,0:T(8,128)S(1)}) custom-call(f32[1]{0:T(128)S(6)} %copy.7.refs_0_, f32[1]{0:T(128)S(6)} %copy.8.refs_1_, bf16[256,1152]{1,0:T(8,128)(2,1)S(1)} %collective-permute-done.4.refs_2_.refs_5_, bf16[256,1152]{1,0:T(8,128)(2,1)S(1)} %collective-permute-done.7.refs_4_.refs_3_.refs_5_, ...), custom_call_target="tpu_custom_call" | custom-call | flops 3623878656 | bytes 7077888 | tf_op jit(solution)/shard_map/pallas_call | solution.py:136
  60.1 0.1 shard_map.81.refs_3_
  60.2 0.4 collective-permute-start.16
  60.6 0.1 shard_map.82.refs_4_
  60.7 1.0 %collective-permute-start.17 = (bf16[256,1152]{1,0:T(8,128)(2,1)S(1)}, bf16[256,1152]{1,0:T(8,128)(2,1)S(1)}, u32[]{:S(2)}, u32[]{:S(2)}) collective-permute-start(bf16[256,1152]{1,0:T(8,128)(2,1)S(1)} %shard_map.82.refs_4_), channel_id=1, source_target_pairs={{0,6},{32,97},{2,4},{34,99},{4,2},{36,101},{6,0},{38,103},{64,70},... | collective-permute-start | bytes 1769480 | tf_op jit(solution)/shard_map/ppermute | solution.py:50
  61.7 1.7 %collective-permute-done.13.refs_2_ = bf16[256,1152]{1,0:T(8,128)(2,1)S(1)} collective-permute-done((bf16[256,1152]{1,0:T(8,128)(2,1)S(1)}, bf16[256,1152]{1,0:T(8,128)(2,1)S(1)}, u32[]{:S(2)}, u32[]{:S(2)}) %collective-permute-start.13) | collective-permute-done | bytes 589856 | tf_op jit(solution)/shard_map/ppermute | solution.py:50
  63.3 0.1 shard_map.83
  63.4 3.4 %collective-permute-start.18 = (bf16[128,1152]{1,0:T(8,128)(2,1)S(1)}, bf16[128,1152]{1,0:T(8,128)(2,1)S(1)}, u32[]{:S(2)}, u32[]{:S(2)}) collective-permute-start(bf16[128,1152]{1,0:T(8,128)(2,1)S(1)} %get-tuple-element.37), channel_id=1, source_target_pairs={{0,96},{32,24},{2,98},{34,26},{4,100},{36,28},{6,102},{38,30},{64,... | collective-permute-start | bytes 884744 | tf_op jit(solution)/shard_map/ppermute | solution.py:50
  66.8 0.9 %collective-permute-start.20 = (bf16[128,1152]{1,0:T(8,128)(2,1)S(1)}, bf16[128,1152]{1,0:T(8,128)(2,1)S(1)}, u32[]{:S(2)}, u32[]{:S(2)}) collective-permute-start(bf16[128,1152]{1,0:T(8,128)(2,1)S(1)} %get-tuple-element.36.refs_6_), channel_id=1, source_target_pairs={{0,64},{32,56},{2,66},{34,58},{4,68},{36,60},{6,70},{38,62},{64,0}... | collective-permute-start | bytes 884744 | tf_op jit(solution)/shard_map/ppermute | solution.py:50
  67.7 1.6 %shard_map.84.refs_1_ = f32[256,1152]{1,0:T(8,128)S(1)} custom-call(f32[1]{0:T(128)S(6)} %copy.7.refs_0_, f32[1]{0:T(128)S(6)} %copy.8.refs_1_, bf16[256,1152]{1,0:T(8,128)(2,1)S(1)} %get-tuple-element.23.refs_2_, bf16[256,1152]{1,0:T(8,128)(2,1)S(1)} %collective-permute-done.7.refs_4_.refs_3_.refs_5_, ...), custom_call_target="tpu_custom_call" | custom-call | flops 1207959552 | bytes 2359296 | tf_op jit(solution)/shard_map/pallas_call | solution.py:136
  69.3 1.7 %collective-permute-done.17.refs_3_ = bf16[256,1152]{1,0:T(8,128)(2,1)S(1)} collective-permute-done((bf16[256,1152]{1,0:T(8,128)(2,1)S(1)}, bf16[256,1152]{1,0:T(8,128)(2,1)S(1)}, u32[]{:S(2)}, u32[]{:S(2)}) %collective-permute-start.17) | collective-permute-done | bytes 589856 | tf_op jit(solution)/shard_map/ppermute | solution.py:50
  71.0 0.2 shard_map.85
  71.2 1.6 %collective-permute-start.19 = (bf16[128,1152]{1,0:T(8,128)(2,1)S(1)}, bf16[128,1152]{1,0:T(8,128)(2,1)S(1)}, u32[]{:S(2)}, u32[]{:S(2)}) collective-permute-start(bf16[128,1152]{1,0:T(8,128)(2,1)S(1)} %get-tuple-element.39), channel_id=1, source_target_pairs={{0,32},{32,0},{1,33},{33,1},{2,34},{34,2},{3,35},{35,3},{4,36},{36... | collective-permute-start | bytes 884744 | tf_op jit(solution)/shard_map/ppermute | solution.py:54
  73.4 1.5 %collective-permute-done.20.refs_4_ = bf16[128,1152]{1,0:T(8,128)(2,1)S(1)} collective-permute-done((bf16[128,1152]{1,0:T(8,128)(2,1)S(1)}, bf16[128,1152]{1,0:T(8,128)(2,1)S(1)}, u32[]{:S(2)}, u32[]{:S(2)}) %collective-permute-start.20) | collective-permute-done | bytes 294944 | tf_op jit(solution)/shard_map/ppermute | solution.py:50
  75.0 1.6 %shard_map.86 = (f32[128,1152]{1,0:T(8,128)}, f32[128,1152]{1,0:T(8,128)}) custom-call(f32[1]{0:T(128)} %bitcast.refs_0_.is_first, f32[1]{0:T(128)S(6)} %div.3.multiplier, bf16[128,1152]{1,0:T(8,128)(2,1)S(1)} %copy-done, bf16[128,1152]{1,0:T(8,128)(2,1)S(1)} %copy-done.1, f32[128,1152]{1,0:T(8,128)S(1)} %get-tuple-element.38.refs_2_, ...), custom_call_target="tpu_custom_call" | custom-call | tf_op jit(solution)/shard_map/pallas_call | solution.py:275
  (18 shorter events, 0.3 us)
Async XLA Ops:
  0.6 2.9 %collective-permute-start = (bf16[128,1152]{1,0:T(8,128)(2,1)}, bf16[128,1152]{1,0:T(8,128)(2,1)S(1)}, u32[]{:S(2)}, u32[]{:S(2)}) collective-permute-start(bf16[128,1152]{1,0:T(8,128)(2,1)} %refs_0_.10), channel_id=1, source_target_pairs={{0,32},{32,0},{1,33},{33,1},{2,34},{34,2},{3,35},{35,3},{4,36},{36... | collective-permute-start | bytes 884744 | tf_op jit(solution)/shard_map/ppermute | solution.py:54
  2.1 1.8 %collective-permute-start.1 = (bf16[128,1152]{1,0:T(8,128)(2,1)}, bf16[128,1152]{1,0:T(8,128)(2,1)S(1)}, u32[]{:S(2)}, u32[]{:S(2)}) collective-permute-start(bf16[128,1152]{1,0:T(8,128)(2,1)} %refs_1_.10), channel_id=1, source_target_pairs={{0,32},{32,0},{1,33},{33,1},{2,34},{34,2},{3,35},{35,3},{4,36},{36... | collective-permute-start | bytes 884744 | tf_op jit(solution)/shard_map/ppermute | solution.py:54
  4.3 10.5 %collective-permute-start.2 = (bf16[256,1152]{1,0:T(8,128)(2,1)S(1)}, bf16[256,1152]{1,0:T(8,128)(2,1)S(1)}, u32[]{:S(2)}, u32[]{:S(2)}) collective-permute-start(bf16[256,1152]{1,0:T(8,128)(2,1)S(1)} %get-tuple-element.23.refs_2_), channel_id=1, source_target_pairs={{0,6},{32,97},{2,4},{34,99},{4,2},{36,101},{6,0},{38,103},{64,70},... | collective-permute-start | bytes 1769480 | tf_op jit(solution)/shard_map/ppermute | solution.py:50
  7.2 9.2 %collective-permute-start.4 = (bf16[256,1152]{1,0:T(8,128)(2,1)S(1)}, bf16[256,1152]{1,0:T(8,128)(2,1)S(1)}, u32[]{:S(2)}, u32[]{:S(2)}) collective-permute-start(bf16[256,1152]{1,0:T(8,128)(2,1)S(1)} %get-tuple-element.23.refs_2_), channel_id=1, source_target_pairs={{0,8},{32,34},{2,10},{34,32},{4,12},{36,38},{6,14},{38,36},{64,72}... | collective-permute-start | bytes 1769480 | tf_op jit(solution)/shard_map/ppermute | solution.py:50
  8.9 9.9 %collective-permute-start.5 = (bf16[256,1152]{1,0:T(8,128)(2,1)S(1)}, bf16[256,1152]{1,0:T(8,128)(2,1)S(1)}, u32[]{:S(2)}, u32[]{:S(2)}) collective-permute-start(bf16[256,1152]{1,0:T(8,128)(2,1)S(1)} %get-tuple-element.23.refs_2_), channel_id=1, source_target_pairs={{0,64},{32,56},{2,66},{34,58},{4,68},{36,60},{6,70},{38,62},{64,0}... | collective-permute-start | bytes 1769480 | tf_op jit(solution)/shard_map/ppermute | solution.py:50
  19.0 8.1 %collective-permute-start.6 = (bf16[768,1152]{1,0:T(8,128)(2,1)S(1)}, bf16[768,1152]{1,0:T(8,128)(2,1)S(1)}, u32[]{:S(2)}, u32[]{:S(2)}) collective-permute-start(bf16[768,1152]{1,0:T(8,128)(2,1)S(1)} %shard_map.70), channel_id=1, source_target_pairs={{0,32},{32,0},{1,33},{33,1},{2,34},{34,2},{3,35},{35,3},{4,36},{36... | collective-permute-start | bytes 5308424 | tf_op jit(solution)/shard_map/ppermute | solution.py:54
  20.5 12.3 %collective-permute-start.3 = (bf16[256,1152]{1,0:T(8,128)(2,1)S(1)}, bf16[256,1152]{1,0:T(8,128)(2,1)S(1)}, u32[]{:S(2)}, u32[]{:S(2)}) collective-permute-start(bf16[256,1152]{1,0:T(8,128)(2,1)S(1)} %collective-permute-done.2.refs_4_.refs_7_.refs_8_), channel_id=1, source_target_pairs={{0,72},{32,58},{2,74},{34,56},{4,76},{36,62},{6,78},{38,60},{64,8}... | collective-permute-start | bytes 1769480 | tf_op jit(solution)/shard_map/ppermute | solution.py:50
  21.6 14.4 %collective-permute-start.8 = (bf16[256,1152]{1,0:T(8,128)(2,1)S(1)}, bf16[256,1152]{1,0:T(8,128)(2,1)S(1)}, u32[]{:S(2)}, u32[]{:S(2)}) collective-permute-start(bf16[256,1152]{1,0:T(8,128)(2,1)S(1)} %collective-permute-done.4.refs_2_.refs_5_), channel_id=1, source_target_pairs={{0,64},{32,56},{2,66},{34,58},{4,68},{36,60},{6,70},{38,62},{64,0}... | collective-permute-start | bytes 1769480 | tf_op jit(solution)/shard_map/ppermute | solution.py:50
  22.4 13.6 %collective-permute-start.9 = (bf16[256,1152]{1,0:T(8,128)(2,1)S(1)}, bf16[256,1152]{1,0:T(8,128)(2,1)S(1)}, u32[]{:S(2)}, u32[]{:S(2)}) collective-permute-start(bf16[256,1152]{1,0:T(8,128)(2,1)S(1)} %collective-permute-done.5.refs_3_.refs_6_), channel_id=1, source_target_pairs={{0,6},{32,97},{2,4},{34,99},{4,2},{36,101},{6,0},{38,103},{64,70},... | collective-permute-start | bytes 1769480 | tf_op jit(solution)/shard_map/ppermute | solution.py:50
  25.1 12.5 %collective-permute-start.10 = (bf16[256,1152]{1,0:T(8,128)(2,1)S(1)}, bf16[256,1152]{1,0:T(8,128)(2,1)S(1)}, u32[]{:S(2)}, u32[]{:S(2)}) collective-permute-start(bf16[256,1152]{1,0:T(8,128)(2,1)S(1)} %collective-permute-done.2.refs_4_.refs_7_.refs_8_), channel_id=1, source_target_pairs={{0,8},{32,34},{2,10},{34,32},{4,12},{36,38},{6,14},{38,36},{64,72}... | collective-permute-start | bytes 1769480 | tf_op jit(solution)/shard_map/ppermute | solution.py:50
  32.9 4.8 %collective-permute-start.7 = (bf16[256,1152]{1,0:T(8,128)(2,1)S(1)}, bf16[256,1152]{1,0:T(8,128)(2,1)S(1)}, u32[]{:S(2)}, u32[]{:S(2)}) collective-permute-start(bf16[256,1152]{1,0:T(8,128)(2,1)S(1)} %shard_map.72), channel_id=1, source_target_pairs={{0,32},{32,0},{1,33},{33,1},{2,34},{34,2},{3,35},{35,3},{4,36},{36... | collective-permute-start | bytes 1769480 | tf_op jit(solution)/shard_map/ppermute | solution.py:54
  37.8 4.0 %collective-permute-start.11 = (bf16[768,1152]{1,0:T(8,128)(2,1)S(1)}, bf16[768,1152]{1,0:T(8,128)(2,1)S(1)}, u32[]{:S(2)}, u32[]{:S(2)}) collective-permute-start(bf16[768,1152]{1,0:T(8,128)(2,1)S(1)} %shard_map.74), channel_id=1, source_target_pairs={{0,32},{32,0},{1,33},{33,1},{2,34},{34,2},{3,35},{35,3},{4,36},{36... | collective-permute-start | bytes 5308424 | tf_op jit(solution)/shard_map/ppermute | solution.py:54
  43.3 9.3 %collective-permute-start.12 = (bf16[256,1152]{1,0:T(8,128)(2,1)S(1)}, bf16[256,1152]{1,0:T(8,128)(2,1)S(1)}, u32[]{:S(2)}, u32[]{:S(2)}) collective-permute-start(bf16[256,1152]{1,0:T(8,128)(2,1)S(1)} %shard_map.76.refs_8_), channel_id=1, source_target_pairs={{0,8},{32,34},{2,10},{34,32},{4,12},{36,38},{6,14},{38,36},{64,72}... | collective-permute-start | bytes 1769480 | tf_op jit(solution)/shard_map/ppermute | solution.py:50
  46.7 13.4 %collective-permute-start.14 = (bf16[256,1152]{1,0:T(8,128)(2,1)S(1)}, bf16[256,1152]{1,0:T(8,128)(2,1)S(1)}, u32[]{:S(2)}, u32[]{:S(2)}) collective-permute-start(bf16[256,1152]{1,0:T(8,128)(2,1)S(1)} %get-tuple-element.31.refs_7_), channel_id=1, source_target_pairs={{0,64},{32,56},{2,66},{34,58},{4,68},{36,60},{6,70},{38,62},{64,0}... | collective-permute-start | bytes 1769480 | tf_op jit(solution)/shard_map/ppermute | solution.py:50
  48.6 12.0 %collective-permute-start.15 = (bf16[256,1152]{1,0:T(8,128)(2,1)S(1)}, bf16[256,1152]{1,0:T(8,128)(2,1)S(1)}, u32[]{:S(2)}, u32[]{:S(2)}) collective-permute-start(bf16[256,1152]{1,0:T(8,128)(2,1)S(1)} %get-tuple-element.35), channel_id=1, source_target_pairs={{0,8},{32,34},{2,10},{34,32},{4,12},{36,38},{6,14},{38,36},{64,72}... | collective-permute-start | bytes 1769480 | tf_op jit(solution)/shard_map/ppermute | solution.py:50
  52.7 10.6 %collective-permute-start.13 = (bf16[256,1152]{1,0:T(8,128)(2,1)S(1)}, bf16[256,1152]{1,0:T(8,128)(2,1)S(1)}, u32[]{:S(2)}, u32[]{:S(2)}) collective-permute-start(bf16[256,1152]{1,0:T(8,128)(2,1)S(1)} %shard_map.79.refs_10_), channel_id=1, source_target_pairs={{0,6},{32,97},{2,4},{34,99},{4,2},{36,101},{6,0},{38,103},{64,70},... | collective-permute-start | bytes 1769480 | tf_op jit(solution)/shard_map/ppermute | solution.py:50
  60.2 9.1 %collective-permute-start.16 = (bf16[256,1152]{1,0:T(8,128)(2,1)S(1)}, bf16[256,1152]{1,0:T(8,128)(2,1)S(1)}, u32[]{:S(2)}, u32[]{:S(2)}) collective-permute-start(bf16[256,1152]{1,0:T(8,128)(2,1)S(1)} %shard_map.81.refs_3_), channel_id=1, source_target_pairs={{0,8},{32,34},{2,10},{34,32},{4,12},{36,38},{6,14},{38,36},{64,72}... | collective-permute-start | bytes 1769480 | tf_op jit(solution)/shard_map/ppermute | solution.py:50
  60.7 10.3 %collective-permute-start.17 = (bf16[256,1152]{1,0:T(8,128)(2,1)S(1)}, bf16[256,1152]{1,0:T(8,128)(2,1)S(1)}, u32[]{:S(2)}, u32[]{:S(2)}) collective-permute-start(bf16[256,1152]{1,0:T(8,128)(2,1)S(1)} %shard_map.82.refs_4_), channel_id=1, source_target_pairs={{0,6},{32,97},{2,4},{34,99},{4,2},{36,101},{6,0},{38,103},{64,70},... | collective-permute-start | bytes 1769480 | tf_op jit(solution)/shard_map/ppermute | solution.py:50
  63.4 7.6 %collective-permute-start.18 = (bf16[128,1152]{1,0:T(8,128)(2,1)S(1)}, bf16[128,1152]{1,0:T(8,128)(2,1)S(1)}, u32[]{:S(2)}, u32[]{:S(2)}) collective-permute-start(bf16[128,1152]{1,0:T(8,128)(2,1)S(1)} %get-tuple-element.37), channel_id=1, source_target_pairs={{0,96},{32,24},{2,98},{34,26},{4,100},{36,28},{6,102},{38,30},{64,... | collective-permute-start | bytes 884744 | tf_op jit(solution)/shard_map/ppermute | solution.py:50
  66.8 8.1 %collective-permute-start.20 = (bf16[128,1152]{1,0:T(8,128)(2,1)S(1)}, bf16[128,1152]{1,0:T(8,128)(2,1)S(1)}, u32[]{:S(2)}, u32[]{:S(2)}) collective-permute-start(bf16[128,1152]{1,0:T(8,128)(2,1)S(1)} %get-tuple-element.36.refs_6_), channel_id=1, source_target_pairs={{0,64},{32,56},{2,66},{34,58},{4,68},{36,60},{6,70},{38,62},{64,0}... | collective-permute-start | bytes 884744 | tf_op jit(solution)/shard_map/ppermute | solution.py:50
  69.3 5.7 %copy-start = (bf16[128,1152]{1,0:T(8,128)(2,1)S(1)}, bf16[128,1152]{1,0:T(8,128)(2,1)}, u32[]{:S(2)}) copy-start(bf16[128,1152]{1,0:T(8,128)(2,1)} %refs_0_.10) | copy-start | bytes 884740
  69.3 5.7 %copy-start.1 = (bf16[128,1152]{1,0:T(8,128)(2,1)S(1)}, bf16[128,1152]{1,0:T(8,128)(2,1)}, u32[]{:S(2)}) copy-start(bf16[128,1152]{1,0:T(8,128)(2,1)} %refs_1_.10) | copy-start | bytes 884740
  71.2 3.8 %collective-permute-start.19 = (bf16[128,1152]{1,0:T(8,128)(2,1)S(1)}, bf16[128,1152]{1,0:T(8,128)(2,1)S(1)}, u32[]{:S(2)}, u32[]{:S(2)}) collective-permute-start(bf16[128,1152]{1,0:T(8,128)(2,1)S(1)} %get-tuple-element.39), channel_id=1, source_target_pairs={{0,32},{32,0},{1,33},{33,1},{2,34},{34,2},{3,35},{35,3},{4,36},{36... | collective-permute-start | bytes 884744 | tf_op jit(solution)/shard_map/ppermute | solution.py:54
